TPU v7x, 32 devices: a whole 2x2x4 slice. The times are simulated.
32 devices in a mesh: groups: 2 (over y), expert: 8 (over z, x), section: 2 (over core).
Axes of the slice: x: 2, y: 2, z: 4, core: 2. Of those that a mesh axis runs over, the one named last changes fastest.
Arguments:
- decoder_states: bfloat16 [32, 128, 1024], P(('groups', 'expert', 'section')), parts along dimension 0, may hold values from -8 to 8
- memory_keys: bfloat16 [32, 80, 1024], P(('groups', 'expert'), None, 'section'), parts along dimension 0, may hold values from -48 to 48
- memory_values: bfloat16 [32, 80, 1024], P(('groups', 'expert'), None, 'section'), parts along dimension 0, may hold values from -6 to 6
- source_lengths: int32 [32], P(('groups', 'expert', 'section')), parts along dimension 0, may hold values from 2 to 80
- target_lengths: int32 [32], P(('groups', 'expert')), parts along dimension 0, may hold values from 64 to 128
- routes: int32 [32, 128, 2], P(('groups', 'expert')), parts along dimension 0, may hold values from 0 to 3, all different within a row; in each aligned block of 256 rows (0 to 255, 256 to 511, ..., all dimensions but the last counted through in order) at most 192 rows name the same one
- attn_gain: float32 [1024], replicated, may hold values from 0.25 to 1.75
- ffn_gain: float32 [1024], replicated, may hold values from 0.25 to 1.75
- router: bfloat16 [1024, 4], replicated, may hold values from -0.1875 to 0.1875
- fc_in: bfloat16 [1024, 16384], P(None, ('expert', 'section')), may hold values from -0.1875 to 0.1875
- fc_out: bfloat16 [16384, 1024], P(('expert', 'section')), may hold values from -0.09375 to 0.09375
Outputs:
- mixed: bfloat16 [32, 128, 1024], P(('groups', 'expert', 'section')), parts along dimension 0
There are 2 independent parts, one for each index of `groups`. A program takes and returns all parts, laid end to end along the dimension named above; an argument that names none is the same for every part. Nothing has to cross between parts.
Inputs may be any that keep to these rules, and one draw needn't show every extreme that they name: `routes`: in each block of 256 rows (the tokens of one index of expert) no expert is named by more than 192 pairs.
All inputs are finite; a program needn't handle non-finite values.
Results may differ from a plain program's by a relative error of at most 0.006.
Values may be sent and summed in bfloat16 or wider, within the bound.
No kernel may reach another device: no remote copies, remote signals or barrier semaphores. Data moves between devices by JAX's collectives and lax.ppermute only.
A program may use at most 64 MiB of HBM per device.

v0:
```python
import jax
import jax.numpy as jnp
from jax import lax
from jax.sharding import PartitionSpec as P

HEAD_DIM = 128


def layer_norm(values, gain):
    widened = values.astype(jnp.float32)
    centered = widened - jnp.mean(widened, axis=-1, keepdims=True)
    spread = jnp.mean(centered * centered, axis=-1, keepdims=True)
    return (centered * lax.rsqrt(spread + 1e-05) * gain).astype(jnp.bfloat16)


def expert_apply(slot_rows, fc_in, fc_out):
    width = slot_rows.shape[-1]
    flat_rows = slot_rows.reshape(-1, width)
    hidden = jax.nn.relu(jnp.dot(flat_rows, fc_in, preferred_element_type=jnp.float32)).astype(
        jnp.bfloat16
    )
    produced = jnp.dot(hidden, fc_out, preferred_element_type=jnp.float32)
    return produced.reshape(slot_rows.shape[0], slot_rows.shape[1], width)


def local(
    decoder_states,
    memory_keys,
    memory_values,
    source_lengths,
    target_lengths,
    routes,
    attn_gain,
    ffn_gain,
    router,
    fc_in,
    fc_out,
):
    sents, full_len, width = decoder_states.shape
    heads = width // HEAD_DIM
    full_keys, full_values = (
        lax.all_to_all(memory_keys, "section", split_axis=0, concat_axis=2, tiled=True),
        lax.all_to_all(memory_values, "section", split_axis=0, concat_axis=2, tiled=True),
    )
    queries = layer_norm(decoder_states, attn_gain).reshape(sents, full_len, heads, HEAD_DIM)
    key_heads = full_keys.reshape(sents, -1, heads, HEAD_DIM)
    value_heads = full_values.reshape(sents, -1, heads, HEAD_DIM)
    scores = jnp.einsum(
        "sthd,skhd->shtk", queries, key_heads, preferred_element_type=jnp.float32
    ) * HEAD_DIM ** (-0.5)
    valid = jnp.arange(key_heads.shape[1], dtype=jnp.int32)[None, :] < source_lengths[:, None]
    scores = jnp.where(valid[:, None, None, :], scores, -jnp.inf)
    expon = jnp.exp(scores - jnp.max(scores, axis=-1, keepdims=True))
    weights = (expon / jnp.sum(expon, axis=-1, keepdims=True)).astype(jnp.bfloat16)
    attended = jnp.einsum(
        "shtk,skhd->sthd", weights, value_heads, preferred_element_type=jnp.float32
    )
    state = (decoder_states.astype(jnp.float32) + attended.reshape(sents, full_len, width)).astype(
        jnp.bfloat16
    )
    normed = layer_norm(state, ffn_gain)
    all_normed = lax.all_gather(normed, "section", axis=0, tiled=True)
    block_sents = all_normed.shape[0]
    block_rows = block_sents * full_len
    tok_rows = all_normed.reshape(block_rows, width)
    owners = lax.axis_size("expert")
    experts_count = owners // 2
    capacity = 2 * max(1, 3 * block_rows // (2 * experts_count))
    chosen_ids = routes.reshape(block_rows, 2)
    logits = jnp.dot(tok_rows, router, preferred_element_type=jnp.float32)
    onehot = chosen_ids[:, :, None] == jnp.arange(experts_count, dtype=jnp.int32)
    chosen = jnp.sum(jnp.where(onehot, logits[:, None, :], 0.0), axis=-1)
    first = jax.nn.sigmoid(chosen[:, 0] - chosen[:, 1])
    gates = jnp.stack([first, 1.0 - first], axis=-1)
    live = (jnp.arange(full_len, dtype=jnp.int32)[None, :] < target_lengths[:, None]).reshape(
        block_rows
    )
    flags = onehot.reshape(block_rows * 2, experts_count).astype(jnp.int32)
    earlier = jnp.cumsum(flags, axis=0) - flags
    slot = jnp.sum(flags * earlier, axis=-1).reshape(block_rows, 2)
    position = chosen_ids * capacity + slot
    dump_index = experts_count * capacity
    target = jnp.where(live[:, None], position, dump_index)
    row_ids = jnp.broadcast_to(jnp.arange(block_rows, dtype=jnp.int32)[:, None], (block_rows, 2))
    table = (
        jnp.full((dump_index + 1,), block_rows, jnp.int32)
        .at[target.reshape(-1)]
        .set(row_ids.reshape(-1))[:dump_index]
    )
    padded = jnp.concatenate([tok_rows, jnp.zeros((1, width), jnp.bfloat16)], axis=0)
    slot_buffer = padded[table].reshape(experts_count, capacity, width)
    outgoing = jnp.repeat(slot_buffer, 2, axis=0)
    returned = lax.all_to_all(
        expert_apply(
            lax.all_to_all(outgoing, "expert", split_axis=0, concat_axis=0, tiled=True),
            fc_in,
            fc_out,
        ).astype(jnp.bfloat16),
        "expert",
        split_axis=0,
        concat_axis=0,
        tiled=True,
    ).astype(jnp.float32)
    partial_value = jnp.sum(returned.reshape(experts_count, 2, capacity, width), axis=1)
    fetched = partial_value.reshape(dump_index, width)[jnp.where(live[:, None], position, 0)]
    weight = gates * live[:, None].astype(jnp.float32)
    contrib = jnp.sum(weight[:, :, None] * fetched, axis=1).reshape(block_sents, full_len, width)
    summed = lax.psum_scatter(contrib, "section", scatter_dimension=0, tiled=True)
    return (state.astype(jnp.float32) + summed).astype(jnp.bfloat16)


def solution(mesh):
    placed = (
        P(("groups", "expert", "section"), None, None),
        P(("groups", "expert"), None, "section"),
        P(("groups", "expert"), None, "section"),
        P(("groups", "expert", "section")),
        P(("groups", "expert")),
        P(("groups", "expert"), None, None),
        P(),
        P(),
        P(),
        P(None, ("expert", "section")),
        P(("expert", "section"), None),
    )
    return jax.shard_map(
        local,
        mesh=mesh,
        in_specs=placed,
        out_specs=P(("groups", "expert", "section"), None, None),
        check_vma=False,
    )
```

profile of v0, /device:TPU:0, one launch (start us, length us, event | category | flops | bytes accessed | tf_op | source)
XLA Modules:
  0.0 235.0 jit_solution(15206433748042427033)
XLA Ops:
  6.5 0.0 copy-start
  6.5 3.6 %all-to-all-start = ((bf16[2,80,512]{2,1,0:T(8,128)(2,1)}), bf16[2,80,512]{2,1,0:T(8,128)(2,1)S(1)}, u32[]{:S(2)}, u32[]{:S(2)}) async-start(bf16[2,80,512]{2,1,0:T(8,128)(2,1)} %param.12), calls=%async_computation | async-start | bytes 327680 | tf_op jit(solution)/shard_map/all_to_all | solution.py:42
  10.1 0.8 copy.50
  10.9 0.1 eq.42
  11.1 0.1 eq.38
  11.2 0.7 broadcast_multiply_fusion
  11.9 1.1 convert_reduce_fusion.2
  13.0 1.2 fusion.11
  14.1 1.2 fusion.16
  15.4 0.0 all-to-all-done
  15.4 3.4 %all-to-all-start.1 = ((bf16[2,80,512]{2,1,0:T(8,128)(2,1)}), bf16[2,80,512]{2,1,0:T(8,128)(2,1)S(1)}, u32[]{:S(2)}, u32[]{:S(2)}) async-start(bf16[2,80,512]{2,1,0:T(8,128)(2,1)} %param.13), calls=%async_computation.1 | async-start | bytes 327680 | tf_op jit(solution)/shard_map/all_to_all | solution.py:43
  18.9 0.2 copy.42
  19.0 0.1 reshape.305
  19.8 0.0 copy-start.1
  19.8 0.3 fusion.2
  20.1 0.7 copy-done.6
  20.8 0.1 fusion.34
  20.9 0.0 all-to-all-done.1
  20.9 0.2 copy.45
  21.1 0.0 copy-start.4
  21.1 0.1 reshape.306
  21.3 1.3 fusion.18
  22.6 0.0 copy-start.5
  22.6 0.2 copy.47
  22.8 0.0 copy-done.1
  22.8 0.1 convert_reduce_fusion.1
  23.0 0.2 fusion.8
  23.2 0.0 copy-done.4
  23.2 0.2 fusion.10
  23.4 2.3 all_gather.3
  25.7 0.0 copy-done.5
  25.7 0.1 fusion.32
  25.8 1.2 reduce-window.6
  27.0 0.2 slice_reduce_fusion
  27.2 0.2 reduce-window.9
  27.4 0.1 add_bitcast_fusion
  27.5 0.1 broadcast_in_dim.87
  27.6 0.2 broadcast_in_dim.88
  27.8 0.1 copy.49
  27.9 0.1 mul.112
  28.1 0.1 reshape.341
  28.3 2.4 %scatter_custom_fusion = s32[769]{0:T(1024)S(1)} fusion(s32[512]{0:T(512)S(1)} %bitcast.84, s32[512]{0:T(512)S(1)} %reshape.341, s32[]{:T(128)} %constant.9.clone.1), kind=kCustom, calls=%fused_computation.56 | custom fusion | bytes 3080 | tf_op jit(solution)/shard_map/scatter | solution.py:88
  30.8 3.6 %gather_fusion = bf16[768,1024]{1,0:T(8,128)(2,1)} fusion(bf16[257,1024]{1,0:T(8,128)(2,1)S(1)} %concatenate.7, s32[1024]{0:T(1024)S(1)} %pad_clamp_fusion.1), kind=kCustom, calls=%fused_computation | custom fusion | bytes 3148800 | tf_op jit(solution)/shard_map/gather | solution.py:91
  34.4 1.8 broadcast_in_dim.92
  36.2 78.4 %all_to_all.40 = bf16[8,192,1024]{2,1,0:T(8,128)(2,1)} all-to-all(bf16[8,192,1024]{2,1,0:T(8,128)(2,1)S(1)} %bitcast.70), channel_id=1, replica_groups=mesh['groups'=2,'expert'=8,'section'=2] {'expert'}, dimensions={0} | all-to-all | bytes 6291456 | tf_op jit(solution)/shard_map/all_to_all | solution.py:95
  114.5 0.0 copy-done
  114.5 10.1 %convolution_convert_fusion = bf16[1536,1024]{1,0:T(8,128)(2,1)} fusion(bf16[1024,1024]{1,0:T(8,128)(2,1)S(1)} %copy-done, bf16[1536,1024]{1,0:T(8,128)(2,1)} %bitcast.76, bf16[1024,1024]{1,0:T(8,128)(2,1)} %param.20), kind=kOutput, calls=%fused_computation.6 | convolution fusion | flops 6447169536 | bytes 10485760 | tf_op jit(solution)/shard_map/dot_general | solution.py:22
  124.6 4.6 %all-to-all-start.3 = ((bf16[8,192,1024]{2,1,0:T(8,128)(2,1)}), bf16[8,192,1024]{2,1,0:T(8,128)(2,1)}, u32[]{:S(2)}, u32[]{:S(2)}) async-start(bf16[8,192,1024]{2,1,0:T(8,128)(2,1)} %bitcast.75), calls=%async_computation.3 | async-start | bytes 6291456 | tf_op jit(solution)/shard_map/all_to_all | solution.py:93
  129.2 0.2 reduce-scatter.2.cloned.1.call-start
  129.4 0.1 reshape.317
  129.6 0.0 copy-done.3
  129.6 0.2 fusion.35
  129.9 0.1 copy.48
  130.1 0.1 copy.52
  130.2 0.1 copy.53
  130.3 0.1 reshape.331
  130.5 69.1 %all-to-all-done.3 = bf16[8,192,1024]{2,1,0:T(8,128)(2,1)} async-done(((bf16[8,192,1024]{2,1,0:T(8,128)(2,1)}), bf16[8,192,1024]{2,1,0:T(8,128)(2,1)}, u32[]{:S(2)}, u32[]{:S(2)}) %all-to-all-start.3) | async-done | bytes 3145760 | tf_op jit(solution)/shard_map/all_to_all | solution.py:93
  199.6 4.7 %convert_reduce_fusion = f32[4,192,1024]{2,1,0:T(8,128)} fusion(bf16[8,192,1024]{2,1,0:T(8,128)(2,1)} %all-to-all-done.3), kind=kLoop, calls=%fused_computation.4 | loop fusion | flops 2359296 | bytes 6291456 | tf_op jit(solution)/shard_map/reduce_sum | solution.py:104
  204.3 5.5 %gather_fusion.1 = f32[512,1024]{1,0:T(8,128)} fusion(f32[768,1024]{1,0:T(8,128)} %bitcast.69, s32[1024]{0:T(1024)S(1)} %pad_clamp_fusion), kind=kCustom, calls=%fused_computation.1 | custom fusion | bytes 4196352 | tf_op jit(solution)/shard_map/gather | solution.py:105
  209.8 3.5 %reshape.330 = f32[256,2,1024]{2,1,0:T(2,128)} reshape(f32[512,1024]{1,0:T(8,128)} %gather_fusion.1) | data formatting | bytes 4194304 | tf_op jit(solution)/shard_map/gather | solution.py:105
  213.3 5.3 %multiply_reduce_fusion = f32[256,1024]{1,0:T(8,128)} fusion(f32[256,2,1024]{2,1,0:T(2,128)} %reshape.330, f32[256,2]{1,0:T(8,128)S(1)} %copy.48), kind=kLoop, calls=%fused_computation.7 | loop fusion | flops 786432 | bytes 3147776 | tf_op jit(solution)/shard_map/reduce_sum | solution.py:107
  218.6 0.0 reduce-scatter.2.cloned.1.call-update
  218.6 7.8 %reduce-scatter.2.cloned.1.call-done = f32[1,128,1024]{2,1,0:T(8,128)} async-done(((f32[2,128,1024]{2,1,0:T(8,128)}), f32[1,128,1024]{2,1,0:T(8,128)}) %reduce-scatter.2.cloned.1.call-update) | async-done | bytes 524304 | tf_op jit(solution)/shard_map/reduce_scatter | solution.py:108
  226.4 1.8 fusion.15
  (22 shorter events, 0.3 us)
Async XLA Ops:
  6.5 108.0 %copy-start = (bf16[1024,1024]{1,0:T(8,128)(2,1)S(1)}, bf16[1024,1024]{1,0:T(8,128)(2,1)}, u32[]{:S(2)}) copy-start(bf16[1024,1024]{1,0:T(8,128)(2,1)} %param.21) | copy-start | bytes 6291460
  6.5 8.9 %all-to-all-start = ((bf16[2,80,512]{2,1,0:T(8,128)(2,1)}), bf16[2,80,512]{2,1,0:T(8,128)(2,1)S(1)}, u32[]{:S(2)}, u32[]{:S(2)}) async-start(bf16[2,80,512]{2,1,0:T(8,128)(2,1)} %param.12), calls=%async_computation | async-start | bytes 327680 | tf_op jit(solution)/shard_map/all_to_all | solution.py:42
  15.4 5.5 %all-to-all-start.1 = ((bf16[2,80,512]{2,1,0:T(8,128)(2,1)}), bf16[2,80,512]{2,1,0:T(8,128)(2,1)S(1)}, u32[]{:S(2)}, u32[]{:S(2)}) async-start(bf16[2,80,512]{2,1,0:T(8,128)(2,1)} %param.13), calls=%async_computation.1 | async-start | bytes 327680 | tf_op jit(solution)/shard_map/all_to_all | solution.py:43
  19.8 3.0 %copy-start.1 = (bf16[1,128,1024]{2,1,0:T(8,128)(2,1)S(1)}, bf16[1,128,1024]{2,1,0:T(8,128)(2,1)}, u32[]{:S(2)}) copy-start(bf16[1,128,1024]{2,1,0:T(8,128)(2,1)} %param.11) | copy-start | bytes 786436
  20.1 0.7 copy-start.6
  21.1 2.1 copy-start.4
  22.6 3.1 %copy-start.5 = (s32[2]{0:T(128)S(1)}, s32[2]{0:T(128)}, u32[]{:S(2)}) copy-start(s32[2]{0:T(128)} %param.15) | copy-start | bytes 28
  124.6 5.0 %copy-start.3 = (bf16[1024,4]{0,1:T(4,128)(2,1)S(1)}, bf16[1024,4]{0,1:T(4,128)(2,1)}, u32[]{:S(2)}) copy-start(bf16[1024,4]{0,1:T(4,128)(2,1)} %param.19) | copy-start | bytes 24580
  124.6 5.2 %copy-start.2 = (s32[2,128,2]{1,2,0:T(2,128)S(1)}, s32[2,128,2]{1,2,0:T(2,128)}, u32[]{:S(2)}) copy-start(s32[2,128,2]{1,2,0:T(2,128)} %param.16) | copy-start | bytes 6148
  124.6 75.0 %all-to-all-start.3 = ((bf16[8,192,1024]{2,1,0:T(8,128)(2,1)}), bf16[8,192,1024]{2,1,0:T(8,128)(2,1)}, u32[]{:S(2)}, u32[]{:S(2)}) async-start(bf16[8,192,1024]{2,1,0:T(8,128)(2,1)} %bitcast.75), calls=%async_computation.3 | async-start | bytes 6291456 | tf_op jit(solution)/shard_map/all_to_all | solution.py:93
  129.2 97.2 %reduce-scatter.2.cloned.1.call-start = ((), (), s32[]{:S(2)}) async-start(), calls=%async_computation.5 | async-start | bytes 1572864 | tf_op jit(solution)/shard_map/reduce_scatter | solution.py:108
Sparse Core Ops, SparseCore 0:
  218.7 7.5 reduce-scatter.1
where the time goes:
time: 236 us; the launch traced here: 235 us
  blocking collectives  80.6 us (34%)
  waiting for transfers between devices  76.9 us (33%)
  local copies, waits for them, and re-layouts  21.1 us (9%)
  other arithmetic  18.3 us (8%)
  between operations  14.4 us (6%)
  matrix products  12 us (5%)
  starting transfers between devices  11.8 us (5%)
    all_to_all x1, blocking collectives, local(): lax.all_to_all(outgoing, 'expert', split_axis=0, concat_axis=0, tiled=True)  78.4 us
    all_to_all x1, waiting for transfers between devices, local(): lax.all_to_all(expert_apply(lax.all_to_all(outgoing, 'expert', split_axis...  69.1 us
    dot_general x1, matrix products, expert_apply(): produced = jnp.dot(hidden, fc_out, preferred_element_type=jnp.float32)  10.1 us
    gather x2, local copies, waits for them, and re-layouts, local(): partial_value.reshape(dump_index, width)  9 us
    reduce_scatter x1, waiting for transfers between devices, local(): lax.psum_scatter(contrib, 'section', scatter_dimension=0, tiled=True)  7.76 us
    reduce_sum x1, other arithmetic, local(): jnp.sum(weight[:, :, None] * fetched, axis=1)  5.29 us
  transfers between devices with their start and end apart: 4, of which 2 were waited for; matrix products, arithmetic and copies ran while one was open for 3% of the time, Pallas kernels for 0%

commit v1 on v0

--- a/solution.py
+++ b/solution.py
@@ -1,16 +1,144 @@
+import functools
+
 import jax
 import jax.numpy as jnp
 from jax import lax
+from jax.experimental import pallas as pl
+from jax.experimental.pallas import tpu as pltpu
 from jax.sharding import PartitionSpec as P
 
 HEAD_DIM = 128
 
 
 def layer_norm(values, gain):
-    widened = values.astype(jnp.float32)
-    centered = widened - jnp.mean(widened, axis=-1, keepdims=True)
+    centered = values - jnp.mean(values, axis=-1, keepdims=True)
     spread = jnp.mean(centered * centered, axis=-1, keepdims=True)
     return (centered * lax.rsqrt(spread + 1e-05) * gain).astype(jnp.bfloat16)
+
+
+def attend_kernel(
+    core_ref, length_ref, x_ref, own_ref, other_ref, again_ref, fgain_ref, state_ref, normed_ref, query_ref
+):
+    half = own_ref.shape[-1]
+    widened = x_ref[...].astype(jnp.float32)
+    query_ref[...] = layer_norm(widened, again_ref[...])
+    core = core_ref[0]
+    keys_seen = own_ref.shape[1]
+    valid = lax.broadcasted_iota(jnp.int32, (1, keys_seen), 1) < length_ref[0]
+    for part, memory in ((core, own_ref), (1 - core, other_ref)):
+        for head in range(half // HEAD_DIM):
+            local_at = head * HEAD_DIM
+            at = pl.multiple_of(part * half + local_at, HEAD_DIM)
+            span = pl.ds(at, HEAD_DIM)
+            scores = lax.dot_general(
+                query_ref[:, span],
+                memory[0, :, local_at : local_at + HEAD_DIM],
+                (((1,), (1,)), ((), ())),
+                preferred_element_type=jnp.float32,
+            ) * HEAD_DIM ** (-0.5)
+            scores = jnp.where(valid, scores, -jnp.inf)
+            expon = jnp.exp(scores - jnp.max(scores, axis=-1, keepdims=True))
+            weights = (expon / jnp.sum(expon, axis=-1, keepdims=True)).astype(jnp.bfloat16)
+            attended = jnp.dot(
+                weights,
+                memory[1, :, local_at : local_at + HEAD_DIM],
+                preferred_element_type=jnp.float32,
+            )
+            state_ref[:, span] = (x_ref[:, span].astype(jnp.float32) + attended).astype(
+                jnp.bfloat16
+            )
+    normed_ref[...] = layer_norm(state_ref[...].astype(jnp.float32), fgain_ref[...])
+
+
+def attend(decoder_states, memory_keys, memory_values, source_lengths, attn_gain, ffn_gain):
+    full_len, width = decoder_states.shape[1:]
+    core = lax.axis_index("section")
+    memory = jnp.stack([memory_keys, memory_values], axis=1)
+    own = lax.dynamic_index_in_dim(memory, core, 0, keepdims=False)
+    other = lax.ppermute(
+        lax.dynamic_index_in_dim(memory, 1 - core, 0, keepdims=False), "section", [(0, 1), (1, 0)]
+    )
+    vmem = pl.BlockSpec(memory_space=pltpu.VMEM)
+    smem = pl.BlockSpec(memory_space=pltpu.SMEM)
+    shape = jax.ShapeDtypeStruct((full_len, width), jnp.bfloat16)
+    return pl.pallas_call(
+        attend_kernel,
+        out_shape=(shape, shape),
+        in_specs=[smem, smem, vmem, vmem, vmem, vmem, vmem],
+        out_specs=(vmem, vmem),
+        scratch_shapes=[pltpu.VMEM((full_len, width), jnp.bfloat16)],
+        compiler_params=pltpu.CompilerParams(vmem_limit_bytes=16 * 2**20),
+        name="attend",
+    )(
+        core.reshape(1),
+        source_lengths,
+        decoder_states[0],
+        own,
+        other,
+        attn_gain[None],
+        ffn_gain[None],
+    )
+
+
+def dense_kernel(expert_ref, codes_ref, x_ref, router_ref, in_ref, out_ref, result_ref):
+    expert = expert_ref[0]
+    experts_count = router_ref.shape[1]
+    sents, full_len = codes_ref.shape[1:]
+    rows = x_ref[...]
+    hidden = jnp.dot(rows, in_ref[...], preferred_element_type=jnp.float32)
+    hidden = jnp.maximum(hidden, 0.0).astype(jnp.bfloat16)
+    produced = jnp.dot(hidden, out_ref[...], preferred_element_type=jnp.float32)
+    logits = jnp.dot(rows, router_ref[...], preferred_element_type=jnp.float32)
+    names = lax.broadcasted_iota(jnp.int32, (full_len, experts_count), 1)
+    for sent in range(sents):
+        at = slice(sent * full_len, (sent + 1) * full_len)
+        code = codes_ref[0, sent : sent + 1, :].astype(jnp.float32)
+        code = jnp.broadcast_to(code, (full_len, full_len)).T[:, :1].astype(jnp.int32)
+        live = code >= 0
+        first_id = code // experts_count
+        second_id = code - first_id * experts_count
+        chosen = [
+            jnp.sum(jnp.where(names == ids, logits[at], 0.0), axis=-1, keepdims=True)
+            for ids in (first_id, second_id)
+        ]
+        first = jax.nn.sigmoid(chosen[0] - chosen[1])
+        weight = jnp.where(first_id == expert, first, 0.0) + jnp.where(
+            second_id == expert, 1.0 - first, 0.0
+        )
+        weight = jnp.where(live, weight, 0.0)
+        result_ref[at] = (weight * produced[at]).astype(jnp.bfloat16)
+
+
+def dense_experts(normed, target_lengths, routes, router, fc_in, fc_out):
+    full_len, width = normed.shape
+    experts_count = router.shape[1]
+    owners = lax.axis_size("expert")
+    live = jnp.arange(full_len, dtype=jnp.int32)[None, :] < target_lengths[:, None]
+    codes = jnp.where(live, routes[:, :, 0] * experts_count + routes[:, :, 1], -1)
+    codes = lax.all_gather(codes, "expert", axis=0, tiled=True)
+    rows = lax.all_gather(normed, ("expert", "section"), axis=0, tiled=True)
+    tile = 4 * full_len
+    steps = rows.shape[0] // tile
+    codes = codes.reshape(steps, tile // full_len, full_len)
+    expert = lax.axis_index("expert") // (owners // experts_count)
+    whole = lambda i: (0, 0)
+    gated = pl.pallas_call(
+        dense_kernel,
+        grid=(steps,),
+        out_shape=jax.ShapeDtypeStruct(rows.shape, jnp.bfloat16),
+        in_specs=[
+            pl.BlockSpec(memory_space=pltpu.SMEM),
+            pl.BlockSpec((1,) + codes.shape[1:], lambda i: (i, 0, 0)),
+            pl.BlockSpec((tile, width), lambda i: (i, 0)),
+            pl.BlockSpec(router.shape, whole),
+            pl.BlockSpec(fc_in.shape, whole),
+            pl.BlockSpec(fc_out.shape, whole),
+        ],
+        out_specs=pl.BlockSpec((tile, width), lambda i: (i, 0)),
+        compiler_params=pltpu.CompilerParams(vmem_limit_bytes=40 * 2**20),
+        name="dense_experts",
+    )(expert.reshape(1), codes, rows, router, fc_in, fc_out)
+    return lax.psum_scatter(gated, ("expert", "section"), scatter_dimension=0, tiled=True)
 
 
 def expert_apply(slot_rows, fc_in, fc_out):
@@ -23,49 +151,14 @@
     return produced.reshape(slot_rows.shape[0], slot_rows.shape[1], width)
 
 
-def local(
-    decoder_states,
-    memory_keys,
-    memory_values,
-    source_lengths,
-    target_lengths,
-    routes,
-    attn_gain,
-    ffn_gain,
-    router,
-    fc_in,
-    fc_out,
-):
-    sents, full_len, width = decoder_states.shape
-    heads = width // HEAD_DIM
-    full_keys, full_values = (
-        lax.all_to_all(memory_keys, "section", split_axis=0, concat_axis=2, tiled=True),
-        lax.all_to_all(memory_values, "section", split_axis=0, concat_axis=2, tiled=True),
-    )
-    queries = layer_norm(decoder_states, attn_gain).reshape(sents, full_len, heads, HEAD_DIM)
-    key_heads = full_keys.reshape(sents, -1, heads, HEAD_DIM)
-    value_heads = full_values.reshape(sents, -1, heads, HEAD_DIM)
-    scores = jnp.einsum(
-        "sthd,skhd->shtk", queries, key_heads, preferred_element_type=jnp.float32
-    ) * HEAD_DIM ** (-0.5)
-    valid = jnp.arange(key_heads.shape[1], dtype=jnp.int32)[None, :] < source_lengths[:, None]
-    scores = jnp.where(valid[:, None, None, :], scores, -jnp.inf)
-    expon = jnp.exp(scores - jnp.max(scores, axis=-1, keepdims=True))
-    weights = (expon / jnp.sum(expon, axis=-1, keepdims=True)).astype(jnp.bfloat16)
-    attended = jnp.einsum(
-        "shtk,skhd->sthd", weights, value_heads, preferred_element_type=jnp.float32
-    )
-    state = (decoder_states.astype(jnp.float32) + attended.reshape(sents, full_len, width)).astype(
-        jnp.bfloat16
-    )
-    normed = layer_norm(state, ffn_gain)
-    all_normed = lax.all_gather(normed, "section", axis=0, tiled=True)
+def sparse_experts(normed, target_lengths, routes, router, fc_in, fc_out, capacity):
+    full_len, width = normed.shape
+    all_normed = lax.all_gather(normed[None], "section", axis=0, tiled=True)
     block_sents = all_normed.shape[0]
     block_rows = block_sents * full_len
     tok_rows = all_normed.reshape(block_rows, width)
     owners = lax.axis_size("expert")
     experts_count = owners // 2
-    capacity = 2 * max(1, 3 * block_rows // (2 * experts_count))
     chosen_ids = routes.reshape(block_rows, 2)
     logits = jnp.dot(tok_rows, router, preferred_element_type=jnp.float32)
     onehot = chosen_ids[:, :, None] == jnp.arange(experts_count, dtype=jnp.int32)
@@ -106,7 +199,34 @@
     weight = gates * live[:, None].astype(jnp.float32)
     contrib = jnp.sum(weight[:, :, None] * fetched, axis=1).reshape(block_sents, full_len, width)
     summed = lax.psum_scatter(contrib, "section", scatter_dimension=0, tiled=True)
-    return (state.astype(jnp.float32) + summed).astype(jnp.bfloat16)
+    return summed[0]
+
+
+def local(
+    decoder_states,
+    memory_keys,
+    memory_values,
+    source_lengths,
+    target_lengths,
+    routes,
+    attn_gain,
+    ffn_gain,
+    router,
+    fc_in,
+    fc_out,
+):
+    state, normed = attend(
+        decoder_states, memory_keys, memory_values, source_lengths, attn_gain, ffn_gain
+    )
+    block_rows = routes.shape[0] * routes.shape[1]
+    experts_count = router.shape[1]
+    capacity = 2 * max(1, 3 * block_rows // (2 * experts_count))
+    expert_args = (normed, target_lengths, routes, router, fc_in, fc_out)
+    if 2 * capacity >= block_rows:
+        combined = dense_experts(*expert_args)
+    else:
+        combined = sparse_experts(*expert_args, capacity)
+    return (state.astype(jnp.float32) + combined.astype(jnp.float32)).astype(jnp.bfloat16)[None]
 
 
 def solution(mesh):

time: 236 us -> 168 us (0.71)
  blocking collectives: 80.6 us -> 22.2 us
  waiting for transfers between devices: 76.9 us -> 100 us
  Pallas kernels: 0 us -> 16.1 us
  other arithmetic: 18.3 us -> 3.48 us
  matrix products: 12 us -> 0 us
  starting transfers between devices: 11.8 us -> 0.56 us
  local copies, waits for them, and re-layouts: 21.1 us -> 11.3 us
    all_to_all x1 -> x0, blocking collectives: 78.4 us -> none  [local(): lax.all_to_all(outgoing, 'expert', split_axis=0, concat_axis=0, tiled=True)]
    all_to_all x3 -> x0, waiting for transfers between devices: 69.1 us -> none  [the longest x1 69.1 us: local(): lax.all_to_all(expert_apply(lax.all_to_all(outgoing, 'expert', split_axis...]
    reduce_scatter x1, waiting for transfers between devices: 7.76 us -> 71 us  [dense_experts(): lax.psum_scatter(gated, ('expert', 'section'), scatter_dimension=0, tiled...]
    all_gather x0 -> x1, waiting for transfers between devices: none -> 28.9 us  [dense_experts(): rows = lax.all_gather(normed, ('expert', 'section'), axis=0, tiled=True)]
    all_gather x1, blocking collectives: 2.29 us -> 22.2 us  [dense_experts(): codes = lax.all_gather(codes, 'expert', axis=0, tiled=True)]
    pallas_call x0 -> x2, Pallas kernels: none -> 16.1 us  [the longest x1 12.8 us: dense_experts(): pl.pallas_call(dense_kernel, grid=(steps,), out_shape=jax.ShapeDtypeStruc...]
    reduce_sum x8 -> x0, other arithmetic: 12.6 us -> none  [the longest x1 5.29 us: local(): jnp.sum(weight[:, :, None] * fetched, axis=1)]
    gather x3 -> x0, local copies, waits for them, and re-layouts: 12.6 us -> none  [the longest x2 9 us: local(): partial_value.reshape(dump_index, width)]
  transfers between devices with their start and end apart: 4 -> 3, of which waited for: 2 -> 3; matrix products, arithmetic and copies ran while one was open for 3% -> 1% of each run, Pallas kernels for 0% -> 0%
where the time goes in v1:
time: 168 us
  waiting for transfers between devices  100 us (60%)
  blocking collectives  22.2 us (13%)
  Pallas kernels  16.1 us (10%)
  between operations  14.1 us (8%)
  local copies, waits for them, and re-layouts  11.3 us (7%)
  other arithmetic  3.48 us (2%)
    reduce_scatter x1, waiting for transfers between devices, dense_experts(): lax.psum_scatter(gated, ('expert', 'section'), scatter_dimension=0, tiled...  71 us
    all_gather x1, waiting for transfers between devices, dense_experts(): rows = lax.all_gather(normed, ('expert', 'section'), axis=0, tiled=True)  28.9 us
    all_gather x1, blocking collectives, dense_experts(): codes = lax.all_gather(codes, 'expert', axis=0, tiled=True)  22.2 us
    pallas_call x1, Pallas kernels, dense_experts(): pl.pallas_call(dense_kernel, grid=(steps,), out_shape=jax.ShapeDtypeStruc...  12.8 us
    unnamed x15, local copies, waits for them, and re-layouts  10.5 us
  transfers between devices with their start and end apart: 3, of which 3 were waited for; matrix products, arithmetic and copies ran while one was open for 1% of the time, Pallas kernels for 0%

profile of v1, /device:TPU:0, one launch (start us, length us, event | category | flops | bytes accessed | tf_op | source)
XLA Modules:
  0.0 167.9 jit_solution(1257116104092539150)
XLA Ops:
  6.5 0.0 all-gather.3.cloned.1.call-start
  6.5 1.0 fusion.2
  7.6 0.5 collective-permute-start
  8.7 0.4 collective-permute-done.other_ref
  9.1 0.0 copy-start.4
  9.1 0.9 copy-done.4
  10.1 0.0 copy-start.5
  10.1 0.7 copy-done.5
  10.8 0.0 copy-start.6
  10.8 0.7 copy-done.6
  11.4 3.2 %attend.1 = (bf16[128,1024]{1,0:T(8,128)(2,1)S(1)}, bf16[128,1024]{1,0:T(8,128)(2,1)}) custom-call(s32[1]{0:T(128)} %bitcast.core_ref, s32[1]{0:T(128)S(6)} %copy.18.length_ref, bf16[128,1024]{1,0:T(8,128)(2,1)S(1)} %bitcast.20, bf16[2,80,512]{2,1,0:T(8,128)(2,1)S(1)} %get-tuple-element.10.own_ref, bf16[2,80,512]{2,1,0:T(8,128)(2,1)S(1)} %collective-permute-done.other_ref, ...), custom_call_target="tpu_custom_call" | custom-call | tf_op jit(solution)/shard_map/attend/pallas_call | solution.py:64
  14.7 0.0 all-gather.3.cloned.1.call-update
  14.7 0.0 reduce-scatter.2.cloned.1.call-start
  14.8 0.9 copy.15.router_ref
  15.7 0.8 fusion.6
  16.4 0.7 fusion.5
  17.2 22.2 %all-gather = s32[8,2,128]{2,1,0:T(2,128)S(1)} all-gather(s32[1,2,128]{2,1,0:T(2,128)S(1)} %fusion.5), channel_id=1, replica_groups=mesh['groups'=2,'expert'=8,'section'=2] {'expert'}, dimensions={0}, use_global_device_ids=true | all-gather | bytes 9216 | tf_op jit(solution)/shard_map/all_gather | solution.py:118
  39.3 28.9 %all-gather.3.cloned.1.call-done.x_ref = bf16[2048,1024]{1,0:T(8,128)(2,1)} async-done(((bf16[128,1024]{1,0:T(8,128)(2,1)}), bf16[2048,1024]{1,0:T(8,128)(2,1)}) %all-gather.3.cloned.1.call-update) | async-done | bytes 4194320 | tf_op jit(solution)/shard_map/all_gather | solution.py:119
  68.2 0.0 copy-start.1
  68.2 2.2 %copy-done.1 = bf16[2048,1024]{1,0:T(8,128)(2,1)S(1)} copy-done((bf16[2048,1024]{1,0:T(8,128)(2,1)S(1)}, bf16[2048,1024]{1,0:T(8,128)(2,1)}, u32[]{:S(2)}) %copy-start.1) | copy-done | bytes 4194328
  70.4 0.0 copy-start.2
  70.4 1.6 copy-done.2
  72.0 0.0 copy-start.3
  72.0 1.6 copy-done.3
  73.6 12.8 %dense_experts.1 = bf16[2048,1024]{1,0:T(8,128)(2,1)S(1)} custom-call(s32[1]{0:T(128)} %bitcast.8.expert_ref, s32[4,4,128]{2,1,0:T(4,128)S(1)} %bitcast.21, bf16[2048,1024]{1,0:T(8,128)(2,1)S(1)} %copy-done.1, bf16[1024,4]{1,0:T(8,128)(2,1)S(1)} %copy.15.router_ref, bf16[1024,1024]{1,0:T(8,128)(2,1)S(1)} %copy-done.2, bf16[1024,1024]{1,0:T(8,128)(2,1)S(1)} %copy-done.3), custom_call_target="tpu_custom_call" | custom-call | tf_op jit(solution)/shard_map/dense_experts/pallas_call | solution.py:125
  86.4 0.0 copy-start
  86.4 1.9 %copy-done = bf16[2048,1024]{1,0:T(8,128)(2,1)} copy-done((bf16[2048,1024]{1,0:T(8,128)(2,1)}, bf16[2048,1024]{1,0:T(8,128)(2,1)S(1)}, u32[]{:S(2)}) %copy-start) | copy-done | bytes 4194328
  88.4 0.0 reduce-scatter.2.cloned.1.call-update
  88.4 71.0 %reduce-scatter.2.cloned.1.call-done = bf16[128,1024]{1,0:T(8,128)(2,1)} async-done(((bf16[2048,1024]{1,0:T(8,128)(2,1)}), bf16[128,1024]{1,0:T(8,128)(2,1)}) %reduce-scatter.2.cloned.1.call-update) | async-done | bytes 262160 | tf_op jit(solution)/shard_map/reduce_scatter | solution.py:141
  159.4 1.7 %fusion = bf16[1,128,1024]{2,1,0:T(8,128)(2,1)} fusion(bf16[128,1024]{1,0:T(8,128)(2,1)} %reduce-scatter.2.cloned.1.call-done, bf16[128,1024]{1,0:T(8,128)(2,1)S(1)} %get-tuple-element.7), kind=kLoop, calls=%fused_computation.5 | loop fusion | flops 524288 | bytes 786432 | tf_op jit(solution)/shard_map/broadcast_in_dim | solution.py:229
Async XLA Ops:
  6.5 61.7 %all-gather.3.cloned.1.call-start = ((), (), s32[]{:S(2)}) async-start(), calls=%async_computation.1 | async-start | bytes 4456448 | tf_op jit(solution)/shard_map/all_gather | solution.py:119
  7.6 1.5 collective-permute-start
  9.1 0.9 copy-start.4
  10.1 0.7 copy-start.5
  10.8 0.7 copy-start.6
  14.7 144.6 %reduce-scatter.2.cloned.1.call-start = ((), (), s32[]{:S(2)}) async-start(), calls=%async_computation.2 | async-start | bytes 4456448 | tf_op jit(solution)/shard_map/reduce_scatter | solution.py:141
  68.2 2.2 %copy-start.1 = (bf16[2048,1024]{1,0:T(8,128)(2,1)S(1)}, bf16[2048,1024]{1,0:T(8,128)(2,1)}, u32[]{:S(2)}) copy-start(bf16[2048,1024]{1,0:T(8,128)(2,1)} %all-gather.3.cloned.1.call-done.x_ref) | copy-start | bytes 12582916
  70.4 1.6 copy-start.2
  72.0 1.6 copy-start.3
  86.4 2.0 %copy-start = (bf16[2048,1024]{1,0:T(8,128)(2,1)}, bf16[2048,1024]{1,0:T(8,128)(2,1)S(1)}, u32[]{:S(2)}) copy-start(bf16[2048,1024]{1,0:T(8,128)(2,1)S(1)} %dense_experts.1) | copy-start | bytes 12582916
Sparse Core Ops, SparseCore 0:
  14.8 53.3 all-gather.2
  88.5 70.7 reduce-scatter.1

commit v2 on v0

--- a/solution.py
+++ b/solution.py
@@ -1,16 +1,322 @@
+import functools
+
 import jax
 import jax.numpy as jnp
 from jax import lax
+from jax.experimental import pallas as pl
+from jax.experimental.pallas import tpu as pltpu
 from jax.sharding import PartitionSpec as P
 
 HEAD_DIM = 128
 
 
 def layer_norm(values, gain):
-    widened = values.astype(jnp.float32)
-    centered = widened - jnp.mean(widened, axis=-1, keepdims=True)
+    centered = values - jnp.mean(values, axis=-1, keepdims=True)
     spread = jnp.mean(centered * centered, axis=-1, keepdims=True)
     return (centered * lax.rsqrt(spread + 1e-05) * gain).astype(jnp.bfloat16)
+
+
+VMEM = pl.BlockSpec(memory_space=pltpu.VMEM)
+SMEM = pl.BlockSpec(memory_space=pltpu.SMEM)
+
+
+def call(kernel, name, outs, scalars, arrays, scratch=(), vmem_mib=24, cost=None):
+    return pl.pallas_call(
+        kernel,
+        out_shape=tuple(jax.ShapeDtypeStruct(*out) for out in outs),
+        in_specs=[SMEM] * len(scalars) + [VMEM] * len(arrays),
+        out_specs=(VMEM,) * len(outs),
+        scratch_shapes=list(scratch),
+        compiler_params=pltpu.CompilerParams(vmem_limit_bytes=vmem_mib * 2**20),
+        cost_estimate=cost,
+        name=name,
+    )(*scalars, *arrays)
+
+
+def part_of(part, half):
+    return pl.ds(pl.multiple_of(part * half, half), half)
+
+
+def attend_kernel(
+    core_ref,
+    source_ref,
+    target_ref,
+    x_ref,
+    own_ref,
+    other_ref,
+    again_ref,
+    fgain_ref,
+    router_ref,
+    routes_ref,
+    state_ref,
+    keep_ref,
+    send_ref,
+    gates_ref,
+    scratch_ref,
+):
+    full_len = x_ref.shape[0]
+    half = own_ref.shape[-1]
+    widened = x_ref[...].astype(jnp.float32)
+    scratch_ref[...] = layer_norm(widened, again_ref[...])
+    core = core_ref[0]
+    keys_seen = own_ref.shape[1]
+    valid = lax.broadcasted_iota(jnp.int32, (1, keys_seen), 1) < source_ref[0]
+    for part, memory in ((core, own_ref), (1 - core, other_ref)):
+        for head in range(half // HEAD_DIM):
+            at = head * HEAD_DIM
+            span = pl.ds(pl.multiple_of(part * half + at, HEAD_DIM), HEAD_DIM)
+            scores = lax.dot_general(
+                scratch_ref[:, span],
+                memory[0, :, at : at + HEAD_DIM],
+                (((1,), (1,)), ((), ())),
+                preferred_element_type=jnp.float32,
+            ) * HEAD_DIM ** (-0.5)
+            scores = jnp.where(valid, scores, -jnp.inf)
+            expon = jnp.exp(scores - jnp.max(scores, axis=-1, keepdims=True))
+            weights = (expon / jnp.sum(expon, axis=-1, keepdims=True)).astype(jnp.bfloat16)
+            attended = jnp.dot(
+                weights, memory[1, :, at : at + HEAD_DIM], preferred_element_type=jnp.float32
+            )
+            state_ref[:, span] = (x_ref[:, span].astype(jnp.float32) + attended).astype(
+                jnp.bfloat16
+            )
+    scratch_ref[...] = layer_norm(state_ref[...].astype(jnp.float32), fgain_ref[...])
+    keep_ref[...] = scratch_ref[:, part_of(core, half)]
+    send_ref[...] = scratch_ref[:, part_of(1 - core, half)]
+    logits = lax.dot_general(
+        router_ref[...],
+        scratch_ref[...],
+        (((1,), (1,)), ((), ())),
+        preferred_element_type=jnp.float32,
+    )
+    names = lax.broadcasted_iota(jnp.int32, logits.shape, 0)
+    routes = routes_ref[core]
+    chosen = [
+        jnp.sum(jnp.where(names == routes[k : k + 1], logits, 0.0), axis=0, keepdims=True)
+        for k in range(2)
+    ]
+    first = jax.nn.sigmoid(chosen[0] - chosen[1])
+    live = lax.broadcasted_iota(jnp.int32, (1, full_len), 1) < target_ref[core]
+    gates_ref[0:1] = jnp.where(live, first, 0.0)
+    gates_ref[1:2] = jnp.where(live, 1.0 - first, 0.0)
+
+
+def slots_of(routes_ref, experts_count):
+    sents, _, full_len = routes_ref.shape
+    rows = sents * full_len
+    ids = lax.broadcasted_iota(jnp.int32, (max(8, experts_count), full_len), 0)
+    named = jnp.concatenate(
+        [
+            jnp.where((ids == routes_ref[s, 0:1]) | (ids == routes_ref[s, 1:2]), 1.0, 0.0)
+            for s in range(sents)
+        ],
+        axis=1,
+    )
+    before = lax.broadcasted_iota(jnp.int32, (rows, rows), 0) < lax.broadcasted_iota(
+        jnp.int32, (rows, rows), 1
+    )
+    earlier = jnp.dot(
+        named.astype(jnp.bfloat16),
+        jnp.where(before, 1.0, 0.0).astype(jnp.bfloat16),
+        preferred_element_type=jnp.float32,
+    )
+    return named > 0.0, earlier
+
+
+def select_kernel(core_ref, line_ref, routes_ref, own_ref, other_ref, *rest):
+    pieces, block_ref = rest[:-1], rest[-1]
+    experts_count = len(pieces)
+    full_len = own_ref.shape[0]
+    capacity = pieces[0].shape[0]
+    core = core_ref[0]
+    block_ref[part_of(core, full_len)] = own_ref[...]
+    block_ref[part_of(1 - core, full_len)] = other_ref[...]
+    named, earlier = slots_of(routes_ref, experts_count)
+    slot = jnp.where(named, earlier, -1.0)
+    ids = lax.broadcasted_iota(jnp.int32, slot.shape, 0)
+    numbers = lax.broadcasted_iota(jnp.int32, (capacity, slot.shape[1]), 0).astype(jnp.float32)
+    for offset, piece_ref in enumerate(pieces):
+        expert = lax.rem(line_ref[0] + offset, experts_count)
+        wanted = jnp.sum(jnp.where(ids == expert, slot, 0.0), axis=0, keepdims=True)
+        picks = jnp.where(numbers == wanted, 1.0, 0.0).astype(jnp.bfloat16)
+        piece_ref[...] = jnp.dot(
+            picks, block_ref[...], preferred_element_type=jnp.float32
+        ).astype(jnp.bfloat16)
+
+
+def expert_kernel(
+    core_ref, p_ref, q_ref, p2_ref, q2_ref, in_ref, out_ref, keep_ref, send_ref, rows_ref
+):
+    core = core_ref[0]
+    capacity, half = p_ref.shape
+    rows_ref[:capacity, part_of(core, half)] = p_ref[...]
+    rows_ref[capacity:, part_of(core, half)] = q_ref[...]
+    rows_ref[:capacity, part_of(1 - core, half)] = p2_ref[...]
+    rows_ref[capacity:, part_of(1 - core, half)] = q2_ref[...]
+    hidden = jnp.dot(rows_ref[...], in_ref[...], preferred_element_type=jnp.float32)
+    hidden = jnp.maximum(hidden, 0.0).astype(jnp.bfloat16)
+    send = jnp.dot(
+        hidden, out_ref[:, part_of(1 - core, half)], preferred_element_type=jnp.float32
+    ).astype(jnp.bfloat16)
+    send_ref[0] = send[:capacity]
+    send_ref[1] = send[capacity:]
+    keep = jnp.dot(hidden, out_ref[:, part_of(core, half)], preferred_element_type=jnp.float32)
+    keep_ref[0] = keep[:capacity]
+    keep_ref[1] = keep[capacity:]
+
+
+def combine_kernel(core_ref, line_ref, routes_ref, own_gates_ref, other_gates_ref, *rest):
+    pieces, (own_ref, other_ref, rows_ref, gates_ref, sum_ref) = rest[:-5], rest[-5:]
+    experts_count = len(pieces)
+    capacity, half = pieces[0].shape
+    sents, _, full_len = routes_ref.shape
+    core = core_ref[0]
+    for offset, piece_ref in enumerate(pieces):
+        rows_ref[offset * capacity : (offset + 1) * capacity] = piece_ref[...]
+    gates_ref[core] = own_gates_ref[...]
+    gates_ref[1 - core] = other_gates_ref[...]
+    _, earlier = slots_of(routes_ref, experts_count)
+    ids = lax.broadcasted_iota(jnp.int32, (earlier.shape[0], full_len), 0)
+    numbers = lax.broadcasted_iota(
+        jnp.int32, (full_len, experts_count * capacity), 1
+    ).astype(jnp.float32)
+    for sent in range(sents):
+        slots = earlier[:, sent * full_len : (sent + 1) * full_len]
+        total = None
+        for k in range(2):
+            route = routes_ref[sent, k : k + 1]
+            slot = jnp.sum(jnp.where(ids == route, slots, 0.0), axis=0, keepdims=True)
+            offset = lax.rem(route - line_ref[0] + experts_count, experts_count)
+            place = offset.astype(jnp.float32) * capacity + slot
+            place, gate = (
+                jnp.broadcast_to(row, (full_len, full_len)).T[:, :1]
+                for row in (place, gates_ref[sent, k : k + 1])
+            )
+            picks = jnp.where(numbers == place, 1.0, 0.0).astype(jnp.bfloat16)
+            term = gate * jnp.dot(picks, rows_ref[...], preferred_element_type=jnp.float32)
+            total = term if total is None else total + term
+        sum_ref[sent] = total
+    own_ref[...] = sum_ref[core]
+    other_ref[...] = sum_ref[1 - core].astype(jnp.bfloat16)
+
+
+def finish_kernel(core_ref, state_ref, own_ref, other_ref, mixed_ref):
+    core = core_ref[0]
+    half = own_ref.shape[-1]
+    for part, summed in ((core, own_ref), (1 - core, other_ref)):
+        span = part_of(part, half)
+        mixed_ref[:, span] = (
+            state_ref[:, span].astype(jnp.float32) + summed[...].astype(jnp.float32)
+        ).astype(jnp.bfloat16)
+
+
+def swap(values):
+    return lax.ppermute(values, "section", [(0, 1), (1, 0)])
+
+
+def swap_owner(values):
+    owners = lax.axis_size("expert")
+    return lax.ppermute(values, "expert", [(i, i ^ 1) for i in range(owners)])
+
+
+def shift(values, offset):
+    owners = lax.axis_size("expert")
+    return lax.ppermute(
+        values, "expert", [(i, (i + 2 * offset) % owners) for i in range(owners)]
+    )
+
+
+def attend(
+    core, decoder_states, memory_keys, memory_values, source_lengths, target_lengths, routes,
+    attn_gain, ffn_gain, router,
+):
+    full_len, width = decoder_states.shape[1:]
+    memory = jnp.stack([memory_keys, memory_values], axis=1)
+    own = lax.dynamic_index_in_dim(memory, core[0], 0, keepdims=False)
+    other = swap(lax.dynamic_index_in_dim(memory, 1 - core[0], 0, keepdims=False))
+    half = (full_len, width // 2)
+    return call(
+        attend_kernel,
+        "attend",
+        [
+            ((full_len, width), jnp.bfloat16),
+            (half, jnp.bfloat16),
+            (half, jnp.bfloat16),
+            ((2, full_len), jnp.float32),
+        ],
+        [core, source_lengths, target_lengths],
+        [
+            decoder_states[0],
+            own,
+            other,
+            attn_gain[None],
+            ffn_gain[None],
+            router.T,
+            routes,
+        ],
+        scratch=[pltpu.VMEM((full_len, width), jnp.bfloat16)],
+    )
+
+
+def line_experts(core, state, keep, send, gates, routes, fc_in, fc_out, capacity):
+    full_len, width = state.shape
+    half = width // 2
+    count = lax.axis_size("expert") // 2
+    line = (lax.axis_index("expert") // 2).astype(jnp.int32).reshape(1)
+    other = swap(send)
+    other_gates = swap(gates)
+    piece = ((capacity, half), jnp.bfloat16)
+    selected = call(
+        select_kernel,
+        "select",
+        [piece] * count,
+        [core, line],
+        [routes, keep, other],
+        scratch=[pltpu.VMEM((2 * full_len, half), jnp.bfloat16)],
+    )
+    received = [selected[0]] + [shift(selected[r], r) for r in range(1, count)]
+    home = []
+    for offset, p in enumerate(received):
+        q = swap_owner(p)
+        p2, q2 = swap(p), swap(q)
+        kept, sent = call(
+            expert_kernel,
+            "expert",
+            [((2, capacity, half), jnp.float32), ((2, capacity, half), jnp.bfloat16)],
+            [core],
+            [p, q, p2, q2, fc_in, fc_out],
+            scratch=[pltpu.VMEM((2 * capacity, width), jnp.bfloat16)],
+            vmem_mib=32,
+            cost=pl.CostEstimate(
+                flops=8 * capacity * width * fc_in.shape[1],
+                bytes_accessed=4 * width * fc_in.shape[1],
+                transcendentals=0,
+            ),
+        )
+        both = kept + swap(sent).astype(jnp.float32)
+        across = swap_owner(both[1].astype(jnp.bfloat16))
+        total = (both[0] + across.astype(jnp.float32)).astype(jnp.bfloat16)
+        home.append(shift(total, -offset) if offset else total)
+    own_sum, other_sum = call(
+        combine_kernel,
+        "combine",
+        [((full_len, half), jnp.float32), ((full_len, half), jnp.bfloat16)],
+        [core, line],
+        [routes, gates, other_gates, *home],
+        scratch=[
+            pltpu.VMEM((count * capacity, half), jnp.bfloat16),
+            pltpu.VMEM((2, 2, full_len), jnp.float32),
+            pltpu.VMEM((2, full_len, half), jnp.float32),
+        ],
+    )
+    (mixed,) = call(
+        finish_kernel,
+        "finish",
+        [((full_len, width), jnp.bfloat16)],
+        [core],
+        [state, own_sum, swap(other_sum)],
+    )
+    return mixed
 
 
 def expert_apply(slot_rows, fc_in, fc_out):
@@ -23,49 +329,14 @@
     return produced.reshape(slot_rows.shape[0], slot_rows.shape[1], width)
 
 
-def local(
-    decoder_states,
-    memory_keys,
-    memory_values,
-    source_lengths,
-    target_lengths,
-    routes,
-    attn_gain,
-    ffn_gain,
-    router,
-    fc_in,
-    fc_out,
-):
-    sents, full_len, width = decoder_states.shape
-    heads = width // HEAD_DIM
-    full_keys, full_values = (
-        lax.all_to_all(memory_keys, "section", split_axis=0, concat_axis=2, tiled=True),
-        lax.all_to_all(memory_values, "section", split_axis=0, concat_axis=2, tiled=True),
-    )
-    queries = layer_norm(decoder_states, attn_gain).reshape(sents, full_len, heads, HEAD_DIM)
-    key_heads = full_keys.reshape(sents, -1, heads, HEAD_DIM)
-    value_heads = full_values.reshape(sents, -1, heads, HEAD_DIM)
-    scores = jnp.einsum(
-        "sthd,skhd->shtk", queries, key_heads, preferred_element_type=jnp.float32
-    ) * HEAD_DIM ** (-0.5)
-    valid = jnp.arange(key_heads.shape[1], dtype=jnp.int32)[None, :] < source_lengths[:, None]
-    scores = jnp.where(valid[:, None, None, :], scores, -jnp.inf)
-    expon = jnp.exp(scores - jnp.max(scores, axis=-1, keepdims=True))
-    weights = (expon / jnp.sum(expon, axis=-1, keepdims=True)).astype(jnp.bfloat16)
-    attended = jnp.einsum(
-        "shtk,skhd->sthd", weights, value_heads, preferred_element_type=jnp.float32
-    )
-    state = (decoder_states.astype(jnp.float32) + attended.reshape(sents, full_len, width)).astype(
-        jnp.bfloat16
-    )
-    normed = layer_norm(state, ffn_gain)
-    all_normed = lax.all_gather(normed, "section", axis=0, tiled=True)
+def sparse_experts(normed, target_lengths, routes, router, fc_in, fc_out, capacity):
+    full_len, width = normed.shape
+    all_normed = lax.all_gather(normed[None], "section", axis=0, tiled=True)
     block_sents = all_normed.shape[0]
     block_rows = block_sents * full_len
     tok_rows = all_normed.reshape(block_rows, width)
     owners = lax.axis_size("expert")
     experts_count = owners // 2
-    capacity = 2 * max(1, 3 * block_rows // (2 * experts_count))
     chosen_ids = routes.reshape(block_rows, 2)
     logits = jnp.dot(tok_rows, router, preferred_element_type=jnp.float32)
     onehot = chosen_ids[:, :, None] == jnp.arange(experts_count, dtype=jnp.int32)
@@ -106,7 +377,39 @@
     weight = gates * live[:, None].astype(jnp.float32)
     contrib = jnp.sum(weight[:, :, None] * fetched, axis=1).reshape(block_sents, full_len, width)
     summed = lax.psum_scatter(contrib, "section", scatter_dimension=0, tiled=True)
-    return (state.astype(jnp.float32) + summed).astype(jnp.bfloat16)
+    return summed[0]
+
+
+def local(
+    decoder_states,
+    memory_keys,
+    memory_values,
+    source_lengths,
+    target_lengths,
+    routes,
+    attn_gain,
+    ffn_gain,
+    router,
+    fc_in,
+    fc_out,
+):
+    core = lax.axis_index("section").astype(jnp.int32).reshape(1)
+    by_choice = jnp.transpose(routes, (0, 2, 1))
+    state, keep, send, gates = attend(
+        core, decoder_states, memory_keys, memory_values, source_lengths, target_lengths, by_choice,
+        attn_gain, ffn_gain, router,
+    )
+    block_rows = routes.shape[0] * routes.shape[1]
+    experts_count = router.shape[1]
+    capacity = 2 * max(1, 3 * block_rows // (2 * experts_count))
+    if capacity % 16 == 0:
+        mixed = line_experts(core, state, keep, send, gates, by_choice, fc_in, fc_out, capacity)
+    else:
+        halves = jnp.stack([keep, send])
+        normed = jnp.concatenate([halves[core[0]], halves[1 - core[0]]], axis=-1)
+        summed = sparse_experts(normed, target_lengths, routes, router, fc_in, fc_out, capacity)
+        mixed = (state.astype(jnp.float32) + summed).astype(jnp.bfloat16)
+    return mixed[None]
 
 
 def solution(mesh):

time: 236 us -> 89.8 us (0.38)
  blocking collectives: 80.6 us -> 0 us
  waiting for transfers between devices: 76.9 us -> 46.1 us
  other arithmetic: 18.3 us -> 1.65 us
  between operations: 14.4 us -> 0.91 us
  Pallas kernels: 0 us -> 12.8 us
  local copies, waits for them, and re-layouts: 21.1 us -> 8.33 us
  matrix products: 12 us -> 0 us
  starting transfers between devices: 11.8 us -> 19.6 us
    all_to_all x1 -> x0, blocking collectives: 78.4 us -> none  [local(): lax.all_to_all(outgoing, 'expert', split_axis=0, concat_axis=0, tiled=True)]
    all_to_all x3 -> x0, waiting for transfers between devices: 69.1 us -> none  [the longest x1 69.1 us: local(): lax.all_to_all(expert_apply(lax.all_to_all(outgoing, 'expert', split_axis...]
    ppermute x0 -> x30, waiting for transfers between devices: none -> 46.1 us  [the longest x6 23.4 us: shift(): lax.ppermute(values, 'expert', [(i, (i + 2 * offset) % owners) for i in r...]
    ppermute x0 -> x30, starting transfers between devices: none -> 19.6 us  [the longest x8 9.33 us: swap_owner(): return lax.ppermute(values, 'expert', [(i, i ^ 1) for i in range(owners)])]
    pallas_call x0 -> x8, Pallas kernels: none -> 12.8 us  [call(): pl.pallas_call(kernel, out_shape=tuple((jax.ShapeDtypeStruct(*out) for ou...]
    reduce_sum x8 -> x0, other arithmetic: 12.6 us -> none  [the longest x1 5.29 us: local(): jnp.sum(weight[:, :, None] * fetched, axis=1)]
    gather x3 -> x0, local copies, waits for them, and re-layouts: 12.6 us -> none  [the longest x2 9 us: local(): partial_value.reshape(dump_index, width)]
    dot_general x4 -> x0, matrix products: 12 us -> none  [the longest x1 10.1 us: expert_apply(): produced = jnp.dot(hidden, fc_out, preferred_element_type=jnp.float32)]
  transfers between devices with their start and end apart: 4 -> 30, of which waited for: 2 -> 12; matrix products, arithmetic and copies ran while one was open for 3% -> 1% of each run, Pallas kernels for 0% -> 8%
where the time goes in v2:
time: 89.8 us; the launch traced here: 89.3 us
  waiting for transfers between devices  46.1 us (51%)
  starting transfers between devices  19.6 us (22%)
  Pallas kernels  12.8 us (14%)
  local copies, waits for them, and re-layouts  8.33 us (9%)
  other arithmetic  1.65 us (2%)
  between operations  0.91 us (1%)
    ppermute x6, waiting for transfers between devices, shift(): lax.ppermute(values, 'expert', [(i, (i + 2 * offset) % owners) for i in r...  23.4 us
    ppermute x8, waiting for transfers between devices, swap_owner(): return lax.ppermute(values, 'expert', [(i, i ^ 1) for i in range(owners)])  19.9 us
    pallas_call x8, Pallas kernels, call(): pl.pallas_call(kernel, out_shape=tuple((jax.ShapeDtypeStruct(*out) for ou...  12.8 us
    ppermute x8, starting transfers between devices, swap_owner(): return lax.ppermute(values, 'expert', [(i, i ^ 1) for i in range(owners)])  9.33 us
    unnamed x24, local copies, waits for them, and re-layouts  8.23 us
    ppermute x6, starting transfers between devices, shift(): lax.ppermute(values, 'expert', [(i, (i + 2 * offset) % owners) for i in r...  6.32 us
    ppermute x16, starting transfers between devices, swap(): return lax.ppermute(values, 'section', [(0, 1), (1, 0)])  3.91 us
    ppermute x16, waiting for transfers between devices, swap(): return lax.ppermute(values, 'section', [(0, 1), (1, 0)])  2.73 us
  transfers between devices with their start and end apart: 30, of which 12 were waited for; matrix products, arithmetic and copies ran while one was open for 1% of the time, Pallas kernels for 8%

profile of v2, /device:TPU:0, one launch (start us, length us, event | category | flops | bytes accessed | tf_op | source)
XLA Modules:
  0.0 89.3 jit_solution(999578047539238803)
XLA Ops:
  0.0 1.0 %fusion.13 = (bf16[2,80,512]{2,1,0:T(8,128)(2,1)S(1)}, bf16[2,80,512]{2,1,0:T(8,128)(2,1)S(1)}) fusion(s32[]{:T(128)S(6)} %select_n.13, bf16[2,1,80,512]{3,2,0,1:T(8,128)(2,1)} %bitcast.53, bf16[2,1,80,512]{3,2,0,1:T(8,128)(2,1)} %bitcast.54, s32[]{:T(128)S(6)} %select_n.12), kind=kLoop, calls=%fused_computation.29 | loop fusion | flops 163840 | bytes 655368 | tf_op jit(solution)/shard_map/jit(dynamic_index_in_dim)/squeeze | solution.py:236
  1.0 0.5 collective-permute-start
  2.2 0.4 collective-permute-done.other_ref
  2.6 0.9 %copy-done = bf16[1,128,1024]{2,1,0:T(8,128)(2,1)S(1)} copy-done((bf16[1,128,1024]{2,1,0:T(8,128)(2,1)S(1)}, bf16[1,128,1024]{2,1,0:T(8,128)(2,1)}, u32[]{:S(2)}) %copy-start) | copy-done | bytes 262168
  3.5 0.7 copy-done.1
  4.2 0.7 copy-done.4
  4.9 0.7 copy-done.5
  5.6 0.7 copy-done.6
  6.3 0.7 copy-done.7
  6.9 3.2 %attend.1 = (bf16[128,1024]{1,0:T(8,128)(2,1)S(1)}, bf16[128,512]{1,0:T(8,128)(2,1)S(1)}, bf16[128,512]{1,0:T(8,128)(2,1)S(1)}, f32[2,128]{1,0:T(2,128)S(1)}) custom-call(s32[1]{0:T(128)} %bitcast.core_ref, s32[1]{0:T(128)S(6)} %copy.12.source_ref, s32[2]{0:T(128)S(1)} %copy-done.7, bf16[128,1024]{1,0:T(8,128)(2,1)S(1)} %bitcast.46, ...), custom_call_target="tpu_custom_call" | custom-call | tf_op jit(solution)/shard_map/attend/pallas_call | solution.py:24
  10.2 0.4 collective-permute-start.2
  10.6 1.0 %collective-permute-done.2.other_ref = bf16[128,512]{1,0:T(8,128)(2,1)S(1)} collective-permute-done((bf16[128,512]{1,0:T(8,128)(2,1)S(1)}, bf16[128,512]{1,0:T(8,128)(2,1)S(1)}, u32[]{:S(2)}, u32[]{:S(2)}) %collective-permute-start.2) | collective-permute-done | bytes 131104 | tf_op jit(solution)/shard_map/ppermute | solution.py:214
  11.6 0.7 copy-done.2
  12.3 0.5 select.5
  12.8 5.0 %collective-permute-start.22 = (bf16[192,512]{1,0:T(8,128)(2,1)S(1)}, bf16[192,512]{1,0:T(8,128)(2,1)S(1)}, u32[]{:S(2)}, u32[]{:S(2)}) collective-permute-start(bf16[192,512]{1,0:T(8,128)(2,1)S(1)} %get-tuple-element.36), channel_id=1, source_target_pairs={{0,12},{2,14},{4,0},{6,2},{8,4},{10,6},{12,8},{14,10},{1,13},{3,15... | collective-permute-start | bytes 589832 | tf_op jit(solution)/shard_map/ppermute | solution.py:224
  17.8 0.0 collective-permute-start.15
  17.8 1.5 %collective-permute-start.3 = (bf16[192,512]{1,0:T(8,128)(2,1)S(1)}, bf16[192,512]{1,0:T(8,128)(2,1)S(1)}, u32[]{:S(2)}, u32[]{:S(2)}) collective-permute-start(bf16[192,512]{1,0:T(8,128)(2,1)S(1)} %get-tuple-element.27.p_ref), channel_id=1, source_target_pairs={{0,2},{2,0},{4,6},{6,4},{8,10},{10,8},{12,14},{14,12},{1,3},{3,1},... | collective-permute-start | bytes 589832 | tf_op jit(solution)/shard_map/ppermute | solution.py:219
  19.3 1.0 %collective-permute-start.8 = (bf16[192,512]{1,0:T(8,128)(2,1)S(1)}, bf16[192,512]{1,0:T(8,128)(2,1)S(1)}, u32[]{:S(2)}, u32[]{:S(2)}) collective-permute-start(bf16[192,512]{1,0:T(8,128)(2,1)S(1)} %get-tuple-element.30), channel_id=1, source_target_pairs={{0,4},{2,6},{4,8},{6,10},{8,12},{10,14},{12,0},{14,2},{1,5},{3,7},... | collective-permute-start | bytes 589832 | tf_op jit(solution)/shard_map/ppermute | solution.py:224
  20.3 0.0 collective-permute-start.4
  20.3 2.8 %collective-permute-done.22.p_ref = bf16[192,512]{1,0:T(8,128)(2,1)S(1)} collective-permute-done((bf16[192,512]{1,0:T(8,128)(2,1)S(1)}, bf16[192,512]{1,0:T(8,128)(2,1)S(1)}, u32[]{:S(2)}, u32[]{:S(2)}) %collective-permute-start.22) | collective-permute-done | bytes 196640 | tf_op jit(solution)/shard_map/ppermute | solution.py:224
  23.2 1.5 %collective-permute-start.23 = (bf16[192,512]{1,0:T(8,128)(2,1)S(1)}, bf16[192,512]{1,0:T(8,128)(2,1)S(1)}, u32[]{:S(2)}, u32[]{:S(2)}) collective-permute-start(bf16[192,512]{1,0:T(8,128)(2,1)S(1)} %collective-permute-done.22.p_ref), channel_id=1, source_target_pairs={{0,2},{2,0},{4,6},{6,4},{8,10},{10,8},{12,14},{14,12},{1,3},{3,1},... | collective-permute-start | bytes 589832 | tf_op jit(solution)/shard_map/ppermute | solution.py:219
  24.7 10.2 %collective-permute-done.15.p_ref = bf16[192,512]{1,0:T(8,128)(2,1)S(1)} collective-permute-done((bf16[192,512]{1,0:T(8,128)(2,1)S(1)}, bf16[192,512]{1,0:T(8,128)(2,1)S(1)}, u32[]{:S(2)}, u32[]{:S(2)}) %collective-permute-start.15) | collective-permute-done | bytes 196640 | tf_op jit(solution)/shard_map/ppermute | solution.py:224
  34.8 1.5 %collective-permute-start.16 = (bf16[192,512]{1,0:T(8,128)(2,1)S(1)}, bf16[192,512]{1,0:T(8,128)(2,1)S(1)}, u32[]{:S(2)}, u32[]{:S(2)}) collective-permute-start(bf16[192,512]{1,0:T(8,128)(2,1)S(1)} %collective-permute-done.15.p_ref), channel_id=1, source_target_pairs={{0,2},{2,0},{4,6},{6,4},{8,10},{10,8},{12,14},{14,12},{1,3},{3,1},... | collective-permute-start | bytes 589832 | tf_op jit(solution)/shard_map/ppermute | solution.py:219
  36.3 0.0 collective-permute-done.3.q_ref
  36.3 0.5 collective-permute-start.24
  36.9 0.5 collective-permute-start.9
  37.4 5.0 %collective-permute-done.16.q_ref = bf16[192,512]{1,0:T(8,128)(2,1)S(1)} collective-permute-done((bf16[192,512]{1,0:T(8,128)(2,1)S(1)}, bf16[192,512]{1,0:T(8,128)(2,1)S(1)}, u32[]{:S(2)}, u32[]{:S(2)}) %collective-permute-start.16) | collective-permute-done | bytes 196640 | tf_op jit(solution)/shard_map/ppermute | solution.py:219
  42.4 0.5 collective-permute-start.18
  42.9 1.6 %copy-done.8 = bf16[1024,1024]{1,0:T(8,128)(2,1)S(1)} copy-done((bf16[1024,1024]{1,0:T(8,128)(2,1)S(1)}, bf16[1024,1024]{1,0:T(8,128)(2,1)}, u32[]{:S(2)}) %copy-start.8) | copy-done | bytes 2097176
  44.5 1.6 %copy-done.10 = bf16[1024,1024]{1,0:T(8,128)(2,1)S(1)} copy-done((bf16[1024,1024]{1,0:T(8,128)(2,1)S(1)}, bf16[1024,1024]{1,0:T(8,128)(2,1)}, u32[]{:S(2)}) %copy-start.10) | copy-done | bytes 2097176
  46.1 1.8 %expert.4 = (f32[2,192,512]{2,1,0:T(8,128)S(1)}, bf16[2,192,512]{2,1,0:T(8,128)(2,1)S(1)}) custom-call(s32[1]{0:T(128)} %bitcast.core_ref, bf16[192,512]{1,0:T(8,128)(2,1)S(1)} %get-tuple-element.27.p_ref, bf16[192,512]{1,0:T(8,128)(2,1)S(1)} %collective-permute-done.3.q_ref, bf16[192,512]{1,0:T(8,128)(2,1)S(1)} %collective-permute-done.4.p2_ref, ...), custom_call_target="tpu_custom_call" | custom-call | flops 1610612736 | bytes 4194304 | tf_op jit(solution)/shard_map/expert/pallas_call | solution.py:24
  48.0 0.1 collective-permute-start.10
  48.1 0.5 collective-permute-start.6
  48.6 0.1 collective-permute-start.11
  48.6 1.8 %expert.7 = (f32[2,192,512]{2,1,0:T(8,128)S(1)}, bf16[2,192,512]{2,1,0:T(8,128)(2,1)S(1)}) custom-call(s32[1]{0:T(128)} %bitcast.core_ref, bf16[192,512]{1,0:T(8,128)(2,1)S(1)} %collective-permute-done.22.p_ref, bf16[192,512]{1,0:T(8,128)(2,1)S(1)} %collective-permute-done.23.q_ref, bf16[192,512]{1,0:T(8,128)(2,1)S(1)} %collective-permute-done.24.p2_ref, ...), custom_call_target="tpu_custom_call" | custom-call | flops 1610612736 | bytes 4194304 | tf_op jit(solution)/shard_map/expert/pallas_call | solution.py:24
  50.5 0.5 collective-permute-start.1
  51.0 0.1 collective-permute-start.26
  51.1 1.8 %expert.6 = (f32[2,192,512]{2,1,0:T(8,128)S(1)}, bf16[2,192,512]{2,1,0:T(8,128)(2,1)S(1)}) custom-call(s32[1]{0:T(128)} %bitcast.core_ref, bf16[192,512]{1,0:T(8,128)(2,1)S(1)} %collective-permute-done.15.p_ref, bf16[192,512]{1,0:T(8,128)(2,1)S(1)} %collective-permute-done.16.q_ref, bf16[192,512]{1,0:T(8,128)(2,1)S(1)} %collective-permute-done.17.p2_ref, ...), custom_call_target="tpu_custom_call" | custom-call | flops 1610612736 | bytes 4194304 | tf_op jit(solution)/shard_map/expert/pallas_call | solution.py:24
  52.9 0.5 collective-permute-start.19
  53.4 1.8 %expert.5 = (f32[2,192,512]{2,1,0:T(8,128)S(1)}, bf16[2,192,512]{2,1,0:T(8,128)(2,1)S(1)}) custom-call(s32[1]{0:T(128)} %bitcast.core_ref, bf16[192,512]{1,0:T(8,128)(2,1)S(1)} %collective-permute-done.8.p_ref, bf16[192,512]{1,0:T(8,128)(2,1)S(1)} %collective-permute-done.9.q_ref, bf16[192,512]{1,0:T(8,128)(2,1)S(1)} %collective-permute-done.10.p2_ref, ...), custom_call_target="tpu_custom_call" | custom-call | flops 1610612736 | bytes 4194304 | tf_op jit(solution)/shard_map/expert/pallas_call | solution.py:24
  55.3 0.1 collective-permute-start.12
  55.4 0.1 convert_add_fusion.3
  55.6 1.8 %collective-permute-start.7 = (bf16[192,512]{1,0:T(8,128)(2,1)S(1)}, bf16[192,512]{1,0:T(8,128)(2,1)S(1)}, u32[]{:S(2)}, u32[]{:S(2)}) collective-permute-start(bf16[192,512]{1,0:T(8,128)(2,1)S(1)} %fusion.8), channel_id=1, source_target_pairs={{0,2},{2,0},{4,6},{6,4},{8,10},{10,8},{12,14},{14,12},{1,3},{3,1},... | collective-permute-start | bytes 589832 | tf_op jit(solution)/shard_map/ppermute | solution.py:219
  57.4 0.1 convert_add_fusion
  57.6 0.3 collective-permute-start.27
  57.9 0.1 convert_add_fusion.1
  58.1 1.8 %collective-permute-start.20 = (bf16[192,512]{1,0:T(8,128)(2,1)S(1)}, bf16[192,512]{1,0:T(8,128)(2,1)S(1)}, u32[]{:S(2)}, u32[]{:S(2)}) collective-permute-start(bf16[192,512]{1,0:T(8,128)(2,1)S(1)} %fusion.10), channel_id=1, source_target_pairs={{0,2},{2,0},{4,6},{6,4},{8,10},{10,8},{12,14},{14,12},{1,3},{3,1},... | collective-permute-start | bytes 589832 | tf_op jit(solution)/shard_map/ppermute | solution.py:219
  59.9 0.1 convert_add_fusion.2
  60.0 0.0 copy-start.3
  60.1 0.3 collective-permute-start.13
  60.4 7.2 %collective-permute-done.27 = bf16[192,512]{1,0:T(8,128)(2,1)S(1)} collective-permute-done((bf16[192,512]{1,0:T(8,128)(2,1)S(1)}, bf16[192,512]{1,0:T(8,128)(2,1)S(1)}, u32[]{:S(2)}, u32[]{:S(2)}) %collective-permute-start.27) | collective-permute-done | bytes 196640 | tf_op jit(solution)/shard_map/ppermute | solution.py:219
  67.6 0.1 fusion.1
  67.6 0.1 collective-permute-start.28
  67.7 4.1 %collective-permute-done.20 = bf16[192,512]{1,0:T(8,128)(2,1)S(1)} collective-permute-done((bf16[192,512]{1,0:T(8,128)(2,1)S(1)}, bf16[192,512]{1,0:T(8,128)(2,1)S(1)}, u32[]{:S(2)}, u32[]{:S(2)}) %collective-permute-start.20) | collective-permute-done | bytes 196640 | tf_op jit(solution)/shard_map/ppermute | solution.py:219
  71.8 0.1 collective-permute-start.21
  71.9 3.6 %collective-permute-done.13 = bf16[192,512]{1,0:T(8,128)(2,1)S(1)} collective-permute-done((bf16[192,512]{1,0:T(8,128)(2,1)S(1)}, bf16[192,512]{1,0:T(8,128)(2,1)S(1)}, u32[]{:S(2)}, u32[]{:S(2)}) %collective-permute-start.13) | collective-permute-done | bytes 196640 | tf_op jit(solution)/shard_map/ppermute | solution.py:219
  75.6 0.2 collective-permute-start.14
  75.8 1.6 %collective-permute-done.28.rest_3_ = bf16[192,512]{1,0:T(8,128)(2,1)S(1)} collective-permute-done((bf16[192,512]{1,0:T(8,128)(2,1)S(1)}, bf16[192,512]{1,0:T(8,128)(2,1)S(1)}, u32[]{:S(2)}, u32[]{:S(2)}) %collective-permute-start.28) | collective-permute-done | bytes 196640 | tf_op jit(solution)/shard_map/ppermute | solution.py:224
  77.4 6.6 %collective-permute-done.21.rest_2_ = bf16[192,512]{1,0:T(8,128)(2,1)S(1)} collective-permute-done((bf16[192,512]{1,0:T(8,128)(2,1)S(1)}, bf16[192,512]{1,0:T(8,128)(2,1)S(1)}, u32[]{:S(2)}, u32[]{:S(2)}) %collective-permute-start.21) | collective-permute-done | bytes 196640 | tf_op jit(solution)/shard_map/ppermute | solution.py:224
  84.1 2.2 %collective-permute-done.14.rest_1_ = bf16[192,512]{1,0:T(8,128)(2,1)S(1)} collective-permute-done((bf16[192,512]{1,0:T(8,128)(2,1)S(1)}, bf16[192,512]{1,0:T(8,128)(2,1)S(1)}, u32[]{:S(2)}, u32[]{:S(2)}) %collective-permute-start.14) | collective-permute-done | bytes 196640 | tf_op jit(solution)/shard_map/ppermute | solution.py:224
  86.2 0.9 %combine.1 = (f32[128,512]{1,0:T(8,128)S(1)}, bf16[128,512]{1,0:T(8,128)(2,1)S(1)}) custom-call(s32[1]{0:T(128)} %bitcast.core_ref, s32[1]{0:T(128)} %bitcast.10.line_ref, s32[2,2,128]{2,1,0:T(2,128)S(1)} %bitcast.49, f32[2,128]{1,0:T(2,128)S(1)} %get-tuple-element.24.own_gates_ref, f32[2,128]{1,0:T(2,128)S(1)} %collective-permute-done.1.other_gates_ref, ...), custom_call_target="tpu_custom_call" | custom-call | tf_op jit(solution)/shard_map/combine/pallas_call | solution.py:24
  87.2 0.1 collective-permute-start.29
  87.2 1.3 %collective-permute-done.29.other_ref = bf16[128,512]{1,0:T(8,128)(2,1)S(1)} collective-permute-done((bf16[128,512]{1,0:T(8,128)(2,1)S(1)}, bf16[128,512]{1,0:T(8,128)(2,1)S(1)}, u32[]{:S(2)}, u32[]{:S(2)}) %collective-permute-start.29) | collective-permute-done | bytes 131104 | tf_op jit(solution)/shard_map/ppermute | solution.py:214
  88.6 0.8 finish.1
  (41 shorter events, 0.3 us)
Async XLA Ops:
  1.0 1.5 %collective-permute-start = (bf16[2,80,512]{2,1,0:T(8,128)(2,1)S(1)}, bf16[2,80,512]{2,1,0:T(8,128)(2,1)S(1)}, u32[]{:S(2)}, u32[]{:S(2)}) collective-permute-start(bf16[2,80,512]{2,1,0:T(8,128)(2,1)S(1)} %get-tuple-element.41), channel_id=1, source_target_pairs={{0,1},{1,0},{2,3},{3,2},{4,5},{5,4},{6,7},{7,6},{8,9},{9,8},{10,11... | collective-permute-start | bytes 491528 | tf_op jit(solution)/shard_map/ppermute | solution.py:214
  2.6 0.9 %copy-start = (bf16[1,128,1024]{2,1,0:T(8,128)(2,1)S(1)}, bf16[1,128,1024]{2,1,0:T(8,128)(2,1)}, u32[]{:S(2)}) copy-start(bf16[1,128,1024]{2,1,0:T(8,128)(2,1)} %param.11) | copy-start | bytes 786436
  3.5 0.7 copy-start.1
  4.2 0.7 copy-start.4
  4.9 0.7 copy-start.5
  5.6 0.7 copy-start.6
  6.3 0.7 copy-start.7
  10.2 1.4 %collective-permute-start.2 = (bf16[128,512]{1,0:T(8,128)(2,1)S(1)}, bf16[128,512]{1,0:T(8,128)(2,1)S(1)}, u32[]{:S(2)}, u32[]{:S(2)}) collective-permute-start(bf16[128,512]{1,0:T(8,128)(2,1)S(1)} %get-tuple-element.26), channel_id=1, source_target_pairs={{0,1},{1,0},{2,3},{3,2},{4,5},{5,4},{6,7},{7,6},{8,9},{9,8},{10,11... | collective-permute-start | bytes 393224 | tf_op jit(solution)/shard_map/ppermute | solution.py:214
  11.6 0.7 copy-start.2
  12.8 10.4 %collective-permute-start.22 = (bf16[192,512]{1,0:T(8,128)(2,1)S(1)}, bf16[192,512]{1,0:T(8,128)(2,1)S(1)}, u32[]{:S(2)}, u32[]{:S(2)}) collective-permute-start(bf16[192,512]{1,0:T(8,128)(2,1)S(1)} %get-tuple-element.36), channel_id=1, source_target_pairs={{0,12},{2,14},{4,0},{6,2},{8,4},{10,6},{12,8},{14,10},{1,13},{3,15... | collective-permute-start | bytes 589832 | tf_op jit(solution)/shard_map/ppermute | solution.py:224
  17.8 17.0 %collective-permute-start.15 = (bf16[192,512]{1,0:T(8,128)(2,1)S(1)}, bf16[192,512]{1,0:T(8,128)(2,1)S(1)}, u32[]{:S(2)}, u32[]{:S(2)}) collective-permute-start(bf16[192,512]{1,0:T(8,128)(2,1)S(1)} %get-tuple-element.33), channel_id=1, source_target_pairs={{0,8},{2,10},{4,12},{6,14},{8,0},{10,2},{12,4},{14,6},{1,9},{3,11}... | collective-permute-start | bytes 589832 | tf_op jit(solution)/shard_map/ppermute | solution.py:224
  17.8 18.5 %collective-permute-start.3 = (bf16[192,512]{1,0:T(8,128)(2,1)S(1)}, bf16[192,512]{1,0:T(8,128)(2,1)S(1)}, u32[]{:S(2)}, u32[]{:S(2)}) collective-permute-start(bf16[192,512]{1,0:T(8,128)(2,1)S(1)} %get-tuple-element.27.p_ref), channel_id=1, source_target_pairs={{0,2},{2,0},{4,6},{6,4},{8,10},{10,8},{12,14},{14,12},{1,3},{3,1},... | collective-permute-start | bytes 589832 | tf_op jit(solution)/shard_map/ppermute | solution.py:219
  19.3 17.0 %collective-permute-start.8 = (bf16[192,512]{1,0:T(8,128)(2,1)S(1)}, bf16[192,512]{1,0:T(8,128)(2,1)S(1)}, u32[]{:S(2)}, u32[]{:S(2)}) collective-permute-start(bf16[192,512]{1,0:T(8,128)(2,1)S(1)} %get-tuple-element.30), channel_id=1, source_target_pairs={{0,4},{2,6},{4,8},{6,10},{8,12},{10,14},{12,0},{14,2},{1,5},{3,7},... | collective-permute-start | bytes 589832 | tf_op jit(solution)/shard_map/ppermute | solution.py:224
  20.3 16.5 %collective-permute-start.4 = (bf16[192,512]{1,0:T(8,128)(2,1)S(1)}, bf16[192,512]{1,0:T(8,128)(2,1)S(1)}, u32[]{:S(2)}, u32[]{:S(2)}) collective-permute-start(bf16[192,512]{1,0:T(8,128)(2,1)S(1)} %get-tuple-element.27.p_ref), channel_id=1, source_target_pairs={{0,1},{1,0},{2,3},{3,2},{4,5},{5,4},{6,7},{7,6},{8,9},{9,8},{10,11... | collective-permute-start | bytes 589832 | tf_op jit(solution)/shard_map/ppermute | solution.py:214
  23.2 14.2 %collective-permute-start.23 = (bf16[192,512]{1,0:T(8,128)(2,1)S(1)}, bf16[192,512]{1,0:T(8,128)(2,1)S(1)}, u32[]{:S(2)}, u32[]{:S(2)}) collective-permute-start(bf16[192,512]{1,0:T(8,128)(2,1)S(1)} %collective-permute-done.22.p_ref), channel_id=1, source_target_pairs={{0,2},{2,0},{4,6},{6,4},{8,10},{10,8},{12,14},{14,12},{1,3},{3,1},... | collective-permute-start | bytes 589832 | tf_op jit(solution)/shard_map/ppermute | solution.py:219
  34.8 7.6 %collective-permute-start.16 = (bf16[192,512]{1,0:T(8,128)(2,1)S(1)}, bf16[192,512]{1,0:T(8,128)(2,1)S(1)}, u32[]{:S(2)}, u32[]{:S(2)}) collective-permute-start(bf16[192,512]{1,0:T(8,128)(2,1)S(1)} %collective-permute-done.15.p_ref), channel_id=1, source_target_pairs={{0,2},{2,0},{4,6},{6,4},{8,10},{10,8},{12,14},{14,12},{1,3},{3,1},... | collective-permute-start | bytes 589832 | tf_op jit(solution)/shard_map/ppermute | solution.py:219
  36.3 6.1 %collective-permute-start.5 = (bf16[192,512]{1,0:T(8,128)(2,1)S(1)}, bf16[192,512]{1,0:T(8,128)(2,1)S(1)}, u32[]{:S(2)}, u32[]{:S(2)}) collective-permute-start(bf16[192,512]{1,0:T(8,128)(2,1)S(1)} %collective-permute-done.3.q_ref), channel_id=1, source_target_pairs={{0,1},{1,0},{2,3},{3,2},{4,5},{5,4},{6,7},{7,6},{8,9},{9,8},{10,11... | collective-permute-start | bytes 589832 | tf_op jit(solution)/shard_map/ppermute | solution.py:214
  36.3 11.6 %collective-permute-start.24 = (bf16[192,512]{1,0:T(8,128)(2,1)S(1)}, bf16[192,512]{1,0:T(8,128)(2,1)S(1)}, u32[]{:S(2)}, u32[]{:S(2)}) collective-permute-start(bf16[192,512]{1,0:T(8,128)(2,1)S(1)} %collective-permute-done.22.p_ref), channel_id=1, source_target_pairs={{0,1},{1,0},{2,3},{3,2},{4,5},{5,4},{6,7},{7,6},{8,9},{9,8},{10,11... | collective-permute-start | bytes 589832 | tf_op jit(solution)/shard_map/ppermute | solution.py:214
  36.9 11.2 %collective-permute-start.9 = (bf16[192,512]{1,0:T(8,128)(2,1)S(1)}, bf16[192,512]{1,0:T(8,128)(2,1)S(1)}, u32[]{:S(2)}, u32[]{:S(2)}) collective-permute-start(bf16[192,512]{1,0:T(8,128)(2,1)S(1)} %collective-permute-done.8.p_ref), channel_id=1, source_target_pairs={{0,2},{2,0},{4,6},{6,4},{8,10},{10,8},{12,14},{14,12},{1,3},{3,1},... | collective-permute-start | bytes 589832 | tf_op jit(solution)/shard_map/ppermute | solution.py:219
  37.4 11.2 %collective-permute-start.25 = (bf16[192,512]{1,0:T(8,128)(2,1)S(1)}, bf16[192,512]{1,0:T(8,128)(2,1)S(1)}, u32[]{:S(2)}, u32[]{:S(2)}) collective-permute-start(bf16[192,512]{1,0:T(8,128)(2,1)S(1)} %collective-permute-done.23.q_ref), channel_id=1, source_target_pairs={{0,1},{1,0},{2,3},{3,2},{4,5},{5,4},{6,7},{7,6},{8,9},{9,8},{10,11... | collective-permute-start | bytes 589832 | tf_op jit(solution)/shard_map/ppermute | solution.py:214
  42.4 8.1 %collective-permute-start.17 = (bf16[192,512]{1,0:T(8,128)(2,1)S(1)}, bf16[192,512]{1,0:T(8,128)(2,1)S(1)}, u32[]{:S(2)}, u32[]{:S(2)}) collective-permute-start(bf16[192,512]{1,0:T(8,128)(2,1)S(1)} %collective-permute-done.15.p_ref), channel_id=1, source_target_pairs={{0,1},{1,0},{2,3},{3,2},{4,5},{5,4},{6,7},{7,6},{8,9},{9,8},{10,11... | collective-permute-start | bytes 589832 | tf_op jit(solution)/shard_map/ppermute | solution.py:214
  42.4 8.6 %collective-permute-start.18 = (bf16[192,512]{1,0:T(8,128)(2,1)S(1)}, bf16[192,512]{1,0:T(8,128)(2,1)S(1)}, u32[]{:S(2)}, u32[]{:S(2)}) collective-permute-start(bf16[192,512]{1,0:T(8,128)(2,1)S(1)} %collective-permute-done.16.q_ref), channel_id=1, source_target_pairs={{0,1},{1,0},{2,3},{3,2},{4,5},{5,4},{6,7},{7,6},{8,9},{9,8},{10,11... | collective-permute-start | bytes 589832 | tf_op jit(solution)/shard_map/ppermute | solution.py:214
  42.9 1.6 %copy-start.8 = (bf16[1024,1024]{1,0:T(8,128)(2,1)S(1)}, bf16[1024,1024]{1,0:T(8,128)(2,1)}, u32[]{:S(2)}) copy-start(bf16[1024,1024]{1,0:T(8,128)(2,1)} %in_ref.7) | copy-start | bytes 6291460
  44.5 1.6 %copy-start.10 = (bf16[1024,1024]{1,0:T(8,128)(2,1)S(1)}, bf16[1024,1024]{1,0:T(8,128)(2,1)}, u32[]{:S(2)}) copy-start(bf16[1024,1024]{1,0:T(8,128)(2,1)} %out_ref.7) | copy-start | bytes 6291460
  46.1 2.5 %copy-start.9 = (bf16[1024,1024]{1,0:T(8,128)(2,1)S(1)}, bf16[1024,1024]{1,0:T(8,128)(2,1)}, u32[]{:S(2)}) copy-start(bf16[1024,1024]{1,0:T(8,128)(2,1)} %in_ref.7) | copy-start | bytes 6291460
  46.1 2.5 %copy-start.11 = (bf16[1024,1024]{1,0:T(8,128)(2,1)S(1)}, bf16[1024,1024]{1,0:T(8,128)(2,1)}, u32[]{:S(2)}) copy-start(bf16[1024,1024]{1,0:T(8,128)(2,1)} %out_ref.7) | copy-start | bytes 6291460
  48.0 5.0 %collective-permute-start.10 = (bf16[192,512]{1,0:T(8,128)(2,1)S(1)}, bf16[192,512]{1,0:T(8,128)(2,1)S(1)}, u32[]{:S(2)}, u32[]{:S(2)}) collective-permute-start(bf16[192,512]{1,0:T(8,128)(2,1)S(1)} %collective-permute-done.8.p_ref), channel_id=1, source_target_pairs={{0,1},{1,0},{2,3},{3,2},{4,5},{5,4},{6,7},{7,6},{8,9},{9,8},{10,11... | collective-permute-start | bytes 589832 | tf_op jit(solution)/shard_map/ppermute | solution.py:214
  48.1 7.4 %collective-permute-start.6 = (bf16[2,192,512]{2,1,0:T(8,128)(2,1)S(1)}, bf16[2,192,512]{2,1,0:T(8,128)(2,1)S(1)}, u32[]{:S(2)}, u32[]{:S(2)}) collective-permute-start(bf16[2,192,512]{2,1,0:T(8,128)(2,1)S(1)} %get-tuple-element.29), channel_id=1, source_target_pairs={{0,1},{1,0},{2,3},{3,2},{4,5},{5,4},{6,7},{7,6},{8,9},{9,8},{10,11... | collective-permute-start | bytes 1179656 | tf_op jit(solution)/shard_map/ppermute | solution.py:214
  48.6 4.9 %collective-permute-start.11 = (bf16[192,512]{1,0:T(8,128)(2,1)S(1)}, bf16[192,512]{1,0:T(8,128)(2,1)S(1)}, u32[]{:S(2)}, u32[]{:S(2)}) collective-permute-start(bf16[192,512]{1,0:T(8,128)(2,1)S(1)} %collective-permute-done.9.q_ref), channel_id=1, source_target_pairs={{0,1},{1,0},{2,3},{3,2},{4,5},{5,4},{6,7},{7,6},{8,9},{9,8},{10,11... | collective-permute-start | bytes 589832 | tf_op jit(solution)/shard_map/ppermute | solution.py:214
  50.5 25.3 %collective-permute-start.1 = (f32[2,128]{1,0:T(2,128)S(1)}, f32[2,128]{1,0:T(2,128)S(1)}, u32[]{:S(2)}, u32[]{:S(2)}) collective-permute-start(f32[2,128]{1,0:T(2,128)S(1)} %get-tuple-element.24.own_gates_ref), channel_id=1, source_target_pairs={{0,1},{1,0},{2,3},{3,2},{4,5},{5,4},{6,7},{7,6},{8,9},{9,8},{10,11... | collective-permute-start | bytes 3080 | tf_op jit(solution)/shard_map/ppermute | solution.py:214
  51.0 6.4 %collective-permute-start.26 = (bf16[2,192,512]{2,1,0:T(8,128)(2,1)S(1)}, bf16[2,192,512]{2,1,0:T(8,128)(2,1)S(1)}, u32[]{:S(2)}, u32[]{:S(2)}) collective-permute-start(bf16[2,192,512]{2,1,0:T(8,128)(2,1)S(1)} %get-tuple-element.38), channel_id=1, source_target_pairs={{0,1},{1,0},{2,3},{3,2},{4,5},{5,4},{6,7},{7,6},{8,9},{9,8},{10,11... | collective-permute-start | bytes 1179656 | tf_op jit(solution)/shard_map/ppermute | solution.py:214
  52.9 5.0 %collective-permute-start.19 = (bf16[2,192,512]{2,1,0:T(8,128)(2,1)S(1)}, bf16[2,192,512]{2,1,0:T(8,128)(2,1)S(1)}, u32[]{:S(2)}, u32[]{:S(2)}) collective-permute-start(bf16[2,192,512]{2,1,0:T(8,128)(2,1)S(1)} %get-tuple-element.35), channel_id=1, source_target_pairs={{0,1},{1,0},{2,3},{3,2},{4,5},{5,4},{6,7},{7,6},{8,9},{9,8},{10,11... | collective-permute-start | bytes 1179656 | tf_op jit(solution)/shard_map/ppermute | solution.py:214
  55.3 4.6 %collective-permute-start.12 = (bf16[2,192,512]{2,1,0:T(8,128)(2,1)S(1)}, bf16[2,192,512]{2,1,0:T(8,128)(2,1)S(1)}, u32[]{:S(2)}, u32[]{:S(2)}) collective-permute-start(bf16[2,192,512]{2,1,0:T(8,128)(2,1)S(1)} %get-tuple-element.32), channel_id=1, source_target_pairs={{0,1},{1,0},{2,3},{3,2},{4,5},{5,4},{6,7},{7,6},{8,9},{9,8},{10,11... | collective-permute-start | bytes 1179656 | tf_op jit(solution)/shard_map/ppermute | solution.py:214
  55.6 20.2 %collective-permute-start.7 = (bf16[192,512]{1,0:T(8,128)(2,1)S(1)}, bf16[192,512]{1,0:T(8,128)(2,1)S(1)}, u32[]{:S(2)}, u32[]{:S(2)}) collective-permute-start(bf16[192,512]{1,0:T(8,128)(2,1)S(1)} %fusion.8), channel_id=1, source_target_pairs={{0,2},{2,0},{4,6},{6,4},{8,10},{10,8},{12,14},{14,12},{1,3},{3,1},... | collective-permute-start | bytes 589832 | tf_op jit(solution)/shard_map/ppermute | solution.py:219
  57.6 10.0 %collective-permute-start.27 = (bf16[192,512]{1,0:T(8,128)(2,1)S(1)}, bf16[192,512]{1,0:T(8,128)(2,1)S(1)}, u32[]{:S(2)}, u32[]{:S(2)}) collective-permute-start(bf16[192,512]{1,0:T(8,128)(2,1)S(1)} %fusion.11), channel_id=1, source_target_pairs={{0,2},{2,0},{4,6},{6,4},{8,10},{10,8},{12,14},{14,12},{1,3},{3,1},... | collective-permute-start | bytes 589832 | tf_op jit(solution)/shard_map/ppermute | solution.py:219
  58.1 13.7 %collective-permute-start.20 = (bf16[192,512]{1,0:T(8,128)(2,1)S(1)}, bf16[192,512]{1,0:T(8,128)(2,1)S(1)}, u32[]{:S(2)}, u32[]{:S(2)}) collective-permute-start(bf16[192,512]{1,0:T(8,128)(2,1)S(1)} %fusion.10), channel_id=1, source_target_pairs={{0,2},{2,0},{4,6},{6,4},{8,10},{10,8},{12,14},{14,12},{1,3},{3,1},... | collective-permute-start | bytes 589832 | tf_op jit(solution)/shard_map/ppermute | solution.py:219
  60.0 26.2 %copy-start.3 = (s32[2,128,2]{1,2,0:T(2,128)S(1)}, s32[2,128,2]{1,2,0:T(2,128)}, u32[]{:S(2)}) copy-start(s32[2,128,2]{1,2,0:T(2,128)} %param.16) | copy-start | bytes 6148
  60.1 15.5 %collective-permute-start.13 = (bf16[192,512]{1,0:T(8,128)(2,1)S(1)}, bf16[192,512]{1,0:T(8,128)(2,1)S(1)}, u32[]{:S(2)}, u32[]{:S(2)}) collective-permute-start(bf16[192,512]{1,0:T(8,128)(2,1)S(1)} %fusion.9), channel_id=1, source_target_pairs={{0,2},{2,0},{4,6},{6,4},{8,10},{10,8},{12,14},{14,12},{1,3},{3,1},... | collective-permute-start | bytes 589832 | tf_op jit(solution)/shard_map/ppermute | solution.py:219
  67.6 9.8 %collective-permute-start.28 = (bf16[192,512]{1,0:T(8,128)(2,1)S(1)}, bf16[192,512]{1,0:T(8,128)(2,1)S(1)}, u32[]{:S(2)}, u32[]{:S(2)}) collective-permute-start(bf16[192,512]{1,0:T(8,128)(2,1)S(1)} %fusion.1), channel_id=1, source_target_pairs={{0,4},{2,6},{4,8},{6,10},{8,12},{10,14},{12,0},{14,2},{1,5},{3,7},... | collective-permute-start | bytes 589832 | tf_op jit(solution)/shard_map/ppermute | solution.py:224
  71.8 12.2 %collective-permute-start.21 = (bf16[192,512]{1,0:T(8,128)(2,1)S(1)}, bf16[192,512]{1,0:T(8,128)(2,1)S(1)}, u32[]{:S(2)}, u32[]{:S(2)}) collective-permute-start(bf16[192,512]{1,0:T(8,128)(2,1)S(1)} %fusion.3), channel_id=1, source_target_pairs={{0,8},{2,10},{4,12},{6,14},{8,0},{10,2},{12,4},{14,6},{1,9},{3,11}... | collective-permute-start | bytes 589832 | tf_op jit(solution)/shard_map/ppermute | solution.py:224
  75.6 10.6 %collective-permute-start.14 = (bf16[192,512]{1,0:T(8,128)(2,1)S(1)}, bf16[192,512]{1,0:T(8,128)(2,1)S(1)}, u32[]{:S(2)}, u32[]{:S(2)}) collective-permute-start(bf16[192,512]{1,0:T(8,128)(2,1)S(1)} %fusion.5), channel_id=1, source_target_pairs={{0,12},{2,14},{4,0},{6,2},{8,4},{10,6},{12,8},{14,10},{1,13},{3,15... | collective-permute-start | bytes 589832 | tf_op jit(solution)/shard_map/ppermute | solution.py:224
  87.2 1.4 %collective-permute-start.29 = (bf16[128,512]{1,0:T(8,128)(2,1)S(1)}, bf16[128,512]{1,0:T(8,128)(2,1)S(1)}, u32[]{:S(2)}, u32[]{:S(2)}) collective-permute-start(bf16[128,512]{1,0:T(8,128)(2,1)S(1)} %get-tuple-element.40), channel_id=1, source_target_pairs={{0,1},{1,0},{2,3},{3,2},{4,5},{5,4},{6,7},{7,6},{8,9},{9,8},{10,11... | collective-permute-start | bytes 393224 | tf_op jit(solution)/shard_map/ppermute | solution.py:214

commit v3 on v2

--- a/solution.py
+++ b/solution.py
@@ -226,6 +226,26 @@
     )
 
 
+def after_kernel(value_ref, first_ref, out_ref):
+    pass
+
+
+def after(value, first):
+    anywhere = pl.BlockSpec(memory_space=pl.ANY)
+    return pl.pallas_call(
+        after_kernel,
+        out_shape=jax.ShapeDtypeStruct(value.shape, value.dtype),
+        in_specs=[anywhere, anywhere],
+        out_specs=anywhere,
+        input_output_aliases={0: 0},
+        name="after",
+    )(value, first)
+
+
+def piece_order(count):
+    return sorted(range(count), key=lambda offset: min(offset, count - offset))
+
+
 def attend(
     core, decoder_states, memory_keys, memory_values, source_lengths, target_lengths, routes,
     attn_gain, ffn_gain, router,
@@ -274,11 +294,19 @@
         [routes, keep, other],
         scratch=[pltpu.VMEM((2 * full_len, half), jnp.bfloat16)],
     )
-    received = [selected[0]] + [shift(selected[r], r) for r in range(1, count)]
-    home = []
-    for offset, p in enumerate(received):
+    travelling = [shift(selected[r], r) for r in range(1, count)]
+    home = [None] * count
+    home = [None] * count
+    kepts, halves, wholes = [], [], []
+    for at, offset in enumerate(piece_order(count)):
+        p = travelling[offset - 1] if offset else selected[0]
+        if at >= 2:
+            p = after(p, kepts[at - 2])
         q = swap_owner(p)
-        p2, q2 = swap(p), swap(q)
+        p2 = swap(p)
+        q2 = swap(q)
+        if at >= 2:
+            q2 = after(q2, halves[at - 2])
         kept, sent = call(
             expert_kernel,
             "expert",
@@ -287,16 +315,13 @@
             [p, q, p2, q2, fc_in, fc_out],
             scratch=[pltpu.VMEM((2 * capacity, width), jnp.bfloat16)],
             vmem_mib=32,
-            cost=pl.CostEstimate(
-                flops=8 * capacity * width * fc_in.shape[1],
-                bytes_accessed=4 * width * fc_in.shape[1],
-                transcendentals=0,
-            ),
         )
+        kepts.append(kept)
         both = kept + swap(sent).astype(jnp.float32)
-        across = swap_owner(both[1].astype(jnp.bfloat16))
-        total = (both[0] + across.astype(jnp.float32)).astype(jnp.bfloat16)
-        home.append(shift(total, -offset) if offset else total)
+        halves.append(both[1].astype(jnp.bfloat16))
+        across = swap_owner(halves[-1])
+        wholes.append((both[0] + across.astype(jnp.float32)).astype(jnp.bfloat16))
+        home[offset] = shift(wholes[-1], -offset) if offset else wholes[-1]
     own_sum, other_sum = call(
         combine_kernel,
         "combine",

time: 89.8 us -> 103 us (1.15)
  waiting for transfers between devices: 46.1 us -> 30.4 us
  local copies, waits for them, and re-layouts: 8.33 us -> 21.9 us
  starting transfers between devices: 19.6 us -> 26.4 us
  Pallas kernels: 12.8 us -> 17.4 us
  other arithmetic: 1.65 us -> 5.49 us
    unnamed x24 -> x66, local copies, waits for them, and re-layouts: 8.23 us -> 20.2 us
    ppermute x6, waiting for transfers between devices: 23.4 us -> 13.5 us  [shift(): lax.ppermute(values, 'expert', [(i, (i + 2 * offset) % owners) for i in r...]
    ppermute x6, starting transfers between devices: 6.32 us -> 14.1 us  [shift(): lax.ppermute(values, 'expert', [(i, (i + 2 * offset) % owners) for i in r...]
    ppermute x8, waiting for transfers between devices: 19.9 us -> 14.1 us  [swap_owner(): return lax.ppermute(values, 'expert', [(i, i ^ 1) for i in range(owners)])]
    pallas_call x8, Pallas kernels: 12.8 us -> 17.4 us  [call(): pl.pallas_call(kernel, out_shape=tuple((jax.ShapeDtypeStruct(*out) for ou...]
    add x4, other arithmetic: 0.45 us -> 2.42 us  [line_experts(): both = kept + swap(sent).astype(jnp.float32)]
    convert_element_type x4, other arithmetic: 0.17 us -> 2.04 us  [line_experts(): wholes.append((both[0] + across.astype(jnp.float32)).astype(jnp.bfloat16))]
    convert_element_type x4, local copies, waits for them, and re-layouts: 0.1 us -> 1.69 us  [line_experts(): halves.append(both[1].astype(jnp.bfloat16))]
  transfers between devices with their start and end apart: 30 -> 30, of which waited for: 12 -> 10; matrix products, arithmetic and copies ran while one was open for 1% -> 6% of each run, Pallas kernels for 8% -> 11%
where the time goes in v3:
time: 103 us; the launch traced here: 102 us
  waiting for transfers between devices  30.4 us (30%)
  starting transfers between devices  26.4 us (26%)
  local copies, waits for them, and re-layouts  21.9 us (21%)
  Pallas kernels  17.4 us (17%)
  other arithmetic  5.49 us (5%)
    unnamed x66, local copies, waits for them, and re-layouts  20.2 us
    pallas_call x8, Pallas kernels, call(): pl.pallas_call(kernel, out_shape=tuple((jax.ShapeDtypeStruct(*out) for ou...  17.4 us
    ppermute x6, starting transfers between devices, shift(): lax.ppermute(values, 'expert', [(i, (i + 2 * offset) % owners) for i in r...  14.1 us
    ppermute x8, waiting for transfers between devices, swap_owner(): return lax.ppermute(values, 'expert', [(i, i ^ 1) for i in range(owners)])  14.1 us
    ppermute x6, waiting for transfers between devices, shift(): lax.ppermute(values, 'expert', [(i, (i + 2 * offset) % owners) for i in r...  13.5 us
    ppermute x8, starting transfers between devices, swap_owner(): return lax.ppermute(values, 'expert', [(i, i ^ 1) for i in range(owners)])  9.18 us
    ppermute x16, starting transfers between devices, swap(): return lax.ppermute(values, 'section', [(0, 1), (1, 0)])  3.08 us
    ppermute x16, waiting for transfers between devices, swap(): return lax.ppermute(values, 'section', [(0, 1), (1, 0)])  2.73 us
  transfers between devices with their start and end apart: 30, of which 10 were waited for; matrix products, arithmetic and copies ran while one was open for 6% of the time, Pallas kernels for 11%

profile of v3, /device:TPU:0, one launch (start us, length us, event | category | flops | bytes accessed | tf_op | source)
XLA Modules:
  0.0 102.5 jit_solution(324500134458336084)
XLA Ops:
  0.0 1.0 %fusion.13 = (bf16[2,80,512]{2,1,0:T(8,128)(2,1)S(1)}, bf16[2,80,512]{2,1,0:T(8,128)(2,1)S(1)}) fusion(s32[]{:T(128)S(6)} %select_n.13, bf16[2,1,80,512]{3,2,0,1:T(8,128)(2,1)} %bitcast.53, bf16[2,1,80,512]{3,2,0,1:T(8,128)(2,1)} %bitcast.54, s32[]{:T(128)S(6)} %select_n.12), kind=kLoop, calls=%fused_computation.29 | loop fusion | flops 163840 | bytes 655368 | tf_op jit(solution)/shard_map/jit(dynamic_index_in_dim)/squeeze | solution.py:256
  1.0 0.5 collective-permute-start
  2.2 0.4 collective-permute-done.other_ref
  2.6 0.9 copy-done.20
  3.5 0.7 copy-done.21
  4.2 0.7 copy-done.24
  4.9 0.7 copy-done.25
  5.6 0.7 copy-done.26
  6.3 0.7 copy-done.27
  6.9 3.2 %attend.1 = (bf16[128,1024]{1,0:T(8,128)(2,1)S(1)}, bf16[128,512]{1,0:T(8,128)(2,1)S(1)}, bf16[128,512]{1,0:T(8,128)(2,1)S(1)}, f32[2,128]{1,0:T(2,128)S(1)}) custom-call(s32[1]{0:T(128)} %bitcast.core_ref, s32[1]{0:T(128)S(6)} %copy.20.source_ref, s32[2]{0:T(128)S(1)} %copy-done.27, bf16[128,1024]{1,0:T(8,128)(2,1)S(1)} %bitcast.46, ...), custom_call_target="tpu_custom_call" | custom-call | tf_op jit(solution)/shard_map/attend/pallas_call | solution.py:24
  10.2 0.7 copy-done.18
  10.9 0.4 collective-permute-start.2
  11.3 1.0 collective-permute-done.2.other_ref
  12.3 0.7 copy-done.22
  12.9 1.1 %select.5 = (bf16[192,512]{1,0:T(8,128)(2,1)S(1)}, bf16[192,512]{1,0:T(8,128)(2,1)S(1)}, bf16[192,512]{1,0:T(8,128)(2,1)}, bf16[192,512]{1,0:T(8,128)(2,1)S(1)}) custom-call(s32[1]{0:T(128)} %bitcast.core_ref, s32[1]{0:T(128)} %bitcast.10.line_ref, s32[2,2,128]{2,1,0:T(2,128)S(1)} %bitcast.48, bf16[128,512]{1,0:T(8,128)(2,1)S(1)} %get-tuple-element.25.own_ref, ...), custom_call_target="tpu_custom_call" | custom-call | tf_op jit(solution)/shard_map/select/pallas_call | solution.py:24
  14.1 2.9 %collective-permute-start.8 = (bf16[192,512]{1,0:T(8,128)(2,1)S(1)}, bf16[192,512]{1,0:T(8,128)(2,1)S(1)}, u32[]{:S(2)}, u32[]{:S(2)}) collective-permute-start(bf16[192,512]{1,0:T(8,128)(2,1)S(1)} %get-tuple-element.30), channel_id=1, source_target_pairs={{0,4},{2,6},{4,8},{6,10},{8,12},{10,14},{12,0},{14,2},{1,5},{3,7},... | collective-permute-start | bytes 589832 | tf_op jit(solution)/shard_map/ppermute | solution.py:224
  17.0 1.5 %collective-permute-start.3 = (bf16[192,512]{1,0:T(8,128)(2,1)S(1)}, bf16[192,512]{1,0:T(8,128)(2,1)S(1)}, u32[]{:S(2)}, u32[]{:S(2)}) collective-permute-start(bf16[192,512]{1,0:T(8,128)(2,1)S(1)} %get-tuple-element.27.p_ref), channel_id=1, source_target_pairs={{0,2},{2,0},{4,6},{6,4},{8,10},{10,8},{12,14},{14,12},{1,3},{3,1},... | collective-permute-start | bytes 589832 | tf_op jit(solution)/shard_map/ppermute | solution.py:219
  18.5 5.8 %collective-permute-done.8.p_ref = bf16[192,512]{1,0:T(8,128)(2,1)S(1)} collective-permute-done((bf16[192,512]{1,0:T(8,128)(2,1)S(1)}, bf16[192,512]{1,0:T(8,128)(2,1)S(1)}, u32[]{:S(2)}, u32[]{:S(2)}) %collective-permute-start.8) | collective-permute-done | bytes 196640 | tf_op jit(solution)/shard_map/ppermute | solution.py:224
  24.2 1.5 %collective-permute-start.9 = (bf16[192,512]{1,0:T(8,128)(2,1)S(1)}, bf16[192,512]{1,0:T(8,128)(2,1)}, u32[]{:S(2)}, u32[]{:S(2)}) collective-permute-start(bf16[192,512]{1,0:T(8,128)(2,1)S(1)} %collective-permute-done.8.p_ref), channel_id=1, source_target_pairs={{0,2},{2,0},{4,6},{6,4},{8,10},{10,8},{12,14},{14,12},{1,3},{3,1},... | collective-permute-start | bytes 589832 | tf_op jit(solution)/shard_map/ppermute | solution.py:219
  25.7 0.7 collective-permute-start.15
  26.5 1.3 %collective-permute-start.22 = (bf16[192,512]{1,0:T(8,128)(2,1)S(1)}, bf16[192,512]{1,0:T(8,128)(2,1)S(1)}, u32[]{:S(2)}, u32[]{:S(2)}) collective-permute-start(bf16[192,512]{1,0:T(8,128)(2,1)S(1)} %get-tuple-element.36), channel_id=1, source_target_pairs={{0,12},{2,14},{4,0},{6,2},{8,4},{10,6},{12,8},{14,10},{1,13},{3,15... | collective-permute-start | bytes 589832 | tf_op jit(solution)/shard_map/ppermute | solution.py:224
  27.8 3.0 %collective-permute-done.9.q_ref = bf16[192,512]{1,0:T(8,128)(2,1)} collective-permute-done((bf16[192,512]{1,0:T(8,128)(2,1)S(1)}, bf16[192,512]{1,0:T(8,128)(2,1)}, u32[]{:S(2)}, u32[]{:S(2)}) %collective-permute-start.9) | collective-permute-done | bytes 196640 | tf_op jit(solution)/shard_map/ppermute | solution.py:219
  30.8 1.6 %copy-done = bf16[1024,1024]{1,0:T(8,128)(2,1)S(1)} copy-done((bf16[1024,1024]{1,0:T(8,128)(2,1)S(1)}, bf16[1024,1024]{1,0:T(8,128)(2,1)}, u32[]{:S(2)}) %copy-start) | copy-done | bytes 2097176
  32.4 1.6 %copy-done.2 = bf16[1024,1024]{1,0:T(8,128)(2,1)S(1)} copy-done((bf16[1024,1024]{1,0:T(8,128)(2,1)S(1)}, bf16[1024,1024]{1,0:T(8,128)(2,1)}, u32[]{:S(2)}) %copy-start.2) | copy-done | bytes 2097176
  34.0 2.2 %expert.4 = (f32[2,192,512]{2,1,0:T(8,128)S(1)}, bf16[2,192,512]{2,1,0:T(8,128)(2,1)}) custom-call(s32[1]{0:T(128)} %bitcast.core_ref, bf16[192,512]{1,0:T(8,128)(2,1)S(1)} %get-tuple-element.27.p_ref, bf16[192,512]{1,0:T(8,128)(2,1)S(1)} %collective-permute-done.3.q_ref, bf16[192,512]{1,0:T(8,128)(2,1)S(1)} %collective-permute-done.4.p2_ref, ...), custom_call_target="tpu_custom_call" | custom-call | tf_op jit(solution)/shard_map/expert/pallas_call | solution.py:24
  36.2 0.9 copy-done.6
  37.1 0.5 collective-permute-start.6
  37.7 0.7 copy-done.12
  38.4 1.3 %collective-permute-start.23 = (bf16[192,512]{1,0:T(8,128)(2,1)}, bf16[192,512]{1,0:T(8,128)(2,1)}, u32[]{:S(2)}, u32[]{:S(2)}) collective-permute-start(bf16[192,512]{1,0:T(8,128)(2,1)} %after.6.p_ref), channel_id=1, source_target_pairs={{0,2},{2,0},{4,6},{6,4},{8,10},{10,8},{12,14},{14,12},{1,3},{3,1},... | collective-permute-start | bytes 589832 | tf_op jit(solution)/shard_map/ppermute | solution.py:219
  39.7 1.6 %copy-done.3 = bf16[1024,1024]{1,0:T(8,128)(2,1)S(1)} copy-done((bf16[1024,1024]{1,0:T(8,128)(2,1)S(1)}, bf16[1024,1024]{1,0:T(8,128)(2,1)}, u32[]{:S(2)}) %copy-start.3) | copy-done | bytes 2097176
  41.3 3.0 %expert.5 = (f32[2,192,512]{2,1,0:T(8,128)S(1)}, bf16[2,192,512]{2,1,0:T(8,128)(2,1)S(1)}) custom-call(s32[1]{0:T(128)} %bitcast.core_ref, bf16[192,512]{1,0:T(8,128)(2,1)S(1)} %collective-permute-done.8.p_ref, bf16[192,512]{1,0:T(8,128)(2,1)} %collective-permute-done.9.q_ref, bf16[192,512]{1,0:T(8,128)(2,1)} %collective-permute-done.10.p2_ref, ...), custom_call_target="tpu_custom_call" | custom-call | tf_op jit(solution)/shard_map/expert/pallas_call | solution.py:24
  44.3 0.9 copy-done.8
  45.2 0.7 copy-done.28
  45.9 0.7 copy-done.10
  46.6 0.7 collective-permute-start.16
  47.4 0.5 collective-permute-start.24
  47.9 0.4 collective-permute-start.25
  48.4 4.9 %collective-permute-done.16.q_ref = bf16[192,512]{1,0:T(8,128)(2,1)} collective-permute-done((bf16[192,512]{1,0:T(8,128)(2,1)}, bf16[192,512]{1,0:T(8,128)(2,1)}, u32[]{:S(2)}, u32[]{:S(2)}) %collective-permute-start.16) | collective-permute-done | bytes 196640 | tf_op jit(solution)/shard_map/ppermute | solution.py:219
  53.3 1.1 %convert_add_fusion.3 = f32[2,192,512]{2,1,0:T(8,128)S(1)} fusion(f32[2,192,512]{2,1,0:T(8,128)S(1)} %copy-done.7, bf16[2,192,512]{2,1,0:T(8,128)(2,1)} %collective-permute-done.6), kind=kLoop, calls=%fused_computation.3 | loop fusion | flops 393216 | bytes 1966080 | tf_op jit(solution)/shard_map/add | solution.py:320
  54.6 0.9 fusion.9.first_ref
  55.5 0.8 collective-permute-start.13
  56.3 0.7 fusion.8.first_ref
  57.0 0.7 copy-done.16
  57.7 1.6 %copy-done.4 = bf16[1024,1024]{1,0:T(8,128)(2,1)S(1)} copy-done((bf16[1024,1024]{1,0:T(8,128)(2,1)S(1)}, bf16[1024,1024]{1,0:T(8,128)(2,1)}, u32[]{:S(2)}) %copy-start.4) | copy-done | bytes 2097176
  59.3 0.9 copy-done.17
  60.2 3.3 %expert.7 = (f32[2,192,512]{2,1,0:T(8,128)S(1)}, bf16[2,192,512]{2,1,0:T(8,128)(2,1)}) custom-call(s32[1]{0:T(128)} %bitcast.core_ref, bf16[192,512]{1,0:T(8,128)(2,1)S(1)} %copy-done.13, bf16[192,512]{1,0:T(8,128)(2,1)} %collective-permute-done.23.q_ref, bf16[192,512]{1,0:T(8,128)(2,1)} %collective-permute-done.24.p2_ref, bf16[192,512]{1,0:T(8,128)(2,1)S(1)} %copy-done.17, ...), custom_call_target="tpu_custom_call" | custom-call | tf_op jit(solution)/shard_map/expert/pallas_call | solution.py:24
  64.0 1.2 %collective-permute-start.7 = (bf16[192,512]{1,0:T(8,128)(2,1)}, bf16[192,512]{1,0:T(8,128)(2,1)}, u32[]{:S(2)}, u32[]{:S(2)}) collective-permute-start(bf16[192,512]{1,0:T(8,128)(2,1)} %fusion.8.first_ref), channel_id=1, source_target_pairs={{0,2},{2,0},{4,6},{6,4},{8,10},{10,8},{12,14},{14,12},{1,3},{3,1},... | collective-permute-start | bytes 589832 | tf_op jit(solution)/shard_map/ppermute | solution.py:219
  65.3 1.6 %copy-done.5 = bf16[1024,1024]{1,0:T(8,128)(2,1)S(1)} copy-done((bf16[1024,1024]{1,0:T(8,128)(2,1)S(1)}, bf16[1024,1024]{1,0:T(8,128)(2,1)}, u32[]{:S(2)}) %copy-start.5) | copy-done | bytes 2097176
  66.8 0.9 copy-done.15
  67.8 2.9 %expert.6 = (f32[2,192,512]{2,1,0:T(8,128)S(1)}, bf16[2,192,512]{2,1,0:T(8,128)(2,1)S(1)}) custom-call(s32[1]{0:T(128)} %bitcast.core_ref, bf16[192,512]{1,0:T(8,128)(2,1)S(1)} %copy-done.11, bf16[192,512]{1,0:T(8,128)(2,1)} %collective-permute-done.16.q_ref, bf16[192,512]{1,0:T(8,128)(2,1)} %collective-permute-done.17.p2_ref, ...), custom_call_target="tpu_custom_call" | custom-call | tf_op jit(solution)/shard_map/expert/pallas_call | solution.py:24
  70.8 1.0 fusion.5
  71.8 2.3 %collective-permute-start.14 = (bf16[192,512]{1,0:T(8,128)(2,1)S(1)}, bf16[192,512]{1,0:T(8,128)(2,1)S(1)}, u32[]{:S(2)}, u32[]{:S(2)}) collective-permute-start(bf16[192,512]{1,0:T(8,128)(2,1)S(1)} %fusion.5), channel_id=1, source_target_pairs={{0,12},{2,14},{4,0},{6,2},{8,4},{10,6},{12,8},{14,10},{1,13},{3,15... | collective-permute-start | bytes 589832 | tf_op jit(solution)/shard_map/ppermute | solution.py:224
  74.0 1.1 %convert_add_fusion = f32[2,192,512]{2,1,0:T(8,128)S(1)} fusion(f32[2,192,512]{2,1,0:T(8,128)S(1)} %get-tuple-element.37, bf16[2,192,512]{2,1,0:T(8,128)(2,1)} %collective-permute-done.26), kind=kLoop, calls=%fused_computation | loop fusion | flops 393216 | bytes 1966080 | tf_op jit(solution)/shard_map/add | solution.py:320
  75.2 0.9 collective-permute-start.27
  76.3 1.2 %collective-permute-start.20 = (bf16[192,512]{1,0:T(8,128)(2,1)S(1)}, bf16[192,512]{1,0:T(8,128)(2,1)S(1)}, u32[]{:S(2)}, u32[]{:S(2)}) collective-permute-start(bf16[192,512]{1,0:T(8,128)(2,1)S(1)} %fusion.10), channel_id=1, source_target_pairs={{0,2},{2,0},{4,6},{6,4},{8,10},{10,8},{12,14},{14,12},{1,3},{3,1},... | collective-permute-start | bytes 589832 | tf_op jit(solution)/shard_map/ppermute | solution.py:219
  77.5 5.5 %collective-permute-done.27 = bf16[192,512]{1,0:T(8,128)(2,1)S(1)} collective-permute-done((bf16[192,512]{1,0:T(8,128)(2,1)S(1)}, bf16[192,512]{1,0:T(8,128)(2,1)S(1)}, u32[]{:S(2)}, u32[]{:S(2)}) %collective-permute-start.27) | collective-permute-done | bytes 196640 | tf_op jit(solution)/shard_map/ppermute | solution.py:219
  83.1 2.7 %collective-permute-start.28 = (bf16[192,512]{1,0:T(8,128)(2,1)S(1)}, bf16[192,512]{1,0:T(8,128)(2,1)S(1)}, u32[]{:S(2)}, u32[]{:S(2)}) collective-permute-start(bf16[192,512]{1,0:T(8,128)(2,1)S(1)} %fusion.1), channel_id=1, source_target_pairs={{0,4},{2,6},{4,8},{6,10},{8,12},{10,14},{12,0},{14,2},{1,5},{3,7},... | collective-permute-start | bytes 589832 | tf_op jit(solution)/shard_map/ppermute | solution.py:224
  85.7 0.7 collective-permute-done.20
  86.5 4.2 %collective-permute-start.21 = (bf16[192,512]{1,0:T(8,128)(2,1)S(1)}, bf16[192,512]{1,0:T(8,128)(2,1)S(1)}, u32[]{:S(2)}, u32[]{:S(2)}) collective-permute-start(bf16[192,512]{1,0:T(8,128)(2,1)S(1)} %fusion.3), channel_id=1, source_target_pairs={{0,8},{2,10},{4,12},{6,14},{8,0},{10,2},{12,4},{14,6},{1,9},{3,11}... | collective-permute-start | bytes 589832 | tf_op jit(solution)/shard_map/ppermute | solution.py:224
  90.7 1.0 fusion.7.rest_0_
  91.7 7.6 %collective-permute-done.21.rest_2_ = bf16[192,512]{1,0:T(8,128)(2,1)S(1)} collective-permute-done((bf16[192,512]{1,0:T(8,128)(2,1)S(1)}, bf16[192,512]{1,0:T(8,128)(2,1)S(1)}, u32[]{:S(2)}, u32[]{:S(2)}) %collective-permute-start.21) | collective-permute-done | bytes 196640 | tf_op jit(solution)/shard_map/ppermute | solution.py:224
  99.4 0.9 combine.1
  100.4 1.3 %collective-permute-done.29.other_ref = bf16[128,512]{1,0:T(8,128)(2,1)S(1)} collective-permute-done((bf16[128,512]{1,0:T(8,128)(2,1)S(1)}, bf16[128,512]{1,0:T(8,128)(2,1)S(1)}, u32[]{:S(2)}, u32[]{:S(2)}) %collective-permute-start.29) | collective-permute-done | bytes 131104 | tf_op jit(solution)/shard_map/ppermute | solution.py:214
  101.7 0.8 finish.1
  (87 shorter events, 1.4 us)
Async XLA Ops:
  1.0 1.5 %collective-permute-start = (bf16[2,80,512]{2,1,0:T(8,128)(2,1)S(1)}, bf16[2,80,512]{2,1,0:T(8,128)(2,1)S(1)}, u32[]{:S(2)}, u32[]{:S(2)}) collective-permute-start(bf16[2,80,512]{2,1,0:T(8,128)(2,1)S(1)} %get-tuple-element.41), channel_id=1, source_target_pairs={{0,1},{1,0},{2,3},{3,2},{4,5},{5,4},{6,7},{7,6},{8,9},{9,8},{10,11... | collective-permute-start | bytes 491528 | tf_op jit(solution)/shard_map/ppermute | solution.py:214
  2.6 0.9 copy-start.20
  3.5 0.7 copy-start.21
  4.2 0.7 copy-start.24
  4.9 0.7 copy-start.25
  5.6 0.7 copy-start.26
  6.3 0.7 copy-start.27
  10.2 0.7 copy-start.18
  10.9 1.4 %collective-permute-start.2 = (bf16[128,512]{1,0:T(8,128)(2,1)S(1)}, bf16[128,512]{1,0:T(8,128)(2,1)S(1)}, u32[]{:S(2)}, u32[]{:S(2)}) collective-permute-start(bf16[128,512]{1,0:T(8,128)(2,1)S(1)} %get-tuple-element.26), channel_id=1, source_target_pairs={{0,1},{1,0},{2,3},{3,2},{4,5},{5,4},{6,7},{7,6},{8,9},{9,8},{10,11... | collective-permute-start | bytes 393224 | tf_op jit(solution)/shard_map/ppermute | solution.py:214
  12.3 0.7 copy-start.22
  14.1 10.2 %collective-permute-start.8 = (bf16[192,512]{1,0:T(8,128)(2,1)S(1)}, bf16[192,512]{1,0:T(8,128)(2,1)S(1)}, u32[]{:S(2)}, u32[]{:S(2)}) collective-permute-start(bf16[192,512]{1,0:T(8,128)(2,1)S(1)} %get-tuple-element.30), channel_id=1, source_target_pairs={{0,4},{2,6},{4,8},{6,10},{8,12},{10,14},{12,0},{14,2},{1,5},{3,7},... | collective-permute-start | bytes 589832 | tf_op jit(solution)/shard_map/ppermute | solution.py:224
  17.0 8.7 %collective-permute-start.3 = (bf16[192,512]{1,0:T(8,128)(2,1)S(1)}, bf16[192,512]{1,0:T(8,128)(2,1)S(1)}, u32[]{:S(2)}, u32[]{:S(2)}) collective-permute-start(bf16[192,512]{1,0:T(8,128)(2,1)S(1)} %get-tuple-element.27.p_ref), channel_id=1, source_target_pairs={{0,2},{2,0},{4,6},{6,4},{8,10},{10,8},{12,14},{14,12},{1,3},{3,1},... | collective-permute-start | bytes 589832 | tf_op jit(solution)/shard_map/ppermute | solution.py:219
  18.5 9.3 %collective-permute-start.4 = (bf16[192,512]{1,0:T(8,128)(2,1)S(1)}, bf16[192,512]{1,0:T(8,128)(2,1)S(1)}, u32[]{:S(2)}, u32[]{:S(2)}) collective-permute-start(bf16[192,512]{1,0:T(8,128)(2,1)S(1)} %get-tuple-element.27.p_ref), channel_id=1, source_target_pairs={{0,1},{1,0},{2,3},{3,2},{4,5},{5,4},{6,7},{7,6},{8,9},{9,8},{10,11... | collective-permute-start | bytes 589832 | tf_op jit(solution)/shard_map/ppermute | solution.py:214
  24.2 6.5 %collective-permute-start.9 = (bf16[192,512]{1,0:T(8,128)(2,1)S(1)}, bf16[192,512]{1,0:T(8,128)(2,1)}, u32[]{:S(2)}, u32[]{:S(2)}) collective-permute-start(bf16[192,512]{1,0:T(8,128)(2,1)S(1)} %collective-permute-done.8.p_ref), channel_id=1, source_target_pairs={{0,2},{2,0},{4,6},{6,4},{8,10},{10,8},{12,14},{14,12},{1,3},{3,1},... | collective-permute-start | bytes 589832 | tf_op jit(solution)/shard_map/ppermute | solution.py:219
  25.7 5.1 %collective-permute-start.5 = (bf16[192,512]{1,0:T(8,128)(2,1)S(1)}, bf16[192,512]{1,0:T(8,128)(2,1)S(1)}, u32[]{:S(2)}, u32[]{:S(2)}) collective-permute-start(bf16[192,512]{1,0:T(8,128)(2,1)S(1)} %collective-permute-done.3.q_ref), channel_id=1, source_target_pairs={{0,1},{1,0},{2,3},{3,2},{4,5},{5,4},{6,7},{7,6},{8,9},{9,8},{10,11... | collective-permute-start | bytes 589832 | tf_op jit(solution)/shard_map/ppermute | solution.py:214
  25.7 19.4 %collective-permute-start.15 = (bf16[192,512]{1,0:T(8,128)(2,1)}, bf16[192,512]{1,0:T(8,128)(2,1)S(1)}, u32[]{:S(2)}, u32[]{:S(2)}) collective-permute-start(bf16[192,512]{1,0:T(8,128)(2,1)} %get-tuple-element.33), channel_id=1, source_target_pairs={{0,8},{2,10},{4,12},{6,14},{8,0},{10,2},{12,4},{14,6},{1,9},{3,11}... | collective-permute-start | bytes 589832 | tf_op jit(solution)/shard_map/ppermute | solution.py:224
  26.5 11.2 %collective-permute-start.22 = (bf16[192,512]{1,0:T(8,128)(2,1)S(1)}, bf16[192,512]{1,0:T(8,128)(2,1)S(1)}, u32[]{:S(2)}, u32[]{:S(2)}) collective-permute-start(bf16[192,512]{1,0:T(8,128)(2,1)S(1)} %get-tuple-element.36), channel_id=1, source_target_pairs={{0,12},{2,14},{4,0},{6,2},{8,4},{10,6},{12,8},{14,10},{1,13},{3,15... | collective-permute-start | bytes 589832 | tf_op jit(solution)/shard_map/ppermute | solution.py:224
  27.8 11.9 %collective-permute-start.10 = (bf16[192,512]{1,0:T(8,128)(2,1)S(1)}, bf16[192,512]{1,0:T(8,128)(2,1)}, u32[]{:S(2)}, u32[]{:S(2)}) collective-permute-start(bf16[192,512]{1,0:T(8,128)(2,1)S(1)} %collective-permute-done.8.p_ref), channel_id=1, source_target_pairs={{0,1},{1,0},{2,3},{3,2},{4,5},{5,4},{6,7},{7,6},{8,9},{9,8},{10,11... | collective-permute-start | bytes 589832 | tf_op jit(solution)/shard_map/ppermute | solution.py:214
  30.8 8.9 %collective-permute-start.11 = (bf16[192,512]{1,0:T(8,128)(2,1)}, bf16[192,512]{1,0:T(8,128)(2,1)}, u32[]{:S(2)}, u32[]{:S(2)}) collective-permute-start(bf16[192,512]{1,0:T(8,128)(2,1)} %collective-permute-done.9.q_ref), channel_id=1, source_target_pairs={{0,1},{1,0},{2,3},{3,2},{4,5},{5,4},{6,7},{7,6},{8,9},{9,8},{10,11... | collective-permute-start | bytes 589832 | tf_op jit(solution)/shard_map/ppermute | solution.py:214
  30.8 1.6 %copy-start = (bf16[1024,1024]{1,0:T(8,128)(2,1)S(1)}, bf16[1024,1024]{1,0:T(8,128)(2,1)}, u32[]{:S(2)}) copy-start(bf16[1024,1024]{1,0:T(8,128)(2,1)} %in_ref.7) | copy-start | bytes 6291460
  32.4 1.6 %copy-start.2 = (bf16[1024,1024]{1,0:T(8,128)(2,1)S(1)}, bf16[1024,1024]{1,0:T(8,128)(2,1)}, u32[]{:S(2)}) copy-start(bf16[1024,1024]{1,0:T(8,128)(2,1)} %out_ref.7) | copy-start | bytes 6291460
  34.0 5.7 %copy-start.1 = (bf16[1024,1024]{1,0:T(8,128)(2,1)S(1)}, bf16[1024,1024]{1,0:T(8,128)(2,1)}, u32[]{:S(2)}) copy-start(bf16[1024,1024]{1,0:T(8,128)(2,1)} %in_ref.7) | copy-start | bytes 6291460
  36.2 0.9 copy-start.6
  37.1 10.9 %collective-permute-start.6 = (bf16[2,192,512]{2,1,0:T(8,128)(2,1)}, bf16[2,192,512]{2,1,0:T(8,128)(2,1)}, u32[]{:S(2)}, u32[]{:S(2)}) collective-permute-start(bf16[2,192,512]{2,1,0:T(8,128)(2,1)} %get-tuple-element.29), channel_id=1, source_target_pairs={{0,1},{1,0},{2,3},{3,2},{4,5},{5,4},{6,7},{7,6},{8,9},{9,8},{10,11... | collective-permute-start | bytes 1179656 | tf_op jit(solution)/shard_map/ppermute | solution.py:214
  37.7 0.7 copy-start.12
  38.4 14.9 %copy-start.7 = (f32[2,192,512]{2,1,0:T(8,128)S(1)}, f32[2,192,512]{2,1,0:T(8,128)}, u32[]{:S(2)}) copy-start(f32[2,192,512]{2,1,0:T(8,128)} %copy-done.6) | copy-start | bytes 2359300
  38.4 9.5 %collective-permute-start.23 = (bf16[192,512]{1,0:T(8,128)(2,1)}, bf16[192,512]{1,0:T(8,128)(2,1)}, u32[]{:S(2)}, u32[]{:S(2)}) collective-permute-start(bf16[192,512]{1,0:T(8,128)(2,1)} %after.6.p_ref), channel_id=1, source_target_pairs={{0,2},{2,0},{4,6},{6,4},{8,10},{10,8},{12,14},{14,12},{1,3},{3,1},... | collective-permute-start | bytes 589832 | tf_op jit(solution)/shard_map/ppermute | solution.py:219
  39.7 1.6 %copy-start.3 = (bf16[1024,1024]{1,0:T(8,128)(2,1)S(1)}, bf16[1024,1024]{1,0:T(8,128)(2,1)}, u32[]{:S(2)}) copy-start(bf16[1024,1024]{1,0:T(8,128)(2,1)} %out_ref.7) | copy-start | bytes 6291460
  41.3 6.1 %copy-start.13 = (bf16[192,512]{1,0:T(8,128)(2,1)S(1)}, bf16[192,512]{1,0:T(8,128)(2,1)}, u32[]{:S(2)}) copy-start(bf16[192,512]{1,0:T(8,128)(2,1)} %after.6.p_ref) | copy-start | bytes 589828
  44.3 0.9 copy-start.8
  45.2 0.8 copy-start.28
  45.9 0.7 copy-start.10
  46.6 7.8 %copy-start.9 = (f32[2,192,512]{2,1,0:T(8,128)S(1)}, f32[2,192,512]{2,1,0:T(8,128)}, u32[]{:S(2)}) copy-start(f32[2,192,512]{2,1,0:T(8,128)} %copy-done.8) | copy-start | bytes 2359300
  46.6 6.7 %collective-permute-start.16 = (bf16[192,512]{1,0:T(8,128)(2,1)}, bf16[192,512]{1,0:T(8,128)(2,1)}, u32[]{:S(2)}, u32[]{:S(2)}) collective-permute-start(bf16[192,512]{1,0:T(8,128)(2,1)} %after.4.p_ref), channel_id=1, source_target_pairs={{0,2},{2,0},{4,6},{6,4},{8,10},{10,8},{12,14},{14,12},{1,3},{3,1},... | collective-permute-start | bytes 589832 | tf_op jit(solution)/shard_map/ppermute | solution.py:219
  47.4 7.1 %collective-permute-start.12 = (bf16[2,192,512]{2,1,0:T(8,128)(2,1)}, bf16[2,192,512]{2,1,0:T(8,128)(2,1)S(1)}, u32[]{:S(2)}, u32[]{:S(2)}) collective-permute-start(bf16[2,192,512]{2,1,0:T(8,128)(2,1)} %copy-done.28), channel_id=1, source_target_pairs={{0,1},{1,0},{2,3},{3,2},{4,5},{5,4},{6,7},{7,6},{8,9},{9,8},{10,11... | collective-permute-start | bytes 1179656 | tf_op jit(solution)/shard_map/ppermute | solution.py:214
  47.4 10.3 %collective-permute-start.24 = (bf16[192,512]{1,0:T(8,128)(2,1)S(1)}, bf16[192,512]{1,0:T(8,128)(2,1)}, u32[]{:S(2)}, u32[]{:S(2)}) collective-permute-start(bf16[192,512]{1,0:T(8,128)(2,1)S(1)} %copy-done.13), channel_id=1, source_target_pairs={{0,1},{1,0},{2,3},{3,2},{4,5},{5,4},{6,7},{7,6},{8,9},{9,8},{10,11... | collective-permute-start | bytes 589832 | tf_op jit(solution)/shard_map/ppermute | solution.py:214
  47.9 17.4 %collective-permute-start.17 = (bf16[192,512]{1,0:T(8,128)(2,1)}, bf16[192,512]{1,0:T(8,128)(2,1)}, u32[]{:S(2)}, u32[]{:S(2)}) collective-permute-start(bf16[192,512]{1,0:T(8,128)(2,1)} %after.4.p_ref), channel_id=1, source_target_pairs={{0,1},{1,0},{2,3},{3,2},{4,5},{5,4},{6,7},{7,6},{8,9},{9,8},{10,11... | collective-permute-start | bytes 589832 | tf_op jit(solution)/shard_map/ppermute | solution.py:214
  47.9 9.1 %collective-permute-start.25 = (bf16[192,512]{1,0:T(8,128)(2,1)}, bf16[192,512]{1,0:T(8,128)(2,1)S(1)}, u32[]{:S(2)}, u32[]{:S(2)}) collective-permute-start(bf16[192,512]{1,0:T(8,128)(2,1)} %collective-permute-done.23.q_ref), channel_id=1, source_target_pairs={{0,1},{1,0},{2,3},{3,2},{4,5},{5,4},{6,7},{7,6},{8,9},{9,8},{10,11... | collective-permute-start | bytes 589832 | tf_op jit(solution)/shard_map/ppermute | solution.py:214
  53.3 10.7 %collective-permute-start.18 = (bf16[192,512]{1,0:T(8,128)(2,1)}, bf16[192,512]{1,0:T(8,128)(2,1)S(1)}, u32[]{:S(2)}, u32[]{:S(2)}) collective-permute-start(bf16[192,512]{1,0:T(8,128)(2,1)} %collective-permute-done.16.q_ref), channel_id=1, source_target_pairs={{0,1},{1,0},{2,3},{3,2},{4,5},{5,4},{6,7},{7,6},{8,9},{9,8},{10,11... | collective-permute-start | bytes 589832 | tf_op jit(solution)/shard_map/ppermute | solution.py:214
  54.4 1.9 %copy-start.29 = (f32[2,192,512]{2,1,0:T(8,128)}, f32[2,192,512]{2,1,0:T(8,128)S(1)}, u32[]{:S(2)}) copy-start(f32[2,192,512]{2,1,0:T(8,128)S(1)} %convert_add_fusion.3) | copy-start | bytes 2359300
  54.6 3.1 %copy-start.31 = (f32[2,192,512]{2,1,0:T(8,128)}, f32[2,192,512]{2,1,0:T(8,128)S(1)}, u32[]{:S(2)}) copy-start(f32[2,192,512]{2,1,0:T(8,128)S(1)} %convert_add_fusion.2) | copy-start | bytes 2359300
  55.5 15.3 %collective-permute-start.13 = (bf16[192,512]{1,0:T(8,128)(2,1)}, bf16[192,512]{1,0:T(8,128)(2,1)}, u32[]{:S(2)}, u32[]{:S(2)}) collective-permute-start(bf16[192,512]{1,0:T(8,128)(2,1)} %fusion.9.first_ref), channel_id=1, source_target_pairs={{0,2},{2,0},{4,6},{6,4},{8,10},{10,8},{12,14},{14,12},{1,3},{3,1},... | collective-permute-start | bytes 589832 | tf_op jit(solution)/shard_map/ppermute | solution.py:219
  57.0 0.7 copy-start.16
  57.7 1.6 %copy-start.4 = (bf16[1024,1024]{1,0:T(8,128)(2,1)S(1)}, bf16[1024,1024]{1,0:T(8,128)(2,1)}, u32[]{:S(2)}) copy-start(bf16[1024,1024]{1,0:T(8,128)(2,1)} %out_ref.7) | copy-start | bytes 6291460
  59.3 0.9 copy-start.17
  60.2 5.0 %copy-start.11 = (bf16[192,512]{1,0:T(8,128)(2,1)S(1)}, bf16[192,512]{1,0:T(8,128)(2,1)}, u32[]{:S(2)}) copy-start(bf16[192,512]{1,0:T(8,128)(2,1)} %after.4.p_ref) | copy-start | bytes 589828
  63.5 10.6 %collective-permute-start.26 = (bf16[2,192,512]{2,1,0:T(8,128)(2,1)}, bf16[2,192,512]{2,1,0:T(8,128)(2,1)}, u32[]{:S(2)}, u32[]{:S(2)}) collective-permute-start(bf16[2,192,512]{2,1,0:T(8,128)(2,1)} %get-tuple-element.38), channel_id=1, source_target_pairs={{0,1},{1,0},{2,3},{3,2},{4,5},{5,4},{6,7},{7,6},{8,9},{9,8},{10,11... | collective-permute-start | bytes 1179656 | tf_op jit(solution)/shard_map/ppermute | solution.py:214
  63.7 28.0 %collective-permute-start.1 = (f32[2,128]{1,0:T(2,128)S(1)}, f32[2,128]{1,0:T(2,128)S(1)}, u32[]{:S(2)}, u32[]{:S(2)}) collective-permute-start(f32[2,128]{1,0:T(2,128)S(1)} %get-tuple-element.24.own_gates_ref), channel_id=1, source_target_pairs={{0,1},{1,0},{2,3},{3,2},{4,5},{5,4},{6,7},{7,6},{8,9},{9,8},{10,11... | collective-permute-start | bytes 3080 | tf_op jit(solution)/shard_map/ppermute | solution.py:214
  64.0 1.2 %copy-start.14 = (bf16[192,512]{1,0:T(8,128)(2,1)}, bf16[192,512]{1,0:T(8,128)(2,1)S(1)}, u32[]{:S(2)}) copy-start(bf16[192,512]{1,0:T(8,128)(2,1)S(1)} %collective-permute-done.18.value_ref) | copy-start | bytes 589828
  64.0 26.7 %collective-permute-start.7 = (bf16[192,512]{1,0:T(8,128)(2,1)}, bf16[192,512]{1,0:T(8,128)(2,1)}, u32[]{:S(2)}, u32[]{:S(2)}) collective-permute-start(bf16[192,512]{1,0:T(8,128)(2,1)} %fusion.8.first_ref), channel_id=1, source_target_pairs={{0,2},{2,0},{4,6},{6,4},{8,10},{10,8},{12,14},{14,12},{1,3},{3,1},... | collective-permute-start | bytes 589832 | tf_op jit(solution)/shard_map/ppermute | solution.py:219
  65.2 1.6 %copy-start.5 = (bf16[1024,1024]{1,0:T(8,128)(2,1)S(1)}, bf16[1024,1024]{1,0:T(8,128)(2,1)}, u32[]{:S(2)}) copy-start(bf16[1024,1024]{1,0:T(8,128)(2,1)} %out_ref.7) | copy-start | bytes 6291460
  66.8 0.9 copy-start.15
  67.8 3.0 %copy-start.32 = (f32[2,192,512]{2,1,0:T(8,128)S(1)}, f32[2,192,512]{2,1,0:T(8,128)}, u32[]{:S(2)}) copy-start(f32[2,192,512]{2,1,0:T(8,128)} %copy-done.31) | copy-start | bytes 2359300
  70.7 5.4 %collective-permute-start.19 = (bf16[2,192,512]{2,1,0:T(8,128)(2,1)S(1)}, bf16[2,192,512]{2,1,0:T(8,128)(2,1)S(1)}, u32[]{:S(2)}, u32[]{:S(2)}) collective-permute-start(bf16[2,192,512]{2,1,0:T(8,128)(2,1)S(1)} %get-tuple-element.35), channel_id=1, source_target_pairs={{0,1},{1,0},{2,3},{3,2},{4,5},{5,4},{6,7},{7,6},{8,9},{9,8},{10,11... | collective-permute-start | bytes 1179656 | tf_op jit(solution)/shard_map/ppermute | solution.py:214
  71.8 19.9 %collective-permute-start.14 = (bf16[192,512]{1,0:T(8,128)(2,1)S(1)}, bf16[192,512]{1,0:T(8,128)(2,1)S(1)}, u32[]{:S(2)}, u32[]{:S(2)}) collective-permute-start(bf16[192,512]{1,0:T(8,128)(2,1)S(1)} %fusion.5), channel_id=1, source_target_pairs={{0,12},{2,14},{4,0},{6,2},{8,4},{10,6},{12,8},{14,10},{1,13},{3,15... | collective-permute-start | bytes 589832 | tf_op jit(solution)/shard_map/ppermute | solution.py:224
  75.2 15.6 %copy-start.30 = (f32[2,192,512]{2,1,0:T(8,128)S(1)}, f32[2,192,512]{2,1,0:T(8,128)}, u32[]{:S(2)}) copy-start(f32[2,192,512]{2,1,0:T(8,128)} %copy-done.29) | copy-start | bytes 2359300
  75.2 7.8 %collective-permute-start.27 = (bf16[192,512]{1,0:T(8,128)(2,1)S(1)}, bf16[192,512]{1,0:T(8,128)(2,1)S(1)}, u32[]{:S(2)}, u32[]{:S(2)}) collective-permute-start(bf16[192,512]{1,0:T(8,128)(2,1)S(1)} %fusion.11), channel_id=1, source_target_pairs={{0,2},{2,0},{4,6},{6,4},{8,10},{10,8},{12,14},{14,12},{1,3},{3,1},... | collective-permute-start | bytes 589832 | tf_op jit(solution)/shard_map/ppermute | solution.py:219
  76.1 23.2 %copy-start.23 = (s32[2,128,2]{1,2,0:T(2,128)S(1)}, s32[2,128,2]{1,2,0:T(2,128)}, u32[]{:S(2)}) copy-start(s32[2,128,2]{1,2,0:T(2,128)} %param.16) | copy-start | bytes 6148
  76.2 25.4 %copy-start.19 = (bf16[128,1024]{1,0:T(8,128)(2,1)S(1)}, bf16[128,1024]{1,0:T(8,128)(2,1)}, u32[]{:S(2)}) copy-start(bf16[128,1024]{1,0:T(8,128)(2,1)} %copy-done.18) | copy-start | bytes 786436
  76.3 10.2 %collective-permute-start.20 = (bf16[192,512]{1,0:T(8,128)(2,1)S(1)}, bf16[192,512]{1,0:T(8,128)(2,1)S(1)}, u32[]{:S(2)}, u32[]{:S(2)}) collective-permute-start(bf16[192,512]{1,0:T(8,128)(2,1)S(1)} %fusion.10), channel_id=1, source_target_pairs={{0,2},{2,0},{4,6},{6,4},{8,10},{10,8},{12,14},{14,12},{1,3},{3,1},... | collective-permute-start | bytes 589832 | tf_op jit(solution)/shard_map/ppermute | solution.py:219
  83.1 8.7 %collective-permute-start.28 = (bf16[192,512]{1,0:T(8,128)(2,1)S(1)}, bf16[192,512]{1,0:T(8,128)(2,1)S(1)}, u32[]{:S(2)}, u32[]{:S(2)}) collective-permute-start(bf16[192,512]{1,0:T(8,128)(2,1)S(1)} %fusion.1), channel_id=1, source_target_pairs={{0,4},{2,6},{4,8},{6,10},{8,12},{10,14},{12,0},{14,2},{1,5},{3,7},... | collective-permute-start | bytes 589832 | tf_op jit(solution)/shard_map/ppermute | solution.py:224
  86.5 12.8 %collective-permute-start.21 = (bf16[192,512]{1,0:T(8,128)(2,1)S(1)}, bf16[192,512]{1,0:T(8,128)(2,1)S(1)}, u32[]{:S(2)}, u32[]{:S(2)}) collective-permute-start(bf16[192,512]{1,0:T(8,128)(2,1)S(1)} %fusion.3), channel_id=1, source_target_pairs={{0,8},{2,10},{4,12},{6,14},{8,0},{10,2},{12,4},{14,6},{1,9},{3,11}... | collective-permute-start | bytes 589832 | tf_op jit(solution)/shard_map/ppermute | solution.py:224
  100.3 1.4 %collective-permute-start.29 = (bf16[128,512]{1,0:T(8,128)(2,1)S(1)}, bf16[128,512]{1,0:T(8,128)(2,1)S(1)}, u32[]{:S(2)}, u32[]{:S(2)}) collective-permute-start(bf16[128,512]{1,0:T(8,128)(2,1)S(1)} %get-tuple-element.40), channel_id=1, source_target_pairs={{0,1},{1,0},{2,3},{3,2},{4,5},{5,4},{6,7},{7,6},{8,9},{9,8},{10,11... | collective-permute-start | bytes 393224 | tf_op jit(solution)/shard_map/ppermute | solution.py:214

commit v4 on v3

--- a/solution.py
+++ b/solution.py
@@ -20,7 +20,7 @@
 SMEM = pl.BlockSpec(memory_space=pltpu.SMEM)
 
 
-def call(kernel, name, outs, scalars, arrays, scratch=(), vmem_mib=24, cost=None):
+def call(kernel, name, outs, scalars, arrays, scratch=(), vmem_mib=12, cost=None):
     return pl.pallas_call(
         kernel,
         out_shape=tuple(jax.ShapeDtypeStruct(*out) for out in outs),
@@ -238,6 +238,7 @@
         in_specs=[anywhere, anywhere],
         out_specs=anywhere,
         input_output_aliases={0: 0},
+        compiler_params=pltpu.CompilerParams(vmem_limit_bytes=2**20),
         name="after",
     )(value, first)
 
@@ -306,7 +307,7 @@
         p2 = swap(p)
         q2 = swap(q)
         if at >= 2:
-            q2 = after(q2, halves[at - 2])
+            q2 = after(q2, wholes[at - 2])
         kept, sent = call(
             expert_kernel,
             "expert",
@@ -314,7 +315,7 @@
             [core],
             [p, q, p2, q2, fc_in, fc_out],
             scratch=[pltpu.VMEM((2 * capacity, width), jnp.bfloat16)],
-            vmem_mib=32,
+            vmem_mib=16,
         )
         kepts.append(kept)
         both = kept + swap(sent).astype(jnp.float32)

time: 103 us -> 90.2 us (0.88)
  waiting for transfers between devices: 30.4 us -> 46.9 us
  local copies, waits for them, and re-layouts: 21.9 us -> 8.33 us
  starting transfers between devices: 26.4 us -> 19.2 us
  Pallas kernels: 17.4 us -> 12.8 us
  other arithmetic: 5.49 us -> 1.64 us
    unnamed x66 -> x24, local copies, waits for them, and re-layouts: 20.2 us -> 8.23 us
    ppermute x6, waiting for transfers between devices: 13.5 us -> 23 us  [shift(): lax.ppermute(values, 'expert', [(i, (i + 2 * offset) % owners) for i in r...]
    ppermute x6, starting transfers between devices: 14.1 us -> 4.85 us  [shift(): lax.ppermute(values, 'expert', [(i, (i + 2 * offset) % owners) for i in r...]
    ppermute x8, waiting for transfers between devices: 14.1 us -> 19.1 us  [swap_owner(): return lax.ppermute(values, 'expert', [(i, i ^ 1) for i in range(owners)])]
    pallas_call x8, Pallas kernels: 17.4 us -> 12.8 us  [call(): pl.pallas_call(kernel, out_shape=tuple((jax.ShapeDtypeStruct(*out) for ou...]
    ppermute x16, waiting for transfers between devices: 2.73 us -> 4.85 us  [swap(): return lax.ppermute(values, 'section', [(0, 1), (1, 0)])]
    ppermute x8, starting transfers between devices: 9.18 us -> 11.2 us  [swap_owner(): return lax.ppermute(values, 'expert', [(i, i ^ 1) for i in range(owners)])]
    add x4, other arithmetic: 2.42 us -> 0.43 us  [line_experts(): both = kept + swap(sent).astype(jnp.float32)]
  transfers between devices with their start and end apart: 30 -> 30, of which waited for: 10 -> 15; matrix products, arithmetic and copies ran while one was open for 6% -> 1% of each run, Pallas kernels for 11% -> 8%
where the time goes in v4:
time: 90.2 us; the launch traced here: 89.8 us
  waiting for transfers between devices  46.9 us (52%)
  starting transfers between devices  19.2 us (21%)
  Pallas kernels  12.8 us (14%)
  local copies, waits for them, and re-layouts  8.33 us (9%)
  other arithmetic  1.64 us (2%)
    ppermute x6, waiting for transfers between devices, shift(): lax.ppermute(values, 'expert', [(i, (i + 2 * offset) % owners) for i in r...  23 us
    ppermute x8, waiting for transfers between devices, swap_owner(): return lax.ppermute(values, 'expert', [(i, i ^ 1) for i in range(owners)])  19.1 us
    pallas_call x8, Pallas kernels, call(): pl.pallas_call(kernel, out_shape=tuple((jax.ShapeDtypeStruct(*out) for ou...  12.8 us
    ppermute x8, starting transfers between devices, swap_owner(): return lax.ppermute(values, 'expert', [(i, i ^ 1) for i in range(owners)])  11.2 us
    unnamed x24, local copies, waits for them, and re-layouts  8.23 us
    ppermute x16, waiting for transfers between devices, swap(): return lax.ppermute(values, 'section', [(0, 1), (1, 0)])  4.85 us
    ppermute x6, starting transfers between devices, shift(): lax.ppermute(values, 'expert', [(i, (i + 2 * offset) % owners) for i in r...  4.85 us
    ppermute x16, starting transfers between devices, swap(): return lax.ppermute(values, 'section', [(0, 1), (1, 0)])  3.2 us
  transfers between devices with their start and end apart: 30, of which 15 were waited for; matrix products, arithmetic and copies ran while one was open for 1% of the time, Pallas kernels for 8%

profile of v4, /device:TPU:0, one launch (start us, length us, event | category | flops | bytes accessed | tf_op | source)
XLA Modules:
  0.0 89.8 jit_solution(8487795507356160299)
XLA Ops:
  0.0 1.0 %fusion.13 = (bf16[2,80,512]{2,1,0:T(8,128)(2,1)S(1)}, bf16[2,80,512]{2,1,0:T(8,128)(2,1)S(1)}) fusion(s32[]{:T(128)S(6)} %select_n.13, bf16[2,1,80,512]{3,2,0,1:T(8,128)(2,1)} %bitcast.53, bf16[2,1,80,512]{3,2,0,1:T(8,128)(2,1)} %bitcast.54, s32[]{:T(128)S(6)} %select_n.12), kind=kLoop, calls=%fused_computation.29 | loop fusion | flops 163840 | bytes 655368 | tf_op jit(solution)/shard_map/jit(dynamic_index_in_dim)/squeeze | solution.py:257
  1.0 0.5 collective-permute-start
  2.2 0.4 collective-permute-done.other_ref
  2.6 0.9 %copy-done.4 = bf16[1,128,1024]{2,1,0:T(8,128)(2,1)S(1)} copy-done((bf16[1,128,1024]{2,1,0:T(8,128)(2,1)S(1)}, bf16[1,128,1024]{2,1,0:T(8,128)(2,1)}, u32[]{:S(2)}) %copy-start.4) | copy-done | bytes 262168
  3.5 0.7 copy-done.5
  4.2 0.7 copy-done.8
  4.9 0.7 copy-done.9
  5.6 0.7 copy-done.10
  6.3 0.7 copy-done.11
  6.9 3.2 %attend.1 = (bf16[128,1024]{1,0:T(8,128)(2,1)S(1)}, bf16[128,512]{1,0:T(8,128)(2,1)S(1)}, bf16[128,512]{1,0:T(8,128)(2,1)S(1)}, f32[2,128]{1,0:T(2,128)S(1)}) custom-call(s32[1]{0:T(128)} %bitcast.core_ref, s32[1]{0:T(128)S(6)} %copy.20.source_ref, s32[2]{0:T(128)S(1)} %copy-done.11, bf16[128,1024]{1,0:T(8,128)(2,1)S(1)} %bitcast.46, ...), custom_call_target="tpu_custom_call" | custom-call | tf_op jit(solution)/shard_map/attend/pallas_call | solution.py:24
  10.2 0.4 collective-permute-start.2
  10.6 1.0 %collective-permute-done.2.other_ref = bf16[128,512]{1,0:T(8,128)(2,1)S(1)} collective-permute-done((bf16[128,512]{1,0:T(8,128)(2,1)S(1)}, bf16[128,512]{1,0:T(8,128)(2,1)S(1)}, u32[]{:S(2)}, u32[]{:S(2)}) %collective-permute-start.2) | collective-permute-done | bytes 131104 | tf_op jit(solution)/shard_map/ppermute | solution.py:214
  11.6 0.7 copy-done.6
  12.3 0.5 select.5
  12.8 2.9 %collective-permute-start.3 = (bf16[192,512]{1,0:T(8,128)(2,1)S(1)}, bf16[192,512]{1,0:T(8,128)(2,1)S(1)}, u32[]{:S(2)}, u32[]{:S(2)}) collective-permute-start(bf16[192,512]{1,0:T(8,128)(2,1)S(1)} %get-tuple-element.27.p_ref), channel_id=1, source_target_pairs={{0,2},{2,0},{4,6},{6,4},{8,10},{10,8},{12,14},{14,12},{1,3},{3,1},... | collective-permute-start | bytes 589832 | tf_op jit(solution)/shard_map/ppermute | solution.py:219
  15.7 1.6 %collective-permute-start.8 = (bf16[192,512]{1,0:T(8,128)(2,1)S(1)}, bf16[192,512]{1,0:T(8,128)(2,1)S(1)}, u32[]{:S(2)}, u32[]{:S(2)}) collective-permute-start(bf16[192,512]{1,0:T(8,128)(2,1)S(1)} %get-tuple-element.30), channel_id=1, source_target_pairs={{0,4},{2,6},{4,8},{6,10},{8,12},{10,14},{12,0},{14,2},{1,5},{3,7},... | collective-permute-start | bytes 589832 | tf_op jit(solution)/shard_map/ppermute | solution.py:224
  17.3 3.6 %collective-permute-done.3.q_ref = bf16[192,512]{1,0:T(8,128)(2,1)S(1)} collective-permute-done((bf16[192,512]{1,0:T(8,128)(2,1)S(1)}, bf16[192,512]{1,0:T(8,128)(2,1)S(1)}, u32[]{:S(2)}, u32[]{:S(2)}) %collective-permute-start.3) | collective-permute-done | bytes 196640 | tf_op jit(solution)/shard_map/ppermute | solution.py:219
  21.0 3.3 %collective-permute-done.8.p_ref = bf16[192,512]{1,0:T(8,128)(2,1)S(1)} collective-permute-done((bf16[192,512]{1,0:T(8,128)(2,1)S(1)}, bf16[192,512]{1,0:T(8,128)(2,1)S(1)}, u32[]{:S(2)}, u32[]{:S(2)}) %collective-permute-start.8) | collective-permute-done | bytes 196640 | tf_op jit(solution)/shard_map/ppermute | solution.py:224
  24.3 0.5 collective-permute-start.9
  24.8 1.7 %collective-permute-start.22 = (bf16[192,512]{1,0:T(8,128)(2,1)S(1)}, bf16[192,512]{1,0:T(8,128)(2,1)S(1)}, u32[]{:S(2)}, u32[]{:S(2)}) collective-permute-start(bf16[192,512]{1,0:T(8,128)(2,1)S(1)} %get-tuple-element.36), channel_id=1, source_target_pairs={{0,12},{2,14},{4,0},{6,2},{8,4},{10,6},{12,8},{14,10},{1,13},{3,15... | collective-permute-start | bytes 589832 | tf_op jit(solution)/shard_map/ppermute | solution.py:224
  26.6 1.6 %copy-done = bf16[1024,1024]{1,0:T(8,128)(2,1)S(1)} copy-done((bf16[1024,1024]{1,0:T(8,128)(2,1)S(1)}, bf16[1024,1024]{1,0:T(8,128)(2,1)}, u32[]{:S(2)}) %copy-start) | copy-done | bytes 2097176
  28.1 1.6 %copy-done.2 = bf16[1024,1024]{1,0:T(8,128)(2,1)S(1)} copy-done((bf16[1024,1024]{1,0:T(8,128)(2,1)S(1)}, bf16[1024,1024]{1,0:T(8,128)(2,1)}, u32[]{:S(2)}) %copy-start.2) | copy-done | bytes 2097176
  29.7 1.8 %expert.4 = (f32[2,192,512]{2,1,0:T(8,128)S(1)}, bf16[2,192,512]{2,1,0:T(8,128)(2,1)S(1)}) custom-call(s32[1]{0:T(128)} %bitcast.core_ref, bf16[192,512]{1,0:T(8,128)(2,1)S(1)} %get-tuple-element.27.p_ref, bf16[192,512]{1,0:T(8,128)(2,1)S(1)} %collective-permute-done.3.q_ref, bf16[192,512]{1,0:T(8,128)(2,1)S(1)} %collective-permute-done.4.p2_ref, ...), custom_call_target="tpu_custom_call" | custom-call | tf_op jit(solution)/shard_map/expert/pallas_call | solution.py:24
  31.6 0.1 collective-permute-start.6
  31.7 0.5 collective-permute-start.10
  32.2 0.1 collective-permute-start.11
  32.3 1.6 %collective-permute-start.23 = (bf16[192,512]{1,0:T(8,128)(2,1)S(1)}, bf16[192,512]{1,0:T(8,128)(2,1)S(1)}, u32[]{:S(2)}, u32[]{:S(2)}) collective-permute-start(bf16[192,512]{1,0:T(8,128)(2,1)S(1)} %after.6.p_ref), channel_id=1, source_target_pairs={{0,2},{2,0},{4,6},{6,4},{8,10},{10,8},{12,14},{14,12},{1,3},{3,1},... | collective-permute-start | bytes 589832 | tf_op jit(solution)/shard_map/ppermute | solution.py:219
  33.8 0.1 collective-permute-start.24
  33.9 1.8 %expert.5 = (f32[2,192,512]{2,1,0:T(8,128)S(1)}, bf16[2,192,512]{2,1,0:T(8,128)(2,1)S(1)}) custom-call(s32[1]{0:T(128)} %bitcast.core_ref, bf16[192,512]{1,0:T(8,128)(2,1)S(1)} %collective-permute-done.8.p_ref, bf16[192,512]{1,0:T(8,128)(2,1)S(1)} %collective-permute-done.9.q_ref, bf16[192,512]{1,0:T(8,128)(2,1)S(1)} %collective-permute-done.10.p2_ref, ...), custom_call_target="tpu_custom_call" | custom-call | tf_op jit(solution)/shard_map/expert/pallas_call | solution.py:24
  35.8 8.5 %collective-permute-done.15.value_ref = bf16[192,512]{1,0:T(8,128)(2,1)S(1)} collective-permute-done((bf16[192,512]{1,0:T(8,128)(2,1)S(1)}, bf16[192,512]{1,0:T(8,128)(2,1)S(1)}, u32[]{:S(2)}, u32[]{:S(2)}) %collective-permute-start.15) | collective-permute-done | bytes 196640 | tf_op jit(solution)/shard_map/ppermute | solution.py:224
  44.3 1.5 %collective-permute-start.16 = (bf16[192,512]{1,0:T(8,128)(2,1)S(1)}, bf16[192,512]{1,0:T(8,128)(2,1)S(1)}, u32[]{:S(2)}, u32[]{:S(2)}) collective-permute-start(bf16[192,512]{1,0:T(8,128)(2,1)S(1)} %after.4.p_ref), channel_id=1, source_target_pairs={{0,2},{2,0},{4,6},{6,4},{8,10},{10,8},{12,14},{14,12},{1,3},{3,1},... | collective-permute-start | bytes 589832 | tf_op jit(solution)/shard_map/ppermute | solution.py:219
  45.8 0.5 collective-permute-start.25
  46.3 0.1 convert_add_fusion.3
  46.5 0.6 collective-permute-start.7
  47.1 0.5 collective-permute-done.12
  47.6 0.1 convert_add_fusion.2
  47.7 1.1 %collective-permute-start.13 = (bf16[192,512]{1,0:T(8,128)(2,1)S(1)}, bf16[192,512]{1,0:T(8,128)(2,1)S(1)}, u32[]{:S(2)}, u32[]{:S(2)}) collective-permute-start(bf16[192,512]{1,0:T(8,128)(2,1)S(1)} %fusion.9), channel_id=1, source_target_pairs={{0,2},{2,0},{4,6},{6,4},{8,10},{10,8},{12,14},{14,12},{1,3},{3,1},... | collective-permute-start | bytes 589832 | tf_op jit(solution)/shard_map/ppermute | solution.py:219
  48.8 7.5 %collective-permute-done.7 = bf16[192,512]{1,0:T(8,128)(2,1)S(1)} collective-permute-done((bf16[192,512]{1,0:T(8,128)(2,1)S(1)}, bf16[192,512]{1,0:T(8,128)(2,1)S(1)}, u32[]{:S(2)}, u32[]{:S(2)}) %collective-permute-start.7) | collective-permute-done | bytes 196640 | tf_op jit(solution)/shard_map/ppermute | solution.py:219
  56.4 1.8 %expert.7 = (f32[2,192,512]{2,1,0:T(8,128)S(1)}, bf16[2,192,512]{2,1,0:T(8,128)(2,1)S(1)}) custom-call(s32[1]{0:T(128)} %bitcast.core_ref, bf16[192,512]{1,0:T(8,128)(2,1)S(1)} %after.6.p_ref, bf16[192,512]{1,0:T(8,128)(2,1)S(1)} %collective-permute-done.23.q_ref, bf16[192,512]{1,0:T(8,128)(2,1)S(1)} %collective-permute-done.24.p2_ref, ...), custom_call_target="tpu_custom_call" | custom-call | tf_op jit(solution)/shard_map/expert/pallas_call | solution.py:24
  58.2 0.1 collective-permute-start.26
  58.3 0.5 collective-permute-start.17
  58.8 0.1 collective-permute-start.18
  58.9 0.7 collective-permute-done.13
  59.7 0.4 collective-permute-start.14
  60.1 0.5 collective-permute-done.18.value_ref
  60.6 1.8 %expert.6 = (f32[2,192,512]{2,1,0:T(8,128)S(1)}, bf16[2,192,512]{2,1,0:T(8,128)(2,1)S(1)}) custom-call(s32[1]{0:T(128)} %bitcast.core_ref, bf16[192,512]{1,0:T(8,128)(2,1)S(1)} %after.4.p_ref, bf16[192,512]{1,0:T(8,128)(2,1)S(1)} %collective-permute-done.16.q_ref, bf16[192,512]{1,0:T(8,128)(2,1)S(1)} %collective-permute-done.17.p2_ref, ...), custom_call_target="tpu_custom_call" | custom-call | tf_op jit(solution)/shard_map/expert/pallas_call | solution.py:24
  62.4 0.2 collective-permute-start.19
  62.6 0.1 convert_add_fusion
  62.8 1.6 %collective-permute-start.27 = (bf16[192,512]{1,0:T(8,128)(2,1)S(1)}, bf16[192,512]{1,0:T(8,128)(2,1)S(1)}, u32[]{:S(2)}, u32[]{:S(2)}) collective-permute-start(bf16[192,512]{1,0:T(8,128)(2,1)S(1)} %fusion.11), channel_id=1, source_target_pairs={{0,2},{2,0},{4,6},{6,4},{8,10},{10,8},{12,14},{14,12},{1,3},{3,1},... | collective-permute-start | bytes 589832 | tf_op jit(solution)/shard_map/ppermute | solution.py:219
  64.4 0.1 convert_add_fusion.1
  64.5 1.4 %collective-permute-start.20 = (bf16[192,512]{1,0:T(8,128)(2,1)S(1)}, bf16[192,512]{1,0:T(8,128)(2,1)S(1)}, u32[]{:S(2)}, u32[]{:S(2)}) collective-permute-start(bf16[192,512]{1,0:T(8,128)(2,1)S(1)} %fusion.10), channel_id=1, source_target_pairs={{0,2},{2,0},{4,6},{6,4},{8,10},{10,8},{12,14},{14,12},{1,3},{3,1},... | collective-permute-start | bytes 589832 | tf_op jit(solution)/shard_map/ppermute | solution.py:219
  65.9 4.7 %collective-permute-done.27 = bf16[192,512]{1,0:T(8,128)(2,1)S(1)} collective-permute-done((bf16[192,512]{1,0:T(8,128)(2,1)S(1)}, bf16[192,512]{1,0:T(8,128)(2,1)S(1)}, u32[]{:S(2)}, u32[]{:S(2)}) %collective-permute-start.27) | collective-permute-done | bytes 196640 | tf_op jit(solution)/shard_map/ppermute | solution.py:219
  70.6 1.1 %collective-permute-start.28 = (bf16[192,512]{1,0:T(8,128)(2,1)S(1)}, bf16[192,512]{1,0:T(8,128)(2,1)S(1)}, u32[]{:S(2)}, u32[]{:S(2)}) collective-permute-start(bf16[192,512]{1,0:T(8,128)(2,1)S(1)} %fusion.1), channel_id=1, source_target_pairs={{0,4},{2,6},{4,8},{6,10},{8,12},{10,14},{12,0},{14,2},{1,5},{3,7},... | collective-permute-start | bytes 589832 | tf_op jit(solution)/shard_map/ppermute | solution.py:224
  71.7 2.5 %collective-permute-done.20 = bf16[192,512]{1,0:T(8,128)(2,1)S(1)} collective-permute-done((bf16[192,512]{1,0:T(8,128)(2,1)S(1)}, bf16[192,512]{1,0:T(8,128)(2,1)S(1)}, u32[]{:S(2)}, u32[]{:S(2)}) %collective-permute-start.20) | collective-permute-done | bytes 196640 | tf_op jit(solution)/shard_map/ppermute | solution.py:219
  74.3 0.1 fusion.3
  74.3 0.1 collective-permute-start.21
  74.4 0.1 collective-permute-start.1
  74.5 1.1 %collective-permute-done.1.other_gates_ref = f32[2,128]{1,0:T(2,128)S(1)} collective-permute-done((f32[2,128]{1,0:T(2,128)S(1)}, f32[2,128]{1,0:T(2,128)S(1)}, u32[]{:S(2)}, u32[]{:S(2)}) %collective-permute-start.1) | collective-permute-done | bytes 1056 | tf_op jit(solution)/shard_map/ppermute | solution.py:214
  75.6 2.8 %collective-permute-done.28.rest_3_ = bf16[192,512]{1,0:T(8,128)(2,1)S(1)} collective-permute-done((bf16[192,512]{1,0:T(8,128)(2,1)S(1)}, bf16[192,512]{1,0:T(8,128)(2,1)S(1)}, u32[]{:S(2)}, u32[]{:S(2)}) %collective-permute-start.28) | collective-permute-done | bytes 196640 | tf_op jit(solution)/shard_map/ppermute | solution.py:224
  78.4 8.3 %collective-permute-done.21.rest_2_ = bf16[192,512]{1,0:T(8,128)(2,1)S(1)} collective-permute-done((bf16[192,512]{1,0:T(8,128)(2,1)S(1)}, bf16[192,512]{1,0:T(8,128)(2,1)S(1)}, u32[]{:S(2)}, u32[]{:S(2)}) %collective-permute-start.21) | collective-permute-done | bytes 196640 | tf_op jit(solution)/shard_map/ppermute | solution.py:224
  86.7 0.9 %combine.1 = (f32[128,512]{1,0:T(8,128)S(1)}, bf16[128,512]{1,0:T(8,128)(2,1)S(1)}) custom-call(s32[1]{0:T(128)} %bitcast.core_ref, s32[1]{0:T(128)} %bitcast.10.line_ref, s32[2,2,128]{2,1,0:T(2,128)S(1)} %bitcast.49, f32[2,128]{1,0:T(2,128)S(1)} %get-tuple-element.24.own_gates_ref, f32[2,128]{1,0:T(2,128)S(1)} %collective-permute-done.1.other_gates_ref, ...), custom_call_target="tpu_custom_call" | custom-call | tf_op jit(solution)/shard_map/combine/pallas_call | solution.py:24
  87.7 0.1 collective-permute-start.29
  87.7 1.3 %collective-permute-done.29.other_ref = bf16[128,512]{1,0:T(8,128)(2,1)S(1)} collective-permute-done((bf16[128,512]{1,0:T(8,128)(2,1)S(1)}, bf16[128,512]{1,0:T(8,128)(2,1)S(1)}, u32[]{:S(2)}, u32[]{:S(2)}) %collective-permute-start.29) | collective-permute-done | bytes 131104 | tf_op jit(solution)/shard_map/ppermute | solution.py:214
  89.1 0.8 finish.1
  (45 shorter events, 0.3 us)
Async XLA Ops:
  1.0 1.5 %collective-permute-start = (bf16[2,80,512]{2,1,0:T(8,128)(2,1)S(1)}, bf16[2,80,512]{2,1,0:T(8,128)(2,1)S(1)}, u32[]{:S(2)}, u32[]{:S(2)}) collective-permute-start(bf16[2,80,512]{2,1,0:T(8,128)(2,1)S(1)} %get-tuple-element.41), channel_id=1, source_target_pairs={{0,1},{1,0},{2,3},{3,2},{4,5},{5,4},{6,7},{7,6},{8,9},{9,8},{10,11... | collective-permute-start | bytes 491528 | tf_op jit(solution)/shard_map/ppermute | solution.py:214
  2.6 0.9 %copy-start.4 = (bf16[1,128,1024]{2,1,0:T(8,128)(2,1)S(1)}, bf16[1,128,1024]{2,1,0:T(8,128)(2,1)}, u32[]{:S(2)}) copy-start(bf16[1,128,1024]{2,1,0:T(8,128)(2,1)} %param.11) | copy-start | bytes 786436
  3.5 0.7 copy-start.5
  4.2 0.7 copy-start.8
  4.9 0.7 copy-start.9
  5.6 0.7 copy-start.10
  6.3 0.7 copy-start.11
  10.2 1.4 %collective-permute-start.2 = (bf16[128,512]{1,0:T(8,128)(2,1)S(1)}, bf16[128,512]{1,0:T(8,128)(2,1)S(1)}, u32[]{:S(2)}, u32[]{:S(2)}) collective-permute-start(bf16[128,512]{1,0:T(8,128)(2,1)S(1)} %get-tuple-element.26), channel_id=1, source_target_pairs={{0,1},{1,0},{2,3},{3,2},{4,5},{5,4},{6,7},{7,6},{8,9},{9,8},{10,11... | collective-permute-start | bytes 393224 | tf_op jit(solution)/shard_map/ppermute | solution.py:214
  11.6 0.7 copy-start.6
  12.8 8.1 %collective-permute-start.3 = (bf16[192,512]{1,0:T(8,128)(2,1)S(1)}, bf16[192,512]{1,0:T(8,128)(2,1)S(1)}, u32[]{:S(2)}, u32[]{:S(2)}) collective-permute-start(bf16[192,512]{1,0:T(8,128)(2,1)S(1)} %get-tuple-element.27.p_ref), channel_id=1, source_target_pairs={{0,2},{2,0},{4,6},{6,4},{8,10},{10,8},{12,14},{14,12},{1,3},{3,1},... | collective-permute-start | bytes 589832 | tf_op jit(solution)/shard_map/ppermute | solution.py:219
  15.7 8.5 %collective-permute-start.8 = (bf16[192,512]{1,0:T(8,128)(2,1)S(1)}, bf16[192,512]{1,0:T(8,128)(2,1)S(1)}, u32[]{:S(2)}, u32[]{:S(2)}) collective-permute-start(bf16[192,512]{1,0:T(8,128)(2,1)S(1)} %get-tuple-element.30), channel_id=1, source_target_pairs={{0,4},{2,6},{4,8},{6,10},{8,12},{10,14},{12,0},{14,2},{1,5},{3,7},... | collective-permute-start | bytes 589832 | tf_op jit(solution)/shard_map/ppermute | solution.py:224
  17.3 9.2 %collective-permute-start.4 = (bf16[192,512]{1,0:T(8,128)(2,1)S(1)}, bf16[192,512]{1,0:T(8,128)(2,1)S(1)}, u32[]{:S(2)}, u32[]{:S(2)}) collective-permute-start(bf16[192,512]{1,0:T(8,128)(2,1)S(1)} %get-tuple-element.27.p_ref), channel_id=1, source_target_pairs={{0,1},{1,0},{2,3},{3,2},{4,5},{5,4},{6,7},{7,6},{8,9},{9,8},{10,11... | collective-permute-start | bytes 589832 | tf_op jit(solution)/shard_map/ppermute | solution.py:214
  21.0 5.6 %collective-permute-start.5 = (bf16[192,512]{1,0:T(8,128)(2,1)S(1)}, bf16[192,512]{1,0:T(8,128)(2,1)S(1)}, u32[]{:S(2)}, u32[]{:S(2)}) collective-permute-start(bf16[192,512]{1,0:T(8,128)(2,1)S(1)} %collective-permute-done.3.q_ref), channel_id=1, source_target_pairs={{0,1},{1,0},{2,3},{3,2},{4,5},{5,4},{6,7},{7,6},{8,9},{9,8},{10,11... | collective-permute-start | bytes 589832 | tf_op jit(solution)/shard_map/ppermute | solution.py:214
  24.3 7.9 %collective-permute-start.9 = (bf16[192,512]{1,0:T(8,128)(2,1)S(1)}, bf16[192,512]{1,0:T(8,128)(2,1)S(1)}, u32[]{:S(2)}, u32[]{:S(2)}) collective-permute-start(bf16[192,512]{1,0:T(8,128)(2,1)S(1)} %collective-permute-done.8.p_ref), channel_id=1, source_target_pairs={{0,2},{2,0},{4,6},{6,4},{8,10},{10,8},{12,14},{14,12},{1,3},{3,1},... | collective-permute-start | bytes 589832 | tf_op jit(solution)/shard_map/ppermute | solution.py:219
  24.8 7.5 %collective-permute-start.22 = (bf16[192,512]{1,0:T(8,128)(2,1)S(1)}, bf16[192,512]{1,0:T(8,128)(2,1)S(1)}, u32[]{:S(2)}, u32[]{:S(2)}) collective-permute-start(bf16[192,512]{1,0:T(8,128)(2,1)S(1)} %get-tuple-element.36), channel_id=1, source_target_pairs={{0,12},{2,14},{4,0},{6,2},{8,4},{10,6},{12,8},{14,10},{1,13},{3,15... | collective-permute-start | bytes 589832 | tf_op jit(solution)/shard_map/ppermute | solution.py:224
  26.6 1.6 %copy-start = (bf16[1024,1024]{1,0:T(8,128)(2,1)S(1)}, bf16[1024,1024]{1,0:T(8,128)(2,1)}, u32[]{:S(2)}) copy-start(bf16[1024,1024]{1,0:T(8,128)(2,1)} %in_ref.7) | copy-start | bytes 6291460
  28.1 1.6 %copy-start.2 = (bf16[1024,1024]{1,0:T(8,128)(2,1)S(1)}, bf16[1024,1024]{1,0:T(8,128)(2,1)}, u32[]{:S(2)}) copy-start(bf16[1024,1024]{1,0:T(8,128)(2,1)} %out_ref.7) | copy-start | bytes 6291460
  29.7 4.2 %copy-start.1 = (bf16[1024,1024]{1,0:T(8,128)(2,1)S(1)}, bf16[1024,1024]{1,0:T(8,128)(2,1)}, u32[]{:S(2)}) copy-start(bf16[1024,1024]{1,0:T(8,128)(2,1)} %in_ref.7) | copy-start | bytes 6291460
  29.7 4.2 %copy-start.3 = (bf16[1024,1024]{1,0:T(8,128)(2,1)S(1)}, bf16[1024,1024]{1,0:T(8,128)(2,1)}, u32[]{:S(2)}) copy-start(bf16[1024,1024]{1,0:T(8,128)(2,1)} %out_ref.7) | copy-start | bytes 6291460
  31.6 14.8 %collective-permute-start.6 = (bf16[2,192,512]{2,1,0:T(8,128)(2,1)S(1)}, bf16[2,192,512]{2,1,0:T(8,128)(2,1)S(1)}, u32[]{:S(2)}, u32[]{:S(2)}) collective-permute-start(bf16[2,192,512]{2,1,0:T(8,128)(2,1)S(1)} %get-tuple-element.29), channel_id=1, source_target_pairs={{0,1},{1,0},{2,3},{3,2},{4,5},{5,4},{6,7},{7,6},{8,9},{9,8},{10,11... | collective-permute-start | bytes 1179656 | tf_op jit(solution)/shard_map/ppermute | solution.py:214
  31.7 2.2 %collective-permute-start.10 = (bf16[192,512]{1,0:T(8,128)(2,1)S(1)}, bf16[192,512]{1,0:T(8,128)(2,1)S(1)}, u32[]{:S(2)}, u32[]{:S(2)}) collective-permute-start(bf16[192,512]{1,0:T(8,128)(2,1)S(1)} %collective-permute-done.8.p_ref), channel_id=1, source_target_pairs={{0,1},{1,0},{2,3},{3,2},{4,5},{5,4},{6,7},{7,6},{8,9},{9,8},{10,11... | collective-permute-start | bytes 589832 | tf_op jit(solution)/shard_map/ppermute | solution.py:214
  32.2 1.8 %collective-permute-start.11 = (bf16[192,512]{1,0:T(8,128)(2,1)S(1)}, bf16[192,512]{1,0:T(8,128)(2,1)S(1)}, u32[]{:S(2)}, u32[]{:S(2)}) collective-permute-start(bf16[192,512]{1,0:T(8,128)(2,1)S(1)} %collective-permute-done.9.q_ref), channel_id=1, source_target_pairs={{0,1},{1,0},{2,3},{3,2},{4,5},{5,4},{6,7},{7,6},{8,9},{9,8},{10,11... | collective-permute-start | bytes 589832 | tf_op jit(solution)/shard_map/ppermute | solution.py:214
  32.2 12.1 %collective-permute-start.15 = (bf16[192,512]{1,0:T(8,128)(2,1)S(1)}, bf16[192,512]{1,0:T(8,128)(2,1)S(1)}, u32[]{:S(2)}, u32[]{:S(2)}) collective-permute-start(bf16[192,512]{1,0:T(8,128)(2,1)S(1)} %get-tuple-element.33), channel_id=1, source_target_pairs={{0,8},{2,10},{4,12},{6,14},{8,0},{10,2},{12,4},{14,6},{1,9},{3,11}... | collective-permute-start | bytes 589832 | tf_op jit(solution)/shard_map/ppermute | solution.py:224
  32.3 13.6 %collective-permute-start.23 = (bf16[192,512]{1,0:T(8,128)(2,1)S(1)}, bf16[192,512]{1,0:T(8,128)(2,1)S(1)}, u32[]{:S(2)}, u32[]{:S(2)}) collective-permute-start(bf16[192,512]{1,0:T(8,128)(2,1)S(1)} %after.6.p_ref), channel_id=1, source_target_pairs={{0,2},{2,0},{4,6},{6,4},{8,10},{10,8},{12,14},{14,12},{1,3},{3,1},... | collective-permute-start | bytes 589832 | tf_op jit(solution)/shard_map/ppermute | solution.py:219
  33.8 22.5 %collective-permute-start.24 = (bf16[192,512]{1,0:T(8,128)(2,1)S(1)}, bf16[192,512]{1,0:T(8,128)(2,1)S(1)}, u32[]{:S(2)}, u32[]{:S(2)}) collective-permute-start(bf16[192,512]{1,0:T(8,128)(2,1)S(1)} %after.6.p_ref), channel_id=1, source_target_pairs={{0,1},{1,0},{2,3},{3,2},{4,5},{5,4},{6,7},{7,6},{8,9},{9,8},{10,11... | collective-permute-start | bytes 589832 | tf_op jit(solution)/shard_map/ppermute | solution.py:214
  44.3 14.5 %collective-permute-start.16 = (bf16[192,512]{1,0:T(8,128)(2,1)S(1)}, bf16[192,512]{1,0:T(8,128)(2,1)S(1)}, u32[]{:S(2)}, u32[]{:S(2)}) collective-permute-start(bf16[192,512]{1,0:T(8,128)(2,1)S(1)} %after.4.p_ref), channel_id=1, source_target_pairs={{0,2},{2,0},{4,6},{6,4},{8,10},{10,8},{12,14},{14,12},{1,3},{3,1},... | collective-permute-start | bytes 589832 | tf_op jit(solution)/shard_map/ppermute | solution.py:219
  45.8 1.7 %collective-permute-start.12 = (bf16[2,192,512]{2,1,0:T(8,128)(2,1)S(1)}, bf16[2,192,512]{2,1,0:T(8,128)(2,1)S(1)}, u32[]{:S(2)}, u32[]{:S(2)}) collective-permute-start(bf16[2,192,512]{2,1,0:T(8,128)(2,1)S(1)} %get-tuple-element.32), channel_id=1, source_target_pairs={{0,1},{1,0},{2,3},{3,2},{4,5},{5,4},{6,7},{7,6},{8,9},{9,8},{10,11... | collective-permute-start | bytes 1179656 | tf_op jit(solution)/shard_map/ppermute | solution.py:214
  45.8 10.5 %collective-permute-start.25 = (bf16[192,512]{1,0:T(8,128)(2,1)S(1)}, bf16[192,512]{1,0:T(8,128)(2,1)S(1)}, u32[]{:S(2)}, u32[]{:S(2)}) collective-permute-start(bf16[192,512]{1,0:T(8,128)(2,1)S(1)} %collective-permute-done.23.q_ref), channel_id=1, source_target_pairs={{0,1},{1,0},{2,3},{3,2},{4,5},{5,4},{6,7},{7,6},{8,9},{9,8},{10,11... | collective-permute-start | bytes 589832 | tf_op jit(solution)/shard_map/ppermute | solution.py:214
  46.5 9.8 %collective-permute-start.7 = (bf16[192,512]{1,0:T(8,128)(2,1)S(1)}, bf16[192,512]{1,0:T(8,128)(2,1)S(1)}, u32[]{:S(2)}, u32[]{:S(2)}) collective-permute-start(bf16[192,512]{1,0:T(8,128)(2,1)S(1)} %fusion.8), channel_id=1, source_target_pairs={{0,2},{2,0},{4,6},{6,4},{8,10},{10,8},{12,14},{14,12},{1,3},{3,1},... | collective-permute-start | bytes 589832 | tf_op jit(solution)/shard_map/ppermute | solution.py:219
  47.7 11.9 %collective-permute-start.13 = (bf16[192,512]{1,0:T(8,128)(2,1)S(1)}, bf16[192,512]{1,0:T(8,128)(2,1)S(1)}, u32[]{:S(2)}, u32[]{:S(2)}) collective-permute-start(bf16[192,512]{1,0:T(8,128)(2,1)S(1)} %fusion.9), channel_id=1, source_target_pairs={{0,2},{2,0},{4,6},{6,4},{8,10},{10,8},{12,14},{14,12},{1,3},{3,1},... | collective-permute-start | bytes 589832 | tf_op jit(solution)/shard_map/ppermute | solution.py:219
  58.2 4.4 %collective-permute-start.26 = (bf16[2,192,512]{2,1,0:T(8,128)(2,1)S(1)}, bf16[2,192,512]{2,1,0:T(8,128)(2,1)S(1)}, u32[]{:S(2)}, u32[]{:S(2)}) collective-permute-start(bf16[2,192,512]{2,1,0:T(8,128)(2,1)S(1)} %get-tuple-element.38), channel_id=1, source_target_pairs={{0,1},{1,0},{2,3},{3,2},{4,5},{5,4},{6,7},{7,6},{8,9},{9,8},{10,11... | collective-permute-start | bytes 1179656 | tf_op jit(solution)/shard_map/ppermute | solution.py:214
  58.3 2.3 %collective-permute-start.17 = (bf16[192,512]{1,0:T(8,128)(2,1)S(1)}, bf16[192,512]{1,0:T(8,128)(2,1)S(1)}, u32[]{:S(2)}, u32[]{:S(2)}) collective-permute-start(bf16[192,512]{1,0:T(8,128)(2,1)S(1)} %after.4.p_ref), channel_id=1, source_target_pairs={{0,1},{1,0},{2,3},{3,2},{4,5},{5,4},{6,7},{7,6},{8,9},{9,8},{10,11... | collective-permute-start | bytes 589832 | tf_op jit(solution)/shard_map/ppermute | solution.py:214
  58.8 1.8 %collective-permute-start.18 = (bf16[192,512]{1,0:T(8,128)(2,1)S(1)}, bf16[192,512]{1,0:T(8,128)(2,1)S(1)}, u32[]{:S(2)}, u32[]{:S(2)}) collective-permute-start(bf16[192,512]{1,0:T(8,128)(2,1)S(1)} %collective-permute-done.16.q_ref), channel_id=1, source_target_pairs={{0,1},{1,0},{2,3},{3,2},{4,5},{5,4},{6,7},{7,6},{8,9},{9,8},{10,11... | collective-permute-start | bytes 589832 | tf_op jit(solution)/shard_map/ppermute | solution.py:214
  59.7 15.9 %collective-permute-start.14 = (bf16[192,512]{1,0:T(8,128)(2,1)S(1)}, bf16[192,512]{1,0:T(8,128)(2,1)S(1)}, u32[]{:S(2)}, u32[]{:S(2)}) collective-permute-start(bf16[192,512]{1,0:T(8,128)(2,1)S(1)} %fusion.5.first_ref), channel_id=1, source_target_pairs={{0,12},{2,14},{4,0},{6,2},{8,4},{10,6},{12,8},{14,10},{1,13},{3,15... | collective-permute-start | bytes 589832 | tf_op jit(solution)/shard_map/ppermute | solution.py:224
  62.4 1.9 %collective-permute-start.19 = (bf16[2,192,512]{2,1,0:T(8,128)(2,1)S(1)}, bf16[2,192,512]{2,1,0:T(8,128)(2,1)S(1)}, u32[]{:S(2)}, u32[]{:S(2)}) collective-permute-start(bf16[2,192,512]{2,1,0:T(8,128)(2,1)S(1)} %get-tuple-element.35), channel_id=1, source_target_pairs={{0,1},{1,0},{2,3},{3,2},{4,5},{5,4},{6,7},{7,6},{8,9},{9,8},{10,11... | collective-permute-start | bytes 1179656 | tf_op jit(solution)/shard_map/ppermute | solution.py:214
  62.8 24.0 %copy-start.7 = (s32[2,128,2]{1,2,0:T(2,128)S(1)}, s32[2,128,2]{1,2,0:T(2,128)}, u32[]{:S(2)}) copy-start(s32[2,128,2]{1,2,0:T(2,128)} %param.16) | copy-start | bytes 6148
  62.8 7.8 %collective-permute-start.27 = (bf16[192,512]{1,0:T(8,128)(2,1)S(1)}, bf16[192,512]{1,0:T(8,128)(2,1)S(1)}, u32[]{:S(2)}, u32[]{:S(2)}) collective-permute-start(bf16[192,512]{1,0:T(8,128)(2,1)S(1)} %fusion.11), channel_id=1, source_target_pairs={{0,2},{2,0},{4,6},{6,4},{8,10},{10,8},{12,14},{14,12},{1,3},{3,1},... | collective-permute-start | bytes 589832 | tf_op jit(solution)/shard_map/ppermute | solution.py:219
  64.5 9.7 %collective-permute-start.20 = (bf16[192,512]{1,0:T(8,128)(2,1)S(1)}, bf16[192,512]{1,0:T(8,128)(2,1)S(1)}, u32[]{:S(2)}, u32[]{:S(2)}) collective-permute-start(bf16[192,512]{1,0:T(8,128)(2,1)S(1)} %fusion.10), channel_id=1, source_target_pairs={{0,2},{2,0},{4,6},{6,4},{8,10},{10,8},{12,14},{14,12},{1,3},{3,1},... | collective-permute-start | bytes 589832 | tf_op jit(solution)/shard_map/ppermute | solution.py:219
  70.6 7.8 %collective-permute-start.28 = (bf16[192,512]{1,0:T(8,128)(2,1)S(1)}, bf16[192,512]{1,0:T(8,128)(2,1)S(1)}, u32[]{:S(2)}, u32[]{:S(2)}) collective-permute-start(bf16[192,512]{1,0:T(8,128)(2,1)S(1)} %fusion.1), channel_id=1, source_target_pairs={{0,4},{2,6},{4,8},{6,10},{8,12},{10,14},{12,0},{14,2},{1,5},{3,7},... | collective-permute-start | bytes 589832 | tf_op jit(solution)/shard_map/ppermute | solution.py:224
  74.3 12.4 %collective-permute-start.21 = (bf16[192,512]{1,0:T(8,128)(2,1)S(1)}, bf16[192,512]{1,0:T(8,128)(2,1)S(1)}, u32[]{:S(2)}, u32[]{:S(2)}) collective-permute-start(bf16[192,512]{1,0:T(8,128)(2,1)S(1)} %fusion.3), channel_id=1, source_target_pairs={{0,8},{2,10},{4,12},{6,14},{8,0},{10,2},{12,4},{14,6},{1,9},{3,11}... | collective-permute-start | bytes 589832 | tf_op jit(solution)/shard_map/ppermute | solution.py:224
  74.4 1.2 %collective-permute-start.1 = (f32[2,128]{1,0:T(2,128)S(1)}, f32[2,128]{1,0:T(2,128)S(1)}, u32[]{:S(2)}, u32[]{:S(2)}) collective-permute-start(f32[2,128]{1,0:T(2,128)S(1)} %get-tuple-element.24.own_gates_ref), channel_id=1, source_target_pairs={{0,1},{1,0},{2,3},{3,2},{4,5},{5,4},{6,7},{7,6},{8,9},{9,8},{10,11... | collective-permute-start | bytes 3080 | tf_op jit(solution)/shard_map/ppermute | solution.py:214
  87.7 1.4 %collective-permute-start.29 = (bf16[128,512]{1,0:T(8,128)(2,1)S(1)}, bf16[128,512]{1,0:T(8,128)(2,1)S(1)}, u32[]{:S(2)}, u32[]{:S(2)}) collective-permute-start(bf16[128,512]{1,0:T(8,128)(2,1)S(1)} %get-tuple-element.40), channel_id=1, source_target_pairs={{0,1},{1,0},{2,3},{3,2},{4,5},{5,4},{6,7},{7,6},{8,9},{9,8},{10,11... | collective-permute-start | bytes 393224 | tf_op jit(solution)/shard_map/ppermute | solution.py:214

commit v5 on v4

--- a/solution.py
+++ b/solution.py
@@ -244,7 +244,7 @@
 
 
 def piece_order(count):
-    return sorted(range(count), key=lambda offset: min(offset, count - offset))
+    return sorted(range(count), key=lambda offset: (offset > 0, -min(offset, count - offset)))
 
 
 def attend(
@@ -301,9 +301,9 @@
     kepts, halves, wholes = [], [], []
     for at, offset in enumerate(piece_order(count)):
         p = travelling[offset - 1] if offset else selected[0]
+        q = swap_owner(p)
         if at >= 2:
-            p = after(p, kepts[at - 2])
-        q = swap_owner(p)
+            q = after(q, kepts[at - 2])
         p2 = swap(p)
         q2 = swap(q)
         if at >= 2:

time: 90.2 us -> 86.7 us (0.961)
  waiting for transfers between devices: 46.9 us -> 38.5 us
  starting transfers between devices: 19.2 us -> 24 us
    ppermute x6, starting transfers between devices: 4.85 us -> 10 us  [shift(): lax.ppermute(values, 'expert', [(i, (i + 2 * offset) % owners) for i in r...]
    ppermute x8, waiting for transfers between devices: 19.1 us -> 14.4 us  [swap_owner(): return lax.ppermute(values, 'expert', [(i, i ^ 1) for i in range(owners)])]
    ppermute x6, waiting for transfers between devices: 23 us -> 19.1 us  [shift(): lax.ppermute(values, 'expert', [(i, (i + 2 * offset) % owners) for i in r...]
  transfers between devices with their start and end apart: 30 -> 30, of which waited for: 15 -> 15; matrix products, arithmetic and copies ran while one was open for 1% -> 1% of each run, Pallas kernels for 8% -> 9%
where the time goes in v5:
time: 86.7 us; the launch traced here: 86.3 us
  waiting for transfers between devices  38.5 us (44%)
  starting transfers between devices  24 us (28%)
  Pallas kernels  12.8 us (15%)
  local copies, waits for them, and re-layouts  8.33 us (10%)
  other arithmetic  1.65 us (2%)
  between operations  0.91 us (1%)
    ppermute x6, waiting for transfers between devices, shift(): lax.ppermute(values, 'expert', [(i, (i + 2 * offset) % owners) for i in r...  19.1 us
    ppermute x8, waiting for transfers between devices, swap_owner(): return lax.ppermute(values, 'expert', [(i, i ^ 1) for i in range(owners)])  14.4 us
    pallas_call x8, Pallas kernels, call(): pl.pallas_call(kernel, out_shape=tuple((jax.ShapeDtypeStruct(*out) for ou...  12.8 us
    ppermute x8, starting transfers between devices, swap_owner(): return lax.ppermute(values, 'expert', [(i, i ^ 1) for i in range(owners)])  11 us
    ppermute x6, starting transfers between devices, shift(): lax.ppermute(values, 'expert', [(i, (i + 2 * offset) % owners) for i in r...  10 us
    unnamed x24, local copies, waits for them, and re-layouts  8.23 us
    ppermute x16, waiting for transfers between devices, swap(): return lax.ppermute(values, 'section', [(0, 1), (1, 0)])  4.97 us
    ppermute x16, starting transfers between devices, swap(): return lax.ppermute(values, 'section', [(0, 1), (1, 0)])  3.04 us
  transfers between devices with their start and end apart: 30, of which 15 were waited for; matrix products, arithmetic and copies ran while one was open for 1% of the time, Pallas kernels for 9%

profile of v5, /device:TPU:0, one launch (start us, length us, event | category | flops | bytes accessed | tf_op | source)
XLA Modules:
  0.0 86.3 jit_solution(144348362042897336)
XLA Ops:
  0.0 1.0 %fusion.13 = (bf16[2,80,512]{2,1,0:T(8,128)(2,1)S(1)}, bf16[2,80,512]{2,1,0:T(8,128)(2,1)S(1)}) fusion(s32[]{:T(128)S(6)} %select_n.13, bf16[2,1,80,512]{3,2,0,1:T(8,128)(2,1)} %bitcast.53, bf16[2,1,80,512]{3,2,0,1:T(8,128)(2,1)} %bitcast.54, s32[]{:T(128)S(6)} %select_n.12), kind=kLoop, calls=%fused_computation.29 | loop fusion | flops 163840 | bytes 655368 | tf_op jit(solution)/shard_map/jit(dynamic_index_in_dim)/squeeze | solution.py:257
  1.0 0.5 collective-permute-start
  2.2 0.4 collective-permute-done.other_ref
  2.6 0.9 %copy-done.4 = bf16[1,128,1024]{2,1,0:T(8,128)(2,1)S(1)} copy-done((bf16[1,128,1024]{2,1,0:T(8,128)(2,1)S(1)}, bf16[1,128,1024]{2,1,0:T(8,128)(2,1)}, u32[]{:S(2)}) %copy-start.4) | copy-done | bytes 262168
  3.5 0.7 copy-done.5
  4.2 0.7 copy-done.8
  4.9 0.7 copy-done.9
  5.6 0.7 copy-done.10
  6.3 0.7 copy-done.11
  6.9 3.2 %attend.1 = (bf16[128,1024]{1,0:T(8,128)(2,1)S(1)}, bf16[128,512]{1,0:T(8,128)(2,1)S(1)}, bf16[128,512]{1,0:T(8,128)(2,1)S(1)}, f32[2,128]{1,0:T(2,128)S(1)}) custom-call(s32[1]{0:T(128)} %bitcast.core_ref, s32[1]{0:T(128)S(6)} %copy.20.source_ref, s32[2]{0:T(128)S(1)} %copy-done.11, bf16[128,1024]{1,0:T(8,128)(2,1)S(1)} %bitcast.46, ...), custom_call_target="tpu_custom_call" | custom-call | tf_op jit(solution)/shard_map/attend/pallas_call | solution.py:24
  10.2 0.4 collective-permute-start.2
  10.6 1.0 %collective-permute-done.2.other_ref = bf16[128,512]{1,0:T(8,128)(2,1)S(1)} collective-permute-done((bf16[128,512]{1,0:T(8,128)(2,1)S(1)}, bf16[128,512]{1,0:T(8,128)(2,1)S(1)}, u32[]{:S(2)}, u32[]{:S(2)}) %collective-permute-start.2) | collective-permute-done | bytes 131104 | tf_op jit(solution)/shard_map/ppermute | solution.py:214
  11.6 0.7 copy-done.6
  12.3 0.5 select.5
  12.8 2.9 %collective-permute-start.3 = (bf16[192,512]{1,0:T(8,128)(2,1)S(1)}, bf16[192,512]{1,0:T(8,128)(2,1)S(1)}, u32[]{:S(2)}, u32[]{:S(2)}) collective-permute-start(bf16[192,512]{1,0:T(8,128)(2,1)S(1)} %get-tuple-element.27.p_ref), channel_id=1, source_target_pairs={{0,2},{2,0},{4,6},{6,4},{8,10},{10,8},{12,14},{14,12},{1,3},{3,1},... | collective-permute-start | bytes 589832 | tf_op jit(solution)/shard_map/ppermute | solution.py:219
  15.7 2.6 %collective-permute-start.15 = (bf16[192,512]{1,0:T(8,128)(2,1)S(1)}, bf16[192,512]{1,0:T(8,128)(2,1)S(1)}, u32[]{:S(2)}, u32[]{:S(2)}) collective-permute-start(bf16[192,512]{1,0:T(8,128)(2,1)S(1)} %get-tuple-element.33), channel_id=1, source_target_pairs={{0,8},{2,10},{4,12},{6,14},{8,0},{10,2},{12,4},{14,6},{1,9},{3,11}... | collective-permute-start | bytes 589832 | tf_op jit(solution)/shard_map/ppermute | solution.py:224
  18.3 2.6 %collective-permute-done.3.q_ref = bf16[192,512]{1,0:T(8,128)(2,1)S(1)} collective-permute-done((bf16[192,512]{1,0:T(8,128)(2,1)S(1)}, bf16[192,512]{1,0:T(8,128)(2,1)S(1)}, u32[]{:S(2)}, u32[]{:S(2)}) %collective-permute-start.3) | collective-permute-done | bytes 196640 | tf_op jit(solution)/shard_map/ppermute | solution.py:219
  21.0 1.8 %collective-permute-start.8 = (bf16[192,512]{1,0:T(8,128)(2,1)S(1)}, bf16[192,512]{1,0:T(8,128)(2,1)S(1)}, u32[]{:S(2)}, u32[]{:S(2)}) collective-permute-start(bf16[192,512]{1,0:T(8,128)(2,1)S(1)} %get-tuple-element.30), channel_id=1, source_target_pairs={{0,4},{2,6},{4,8},{6,10},{8,12},{10,14},{12,0},{14,2},{1,5},{3,7},... | collective-permute-start | bytes 589832 | tf_op jit(solution)/shard_map/ppermute | solution.py:224
  22.8 9.0 %collective-permute-done.15.p_ref = bf16[192,512]{1,0:T(8,128)(2,1)S(1)} collective-permute-done((bf16[192,512]{1,0:T(8,128)(2,1)S(1)}, bf16[192,512]{1,0:T(8,128)(2,1)S(1)}, u32[]{:S(2)}, u32[]{:S(2)}) %collective-permute-start.15) | collective-permute-done | bytes 196640 | tf_op jit(solution)/shard_map/ppermute | solution.py:224
  31.7 0.5 collective-permute-start.16
  32.2 1.6 %copy-done = bf16[1024,1024]{1,0:T(8,128)(2,1)S(1)} copy-done((bf16[1024,1024]{1,0:T(8,128)(2,1)S(1)}, bf16[1024,1024]{1,0:T(8,128)(2,1)}, u32[]{:S(2)}) %copy-start) | copy-done | bytes 2097176
  33.8 1.6 %copy-done.2 = bf16[1024,1024]{1,0:T(8,128)(2,1)S(1)} copy-done((bf16[1024,1024]{1,0:T(8,128)(2,1)S(1)}, bf16[1024,1024]{1,0:T(8,128)(2,1)}, u32[]{:S(2)}) %copy-start.2) | copy-done | bytes 2097176
  35.4 1.8 %expert.4 = (f32[2,192,512]{2,1,0:T(8,128)S(1)}, bf16[2,192,512]{2,1,0:T(8,128)(2,1)S(1)}) custom-call(s32[1]{0:T(128)} %bitcast.core_ref, bf16[192,512]{1,0:T(8,128)(2,1)S(1)} %get-tuple-element.27.p_ref, bf16[192,512]{1,0:T(8,128)(2,1)S(1)} %collective-permute-done.3.q_ref, bf16[192,512]{1,0:T(8,128)(2,1)S(1)} %collective-permute-done.4.p2_ref, ...), custom_call_target="tpu_custom_call" | custom-call | tf_op jit(solution)/shard_map/expert/pallas_call | solution.py:24
  37.3 0.1 collective-permute-start.6
  37.3 0.1 collective-permute-start.22
  37.4 1.6 %collective-permute-start.9 = (bf16[192,512]{1,0:T(8,128)(2,1)S(1)}, bf16[192,512]{1,0:T(8,128)(2,1)S(1)}, u32[]{:S(2)}, u32[]{:S(2)}) collective-permute-start(bf16[192,512]{1,0:T(8,128)(2,1)S(1)} %collective-permute-done.8.p_ref), channel_id=1, source_target_pairs={{0,2},{2,0},{4,6},{6,4},{8,10},{10,8},{12,14},{14,12},{1,3},{3,1},... | collective-permute-start | bytes 589832 | tf_op jit(solution)/shard_map/ppermute | solution.py:219
  39.0 0.1 collective-permute-start.17
  39.1 0.4 collective-permute-start.18
  39.6 5.1 %collective-permute-done.22.p_ref = bf16[192,512]{1,0:T(8,128)(2,1)S(1)} collective-permute-done((bf16[192,512]{1,0:T(8,128)(2,1)S(1)}, bf16[192,512]{1,0:T(8,128)(2,1)S(1)}, u32[]{:S(2)}, u32[]{:S(2)}) %collective-permute-start.22) | collective-permute-done | bytes 196640 | tf_op jit(solution)/shard_map/ppermute | solution.py:224
  44.6 1.5 %collective-permute-start.23 = (bf16[192,512]{1,0:T(8,128)(2,1)S(1)}, bf16[192,512]{1,0:T(8,128)(2,1)S(1)}, u32[]{:S(2)}, u32[]{:S(2)}) collective-permute-start(bf16[192,512]{1,0:T(8,128)(2,1)S(1)} %collective-permute-done.22.p_ref), channel_id=1, source_target_pairs={{0,2},{2,0},{4,6},{6,4},{8,10},{10,8},{12,14},{14,12},{1,3},{3,1},... | collective-permute-start | bytes 589832 | tf_op jit(solution)/shard_map/ppermute | solution.py:219
  46.2 0.2 collective-permute-start.11
  46.4 1.8 %expert.6 = (f32[2,192,512]{2,1,0:T(8,128)S(1)}, bf16[2,192,512]{2,1,0:T(8,128)(2,1)S(1)}) custom-call(s32[1]{0:T(128)} %bitcast.core_ref, bf16[192,512]{1,0:T(8,128)(2,1)S(1)} %collective-permute-done.15.p_ref, bf16[192,512]{1,0:T(8,128)(2,1)S(1)} %collective-permute-done.16.q_ref, bf16[192,512]{1,0:T(8,128)(2,1)S(1)} %collective-permute-done.17.p2_ref, ...), custom_call_target="tpu_custom_call" | custom-call | tf_op jit(solution)/shard_map/expert/pallas_call | solution.py:24
  48.3 0.4 collective-permute-start.19
  48.6 0.1 convert_add_fusion.3
  48.8 0.5 collective-permute-start.7
  49.3 0.7 collective-permute-done.19
  50.1 0.1 convert_add_fusion.1
  50.2 0.9 %collective-permute-start.20 = (bf16[192,512]{1,0:T(8,128)(2,1)S(1)}, bf16[192,512]{1,0:T(8,128)(2,1)S(1)}, u32[]{:S(2)}, u32[]{:S(2)}) collective-permute-start(bf16[192,512]{1,0:T(8,128)(2,1)S(1)} %fusion.10), channel_id=1, source_target_pairs={{0,2},{2,0},{4,6},{6,4},{8,10},{10,8},{12,14},{14,12},{1,3},{3,1},... | collective-permute-start | bytes 589832 | tf_op jit(solution)/shard_map/ppermute | solution.py:219
  51.1 5.5 %collective-permute-done.7 = bf16[192,512]{1,0:T(8,128)(2,1)S(1)} collective-permute-done((bf16[192,512]{1,0:T(8,128)(2,1)S(1)}, bf16[192,512]{1,0:T(8,128)(2,1)S(1)}, u32[]{:S(2)}, u32[]{:S(2)}) %collective-permute-start.7) | collective-permute-done | bytes 196640 | tf_op jit(solution)/shard_map/ppermute | solution.py:219
  56.7 1.8 %expert.5 = (f32[2,192,512]{2,1,0:T(8,128)S(1)}, bf16[2,192,512]{2,1,0:T(8,128)(2,1)S(1)}) custom-call(s32[1]{0:T(128)} %bitcast.core_ref, bf16[192,512]{1,0:T(8,128)(2,1)S(1)} %collective-permute-done.8.p_ref, bf16[192,512]{1,0:T(8,128)(2,1)S(1)} %after.4.q_ref, bf16[192,512]{1,0:T(8,128)(2,1)S(1)} %collective-permute-done.10.p2_ref, ...), custom_call_target="tpu_custom_call" | custom-call | tf_op jit(solution)/shard_map/expert/pallas_call | solution.py:24
  58.5 0.1 collective-permute-start.12
  58.6 0.5 collective-permute-start.24
  59.1 0.1 collective-permute-start.25
  59.2 1.2 %collective-permute-done.20 = bf16[192,512]{1,0:T(8,128)(2,1)S(1)} collective-permute-done((bf16[192,512]{1,0:T(8,128)(2,1)S(1)}, bf16[192,512]{1,0:T(8,128)(2,1)S(1)}, u32[]{:S(2)}, u32[]{:S(2)}) %collective-permute-start.20) | collective-permute-done | bytes 196640 | tf_op jit(solution)/shard_map/ppermute | solution.py:219
  60.4 0.1 collective-permute-start.21
  60.5 0.4 collective-permute-done.25.value_ref
  60.9 1.8 %expert.7 = (f32[2,192,512]{2,1,0:T(8,128)S(1)}, bf16[2,192,512]{2,1,0:T(8,128)(2,1)S(1)}) custom-call(s32[1]{0:T(128)} %bitcast.core_ref, bf16[192,512]{1,0:T(8,128)(2,1)S(1)} %collective-permute-done.22.p_ref, bf16[192,512]{1,0:T(8,128)(2,1)S(1)} %after.6.q_ref, bf16[192,512]{1,0:T(8,128)(2,1)S(1)} %collective-permute-done.24.p2_ref, ...), custom_call_target="tpu_custom_call" | custom-call | tf_op jit(solution)/shard_map/expert/pallas_call | solution.py:24
  62.7 0.2 collective-permute-start.26
  62.9 0.1 convert_add_fusion.2
  63.1 0.0 copy-start.7
  63.1 1.6 %collective-permute-start.13 = (bf16[192,512]{1,0:T(8,128)(2,1)S(1)}, bf16[192,512]{1,0:T(8,128)(2,1)S(1)}, u32[]{:S(2)}, u32[]{:S(2)}) collective-permute-start(bf16[192,512]{1,0:T(8,128)(2,1)S(1)} %fusion.9), channel_id=1, source_target_pairs={{0,2},{2,0},{4,6},{6,4},{8,10},{10,8},{12,14},{14,12},{1,3},{3,1},... | collective-permute-start | bytes 589832 | tf_op jit(solution)/shard_map/ppermute | solution.py:219
  64.7 0.1 convert_add_fusion
  64.9 1.4 %collective-permute-start.27 = (bf16[192,512]{1,0:T(8,128)(2,1)S(1)}, bf16[192,512]{1,0:T(8,128)(2,1)S(1)}, u32[]{:S(2)}, u32[]{:S(2)}) collective-permute-start(bf16[192,512]{1,0:T(8,128)(2,1)S(1)} %fusion.11), channel_id=1, source_target_pairs={{0,2},{2,0},{4,6},{6,4},{8,10},{10,8},{12,14},{14,12},{1,3},{3,1},... | collective-permute-start | bytes 589832 | tf_op jit(solution)/shard_map/ppermute | solution.py:219
  66.3 4.7 %collective-permute-done.13 = bf16[192,512]{1,0:T(8,128)(2,1)S(1)} collective-permute-done((bf16[192,512]{1,0:T(8,128)(2,1)S(1)}, bf16[192,512]{1,0:T(8,128)(2,1)S(1)}, u32[]{:S(2)}, u32[]{:S(2)}) %collective-permute-start.13) | collective-permute-done | bytes 196640 | tf_op jit(solution)/shard_map/ppermute | solution.py:219
  71.0 3.1 %collective-permute-start.14 = (bf16[192,512]{1,0:T(8,128)(2,1)S(1)}, bf16[192,512]{1,0:T(8,128)(2,1)S(1)}, u32[]{:S(2)}, u32[]{:S(2)}) collective-permute-start(bf16[192,512]{1,0:T(8,128)(2,1)S(1)} %fusion.5), channel_id=1, source_target_pairs={{0,12},{2,14},{4,0},{6,2},{8,4},{10,6},{12,8},{14,10},{1,13},{3,15... | collective-permute-start | bytes 589832 | tf_op jit(solution)/shard_map/ppermute | solution.py:224
  74.1 0.5 collective-permute-done.27
  74.6 2.3 %collective-permute-start.28 = (bf16[192,512]{1,0:T(8,128)(2,1)S(1)}, bf16[192,512]{1,0:T(8,128)(2,1)S(1)}, u32[]{:S(2)}, u32[]{:S(2)}) collective-permute-start(bf16[192,512]{1,0:T(8,128)(2,1)S(1)} %fusion.1), channel_id=1, source_target_pairs={{0,4},{2,6},{4,8},{6,10},{8,12},{10,14},{12,0},{14,2},{1,5},{3,7},... | collective-permute-start | bytes 589832 | tf_op jit(solution)/shard_map/ppermute | solution.py:224
  76.9 1.1 %collective-permute-done.1.other_gates_ref = f32[2,128]{1,0:T(2,128)S(1)} collective-permute-done((f32[2,128]{1,0:T(2,128)S(1)}, f32[2,128]{1,0:T(2,128)S(1)}, u32[]{:S(2)}, u32[]{:S(2)}) %collective-permute-start.1) | collective-permute-done | bytes 1056 | tf_op jit(solution)/shard_map/ppermute | solution.py:214
  78.1 0.6 collective-permute-done.14.rest_1_
  78.6 4.5 %collective-permute-done.28.rest_3_ = bf16[192,512]{1,0:T(8,128)(2,1)S(1)} collective-permute-done((bf16[192,512]{1,0:T(8,128)(2,1)S(1)}, bf16[192,512]{1,0:T(8,128)(2,1)S(1)}, u32[]{:S(2)}, u32[]{:S(2)}) %collective-permute-start.28) | collective-permute-done | bytes 196640 | tf_op jit(solution)/shard_map/ppermute | solution.py:224
  83.2 0.9 %combine.1 = (f32[128,512]{1,0:T(8,128)S(1)}, bf16[128,512]{1,0:T(8,128)(2,1)S(1)}) custom-call(s32[1]{0:T(128)} %bitcast.core_ref, s32[1]{0:T(128)} %bitcast.10.line_ref, s32[2,2,128]{2,1,0:T(2,128)S(1)} %bitcast.49, f32[2,128]{1,0:T(2,128)S(1)} %get-tuple-element.24.own_gates_ref, f32[2,128]{1,0:T(2,128)S(1)} %collective-permute-done.1.other_gates_ref, ...), custom_call_target="tpu_custom_call" | custom-call | tf_op jit(solution)/shard_map/combine/pallas_call | solution.py:24
  84.1 0.1 collective-permute-start.29
  84.2 1.3 %collective-permute-done.29.other_ref = bf16[128,512]{1,0:T(8,128)(2,1)S(1)} collective-permute-done((bf16[128,512]{1,0:T(8,128)(2,1)S(1)}, bf16[128,512]{1,0:T(8,128)(2,1)S(1)}, u32[]{:S(2)}, u32[]{:S(2)}) %collective-permute-start.29) | collective-permute-done | bytes 131104 | tf_op jit(solution)/shard_map/ppermute | solution.py:214
  85.5 0.8 finish.1
  (45 shorter events, 0.4 us)
Async XLA Ops:
  1.0 1.5 %collective-permute-start = (bf16[2,80,512]{2,1,0:T(8,128)(2,1)S(1)}, bf16[2,80,512]{2,1,0:T(8,128)(2,1)S(1)}, u32[]{:S(2)}, u32[]{:S(2)}) collective-permute-start(bf16[2,80,512]{2,1,0:T(8,128)(2,1)S(1)} %get-tuple-element.41), channel_id=1, source_target_pairs={{0,1},{1,0},{2,3},{3,2},{4,5},{5,4},{6,7},{7,6},{8,9},{9,8},{10,11... | collective-permute-start | bytes 491528 | tf_op jit(solution)/shard_map/ppermute | solution.py:214
  2.6 0.9 %copy-start.4 = (bf16[1,128,1024]{2,1,0:T(8,128)(2,1)S(1)}, bf16[1,128,1024]{2,1,0:T(8,128)(2,1)}, u32[]{:S(2)}) copy-start(bf16[1,128,1024]{2,1,0:T(8,128)(2,1)} %param.11) | copy-start | bytes 786436
  3.5 0.7 copy-start.5
  4.2 0.7 copy-start.8
  4.9 0.7 copy-start.9
  5.6 0.7 copy-start.10
  6.3 0.7 copy-start.11
  10.2 1.4 %collective-permute-start.2 = (bf16[128,512]{1,0:T(8,128)(2,1)S(1)}, bf16[128,512]{1,0:T(8,128)(2,1)S(1)}, u32[]{:S(2)}, u32[]{:S(2)}) collective-permute-start(bf16[128,512]{1,0:T(8,128)(2,1)S(1)} %get-tuple-element.26), channel_id=1, source_target_pairs={{0,1},{1,0},{2,3},{3,2},{4,5},{5,4},{6,7},{7,6},{8,9},{9,8},{10,11... | collective-permute-start | bytes 393224 | tf_op jit(solution)/shard_map/ppermute | solution.py:214
  11.6 0.7 copy-start.6
  12.8 8.1 %collective-permute-start.3 = (bf16[192,512]{1,0:T(8,128)(2,1)S(1)}, bf16[192,512]{1,0:T(8,128)(2,1)S(1)}, u32[]{:S(2)}, u32[]{:S(2)}) collective-permute-start(bf16[192,512]{1,0:T(8,128)(2,1)S(1)} %get-tuple-element.27.p_ref), channel_id=1, source_target_pairs={{0,2},{2,0},{4,6},{6,4},{8,10},{10,8},{12,14},{14,12},{1,3},{3,1},... | collective-permute-start | bytes 589832 | tf_op jit(solution)/shard_map/ppermute | solution.py:219
  15.7 16.0 %collective-permute-start.15 = (bf16[192,512]{1,0:T(8,128)(2,1)S(1)}, bf16[192,512]{1,0:T(8,128)(2,1)S(1)}, u32[]{:S(2)}, u32[]{:S(2)}) collective-permute-start(bf16[192,512]{1,0:T(8,128)(2,1)S(1)} %get-tuple-element.33), channel_id=1, source_target_pairs={{0,8},{2,10},{4,12},{6,14},{8,0},{10,2},{12,4},{14,6},{1,9},{3,11}... | collective-permute-start | bytes 589832 | tf_op jit(solution)/shard_map/ppermute | solution.py:224
  18.3 13.9 %collective-permute-start.4 = (bf16[192,512]{1,0:T(8,128)(2,1)S(1)}, bf16[192,512]{1,0:T(8,128)(2,1)S(1)}, u32[]{:S(2)}, u32[]{:S(2)}) collective-permute-start(bf16[192,512]{1,0:T(8,128)(2,1)S(1)} %get-tuple-element.27.p_ref), channel_id=1, source_target_pairs={{0,1},{1,0},{2,3},{3,2},{4,5},{5,4},{6,7},{7,6},{8,9},{9,8},{10,11... | collective-permute-start | bytes 589832 | tf_op jit(solution)/shard_map/ppermute | solution.py:214
  21.0 11.3 %collective-permute-start.5 = (bf16[192,512]{1,0:T(8,128)(2,1)S(1)}, bf16[192,512]{1,0:T(8,128)(2,1)S(1)}, u32[]{:S(2)}, u32[]{:S(2)}) collective-permute-start(bf16[192,512]{1,0:T(8,128)(2,1)S(1)} %collective-permute-done.3.q_ref), channel_id=1, source_target_pairs={{0,1},{1,0},{2,3},{3,2},{4,5},{5,4},{6,7},{7,6},{8,9},{9,8},{10,11... | collective-permute-start | bytes 589832 | tf_op jit(solution)/shard_map/ppermute | solution.py:214
  21.0 16.5 %collective-permute-start.8 = (bf16[192,512]{1,0:T(8,128)(2,1)S(1)}, bf16[192,512]{1,0:T(8,128)(2,1)S(1)}, u32[]{:S(2)}, u32[]{:S(2)}) collective-permute-start(bf16[192,512]{1,0:T(8,128)(2,1)S(1)} %get-tuple-element.30), channel_id=1, source_target_pairs={{0,4},{2,6},{4,8},{6,10},{8,12},{10,14},{12,0},{14,2},{1,5},{3,7},... | collective-permute-start | bytes 589832 | tf_op jit(solution)/shard_map/ppermute | solution.py:224
  31.7 7.4 %collective-permute-start.16 = (bf16[192,512]{1,0:T(8,128)(2,1)S(1)}, bf16[192,512]{1,0:T(8,128)(2,1)S(1)}, u32[]{:S(2)}, u32[]{:S(2)}) collective-permute-start(bf16[192,512]{1,0:T(8,128)(2,1)S(1)} %collective-permute-done.15.p_ref), channel_id=1, source_target_pairs={{0,2},{2,0},{4,6},{6,4},{8,10},{10,8},{12,14},{14,12},{1,3},{3,1},... | collective-permute-start | bytes 589832 | tf_op jit(solution)/shard_map/ppermute | solution.py:219
  32.2 1.6 %copy-start = (bf16[1024,1024]{1,0:T(8,128)(2,1)S(1)}, bf16[1024,1024]{1,0:T(8,128)(2,1)}, u32[]{:S(2)}) copy-start(bf16[1024,1024]{1,0:T(8,128)(2,1)} %in_ref.7) | copy-start | bytes 6291460
  33.8 1.6 %copy-start.2 = (bf16[1024,1024]{1,0:T(8,128)(2,1)S(1)}, bf16[1024,1024]{1,0:T(8,128)(2,1)}, u32[]{:S(2)}) copy-start(bf16[1024,1024]{1,0:T(8,128)(2,1)} %out_ref.7) | copy-start | bytes 6291460
  35.4 11.0 %copy-start.1 = (bf16[1024,1024]{1,0:T(8,128)(2,1)S(1)}, bf16[1024,1024]{1,0:T(8,128)(2,1)}, u32[]{:S(2)}) copy-start(bf16[1024,1024]{1,0:T(8,128)(2,1)} %in_ref.7) | copy-start | bytes 6291460
  35.4 11.0 %copy-start.3 = (bf16[1024,1024]{1,0:T(8,128)(2,1)S(1)}, bf16[1024,1024]{1,0:T(8,128)(2,1)}, u32[]{:S(2)}) copy-start(bf16[1024,1024]{1,0:T(8,128)(2,1)} %out_ref.7) | copy-start | bytes 6291460
  37.3 11.4 %collective-permute-start.6 = (bf16[2,192,512]{2,1,0:T(8,128)(2,1)S(1)}, bf16[2,192,512]{2,1,0:T(8,128)(2,1)S(1)}, u32[]{:S(2)}, u32[]{:S(2)}) collective-permute-start(bf16[2,192,512]{2,1,0:T(8,128)(2,1)S(1)} %get-tuple-element.29), channel_id=1, source_target_pairs={{0,1},{1,0},{2,3},{3,2},{4,5},{5,4},{6,7},{7,6},{8,9},{9,8},{10,11... | collective-permute-start | bytes 1179656 | tf_op jit(solution)/shard_map/ppermute | solution.py:214
  37.3 7.3 %collective-permute-start.22 = (bf16[192,512]{1,0:T(8,128)(2,1)S(1)}, bf16[192,512]{1,0:T(8,128)(2,1)S(1)}, u32[]{:S(2)}, u32[]{:S(2)}) collective-permute-start(bf16[192,512]{1,0:T(8,128)(2,1)S(1)} %get-tuple-element.36), channel_id=1, source_target_pairs={{0,12},{2,14},{4,0},{6,2},{8,4},{10,6},{12,8},{14,10},{1,13},{3,15... | collective-permute-start | bytes 589832 | tf_op jit(solution)/shard_map/ppermute | solution.py:224
  37.4 7.2 %collective-permute-start.9 = (bf16[192,512]{1,0:T(8,128)(2,1)S(1)}, bf16[192,512]{1,0:T(8,128)(2,1)S(1)}, u32[]{:S(2)}, u32[]{:S(2)}) collective-permute-start(bf16[192,512]{1,0:T(8,128)(2,1)S(1)} %collective-permute-done.8.p_ref), channel_id=1, source_target_pairs={{0,2},{2,0},{4,6},{6,4},{8,10},{10,8},{12,14},{14,12},{1,3},{3,1},... | collective-permute-start | bytes 589832 | tf_op jit(solution)/shard_map/ppermute | solution.py:219
  39.0 7.2 %collective-permute-start.17 = (bf16[192,512]{1,0:T(8,128)(2,1)S(1)}, bf16[192,512]{1,0:T(8,128)(2,1)S(1)}, u32[]{:S(2)}, u32[]{:S(2)}) collective-permute-start(bf16[192,512]{1,0:T(8,128)(2,1)S(1)} %collective-permute-done.15.p_ref), channel_id=1, source_target_pairs={{0,1},{1,0},{2,3},{3,2},{4,5},{5,4},{6,7},{7,6},{8,9},{9,8},{10,11... | collective-permute-start | bytes 589832 | tf_op jit(solution)/shard_map/ppermute | solution.py:214
  39.1 7.3 %collective-permute-start.18 = (bf16[192,512]{1,0:T(8,128)(2,1)S(1)}, bf16[192,512]{1,0:T(8,128)(2,1)S(1)}, u32[]{:S(2)}, u32[]{:S(2)}) collective-permute-start(bf16[192,512]{1,0:T(8,128)(2,1)S(1)} %collective-permute-done.16.q_ref), channel_id=1, source_target_pairs={{0,1},{1,0},{2,3},{3,2},{4,5},{5,4},{6,7},{7,6},{8,9},{9,8},{10,11... | collective-permute-start | bytes 589832 | tf_op jit(solution)/shard_map/ppermute | solution.py:214
  44.6 12.0 %collective-permute-start.10 = (bf16[192,512]{1,0:T(8,128)(2,1)S(1)}, bf16[192,512]{1,0:T(8,128)(2,1)S(1)}, u32[]{:S(2)}, u32[]{:S(2)}) collective-permute-start(bf16[192,512]{1,0:T(8,128)(2,1)S(1)} %collective-permute-done.8.p_ref), channel_id=1, source_target_pairs={{0,1},{1,0},{2,3},{3,2},{4,5},{5,4},{6,7},{7,6},{8,9},{9,8},{10,11... | collective-permute-start | bytes 589832 | tf_op jit(solution)/shard_map/ppermute | solution.py:214
  44.6 14.5 %collective-permute-start.23 = (bf16[192,512]{1,0:T(8,128)(2,1)S(1)}, bf16[192,512]{1,0:T(8,128)(2,1)S(1)}, u32[]{:S(2)}, u32[]{:S(2)}) collective-permute-start(bf16[192,512]{1,0:T(8,128)(2,1)S(1)} %collective-permute-done.22.p_ref), channel_id=1, source_target_pairs={{0,2},{2,0},{4,6},{6,4},{8,10},{10,8},{12,14},{14,12},{1,3},{3,1},... | collective-permute-start | bytes 589832 | tf_op jit(solution)/shard_map/ppermute | solution.py:219
  46.2 10.5 %collective-permute-start.11 = (bf16[192,512]{1,0:T(8,128)(2,1)S(1)}, bf16[192,512]{1,0:T(8,128)(2,1)S(1)}, u32[]{:S(2)}, u32[]{:S(2)}) collective-permute-start(bf16[192,512]{1,0:T(8,128)(2,1)S(1)} %after.4.q_ref), channel_id=1, source_target_pairs={{0,1},{1,0},{2,3},{3,2},{4,5},{5,4},{6,7},{7,6},{8,9},{9,8},{10,11... | collective-permute-start | bytes 589832 | tf_op jit(solution)/shard_map/ppermute | solution.py:214
  48.3 1.8 %collective-permute-start.19 = (bf16[2,192,512]{2,1,0:T(8,128)(2,1)S(1)}, bf16[2,192,512]{2,1,0:T(8,128)(2,1)S(1)}, u32[]{:S(2)}, u32[]{:S(2)}) collective-permute-start(bf16[2,192,512]{2,1,0:T(8,128)(2,1)S(1)} %get-tuple-element.35), channel_id=1, source_target_pairs={{0,1},{1,0},{2,3},{3,2},{4,5},{5,4},{6,7},{7,6},{8,9},{9,8},{10,11... | collective-permute-start | bytes 1179656 | tf_op jit(solution)/shard_map/ppermute | solution.py:214
  48.8 7.8 %collective-permute-start.7 = (bf16[192,512]{1,0:T(8,128)(2,1)S(1)}, bf16[192,512]{1,0:T(8,128)(2,1)S(1)}, u32[]{:S(2)}, u32[]{:S(2)}) collective-permute-start(bf16[192,512]{1,0:T(8,128)(2,1)S(1)} %fusion.8), channel_id=1, source_target_pairs={{0,2},{2,0},{4,6},{6,4},{8,10},{10,8},{12,14},{14,12},{1,3},{3,1},... | collective-permute-start | bytes 589832 | tf_op jit(solution)/shard_map/ppermute | solution.py:219
  50.2 10.2 %collective-permute-start.20 = (bf16[192,512]{1,0:T(8,128)(2,1)S(1)}, bf16[192,512]{1,0:T(8,128)(2,1)S(1)}, u32[]{:S(2)}, u32[]{:S(2)}) collective-permute-start(bf16[192,512]{1,0:T(8,128)(2,1)S(1)} %fusion.10), channel_id=1, source_target_pairs={{0,2},{2,0},{4,6},{6,4},{8,10},{10,8},{12,14},{14,12},{1,3},{3,1},... | collective-permute-start | bytes 589832 | tf_op jit(solution)/shard_map/ppermute | solution.py:219
  58.5 4.4 %collective-permute-start.12 = (bf16[2,192,512]{2,1,0:T(8,128)(2,1)S(1)}, bf16[2,192,512]{2,1,0:T(8,128)(2,1)S(1)}, u32[]{:S(2)}, u32[]{:S(2)}) collective-permute-start(bf16[2,192,512]{2,1,0:T(8,128)(2,1)S(1)} %get-tuple-element.32), channel_id=1, source_target_pairs={{0,1},{1,0},{2,3},{3,2},{4,5},{5,4},{6,7},{7,6},{8,9},{9,8},{10,11... | collective-permute-start | bytes 1179656 | tf_op jit(solution)/shard_map/ppermute | solution.py:214
  58.6 2.3 %collective-permute-start.24 = (bf16[192,512]{1,0:T(8,128)(2,1)S(1)}, bf16[192,512]{1,0:T(8,128)(2,1)S(1)}, u32[]{:S(2)}, u32[]{:S(2)}) collective-permute-start(bf16[192,512]{1,0:T(8,128)(2,1)S(1)} %collective-permute-done.22.p_ref), channel_id=1, source_target_pairs={{0,1},{1,0},{2,3},{3,2},{4,5},{5,4},{6,7},{7,6},{8,9},{9,8},{10,11... | collective-permute-start | bytes 589832 | tf_op jit(solution)/shard_map/ppermute | solution.py:214
  59.1 1.8 %collective-permute-start.25 = (bf16[192,512]{1,0:T(8,128)(2,1)S(1)}, bf16[192,512]{1,0:T(8,128)(2,1)S(1)}, u32[]{:S(2)}, u32[]{:S(2)}) collective-permute-start(bf16[192,512]{1,0:T(8,128)(2,1)S(1)} %after.6.q_ref), channel_id=1, source_target_pairs={{0,1},{1,0},{2,3},{3,2},{4,5},{5,4},{6,7},{7,6},{8,9},{9,8},{10,11... | collective-permute-start | bytes 589832 | tf_op jit(solution)/shard_map/ppermute | solution.py:214
  60.4 17.6 %collective-permute-start.21 = (bf16[192,512]{1,0:T(8,128)(2,1)S(1)}, bf16[192,512]{1,0:T(8,128)(2,1)S(1)}, u32[]{:S(2)}, u32[]{:S(2)}) collective-permute-start(bf16[192,512]{1,0:T(8,128)(2,1)S(1)} %fusion.3.first_ref), channel_id=1, source_target_pairs={{0,8},{2,10},{4,12},{6,14},{8,0},{10,2},{12,4},{14,6},{1,9},{3,11}... | collective-permute-start | bytes 589832 | tf_op jit(solution)/shard_map/ppermute | solution.py:224
  62.7 2.0 %collective-permute-start.26 = (bf16[2,192,512]{2,1,0:T(8,128)(2,1)S(1)}, bf16[2,192,512]{2,1,0:T(8,128)(2,1)S(1)}, u32[]{:S(2)}, u32[]{:S(2)}) collective-permute-start(bf16[2,192,512]{2,1,0:T(8,128)(2,1)S(1)} %get-tuple-element.38), channel_id=1, source_target_pairs={{0,1},{1,0},{2,3},{3,2},{4,5},{5,4},{6,7},{7,6},{8,9},{9,8},{10,11... | collective-permute-start | bytes 1179656 | tf_op jit(solution)/shard_map/ppermute | solution.py:214
  63.1 20.1 %copy-start.7 = (s32[2,128,2]{1,2,0:T(2,128)S(1)}, s32[2,128,2]{1,2,0:T(2,128)}, u32[]{:S(2)}) copy-start(s32[2,128,2]{1,2,0:T(2,128)} %param.16) | copy-start | bytes 6148
  63.1 7.8 %collective-permute-start.13 = (bf16[192,512]{1,0:T(8,128)(2,1)S(1)}, bf16[192,512]{1,0:T(8,128)(2,1)S(1)}, u32[]{:S(2)}, u32[]{:S(2)}) collective-permute-start(bf16[192,512]{1,0:T(8,128)(2,1)S(1)} %fusion.9), channel_id=1, source_target_pairs={{0,2},{2,0},{4,6},{6,4},{8,10},{10,8},{12,14},{14,12},{1,3},{3,1},... | collective-permute-start | bytes 589832 | tf_op jit(solution)/shard_map/ppermute | solution.py:219
  64.9 9.7 %collective-permute-start.27 = (bf16[192,512]{1,0:T(8,128)(2,1)S(1)}, bf16[192,512]{1,0:T(8,128)(2,1)S(1)}, u32[]{:S(2)}, u32[]{:S(2)}) collective-permute-start(bf16[192,512]{1,0:T(8,128)(2,1)S(1)} %fusion.11), channel_id=1, source_target_pairs={{0,2},{2,0},{4,6},{6,4},{8,10},{10,8},{12,14},{14,12},{1,3},{3,1},... | collective-permute-start | bytes 589832 | tf_op jit(solution)/shard_map/ppermute | solution.py:219
  71.0 7.7 %collective-permute-start.14 = (bf16[192,512]{1,0:T(8,128)(2,1)S(1)}, bf16[192,512]{1,0:T(8,128)(2,1)S(1)}, u32[]{:S(2)}, u32[]{:S(2)}) collective-permute-start(bf16[192,512]{1,0:T(8,128)(2,1)S(1)} %fusion.5), channel_id=1, source_target_pairs={{0,12},{2,14},{4,0},{6,2},{8,4},{10,6},{12,8},{14,10},{1,13},{3,15... | collective-permute-start | bytes 589832 | tf_op jit(solution)/shard_map/ppermute | solution.py:224
  74.6 8.5 %collective-permute-start.28 = (bf16[192,512]{1,0:T(8,128)(2,1)S(1)}, bf16[192,512]{1,0:T(8,128)(2,1)S(1)}, u32[]{:S(2)}, u32[]{:S(2)}) collective-permute-start(bf16[192,512]{1,0:T(8,128)(2,1)S(1)} %fusion.1), channel_id=1, source_target_pairs={{0,4},{2,6},{4,8},{6,10},{8,12},{10,14},{12,0},{14,2},{1,5},{3,7},... | collective-permute-start | bytes 589832 | tf_op jit(solution)/shard_map/ppermute | solution.py:224
  76.9 1.1 %collective-permute-start.1 = (f32[2,128]{1,0:T(2,128)S(1)}, f32[2,128]{1,0:T(2,128)S(1)}, u32[]{:S(2)}, u32[]{:S(2)}) collective-permute-start(f32[2,128]{1,0:T(2,128)S(1)} %get-tuple-element.24.own_gates_ref), channel_id=1, source_target_pairs={{0,1},{1,0},{2,3},{3,2},{4,5},{5,4},{6,7},{7,6},{8,9},{9,8},{10,11... | collective-permute-start | bytes 3080 | tf_op jit(solution)/shard_map/ppermute | solution.py:214
  84.1 1.4 %collective-permute-start.29 = (bf16[128,512]{1,0:T(8,128)(2,1)S(1)}, bf16[128,512]{1,0:T(8,128)(2,1)S(1)}, u32[]{:S(2)}, u32[]{:S(2)}) collective-permute-start(bf16[128,512]{1,0:T(8,128)(2,1)S(1)} %get-tuple-element.40), channel_id=1, source_target_pairs={{0,1},{1,0},{2,3},{3,2},{4,5},{5,4},{6,7},{7,6},{8,9},{9,8},{10,11... | collective-permute-start | bytes 393224 | tf_op jit(solution)/shard_map/ppermute | solution.py:214

commit v6 on v5

--- a/solution.py
+++ b/solution.py
@@ -302,10 +302,10 @@
     for at, offset in enumerate(piece_order(count)):
         p = travelling[offset - 1] if offset else selected[0]
         q = swap_owner(p)
-        if at >= 2:
-            q = after(q, kepts[at - 2])
         p2 = swap(p)
         q2 = swap(q)
+        if at >= 2:
+            q2 = after(q2, kepts[at - 2])
         if at >= 2:
             q2 = after(q2, wholes[at - 2])
         kept, sent = call(

time: 86.7 us -> 91 us (1.050)
  waiting for transfers between devices: 38.5 us -> 41.4 us
  starting transfers between devices: 24 us -> 25.5 us
    ppermute x8, waiting for transfers between devices: 14.4 us -> 21.3 us  [swap_owner(): return lax.ppermute(values, 'expert', [(i, i ^ 1) for i in range(owners)])]
    ppermute x6, waiting for transfers between devices: 19.1 us -> 15.2 us  [shift(): lax.ppermute(values, 'expert', [(i, (i + 2 * offset) % owners) for i in r...]
    ppermute x6, starting transfers between devices: 10 us -> 12.8 us  [shift(): lax.ppermute(values, 'expert', [(i, (i + 2 * offset) % owners) for i in r...]
    ppermute x8, starting transfers between devices: 11 us -> 9.53 us  [swap_owner(): return lax.ppermute(values, 'expert', [(i, i ^ 1) for i in range(owners)])]
  transfers between devices with their start and end apart: 30 -> 30, of which waited for: 15 -> 16; matrix products, arithmetic and copies ran while one was open for 1% -> 1% of each run, Pallas kernels for 9% -> 8%
where the time goes in v6:
time: 91 us; the launch traced here: 90.6 us
  waiting for transfers between devices  41.4 us (45%)
  starting transfers between devices  25.5 us (28%)
  Pallas kernels  12.8 us (14%)
  local copies, waits for them, and re-layouts  8.33 us (9%)
  other arithmetic  1.64 us (2%)
  between operations  0.92 us (1%)
    ppermute x8, waiting for transfers between devices, swap_owner(): return lax.ppermute(values, 'expert', [(i, i ^ 1) for i in range(owners)])  21.3 us
    ppermute x6, waiting for transfers between devices, shift(): lax.ppermute(values, 'expert', [(i, (i + 2 * offset) % owners) for i in r...  15.2 us
    pallas_call x8, Pallas kernels, call(): pl.pallas_call(kernel, out_shape=tuple((jax.ShapeDtypeStruct(*out) for ou...  12.8 us
    ppermute x6, starting transfers between devices, shift(): lax.ppermute(values, 'expert', [(i, (i + 2 * offset) % owners) for i in r...  12.8 us
    ppermute x8, starting transfers between devices, swap_owner(): return lax.ppermute(values, 'expert', [(i, i ^ 1) for i in range(owners)])  9.53 us
    unnamed x24, local copies, waits for them, and re-layouts  8.23 us
    ppermute x16, waiting for transfers between devices, swap(): return lax.ppermute(values, 'section', [(0, 1), (1, 0)])  4.89 us
    ppermute x16, starting transfers between devices, swap(): return lax.ppermute(values, 'section', [(0, 1), (1, 0)])  3.19 us
  transfers between devices with their start and end apart: 30, of which 16 were waited for; matrix products, arithmetic and copies ran while one was open for 1% of the time, Pallas kernels for 8%

profile of v6, /device:TPU:0, one launch (start us, length us, event | category | flops | bytes accessed | tf_op | source)
XLA Modules:
  0.0 90.6 jit_solution(7437338330819289782)
XLA Ops:
  0.0 1.0 %fusion.13 = (bf16[2,80,512]{2,1,0:T(8,128)(2,1)S(1)}, bf16[2,80,512]{2,1,0:T(8,128)(2,1)S(1)}) fusion(s32[]{:T(128)S(6)} %select_n.13, bf16[2,1,80,512]{3,2,0,1:T(8,128)(2,1)} %bitcast.53, bf16[2,1,80,512]{3,2,0,1:T(8,128)(2,1)} %bitcast.54, s32[]{:T(128)S(6)} %select_n.12), kind=kLoop, calls=%fused_computation.29 | loop fusion | flops 163840 | bytes 655368 | tf_op jit(solution)/shard_map/jit(dynamic_index_in_dim)/squeeze | solution.py:257
  1.0 0.5 collective-permute-start
  2.2 0.4 collective-permute-done.other_ref
  2.6 0.9 %copy-done.4 = bf16[1,128,1024]{2,1,0:T(8,128)(2,1)S(1)} copy-done((bf16[1,128,1024]{2,1,0:T(8,128)(2,1)S(1)}, bf16[1,128,1024]{2,1,0:T(8,128)(2,1)}, u32[]{:S(2)}) %copy-start.4) | copy-done | bytes 262168
  3.5 0.7 copy-done.5
  4.2 0.7 copy-done.8
  4.9 0.7 copy-done.9
  5.6 0.7 copy-done.10
  6.3 0.7 copy-done.11
  6.9 3.2 %attend.1 = (bf16[128,1024]{1,0:T(8,128)(2,1)S(1)}, bf16[128,512]{1,0:T(8,128)(2,1)S(1)}, bf16[128,512]{1,0:T(8,128)(2,1)S(1)}, f32[2,128]{1,0:T(2,128)S(1)}) custom-call(s32[1]{0:T(128)} %bitcast.core_ref, s32[1]{0:T(128)S(6)} %copy.20.source_ref, s32[2]{0:T(128)S(1)} %copy-done.11, bf16[128,1024]{1,0:T(8,128)(2,1)S(1)} %bitcast.46, ...), custom_call_target="tpu_custom_call" | custom-call | tf_op jit(solution)/shard_map/attend/pallas_call | solution.py:24
  10.2 0.4 collective-permute-start.2
  10.6 1.0 %collective-permute-done.2.other_ref = bf16[128,512]{1,0:T(8,128)(2,1)S(1)} collective-permute-done((bf16[128,512]{1,0:T(8,128)(2,1)S(1)}, bf16[128,512]{1,0:T(8,128)(2,1)S(1)}, u32[]{:S(2)}, u32[]{:S(2)}) %collective-permute-start.2) | collective-permute-done | bytes 131104 | tf_op jit(solution)/shard_map/ppermute | solution.py:214
  11.6 0.7 copy-done.6
  12.3 0.5 select.5
  12.8 2.9 %collective-permute-start.3 = (bf16[192,512]{1,0:T(8,128)(2,1)S(1)}, bf16[192,512]{1,0:T(8,128)(2,1)S(1)}, u32[]{:S(2)}, u32[]{:S(2)}) collective-permute-start(bf16[192,512]{1,0:T(8,128)(2,1)S(1)} %get-tuple-element.27.p_ref), channel_id=1, source_target_pairs={{0,2},{2,0},{4,6},{6,4},{8,10},{10,8},{12,14},{14,12},{1,3},{3,1},... | collective-permute-start | bytes 589832 | tf_op jit(solution)/shard_map/ppermute | solution.py:219
  15.7 2.6 %collective-permute-start.15 = (bf16[192,512]{1,0:T(8,128)(2,1)S(1)}, bf16[192,512]{1,0:T(8,128)(2,1)S(1)}, u32[]{:S(2)}, u32[]{:S(2)}) collective-permute-start(bf16[192,512]{1,0:T(8,128)(2,1)S(1)} %get-tuple-element.33), channel_id=1, source_target_pairs={{0,8},{2,10},{4,12},{6,14},{8,0},{10,2},{12,4},{14,6},{1,9},{3,11}... | collective-permute-start | bytes 589832 | tf_op jit(solution)/shard_map/ppermute | solution.py:224
  18.3 1.6 %collective-permute-start.8 = (bf16[192,512]{1,0:T(8,128)(2,1)S(1)}, bf16[192,512]{1,0:T(8,128)(2,1)S(1)}, u32[]{:S(2)}, u32[]{:S(2)}) collective-permute-start(bf16[192,512]{1,0:T(8,128)(2,1)S(1)} %get-tuple-element.30), channel_id=1, source_target_pairs={{0,4},{2,6},{4,8},{6,10},{8,12},{10,14},{12,0},{14,2},{1,5},{3,7},... | collective-permute-start | bytes 589832 | tf_op jit(solution)/shard_map/ppermute | solution.py:224
  19.9 1.0 %collective-permute-done.3.q_ref = bf16[192,512]{1,0:T(8,128)(2,1)S(1)} collective-permute-done((bf16[192,512]{1,0:T(8,128)(2,1)S(1)}, bf16[192,512]{1,0:T(8,128)(2,1)S(1)}, u32[]{:S(2)}, u32[]{:S(2)}) %collective-permute-start.3) | collective-permute-done | bytes 196640 | tf_op jit(solution)/shard_map/ppermute | solution.py:219
  21.0 3.8 %collective-permute-start.22 = (bf16[192,512]{1,0:T(8,128)(2,1)S(1)}, bf16[192,512]{1,0:T(8,128)(2,1)S(1)}, u32[]{:S(2)}, u32[]{:S(2)}) collective-permute-start(bf16[192,512]{1,0:T(8,128)(2,1)S(1)} %get-tuple-element.36), channel_id=1, source_target_pairs={{0,12},{2,14},{4,0},{6,2},{8,4},{10,6},{12,8},{14,10},{1,13},{3,15... | collective-permute-start | bytes 589832 | tf_op jit(solution)/shard_map/ppermute | solution.py:224
  24.8 8.1 %collective-permute-done.15.p_ref = bf16[192,512]{1,0:T(8,128)(2,1)S(1)} collective-permute-done((bf16[192,512]{1,0:T(8,128)(2,1)S(1)}, bf16[192,512]{1,0:T(8,128)(2,1)S(1)}, u32[]{:S(2)}, u32[]{:S(2)}) %collective-permute-start.15) | collective-permute-done | bytes 196640 | tf_op jit(solution)/shard_map/ppermute | solution.py:224
  32.9 0.2 collective-permute-start.16
  33.1 1.9 %collective-permute-start.9 = (bf16[192,512]{1,0:T(8,128)(2,1)S(1)}, bf16[192,512]{1,0:T(8,128)(2,1)S(1)}, u32[]{:S(2)}, u32[]{:S(2)}) collective-permute-start(bf16[192,512]{1,0:T(8,128)(2,1)S(1)} %collective-permute-done.8.p_ref), channel_id=1, source_target_pairs={{0,2},{2,0},{4,6},{6,4},{8,10},{10,8},{12,14},{14,12},{1,3},{3,1},... | collective-permute-start | bytes 589832 | tf_op jit(solution)/shard_map/ppermute | solution.py:219
  34.9 1.6 %copy-done = bf16[1024,1024]{1,0:T(8,128)(2,1)S(1)} copy-done((bf16[1024,1024]{1,0:T(8,128)(2,1)S(1)}, bf16[1024,1024]{1,0:T(8,128)(2,1)}, u32[]{:S(2)}) %copy-start) | copy-done | bytes 2097176
  36.5 1.6 %copy-done.2 = bf16[1024,1024]{1,0:T(8,128)(2,1)S(1)} copy-done((bf16[1024,1024]{1,0:T(8,128)(2,1)S(1)}, bf16[1024,1024]{1,0:T(8,128)(2,1)}, u32[]{:S(2)}) %copy-start.2) | copy-done | bytes 2097176
  38.1 1.8 %expert.4 = (f32[2,192,512]{2,1,0:T(8,128)S(1)}, bf16[2,192,512]{2,1,0:T(8,128)(2,1)S(1)}) custom-call(s32[1]{0:T(128)} %bitcast.core_ref, bf16[192,512]{1,0:T(8,128)(2,1)S(1)} %get-tuple-element.27.p_ref, bf16[192,512]{1,0:T(8,128)(2,1)S(1)} %collective-permute-done.3.q_ref, bf16[192,512]{1,0:T(8,128)(2,1)S(1)} %collective-permute-done.4.p2_ref, ...), custom_call_target="tpu_custom_call" | custom-call | tf_op jit(solution)/shard_map/expert/pallas_call | solution.py:24
  40.0 0.1 collective-permute-start.6
  40.0 0.5 collective-permute-start.17
  40.5 0.2 collective-permute-start.23
  40.7 1.1 %collective-permute-done.9.q_ref = bf16[192,512]{1,0:T(8,128)(2,1)S(1)} collective-permute-done((bf16[192,512]{1,0:T(8,128)(2,1)S(1)}, bf16[192,512]{1,0:T(8,128)(2,1)S(1)}, u32[]{:S(2)}, u32[]{:S(2)}) %collective-permute-start.9) | collective-permute-done | bytes 196640 | tf_op jit(solution)/shard_map/ppermute | solution.py:219
  41.8 0.2 collective-permute-done.17.p2_ref
  42.0 0.3 collective-permute-start.10
  42.3 5.1 %collective-permute-done.23.q_ref = bf16[192,512]{1,0:T(8,128)(2,1)S(1)} collective-permute-done((bf16[192,512]{1,0:T(8,128)(2,1)S(1)}, bf16[192,512]{1,0:T(8,128)(2,1)S(1)}, u32[]{:S(2)}, u32[]{:S(2)}) %collective-permute-start.23) | collective-permute-done | bytes 196640 | tf_op jit(solution)/shard_map/ppermute | solution.py:219
  47.4 1.8 %expert.6 = (f32[2,192,512]{2,1,0:T(8,128)S(1)}, bf16[2,192,512]{2,1,0:T(8,128)(2,1)S(1)}) custom-call(s32[1]{0:T(128)} %bitcast.core_ref, bf16[192,512]{1,0:T(8,128)(2,1)S(1)} %collective-permute-done.15.p_ref, bf16[192,512]{1,0:T(8,128)(2,1)S(1)} %collective-permute-done.16.q_ref, bf16[192,512]{1,0:T(8,128)(2,1)S(1)} %collective-permute-done.17.p2_ref, ...), custom_call_target="tpu_custom_call" | custom-call | tf_op jit(solution)/shard_map/expert/pallas_call | solution.py:24
  49.3 0.6 collective-permute-start.19
  49.9 0.1 convert_add_fusion.3
  50.0 0.3 collective-permute-start.7
  50.4 0.8 collective-permute-done.19
  51.2 0.1 convert_add_fusion.1
  51.4 1.0 %collective-permute-start.20 = (bf16[192,512]{1,0:T(8,128)(2,1)S(1)}, bf16[192,512]{1,0:T(8,128)(2,1)S(1)}, u32[]{:S(2)}, u32[]{:S(2)}) collective-permute-start(bf16[192,512]{1,0:T(8,128)(2,1)S(1)} %fusion.10), channel_id=1, source_target_pairs={{0,2},{2,0},{4,6},{6,4},{8,10},{10,8},{12,14},{14,12},{1,3},{3,1},... | collective-permute-start | bytes 589832 | tf_op jit(solution)/shard_map/ppermute | solution.py:219
  52.3 5.5 %collective-permute-done.7 = bf16[192,512]{1,0:T(8,128)(2,1)S(1)} collective-permute-done((bf16[192,512]{1,0:T(8,128)(2,1)S(1)}, bf16[192,512]{1,0:T(8,128)(2,1)S(1)}, u32[]{:S(2)}, u32[]{:S(2)}) %collective-permute-start.7) | collective-permute-done | bytes 196640 | tf_op jit(solution)/shard_map/ppermute | solution.py:219
  57.9 1.8 %expert.5 = (f32[2,192,512]{2,1,0:T(8,128)S(1)}, bf16[2,192,512]{2,1,0:T(8,128)(2,1)S(1)}) custom-call(s32[1]{0:T(128)} %bitcast.core_ref, bf16[192,512]{1,0:T(8,128)(2,1)S(1)} %collective-permute-done.8.p_ref, bf16[192,512]{1,0:T(8,128)(2,1)S(1)} %collective-permute-done.9.q_ref, bf16[192,512]{1,0:T(8,128)(2,1)S(1)} %collective-permute-done.10.p2_ref, ...), custom_call_target="tpu_custom_call" | custom-call | tf_op jit(solution)/shard_map/expert/pallas_call | solution.py:24
  59.8 0.1 collective-permute-start.12
  59.9 0.5 collective-permute-start.24
  60.4 0.8 collective-permute-done.20
  61.2 4.2 %collective-permute-start.21 = (bf16[192,512]{1,0:T(8,128)(2,1)S(1)}, bf16[192,512]{1,0:T(8,128)(2,1)S(1)}, u32[]{:S(2)}, u32[]{:S(2)}) collective-permute-start(bf16[192,512]{1,0:T(8,128)(2,1)S(1)} %fusion.3.first_ref), channel_id=1, source_target_pairs={{0,8},{2,10},{4,12},{6,14},{8,0},{10,2},{12,4},{14,6},{1,9},{3,11}... | collective-permute-start | bytes 589832 | tf_op jit(solution)/shard_map/ppermute | solution.py:224
  65.4 1.8 %expert.7 = (f32[2,192,512]{2,1,0:T(8,128)S(1)}, bf16[2,192,512]{2,1,0:T(8,128)(2,1)S(1)}) custom-call(s32[1]{0:T(128)} %bitcast.core_ref, bf16[192,512]{1,0:T(8,128)(2,1)S(1)} %collective-permute-done.22.p_ref, bf16[192,512]{1,0:T(8,128)(2,1)S(1)} %collective-permute-done.23.q_ref, bf16[192,512]{1,0:T(8,128)(2,1)S(1)} %collective-permute-done.24.p2_ref, ...), custom_call_target="tpu_custom_call" | custom-call | tf_op jit(solution)/shard_map/expert/pallas_call | solution.py:24
  67.3 0.1 collective-permute-start.26
  67.4 0.1 convert_add_fusion.2
  67.5 1.6 %collective-permute-start.13 = (bf16[192,512]{1,0:T(8,128)(2,1)S(1)}, bf16[192,512]{1,0:T(8,128)(2,1)S(1)}, u32[]{:S(2)}, u32[]{:S(2)}) collective-permute-start(bf16[192,512]{1,0:T(8,128)(2,1)S(1)} %fusion.9), channel_id=1, source_target_pairs={{0,2},{2,0},{4,6},{6,4},{8,10},{10,8},{12,14},{14,12},{1,3},{3,1},... | collective-permute-start | bytes 589832 | tf_op jit(solution)/shard_map/ppermute | solution.py:219
  69.1 0.1 convert_add_fusion
  69.2 1.5 %collective-permute-start.27 = (bf16[192,512]{1,0:T(8,128)(2,1)S(1)}, bf16[192,512]{1,0:T(8,128)(2,1)S(1)}, u32[]{:S(2)}, u32[]{:S(2)}) collective-permute-start(bf16[192,512]{1,0:T(8,128)(2,1)S(1)} %fusion.11), channel_id=1, source_target_pairs={{0,2},{2,0},{4,6},{6,4},{8,10},{10,8},{12,14},{14,12},{1,3},{3,1},... | collective-permute-start | bytes 589832 | tf_op jit(solution)/shard_map/ppermute | solution.py:219
  70.8 4.5 %collective-permute-done.13 = bf16[192,512]{1,0:T(8,128)(2,1)S(1)} collective-permute-done((bf16[192,512]{1,0:T(8,128)(2,1)S(1)}, bf16[192,512]{1,0:T(8,128)(2,1)S(1)}, u32[]{:S(2)}, u32[]{:S(2)}) %collective-permute-start.13) | collective-permute-done | bytes 196640 | tf_op jit(solution)/shard_map/ppermute | solution.py:219
  75.3 0.5 collective-permute-start.14
  75.8 3.3 %collective-permute-done.27 = bf16[192,512]{1,0:T(8,128)(2,1)S(1)} collective-permute-done((bf16[192,512]{1,0:T(8,128)(2,1)S(1)}, bf16[192,512]{1,0:T(8,128)(2,1)S(1)}, u32[]{:S(2)}, u32[]{:S(2)}) %collective-permute-start.27) | collective-permute-done | bytes 196640 | tf_op jit(solution)/shard_map/ppermute | solution.py:219
  79.1 0.1 fusion.1
  79.1 0.1 collective-permute-start.28
  79.2 0.1 collective-permute-start.1
  79.3 1.1 %collective-permute-done.1.other_gates_ref = f32[2,128]{1,0:T(2,128)S(1)} collective-permute-done((f32[2,128]{1,0:T(2,128)S(1)}, f32[2,128]{1,0:T(2,128)S(1)}, u32[]{:S(2)}, u32[]{:S(2)}) %collective-permute-start.1) | collective-permute-done | bytes 1056 | tf_op jit(solution)/shard_map/ppermute | solution.py:214
  80.4 1.1 %collective-permute-done.14.rest_1_ = bf16[192,512]{1,0:T(8,128)(2,1)S(1)} collective-permute-done((bf16[192,512]{1,0:T(8,128)(2,1)S(1)}, bf16[192,512]{1,0:T(8,128)(2,1)S(1)}, u32[]{:S(2)}, u32[]{:S(2)}) %collective-permute-start.14) | collective-permute-done | bytes 196640 | tf_op jit(solution)/shard_map/ppermute | solution.py:224
  81.5 6.0 %collective-permute-done.28.rest_3_ = bf16[192,512]{1,0:T(8,128)(2,1)S(1)} collective-permute-done((bf16[192,512]{1,0:T(8,128)(2,1)S(1)}, bf16[192,512]{1,0:T(8,128)(2,1)S(1)}, u32[]{:S(2)}, u32[]{:S(2)}) %collective-permute-start.28) | collective-permute-done | bytes 196640 | tf_op jit(solution)/shard_map/ppermute | solution.py:224
  87.5 0.9 %combine.1 = (f32[128,512]{1,0:T(8,128)S(1)}, bf16[128,512]{1,0:T(8,128)(2,1)S(1)}) custom-call(s32[1]{0:T(128)} %bitcast.core_ref, s32[1]{0:T(128)} %bitcast.10.line_ref, s32[2,2,128]{2,1,0:T(2,128)S(1)} %bitcast.49, f32[2,128]{1,0:T(2,128)S(1)} %get-tuple-element.24.own_gates_ref, f32[2,128]{1,0:T(2,128)S(1)} %collective-permute-done.1.other_gates_ref, ...), custom_call_target="tpu_custom_call" | custom-call | tf_op jit(solution)/shard_map/combine/pallas_call | solution.py:24
  88.4 0.1 collective-permute-start.29
  88.5 1.3 %collective-permute-done.29.other_ref = bf16[128,512]{1,0:T(8,128)(2,1)S(1)} collective-permute-done((bf16[128,512]{1,0:T(8,128)(2,1)S(1)}, bf16[128,512]{1,0:T(8,128)(2,1)S(1)}, u32[]{:S(2)}, u32[]{:S(2)}) %collective-permute-start.29) | collective-permute-done | bytes 131104 | tf_op jit(solution)/shard_map/ppermute | solution.py:214
  89.9 0.8 finish.1
  (45 shorter events, 0.3 us)
Async XLA Ops:
  1.0 1.5 %collective-permute-start = (bf16[2,80,512]{2,1,0:T(8,128)(2,1)S(1)}, bf16[2,80,512]{2,1,0:T(8,128)(2,1)S(1)}, u32[]{:S(2)}, u32[]{:S(2)}) collective-permute-start(bf16[2,80,512]{2,1,0:T(8,128)(2,1)S(1)} %get-tuple-element.41), channel_id=1, source_target_pairs={{0,1},{1,0},{2,3},{3,2},{4,5},{5,4},{6,7},{7,6},{8,9},{9,8},{10,11... | collective-permute-start | bytes 491528 | tf_op jit(solution)/shard_map/ppermute | solution.py:214
  2.6 0.9 %copy-start.4 = (bf16[1,128,1024]{2,1,0:T(8,128)(2,1)S(1)}, bf16[1,128,1024]{2,1,0:T(8,128)(2,1)}, u32[]{:S(2)}) copy-start(bf16[1,128,1024]{2,1,0:T(8,128)(2,1)} %param.11) | copy-start | bytes 786436
  3.5 0.7 copy-start.5
  4.2 0.7 copy-start.8
  4.9 0.7 copy-start.9
  5.6 0.7 copy-start.10
  6.3 0.7 copy-start.11
  10.2 1.4 %collective-permute-start.2 = (bf16[128,512]{1,0:T(8,128)(2,1)S(1)}, bf16[128,512]{1,0:T(8,128)(2,1)S(1)}, u32[]{:S(2)}, u32[]{:S(2)}) collective-permute-start(bf16[128,512]{1,0:T(8,128)(2,1)S(1)} %get-tuple-element.26), channel_id=1, source_target_pairs={{0,1},{1,0},{2,3},{3,2},{4,5},{5,4},{6,7},{7,6},{8,9},{9,8},{10,11... | collective-permute-start | bytes 393224 | tf_op jit(solution)/shard_map/ppermute | solution.py:214
  11.6 0.7 copy-start.6
  12.8 8.1 %collective-permute-start.3 = (bf16[192,512]{1,0:T(8,128)(2,1)S(1)}, bf16[192,512]{1,0:T(8,128)(2,1)S(1)}, u32[]{:S(2)}, u32[]{:S(2)}) collective-permute-start(bf16[192,512]{1,0:T(8,128)(2,1)S(1)} %get-tuple-element.27.p_ref), channel_id=1, source_target_pairs={{0,2},{2,0},{4,6},{6,4},{8,10},{10,8},{12,14},{14,12},{1,3},{3,1},... | collective-permute-start | bytes 589832 | tf_op jit(solution)/shard_map/ppermute | solution.py:219
  15.7 17.1 %collective-permute-start.15 = (bf16[192,512]{1,0:T(8,128)(2,1)S(1)}, bf16[192,512]{1,0:T(8,128)(2,1)S(1)}, u32[]{:S(2)}, u32[]{:S(2)}) collective-permute-start(bf16[192,512]{1,0:T(8,128)(2,1)S(1)} %get-tuple-element.33), channel_id=1, source_target_pairs={{0,8},{2,10},{4,12},{6,14},{8,0},{10,2},{12,4},{14,6},{1,9},{3,11}... | collective-permute-start | bytes 589832 | tf_op jit(solution)/shard_map/ppermute | solution.py:224
  18.3 14.7 %collective-permute-start.8 = (bf16[192,512]{1,0:T(8,128)(2,1)S(1)}, bf16[192,512]{1,0:T(8,128)(2,1)S(1)}, u32[]{:S(2)}, u32[]{:S(2)}) collective-permute-start(bf16[192,512]{1,0:T(8,128)(2,1)S(1)} %get-tuple-element.30), channel_id=1, source_target_pairs={{0,4},{2,6},{4,8},{6,10},{8,12},{10,14},{12,0},{14,2},{1,5},{3,7},... | collective-permute-start | bytes 589832 | tf_op jit(solution)/shard_map/ppermute | solution.py:224
  19.9 15.0 %collective-permute-start.4 = (bf16[192,512]{1,0:T(8,128)(2,1)S(1)}, bf16[192,512]{1,0:T(8,128)(2,1)S(1)}, u32[]{:S(2)}, u32[]{:S(2)}) collective-permute-start(bf16[192,512]{1,0:T(8,128)(2,1)S(1)} %get-tuple-element.27.p_ref), channel_id=1, source_target_pairs={{0,1},{1,0},{2,3},{3,2},{4,5},{5,4},{6,7},{7,6},{8,9},{9,8},{10,11... | collective-permute-start | bytes 589832 | tf_op jit(solution)/shard_map/ppermute | solution.py:214
  21.0 14.0 %collective-permute-start.5 = (bf16[192,512]{1,0:T(8,128)(2,1)S(1)}, bf16[192,512]{1,0:T(8,128)(2,1)S(1)}, u32[]{:S(2)}, u32[]{:S(2)}) collective-permute-start(bf16[192,512]{1,0:T(8,128)(2,1)S(1)} %collective-permute-done.3.q_ref), channel_id=1, source_target_pairs={{0,1},{1,0},{2,3},{3,2},{4,5},{5,4},{6,7},{7,6},{8,9},{9,8},{10,11... | collective-permute-start | bytes 589832 | tf_op jit(solution)/shard_map/ppermute | solution.py:214
  21.0 19.6 %collective-permute-start.22 = (bf16[192,512]{1,0:T(8,128)(2,1)S(1)}, bf16[192,512]{1,0:T(8,128)(2,1)S(1)}, u32[]{:S(2)}, u32[]{:S(2)}) collective-permute-start(bf16[192,512]{1,0:T(8,128)(2,1)S(1)} %get-tuple-element.36), channel_id=1, source_target_pairs={{0,12},{2,14},{4,0},{6,2},{8,4},{10,6},{12,8},{14,10},{1,13},{3,15... | collective-permute-start | bytes 589832 | tf_op jit(solution)/shard_map/ppermute | solution.py:224
  32.9 7.8 %collective-permute-start.16 = (bf16[192,512]{1,0:T(8,128)(2,1)S(1)}, bf16[192,512]{1,0:T(8,128)(2,1)S(1)}, u32[]{:S(2)}, u32[]{:S(2)}) collective-permute-start(bf16[192,512]{1,0:T(8,128)(2,1)S(1)} %collective-permute-done.15.p_ref), channel_id=1, source_target_pairs={{0,2},{2,0},{4,6},{6,4},{8,10},{10,8},{12,14},{14,12},{1,3},{3,1},... | collective-permute-start | bytes 589832 | tf_op jit(solution)/shard_map/ppermute | solution.py:219
  33.1 8.8 %collective-permute-start.9 = (bf16[192,512]{1,0:T(8,128)(2,1)S(1)}, bf16[192,512]{1,0:T(8,128)(2,1)S(1)}, u32[]{:S(2)}, u32[]{:S(2)}) collective-permute-start(bf16[192,512]{1,0:T(8,128)(2,1)S(1)} %collective-permute-done.8.p_ref), channel_id=1, source_target_pairs={{0,2},{2,0},{4,6},{6,4},{8,10},{10,8},{12,14},{14,12},{1,3},{3,1},... | collective-permute-start | bytes 589832 | tf_op jit(solution)/shard_map/ppermute | solution.py:219
  34.9 1.6 %copy-start = (bf16[1024,1024]{1,0:T(8,128)(2,1)S(1)}, bf16[1024,1024]{1,0:T(8,128)(2,1)}, u32[]{:S(2)}) copy-start(bf16[1024,1024]{1,0:T(8,128)(2,1)} %in_ref.7) | copy-start | bytes 6291460
  36.5 1.6 %copy-start.2 = (bf16[1024,1024]{1,0:T(8,128)(2,1)S(1)}, bf16[1024,1024]{1,0:T(8,128)(2,1)}, u32[]{:S(2)}) copy-start(bf16[1024,1024]{1,0:T(8,128)(2,1)} %out_ref.7) | copy-start | bytes 6291460
  38.1 9.3 %copy-start.1 = (bf16[1024,1024]{1,0:T(8,128)(2,1)S(1)}, bf16[1024,1024]{1,0:T(8,128)(2,1)}, u32[]{:S(2)}) copy-start(bf16[1024,1024]{1,0:T(8,128)(2,1)} %in_ref.7) | copy-start | bytes 6291460
  38.1 9.3 %copy-start.3 = (bf16[1024,1024]{1,0:T(8,128)(2,1)S(1)}, bf16[1024,1024]{1,0:T(8,128)(2,1)}, u32[]{:S(2)}) copy-start(bf16[1024,1024]{1,0:T(8,128)(2,1)} %out_ref.7) | copy-start | bytes 6291460
  40.0 9.9 %collective-permute-start.6 = (bf16[2,192,512]{2,1,0:T(8,128)(2,1)S(1)}, bf16[2,192,512]{2,1,0:T(8,128)(2,1)S(1)}, u32[]{:S(2)}, u32[]{:S(2)}) collective-permute-start(bf16[2,192,512]{2,1,0:T(8,128)(2,1)S(1)} %get-tuple-element.29), channel_id=1, source_target_pairs={{0,1},{1,0},{2,3},{3,2},{4,5},{5,4},{6,7},{7,6},{8,9},{9,8},{10,11... | collective-permute-start | bytes 1179656 | tf_op jit(solution)/shard_map/ppermute | solution.py:214
  40.0 2.0 %collective-permute-start.17 = (bf16[192,512]{1,0:T(8,128)(2,1)S(1)}, bf16[192,512]{1,0:T(8,128)(2,1)S(1)}, u32[]{:S(2)}, u32[]{:S(2)}) collective-permute-start(bf16[192,512]{1,0:T(8,128)(2,1)S(1)} %collective-permute-done.15.p_ref), channel_id=1, source_target_pairs={{0,1},{1,0},{2,3},{3,2},{4,5},{5,4},{6,7},{7,6},{8,9},{9,8},{10,11... | collective-permute-start | bytes 589832 | tf_op jit(solution)/shard_map/ppermute | solution.py:214
  40.5 6.9 %collective-permute-start.23 = (bf16[192,512]{1,0:T(8,128)(2,1)S(1)}, bf16[192,512]{1,0:T(8,128)(2,1)S(1)}, u32[]{:S(2)}, u32[]{:S(2)}) collective-permute-start(bf16[192,512]{1,0:T(8,128)(2,1)S(1)} %collective-permute-done.22.p_ref), channel_id=1, source_target_pairs={{0,2},{2,0},{4,6},{6,4},{8,10},{10,8},{12,14},{14,12},{1,3},{3,1},... | collective-permute-start | bytes 589832 | tf_op jit(solution)/shard_map/ppermute | solution.py:219
  40.7 6.7 %collective-permute-start.18 = (bf16[192,512]{1,0:T(8,128)(2,1)S(1)}, bf16[192,512]{1,0:T(8,128)(2,1)S(1)}, u32[]{:S(2)}, u32[]{:S(2)}) collective-permute-start(bf16[192,512]{1,0:T(8,128)(2,1)S(1)} %collective-permute-done.16.q_ref), channel_id=1, source_target_pairs={{0,1},{1,0},{2,3},{3,2},{4,5},{5,4},{6,7},{7,6},{8,9},{9,8},{10,11... | collective-permute-start | bytes 589832 | tf_op jit(solution)/shard_map/ppermute | solution.py:214
  41.8 8.0 %collective-permute-start.11 = (bf16[192,512]{1,0:T(8,128)(2,1)S(1)}, bf16[192,512]{1,0:T(8,128)(2,1)S(1)}, u32[]{:S(2)}, u32[]{:S(2)}) collective-permute-start(bf16[192,512]{1,0:T(8,128)(2,1)S(1)} %collective-permute-done.9.q_ref), channel_id=1, source_target_pairs={{0,1},{1,0},{2,3},{3,2},{4,5},{5,4},{6,7},{7,6},{8,9},{9,8},{10,11... | collective-permute-start | bytes 589832 | tf_op jit(solution)/shard_map/ppermute | solution.py:214
  42.0 15.9 %collective-permute-start.10 = (bf16[192,512]{1,0:T(8,128)(2,1)S(1)}, bf16[192,512]{1,0:T(8,128)(2,1)S(1)}, u32[]{:S(2)}, u32[]{:S(2)}) collective-permute-start(bf16[192,512]{1,0:T(8,128)(2,1)S(1)} %collective-permute-done.8.p_ref), channel_id=1, source_target_pairs={{0,1},{1,0},{2,3},{3,2},{4,5},{5,4},{6,7},{7,6},{8,9},{9,8},{10,11... | collective-permute-start | bytes 589832 | tf_op jit(solution)/shard_map/ppermute | solution.py:214
  47.4 12.9 %collective-permute-start.25 = (bf16[192,512]{1,0:T(8,128)(2,1)S(1)}, bf16[192,512]{1,0:T(8,128)(2,1)S(1)}, u32[]{:S(2)}, u32[]{:S(2)}) collective-permute-start(bf16[192,512]{1,0:T(8,128)(2,1)S(1)} %collective-permute-done.23.q_ref), channel_id=1, source_target_pairs={{0,1},{1,0},{2,3},{3,2},{4,5},{5,4},{6,7},{7,6},{8,9},{9,8},{10,11... | collective-permute-start | bytes 589832 | tf_op jit(solution)/shard_map/ppermute | solution.py:214
  49.3 1.9 %collective-permute-start.19 = (bf16[2,192,512]{2,1,0:T(8,128)(2,1)S(1)}, bf16[2,192,512]{2,1,0:T(8,128)(2,1)S(1)}, u32[]{:S(2)}, u32[]{:S(2)}) collective-permute-start(bf16[2,192,512]{2,1,0:T(8,128)(2,1)S(1)} %get-tuple-element.35), channel_id=1, source_target_pairs={{0,1},{1,0},{2,3},{3,2},{4,5},{5,4},{6,7},{7,6},{8,9},{9,8},{10,11... | collective-permute-start | bytes 1179656 | tf_op jit(solution)/shard_map/ppermute | solution.py:214
  50.0 7.8 %collective-permute-start.7 = (bf16[192,512]{1,0:T(8,128)(2,1)S(1)}, bf16[192,512]{1,0:T(8,128)(2,1)S(1)}, u32[]{:S(2)}, u32[]{:S(2)}) collective-permute-start(bf16[192,512]{1,0:T(8,128)(2,1)S(1)} %fusion.8), channel_id=1, source_target_pairs={{0,2},{2,0},{4,6},{6,4},{8,10},{10,8},{12,14},{14,12},{1,3},{3,1},... | collective-permute-start | bytes 589832 | tf_op jit(solution)/shard_map/ppermute | solution.py:219
  51.4 9.8 %collective-permute-start.20 = (bf16[192,512]{1,0:T(8,128)(2,1)S(1)}, bf16[192,512]{1,0:T(8,128)(2,1)S(1)}, u32[]{:S(2)}, u32[]{:S(2)}) collective-permute-start(bf16[192,512]{1,0:T(8,128)(2,1)S(1)} %fusion.10), channel_id=1, source_target_pairs={{0,2},{2,0},{4,6},{6,4},{8,10},{10,8},{12,14},{14,12},{1,3},{3,1},... | collective-permute-start | bytes 589832 | tf_op jit(solution)/shard_map/ppermute | solution.py:219
  59.8 7.6 %collective-permute-start.12 = (bf16[2,192,512]{2,1,0:T(8,128)(2,1)S(1)}, bf16[2,192,512]{2,1,0:T(8,128)(2,1)S(1)}, u32[]{:S(2)}, u32[]{:S(2)}) collective-permute-start(bf16[2,192,512]{2,1,0:T(8,128)(2,1)S(1)} %get-tuple-element.32), channel_id=1, source_target_pairs={{0,1},{1,0},{2,3},{3,2},{4,5},{5,4},{6,7},{7,6},{8,9},{9,8},{10,11... | collective-permute-start | bytes 1179656 | tf_op jit(solution)/shard_map/ppermute | solution.py:214
  59.9 5.6 %collective-permute-start.24 = (bf16[192,512]{1,0:T(8,128)(2,1)S(1)}, bf16[192,512]{1,0:T(8,128)(2,1)S(1)}, u32[]{:S(2)}, u32[]{:S(2)}) collective-permute-start(bf16[192,512]{1,0:T(8,128)(2,1)S(1)} %collective-permute-done.22.p_ref), channel_id=1, source_target_pairs={{0,1},{1,0},{2,3},{3,2},{4,5},{5,4},{6,7},{7,6},{8,9},{9,8},{10,11... | collective-permute-start | bytes 589832 | tf_op jit(solution)/shard_map/ppermute | solution.py:214
  61.2 19.2 %collective-permute-start.21 = (bf16[192,512]{1,0:T(8,128)(2,1)S(1)}, bf16[192,512]{1,0:T(8,128)(2,1)S(1)}, u32[]{:S(2)}, u32[]{:S(2)}) collective-permute-start(bf16[192,512]{1,0:T(8,128)(2,1)S(1)} %fusion.3.first_ref), channel_id=1, source_target_pairs={{0,8},{2,10},{4,12},{6,14},{8,0},{10,2},{12,4},{14,6},{1,9},{3,11}... | collective-permute-start | bytes 589832 | tf_op jit(solution)/shard_map/ppermute | solution.py:224
  67.3 1.8 %collective-permute-start.26 = (bf16[2,192,512]{2,1,0:T(8,128)(2,1)S(1)}, bf16[2,192,512]{2,1,0:T(8,128)(2,1)S(1)}, u32[]{:S(2)}, u32[]{:S(2)}) collective-permute-start(bf16[2,192,512]{2,1,0:T(8,128)(2,1)S(1)} %get-tuple-element.38), channel_id=1, source_target_pairs={{0,1},{1,0},{2,3},{3,2},{4,5},{5,4},{6,7},{7,6},{8,9},{9,8},{10,11... | collective-permute-start | bytes 1179656 | tf_op jit(solution)/shard_map/ppermute | solution.py:214
  67.5 20.0 %copy-start.7 = (s32[2,128,2]{1,2,0:T(2,128)S(1)}, s32[2,128,2]{1,2,0:T(2,128)}, u32[]{:S(2)}) copy-start(s32[2,128,2]{1,2,0:T(2,128)} %param.16) | copy-start | bytes 6148
  67.5 7.8 %collective-permute-start.13 = (bf16[192,512]{1,0:T(8,128)(2,1)S(1)}, bf16[192,512]{1,0:T(8,128)(2,1)S(1)}, u32[]{:S(2)}, u32[]{:S(2)}) collective-permute-start(bf16[192,512]{1,0:T(8,128)(2,1)S(1)} %fusion.9), channel_id=1, source_target_pairs={{0,2},{2,0},{4,6},{6,4},{8,10},{10,8},{12,14},{14,12},{1,3},{3,1},... | collective-permute-start | bytes 589832 | tf_op jit(solution)/shard_map/ppermute | solution.py:219
  69.2 9.9 %collective-permute-start.27 = (bf16[192,512]{1,0:T(8,128)(2,1)S(1)}, bf16[192,512]{1,0:T(8,128)(2,1)S(1)}, u32[]{:S(2)}, u32[]{:S(2)}) collective-permute-start(bf16[192,512]{1,0:T(8,128)(2,1)S(1)} %fusion.11), channel_id=1, source_target_pairs={{0,2},{2,0},{4,6},{6,4},{8,10},{10,8},{12,14},{14,12},{1,3},{3,1},... | collective-permute-start | bytes 589832 | tf_op jit(solution)/shard_map/ppermute | solution.py:219
  75.3 6.2 %collective-permute-start.14 = (bf16[192,512]{1,0:T(8,128)(2,1)S(1)}, bf16[192,512]{1,0:T(8,128)(2,1)S(1)}, u32[]{:S(2)}, u32[]{:S(2)}) collective-permute-start(bf16[192,512]{1,0:T(8,128)(2,1)S(1)} %fusion.5), channel_id=1, source_target_pairs={{0,12},{2,14},{4,0},{6,2},{8,4},{10,6},{12,8},{14,10},{1,13},{3,15... | collective-permute-start | bytes 589832 | tf_op jit(solution)/shard_map/ppermute | solution.py:224
  79.1 8.4 %collective-permute-start.28 = (bf16[192,512]{1,0:T(8,128)(2,1)S(1)}, bf16[192,512]{1,0:T(8,128)(2,1)S(1)}, u32[]{:S(2)}, u32[]{:S(2)}) collective-permute-start(bf16[192,512]{1,0:T(8,128)(2,1)S(1)} %fusion.1), channel_id=1, source_target_pairs={{0,4},{2,6},{4,8},{6,10},{8,12},{10,14},{12,0},{14,2},{1,5},{3,7},... | collective-permute-start | bytes 589832 | tf_op jit(solution)/shard_map/ppermute | solution.py:224
  79.2 1.2 %collective-permute-start.1 = (f32[2,128]{1,0:T(2,128)S(1)}, f32[2,128]{1,0:T(2,128)S(1)}, u32[]{:S(2)}, u32[]{:S(2)}) collective-permute-start(f32[2,128]{1,0:T(2,128)S(1)} %get-tuple-element.24.own_gates_ref), channel_id=1, source_target_pairs={{0,1},{1,0},{2,3},{3,2},{4,5},{5,4},{6,7},{7,6},{8,9},{9,8},{10,11... | collective-permute-start | bytes 3080 | tf_op jit(solution)/shard_map/ppermute | solution.py:214
  88.4 1.4 %collective-permute-start.29 = (bf16[128,512]{1,0:T(8,128)(2,1)S(1)}, bf16[128,512]{1,0:T(8,128)(2,1)S(1)}, u32[]{:S(2)}, u32[]{:S(2)}) collective-permute-start(bf16[128,512]{1,0:T(8,128)(2,1)S(1)} %get-tuple-element.40), channel_id=1, source_target_pairs={{0,1},{1,0},{2,3},{3,2},{4,5},{5,4},{6,7},{7,6},{8,9},{9,8},{10,11... | collective-permute-start | bytes 393224 | tf_op jit(solution)/shard_map/ppermute | solution.py:214

commit v7 on v6

--- a/solution.py
+++ b/solution.py
@@ -136,7 +136,7 @@
     ids = lax.broadcasted_iota(jnp.int32, slot.shape, 0)
     numbers = lax.broadcasted_iota(jnp.int32, (capacity, slot.shape[1]), 0).astype(jnp.float32)
     for offset, piece_ref in enumerate(pieces):
-        expert = lax.rem(line_ref[0] + offset, experts_count)
+        expert = line_ref[0] ^ offset
         wanted = jnp.sum(jnp.where(ids == expert, slot, 0.0), axis=0, keepdims=True)
         picks = jnp.where(numbers == wanted, 1.0, 0.0).astype(jnp.bfloat16)
         piece_ref[...] = jnp.dot(
@@ -186,8 +186,7 @@
         for k in range(2):
             route = routes_ref[sent, k : k + 1]
             slot = jnp.sum(jnp.where(ids == route, slots, 0.0), axis=0, keepdims=True)
-            offset = lax.rem(route - line_ref[0] + experts_count, experts_count)
-            place = offset.astype(jnp.float32) * capacity + slot
+            place = (route ^ line_ref[0]).astype(jnp.float32) * capacity + slot
             place, gate = (
                 jnp.broadcast_to(row, (full_len, full_len)).T[:, :1]
                 for row in (place, gates_ref[sent, k : k + 1])
@@ -219,32 +218,29 @@
     return lax.ppermute(values, "expert", [(i, i ^ 1) for i in range(owners)])
 
 
-def shift(values, offset):
+def exchange(values, offset):
     owners = lax.axis_size("expert")
-    return lax.ppermute(
-        values, "expert", [(i, (i + 2 * offset) % owners) for i in range(owners)]
-    )
-
-
-def after_kernel(value_ref, first_ref, out_ref):
+    return lax.ppermute(values, "expert", [(i, i ^ (2 * offset)) for i in range(owners)])
+
+
+def after_kernel(*refs):
     pass
 
 
-def after(value, first):
-    anywhere = pl.BlockSpec(memory_space=pl.ANY)
+def after(value, *firsts):
     return pl.pallas_call(
         after_kernel,
         out_shape=jax.ShapeDtypeStruct(value.shape, value.dtype),
-        in_specs=[anywhere, anywhere],
-        out_specs=anywhere,
+        in_specs=[pl.BlockSpec(memory_space=pl.ANY)] * (1 + len(firsts)),
+        out_specs=pl.BlockSpec(memory_space=pl.ANY),
         input_output_aliases={0: 0},
         compiler_params=pltpu.CompilerParams(vmem_limit_bytes=2**20),
         name="after",
-    )(value, first)
+    )(value, *firsts)
 
 
 def piece_order(count):
-    return sorted(range(count), key=lambda offset: (offset > 0, -min(offset, count - offset)))
+    return [0, *range(2, count), 1]
 
 
 def attend(
@@ -295,19 +291,26 @@
         [routes, keep, other],
         scratch=[pltpu.VMEM((2 * full_len, half), jnp.bfloat16)],
     )
-    travelling = [shift(selected[r], r) for r in range(1, count)]
+    travelling = [exchange(selected[r], r) for r in range(1, count)]
+    order = piece_order(count)
     home = [None] * count
-    home = [None] * count
-    kepts, halves, wholes = [], [], []
-    for at, offset in enumerate(piece_order(count)):
+    qs, kepts, halves, wholes, homes = [], [], [], [], []
+    for at, offset in enumerate(order):
         p = travelling[offset - 1] if offset else selected[0]
+        if at < count - 1:
+            coming = travelling[order[at + 1] - 1]
         q = swap_owner(p)
+        if at == 0:
+            q = after(q, coming)
+        if at == 1:
+            q = after(q, coming, kepts[at - 1])
+        if at == 2:
+            q = after(q, coming, wholes[at - 2])
+        if at == 3:
+            q = after(q, wholes[at - 2])
+        qs.append(q)
         p2 = swap(p)
         q2 = swap(q)
-        if at >= 2:
-            q2 = after(q2, kepts[at - 2])
-        if at >= 2:
-            q2 = after(q2, wholes[at - 2])
         kept, sent = call(
             expert_kernel,
             "expert",
@@ -318,11 +321,15 @@
             vmem_mib=16,
         )
         kepts.append(kept)
-        both = kept + swap(sent).astype(jnp.float32)
+        moved = swap(sent)
+        if at == 3:
+            moved = after(moved, wholes[at - 1])
+        both = kept + moved.astype(jnp.float32)
         halves.append(both[1].astype(jnp.bfloat16))
         across = swap_owner(halves[-1])
         wholes.append((both[0] + across.astype(jnp.float32)).astype(jnp.bfloat16))
-        home[offset] = shift(wholes[-1], -offset) if offset else wholes[-1]
+        homes.append(exchange(wholes[-1], offset) if offset else wholes[-1])
+        home[offset] = homes[-1]
     own_sum, other_sum = call(
         combine_kernel,
         "combine",
@@ -428,7 +435,7 @@
     block_rows = routes.shape[0] * routes.shape[1]
     experts_count = router.shape[1]
     capacity = 2 * max(1, 3 * block_rows // (2 * experts_count))
-    if capacity % 16 == 0:
+    if capacity % 16 == 0 and experts_count & (experts_count - 1) == 0:
         mixed = line_experts(core, state, keep, send, gates, by_choice, fc_in, fc_out, capacity)
     else:
         halves = jnp.stack([keep, send])

time: 91 us -> 97.9 us (1.076)
  waiting for transfers between devices: 41.4 us -> 52.2 us
  starting transfers between devices: 25.5 us -> 23.1 us
  local copies, waits for them, and re-layouts: 8.33 us -> 6.74 us
    ppermute x6, waiting for transfers between devices: 15.2 us -> 25.1 us  [exchange(): lax.ppermute(values, 'expert', [(i, i ^ 2 * offset) for i in range(owners)])]
    ppermute x16, waiting for transfers between devices: 4.89 us -> 6.72 us  [swap(): return lax.ppermute(values, 'section', [(0, 1), (1, 0)])]
    unnamed x24 -> x20, local copies, waits for them, and re-layouts: 8.23 us -> 6.64 us
    ppermute x16, starting transfers between devices: 3.19 us -> 1.88 us  [swap(): return lax.ppermute(values, 'section', [(0, 1), (1, 0)])]
    ppermute x8, starting transfers between devices: 9.53 us -> 8.52 us  [swap_owner(): return lax.ppermute(values, 'expert', [(i, i ^ 1) for i in range(owners)])]
  transfers between devices with their start and end apart: 30 -> 30, of which waited for: 16 -> 21; matrix products, arithmetic and copies ran while one was open for 1% -> 1% of each run, Pallas kernels for 8% -> 6%
where the time goes in v7:
time: 97.9 us; the launch traced here: 97.5 us
  waiting for transfers between devices  52.2 us (53%)
  starting transfers between devices  23.1 us (24%)
  Pallas kernels  12.8 us (13%)
  local copies, waits for them, and re-layouts  6.74 us (7%)
  other arithmetic  1.84 us (2%)
    ppermute x6, waiting for transfers between devices, exchange(): lax.ppermute(values, 'expert', [(i, i ^ 2 * offset) for i in range(owners)])  25.1 us
    ppermute x8, waiting for transfers between devices, swap_owner(): return lax.ppermute(values, 'expert', [(i, i ^ 1) for i in range(owners)])  20.4 us
    pallas_call x8, Pallas kernels, call(): pl.pallas_call(kernel, out_shape=tuple((jax.ShapeDtypeStruct(*out) for ou...  12.8 us
    ppermute x6, starting transfers between devices, exchange(): lax.ppermute(values, 'expert', [(i, i ^ 2 * offset) for i in range(owners)])  12.7 us
    ppermute x8, starting transfers between devices, swap_owner(): return lax.ppermute(values, 'expert', [(i, i ^ 1) for i in range(owners)])  8.52 us
    ppermute x16, waiting for transfers between devices, swap(): return lax.ppermute(values, 'section', [(0, 1), (1, 0)])  6.72 us
    unnamed x20, local copies, waits for them, and re-layouts  6.64 us
  transfers between devices with their start and end apart: 30, of which 21 were waited for; matrix products, arithmetic and copies ran while one was open for 1% of the time, Pallas kernels for 6%

profile of v7, /device:TPU:0, one launch (start us, length us, event | category | flops | bytes accessed | tf_op | source)
XLA Modules:
  0.0 97.5 jit_solution(11609429562083778619)
XLA Ops:
  0.0 1.2 %fusion.13 = (bf16[2,80,512]{2,1,0:T(8,128)(2,1)S(1)}, bf16[2,80,512]{2,1,0:T(8,128)(2,1)S(1)}) fusion(s32[]{:T(128)S(6)} %select_n.13, bf16[2,1,80,512]{3,2,0,1:T(8,128)(2,1)} %bitcast.53, bf16[2,1,80,512]{3,2,0,1:T(8,128)(2,1)} %bitcast.54, s32[]{:T(128)S(6)} %select_n.12), kind=kLoop, calls=%fused_computation.29 | loop fusion | flops 163840 | bytes 655368 | tf_op jit(solution)/shard_map/jit(dynamic_index_in_dim)/squeeze | solution.py:253
  1.2 0.5 collective-permute-start
  2.4 0.4 collective-permute-done.other_ref
  2.7 0.9 copy-done.2
  3.7 0.7 copy-done.3
  4.4 0.7 copy-done.6
  5.1 0.7 copy-done.7
  5.8 0.7 copy-done.8
  6.4 0.7 copy-done.9
  7.1 3.2 %attend.1 = (bf16[128,1024]{1,0:T(8,128)(2,1)S(1)}, bf16[128,512]{1,0:T(8,128)(2,1)S(1)}, bf16[128,512]{1,0:T(8,128)(2,1)S(1)}, f32[2,128]{1,0:T(2,128)S(1)}) custom-call(s32[1]{0:T(128)} %bitcast.core_ref, s32[1]{0:T(128)S(6)} %copy.22.source_ref, s32[2]{0:T(128)S(1)} %copy-done.9, bf16[128,1024]{1,0:T(8,128)(2,1)S(1)} %bitcast.46, ...), custom_call_target="tpu_custom_call" | custom-call | tf_op jit(solution)/shard_map/attend/pallas_call | solution.py:24
  10.3 0.4 collective-permute-start.2
  10.8 1.0 %collective-permute-done.2.other_ref = bf16[128,512]{1,0:T(8,128)(2,1)S(1)} collective-permute-done((bf16[128,512]{1,0:T(8,128)(2,1)S(1)}, bf16[128,512]{1,0:T(8,128)(2,1)S(1)}, u32[]{:S(2)}, u32[]{:S(2)}) %collective-permute-start.2) | collective-permute-done | bytes 131104 | tf_op jit(solution)/shard_map/ppermute | solution.py:213
  11.8 0.7 copy-done.4
  12.4 0.5 select.5
  13.0 2.9 %collective-permute-start.3 = (bf16[192,512]{1,0:T(8,128)(2,1)S(1)}, bf16[192,512]{1,0:T(8,128)(2,1)S(1)}, u32[]{:S(2)}, u32[]{:S(2)}) collective-permute-start(bf16[192,512]{1,0:T(8,128)(2,1)S(1)} %get-tuple-element.27.p_ref), channel_id=1, source_target_pairs={{0,2},{2,0},{4,6},{6,4},{8,10},{10,8},{12,14},{14,12},{1,3},{3,1},... | collective-permute-start | bytes 589832 | tf_op jit(solution)/shard_map/ppermute | solution.py:218
  15.9 2.6 %collective-permute-start.4 = (bf16[192,512]{1,0:T(8,128)(2,1)S(1)}, bf16[192,512]{1,0:T(8,128)(2,1)S(1)}, u32[]{:S(2)}, u32[]{:S(2)}) collective-permute-start(bf16[192,512]{1,0:T(8,128)(2,1)S(1)} %get-tuple-element.28), channel_id=1, source_target_pairs={{0,8},{2,10},{4,12},{6,14},{8,0},{10,2},{12,4},{14,6},{1,9},{3,11}... | collective-permute-start | bytes 589832 | tf_op jit(solution)/shard_map/ppermute | solution.py:223
  18.5 2.6 %collective-permute-done.3.refs_0_ = bf16[192,512]{1,0:T(8,128)(2,1)S(1)} collective-permute-done((bf16[192,512]{1,0:T(8,128)(2,1)S(1)}, bf16[192,512]{1,0:T(8,128)(2,1)S(1)}, u32[]{:S(2)}, u32[]{:S(2)}) %collective-permute-start.3) | collective-permute-done | bytes 196640 | tf_op jit(solution)/shard_map/ppermute | solution.py:218
  21.1 6.6 %collective-permute-done.4.refs_1_.p_ref = bf16[192,512]{1,0:T(8,128)(2,1)S(1)} collective-permute-done((bf16[192,512]{1,0:T(8,128)(2,1)S(1)}, bf16[192,512]{1,0:T(8,128)(2,1)S(1)}, u32[]{:S(2)}, u32[]{:S(2)}) %collective-permute-start.4) | collective-permute-done | bytes 196640 | tf_op jit(solution)/shard_map/ppermute | solution.py:223
  27.7 1.4 %collective-permute-done.6.q2_ref = bf16[192,512]{1,0:T(8,128)(2,1)S(1)} collective-permute-done((bf16[192,512]{1,0:T(8,128)(2,1)S(1)}, bf16[192,512]{1,0:T(8,128)(2,1)S(1)}, u32[]{:S(2)}, u32[]{:S(2)}) %collective-permute-start.6) | collective-permute-done | bytes 196640 | tf_op jit(solution)/shard_map/ppermute | solution.py:213
  29.1 1.6 %copy-done.1 = bf16[1024,1024]{1,0:T(8,128)(2,1)S(1)} copy-done((bf16[1024,1024]{1,0:T(8,128)(2,1)S(1)}, bf16[1024,1024]{1,0:T(8,128)(2,1)}, u32[]{:S(2)}) %copy-start.1) | copy-done | bytes 2097176
  30.7 1.8 %expert.4 = (f32[2,192,512]{2,1,0:T(8,128)S(1)}, bf16[2,192,512]{2,1,0:T(8,128)(2,1)S(1)}) custom-call(s32[1]{0:T(128)} %bitcast.core_ref, bf16[192,512]{1,0:T(8,128)(2,1)S(1)} %get-tuple-element.27.p_ref, bf16[192,512]{1,0:T(8,128)(2,1)S(1)} %after.5.q_ref, bf16[192,512]{1,0:T(8,128)(2,1)S(1)} %collective-permute-done.5.p2_ref, ...), custom_call_target="tpu_custom_call" | custom-call | tf_op jit(solution)/shard_map/expert/pallas_call | solution.py:24
  32.6 0.2 collective-permute-start.7
  32.8 3.5 %collective-permute-start.12 = (bf16[192,512]{1,0:T(8,128)(2,1)S(1)}, bf16[192,512]{1,0:T(8,128)(2,1)S(1)}, u32[]{:S(2)}, u32[]{:S(2)}) collective-permute-start(bf16[192,512]{1,0:T(8,128)(2,1)S(1)} %get-tuple-element.32), channel_id=1, source_target_pairs={{0,12},{2,14},{4,8},{6,10},{8,4},{10,6},{12,0},{14,2},{1,13},{3,15... | collective-permute-start | bytes 589832 | tf_op jit(solution)/shard_map/ppermute | solution.py:223
  36.3 0.5 collective-permute-start.11
  36.8 5.0 %collective-permute-done.12.refs_1_.p_ref = bf16[192,512]{1,0:T(8,128)(2,1)S(1)} collective-permute-done((bf16[192,512]{1,0:T(8,128)(2,1)S(1)}, bf16[192,512]{1,0:T(8,128)(2,1)S(1)}, u32[]{:S(2)}, u32[]{:S(2)}) %collective-permute-start.12) | collective-permute-done | bytes 196640 | tf_op jit(solution)/shard_map/ppermute | solution.py:223
  41.8 1.3 %collective-permute-done.11.refs_0_ = bf16[192,512]{1,0:T(8,128)(2,1)S(1)} collective-permute-done((bf16[192,512]{1,0:T(8,128)(2,1)S(1)}, bf16[192,512]{1,0:T(8,128)(2,1)S(1)}, u32[]{:S(2)}, u32[]{:S(2)}) %collective-permute-start.11) | collective-permute-done | bytes 196640 | tf_op jit(solution)/shard_map/ppermute | solution.py:218
  43.2 0.1 convert_add_fusion.3
  43.3 0.6 collective-permute-start.8
  43.9 0.7 collective-permute-done.14.q2_ref
  44.6 1.8 %expert.5 = (f32[2,192,512]{2,1,0:T(8,128)S(1)}, bf16[2,192,512]{2,1,0:T(8,128)(2,1)S(1)}) custom-call(s32[1]{0:T(128)} %bitcast.core_ref, bf16[192,512]{1,0:T(8,128)(2,1)S(1)} %collective-permute-done.4.refs_1_.p_ref, bf16[192,512]{1,0:T(8,128)(2,1)S(1)} %after.6.q_ref, bf16[192,512]{1,0:T(8,128)(2,1)S(1)} %collective-permute-done.13.p2_ref, ...), custom_call_target="tpu_custom_call" | custom-call | tf_op jit(solution)/shard_map/expert/pallas_call | solution.py:24
  46.4 0.2 collective-permute-start.15
  46.6 1.7 %collective-permute-start.9 = (bf16[192,512]{1,0:T(8,128)(2,1)S(1)}, bf16[192,512]{1,0:T(8,128)(2,1)S(1)}, u32[]{:S(2)}, u32[]{:S(2)}) collective-permute-start(bf16[192,512]{1,0:T(8,128)(2,1)S(1)} %get-tuple-element.31), channel_id=1, source_target_pairs={{0,4},{2,6},{4,0},{6,2},{8,12},{10,14},{12,8},{14,10},{1,5},{3,7},... | collective-permute-start | bytes 589832 | tf_op jit(solution)/shard_map/ppermute | solution.py:223
  48.3 0.9 collective-permute-start.20
  49.2 1.5 %collective-permute-done.8 = bf16[192,512]{1,0:T(8,128)(2,1)S(1)} collective-permute-done((bf16[192,512]{1,0:T(8,128)(2,1)S(1)}, bf16[192,512]{1,0:T(8,128)(2,1)S(1)}, u32[]{:S(2)}, u32[]{:S(2)}) %collective-permute-start.8) | collective-permute-done | bytes 196640 | tf_op jit(solution)/shard_map/ppermute | solution.py:218
  50.8 3.1 %collective-permute-done.9.p_ref.refs_1_ = bf16[192,512]{1,0:T(8,128)(2,1)S(1)} collective-permute-done((bf16[192,512]{1,0:T(8,128)(2,1)S(1)}, bf16[192,512]{1,0:T(8,128)(2,1)S(1)}, u32[]{:S(2)}, u32[]{:S(2)}) %collective-permute-start.9) | collective-permute-done | bytes 196640 | tf_op jit(solution)/shard_map/ppermute | solution.py:223
  53.8 1.4 %collective-permute-done.20.refs_0_ = bf16[192,512]{1,0:T(8,128)(2,1)S(1)} collective-permute-done((bf16[192,512]{1,0:T(8,128)(2,1)S(1)}, bf16[192,512]{1,0:T(8,128)(2,1)S(1)}, u32[]{:S(2)}, u32[]{:S(2)}) %collective-permute-start.20) | collective-permute-done | bytes 196640 | tf_op jit(solution)/shard_map/ppermute | solution.py:218
  55.2 0.1 convert_add_fusion.2
  55.4 0.9 collective-permute-start.16
  56.3 0.4 collective-permute-done.22.q2_ref
  56.7 1.8 %expert.7 = (f32[2,192,512]{2,1,0:T(8,128)S(1)}, bf16[2,192,512]{2,1,0:T(8,128)(2,1)S(1)}) custom-call(s32[1]{0:T(128)} %bitcast.core_ref, bf16[192,512]{1,0:T(8,128)(2,1)S(1)} %collective-permute-done.12.refs_1_.p_ref, bf16[192,512]{1,0:T(8,128)(2,1)S(1)} %after.8.q_ref, bf16[192,512]{1,0:T(8,128)(2,1)S(1)} %collective-permute-done.21.p2_ref, ...), custom_call_target="tpu_custom_call" | custom-call | tf_op jit(solution)/shard_map/expert/pallas_call | solution.py:24
  58.5 0.2 collective-permute-start.23
  58.7 0.9 collective-permute-start.10
  59.6 0.0 collective-permute-start.17
  59.6 3.5 %collective-permute-done.16 = bf16[192,512]{1,0:T(8,128)(2,1)S(1)} collective-permute-done((bf16[192,512]{1,0:T(8,128)(2,1)S(1)}, bf16[192,512]{1,0:T(8,128)(2,1)S(1)}, u32[]{:S(2)}, u32[]{:S(2)}) %collective-permute-start.16) | collective-permute-done | bytes 196640 | tf_op jit(solution)/shard_map/ppermute | solution.py:218
  63.2 3.8 %collective-permute-done.10.refs_0_ = bf16[192,512]{1,0:T(8,128)(2,1)S(1)} collective-permute-done((bf16[192,512]{1,0:T(8,128)(2,1)S(1)}, bf16[192,512]{1,0:T(8,128)(2,1)S(1)}, u32[]{:S(2)}, u32[]{:S(2)}) %collective-permute-start.10) | collective-permute-done | bytes 196640 | tf_op jit(solution)/shard_map/ppermute | solution.py:218
  67.0 0.1 convert_add_fusion.1
  67.1 0.9 collective-permute-start.24
  68.0 0.4 collective-permute-done.18.q2_ref
  68.4 1.8 %expert.6 = (f32[2,192,512]{2,1,0:T(8,128)S(1)}, bf16[2,192,512]{2,1,0:T(8,128)(2,1)S(1)}) custom-call(s32[1]{0:T(128)} %bitcast.core_ref, bf16[192,512]{1,0:T(8,128)(2,1)S(1)} %collective-permute-done.9.p_ref.refs_1_, bf16[192,512]{1,0:T(8,128)(2,1)S(1)} %after.7.q_ref, bf16[192,512]{1,0:T(8,128)(2,1)S(1)} %collective-permute-done.17.p2_ref, ...), custom_call_target="tpu_custom_call" | custom-call | tf_op jit(solution)/shard_map/expert/pallas_call | solution.py:24
  70.3 0.2 collective-permute-start.19
  70.5 4.1 %collective-permute-done.24 = bf16[192,512]{1,0:T(8,128)(2,1)S(1)} collective-permute-done((bf16[192,512]{1,0:T(8,128)(2,1)S(1)}, bf16[192,512]{1,0:T(8,128)(2,1)S(1)}, u32[]{:S(2)}, u32[]{:S(2)}) %collective-permute-start.24) | collective-permute-done | bytes 196640 | tf_op jit(solution)/shard_map/ppermute | solution.py:218
  74.6 0.1 convert_add_fusion
  74.8 0.9 collective-permute-start.25
  75.7 1.1 %collective-permute-start.27 = (bf16[192,512]{1,0:T(8,128)(2,1)S(1)}, bf16[192,512]{1,0:T(8,128)(2,1)S(1)}, u32[]{:S(2)}, u32[]{:S(2)}) collective-permute-start(bf16[192,512]{1,0:T(8,128)(2,1)S(1)} %fusion.5.refs_1_), channel_id=1, source_target_pairs={{0,8},{2,10},{4,12},{6,14},{8,0},{10,2},{12,4},{14,6},{1,9},{3,11}... | collective-permute-start | bytes 589832 | tf_op jit(solution)/shard_map/ppermute | solution.py:223
  76.7 2.4 %collective-permute-start.28 = (bf16[192,512]{1,0:T(8,128)(2,1)S(1)}, bf16[192,512]{1,0:T(8,128)(2,1)S(1)}, u32[]{:S(2)}, u32[]{:S(2)}) collective-permute-start(bf16[192,512]{1,0:T(8,128)(2,1)S(1)} %fusion.3.refs_1_), channel_id=1, source_target_pairs={{0,12},{2,14},{4,8},{6,10},{8,4},{10,6},{12,0},{14,2},{1,13},{3,15... | collective-permute-start | bytes 589832 | tf_op jit(solution)/shard_map/ppermute | solution.py:223
  79.1 2.3 %collective-permute-done.25 = bf16[192,512]{1,0:T(8,128)(2,1)S(1)} collective-permute-done((bf16[192,512]{1,0:T(8,128)(2,1)S(1)}, bf16[192,512]{1,0:T(8,128)(2,1)S(1)}, u32[]{:S(2)}, u32[]{:S(2)}) %collective-permute-start.25) | collective-permute-done | bytes 196640 | tf_op jit(solution)/shard_map/ppermute | solution.py:218
  81.4 1.4 %collective-permute-start.26 = (bf16[192,512]{1,0:T(8,128)(2,1)S(1)}, bf16[192,512]{1,0:T(8,128)(2,1)S(1)}, u32[]{:S(2)}, u32[]{:S(2)}) collective-permute-start(bf16[192,512]{1,0:T(8,128)(2,1)S(1)} %fusion.1), channel_id=1, source_target_pairs={{0,4},{2,6},{4,0},{6,2},{8,12},{10,14},{12,8},{14,10},{1,5},{3,7},... | collective-permute-start | bytes 589832 | tf_op jit(solution)/shard_map/ppermute | solution.py:223
  82.9 1.1 %collective-permute-done.1.other_gates_ref = f32[2,128]{1,0:T(2,128)S(1)} collective-permute-done((f32[2,128]{1,0:T(2,128)S(1)}, f32[2,128]{1,0:T(2,128)S(1)}, u32[]{:S(2)}, u32[]{:S(2)}) %collective-permute-start.1) | collective-permute-done | bytes 1056 | tf_op jit(solution)/shard_map/ppermute | solution.py:213
  84.0 8.0 %collective-permute-done.27.rest_2_ = bf16[192,512]{1,0:T(8,128)(2,1)S(1)} collective-permute-done((bf16[192,512]{1,0:T(8,128)(2,1)S(1)}, bf16[192,512]{1,0:T(8,128)(2,1)S(1)}, u32[]{:S(2)}, u32[]{:S(2)}) %collective-permute-start.27) | collective-permute-done | bytes 196640 | tf_op jit(solution)/shard_map/ppermute | solution.py:223
  92.0 2.5 %collective-permute-done.26.rest_1_ = bf16[192,512]{1,0:T(8,128)(2,1)S(1)} collective-permute-done((bf16[192,512]{1,0:T(8,128)(2,1)S(1)}, bf16[192,512]{1,0:T(8,128)(2,1)S(1)}, u32[]{:S(2)}, u32[]{:S(2)}) %collective-permute-start.26) | collective-permute-done | bytes 196640 | tf_op jit(solution)/shard_map/ppermute | solution.py:223
  94.4 0.9 combine.1
  95.4 0.1 collective-permute-start.29
  95.4 1.3 %collective-permute-done.29.other_ref = bf16[128,512]{1,0:T(8,128)(2,1)S(1)} collective-permute-done((bf16[128,512]{1,0:T(8,128)(2,1)S(1)}, bf16[128,512]{1,0:T(8,128)(2,1)S(1)}, u32[]{:S(2)}, u32[]{:S(2)}) %collective-permute-start.29) | collective-permute-done | bytes 131104 | tf_op jit(solution)/shard_map/ppermute | solution.py:213
  96.8 0.8 finish.1
  (42 shorter events, 0.3 us)
Async XLA Ops:
  0.0 29.1 %copy-start = (bf16[1024,1024]{1,0:T(8,128)(2,1)S(1)}, bf16[1024,1024]{1,0:T(8,128)(2,1)}, u32[]{:S(2)}) copy-start(bf16[1024,1024]{1,0:T(8,128)(2,1)} %in_ref.7) | copy-start | bytes 6291460
  1.2 1.5 %collective-permute-start = (bf16[2,80,512]{2,1,0:T(8,128)(2,1)S(1)}, bf16[2,80,512]{2,1,0:T(8,128)(2,1)S(1)}, u32[]{:S(2)}, u32[]{:S(2)}) collective-permute-start(bf16[2,80,512]{2,1,0:T(8,128)(2,1)S(1)} %get-tuple-element.41), channel_id=1, source_target_pairs={{0,1},{1,0},{2,3},{3,2},{4,5},{5,4},{6,7},{7,6},{8,9},{9,8},{10,11... | collective-permute-start | bytes 491528 | tf_op jit(solution)/shard_map/ppermute | solution.py:213
  2.7 0.9 copy-start.2
  3.7 0.7 copy-start.3
  4.4 0.7 copy-start.6
  5.1 0.7 copy-start.7
  5.8 0.7 copy-start.8
  6.4 0.7 copy-start.9
  10.3 1.4 %collective-permute-start.2 = (bf16[128,512]{1,0:T(8,128)(2,1)S(1)}, bf16[128,512]{1,0:T(8,128)(2,1)S(1)}, u32[]{:S(2)}, u32[]{:S(2)}) collective-permute-start(bf16[128,512]{1,0:T(8,128)(2,1)S(1)} %get-tuple-element.26), channel_id=1, source_target_pairs={{0,1},{1,0},{2,3},{3,2},{4,5},{5,4},{6,7},{7,6},{8,9},{9,8},{10,11... | collective-permute-start | bytes 393224 | tf_op jit(solution)/shard_map/ppermute | solution.py:213
  11.8 0.7 copy-start.4
  13.0 8.1 %collective-permute-start.3 = (bf16[192,512]{1,0:T(8,128)(2,1)S(1)}, bf16[192,512]{1,0:T(8,128)(2,1)S(1)}, u32[]{:S(2)}, u32[]{:S(2)}) collective-permute-start(bf16[192,512]{1,0:T(8,128)(2,1)S(1)} %get-tuple-element.27.p_ref), channel_id=1, source_target_pairs={{0,2},{2,0},{4,6},{6,4},{8,10},{10,8},{12,14},{14,12},{1,3},{3,1},... | collective-permute-start | bytes 589832 | tf_op jit(solution)/shard_map/ppermute | solution.py:218
  15.9 11.8 %collective-permute-start.4 = (bf16[192,512]{1,0:T(8,128)(2,1)S(1)}, bf16[192,512]{1,0:T(8,128)(2,1)S(1)}, u32[]{:S(2)}, u32[]{:S(2)}) collective-permute-start(bf16[192,512]{1,0:T(8,128)(2,1)S(1)} %get-tuple-element.28), channel_id=1, source_target_pairs={{0,8},{2,10},{4,12},{6,14},{8,0},{10,2},{12,4},{14,6},{1,9},{3,11}... | collective-permute-start | bytes 589832 | tf_op jit(solution)/shard_map/ppermute | solution.py:223
  18.5 9.2 %collective-permute-start.5 = (bf16[192,512]{1,0:T(8,128)(2,1)S(1)}, bf16[192,512]{1,0:T(8,128)(2,1)S(1)}, u32[]{:S(2)}, u32[]{:S(2)}) collective-permute-start(bf16[192,512]{1,0:T(8,128)(2,1)S(1)} %get-tuple-element.27.p_ref), channel_id=1, source_target_pairs={{0,1},{1,0},{2,3},{3,2},{4,5},{5,4},{6,7},{7,6},{8,9},{9,8},{10,11... | collective-permute-start | bytes 589832 | tf_op jit(solution)/shard_map/ppermute | solution.py:213
  27.7 1.4 %collective-permute-start.6 = (bf16[192,512]{1,0:T(8,128)(2,1)S(1)}, bf16[192,512]{1,0:T(8,128)(2,1)S(1)}, u32[]{:S(2)}, u32[]{:S(2)}) collective-permute-start(bf16[192,512]{1,0:T(8,128)(2,1)S(1)} %after.5.q_ref), channel_id=1, source_target_pairs={{0,1},{1,0},{2,3},{3,2},{4,5},{5,4},{6,7},{7,6},{8,9},{9,8},{10,11... | collective-permute-start | bytes 589832 | tf_op jit(solution)/shard_map/ppermute | solution.py:213
  29.1 1.6 %copy-start.1 = (bf16[1024,1024]{1,0:T(8,128)(2,1)S(1)}, bf16[1024,1024]{1,0:T(8,128)(2,1)}, u32[]{:S(2)}) copy-start(bf16[1024,1024]{1,0:T(8,128)(2,1)} %out_ref.7) | copy-start | bytes 6291460
  32.6 10.6 %collective-permute-start.7 = (bf16[2,192,512]{2,1,0:T(8,128)(2,1)S(1)}, bf16[2,192,512]{2,1,0:T(8,128)(2,1)S(1)}, u32[]{:S(2)}, u32[]{:S(2)}) collective-permute-start(bf16[2,192,512]{2,1,0:T(8,128)(2,1)S(1)} %get-tuple-element.30), channel_id=1, source_target_pairs={{0,1},{1,0},{2,3},{3,2},{4,5},{5,4},{6,7},{7,6},{8,9},{9,8},{10,11... | collective-permute-start | bytes 1179656 | tf_op jit(solution)/shard_map/ppermute | solution.py:213
  32.8 9.1 %collective-permute-start.12 = (bf16[192,512]{1,0:T(8,128)(2,1)S(1)}, bf16[192,512]{1,0:T(8,128)(2,1)S(1)}, u32[]{:S(2)}, u32[]{:S(2)}) collective-permute-start(bf16[192,512]{1,0:T(8,128)(2,1)S(1)} %get-tuple-element.32), channel_id=1, source_target_pairs={{0,12},{2,14},{4,8},{6,10},{8,4},{10,6},{12,0},{14,2},{1,13},{3,15... | collective-permute-start | bytes 589832 | tf_op jit(solution)/shard_map/ppermute | solution.py:223
  36.3 6.9 %collective-permute-start.11 = (bf16[192,512]{1,0:T(8,128)(2,1)S(1)}, bf16[192,512]{1,0:T(8,128)(2,1)S(1)}, u32[]{:S(2)}, u32[]{:S(2)}) collective-permute-start(bf16[192,512]{1,0:T(8,128)(2,1)S(1)} %collective-permute-done.4.refs_1_.p_ref), channel_id=1, source_target_pairs={{0,2},{2,0},{4,6},{6,4},{8,10},{10,8},{12,14},{14,12},{1,3},{3,1},... | collective-permute-start | bytes 589832 | tf_op jit(solution)/shard_map/ppermute | solution.py:218
  36.8 7.1 %collective-permute-start.13 = (bf16[192,512]{1,0:T(8,128)(2,1)S(1)}, bf16[192,512]{1,0:T(8,128)(2,1)S(1)}, u32[]{:S(2)}, u32[]{:S(2)}) collective-permute-start(bf16[192,512]{1,0:T(8,128)(2,1)S(1)} %collective-permute-done.4.refs_1_.p_ref), channel_id=1, source_target_pairs={{0,1},{1,0},{2,3},{3,2},{4,5},{5,4},{6,7},{7,6},{8,9},{9,8},{10,11... | collective-permute-start | bytes 589832 | tf_op jit(solution)/shard_map/ppermute | solution.py:213
  43.2 1.4 %collective-permute-start.14 = (bf16[192,512]{1,0:T(8,128)(2,1)S(1)}, bf16[192,512]{1,0:T(8,128)(2,1)S(1)}, u32[]{:S(2)}, u32[]{:S(2)}) collective-permute-start(bf16[192,512]{1,0:T(8,128)(2,1)S(1)} %after.6.q_ref), channel_id=1, source_target_pairs={{0,1},{1,0},{2,3},{3,2},{4,5},{5,4},{6,7},{7,6},{8,9},{9,8},{10,11... | collective-permute-start | bytes 589832 | tf_op jit(solution)/shard_map/ppermute | solution.py:213
  43.3 7.4 %collective-permute-start.8 = (bf16[192,512]{1,0:T(8,128)(2,1)S(1)}, bf16[192,512]{1,0:T(8,128)(2,1)S(1)}, u32[]{:S(2)}, u32[]{:S(2)}) collective-permute-start(bf16[192,512]{1,0:T(8,128)(2,1)S(1)} %fusion.8), channel_id=1, source_target_pairs={{0,2},{2,0},{4,6},{6,4},{8,10},{10,8},{12,14},{14,12},{1,3},{3,1},... | collective-permute-start | bytes 589832 | tf_op jit(solution)/shard_map/ppermute | solution.py:218
  46.4 8.8 %collective-permute-start.15 = (bf16[2,192,512]{2,1,0:T(8,128)(2,1)S(1)}, bf16[2,192,512]{2,1,0:T(8,128)(2,1)S(1)}, u32[]{:S(2)}, u32[]{:S(2)}) collective-permute-start(bf16[2,192,512]{2,1,0:T(8,128)(2,1)S(1)} %get-tuple-element.34), channel_id=1, source_target_pairs={{0,1},{1,0},{2,3},{3,2},{4,5},{5,4},{6,7},{7,6},{8,9},{9,8},{10,11... | collective-permute-start | bytes 1179656 | tf_op jit(solution)/shard_map/ppermute | solution.py:213
  46.6 7.2 %collective-permute-start.9 = (bf16[192,512]{1,0:T(8,128)(2,1)S(1)}, bf16[192,512]{1,0:T(8,128)(2,1)S(1)}, u32[]{:S(2)}, u32[]{:S(2)}) collective-permute-start(bf16[192,512]{1,0:T(8,128)(2,1)S(1)} %get-tuple-element.31), channel_id=1, source_target_pairs={{0,4},{2,6},{4,0},{6,2},{8,12},{10,14},{12,8},{14,10},{1,5},{3,7},... | collective-permute-start | bytes 589832 | tf_op jit(solution)/shard_map/ppermute | solution.py:223
  48.3 6.9 %collective-permute-start.20 = (bf16[192,512]{1,0:T(8,128)(2,1)S(1)}, bf16[192,512]{1,0:T(8,128)(2,1)S(1)}, u32[]{:S(2)}, u32[]{:S(2)}) collective-permute-start(bf16[192,512]{1,0:T(8,128)(2,1)S(1)} %collective-permute-done.12.refs_1_.p_ref), channel_id=1, source_target_pairs={{0,2},{2,0},{4,6},{6,4},{8,10},{10,8},{12,14},{14,12},{1,3},{3,1},... | collective-permute-start | bytes 589832 | tf_op jit(solution)/shard_map/ppermute | solution.py:218
  49.2 7.0 %collective-permute-start.21 = (bf16[192,512]{1,0:T(8,128)(2,1)S(1)}, bf16[192,512]{1,0:T(8,128)(2,1)S(1)}, u32[]{:S(2)}, u32[]{:S(2)}) collective-permute-start(bf16[192,512]{1,0:T(8,128)(2,1)S(1)} %collective-permute-done.12.refs_1_.p_ref), channel_id=1, source_target_pairs={{0,1},{1,0},{2,3},{3,2},{4,5},{5,4},{6,7},{7,6},{8,9},{9,8},{10,11... | collective-permute-start | bytes 589832 | tf_op jit(solution)/shard_map/ppermute | solution.py:213
  55.2 1.4 %collective-permute-start.22 = (bf16[192,512]{1,0:T(8,128)(2,1)S(1)}, bf16[192,512]{1,0:T(8,128)(2,1)S(1)}, u32[]{:S(2)}, u32[]{:S(2)}) collective-permute-start(bf16[192,512]{1,0:T(8,128)(2,1)S(1)} %after.8.q_ref), channel_id=1, source_target_pairs={{0,1},{1,0},{2,3},{3,2},{4,5},{5,4},{6,7},{7,6},{8,9},{9,8},{10,11... | collective-permute-start | bytes 589832 | tf_op jit(solution)/shard_map/ppermute | solution.py:213
  55.4 7.8 %collective-permute-start.16 = (bf16[192,512]{1,0:T(8,128)(2,1)S(1)}, bf16[192,512]{1,0:T(8,128)(2,1)S(1)}, u32[]{:S(2)}, u32[]{:S(2)}) collective-permute-start(bf16[192,512]{1,0:T(8,128)(2,1)S(1)} %fusion.9), channel_id=1, source_target_pairs={{0,2},{2,0},{4,6},{6,4},{8,10},{10,8},{12,14},{14,12},{1,3},{3,1},... | collective-permute-start | bytes 589832 | tf_op jit(solution)/shard_map/ppermute | solution.py:218
  58.5 8.5 %collective-permute-start.23 = (bf16[2,192,512]{2,1,0:T(8,128)(2,1)S(1)}, bf16[2,192,512]{2,1,0:T(8,128)(2,1)S(1)}, u32[]{:S(2)}, u32[]{:S(2)}) collective-permute-start(bf16[2,192,512]{2,1,0:T(8,128)(2,1)S(1)} %get-tuple-element.38), channel_id=1, source_target_pairs={{0,1},{1,0},{2,3},{3,2},{4,5},{5,4},{6,7},{7,6},{8,9},{9,8},{10,11... | collective-permute-start | bytes 1179656 | tf_op jit(solution)/shard_map/ppermute | solution.py:213
  58.7 8.3 %collective-permute-start.10 = (bf16[192,512]{1,0:T(8,128)(2,1)S(1)}, bf16[192,512]{1,0:T(8,128)(2,1)S(1)}, u32[]{:S(2)}, u32[]{:S(2)}) collective-permute-start(bf16[192,512]{1,0:T(8,128)(2,1)S(1)} %collective-permute-done.9.p_ref.refs_1_), channel_id=1, source_target_pairs={{0,2},{2,0},{4,6},{6,4},{8,10},{10,8},{12,14},{14,12},{1,3},{3,1},... | collective-permute-start | bytes 589832 | tf_op jit(solution)/shard_map/ppermute | solution.py:218
  59.6 8.4 %collective-permute-start.17 = (bf16[192,512]{1,0:T(8,128)(2,1)S(1)}, bf16[192,512]{1,0:T(8,128)(2,1)S(1)}, u32[]{:S(2)}, u32[]{:S(2)}) collective-permute-start(bf16[192,512]{1,0:T(8,128)(2,1)S(1)} %collective-permute-done.9.p_ref.refs_1_), channel_id=1, source_target_pairs={{0,1},{1,0},{2,3},{3,2},{4,5},{5,4},{6,7},{7,6},{8,9},{9,8},{10,11... | collective-permute-start | bytes 589832 | tf_op jit(solution)/shard_map/ppermute | solution.py:213
  67.0 1.4 %collective-permute-start.18 = (bf16[192,512]{1,0:T(8,128)(2,1)S(1)}, bf16[192,512]{1,0:T(8,128)(2,1)S(1)}, u32[]{:S(2)}, u32[]{:S(2)}) collective-permute-start(bf16[192,512]{1,0:T(8,128)(2,1)S(1)} %after.7.q_ref), channel_id=1, source_target_pairs={{0,1},{1,0},{2,3},{3,2},{4,5},{5,4},{6,7},{7,6},{8,9},{9,8},{10,11... | collective-permute-start | bytes 589832 | tf_op jit(solution)/shard_map/ppermute | solution.py:213
  67.1 7.4 %collective-permute-start.24 = (bf16[192,512]{1,0:T(8,128)(2,1)S(1)}, bf16[192,512]{1,0:T(8,128)(2,1)S(1)}, u32[]{:S(2)}, u32[]{:S(2)}) collective-permute-start(bf16[192,512]{1,0:T(8,128)(2,1)S(1)} %fusion.10), channel_id=1, source_target_pairs={{0,2},{2,0},{4,6},{6,4},{8,10},{10,8},{12,14},{14,12},{1,3},{3,1},... | collective-permute-start | bytes 589832 | tf_op jit(solution)/shard_map/ppermute | solution.py:218
  70.3 4.3 %collective-permute-start.19 = (bf16[2,192,512]{2,1,0:T(8,128)(2,1)S(1)}, bf16[2,192,512]{2,1,0:T(8,128)(2,1)S(1)}, u32[]{:S(2)}, u32[]{:S(2)}) collective-permute-start(bf16[2,192,512]{2,1,0:T(8,128)(2,1)S(1)} %get-tuple-element.36), channel_id=1, source_target_pairs={{0,1},{1,0},{2,3},{3,2},{4,5},{5,4},{6,7},{7,6},{8,9},{9,8},{10,11... | collective-permute-start | bytes 1179656 | tf_op jit(solution)/shard_map/ppermute | solution.py:213
  74.6 19.9 %copy-start.5 = (s32[2,128,2]{1,2,0:T(2,128)S(1)}, s32[2,128,2]{1,2,0:T(2,128)}, u32[]{:S(2)}) copy-start(s32[2,128,2]{1,2,0:T(2,128)} %param.16) | copy-start | bytes 6148
  74.8 6.6 %collective-permute-start.25 = (bf16[192,512]{1,0:T(8,128)(2,1)S(1)}, bf16[192,512]{1,0:T(8,128)(2,1)S(1)}, u32[]{:S(2)}, u32[]{:S(2)}) collective-permute-start(bf16[192,512]{1,0:T(8,128)(2,1)S(1)} %fusion.11), channel_id=1, source_target_pairs={{0,2},{2,0},{4,6},{6,4},{8,10},{10,8},{12,14},{14,12},{1,3},{3,1},... | collective-permute-start | bytes 589832 | tf_op jit(solution)/shard_map/ppermute | solution.py:218
  75.7 16.3 %collective-permute-start.27 = (bf16[192,512]{1,0:T(8,128)(2,1)S(1)}, bf16[192,512]{1,0:T(8,128)(2,1)S(1)}, u32[]{:S(2)}, u32[]{:S(2)}) collective-permute-start(bf16[192,512]{1,0:T(8,128)(2,1)S(1)} %fusion.5.refs_1_), channel_id=1, source_target_pairs={{0,8},{2,10},{4,12},{6,14},{8,0},{10,2},{12,4},{14,6},{1,9},{3,11}... | collective-permute-start | bytes 589832 | tf_op jit(solution)/shard_map/ppermute | solution.py:223
  76.7 15.2 %collective-permute-start.28 = (bf16[192,512]{1,0:T(8,128)(2,1)S(1)}, bf16[192,512]{1,0:T(8,128)(2,1)S(1)}, u32[]{:S(2)}, u32[]{:S(2)}) collective-permute-start(bf16[192,512]{1,0:T(8,128)(2,1)S(1)} %fusion.3.refs_1_), channel_id=1, source_target_pairs={{0,12},{2,14},{4,8},{6,10},{8,4},{10,6},{12,0},{14,2},{1,13},{3,15... | collective-permute-start | bytes 589832 | tf_op jit(solution)/shard_map/ppermute | solution.py:223
  81.4 13.0 %collective-permute-start.26 = (bf16[192,512]{1,0:T(8,128)(2,1)S(1)}, bf16[192,512]{1,0:T(8,128)(2,1)S(1)}, u32[]{:S(2)}, u32[]{:S(2)}) collective-permute-start(bf16[192,512]{1,0:T(8,128)(2,1)S(1)} %fusion.1), channel_id=1, source_target_pairs={{0,4},{2,6},{4,0},{6,2},{8,12},{10,14},{12,8},{14,10},{1,5},{3,7},... | collective-permute-start | bytes 589832 | tf_op jit(solution)/shard_map/ppermute | solution.py:223
  82.9 1.1 %collective-permute-start.1 = (f32[2,128]{1,0:T(2,128)S(1)}, f32[2,128]{1,0:T(2,128)S(1)}, u32[]{:S(2)}, u32[]{:S(2)}) collective-permute-start(f32[2,128]{1,0:T(2,128)S(1)} %get-tuple-element.24.own_gates_ref), channel_id=1, source_target_pairs={{0,1},{1,0},{2,3},{3,2},{4,5},{5,4},{6,7},{7,6},{8,9},{9,8},{10,11... | collective-permute-start | bytes 3080 | tf_op jit(solution)/shard_map/ppermute | solution.py:213
  95.4 1.4 %collective-permute-start.29 = (bf16[128,512]{1,0:T(8,128)(2,1)S(1)}, bf16[128,512]{1,0:T(8,128)(2,1)S(1)}, u32[]{:S(2)}, u32[]{:S(2)}) collective-permute-start(bf16[128,512]{1,0:T(8,128)(2,1)S(1)} %get-tuple-element.40), channel_id=1, source_target_pairs={{0,1},{1,0},{2,3},{3,2},{4,5},{5,4},{6,7},{7,6},{8,9},{9,8},{10,11... | collective-permute-start | bytes 393224 | tf_op jit(solution)/shard_map/ppermute | solution.py:213

commit v8 on v6

--- a/solution.py
+++ b/solution.py
@@ -307,7 +307,7 @@
         if at >= 2:
             q2 = after(q2, kepts[at - 2])
         if at >= 2:
-            q2 = after(q2, wholes[at - 2])
+            q2 = after(q2, halves[at - 2])
         kept, sent = call(
             expert_kernel,
             "expert",

time: 91 us -> 81.2 us (0.89)
  waiting for transfers between devices: 41.4 us -> 27.6 us
  starting transfers between devices: 25.5 us -> 28.8 us
    ppermute x8, waiting for transfers between devices: 21.3 us -> 7.76 us  [swap_owner(): return lax.ppermute(values, 'expert', [(i, i ^ 1) for i in range(owners)])]
    ppermute x6, starting transfers between devices: 12.8 us -> 16.1 us  [shift(): lax.ppermute(values, 'expert', [(i, (i + 2 * offset) % owners) for i in r...]
    ppermute x16, waiting for transfers between devices: 4.89 us -> 2.73 us  [swap(): return lax.ppermute(values, 'section', [(0, 1), (1, 0)])]
    ppermute x6, waiting for transfers between devices: 15.2 us -> 17.1 us  [shift(): lax.ppermute(values, 'expert', [(i, (i + 2 * offset) % owners) for i in r...]
    ppermute x8, starting transfers between devices: 9.53 us -> 8.61 us  [swap_owner(): return lax.ppermute(values, 'expert', [(i, i ^ 1) for i in range(owners)])]
  transfers between devices with their start and end apart: 30 -> 30, of which waited for: 16 -> 11; matrix products, arithmetic and copies ran while one was open for 1% -> 1% of each run, Pallas kernels for 8% -> 9%
where the time goes in v8:
time: 81.2 us; the launch traced here: 80 us
  starting transfers between devices  28.8 us (35%)
  waiting for transfers between devices  27.6 us (34%)
  Pallas kernels  12.8 us (16%)
  local copies, waits for them, and re-layouts  8.33 us (10%)
  other arithmetic  1.64 us (2%)
  between operations  0.87 us (1%)
    ppermute x6, waiting for transfers between devices, shift(): lax.ppermute(values, 'expert', [(i, (i + 2 * offset) % owners) for i in r...  17.1 us
    ppermute x6, starting transfers between devices, shift(): lax.ppermute(values, 'expert', [(i, (i + 2 * offset) % owners) for i in r...  16.1 us
    pallas_call x8, Pallas kernels, call(): pl.pallas_call(kernel, out_shape=tuple((jax.ShapeDtypeStruct(*out) for ou...  12.8 us
    ppermute x8, starting transfers between devices, swap_owner(): return lax.ppermute(values, 'expert', [(i, i ^ 1) for i in range(owners)])  8.61 us
    unnamed x24, local copies, waits for them, and re-layouts  8.23 us
    ppermute x8, waiting for transfers between devices, swap_owner(): return lax.ppermute(values, 'expert', [(i, i ^ 1) for i in range(owners)])  7.76 us
    ppermute x16, starting transfers between devices, swap(): return lax.ppermute(values, 'section', [(0, 1), (1, 0)])  4.09 us
    ppermute x16, waiting for transfers between devices, swap(): return lax.ppermute(values, 'section', [(0, 1), (1, 0)])  2.73 us
  transfers between devices with their start and end apart: 30, of which 11 were waited for; matrix products, arithmetic and copies ran while one was open for 1% of the time, Pallas kernels for 9%

profile of v8, /device:TPU:0, one launch (start us, length us, event | category | flops | bytes accessed | tf_op | source)
XLA Modules:
  0.0 80.0 jit_solution(4674259594622359226)
XLA Ops:
  0.0 1.0 %fusion.13 = (bf16[2,80,512]{2,1,0:T(8,128)(2,1)S(1)}, bf16[2,80,512]{2,1,0:T(8,128)(2,1)S(1)}) fusion(s32[]{:T(128)S(6)} %select_n.13, bf16[2,1,80,512]{3,2,0,1:T(8,128)(2,1)} %bitcast.53, bf16[2,1,80,512]{3,2,0,1:T(8,128)(2,1)} %bitcast.54, s32[]{:T(128)S(6)} %select_n.12), kind=kLoop, calls=%fused_computation.29 | loop fusion | flops 163840 | bytes 655368 | tf_op jit(solution)/shard_map/jit(dynamic_index_in_dim)/squeeze | solution.py:257
  1.0 0.5 collective-permute-start
  2.2 0.4 collective-permute-done.other_ref
  2.6 0.9 %copy-done.4 = bf16[1,128,1024]{2,1,0:T(8,128)(2,1)S(1)} copy-done((bf16[1,128,1024]{2,1,0:T(8,128)(2,1)S(1)}, bf16[1,128,1024]{2,1,0:T(8,128)(2,1)}, u32[]{:S(2)}) %copy-start.4) | copy-done | bytes 262168
  3.5 0.7 copy-done.5
  4.2 0.7 copy-done.8
  4.9 0.7 copy-done.9
  5.6 0.7 copy-done.10
  6.3 0.7 copy-done.11
  6.9 3.2 %attend.1 = (bf16[128,1024]{1,0:T(8,128)(2,1)S(1)}, bf16[128,512]{1,0:T(8,128)(2,1)S(1)}, bf16[128,512]{1,0:T(8,128)(2,1)S(1)}, f32[2,128]{1,0:T(2,128)S(1)}) custom-call(s32[1]{0:T(128)} %bitcast.core_ref, s32[1]{0:T(128)S(6)} %copy.20.source_ref, s32[2]{0:T(128)S(1)} %copy-done.11, bf16[128,1024]{1,0:T(8,128)(2,1)S(1)} %bitcast.46, ...), custom_call_target="tpu_custom_call" | custom-call | tf_op jit(solution)/shard_map/attend/pallas_call | solution.py:24
  10.2 0.4 collective-permute-start.2
  10.6 1.0 %collective-permute-done.2.other_ref = bf16[128,512]{1,0:T(8,128)(2,1)S(1)} collective-permute-done((bf16[128,512]{1,0:T(8,128)(2,1)S(1)}, bf16[128,512]{1,0:T(8,128)(2,1)S(1)}, u32[]{:S(2)}, u32[]{:S(2)}) %collective-permute-start.2) | collective-permute-done | bytes 131104 | tf_op jit(solution)/shard_map/ppermute | solution.py:214
  11.6 0.7 copy-done.6
  12.3 0.5 select.5
  12.8 2.9 %collective-permute-start.3 = (bf16[192,512]{1,0:T(8,128)(2,1)S(1)}, bf16[192,512]{1,0:T(8,128)(2,1)S(1)}, u32[]{:S(2)}, u32[]{:S(2)}) collective-permute-start(bf16[192,512]{1,0:T(8,128)(2,1)S(1)} %get-tuple-element.27.p_ref), channel_id=1, source_target_pairs={{0,2},{2,0},{4,6},{6,4},{8,10},{10,8},{12,14},{14,12},{1,3},{3,1},... | collective-permute-start | bytes 589832 | tf_op jit(solution)/shard_map/ppermute | solution.py:219
  15.7 1.6 %collective-permute-start.8 = (bf16[192,512]{1,0:T(8,128)(2,1)S(1)}, bf16[192,512]{1,0:T(8,128)(2,1)S(1)}, u32[]{:S(2)}, u32[]{:S(2)}) collective-permute-start(bf16[192,512]{1,0:T(8,128)(2,1)S(1)} %get-tuple-element.30), channel_id=1, source_target_pairs={{0,4},{2,6},{4,8},{6,10},{8,12},{10,14},{12,0},{14,2},{1,5},{3,7},... | collective-permute-start | bytes 589832 | tf_op jit(solution)/shard_map/ppermute | solution.py:224
  17.3 2.6 %collective-permute-start.15 = (bf16[192,512]{1,0:T(8,128)(2,1)S(1)}, bf16[192,512]{1,0:T(8,128)(2,1)S(1)}, u32[]{:S(2)}, u32[]{:S(2)}) collective-permute-start(bf16[192,512]{1,0:T(8,128)(2,1)S(1)} %get-tuple-element.33), channel_id=1, source_target_pairs={{0,8},{2,10},{4,12},{6,14},{8,0},{10,2},{12,4},{14,6},{1,9},{3,11}... | collective-permute-start | bytes 589832 | tf_op jit(solution)/shard_map/ppermute | solution.py:224
  19.9 1.3 %collective-permute-start.22 = (bf16[192,512]{1,0:T(8,128)(2,1)S(1)}, bf16[192,512]{1,0:T(8,128)(2,1)S(1)}, u32[]{:S(2)}, u32[]{:S(2)}) collective-permute-start(bf16[192,512]{1,0:T(8,128)(2,1)S(1)} %get-tuple-element.36), channel_id=1, source_target_pairs={{0,12},{2,14},{4,0},{6,2},{8,4},{10,6},{12,8},{14,10},{1,13},{3,15... | collective-permute-start | bytes 589832 | tf_op jit(solution)/shard_map/ppermute | solution.py:224
  21.3 0.0 collective-permute-start.4
  21.3 0.0 collective-permute-done.3.q_ref
  21.3 0.5 collective-permute-start.5
  21.8 3.6 %collective-permute-done.8.p_ref = bf16[192,512]{1,0:T(8,128)(2,1)S(1)} collective-permute-done((bf16[192,512]{1,0:T(8,128)(2,1)S(1)}, bf16[192,512]{1,0:T(8,128)(2,1)S(1)}, u32[]{:S(2)}, u32[]{:S(2)}) %collective-permute-start.8) | collective-permute-done | bytes 196640 | tf_op jit(solution)/shard_map/ppermute | solution.py:224
  25.4 0.3 collective-permute-start.9
  25.7 7.1 %collective-permute-done.15.p_ref = bf16[192,512]{1,0:T(8,128)(2,1)S(1)} collective-permute-done((bf16[192,512]{1,0:T(8,128)(2,1)S(1)}, bf16[192,512]{1,0:T(8,128)(2,1)S(1)}, u32[]{:S(2)}, u32[]{:S(2)}) %collective-permute-start.15) | collective-permute-done | bytes 196640 | tf_op jit(solution)/shard_map/ppermute | solution.py:224
  32.8 0.6 collective-permute-start.16
  33.4 1.5 %collective-permute-start.23 = (bf16[192,512]{1,0:T(8,128)(2,1)S(1)}, bf16[192,512]{1,0:T(8,128)(2,1)S(1)}, u32[]{:S(2)}, u32[]{:S(2)}) collective-permute-start(bf16[192,512]{1,0:T(8,128)(2,1)S(1)} %collective-permute-done.22.p_ref), channel_id=1, source_target_pairs={{0,2},{2,0},{4,6},{6,4},{8,10},{10,8},{12,14},{14,12},{1,3},{3,1},... | collective-permute-start | bytes 589832 | tf_op jit(solution)/shard_map/ppermute | solution.py:219
  34.8 1.6 %copy-done = bf16[1024,1024]{1,0:T(8,128)(2,1)S(1)} copy-done((bf16[1024,1024]{1,0:T(8,128)(2,1)S(1)}, bf16[1024,1024]{1,0:T(8,128)(2,1)}, u32[]{:S(2)}) %copy-start) | copy-done | bytes 2097176
  36.4 1.6 %copy-done.2 = bf16[1024,1024]{1,0:T(8,128)(2,1)S(1)} copy-done((bf16[1024,1024]{1,0:T(8,128)(2,1)S(1)}, bf16[1024,1024]{1,0:T(8,128)(2,1)}, u32[]{:S(2)}) %copy-start.2) | copy-done | bytes 2097176
  38.0 1.8 %expert.4 = (f32[2,192,512]{2,1,0:T(8,128)S(1)}, bf16[2,192,512]{2,1,0:T(8,128)(2,1)S(1)}) custom-call(s32[1]{0:T(128)} %bitcast.core_ref, bf16[192,512]{1,0:T(8,128)(2,1)S(1)} %get-tuple-element.27.p_ref, bf16[192,512]{1,0:T(8,128)(2,1)S(1)} %collective-permute-done.3.q_ref, bf16[192,512]{1,0:T(8,128)(2,1)S(1)} %collective-permute-done.4.p2_ref, ...), custom_call_target="tpu_custom_call" | custom-call | tf_op jit(solution)/shard_map/expert/pallas_call | solution.py:24
  39.9 0.1 collective-permute-start.6
  40.0 0.5 collective-permute-start.11
  40.5 0.1 collective-permute-start.17
  40.5 0.0 collective-permute-done.16.q_ref
  40.6 0.4 collective-permute-start.18
  41.0 2.8 %collective-permute-done.23.q_ref = bf16[192,512]{1,0:T(8,128)(2,1)S(1)} collective-permute-done((bf16[192,512]{1,0:T(8,128)(2,1)S(1)}, bf16[192,512]{1,0:T(8,128)(2,1)S(1)}, u32[]{:S(2)}, u32[]{:S(2)}) %collective-permute-start.23) | collective-permute-done | bytes 196640 | tf_op jit(solution)/shard_map/ppermute | solution.py:219
  43.7 0.5 collective-permute-start.1
  44.3 0.1 collective-permute-start.10
  44.3 0.4 collective-permute-start.24
  44.8 1.8 %expert.6 = (f32[2,192,512]{2,1,0:T(8,128)S(1)}, bf16[2,192,512]{2,1,0:T(8,128)(2,1)S(1)}) custom-call(s32[1]{0:T(128)} %bitcast.core_ref, bf16[192,512]{1,0:T(8,128)(2,1)S(1)} %collective-permute-done.15.p_ref, bf16[192,512]{1,0:T(8,128)(2,1)S(1)} %collective-permute-done.16.q_ref, bf16[192,512]{1,0:T(8,128)(2,1)S(1)} %collective-permute-done.17.p2_ref, ...), custom_call_target="tpu_custom_call" | custom-call | tf_op jit(solution)/shard_map/expert/pallas_call | solution.py:24
  46.6 0.1 collective-permute-start.19
  46.8 0.1 convert_add_fusion.3
  46.9 0.6 collective-permute-start.7
  47.6 1.8 %expert.5 = (f32[2,192,512]{2,1,0:T(8,128)S(1)}, bf16[2,192,512]{2,1,0:T(8,128)(2,1)S(1)}) custom-call(s32[1]{0:T(128)} %bitcast.core_ref, bf16[192,512]{1,0:T(8,128)(2,1)S(1)} %collective-permute-done.8.p_ref, bf16[192,512]{1,0:T(8,128)(2,1)S(1)} %collective-permute-done.9.q_ref, bf16[192,512]{1,0:T(8,128)(2,1)S(1)} %collective-permute-done.10.p2_ref, ...), custom_call_target="tpu_custom_call" | custom-call | tf_op jit(solution)/shard_map/expert/pallas_call | solution.py:24
  49.4 0.2 collective-permute-start.12
  49.6 0.1 convert_add_fusion.1
  49.8 1.5 %collective-permute-start.20 = (bf16[192,512]{1,0:T(8,128)(2,1)S(1)}, bf16[192,512]{1,0:T(8,128)(2,1)S(1)}, u32[]{:S(2)}, u32[]{:S(2)}) collective-permute-start(bf16[192,512]{1,0:T(8,128)(2,1)S(1)} %fusion.10.first_ref), channel_id=1, source_target_pairs={{0,2},{2,0},{4,6},{6,4},{8,10},{10,8},{12,14},{14,12},{1,3},{3,1},... | collective-permute-start | bytes 589832 | tf_op jit(solution)/shard_map/ppermute | solution.py:219
  51.3 1.8 %expert.7 = (f32[2,192,512]{2,1,0:T(8,128)S(1)}, bf16[2,192,512]{2,1,0:T(8,128)(2,1)S(1)}) custom-call(s32[1]{0:T(128)} %bitcast.core_ref, bf16[192,512]{1,0:T(8,128)(2,1)S(1)} %collective-permute-done.22.p_ref, bf16[192,512]{1,0:T(8,128)(2,1)S(1)} %collective-permute-done.23.q_ref, bf16[192,512]{1,0:T(8,128)(2,1)S(1)} %collective-permute-done.24.p2_ref, ...), custom_call_target="tpu_custom_call" | custom-call | tf_op jit(solution)/shard_map/expert/pallas_call | solution.py:24
  53.2 0.1 collective-permute-start.26
  53.3 0.1 convert_add_fusion.2
  53.5 0.6 collective-permute-start.13
  54.1 4.8 %collective-permute-done.20 = bf16[192,512]{1,0:T(8,128)(2,1)S(1)} collective-permute-done((bf16[192,512]{1,0:T(8,128)(2,1)S(1)}, bf16[192,512]{1,0:T(8,128)(2,1)S(1)}, u32[]{:S(2)}, u32[]{:S(2)}) %collective-permute-start.20) | collective-permute-done | bytes 196640 | tf_op jit(solution)/shard_map/ppermute | solution.py:219
  59.0 2.9 %collective-permute-start.21 = (bf16[192,512]{1,0:T(8,128)(2,1)S(1)}, bf16[192,512]{1,0:T(8,128)(2,1)S(1)}, u32[]{:S(2)}, u32[]{:S(2)}) collective-permute-start(bf16[192,512]{1,0:T(8,128)(2,1)S(1)} %fusion.3), channel_id=1, source_target_pairs={{0,8},{2,10},{4,12},{6,14},{8,0},{10,2},{12,4},{14,6},{1,9},{3,11}... | collective-permute-start | bytes 589832 | tf_op jit(solution)/shard_map/ppermute | solution.py:224
  61.8 0.1 convert_add_fusion
  62.0 0.6 collective-permute-start.27
  62.6 0.1 collective-permute-done.13
  62.7 5.3 %collective-permute-start.14 = (bf16[192,512]{1,0:T(8,128)(2,1)S(1)}, bf16[192,512]{1,0:T(8,128)(2,1)S(1)}, u32[]{:S(2)}, u32[]{:S(2)}) collective-permute-start(bf16[192,512]{1,0:T(8,128)(2,1)S(1)} %fusion.5), channel_id=1, source_target_pairs={{0,12},{2,14},{4,0},{6,2},{8,4},{10,6},{12,8},{14,10},{1,13},{3,15... | collective-permute-start | bytes 589832 | tf_op jit(solution)/shard_map/ppermute | solution.py:224
  68.1 2.4 %collective-permute-start.28 = (bf16[192,512]{1,0:T(8,128)(2,1)S(1)}, bf16[192,512]{1,0:T(8,128)(2,1)S(1)}, u32[]{:S(2)}, u32[]{:S(2)}) collective-permute-start(bf16[192,512]{1,0:T(8,128)(2,1)S(1)} %fusion.1), channel_id=1, source_target_pairs={{0,4},{2,6},{4,8},{6,10},{8,12},{10,14},{12,0},{14,2},{1,5},{3,7},... | collective-permute-start | bytes 589832 | tf_op jit(solution)/shard_map/ppermute | solution.py:224
  70.5 1.5 %collective-permute-done.21.rest_2_ = bf16[192,512]{1,0:T(8,128)(2,1)S(1)} collective-permute-done((bf16[192,512]{1,0:T(8,128)(2,1)S(1)}, bf16[192,512]{1,0:T(8,128)(2,1)S(1)}, u32[]{:S(2)}, u32[]{:S(2)}) %collective-permute-start.21) | collective-permute-done | bytes 196640 | tf_op jit(solution)/shard_map/ppermute | solution.py:224
  72.0 1.4 %collective-permute-done.14.rest_1_ = bf16[192,512]{1,0:T(8,128)(2,1)S(1)} collective-permute-done((bf16[192,512]{1,0:T(8,128)(2,1)S(1)}, bf16[192,512]{1,0:T(8,128)(2,1)S(1)}, u32[]{:S(2)}, u32[]{:S(2)}) %collective-permute-start.14) | collective-permute-done | bytes 196640 | tf_op jit(solution)/shard_map/ppermute | solution.py:224
  73.4 3.5 %collective-permute-done.28.rest_3_ = bf16[192,512]{1,0:T(8,128)(2,1)S(1)} collective-permute-done((bf16[192,512]{1,0:T(8,128)(2,1)S(1)}, bf16[192,512]{1,0:T(8,128)(2,1)S(1)}, u32[]{:S(2)}, u32[]{:S(2)}) %collective-permute-start.28) | collective-permute-done | bytes 196640 | tf_op jit(solution)/shard_map/ppermute | solution.py:224
  76.9 0.9 %combine.1 = (f32[128,512]{1,0:T(8,128)S(1)}, bf16[128,512]{1,0:T(8,128)(2,1)S(1)}) custom-call(s32[1]{0:T(128)} %bitcast.core_ref, s32[1]{0:T(128)} %bitcast.10.line_ref, s32[2,2,128]{2,1,0:T(2,128)S(1)} %bitcast.49, f32[2,128]{1,0:T(2,128)S(1)} %get-tuple-element.24.own_gates_ref, f32[2,128]{1,0:T(2,128)S(1)} %collective-permute-done.1.other_gates_ref, ...), custom_call_target="tpu_custom_call" | custom-call | tf_op jit(solution)/shard_map/combine/pallas_call | solution.py:24
  77.8 0.1 collective-permute-start.29
  77.9 1.3 %collective-permute-done.29.other_ref = bf16[128,512]{1,0:T(8,128)(2,1)S(1)} collective-permute-done((bf16[128,512]{1,0:T(8,128)(2,1)S(1)}, bf16[128,512]{1,0:T(8,128)(2,1)S(1)}, u32[]{:S(2)}, u32[]{:S(2)}) %collective-permute-start.29) | collective-permute-done | bytes 131104 | tf_op jit(solution)/shard_map/ppermute | solution.py:214
  79.3 0.8 finish.1
  (45 shorter events, 0.3 us)
Async XLA Ops:
  1.0 1.5 %collective-permute-start = (bf16[2,80,512]{2,1,0:T(8,128)(2,1)S(1)}, bf16[2,80,512]{2,1,0:T(8,128)(2,1)S(1)}, u32[]{:S(2)}, u32[]{:S(2)}) collective-permute-start(bf16[2,80,512]{2,1,0:T(8,128)(2,1)S(1)} %get-tuple-element.41), channel_id=1, source_target_pairs={{0,1},{1,0},{2,3},{3,2},{4,5},{5,4},{6,7},{7,6},{8,9},{9,8},{10,11... | collective-permute-start | bytes 491528 | tf_op jit(solution)/shard_map/ppermute | solution.py:214
  2.6 0.9 %copy-start.4 = (bf16[1,128,1024]{2,1,0:T(8,128)(2,1)S(1)}, bf16[1,128,1024]{2,1,0:T(8,128)(2,1)}, u32[]{:S(2)}) copy-start(bf16[1,128,1024]{2,1,0:T(8,128)(2,1)} %param.11) | copy-start | bytes 786436
  3.5 0.7 copy-start.5
  4.2 0.7 copy-start.8
  4.9 0.7 copy-start.9
  5.6 0.7 copy-start.10
  6.3 0.7 copy-start.11
  10.2 1.4 %collective-permute-start.2 = (bf16[128,512]{1,0:T(8,128)(2,1)S(1)}, bf16[128,512]{1,0:T(8,128)(2,1)S(1)}, u32[]{:S(2)}, u32[]{:S(2)}) collective-permute-start(bf16[128,512]{1,0:T(8,128)(2,1)S(1)} %get-tuple-element.26), channel_id=1, source_target_pairs={{0,1},{1,0},{2,3},{3,2},{4,5},{5,4},{6,7},{7,6},{8,9},{9,8},{10,11... | collective-permute-start | bytes 393224 | tf_op jit(solution)/shard_map/ppermute | solution.py:214
  11.6 0.7 copy-start.6
  12.8 8.4 %collective-permute-start.3 = (bf16[192,512]{1,0:T(8,128)(2,1)S(1)}, bf16[192,512]{1,0:T(8,128)(2,1)S(1)}, u32[]{:S(2)}, u32[]{:S(2)}) collective-permute-start(bf16[192,512]{1,0:T(8,128)(2,1)S(1)} %get-tuple-element.27.p_ref), channel_id=1, source_target_pairs={{0,2},{2,0},{4,6},{6,4},{8,10},{10,8},{12,14},{14,12},{1,3},{3,1},... | collective-permute-start | bytes 589832 | tf_op jit(solution)/shard_map/ppermute | solution.py:219
  15.7 9.7 %collective-permute-start.8 = (bf16[192,512]{1,0:T(8,128)(2,1)S(1)}, bf16[192,512]{1,0:T(8,128)(2,1)S(1)}, u32[]{:S(2)}, u32[]{:S(2)}) collective-permute-start(bf16[192,512]{1,0:T(8,128)(2,1)S(1)} %get-tuple-element.30), channel_id=1, source_target_pairs={{0,4},{2,6},{4,8},{6,10},{8,12},{10,14},{12,0},{14,2},{1,5},{3,7},... | collective-permute-start | bytes 589832 | tf_op jit(solution)/shard_map/ppermute | solution.py:224
  17.3 15.5 %collective-permute-start.15 = (bf16[192,512]{1,0:T(8,128)(2,1)S(1)}, bf16[192,512]{1,0:T(8,128)(2,1)S(1)}, u32[]{:S(2)}, u32[]{:S(2)}) collective-permute-start(bf16[192,512]{1,0:T(8,128)(2,1)S(1)} %get-tuple-element.33), channel_id=1, source_target_pairs={{0,8},{2,10},{4,12},{6,14},{8,0},{10,2},{12,4},{14,6},{1,9},{3,11}... | collective-permute-start | bytes 589832 | tf_op jit(solution)/shard_map/ppermute | solution.py:224
  19.9 13.4 %collective-permute-start.22 = (bf16[192,512]{1,0:T(8,128)(2,1)S(1)}, bf16[192,512]{1,0:T(8,128)(2,1)S(1)}, u32[]{:S(2)}, u32[]{:S(2)}) collective-permute-start(bf16[192,512]{1,0:T(8,128)(2,1)S(1)} %get-tuple-element.36), channel_id=1, source_target_pairs={{0,12},{2,14},{4,0},{6,2},{8,4},{10,6},{12,8},{14,10},{1,13},{3,15... | collective-permute-start | bytes 589832 | tf_op jit(solution)/shard_map/ppermute | solution.py:224
  21.3 13.6 %collective-permute-start.4 = (bf16[192,512]{1,0:T(8,128)(2,1)S(1)}, bf16[192,512]{1,0:T(8,128)(2,1)S(1)}, u32[]{:S(2)}, u32[]{:S(2)}) collective-permute-start(bf16[192,512]{1,0:T(8,128)(2,1)S(1)} %get-tuple-element.27.p_ref), channel_id=1, source_target_pairs={{0,1},{1,0},{2,3},{3,2},{4,5},{5,4},{6,7},{7,6},{8,9},{9,8},{10,11... | collective-permute-start | bytes 589832 | tf_op jit(solution)/shard_map/ppermute | solution.py:214
  21.3 13.6 %collective-permute-start.5 = (bf16[192,512]{1,0:T(8,128)(2,1)S(1)}, bf16[192,512]{1,0:T(8,128)(2,1)S(1)}, u32[]{:S(2)}, u32[]{:S(2)}) collective-permute-start(bf16[192,512]{1,0:T(8,128)(2,1)S(1)} %collective-permute-done.3.q_ref), channel_id=1, source_target_pairs={{0,1},{1,0},{2,3},{3,2},{4,5},{5,4},{6,7},{7,6},{8,9},{9,8},{10,11... | collective-permute-start | bytes 589832 | tf_op jit(solution)/shard_map/ppermute | solution.py:214
  25.4 14.5 %collective-permute-start.9 = (bf16[192,512]{1,0:T(8,128)(2,1)S(1)}, bf16[192,512]{1,0:T(8,128)(2,1)S(1)}, u32[]{:S(2)}, u32[]{:S(2)}) collective-permute-start(bf16[192,512]{1,0:T(8,128)(2,1)S(1)} %collective-permute-done.8.p_ref), channel_id=1, source_target_pairs={{0,2},{2,0},{4,6},{6,4},{8,10},{10,8},{12,14},{14,12},{1,3},{3,1},... | collective-permute-start | bytes 589832 | tf_op jit(solution)/shard_map/ppermute | solution.py:219
  32.8 7.8 %collective-permute-start.16 = (bf16[192,512]{1,0:T(8,128)(2,1)S(1)}, bf16[192,512]{1,0:T(8,128)(2,1)S(1)}, u32[]{:S(2)}, u32[]{:S(2)}) collective-permute-start(bf16[192,512]{1,0:T(8,128)(2,1)S(1)} %collective-permute-done.15.p_ref), channel_id=1, source_target_pairs={{0,2},{2,0},{4,6},{6,4},{8,10},{10,8},{12,14},{14,12},{1,3},{3,1},... | collective-permute-start | bytes 589832 | tf_op jit(solution)/shard_map/ppermute | solution.py:219
  33.4 10.4 %collective-permute-start.23 = (bf16[192,512]{1,0:T(8,128)(2,1)S(1)}, bf16[192,512]{1,0:T(8,128)(2,1)S(1)}, u32[]{:S(2)}, u32[]{:S(2)}) collective-permute-start(bf16[192,512]{1,0:T(8,128)(2,1)S(1)} %collective-permute-done.22.p_ref), channel_id=1, source_target_pairs={{0,2},{2,0},{4,6},{6,4},{8,10},{10,8},{12,14},{14,12},{1,3},{3,1},... | collective-permute-start | bytes 589832 | tf_op jit(solution)/shard_map/ppermute | solution.py:219
  34.8 1.6 %copy-start = (bf16[1024,1024]{1,0:T(8,128)(2,1)S(1)}, bf16[1024,1024]{1,0:T(8,128)(2,1)}, u32[]{:S(2)}) copy-start(bf16[1024,1024]{1,0:T(8,128)(2,1)} %in_ref.7) | copy-start | bytes 6291460
  36.4 1.6 %copy-start.2 = (bf16[1024,1024]{1,0:T(8,128)(2,1)S(1)}, bf16[1024,1024]{1,0:T(8,128)(2,1)}, u32[]{:S(2)}) copy-start(bf16[1024,1024]{1,0:T(8,128)(2,1)} %out_ref.7) | copy-start | bytes 6291460
  38.0 6.8 %copy-start.1 = (bf16[1024,1024]{1,0:T(8,128)(2,1)S(1)}, bf16[1024,1024]{1,0:T(8,128)(2,1)}, u32[]{:S(2)}) copy-start(bf16[1024,1024]{1,0:T(8,128)(2,1)} %in_ref.7) | copy-start | bytes 6291460
  38.0 6.8 %copy-start.3 = (bf16[1024,1024]{1,0:T(8,128)(2,1)S(1)}, bf16[1024,1024]{1,0:T(8,128)(2,1)}, u32[]{:S(2)}) copy-start(bf16[1024,1024]{1,0:T(8,128)(2,1)} %out_ref.7) | copy-start | bytes 6291460
  39.9 6.9 %collective-permute-start.6 = (bf16[2,192,512]{2,1,0:T(8,128)(2,1)S(1)}, bf16[2,192,512]{2,1,0:T(8,128)(2,1)S(1)}, u32[]{:S(2)}, u32[]{:S(2)}) collective-permute-start(bf16[2,192,512]{2,1,0:T(8,128)(2,1)S(1)} %get-tuple-element.29), channel_id=1, source_target_pairs={{0,1},{1,0},{2,3},{3,2},{4,5},{5,4},{6,7},{7,6},{8,9},{9,8},{10,11... | collective-permute-start | bytes 1179656 | tf_op jit(solution)/shard_map/ppermute | solution.py:214
  40.0 3.8 %collective-permute-start.11 = (bf16[192,512]{1,0:T(8,128)(2,1)S(1)}, bf16[192,512]{1,0:T(8,128)(2,1)S(1)}, u32[]{:S(2)}, u32[]{:S(2)}) collective-permute-start(bf16[192,512]{1,0:T(8,128)(2,1)S(1)} %collective-permute-done.9.q_ref), channel_id=1, source_target_pairs={{0,1},{1,0},{2,3},{3,2},{4,5},{5,4},{6,7},{7,6},{8,9},{9,8},{10,11... | collective-permute-start | bytes 589832 | tf_op jit(solution)/shard_map/ppermute | solution.py:214
  40.5 3.8 %collective-permute-start.17 = (bf16[192,512]{1,0:T(8,128)(2,1)S(1)}, bf16[192,512]{1,0:T(8,128)(2,1)S(1)}, u32[]{:S(2)}, u32[]{:S(2)}) collective-permute-start(bf16[192,512]{1,0:T(8,128)(2,1)S(1)} %collective-permute-done.15.p_ref), channel_id=1, source_target_pairs={{0,1},{1,0},{2,3},{3,2},{4,5},{5,4},{6,7},{7,6},{8,9},{9,8},{10,11... | collective-permute-start | bytes 589832 | tf_op jit(solution)/shard_map/ppermute | solution.py:214
  40.6 3.8 %collective-permute-start.18 = (bf16[192,512]{1,0:T(8,128)(2,1)S(1)}, bf16[192,512]{1,0:T(8,128)(2,1)S(1)}, u32[]{:S(2)}, u32[]{:S(2)}) collective-permute-start(bf16[192,512]{1,0:T(8,128)(2,1)S(1)} %collective-permute-done.16.q_ref), channel_id=1, source_target_pairs={{0,1},{1,0},{2,3},{3,2},{4,5},{5,4},{6,7},{7,6},{8,9},{9,8},{10,11... | collective-permute-start | bytes 589832 | tf_op jit(solution)/shard_map/ppermute | solution.py:214
  43.7 2.9 %collective-permute-start.25 = (bf16[192,512]{1,0:T(8,128)(2,1)S(1)}, bf16[192,512]{1,0:T(8,128)(2,1)S(1)}, u32[]{:S(2)}, u32[]{:S(2)}) collective-permute-start(bf16[192,512]{1,0:T(8,128)(2,1)S(1)} %collective-permute-done.23.q_ref), channel_id=1, source_target_pairs={{0,1},{1,0},{2,3},{3,2},{4,5},{5,4},{6,7},{7,6},{8,9},{9,8},{10,11... | collective-permute-start | bytes 589832 | tf_op jit(solution)/shard_map/ppermute | solution.py:214
  43.7 26.8 %collective-permute-start.1 = (f32[2,128]{1,0:T(2,128)S(1)}, f32[2,128]{1,0:T(2,128)S(1)}, u32[]{:S(2)}, u32[]{:S(2)}) collective-permute-start(f32[2,128]{1,0:T(2,128)S(1)} %get-tuple-element.24.own_gates_ref), channel_id=1, source_target_pairs={{0,1},{1,0},{2,3},{3,2},{4,5},{5,4},{6,7},{7,6},{8,9},{9,8},{10,11... | collective-permute-start | bytes 3080 | tf_op jit(solution)/shard_map/ppermute | solution.py:214
  44.3 3.3 %collective-permute-start.10 = (bf16[192,512]{1,0:T(8,128)(2,1)S(1)}, bf16[192,512]{1,0:T(8,128)(2,1)S(1)}, u32[]{:S(2)}, u32[]{:S(2)}) collective-permute-start(bf16[192,512]{1,0:T(8,128)(2,1)S(1)} %collective-permute-done.8.p_ref), channel_id=1, source_target_pairs={{0,1},{1,0},{2,3},{3,2},{4,5},{5,4},{6,7},{7,6},{8,9},{9,8},{10,11... | collective-permute-start | bytes 589832 | tf_op jit(solution)/shard_map/ppermute | solution.py:214
  44.3 7.0 %collective-permute-start.24 = (bf16[192,512]{1,0:T(8,128)(2,1)S(1)}, bf16[192,512]{1,0:T(8,128)(2,1)S(1)}, u32[]{:S(2)}, u32[]{:S(2)}) collective-permute-start(bf16[192,512]{1,0:T(8,128)(2,1)S(1)} %collective-permute-done.22.p_ref), channel_id=1, source_target_pairs={{0,1},{1,0},{2,3},{3,2},{4,5},{5,4},{6,7},{7,6},{8,9},{9,8},{10,11... | collective-permute-start | bytes 589832 | tf_op jit(solution)/shard_map/ppermute | solution.py:214
  46.6 3.0 %collective-permute-start.19 = (bf16[2,192,512]{2,1,0:T(8,128)(2,1)S(1)}, bf16[2,192,512]{2,1,0:T(8,128)(2,1)S(1)}, u32[]{:S(2)}, u32[]{:S(2)}) collective-permute-start(bf16[2,192,512]{2,1,0:T(8,128)(2,1)S(1)} %get-tuple-element.35), channel_id=1, source_target_pairs={{0,1},{1,0},{2,3},{3,2},{4,5},{5,4},{6,7},{7,6},{8,9},{9,8},{10,11... | collective-permute-start | bytes 1179656 | tf_op jit(solution)/shard_map/ppermute | solution.py:214
  46.9 23.5 %collective-permute-start.7 = (bf16[192,512]{1,0:T(8,128)(2,1)S(1)}, bf16[192,512]{1,0:T(8,128)(2,1)S(1)}, u32[]{:S(2)}, u32[]{:S(2)}) collective-permute-start(bf16[192,512]{1,0:T(8,128)(2,1)S(1)} %fusion.8.first_ref), channel_id=1, source_target_pairs={{0,2},{2,0},{4,6},{6,4},{8,10},{10,8},{12,14},{14,12},{1,3},{3,1},... | collective-permute-start | bytes 589832 | tf_op jit(solution)/shard_map/ppermute | solution.py:219
  49.4 3.9 %collective-permute-start.12 = (bf16[2,192,512]{2,1,0:T(8,128)(2,1)S(1)}, bf16[2,192,512]{2,1,0:T(8,128)(2,1)S(1)}, u32[]{:S(2)}, u32[]{:S(2)}) collective-permute-start(bf16[2,192,512]{2,1,0:T(8,128)(2,1)S(1)} %get-tuple-element.32), channel_id=1, source_target_pairs={{0,1},{1,0},{2,3},{3,2},{4,5},{5,4},{6,7},{7,6},{8,9},{9,8},{10,11... | collective-permute-start | bytes 1179656 | tf_op jit(solution)/shard_map/ppermute | solution.py:214
  49.8 9.1 %collective-permute-start.20 = (bf16[192,512]{1,0:T(8,128)(2,1)S(1)}, bf16[192,512]{1,0:T(8,128)(2,1)S(1)}, u32[]{:S(2)}, u32[]{:S(2)}) collective-permute-start(bf16[192,512]{1,0:T(8,128)(2,1)S(1)} %fusion.10.first_ref), channel_id=1, source_target_pairs={{0,2},{2,0},{4,6},{6,4},{8,10},{10,8},{12,14},{14,12},{1,3},{3,1},... | collective-permute-start | bytes 589832 | tf_op jit(solution)/shard_map/ppermute | solution.py:219
  53.2 8.6 %collective-permute-start.26 = (bf16[2,192,512]{2,1,0:T(8,128)(2,1)S(1)}, bf16[2,192,512]{2,1,0:T(8,128)(2,1)S(1)}, u32[]{:S(2)}, u32[]{:S(2)}) collective-permute-start(bf16[2,192,512]{2,1,0:T(8,128)(2,1)S(1)} %get-tuple-element.38), channel_id=1, source_target_pairs={{0,1},{1,0},{2,3},{3,2},{4,5},{5,4},{6,7},{7,6},{8,9},{9,8},{10,11... | collective-permute-start | bytes 1179656 | tf_op jit(solution)/shard_map/ppermute | solution.py:214
  53.5 9.2 %collective-permute-start.13 = (bf16[192,512]{1,0:T(8,128)(2,1)S(1)}, bf16[192,512]{1,0:T(8,128)(2,1)S(1)}, u32[]{:S(2)}, u32[]{:S(2)}) collective-permute-start(bf16[192,512]{1,0:T(8,128)(2,1)S(1)} %fusion.9), channel_id=1, source_target_pairs={{0,2},{2,0},{4,6},{6,4},{8,10},{10,8},{12,14},{14,12},{1,3},{3,1},... | collective-permute-start | bytes 589832 | tf_op jit(solution)/shard_map/ppermute | solution.py:219
  59.0 13.0 %collective-permute-start.21 = (bf16[192,512]{1,0:T(8,128)(2,1)S(1)}, bf16[192,512]{1,0:T(8,128)(2,1)S(1)}, u32[]{:S(2)}, u32[]{:S(2)}) collective-permute-start(bf16[192,512]{1,0:T(8,128)(2,1)S(1)} %fusion.3), channel_id=1, source_target_pairs={{0,8},{2,10},{4,12},{6,14},{8,0},{10,2},{12,4},{14,6},{1,9},{3,11}... | collective-permute-start | bytes 589832 | tf_op jit(solution)/shard_map/ppermute | solution.py:224
  61.8 15.1 %copy-start.7 = (s32[2,128,2]{1,2,0:T(2,128)S(1)}, s32[2,128,2]{1,2,0:T(2,128)}, u32[]{:S(2)}) copy-start(s32[2,128,2]{1,2,0:T(2,128)} %param.16) | copy-start | bytes 6148
  62.0 6.1 %collective-permute-start.27 = (bf16[192,512]{1,0:T(8,128)(2,1)S(1)}, bf16[192,512]{1,0:T(8,128)(2,1)S(1)}, u32[]{:S(2)}, u32[]{:S(2)}) collective-permute-start(bf16[192,512]{1,0:T(8,128)(2,1)S(1)} %fusion.11), channel_id=1, source_target_pairs={{0,2},{2,0},{4,6},{6,4},{8,10},{10,8},{12,14},{14,12},{1,3},{3,1},... | collective-permute-start | bytes 589832 | tf_op jit(solution)/shard_map/ppermute | solution.py:219
  62.7 10.7 %collective-permute-start.14 = (bf16[192,512]{1,0:T(8,128)(2,1)S(1)}, bf16[192,512]{1,0:T(8,128)(2,1)S(1)}, u32[]{:S(2)}, u32[]{:S(2)}) collective-permute-start(bf16[192,512]{1,0:T(8,128)(2,1)S(1)} %fusion.5), channel_id=1, source_target_pairs={{0,12},{2,14},{4,0},{6,2},{8,4},{10,6},{12,8},{14,10},{1,13},{3,15... | collective-permute-start | bytes 589832 | tf_op jit(solution)/shard_map/ppermute | solution.py:224
  68.1 8.8 %collective-permute-start.28 = (bf16[192,512]{1,0:T(8,128)(2,1)S(1)}, bf16[192,512]{1,0:T(8,128)(2,1)S(1)}, u32[]{:S(2)}, u32[]{:S(2)}) collective-permute-start(bf16[192,512]{1,0:T(8,128)(2,1)S(1)} %fusion.1), channel_id=1, source_target_pairs={{0,4},{2,6},{4,8},{6,10},{8,12},{10,14},{12,0},{14,2},{1,5},{3,7},... | collective-permute-start | bytes 589832 | tf_op jit(solution)/shard_map/ppermute | solution.py:224
  77.8 1.4 %collective-permute-start.29 = (bf16[128,512]{1,0:T(8,128)(2,1)S(1)}, bf16[128,512]{1,0:T(8,128)(2,1)S(1)}, u32[]{:S(2)}, u32[]{:S(2)}) collective-permute-start(bf16[128,512]{1,0:T(8,128)(2,1)S(1)} %get-tuple-element.40), channel_id=1, source_target_pairs={{0,1},{1,0},{2,3},{3,2},{4,5},{5,4},{6,7},{7,6},{8,9},{9,8},{10,11... | collective-permute-start | bytes 393224 | tf_op jit(solution)/shard_map/ppermute | solution.py:214

commit v9 on v8

--- a/solution.py
+++ b/solution.py
@@ -18,71 +18,150 @@
 
 VMEM = pl.BlockSpec(memory_space=pltpu.VMEM)
 SMEM = pl.BlockSpec(memory_space=pltpu.SMEM)
-
-
-def call(kernel, name, outs, scalars, arrays, scratch=(), vmem_mib=12, cost=None):
+HBM = pl.BlockSpec(memory_space=pltpu.HBM)
+
+
+def call(kernel, name, outs, scalars, arrays, far=(), scratch=(), vmem_mib=12):
     return pl.pallas_call(
         kernel,
         out_shape=tuple(jax.ShapeDtypeStruct(*out) for out in outs),
-        in_specs=[SMEM] * len(scalars) + [VMEM] * len(arrays),
+        in_specs=[SMEM] * len(scalars) + [VMEM] * len(arrays) + [HBM] * len(far),
         out_specs=(VMEM,) * len(outs),
         scratch_shapes=list(scratch),
         compiler_params=pltpu.CompilerParams(vmem_limit_bytes=vmem_mib * 2**20),
-        cost_estimate=cost,
         name=name,
-    )(*scalars, *arrays)
+    )(*scalars, *arrays, *(pltpu.with_memory_space_constraint(a, pltpu.HBM) for a in far))
+
+
+def fetch(sems, *pairs):
+    copies = [
+        pltpu.make_async_copy(source, target, sems.at[i]) for i, (source, target) in enumerate(pairs)
+    ]
+    for copy in copies:
+        copy.start()
+    return copies
 
 
 def part_of(part, half):
     return pl.ds(pl.multiple_of(part * half, half), half)
 
 
-def attend_kernel(
+def attend_half(queries, keys, values, length):
+    rows = queries.shape[0]
+    heads = [slice(at, at + HEAD_DIM) for at in range(0, queries.shape[1], HEAD_DIM)]
+    scores = jnp.concatenate(
+        [
+            lax.dot_general(
+                queries[:, head],
+                keys[:, head],
+                (((1,), (1,)), ((), ())),
+                preferred_element_type=jnp.float32,
+            )
+            for head in heads
+        ],
+        axis=0,
+    ) * HEAD_DIM ** (-0.5)
+    valid = lax.broadcasted_iota(jnp.int32, (1, keys.shape[0]), 1) < length
+    scores = jnp.where(valid, scores, -jnp.inf)
+    expon = jnp.exp(scores - jnp.max(scores, axis=-1, keepdims=True))
+    weights = (expon / jnp.sum(expon, axis=-1, keepdims=True)).astype(jnp.bfloat16)
+    return jnp.concatenate(
+        [
+            jnp.dot(
+                weights[i * rows : (i + 1) * rows],
+                values[:, head],
+                preferred_element_type=jnp.float32,
+            )
+            for i, head in enumerate(heads)
+        ],
+        axis=1,
+    )
+
+
+def add_rounded(x, attended):
+    return (x.astype(jnp.float32) + attended).astype(jnp.bfloat16)
+
+
+def attend_own_kernel(
     core_ref,
     source_ref,
-    target_ref,
+    x_in,
+    gain_in,
+    keys_in,
+    values_in,
+    state_ref,
+    query_ref,
+    rest_ref,
     x_ref,
+    gain_ref,
+    keys_ref,
+    values_ref,
+    scratch_ref,
+    sems,
+):
+    core = core_ref[0]
+    copies = fetch(
+        sems,
+        (x_in.at[0], x_ref),
+        (gain_in, gain_ref),
+        (keys_in.at[core], keys_ref),
+        (values_in.at[core], values_ref),
+    )
+    half = keys_ref.shape[1]
+    copies[0].wait()
+    copies[1].wait()
+    scratch_ref[...] = layer_norm(x_ref[...].astype(jnp.float32), gain_ref[...])
+    own, other = part_of(core, half), part_of(1 - core, half)
+    query_ref[...] = scratch_ref[:, other]
+    rest_ref[...] = x_ref[:, other]
+    copies[2].wait()
+    copies[3].wait()
+    attended = attend_half(scratch_ref[:, own], keys_ref[...], values_ref[...], source_ref[0])
+    state_ref[...] = add_rounded(x_ref[:, own], attended)
+
+
+def attend_other_kernel(
+    core_ref,
+    source_ref,
     own_ref,
-    other_ref,
-    again_ref,
-    fgain_ref,
-    router_ref,
-    routes_ref,
+    query_ref,
+    rest_ref,
+    keys_ref,
+    values_ref,
+    gain_in,
+    router_in,
+    routes_in,
+    target_in,
     state_ref,
     keep_ref,
     send_ref,
     gates_ref,
+    routes_ref,
+    gain_ref,
+    router_ref,
+    target_ref,
     scratch_ref,
+    sems,
 ):
-    full_len = x_ref.shape[0]
-    half = own_ref.shape[-1]
-    widened = x_ref[...].astype(jnp.float32)
-    scratch_ref[...] = layer_norm(widened, again_ref[...])
     core = core_ref[0]
-    keys_seen = own_ref.shape[1]
-    valid = lax.broadcasted_iota(jnp.int32, (1, keys_seen), 1) < source_ref[0]
-    for part, memory in ((core, own_ref), (1 - core, other_ref)):
-        for head in range(half // HEAD_DIM):
-            at = head * HEAD_DIM
-            span = pl.ds(pl.multiple_of(part * half + at, HEAD_DIM), HEAD_DIM)
-            scores = lax.dot_general(
-                scratch_ref[:, span],
-                memory[0, :, at : at + HEAD_DIM],
-                (((1,), (1,)), ((), ())),
-                preferred_element_type=jnp.float32,
-            ) * HEAD_DIM ** (-0.5)
-            scores = jnp.where(valid, scores, -jnp.inf)
-            expon = jnp.exp(scores - jnp.max(scores, axis=-1, keepdims=True))
-            weights = (expon / jnp.sum(expon, axis=-1, keepdims=True)).astype(jnp.bfloat16)
-            attended = jnp.dot(
-                weights, memory[1, :, at : at + HEAD_DIM], preferred_element_type=jnp.float32
-            )
-            state_ref[:, span] = (x_ref[:, span].astype(jnp.float32) + attended).astype(
-                jnp.bfloat16
-            )
-    scratch_ref[...] = layer_norm(state_ref[...].astype(jnp.float32), fgain_ref[...])
-    keep_ref[...] = scratch_ref[:, part_of(core, half)]
-    send_ref[...] = scratch_ref[:, part_of(1 - core, half)]
+    copies = fetch(
+        sems,
+        (gain_in, gain_ref),
+        (router_in, router_ref),
+        (routes_in, routes_ref),
+        (target_in, target_ref),
+    )
+    full_len, half = own_ref.shape
+    own, other = part_of(core, half), part_of(1 - core, half)
+    attended = attend_half(query_ref[...], keys_ref[core], values_ref[core], source_ref[0])
+    state_ref[:, own] = own_ref[...]
+    state_ref[:, other] = add_rounded(rest_ref[...], attended)
+    copies[0].wait()
+    scratch_ref[...] = layer_norm(state_ref[...].astype(jnp.float32), gain_ref[...])
+    keep_ref[...] = scratch_ref[:, own]
+    send_ref[...] = scratch_ref[:, other]
+    for copy in copies[1:]:
+        copy.wait()
     logits = lax.dot_general(
         router_ref[...],
         scratch_ref[...],
@@ -161,6 +240,52 @@
     send_ref[0] = send[:capacity]
     send_ref[1] = send[capacity:]
     keep = jnp.dot(hidden, out_ref[:, part_of(core, half)], preferred_element_type=jnp.float32)
+    keep_ref[0] = keep[:capacity]
+    keep_ref[1] = keep[capacity:]
+
+
+def first_expert_kernel(
+    core_ref,
+    p_ref,
+    q_ref,
+    p2_ref,
+    q2_ref,
+    in_in,
+    out_in,
+    keep_ref,
+    send_ref,
+    rows_ref,
+    in_ref,
+    out_ref,
+    hidden_ref,
+    sems,
+):
+    core = core_ref[0]
+    capacity, half = p_ref.shape
+    tile = in_ref.shape[1] // 4
+    tiles = [slice(at, at + tile) for at in range(0, in_ref.shape[1], tile)]
+    copies = fetch(
+        sems,
+        *[(in_in.at[:, at], in_ref.at[:, at]) for at in tiles],
+        (out_in, out_ref),
+    )
+    rows_ref[:capacity, part_of(core, half)] = p_ref[...]
+    rows_ref[capacity:, part_of(core, half)] = q_ref[...]
+    rows_ref[:capacity, part_of(1 - core, half)] = p2_ref[...]
+    rows_ref[capacity:, part_of(1 - core, half)] = q2_ref[...]
+    for copy, at in zip(copies, tiles):
+        copy.wait()
+        hidden = jnp.dot(rows_ref[...], in_ref[:, at], preferred_element_type=jnp.float32)
+        hidden_ref[:, at] = jnp.maximum(hidden, 0.0).astype(jnp.bfloat16)
+    copies[-1].wait()
+    send = jnp.dot(
+        hidden_ref[...], out_ref[:, part_of(1 - core, half)], preferred_element_type=jnp.float32
+    ).astype(jnp.bfloat16)
+    send_ref[0] = send[:capacity]
+    send_ref[1] = send[capacity:]
+    keep = jnp.dot(
+        hidden_ref[...], out_ref[:, part_of(core, half)], preferred_element_type=jnp.float32
+    )
     keep_ref[0] = keep[:capacity]
     keep_ref[1] = keep[capacity:]
 
@@ -252,30 +377,45 @@
     attn_gain, ffn_gain, router,
 ):
     full_len, width = decoder_states.shape[1:]
-    memory = jnp.stack([memory_keys, memory_values], axis=1)
-    own = lax.dynamic_index_in_dim(memory, core[0], 0, keepdims=False)
-    other = swap(lax.dynamic_index_in_dim(memory, 1 - core[0], 0, keepdims=False))
     half = (full_len, width // 2)
+    memory = memory_keys.shape[1:]
+    other_keys, other_values = swap(memory_keys), swap(memory_values)
+    own, query, rest = call(
+        attend_own_kernel,
+        "attend_own",
+        [(half, jnp.bfloat16)] * 3,
+        [core, source_lengths],
+        [],
+        [decoder_states, attn_gain[None], memory_keys, memory_values],
+        scratch=[
+            pltpu.VMEM((full_len, width), jnp.bfloat16),
+            pltpu.VMEM((1, width), jnp.float32),
+            pltpu.VMEM(memory, jnp.bfloat16),
+            pltpu.VMEM(memory, jnp.bfloat16),
+            pltpu.VMEM((full_len, width), jnp.bfloat16),
+            pltpu.SemaphoreType.DMA((4,)),
+        ],
+    )
     return call(
-        attend_kernel,
-        "attend",
+        attend_other_kernel,
+        "attend_other",
         [
             ((full_len, width), jnp.bfloat16),
             (half, jnp.bfloat16),
             (half, jnp.bfloat16),
             ((2, full_len), jnp.float32),
+            (routes.shape, jnp.int32),
         ],
-        [core, source_lengths, target_lengths],
-        [
-            decoder_states[0],
-            own,
-            other,
-            attn_gain[None],
-            ffn_gain[None],
-            router.T,
-            routes,
+        [core, source_lengths],
+        [own, query, rest, other_keys, other_values],
+        [ffn_gain[None], router.T, routes, target_lengths],
+        scratch=[
+            pltpu.VMEM((1, width), jnp.float32),
+            pltpu.VMEM(router.shape[::-1], jnp.bfloat16),
+            pltpu.SMEM(target_lengths.shape, jnp.int32),
+            pltpu.VMEM((full_len, width), jnp.bfloat16),
+            pltpu.SemaphoreType.DMA((4,)),
         ],
-        scratch=[pltpu.VMEM((full_len, width), jnp.bfloat16)],
     )
 
 
@@ -308,15 +448,35 @@
             q2 = after(q2, kepts[at - 2])
         if at >= 2:
             q2 = after(q2, halves[at - 2])
-        kept, sent = call(
-            expert_kernel,
-            "expert",
-            [((2, capacity, half), jnp.float32), ((2, capacity, half), jnp.bfloat16)],
-            [core],
-            [p, q, p2, q2, fc_in, fc_out],
-            scratch=[pltpu.VMEM((2 * capacity, width), jnp.bfloat16)],
-            vmem_mib=16,
-        )
+        outs = [((2, capacity, half), jnp.float32), ((2, capacity, half), jnp.bfloat16)]
+        rows = pltpu.VMEM((2 * capacity, width), jnp.bfloat16)
+        if at == 0:
+            kept, sent = call(
+                first_expert_kernel,
+                "first_expert",
+                outs,
+                [core],
+                [p, q, p2, q2],
+                [fc_in, fc_out],
+                scratch=[
+                    rows,
+                    pltpu.VMEM(fc_in.shape, jnp.bfloat16),
+                    pltpu.VMEM(fc_out.shape, jnp.bfloat16),
+                    pltpu.VMEM((2 * capacity, fc_in.shape[1]), jnp.bfloat16),
+                    pltpu.SemaphoreType.DMA((5,)),
+                ],
+                vmem_mib=20,
+            )
+        else:
+            kept, sent = call(
+                expert_kernel,
+                "expert",
+                outs,
+                [core],
+                [p, q, p2, q2, fc_in, fc_out],
+                scratch=[rows],
+                vmem_mib=16,
+            )
         kepts.append(kept)
         both = kept + swap(sent).astype(jnp.float32)
         halves.append(both[1].astype(jnp.bfloat16))
@@ -421,7 +581,7 @@
 ):
     core = lax.axis_index("section").astype(jnp.int32).reshape(1)
     by_choice = jnp.transpose(routes, (0, 2, 1))
-    state, keep, send, gates = attend(
+    state, keep, send, gates, by_choice = attend(
         core, decoder_states, memory_keys, memory_values, source_lengths, target_lengths, by_choice,
         attn_gain, ffn_gain, router,
     )

time: 81.2 us -> 74.4 us (0.916)
  local copies, waits for them, and re-layouts: 8.33 us -> 0.11 us
  Pallas kernels: 12.8 us -> 15 us
  other arithmetic: 1.64 us -> 0.61 us
    unnamed x24 -> x4, local copies, waits for them, and re-layouts: 8.23 us -> 0.01 us
    pallas_call x8 -> x9, Pallas kernels: 12.8 us -> 15 us  [call(): pl.pallas_call(kernel, out_shape=tuple((jax.ShapeDtypeStruct(*out) for ou...]
    ppermute x8, waiting for transfers between devices: 7.76 us -> 8.83 us  [swap_owner(): return lax.ppermute(values, 'expert', [(i, i ^ 1) for i in range(owners)])]
    squeeze x1 -> x0, other arithmetic: 1.03 us -> none  [attend(): lax.dynamic_index_in_dim(memory, 1 - core[0], 0, keepdims=False)]
    ppermute x16 -> x17, waiting for transfers between devices: 2.73 us -> 2.36 us  [swap(): return lax.ppermute(values, 'section', [(0, 1), (1, 0)])]
    ppermute x16 -> x17, starting transfers between devices: 4.09 us -> 3.78 us  [swap(): return lax.ppermute(values, 'section', [(0, 1), (1, 0)])]
  transfers between devices with their start and end apart: 30 -> 31, of which waited for: 11 -> 11; matrix products, arithmetic and copies ran while one was open for 1% -> 1% of each run, Pallas kernels for 9% -> 16%
where the time goes in v9:
time: 74.4 us; the launch traced here: 73.4 us
  starting transfers between devices  28.5 us (38%)
  waiting for transfers between devices  28.3 us (38%)
  Pallas kernels  15 us (20%)
  between operations  0.88 us (1%)
    ppermute x6, waiting for transfers between devices, shift(): lax.ppermute(values, 'expert', [(i, (i + 2 * offset) % owners) for i in r...  17.1 us
    ppermute x6, starting transfers between devices, shift(): lax.ppermute(values, 'expert', [(i, (i + 2 * offset) % owners) for i in r...  16.1 us
    pallas_call x9, Pallas kernels, call(): pl.pallas_call(kernel, out_shape=tuple((jax.ShapeDtypeStruct(*out) for ou...  15 us
    ppermute x8, waiting for transfers between devices, swap_owner(): return lax.ppermute(values, 'expert', [(i, i ^ 1) for i in range(owners)])  8.83 us
    ppermute x8, starting transfers between devices, swap_owner(): return lax.ppermute(values, 'expert', [(i, i ^ 1) for i in range(owners)])  8.65 us
    ppermute x17, starting transfers between devices, swap(): return lax.ppermute(values, 'section', [(0, 1), (1, 0)])  3.78 us
    ppermute x17, waiting for transfers between devices, swap(): return lax.ppermute(values, 'section', [(0, 1), (1, 0)])  2.36 us
  transfers between devices with their start and end apart: 31, of which 11 were waited for; matrix products, arithmetic and copies ran while one was open for 1% of the time, Pallas kernels for 16%

profile of v9, /device:TPU:0, one launch (start us, length us, event | category | flops | bytes accessed | tf_op | source)
XLA Modules:
  0.0 73.4 jit_solution(8032873139901349809)
XLA Ops:
  0.0 0.5 collective-permute-start
  0.5 0.1 collective-permute-start.1
  1.2 1.8 %attend_own.1 = (bf16[128,512]{1,0:T(8,128)(2,1)S(1)}, bf16[128,512]{1,0:T(8,128)(2,1)S(1)}, bf16[128,512]{1,0:T(8,128)(2,1)S(1)}) custom-call(s32[1]{0:T(128)} %bitcast.core_ref, s32[1]{0:T(128)S(6)} %copy.20.source_ref, bf16[1,128,1024]{2,1,0:T(8,128)(2,1)} %x_in.1, f32[1,1024]{1,0:T(1,128)} %bitcast.40, bf16[2,80,512]{2,1,0:T(8,128)(2,1)} %keys_in.1, ...), custom_call_target="tpu_custom_call" | custom-call | tf_op jit(solution)/shard_map/attend_own/pallas_call | solution.py:25
  2.9 0.0 collective-permute-done.keys_ref
  3.0 1.2 %attend_other.1 = (bf16[128,1024]{1,0:T(8,128)(2,1)S(1)}, bf16[128,512]{1,0:T(8,128)(2,1)S(1)}, bf16[128,512]{1,0:T(8,128)(2,1)S(1)}, f32[2,128]{1,0:T(2,128)S(1)}, s32[2,2,128]{2,1,0:T(2,128)S(1)}) custom-call(s32[1]{0:T(128)} %bitcast.core_ref, s32[1]{0:T(128)S(6)} %copy.20.source_ref, bf16[128,512]{1,0:T(8,128)(2,1)S(1)} %get-tuple-element.27.own_ref, ...), custom_call_target="tpu_custom_call" | custom-call | tf_op jit(solution)/shard_map/attend_other/pallas_call | solution.py:25
  4.2 0.5 collective-permute-start.3
  4.7 1.0 %collective-permute-done.3.other_ref = bf16[128,512]{1,0:T(8,128)(2,1)S(1)} collective-permute-done((bf16[128,512]{1,0:T(8,128)(2,1)S(1)}, bf16[128,512]{1,0:T(8,128)(2,1)S(1)}, u32[]{:S(2)}, u32[]{:S(2)}) %collective-permute-start.3) | collective-permute-done | bytes 131104 | tf_op jit(solution)/shard_map/ppermute | solution.py:339
  5.7 0.5 select.5
  6.2 2.9 %collective-permute-start.4 = (bf16[192,512]{1,0:T(8,128)(2,1)S(1)}, bf16[192,512]{1,0:T(8,128)(2,1)S(1)}, u32[]{:S(2)}, u32[]{:S(2)}) collective-permute-start(bf16[192,512]{1,0:T(8,128)(2,1)S(1)} %get-tuple-element.35.p_ref), channel_id=1, source_target_pairs={{0,2},{2,0},{4,6},{6,4},{8,10},{10,8},{12,14},{14,12},{1,3},{3,1},... | collective-permute-start | bytes 589832 | tf_op jit(solution)/shard_map/ppermute | solution.py:344
  9.2 1.6 %collective-permute-start.9 = (bf16[192,512]{1,0:T(8,128)(2,1)S(1)}, bf16[192,512]{1,0:T(8,128)(2,1)S(1)}, u32[]{:S(2)}, u32[]{:S(2)}) collective-permute-start(bf16[192,512]{1,0:T(8,128)(2,1)S(1)} %get-tuple-element.38), channel_id=1, source_target_pairs={{0,4},{2,6},{4,8},{6,10},{8,12},{10,14},{12,0},{14,2},{1,5},{3,7},... | collective-permute-start | bytes 589832 | tf_op jit(solution)/shard_map/ppermute | solution.py:349
  10.7 2.6 %collective-permute-start.16 = (bf16[192,512]{1,0:T(8,128)(2,1)S(1)}, bf16[192,512]{1,0:T(8,128)(2,1)S(1)}, u32[]{:S(2)}, u32[]{:S(2)}) collective-permute-start(bf16[192,512]{1,0:T(8,128)(2,1)S(1)} %get-tuple-element.41), channel_id=1, source_target_pairs={{0,8},{2,10},{4,12},{6,14},{8,0},{10,2},{12,4},{14,6},{1,9},{3,11}... | collective-permute-start | bytes 589832 | tf_op jit(solution)/shard_map/ppermute | solution.py:349
  13.3 1.3 %collective-permute-start.23 = (bf16[192,512]{1,0:T(8,128)(2,1)S(1)}, bf16[192,512]{1,0:T(8,128)(2,1)S(1)}, u32[]{:S(2)}, u32[]{:S(2)}) collective-permute-start(bf16[192,512]{1,0:T(8,128)(2,1)S(1)} %get-tuple-element.44), channel_id=1, source_target_pairs={{0,12},{2,14},{4,0},{6,2},{8,4},{10,6},{12,8},{14,10},{1,13},{3,15... | collective-permute-start | bytes 589832 | tf_op jit(solution)/shard_map/ppermute | solution.py:349
  14.7 0.0 collective-permute-done.4.q_ref
  14.7 0.5 collective-permute-start.6
  15.2 3.7 %collective-permute-done.9.p_ref = bf16[192,512]{1,0:T(8,128)(2,1)S(1)} collective-permute-done((bf16[192,512]{1,0:T(8,128)(2,1)S(1)}, bf16[192,512]{1,0:T(8,128)(2,1)S(1)}, u32[]{:S(2)}, u32[]{:S(2)}) %collective-permute-start.9) | collective-permute-done | bytes 196640 | tf_op jit(solution)/shard_map/ppermute | solution.py:349
  18.8 0.3 collective-permute-start.10
  19.1 7.1 %collective-permute-done.16.p_ref = bf16[192,512]{1,0:T(8,128)(2,1)S(1)} collective-permute-done((bf16[192,512]{1,0:T(8,128)(2,1)S(1)}, bf16[192,512]{1,0:T(8,128)(2,1)S(1)}, u32[]{:S(2)}, u32[]{:S(2)}) %collective-permute-start.16) | collective-permute-done | bytes 196640 | tf_op jit(solution)/shard_map/ppermute | solution.py:349
  26.2 0.6 collective-permute-start.17
  26.8 1.5 %collective-permute-start.24 = (bf16[192,512]{1,0:T(8,128)(2,1)S(1)}, bf16[192,512]{1,0:T(8,128)(2,1)S(1)}, u32[]{:S(2)}, u32[]{:S(2)}) collective-permute-start(bf16[192,512]{1,0:T(8,128)(2,1)S(1)} %collective-permute-done.23.p_ref), channel_id=1, source_target_pairs={{0,2},{2,0},{4,6},{6,4},{8,10},{10,8},{12,14},{14,12},{1,3},{3,1},... | collective-permute-start | bytes 589832 | tf_op jit(solution)/shard_map/ppermute | solution.py:344
  28.2 4.3 %first_expert.1 = (f32[2,192,512]{2,1,0:T(8,128)S(1)}, bf16[2,192,512]{2,1,0:T(8,128)(2,1)S(1)}) custom-call(s32[1]{0:T(128)} %bitcast.core_ref, bf16[192,512]{1,0:T(8,128)(2,1)S(1)} %get-tuple-element.35.p_ref, bf16[192,512]{1,0:T(8,128)(2,1)S(1)} %collective-permute-done.4.q_ref, bf16[192,512]{1,0:T(8,128)(2,1)S(1)} %collective-permute-done.5.p2_ref, ...), custom_call_target="tpu_custom_call" | custom-call | tf_op jit(solution)/shard_map/first_expert/pallas_call | solution.py:25
  32.5 0.1 collective-permute-start.7
  32.6 0.0 collective-permute-done.10.q_ref
  32.6 0.5 collective-permute-start.12
  33.1 0.1 collective-permute-start.18
  33.2 0.8 %collective-permute-done.17.q_ref = bf16[192,512]{1,0:T(8,128)(2,1)S(1)} collective-permute-done((bf16[192,512]{1,0:T(8,128)(2,1)S(1)}, bf16[192,512]{1,0:T(8,128)(2,1)S(1)}, u32[]{:S(2)}, u32[]{:S(2)}) %collective-permute-start.17) | collective-permute-done | bytes 196640 | tf_op jit(solution)/shard_map/ppermute | solution.py:344
  34.0 3.2 %collective-permute-done.24.q_ref = bf16[192,512]{1,0:T(8,128)(2,1)S(1)} collective-permute-done((bf16[192,512]{1,0:T(8,128)(2,1)S(1)}, bf16[192,512]{1,0:T(8,128)(2,1)S(1)}, u32[]{:S(2)}, u32[]{:S(2)}) %collective-permute-start.24) | collective-permute-done | bytes 196640 | tf_op jit(solution)/shard_map/ppermute | solution.py:344
  37.1 0.0 collective-permute-start.26
  37.1 0.5 collective-permute-start.2
  37.7 0.0 collective-permute-done.18.p2_ref
  37.7 0.1 collective-permute-start.11
  37.7 0.4 collective-permute-start.25
  38.2 1.8 %expert.4 = (f32[2,192,512]{2,1,0:T(8,128)S(1)}, bf16[2,192,512]{2,1,0:T(8,128)(2,1)S(1)}) custom-call(s32[1]{0:T(128)} %bitcast.core_ref, bf16[192,512]{1,0:T(8,128)(2,1)S(1)} %collective-permute-done.16.p_ref, bf16[192,512]{1,0:T(8,128)(2,1)S(1)} %collective-permute-done.17.q_ref, bf16[192,512]{1,0:T(8,128)(2,1)S(1)} %collective-permute-done.18.p2_ref, ...), custom_call_target="tpu_custom_call" | custom-call | tf_op jit(solution)/shard_map/expert/pallas_call | solution.py:25
  40.0 0.0 collective-permute-done.26.value_ref
  40.0 0.1 collective-permute-start.20
  40.2 0.0 collective-permute-done.7
  40.2 0.1 convert_add_fusion.3
  40.3 0.6 collective-permute-start.8
  41.0 0.0 collective-permute-done.11.p2_ref
  41.0 1.8 %expert.3 = (f32[2,192,512]{2,1,0:T(8,128)S(1)}, bf16[2,192,512]{2,1,0:T(8,128)(2,1)S(1)}) custom-call(s32[1]{0:T(128)} %bitcast.core_ref, bf16[192,512]{1,0:T(8,128)(2,1)S(1)} %collective-permute-done.9.p_ref, bf16[192,512]{1,0:T(8,128)(2,1)S(1)} %collective-permute-done.10.q_ref, bf16[192,512]{1,0:T(8,128)(2,1)S(1)} %collective-permute-done.11.p2_ref, ...), custom_call_target="tpu_custom_call" | custom-call | tf_op jit(solution)/shard_map/expert/pallas_call | solution.py:25
  42.8 0.2 collective-permute-start.13
  43.0 0.0 collective-permute-done.20
  43.1 0.1 convert_add_fusion.1
  43.2 1.5 %collective-permute-start.21 = (bf16[192,512]{1,0:T(8,128)(2,1)S(1)}, bf16[192,512]{1,0:T(8,128)(2,1)S(1)}, u32[]{:S(2)}, u32[]{:S(2)}) collective-permute-start(bf16[192,512]{1,0:T(8,128)(2,1)S(1)} %fusion.10.first_ref), channel_id=1, source_target_pairs={{0,2},{2,0},{4,6},{6,4},{8,10},{10,8},{12,14},{14,12},{1,3},{3,1},... | collective-permute-start | bytes 589832 | tf_op jit(solution)/shard_map/ppermute | solution.py:344
  44.7 0.0 collective-permute-done.25.p2_ref
  44.7 1.8 %expert.5 = (f32[2,192,512]{2,1,0:T(8,128)S(1)}, bf16[2,192,512]{2,1,0:T(8,128)(2,1)S(1)}) custom-call(s32[1]{0:T(128)} %bitcast.core_ref, bf16[192,512]{1,0:T(8,128)(2,1)S(1)} %collective-permute-done.23.p_ref, bf16[192,512]{1,0:T(8,128)(2,1)S(1)} %collective-permute-done.24.q_ref, bf16[192,512]{1,0:T(8,128)(2,1)S(1)} %collective-permute-done.25.p2_ref, ...), custom_call_target="tpu_custom_call" | custom-call | tf_op jit(solution)/shard_map/expert/pallas_call | solution.py:25
  46.6 0.1 collective-permute-start.27
  46.7 0.1 convert_add_fusion.2
  46.9 0.6 collective-permute-start.14
  47.5 4.8 %collective-permute-done.21 = bf16[192,512]{1,0:T(8,128)(2,1)S(1)} collective-permute-done((bf16[192,512]{1,0:T(8,128)(2,1)S(1)}, bf16[192,512]{1,0:T(8,128)(2,1)S(1)}, u32[]{:S(2)}, u32[]{:S(2)}) %collective-permute-start.21) | collective-permute-done | bytes 196640 | tf_op jit(solution)/shard_map/ppermute | solution.py:344
  52.4 2.9 %collective-permute-start.22 = (bf16[192,512]{1,0:T(8,128)(2,1)S(1)}, bf16[192,512]{1,0:T(8,128)(2,1)S(1)}, u32[]{:S(2)}, u32[]{:S(2)}) collective-permute-start(bf16[192,512]{1,0:T(8,128)(2,1)S(1)} %fusion.3), channel_id=1, source_target_pairs={{0,8},{2,10},{4,12},{6,14},{8,0},{10,2},{12,4},{14,6},{1,9},{3,11}... | collective-permute-start | bytes 589832 | tf_op jit(solution)/shard_map/ppermute | solution.py:349
  55.2 0.0 collective-permute-done.27
  55.2 0.1 convert_add_fusion
  55.4 0.6 collective-permute-start.28
  56.0 0.1 collective-permute-done.14
  56.1 5.3 %collective-permute-start.15 = (bf16[192,512]{1,0:T(8,128)(2,1)S(1)}, bf16[192,512]{1,0:T(8,128)(2,1)S(1)}, u32[]{:S(2)}, u32[]{:S(2)}) collective-permute-start(bf16[192,512]{1,0:T(8,128)(2,1)S(1)} %fusion.5), channel_id=1, source_target_pairs={{0,12},{2,14},{4,0},{6,2},{8,4},{10,6},{12,8},{14,10},{1,13},{3,15... | collective-permute-start | bytes 589832 | tf_op jit(solution)/shard_map/ppermute | solution.py:349
  61.5 0.0 collective-permute-done.28
  61.5 2.3 %collective-permute-start.29 = (bf16[192,512]{1,0:T(8,128)(2,1)S(1)}, bf16[192,512]{1,0:T(8,128)(2,1)S(1)}, u32[]{:S(2)}, u32[]{:S(2)}) collective-permute-start(bf16[192,512]{1,0:T(8,128)(2,1)S(1)} %fusion.1), channel_id=1, source_target_pairs={{0,4},{2,6},{4,8},{6,10},{8,12},{10,14},{12,0},{14,2},{1,5},{3,7},... | collective-permute-start | bytes 589832 | tf_op jit(solution)/shard_map/ppermute | solution.py:349
  63.9 1.5 %collective-permute-done.22.rest_2_ = bf16[192,512]{1,0:T(8,128)(2,1)S(1)} collective-permute-done((bf16[192,512]{1,0:T(8,128)(2,1)S(1)}, bf16[192,512]{1,0:T(8,128)(2,1)S(1)}, u32[]{:S(2)}, u32[]{:S(2)}) %collective-permute-start.22) | collective-permute-done | bytes 196640 | tf_op jit(solution)/shard_map/ppermute | solution.py:349
  65.4 1.4 %collective-permute-done.15.rest_1_ = bf16[192,512]{1,0:T(8,128)(2,1)S(1)} collective-permute-done((bf16[192,512]{1,0:T(8,128)(2,1)S(1)}, bf16[192,512]{1,0:T(8,128)(2,1)S(1)}, u32[]{:S(2)}, u32[]{:S(2)}) %collective-permute-start.15) | collective-permute-done | bytes 196640 | tf_op jit(solution)/shard_map/ppermute | solution.py:349
  66.8 3.5 %collective-permute-done.29.rest_3_ = bf16[192,512]{1,0:T(8,128)(2,1)S(1)} collective-permute-done((bf16[192,512]{1,0:T(8,128)(2,1)S(1)}, bf16[192,512]{1,0:T(8,128)(2,1)S(1)}, u32[]{:S(2)}, u32[]{:S(2)}) %collective-permute-start.29) | collective-permute-done | bytes 196640 | tf_op jit(solution)/shard_map/ppermute | solution.py:349
  70.3 0.9 %combine.1 = (f32[128,512]{1,0:T(8,128)S(1)}, bf16[128,512]{1,0:T(8,128)(2,1)S(1)}) custom-call(s32[1]{0:T(128)} %bitcast.core_ref, s32[1]{0:T(128)} %bitcast.5.line_ref, s32[2,2,128]{2,1,0:T(2,128)S(1)} %get-tuple-element.31.routes_ref, f32[2,128]{1,0:T(2,128)S(1)} %get-tuple-element.32.own_gates_ref, f32[2,128]{1,0:T(2,128)S(1)} %collective-permute-done.2.other_gates_ref, ...), custom_call_target="tpu_custom_call" | custom-call | tf_op jit(solution)/shard_map/combine/pallas_call | solution.py:25
  71.2 0.1 collective-permute-start.30
  71.3 1.3 %collective-permute-done.30.other_ref = bf16[128,512]{1,0:T(8,128)(2,1)S(1)} collective-permute-done((bf16[128,512]{1,0:T(8,128)(2,1)S(1)}, bf16[128,512]{1,0:T(8,128)(2,1)S(1)}, u32[]{:S(2)}, u32[]{:S(2)}) %collective-permute-start.30) | collective-permute-done | bytes 131104 | tf_op jit(solution)/shard_map/ppermute | solution.py:339
  72.7 0.8 %finish.1 = bf16[128,1024]{1,0:T(8,128)(2,1)} custom-call(s32[1]{0:T(128)} %bitcast.core_ref, bf16[128,1024]{1,0:T(8,128)(2,1)S(1)} %get-tuple-element.30.state_ref, f32[128,512]{1,0:T(8,128)S(1)} %get-tuple-element.47.own_ref, bf16[128,512]{1,0:T(8,128)(2,1)S(1)} %collective-permute-done.30.other_ref), custom_call_target="tpu_custom_call" | custom-call | tf_op jit(solution)/shard_map/finish/pallas_call | solution.py:25
  (27 shorter events, 0.3 us)
Async XLA Ops:
  0.0 2.9 %collective-permute-start = (bf16[2,80,512]{2,1,0:T(8,128)(2,1)}, bf16[2,80,512]{2,1,0:T(8,128)(2,1)S(1)}, u32[]{:S(2)}, u32[]{:S(2)}) collective-permute-start(bf16[2,80,512]{2,1,0:T(8,128)(2,1)} %keys_in.1), channel_id=1, source_target_pairs={{0,1},{1,0},{2,3},{3,2},{4,5},{5,4},{6,7},{7,6},{8,9},{9,8},{10,11... | collective-permute-start | bytes 491528 | tf_op jit(solution)/shard_map/ppermute | solution.py:339
  0.5 2.5 %collective-permute-start.1 = (bf16[2,80,512]{2,1,0:T(8,128)(2,1)}, bf16[2,80,512]{2,1,0:T(8,128)(2,1)S(1)}, u32[]{:S(2)}, u32[]{:S(2)}) collective-permute-start(bf16[2,80,512]{2,1,0:T(8,128)(2,1)} %values_in.1), channel_id=1, source_target_pairs={{0,1},{1,0},{2,3},{3,2},{4,5},{5,4},{6,7},{7,6},{8,9},{9,8},{10,11... | collective-permute-start | bytes 491528 | tf_op jit(solution)/shard_map/ppermute | solution.py:339
  4.2 1.5 %collective-permute-start.3 = (bf16[128,512]{1,0:T(8,128)(2,1)S(1)}, bf16[128,512]{1,0:T(8,128)(2,1)S(1)}, u32[]{:S(2)}, u32[]{:S(2)}) collective-permute-start(bf16[128,512]{1,0:T(8,128)(2,1)S(1)} %get-tuple-element.34), channel_id=1, source_target_pairs={{0,1},{1,0},{2,3},{3,2},{4,5},{5,4},{6,7},{7,6},{8,9},{9,8},{10,11... | collective-permute-start | bytes 393224 | tf_op jit(solution)/shard_map/ppermute | solution.py:339
  6.2 8.4 %collective-permute-start.4 = (bf16[192,512]{1,0:T(8,128)(2,1)S(1)}, bf16[192,512]{1,0:T(8,128)(2,1)S(1)}, u32[]{:S(2)}, u32[]{:S(2)}) collective-permute-start(bf16[192,512]{1,0:T(8,128)(2,1)S(1)} %get-tuple-element.35.p_ref), channel_id=1, source_target_pairs={{0,2},{2,0},{4,6},{6,4},{8,10},{10,8},{12,14},{14,12},{1,3},{3,1},... | collective-permute-start | bytes 589832 | tf_op jit(solution)/shard_map/ppermute | solution.py:344
  9.2 9.7 %collective-permute-start.9 = (bf16[192,512]{1,0:T(8,128)(2,1)S(1)}, bf16[192,512]{1,0:T(8,128)(2,1)S(1)}, u32[]{:S(2)}, u32[]{:S(2)}) collective-permute-start(bf16[192,512]{1,0:T(8,128)(2,1)S(1)} %get-tuple-element.38), channel_id=1, source_target_pairs={{0,4},{2,6},{4,8},{6,10},{8,12},{10,14},{12,0},{14,2},{1,5},{3,7},... | collective-permute-start | bytes 589832 | tf_op jit(solution)/shard_map/ppermute | solution.py:349
  10.7 15.5 %collective-permute-start.16 = (bf16[192,512]{1,0:T(8,128)(2,1)S(1)}, bf16[192,512]{1,0:T(8,128)(2,1)S(1)}, u32[]{:S(2)}, u32[]{:S(2)}) collective-permute-start(bf16[192,512]{1,0:T(8,128)(2,1)S(1)} %get-tuple-element.41), channel_id=1, source_target_pairs={{0,8},{2,10},{4,12},{6,14},{8,0},{10,2},{12,4},{14,6},{1,9},{3,11}... | collective-permute-start | bytes 589832 | tf_op jit(solution)/shard_map/ppermute | solution.py:349
  13.3 24.9 %copy-start = (bf16[1024,1024]{1,0:T(8,128)(2,1)S(1)}, bf16[1024,1024]{1,0:T(8,128)(2,1)}, u32[]{:S(2)}) copy-start(bf16[1024,1024]{1,0:T(8,128)(2,1)} %in_ref.5) | copy-start | bytes 6291460
  13.3 24.9 %copy-start.1 = (bf16[1024,1024]{1,0:T(8,128)(2,1)S(1)}, bf16[1024,1024]{1,0:T(8,128)(2,1)}, u32[]{:S(2)}) copy-start(bf16[1024,1024]{1,0:T(8,128)(2,1)} %out_ref.5) | copy-start | bytes 6291460
  13.3 13.5 %collective-permute-start.23 = (bf16[192,512]{1,0:T(8,128)(2,1)S(1)}, bf16[192,512]{1,0:T(8,128)(2,1)S(1)}, u32[]{:S(2)}, u32[]{:S(2)}) collective-permute-start(bf16[192,512]{1,0:T(8,128)(2,1)S(1)} %get-tuple-element.44), channel_id=1, source_target_pairs={{0,12},{2,14},{4,0},{6,2},{8,4},{10,6},{12,8},{14,10},{1,13},{3,15... | collective-permute-start | bytes 589832 | tf_op jit(solution)/shard_map/ppermute | solution.py:349
  14.7 13.6 %collective-permute-start.5 = (bf16[192,512]{1,0:T(8,128)(2,1)S(1)}, bf16[192,512]{1,0:T(8,128)(2,1)S(1)}, u32[]{:S(2)}, u32[]{:S(2)}) collective-permute-start(bf16[192,512]{1,0:T(8,128)(2,1)S(1)} %get-tuple-element.35.p_ref), channel_id=1, source_target_pairs={{0,1},{1,0},{2,3},{3,2},{4,5},{5,4},{6,7},{7,6},{8,9},{9,8},{10,11... | collective-permute-start | bytes 589832 | tf_op jit(solution)/shard_map/ppermute | solution.py:339
  14.7 13.6 %collective-permute-start.6 = (bf16[192,512]{1,0:T(8,128)(2,1)S(1)}, bf16[192,512]{1,0:T(8,128)(2,1)S(1)}, u32[]{:S(2)}, u32[]{:S(2)}) collective-permute-start(bf16[192,512]{1,0:T(8,128)(2,1)S(1)} %collective-permute-done.4.q_ref), channel_id=1, source_target_pairs={{0,1},{1,0},{2,3},{3,2},{4,5},{5,4},{6,7},{7,6},{8,9},{9,8},{10,11... | collective-permute-start | bytes 589832 | tf_op jit(solution)/shard_map/ppermute | solution.py:339
  18.8 13.8 %collective-permute-start.10 = (bf16[192,512]{1,0:T(8,128)(2,1)S(1)}, bf16[192,512]{1,0:T(8,128)(2,1)S(1)}, u32[]{:S(2)}, u32[]{:S(2)}) collective-permute-start(bf16[192,512]{1,0:T(8,128)(2,1)S(1)} %collective-permute-done.9.p_ref), channel_id=1, source_target_pairs={{0,2},{2,0},{4,6},{6,4},{8,10},{10,8},{12,14},{14,12},{1,3},{3,1},... | collective-permute-start | bytes 589832 | tf_op jit(solution)/shard_map/ppermute | solution.py:344
  26.2 7.8 %collective-permute-start.17 = (bf16[192,512]{1,0:T(8,128)(2,1)S(1)}, bf16[192,512]{1,0:T(8,128)(2,1)S(1)}, u32[]{:S(2)}, u32[]{:S(2)}) collective-permute-start(bf16[192,512]{1,0:T(8,128)(2,1)S(1)} %collective-permute-done.16.p_ref), channel_id=1, source_target_pairs={{0,2},{2,0},{4,6},{6,4},{8,10},{10,8},{12,14},{14,12},{1,3},{3,1},... | collective-permute-start | bytes 589832 | tf_op jit(solution)/shard_map/ppermute | solution.py:344
  26.8 10.4 %collective-permute-start.24 = (bf16[192,512]{1,0:T(8,128)(2,1)S(1)}, bf16[192,512]{1,0:T(8,128)(2,1)S(1)}, u32[]{:S(2)}, u32[]{:S(2)}) collective-permute-start(bf16[192,512]{1,0:T(8,128)(2,1)S(1)} %collective-permute-done.23.p_ref), channel_id=1, source_target_pairs={{0,2},{2,0},{4,6},{6,4},{8,10},{10,8},{12,14},{14,12},{1,3},{3,1},... | collective-permute-start | bytes 589832 | tf_op jit(solution)/shard_map/ppermute | solution.py:344
  32.5 7.6 %collective-permute-start.7 = (bf16[2,192,512]{2,1,0:T(8,128)(2,1)S(1)}, bf16[2,192,512]{2,1,0:T(8,128)(2,1)S(1)}, u32[]{:S(2)}, u32[]{:S(2)}) collective-permute-start(bf16[2,192,512]{2,1,0:T(8,128)(2,1)S(1)} %get-tuple-element.37), channel_id=1, source_target_pairs={{0,1},{1,0},{2,3},{3,2},{4,5},{5,4},{6,7},{7,6},{8,9},{9,8},{10,11... | collective-permute-start | bytes 1179656 | tf_op jit(solution)/shard_map/ppermute | solution.py:339
  32.6 4.5 %collective-permute-start.12 = (bf16[192,512]{1,0:T(8,128)(2,1)S(1)}, bf16[192,512]{1,0:T(8,128)(2,1)S(1)}, u32[]{:S(2)}, u32[]{:S(2)}) collective-permute-start(bf16[192,512]{1,0:T(8,128)(2,1)S(1)} %collective-permute-done.10.q_ref), channel_id=1, source_target_pairs={{0,1},{1,0},{2,3},{3,2},{4,5},{5,4},{6,7},{7,6},{8,9},{9,8},{10,11... | collective-permute-start | bytes 589832 | tf_op jit(solution)/shard_map/ppermute | solution.py:339
  33.1 4.5 %collective-permute-start.18 = (bf16[192,512]{1,0:T(8,128)(2,1)S(1)}, bf16[192,512]{1,0:T(8,128)(2,1)S(1)}, u32[]{:S(2)}, u32[]{:S(2)}) collective-permute-start(bf16[192,512]{1,0:T(8,128)(2,1)S(1)} %collective-permute-done.16.p_ref), channel_id=1, source_target_pairs={{0,1},{1,0},{2,3},{3,2},{4,5},{5,4},{6,7},{7,6},{8,9},{9,8},{10,11... | collective-permute-start | bytes 589832 | tf_op jit(solution)/shard_map/ppermute | solution.py:339
  34.0 3.8 %collective-permute-start.19 = (bf16[192,512]{1,0:T(8,128)(2,1)S(1)}, bf16[192,512]{1,0:T(8,128)(2,1)S(1)}, u32[]{:S(2)}, u32[]{:S(2)}) collective-permute-start(bf16[192,512]{1,0:T(8,128)(2,1)S(1)} %collective-permute-done.17.q_ref), channel_id=1, source_target_pairs={{0,1},{1,0},{2,3},{3,2},{4,5},{5,4},{6,7},{7,6},{8,9},{9,8},{10,11... | collective-permute-start | bytes 589832 | tf_op jit(solution)/shard_map/ppermute | solution.py:339
  37.1 2.9 %collective-permute-start.26 = (bf16[192,512]{1,0:T(8,128)(2,1)S(1)}, bf16[192,512]{1,0:T(8,128)(2,1)S(1)}, u32[]{:S(2)}, u32[]{:S(2)}) collective-permute-start(bf16[192,512]{1,0:T(8,128)(2,1)S(1)} %collective-permute-done.24.q_ref), channel_id=1, source_target_pairs={{0,1},{1,0},{2,3},{3,2},{4,5},{5,4},{6,7},{7,6},{8,9},{9,8},{10,11... | collective-permute-start | bytes 589832 | tf_op jit(solution)/shard_map/ppermute | solution.py:339
  37.1 26.8 %collective-permute-start.2 = (f32[2,128]{1,0:T(2,128)S(1)}, f32[2,128]{1,0:T(2,128)S(1)}, u32[]{:S(2)}, u32[]{:S(2)}) collective-permute-start(f32[2,128]{1,0:T(2,128)S(1)} %get-tuple-element.32.own_gates_ref), channel_id=1, source_target_pairs={{0,1},{1,0},{2,3},{3,2},{4,5},{5,4},{6,7},{7,6},{8,9},{9,8},{10,11... | collective-permute-start | bytes 3080 | tf_op jit(solution)/shard_map/ppermute | solution.py:339
  37.7 3.3 %collective-permute-start.11 = (bf16[192,512]{1,0:T(8,128)(2,1)S(1)}, bf16[192,512]{1,0:T(8,128)(2,1)S(1)}, u32[]{:S(2)}, u32[]{:S(2)}) collective-permute-start(bf16[192,512]{1,0:T(8,128)(2,1)S(1)} %collective-permute-done.9.p_ref), channel_id=1, source_target_pairs={{0,1},{1,0},{2,3},{3,2},{4,5},{5,4},{6,7},{7,6},{8,9},{9,8},{10,11... | collective-permute-start | bytes 589832 | tf_op jit(solution)/shard_map/ppermute | solution.py:339
  37.7 7.0 %collective-permute-start.25 = (bf16[192,512]{1,0:T(8,128)(2,1)S(1)}, bf16[192,512]{1,0:T(8,128)(2,1)S(1)}, u32[]{:S(2)}, u32[]{:S(2)}) collective-permute-start(bf16[192,512]{1,0:T(8,128)(2,1)S(1)} %collective-permute-done.23.p_ref), channel_id=1, source_target_pairs={{0,1},{1,0},{2,3},{3,2},{4,5},{5,4},{6,7},{7,6},{8,9},{9,8},{10,11... | collective-permute-start | bytes 589832 | tf_op jit(solution)/shard_map/ppermute | solution.py:339
  40.0 3.0 %collective-permute-start.20 = (bf16[2,192,512]{2,1,0:T(8,128)(2,1)S(1)}, bf16[2,192,512]{2,1,0:T(8,128)(2,1)S(1)}, u32[]{:S(2)}, u32[]{:S(2)}) collective-permute-start(bf16[2,192,512]{2,1,0:T(8,128)(2,1)S(1)} %get-tuple-element.43), channel_id=1, source_target_pairs={{0,1},{1,0},{2,3},{3,2},{4,5},{5,4},{6,7},{7,6},{8,9},{9,8},{10,11... | collective-permute-start | bytes 1179656 | tf_op jit(solution)/shard_map/ppermute | solution.py:339
  40.3 23.5 %collective-permute-start.8 = (bf16[192,512]{1,0:T(8,128)(2,1)S(1)}, bf16[192,512]{1,0:T(8,128)(2,1)S(1)}, u32[]{:S(2)}, u32[]{:S(2)}) collective-permute-start(bf16[192,512]{1,0:T(8,128)(2,1)S(1)} %fusion.8.first_ref), channel_id=1, source_target_pairs={{0,2},{2,0},{4,6},{6,4},{8,10},{10,8},{12,14},{14,12},{1,3},{3,1},... | collective-permute-start | bytes 589832 | tf_op jit(solution)/shard_map/ppermute | solution.py:344
  42.8 3.9 %collective-permute-start.13 = (bf16[2,192,512]{2,1,0:T(8,128)(2,1)S(1)}, bf16[2,192,512]{2,1,0:T(8,128)(2,1)S(1)}, u32[]{:S(2)}, u32[]{:S(2)}) collective-permute-start(bf16[2,192,512]{2,1,0:T(8,128)(2,1)S(1)} %get-tuple-element.40), channel_id=1, source_target_pairs={{0,1},{1,0},{2,3},{3,2},{4,5},{5,4},{6,7},{7,6},{8,9},{9,8},{10,11... | collective-permute-start | bytes 1179656 | tf_op jit(solution)/shard_map/ppermute | solution.py:339
  43.2 9.1 %collective-permute-start.21 = (bf16[192,512]{1,0:T(8,128)(2,1)S(1)}, bf16[192,512]{1,0:T(8,128)(2,1)S(1)}, u32[]{:S(2)}, u32[]{:S(2)}) collective-permute-start(bf16[192,512]{1,0:T(8,128)(2,1)S(1)} %fusion.10.first_ref), channel_id=1, source_target_pairs={{0,2},{2,0},{4,6},{6,4},{8,10},{10,8},{12,14},{14,12},{1,3},{3,1},... | collective-permute-start | bytes 589832 | tf_op jit(solution)/shard_map/ppermute | solution.py:344
  46.6 8.6 %collective-permute-start.27 = (bf16[2,192,512]{2,1,0:T(8,128)(2,1)S(1)}, bf16[2,192,512]{2,1,0:T(8,128)(2,1)S(1)}, u32[]{:S(2)}, u32[]{:S(2)}) collective-permute-start(bf16[2,192,512]{2,1,0:T(8,128)(2,1)S(1)} %get-tuple-element.46), channel_id=1, source_target_pairs={{0,1},{1,0},{2,3},{3,2},{4,5},{5,4},{6,7},{7,6},{8,9},{9,8},{10,11... | collective-permute-start | bytes 1179656 | tf_op jit(solution)/shard_map/ppermute | solution.py:339
  46.9 9.2 %collective-permute-start.14 = (bf16[192,512]{1,0:T(8,128)(2,1)S(1)}, bf16[192,512]{1,0:T(8,128)(2,1)S(1)}, u32[]{:S(2)}, u32[]{:S(2)}) collective-permute-start(bf16[192,512]{1,0:T(8,128)(2,1)S(1)} %fusion.9), channel_id=1, source_target_pairs={{0,2},{2,0},{4,6},{6,4},{8,10},{10,8},{12,14},{14,12},{1,3},{3,1},... | collective-permute-start | bytes 589832 | tf_op jit(solution)/shard_map/ppermute | solution.py:344
  52.4 13.0 %collective-permute-start.22 = (bf16[192,512]{1,0:T(8,128)(2,1)S(1)}, bf16[192,512]{1,0:T(8,128)(2,1)S(1)}, u32[]{:S(2)}, u32[]{:S(2)}) collective-permute-start(bf16[192,512]{1,0:T(8,128)(2,1)S(1)} %fusion.3), channel_id=1, source_target_pairs={{0,8},{2,10},{4,12},{6,14},{8,0},{10,2},{12,4},{14,6},{1,9},{3,11}... | collective-permute-start | bytes 589832 | tf_op jit(solution)/shard_map/ppermute | solution.py:349
  55.4 6.1 %collective-permute-start.28 = (bf16[192,512]{1,0:T(8,128)(2,1)S(1)}, bf16[192,512]{1,0:T(8,128)(2,1)S(1)}, u32[]{:S(2)}, u32[]{:S(2)}) collective-permute-start(bf16[192,512]{1,0:T(8,128)(2,1)S(1)} %fusion.11), channel_id=1, source_target_pairs={{0,2},{2,0},{4,6},{6,4},{8,10},{10,8},{12,14},{14,12},{1,3},{3,1},... | collective-permute-start | bytes 589832 | tf_op jit(solution)/shard_map/ppermute | solution.py:344
  56.1 10.7 %collective-permute-start.15 = (bf16[192,512]{1,0:T(8,128)(2,1)S(1)}, bf16[192,512]{1,0:T(8,128)(2,1)S(1)}, u32[]{:S(2)}, u32[]{:S(2)}) collective-permute-start(bf16[192,512]{1,0:T(8,128)(2,1)S(1)} %fusion.5), channel_id=1, source_target_pairs={{0,12},{2,14},{4,0},{6,2},{8,4},{10,6},{12,8},{14,10},{1,13},{3,15... | collective-permute-start | bytes 589832 | tf_op jit(solution)/shard_map/ppermute | solution.py:349
  61.5 8.8 %collective-permute-start.29 = (bf16[192,512]{1,0:T(8,128)(2,1)S(1)}, bf16[192,512]{1,0:T(8,128)(2,1)S(1)}, u32[]{:S(2)}, u32[]{:S(2)}) collective-permute-start(bf16[192,512]{1,0:T(8,128)(2,1)S(1)} %fusion.1), channel_id=1, source_target_pairs={{0,4},{2,6},{4,8},{6,10},{8,12},{10,14},{12,0},{14,2},{1,5},{3,7},... | collective-permute-start | bytes 589832 | tf_op jit(solution)/shard_map/ppermute | solution.py:349
  71.2 1.4 %collective-permute-start.30 = (bf16[128,512]{1,0:T(8,128)(2,1)S(1)}, bf16[128,512]{1,0:T(8,128)(2,1)S(1)}, u32[]{:S(2)}, u32[]{:S(2)}) collective-permute-start(bf16[128,512]{1,0:T(8,128)(2,1)S(1)} %get-tuple-element.48), channel_id=1, source_target_pairs={{0,1},{1,0},{2,3},{3,2},{4,5},{5,4},{6,7},{7,6},{8,9},{9,8},{10,11... | collective-permute-start | bytes 393224 | tf_op jit(solution)/shard_map/ppermute | solution.py:339

commit v10 on v9

--- a/solution.py
+++ b/solution.py
@@ -351,25 +351,20 @@
     )
 
 
-def after_kernel(value_ref, first_ref, out_ref):
+def after_kernel(*refs):
     pass
 
 
-def after(value, first):
-    anywhere = pl.BlockSpec(memory_space=pl.ANY)
+def after(value, *firsts):
     return pl.pallas_call(
         after_kernel,
         out_shape=jax.ShapeDtypeStruct(value.shape, value.dtype),
-        in_specs=[anywhere, anywhere],
-        out_specs=anywhere,
+        in_specs=[pl.BlockSpec(memory_space=pl.ANY)] * (1 + len(firsts)),
+        out_specs=pl.BlockSpec(memory_space=pl.ANY),
         input_output_aliases={0: 0},
         compiler_params=pltpu.CompilerParams(vmem_limit_bytes=2**20),
         name="after",
-    )(value, first)
-
-
-def piece_order(count):
-    return sorted(range(count), key=lambda offset: (offset > 0, -min(offset, count - offset)))
+    )(value, *firsts)
 
 
 def attend(
@@ -437,21 +432,22 @@
     )
     travelling = [shift(selected[r], r) for r in range(1, count)]
     home = [None] * count
-    home = [None] * count
-    kepts, halves, wholes = [], [], []
-    for at, offset in enumerate(piece_order(count)):
+    kept, halves, wholes, ps, qs, q2s = {}, {}, {}, {}, {}, {}
+    order = [0, 1, 2, 3]
+    for offset in order:
         p = travelling[offset - 1] if offset else selected[0]
+        if offset == 2:
+            p = after(p, kept[0])
         q = swap_owner(p)
         p2 = swap(p)
         q2 = swap(q)
-        if at >= 2:
-            q2 = after(q2, kepts[at - 2])
-        if at >= 2:
-            q2 = after(q2, halves[at - 2])
+        if offset == 3:
+            q2 = after(q2, halves[1])
+        ps[offset], qs[offset], q2s[offset] = p, q, q2
         outs = [((2, capacity, half), jnp.float32), ((2, capacity, half), jnp.bfloat16)]
         rows = pltpu.VMEM((2 * capacity, width), jnp.bfloat16)
-        if at == 0:
-            kept, sent = call(
+        if offset == order[0]:
+            kept[offset], sent = call(
                 first_expert_kernel,
                 "first_expert",
                 outs,
@@ -468,7 +464,7 @@
                 vmem_mib=20,
             )
         else:
-            kept, sent = call(
+            kept[offset], sent = call(
                 expert_kernel,
                 "expert",
                 outs,
@@ -477,12 +473,17 @@
                 scratch=[rows],
                 vmem_mib=16,
             )
-        kepts.append(kept)
-        both = kept + swap(sent).astype(jnp.float32)
-        halves.append(both[1].astype(jnp.bfloat16))
-        across = swap_owner(halves[-1])
-        wholes.append((both[0] + across.astype(jnp.float32)).astype(jnp.bfloat16))
-        home[offset] = shift(wholes[-1], -offset) if offset else wholes[-1]
+        moving = swap(sent)
+        both = kept[offset] + moving.astype(jnp.float32)
+        halves[offset] = both[1].astype(jnp.bfloat16)
+        if offset == 0:
+            own_both = both
+            continue
+        across = swap_owner(halves[offset])
+        wholes[offset] = (both[0] + across.astype(jnp.float32)).astype(jnp.bfloat16)
+        home[offset] = shift(wholes[offset], -offset)
+    across = swap_owner(after(halves[0], halves[order[-1]]))
+    home[0] = (own_both[0] + across.astype(jnp.float32)).astype(jnp.bfloat16)
     own_sum, other_sum = call(
         combine_kernel,
         "combine",

time: 74.4 us -> 76.1 us (1.023)
  waiting for transfers between devices: 28.3 us -> 31 us
    ppermute x8, waiting for transfers between devices: 8.83 us -> 19.3 us  [swap_owner(): return lax.ppermute(values, 'expert', [(i, i ^ 1) for i in range(owners)])]
    ppermute x6, waiting for transfers between devices: 17.1 us -> 9.29 us  [shift(): lax.ppermute(values, 'expert', [(i, (i + 2 * offset) % owners) for i in r...]
    ppermute x8, starting transfers between devices: 8.65 us -> 11.1 us  [swap_owner(): return lax.ppermute(values, 'expert', [(i, i ^ 1) for i in range(owners)])]
    ppermute x6, starting transfers between devices: 16.1 us -> 13.8 us  [shift(): lax.ppermute(values, 'expert', [(i, (i + 2 * offset) % owners) for i in r...]
  transfers between devices with their start and end apart: 31 -> 31, of which waited for: 11 -> 10; matrix products, arithmetic and copies ran while one was open for 1% -> 1% of each run, Pallas kernels for 16% -> 15%
where the time goes in v10:
time: 76.1 us; the launch traced here: 75.9 us
  waiting for transfers between devices  31 us (41%)
  starting transfers between devices  28.2 us (37%)
  Pallas kernels  15 us (20%)
  between operations  0.92 us (1%)
    ppermute x8, waiting for transfers between devices, swap_owner(): return lax.ppermute(values, 'expert', [(i, i ^ 1) for i in range(owners)])  19.3 us
    pallas_call x9, Pallas kernels, call(): pl.pallas_call(kernel, out_shape=tuple((jax.ShapeDtypeStruct(*out) for ou...  15 us
    ppermute x6, starting transfers between devices, shift(): lax.ppermute(values, 'expert', [(i, (i + 2 * offset) % owners) for i in r...  13.8 us
    ppermute x8, starting transfers between devices, swap_owner(): return lax.ppermute(values, 'expert', [(i, i ^ 1) for i in range(owners)])  11.1 us
    ppermute x6, waiting for transfers between devices, shift(): lax.ppermute(values, 'expert', [(i, (i + 2 * offset) % owners) for i in r...  9.29 us
    ppermute x17, starting transfers between devices, swap(): return lax.ppermute(values, 'section', [(0, 1), (1, 0)])  3.29 us
    ppermute x17, waiting for transfers between devices, swap(): return lax.ppermute(values, 'section', [(0, 1), (1, 0)])  2.36 us
  transfers between devices with their start and end apart: 31, of which 10 were waited for; matrix products, arithmetic and copies ran while one was open for 1% of the time, Pallas kernels for 15%

profile of v10, /device:TPU:0, one launch (start us, length us, event | category | flops | bytes accessed | tf_op | source)
XLA Modules:
  0.0 75.9 jit_solution(1601007000617281463)
XLA Ops:
  0.0 0.5 collective-permute-start
  0.5 0.1 collective-permute-start.1
  1.2 1.8 %attend_own.1 = (bf16[128,512]{1,0:T(8,128)(2,1)S(1)}, bf16[128,512]{1,0:T(8,128)(2,1)S(1)}, bf16[128,512]{1,0:T(8,128)(2,1)S(1)}) custom-call(s32[1]{0:T(128)} %bitcast.core_ref, s32[1]{0:T(128)S(6)} %copy.18.source_ref, bf16[1,128,1024]{2,1,0:T(8,128)(2,1)} %x_in.1, f32[1,1024]{1,0:T(1,128)} %bitcast.40, bf16[2,80,512]{2,1,0:T(8,128)(2,1)} %keys_in.1, ...), custom_call_target="tpu_custom_call" | custom-call | tf_op jit(solution)/shard_map/attend_own/pallas_call | solution.py:25
  2.9 0.0 collective-permute-done.keys_ref
  2.9 0.0 collective-permute-done.1.values_ref
  3.0 1.2 %attend_other.1 = (bf16[128,1024]{1,0:T(8,128)(2,1)S(1)}, bf16[128,512]{1,0:T(8,128)(2,1)S(1)}, bf16[128,512]{1,0:T(8,128)(2,1)S(1)}, f32[2,128]{1,0:T(2,128)S(1)}, s32[2,2,128]{2,1,0:T(2,128)S(1)}) custom-call(s32[1]{0:T(128)} %bitcast.core_ref, s32[1]{0:T(128)S(6)} %copy.18.source_ref, bf16[128,512]{1,0:T(8,128)(2,1)S(1)} %get-tuple-element.27.own_ref, ...), custom_call_target="tpu_custom_call" | custom-call | tf_op jit(solution)/shard_map/attend_other/pallas_call | solution.py:25
  4.2 0.5 collective-permute-start.3
  4.7 1.0 %collective-permute-done.3.other_ref = bf16[128,512]{1,0:T(8,128)(2,1)S(1)} collective-permute-done((bf16[128,512]{1,0:T(8,128)(2,1)S(1)}, bf16[128,512]{1,0:T(8,128)(2,1)S(1)}, u32[]{:S(2)}, u32[]{:S(2)}) %collective-permute-start.3) | collective-permute-done | bytes 131104 | tf_op jit(solution)/shard_map/ppermute | solution.py:339
  5.7 0.5 select.5
  6.2 2.9 %collective-permute-start.4 = (bf16[192,512]{1,0:T(8,128)(2,1)S(1)}, bf16[192,512]{1,0:T(8,128)(2,1)S(1)}, u32[]{:S(2)}, u32[]{:S(2)}) collective-permute-start(bf16[192,512]{1,0:T(8,128)(2,1)S(1)} %get-tuple-element.35.p_ref), channel_id=1, source_target_pairs={{0,2},{2,0},{4,6},{6,4},{8,10},{10,8},{12,14},{14,12},{1,3},{3,1},... | collective-permute-start | bytes 589832 | tf_op jit(solution)/shard_map/ppermute | solution.py:344
  9.2 1.6 %collective-permute-start.12 = (bf16[192,512]{1,0:T(8,128)(2,1)S(1)}, bf16[192,512]{1,0:T(8,128)(2,1)S(1)}, u32[]{:S(2)}, u32[]{:S(2)}) collective-permute-start(bf16[192,512]{1,0:T(8,128)(2,1)S(1)} %get-tuple-element.39), channel_id=1, source_target_pairs={{0,4},{2,6},{4,8},{6,10},{8,12},{10,14},{12,0},{14,2},{1,5},{3,7},... | collective-permute-start | bytes 589832 | tf_op jit(solution)/shard_map/ppermute | solution.py:349
  10.7 0.0 collective-permute-start.5
  10.7 3.6 %collective-permute-done.4.q_ref = bf16[192,512]{1,0:T(8,128)(2,1)S(1)} collective-permute-done((bf16[192,512]{1,0:T(8,128)(2,1)S(1)}, bf16[192,512]{1,0:T(8,128)(2,1)S(1)}, u32[]{:S(2)}, u32[]{:S(2)}) %collective-permute-start.4) | collective-permute-done | bytes 196640 | tf_op jit(solution)/shard_map/ppermute | solution.py:344
  14.4 0.0 collective-permute-start.6
  14.4 2.8 %collective-permute-start.21 = (bf16[192,512]{1,0:T(8,128)(2,1)S(1)}, bf16[192,512]{1,0:T(8,128)(2,1)S(1)}, u32[]{:S(2)}, u32[]{:S(2)}) collective-permute-start(bf16[192,512]{1,0:T(8,128)(2,1)S(1)} %get-tuple-element.44), channel_id=1, source_target_pairs={{0,8},{2,10},{4,12},{6,14},{8,0},{10,2},{12,4},{14,6},{1,9},{3,11}... | collective-permute-start | bytes 589832 | tf_op jit(solution)/shard_map/ppermute | solution.py:349
  17.2 1.3 %collective-permute-start.8 = (bf16[192,512]{1,0:T(8,128)(2,1)S(1)}, bf16[192,512]{1,0:T(8,128)(2,1)S(1)}, u32[]{:S(2)}, u32[]{:S(2)}) collective-permute-start(bf16[192,512]{1,0:T(8,128)(2,1)S(1)} %get-tuple-element.38), channel_id=1, source_target_pairs={{0,12},{2,14},{4,0},{6,2},{8,4},{10,6},{12,8},{14,10},{1,13},{3,15... | collective-permute-start | bytes 589832 | tf_op jit(solution)/shard_map/ppermute | solution.py:349
  18.6 0.0 collective-permute-done.12.p_ref
  18.6 1.5 %collective-permute-start.13 = (bf16[192,512]{1,0:T(8,128)(2,1)S(1)}, bf16[192,512]{1,0:T(8,128)(2,1)S(1)}, u32[]{:S(2)}, u32[]{:S(2)}) collective-permute-start(bf16[192,512]{1,0:T(8,128)(2,1)S(1)} %collective-permute-done.12.p_ref), channel_id=1, source_target_pairs={{0,2},{2,0},{4,6},{6,4},{8,10},{10,8},{12,14},{14,12},{1,3},{3,1},... | collective-permute-start | bytes 589832 | tf_op jit(solution)/shard_map/ppermute | solution.py:344
  20.1 4.3 %first_expert.1 = (f32[2,192,512]{2,1,0:T(8,128)S(1)}, bf16[2,192,512]{2,1,0:T(8,128)(2,1)S(1)}) custom-call(s32[1]{0:T(128)} %bitcast.core_ref, bf16[192,512]{1,0:T(8,128)(2,1)S(1)} %get-tuple-element.35.p_ref, bf16[192,512]{1,0:T(8,128)(2,1)S(1)} %collective-permute-done.4.q_ref, bf16[192,512]{1,0:T(8,128)(2,1)S(1)} %collective-permute-done.5.p2_ref, ...), custom_call_target="tpu_custom_call" | custom-call | tf_op jit(solution)/shard_map/first_expert/pallas_call | solution.py:25
  24.4 2.9 %collective-permute-done.21.refs_0_ = bf16[192,512]{1,0:T(8,128)(2,1)S(1)} collective-permute-done((bf16[192,512]{1,0:T(8,128)(2,1)S(1)}, bf16[192,512]{1,0:T(8,128)(2,1)S(1)}, u32[]{:S(2)}, u32[]{:S(2)}) %collective-permute-start.21) | collective-permute-done | bytes 196640 | tf_op jit(solution)/shard_map/ppermute | solution.py:349
  27.3 1.7 %collective-permute-start.22 = (bf16[192,512]{1,0:T(8,128)(2,1)S(1)}, bf16[192,512]{1,0:T(8,128)(2,1)S(1)}, u32[]{:S(2)}, u32[]{:S(2)}) collective-permute-start(bf16[192,512]{1,0:T(8,128)(2,1)S(1)} %after.5.p_ref), channel_id=1, source_target_pairs={{0,2},{2,0},{4,6},{6,4},{8,10},{10,8},{12,14},{14,12},{1,3},{3,1},... | collective-permute-start | bytes 589832 | tf_op jit(solution)/shard_map/ppermute | solution.py:344
  29.0 0.0 collective-permute-start.7
  29.0 0.0 collective-permute-done.13.q_ref
  29.0 0.5 collective-permute-start.15
  29.5 0.0 collective-permute-done.8.p_ref
  29.5 0.4 collective-permute-start.9
  29.8 0.0 collective-permute-done.14.p2_ref
  29.9 0.0 collective-permute-start.23
  29.9 5.3 %collective-permute-done.22.q_ref = bf16[192,512]{1,0:T(8,128)(2,1)S(1)} collective-permute-done((bf16[192,512]{1,0:T(8,128)(2,1)S(1)}, bf16[192,512]{1,0:T(8,128)(2,1)S(1)}, u32[]{:S(2)}, u32[]{:S(2)}) %collective-permute-start.22) | collective-permute-done | bytes 196640 | tf_op jit(solution)/shard_map/ppermute | solution.py:344
  35.1 0.5 collective-permute-start.2
  35.7 1.8 %expert.3 = (f32[2,192,512]{2,1,0:T(8,128)S(1)}, bf16[2,192,512]{2,1,0:T(8,128)(2,1)S(1)}) custom-call(s32[1]{0:T(128)} %bitcast.core_ref, bf16[192,512]{1,0:T(8,128)(2,1)S(1)} %collective-permute-done.12.p_ref, bf16[192,512]{1,0:T(8,128)(2,1)S(1)} %collective-permute-done.13.q_ref, bf16[192,512]{1,0:T(8,128)(2,1)S(1)} %collective-permute-done.14.p2_ref, ...), custom_call_target="tpu_custom_call" | custom-call | tf_op jit(solution)/shard_map/expert/pallas_call | solution.py:25
  37.5 0.4 collective-permute-done.9.q_ref
  37.9 0.0 collective-permute-done.23.p2_ref
  37.9 0.5 collective-permute-start.11
  38.4 0.0 collective-permute-done.24.q2_ref
  38.4 0.1 collective-permute-start.16
  38.5 1.8 %expert.5 = (f32[2,192,512]{2,1,0:T(8,128)S(1)}, bf16[2,192,512]{2,1,0:T(8,128)(2,1)S(1)}) custom-call(s32[1]{0:T(128)} %bitcast.core_ref, bf16[192,512]{1,0:T(8,128)(2,1)S(1)} %after.5.p_ref, bf16[192,512]{1,0:T(8,128)(2,1)S(1)} %collective-permute-done.22.q_ref, bf16[192,512]{1,0:T(8,128)(2,1)S(1)} %collective-permute-done.23.p2_ref, ...), custom_call_target="tpu_custom_call" | custom-call | tf_op jit(solution)/shard_map/expert/pallas_call | solution.py:25
  40.3 0.5 collective-permute-start.25
  40.8 0.1 convert_add_fusion.3
  41.0 0.0 collective-permute-done.16
  41.0 0.1 convert_add_fusion.2
  41.2 1.5 %collective-permute-start.19 = (bf16[192,512]{1,0:T(8,128)(2,1)S(1)}, bf16[192,512]{1,0:T(8,128)(2,1)S(1)}, u32[]{:S(2)}, u32[]{:S(2)}) collective-permute-start(bf16[192,512]{1,0:T(8,128)(2,1)S(1)} %fusion.9.refs_1_), channel_id=1, source_target_pairs={{0,2},{2,0},{4,6},{6,4},{8,10},{10,8},{12,14},{14,12},{1,3},{3,1},... | collective-permute-start | bytes 589832 | tf_op jit(solution)/shard_map/ppermute | solution.py:344
  42.7 0.0 collective-permute-done.10.p2_ref
  42.7 1.8 %expert.4 = (f32[2,192,512]{2,1,0:T(8,128)S(1)}, bf16[2,192,512]{2,1,0:T(8,128)(2,1)S(1)}) custom-call(s32[1]{0:T(128)} %bitcast.core_ref, bf16[192,512]{1,0:T(8,128)(2,1)S(1)} %collective-permute-done.8.p_ref, bf16[192,512]{1,0:T(8,128)(2,1)S(1)} %collective-permute-done.9.q_ref, bf16[192,512]{1,0:T(8,128)(2,1)S(1)} %collective-permute-done.10.p2_ref, ...), custom_call_target="tpu_custom_call" | custom-call | tf_op jit(solution)/shard_map/expert/pallas_call | solution.py:25
  44.5 0.1 collective-permute-start.17
  44.6 0.1 convert_add_fusion
  44.8 0.7 collective-permute-start.26
  45.4 2.8 %collective-permute-done.19 = bf16[192,512]{1,0:T(8,128)(2,1)S(1)} collective-permute-done((bf16[192,512]{1,0:T(8,128)(2,1)S(1)}, bf16[192,512]{1,0:T(8,128)(2,1)S(1)}, u32[]{:S(2)}, u32[]{:S(2)}) %collective-permute-start.19) | collective-permute-done | bytes 196640 | tf_op jit(solution)/shard_map/ppermute | solution.py:344
  48.3 7.9 %collective-permute-start.20 = (bf16[192,512]{1,0:T(8,128)(2,1)S(1)}, bf16[192,512]{1,0:T(8,128)(2,1)S(1)}, u32[]{:S(2)}, u32[]{:S(2)}) collective-permute-start(bf16[192,512]{1,0:T(8,128)(2,1)S(1)} %fusion.5), channel_id=1, source_target_pairs={{0,12},{2,14},{4,0},{6,2},{8,4},{10,6},{12,8},{14,10},{1,13},{3,15... | collective-permute-start | bytes 589832 | tf_op jit(solution)/shard_map/ppermute | solution.py:349
  56.2 0.0 collective-permute-done.17
  56.2 0.1 convert_add_fusion.1
  56.4 2.4 %collective-permute-start.28 = (bf16[192,512]{1,0:T(8,128)(2,1)S(1)}, bf16[192,512]{1,0:T(8,128)(2,1)S(1)}, u32[]{:S(2)}, u32[]{:S(2)}) collective-permute-start(bf16[192,512]{1,0:T(8,128)(2,1)S(1)} %fusion.10.refs_1_), channel_id=1, source_target_pairs={{0,2},{2,0},{4,6},{6,4},{8,10},{10,8},{12,14},{14,12},{1,3},{3,1},... | collective-permute-start | bytes 589832 | tf_op jit(solution)/shard_map/ppermute | solution.py:344
  58.8 0.1 collective-permute-start.27
  58.9 0.1 collective-permute-start.18
  59.0 5.3 %collective-permute-done.28 = bf16[192,512]{1,0:T(8,128)(2,1)S(1)} collective-permute-done((bf16[192,512]{1,0:T(8,128)(2,1)S(1)}, bf16[192,512]{1,0:T(8,128)(2,1)S(1)}, u32[]{:S(2)}, u32[]{:S(2)}) %collective-permute-start.28) | collective-permute-done | bytes 196640 | tf_op jit(solution)/shard_map/ppermute | solution.py:344
  64.2 0.1 fusion.1
  64.3 0.1 collective-permute-start.29
  64.3 2.0 %collective-permute-done.18 = bf16[192,512]{1,0:T(8,128)(2,1)S(1)} collective-permute-done((bf16[192,512]{1,0:T(8,128)(2,1)S(1)}, bf16[192,512]{1,0:T(8,128)(2,1)S(1)}, u32[]{:S(2)}, u32[]{:S(2)}) %collective-permute-start.18) | collective-permute-done | bytes 196640 | tf_op jit(solution)/shard_map/ppermute | solution.py:344
  66.4 6.4 %collective-permute-done.27.rest_2_ = bf16[192,512]{1,0:T(8,128)(2,1)S(1)} collective-permute-done((bf16[192,512]{1,0:T(8,128)(2,1)S(1)}, bf16[192,512]{1,0:T(8,128)(2,1)S(1)}, u32[]{:S(2)}, u32[]{:S(2)}) %collective-permute-start.27) | collective-permute-done | bytes 196640 | tf_op jit(solution)/shard_map/ppermute | solution.py:349
  72.8 0.0 collective-permute-done.29.rest_3_
  72.8 0.9 %combine.1 = (f32[128,512]{1,0:T(8,128)S(1)}, bf16[128,512]{1,0:T(8,128)(2,1)S(1)}) custom-call(s32[1]{0:T(128)} %bitcast.core_ref, s32[1]{0:T(128)} %bitcast.5.line_ref, s32[2,2,128]{2,1,0:T(2,128)S(1)} %get-tuple-element.31.routes_ref, f32[2,128]{1,0:T(2,128)S(1)} %get-tuple-element.32.own_gates_ref, f32[2,128]{1,0:T(2,128)S(1)} %collective-permute-done.2.other_gates_ref, ...), custom_call_target="tpu_custom_call" | custom-call | tf_op jit(solution)/shard_map/combine/pallas_call | solution.py:25
  73.7 0.1 collective-permute-start.30
  73.8 1.3 %collective-permute-done.30.other_ref = bf16[128,512]{1,0:T(8,128)(2,1)S(1)} collective-permute-done((bf16[128,512]{1,0:T(8,128)(2,1)S(1)}, bf16[128,512]{1,0:T(8,128)(2,1)S(1)}, u32[]{:S(2)}, u32[]{:S(2)}) %collective-permute-start.30) | collective-permute-done | bytes 131104 | tf_op jit(solution)/shard_map/ppermute | solution.py:339
  75.1 0.8 %finish.1 = bf16[128,1024]{1,0:T(8,128)(2,1)} custom-call(s32[1]{0:T(128)} %bitcast.core_ref, bf16[128,1024]{1,0:T(8,128)(2,1)S(1)} %get-tuple-element.30.state_ref, f32[128,512]{1,0:T(8,128)S(1)} %get-tuple-element.47.own_ref, bf16[128,512]{1,0:T(8,128)(2,1)S(1)} %collective-permute-done.30.other_ref), custom_call_target="tpu_custom_call" | custom-call | tf_op jit(solution)/shard_map/finish/pallas_call | solution.py:25
  (26 shorter events, 0.3 us)
Async XLA Ops:
  0.0 2.9 %collective-permute-start = (bf16[2,80,512]{2,1,0:T(8,128)(2,1)}, bf16[2,80,512]{2,1,0:T(8,128)(2,1)S(1)}, u32[]{:S(2)}, u32[]{:S(2)}) collective-permute-start(bf16[2,80,512]{2,1,0:T(8,128)(2,1)} %keys_in.1), channel_id=1, source_target_pairs={{0,1},{1,0},{2,3},{3,2},{4,5},{5,4},{6,7},{7,6},{8,9},{9,8},{10,11... | collective-permute-start | bytes 491528 | tf_op jit(solution)/shard_map/ppermute | solution.py:339
  0.5 2.5 %collective-permute-start.1 = (bf16[2,80,512]{2,1,0:T(8,128)(2,1)}, bf16[2,80,512]{2,1,0:T(8,128)(2,1)S(1)}, u32[]{:S(2)}, u32[]{:S(2)}) collective-permute-start(bf16[2,80,512]{2,1,0:T(8,128)(2,1)} %values_in.1), channel_id=1, source_target_pairs={{0,1},{1,0},{2,3},{3,2},{4,5},{5,4},{6,7},{7,6},{8,9},{9,8},{10,11... | collective-permute-start | bytes 491528 | tf_op jit(solution)/shard_map/ppermute | solution.py:339
  4.2 1.5 %collective-permute-start.3 = (bf16[128,512]{1,0:T(8,128)(2,1)S(1)}, bf16[128,512]{1,0:T(8,128)(2,1)S(1)}, u32[]{:S(2)}, u32[]{:S(2)}) collective-permute-start(bf16[128,512]{1,0:T(8,128)(2,1)S(1)} %get-tuple-element.34), channel_id=1, source_target_pairs={{0,1},{1,0},{2,3},{3,2},{4,5},{5,4},{6,7},{7,6},{8,9},{9,8},{10,11... | collective-permute-start | bytes 393224 | tf_op jit(solution)/shard_map/ppermute | solution.py:339
  6.2 8.1 %collective-permute-start.4 = (bf16[192,512]{1,0:T(8,128)(2,1)S(1)}, bf16[192,512]{1,0:T(8,128)(2,1)S(1)}, u32[]{:S(2)}, u32[]{:S(2)}) collective-permute-start(bf16[192,512]{1,0:T(8,128)(2,1)S(1)} %get-tuple-element.35.p_ref), channel_id=1, source_target_pairs={{0,2},{2,0},{4,6},{6,4},{8,10},{10,8},{12,14},{14,12},{1,3},{3,1},... | collective-permute-start | bytes 589832 | tf_op jit(solution)/shard_map/ppermute | solution.py:344
  9.2 9.4 %collective-permute-start.12 = (bf16[192,512]{1,0:T(8,128)(2,1)S(1)}, bf16[192,512]{1,0:T(8,128)(2,1)S(1)}, u32[]{:S(2)}, u32[]{:S(2)}) collective-permute-start(bf16[192,512]{1,0:T(8,128)(2,1)S(1)} %get-tuple-element.39), channel_id=1, source_target_pairs={{0,4},{2,6},{4,8},{6,10},{8,12},{10,14},{12,0},{14,2},{1,5},{3,7},... | collective-permute-start | bytes 589832 | tf_op jit(solution)/shard_map/ppermute | solution.py:349
  10.7 9.3 %collective-permute-start.5 = (bf16[192,512]{1,0:T(8,128)(2,1)S(1)}, bf16[192,512]{1,0:T(8,128)(2,1)S(1)}, u32[]{:S(2)}, u32[]{:S(2)}) collective-permute-start(bf16[192,512]{1,0:T(8,128)(2,1)S(1)} %get-tuple-element.35.p_ref), channel_id=1, source_target_pairs={{0,1},{1,0},{2,3},{3,2},{4,5},{5,4},{6,7},{7,6},{8,9},{9,8},{10,11... | collective-permute-start | bytes 589832 | tf_op jit(solution)/shard_map/ppermute | solution.py:339
  14.4 5.7 %collective-permute-start.6 = (bf16[192,512]{1,0:T(8,128)(2,1)S(1)}, bf16[192,512]{1,0:T(8,128)(2,1)S(1)}, u32[]{:S(2)}, u32[]{:S(2)}) collective-permute-start(bf16[192,512]{1,0:T(8,128)(2,1)S(1)} %collective-permute-done.4.q_ref), channel_id=1, source_target_pairs={{0,1},{1,0},{2,3},{3,2},{4,5},{5,4},{6,7},{7,6},{8,9},{9,8},{10,11... | collective-permute-start | bytes 589832 | tf_op jit(solution)/shard_map/ppermute | solution.py:339
  14.4 12.9 %collective-permute-start.21 = (bf16[192,512]{1,0:T(8,128)(2,1)S(1)}, bf16[192,512]{1,0:T(8,128)(2,1)S(1)}, u32[]{:S(2)}, u32[]{:S(2)}) collective-permute-start(bf16[192,512]{1,0:T(8,128)(2,1)S(1)} %get-tuple-element.44), channel_id=1, source_target_pairs={{0,8},{2,10},{4,12},{6,14},{8,0},{10,2},{12,4},{14,6},{1,9},{3,11}... | collective-permute-start | bytes 589832 | tf_op jit(solution)/shard_map/ppermute | solution.py:349
  17.2 18.4 %copy-start = (bf16[1024,1024]{1,0:T(8,128)(2,1)S(1)}, bf16[1024,1024]{1,0:T(8,128)(2,1)}, u32[]{:S(2)}) copy-start(bf16[1024,1024]{1,0:T(8,128)(2,1)} %in_ref.5) | copy-start | bytes 6291460
  17.2 18.4 %copy-start.1 = (bf16[1024,1024]{1,0:T(8,128)(2,1)S(1)}, bf16[1024,1024]{1,0:T(8,128)(2,1)}, u32[]{:S(2)}) copy-start(bf16[1024,1024]{1,0:T(8,128)(2,1)} %out_ref.5) | copy-start | bytes 6291460
  17.2 12.3 %collective-permute-start.8 = (bf16[192,512]{1,0:T(8,128)(2,1)S(1)}, bf16[192,512]{1,0:T(8,128)(2,1)S(1)}, u32[]{:S(2)}, u32[]{:S(2)}) collective-permute-start(bf16[192,512]{1,0:T(8,128)(2,1)S(1)} %get-tuple-element.38), channel_id=1, source_target_pairs={{0,12},{2,14},{4,0},{6,2},{8,4},{10,6},{12,8},{14,10},{1,13},{3,15... | collective-permute-start | bytes 589832 | tf_op jit(solution)/shard_map/ppermute | solution.py:349
  18.6 10.4 %collective-permute-start.13 = (bf16[192,512]{1,0:T(8,128)(2,1)S(1)}, bf16[192,512]{1,0:T(8,128)(2,1)S(1)}, u32[]{:S(2)}, u32[]{:S(2)}) collective-permute-start(bf16[192,512]{1,0:T(8,128)(2,1)S(1)} %collective-permute-done.12.p_ref), channel_id=1, source_target_pairs={{0,2},{2,0},{4,6},{6,4},{8,10},{10,8},{12,14},{14,12},{1,3},{3,1},... | collective-permute-start | bytes 589832 | tf_op jit(solution)/shard_map/ppermute | solution.py:344
  20.1 9.8 %collective-permute-start.14 = (bf16[192,512]{1,0:T(8,128)(2,1)S(1)}, bf16[192,512]{1,0:T(8,128)(2,1)S(1)}, u32[]{:S(2)}, u32[]{:S(2)}) collective-permute-start(bf16[192,512]{1,0:T(8,128)(2,1)S(1)} %collective-permute-done.12.p_ref), channel_id=1, source_target_pairs={{0,1},{1,0},{2,3},{3,2},{4,5},{5,4},{6,7},{7,6},{8,9},{9,8},{10,11... | collective-permute-start | bytes 589832 | tf_op jit(solution)/shard_map/ppermute | solution.py:339
  27.3 7.8 %collective-permute-start.22 = (bf16[192,512]{1,0:T(8,128)(2,1)S(1)}, bf16[192,512]{1,0:T(8,128)(2,1)S(1)}, u32[]{:S(2)}, u32[]{:S(2)}) collective-permute-start(bf16[192,512]{1,0:T(8,128)(2,1)S(1)} %after.5.p_ref), channel_id=1, source_target_pairs={{0,2},{2,0},{4,6},{6,4},{8,10},{10,8},{12,14},{14,12},{1,3},{3,1},... | collective-permute-start | bytes 589832 | tf_op jit(solution)/shard_map/ppermute | solution.py:344
  29.0 11.4 %collective-permute-start.7 = (bf16[2,192,512]{2,1,0:T(8,128)(2,1)S(1)}, bf16[2,192,512]{2,1,0:T(8,128)(2,1)S(1)}, u32[]{:S(2)}, u32[]{:S(2)}) collective-permute-start(bf16[2,192,512]{2,1,0:T(8,128)(2,1)S(1)} %get-tuple-element.37), channel_id=1, source_target_pairs={{0,1},{1,0},{2,3},{3,2},{4,5},{5,4},{6,7},{7,6},{8,9},{9,8},{10,11... | collective-permute-start | bytes 1179656 | tf_op jit(solution)/shard_map/ppermute | solution.py:339
  29.0 6.2 %collective-permute-start.15 = (bf16[192,512]{1,0:T(8,128)(2,1)S(1)}, bf16[192,512]{1,0:T(8,128)(2,1)S(1)}, u32[]{:S(2)}, u32[]{:S(2)}) collective-permute-start(bf16[192,512]{1,0:T(8,128)(2,1)S(1)} %collective-permute-done.13.q_ref), channel_id=1, source_target_pairs={{0,1},{1,0},{2,3},{3,2},{4,5},{5,4},{6,7},{7,6},{8,9},{9,8},{10,11... | collective-permute-start | bytes 589832 | tf_op jit(solution)/shard_map/ppermute | solution.py:339
  29.5 8.4 %collective-permute-start.9 = (bf16[192,512]{1,0:T(8,128)(2,1)S(1)}, bf16[192,512]{1,0:T(8,128)(2,1)S(1)}, u32[]{:S(2)}, u32[]{:S(2)}) collective-permute-start(bf16[192,512]{1,0:T(8,128)(2,1)S(1)} %collective-permute-done.8.p_ref), channel_id=1, source_target_pairs={{0,2},{2,0},{4,6},{6,4},{8,10},{10,8},{12,14},{14,12},{1,3},{3,1},... | collective-permute-start | bytes 589832 | tf_op jit(solution)/shard_map/ppermute | solution.py:344
  29.9 8.1 %collective-permute-start.23 = (bf16[192,512]{1,0:T(8,128)(2,1)S(1)}, bf16[192,512]{1,0:T(8,128)(2,1)S(1)}, u32[]{:S(2)}, u32[]{:S(2)}) collective-permute-start(bf16[192,512]{1,0:T(8,128)(2,1)S(1)} %after.5.p_ref), channel_id=1, source_target_pairs={{0,1},{1,0},{2,3},{3,2},{4,5},{5,4},{6,7},{7,6},{8,9},{9,8},{10,11... | collective-permute-start | bytes 589832 | tf_op jit(solution)/shard_map/ppermute | solution.py:339
  35.1 3.3 %collective-permute-start.24 = (bf16[192,512]{1,0:T(8,128)(2,1)S(1)}, bf16[192,512]{1,0:T(8,128)(2,1)S(1)}, u32[]{:S(2)}, u32[]{:S(2)}) collective-permute-start(bf16[192,512]{1,0:T(8,128)(2,1)S(1)} %collective-permute-done.22.q_ref), channel_id=1, source_target_pairs={{0,1},{1,0},{2,3},{3,2},{4,5},{5,4},{6,7},{7,6},{8,9},{9,8},{10,11... | collective-permute-start | bytes 589832 | tf_op jit(solution)/shard_map/ppermute | solution.py:339
  35.1 31.2 %collective-permute-start.2 = (f32[2,128]{1,0:T(2,128)S(1)}, f32[2,128]{1,0:T(2,128)S(1)}, u32[]{:S(2)}, u32[]{:S(2)}) collective-permute-start(f32[2,128]{1,0:T(2,128)S(1)} %get-tuple-element.32.own_gates_ref), channel_id=1, source_target_pairs={{0,1},{1,0},{2,3},{3,2},{4,5},{5,4},{6,7},{7,6},{8,9},{9,8},{10,11... | collective-permute-start | bytes 3080 | tf_op jit(solution)/shard_map/ppermute | solution.py:339
  37.9 4.8 %collective-permute-start.10 = (bf16[192,512]{1,0:T(8,128)(2,1)S(1)}, bf16[192,512]{1,0:T(8,128)(2,1)S(1)}, u32[]{:S(2)}, u32[]{:S(2)}) collective-permute-start(bf16[192,512]{1,0:T(8,128)(2,1)S(1)} %collective-permute-done.8.p_ref), channel_id=1, source_target_pairs={{0,1},{1,0},{2,3},{3,2},{4,5},{5,4},{6,7},{7,6},{8,9},{9,8},{10,11... | collective-permute-start | bytes 589832 | tf_op jit(solution)/shard_map/ppermute | solution.py:339
  37.9 4.8 %collective-permute-start.11 = (bf16[192,512]{1,0:T(8,128)(2,1)S(1)}, bf16[192,512]{1,0:T(8,128)(2,1)S(1)}, u32[]{:S(2)}, u32[]{:S(2)}) collective-permute-start(bf16[192,512]{1,0:T(8,128)(2,1)S(1)} %collective-permute-done.9.q_ref), channel_id=1, source_target_pairs={{0,1},{1,0},{2,3},{3,2},{4,5},{5,4},{6,7},{7,6},{8,9},{9,8},{10,11... | collective-permute-start | bytes 589832 | tf_op jit(solution)/shard_map/ppermute | solution.py:339
  38.4 2.6 %collective-permute-start.16 = (bf16[2,192,512]{2,1,0:T(8,128)(2,1)S(1)}, bf16[2,192,512]{2,1,0:T(8,128)(2,1)S(1)}, u32[]{:S(2)}, u32[]{:S(2)}) collective-permute-start(bf16[2,192,512]{2,1,0:T(8,128)(2,1)S(1)} %get-tuple-element.41), channel_id=1, source_target_pairs={{0,1},{1,0},{2,3},{3,2},{4,5},{5,4},{6,7},{7,6},{8,9},{9,8},{10,11... | collective-permute-start | bytes 1179656 | tf_op jit(solution)/shard_map/ppermute | solution.py:339
  40.3 4.3 %collective-permute-start.25 = (bf16[2,192,512]{2,1,0:T(8,128)(2,1)S(1)}, bf16[2,192,512]{2,1,0:T(8,128)(2,1)S(1)}, u32[]{:S(2)}, u32[]{:S(2)}) collective-permute-start(bf16[2,192,512]{2,1,0:T(8,128)(2,1)S(1)} %get-tuple-element.46), channel_id=1, source_target_pairs={{0,1},{1,0},{2,3},{3,2},{4,5},{5,4},{6,7},{7,6},{8,9},{9,8},{10,11... | collective-permute-start | bytes 1179656 | tf_op jit(solution)/shard_map/ppermute | solution.py:339
  41.2 7.1 %collective-permute-start.19 = (bf16[192,512]{1,0:T(8,128)(2,1)S(1)}, bf16[192,512]{1,0:T(8,128)(2,1)S(1)}, u32[]{:S(2)}, u32[]{:S(2)}) collective-permute-start(bf16[192,512]{1,0:T(8,128)(2,1)S(1)} %fusion.9.refs_1_), channel_id=1, source_target_pairs={{0,2},{2,0},{4,6},{6,4},{8,10},{10,8},{12,14},{14,12},{1,3},{3,1},... | collective-permute-start | bytes 589832 | tf_op jit(solution)/shard_map/ppermute | solution.py:344
  44.5 11.7 %collective-permute-start.17 = (bf16[2,192,512]{2,1,0:T(8,128)(2,1)S(1)}, bf16[2,192,512]{2,1,0:T(8,128)(2,1)S(1)}, u32[]{:S(2)}, u32[]{:S(2)}) collective-permute-start(bf16[2,192,512]{2,1,0:T(8,128)(2,1)S(1)} %get-tuple-element.43), channel_id=1, source_target_pairs={{0,1},{1,0},{2,3},{3,2},{4,5},{5,4},{6,7},{7,6},{8,9},{9,8},{10,11... | collective-permute-start | bytes 1179656 | tf_op jit(solution)/shard_map/ppermute | solution.py:339
  44.8 14.0 %collective-permute-start.26 = (bf16[192,512]{1,0:T(8,128)(2,1)S(1)}, bf16[192,512]{1,0:T(8,128)(2,1)S(1)}, u32[]{:S(2)}, u32[]{:S(2)}) collective-permute-start(bf16[192,512]{1,0:T(8,128)(2,1)S(1)} %fusion.11), channel_id=1, source_target_pairs={{0,2},{2,0},{4,6},{6,4},{8,10},{10,8},{12,14},{14,12},{1,3},{3,1},... | collective-permute-start | bytes 589832 | tf_op jit(solution)/shard_map/ppermute | solution.py:344
  48.3 18.1 %collective-permute-start.20 = (bf16[192,512]{1,0:T(8,128)(2,1)S(1)}, bf16[192,512]{1,0:T(8,128)(2,1)S(1)}, u32[]{:S(2)}, u32[]{:S(2)}) collective-permute-start(bf16[192,512]{1,0:T(8,128)(2,1)S(1)} %fusion.5), channel_id=1, source_target_pairs={{0,12},{2,14},{4,0},{6,2},{8,4},{10,6},{12,8},{14,10},{1,13},{3,15... | collective-permute-start | bytes 589832 | tf_op jit(solution)/shard_map/ppermute | solution.py:349
  56.4 7.9 %collective-permute-start.28 = (bf16[192,512]{1,0:T(8,128)(2,1)S(1)}, bf16[192,512]{1,0:T(8,128)(2,1)S(1)}, u32[]{:S(2)}, u32[]{:S(2)}) collective-permute-start(bf16[192,512]{1,0:T(8,128)(2,1)S(1)} %fusion.10.refs_1_), channel_id=1, source_target_pairs={{0,2},{2,0},{4,6},{6,4},{8,10},{10,8},{12,14},{14,12},{1,3},{3,1},... | collective-permute-start | bytes 589832 | tf_op jit(solution)/shard_map/ppermute | solution.py:344
  58.8 14.0 %collective-permute-start.27 = (bf16[192,512]{1,0:T(8,128)(2,1)S(1)}, bf16[192,512]{1,0:T(8,128)(2,1)S(1)}, u32[]{:S(2)}, u32[]{:S(2)}) collective-permute-start(bf16[192,512]{1,0:T(8,128)(2,1)S(1)} %fusion.3), channel_id=1, source_target_pairs={{0,8},{2,10},{4,12},{6,14},{8,0},{10,2},{12,4},{14,6},{1,9},{3,11}... | collective-permute-start | bytes 589832 | tf_op jit(solution)/shard_map/ppermute | solution.py:349
  58.9 7.5 %collective-permute-start.18 = (bf16[192,512]{1,0:T(8,128)(2,1)S(1)}, bf16[192,512]{1,0:T(8,128)(2,1)S(1)}, u32[]{:S(2)}, u32[]{:S(2)}) collective-permute-start(bf16[192,512]{1,0:T(8,128)(2,1)S(1)} %after.4), channel_id=1, source_target_pairs={{0,2},{2,0},{4,6},{6,4},{8,10},{10,8},{12,14},{14,12},{1,3},{3,1},... | collective-permute-start | bytes 589832 | tf_op jit(solution)/shard_map/ppermute | solution.py:344
  64.3 8.5 %collective-permute-start.29 = (bf16[192,512]{1,0:T(8,128)(2,1)S(1)}, bf16[192,512]{1,0:T(8,128)(2,1)S(1)}, u32[]{:S(2)}, u32[]{:S(2)}) collective-permute-start(bf16[192,512]{1,0:T(8,128)(2,1)S(1)} %fusion.1), channel_id=1, source_target_pairs={{0,4},{2,6},{4,8},{6,10},{8,12},{10,14},{12,0},{14,2},{1,5},{3,7},... | collective-permute-start | bytes 589832 | tf_op jit(solution)/shard_map/ppermute | solution.py:349
  73.7 1.4 %collective-permute-start.30 = (bf16[128,512]{1,0:T(8,128)(2,1)S(1)}, bf16[128,512]{1,0:T(8,128)(2,1)S(1)}, u32[]{:S(2)}, u32[]{:S(2)}) collective-permute-start(bf16[128,512]{1,0:T(8,128)(2,1)S(1)} %get-tuple-element.48), channel_id=1, source_target_pairs={{0,1},{1,0},{2,3},{3,2},{4,5},{5,4},{6,7},{7,6},{8,9},{9,8},{10,11... | collective-permute-start | bytes 393224 | tf_op jit(solution)/shard_map/ppermute | solution.py:339

commit v11 on v10

--- a/solution.py
+++ b/solution.py
@@ -215,7 +215,7 @@
     ids = lax.broadcasted_iota(jnp.int32, slot.shape, 0)
     numbers = lax.broadcasted_iota(jnp.int32, (capacity, slot.shape[1]), 0).astype(jnp.float32)
     for offset, piece_ref in enumerate(pieces):
-        expert = lax.rem(line_ref[0] + offset, experts_count)
+        expert = line_ref[0] ^ offset
         wanted = jnp.sum(jnp.where(ids == expert, slot, 0.0), axis=0, keepdims=True)
         picks = jnp.where(numbers == wanted, 1.0, 0.0).astype(jnp.bfloat16)
         piece_ref[...] = jnp.dot(
@@ -311,8 +311,7 @@
         for k in range(2):
             route = routes_ref[sent, k : k + 1]
             slot = jnp.sum(jnp.where(ids == route, slots, 0.0), axis=0, keepdims=True)
-            offset = lax.rem(route - line_ref[0] + experts_count, experts_count)
-            place = offset.astype(jnp.float32) * capacity + slot
+            place = (route ^ line_ref[0]).astype(jnp.float32) * capacity + slot
             place, gate = (
                 jnp.broadcast_to(row, (full_len, full_len)).T[:, :1]
                 for row in (place, gates_ref[sent, k : k + 1])
@@ -344,11 +343,9 @@
     return lax.ppermute(values, "expert", [(i, i ^ 1) for i in range(owners)])
 
 
-def shift(values, offset):
+def exchange(values, offset):
     owners = lax.axis_size("expert")
-    return lax.ppermute(
-        values, "expert", [(i, (i + 2 * offset) % owners) for i in range(owners)]
-    )
+    return lax.ppermute(values, "expert", [(i, i ^ (2 * offset)) for i in range(owners)])
 
 
 def after_kernel(*refs):
@@ -430,17 +427,19 @@
         [routes, keep, other],
         scratch=[pltpu.VMEM((2 * full_len, half), jnp.bfloat16)],
     )
-    travelling = [shift(selected[r], r) for r in range(1, count)]
+    travelling = [exchange(selected[r], r) for r in range(1, count)]
     home = [None] * count
     kept, halves, wholes, ps, qs, q2s = {}, {}, {}, {}, {}, {}
     order = [0, 1, 2, 3]
     for offset in order:
         p = travelling[offset - 1] if offset else selected[0]
-        if offset == 2:
-            p = after(p, kept[0])
         q = swap_owner(p)
         p2 = swap(p)
         q2 = swap(q)
+        if offset == 1:
+            q2 = after(q2, kept[0])
+        if offset == 2:
+            q2 = after(q2, kept[0], kept[1])
         if offset == 3:
             q2 = after(q2, halves[1])
         ps[offset], qs[offset], q2s[offset] = p, q, q2
@@ -474,6 +473,8 @@
                 vmem_mib=16,
             )
         moving = swap(sent)
+        if offset == 3:
+            moving = after(moving, wholes[1])
         both = kept[offset] + moving.astype(jnp.float32)
         halves[offset] = both[1].astype(jnp.bfloat16)
         if offset == 0:
@@ -481,7 +482,7 @@
             continue
         across = swap_owner(halves[offset])
         wholes[offset] = (both[0] + across.astype(jnp.float32)).astype(jnp.bfloat16)
-        home[offset] = shift(wholes[offset], -offset)
+        home[offset] = exchange(wholes[offset], offset)
     across = swap_owner(after(halves[0], halves[order[-1]]))
     home[0] = (own_both[0] + across.astype(jnp.float32)).astype(jnp.bfloat16)
     own_sum, other_sum = call(
@@ -589,7 +590,7 @@
     block_rows = routes.shape[0] * routes.shape[1]
     experts_count = router.shape[1]
     capacity = 2 * max(1, 3 * block_rows // (2 * experts_count))
-    if capacity % 16 == 0:
+    if capacity % 16 == 0 and experts_count & (experts_count - 1) == 0:
         mixed = line_experts(core, state, keep, send, gates, by_choice, fc_in, fc_out, capacity)
     else:
         halves = jnp.stack([keep, send])

time: 76.1 us -> 73.1 us (0.961); the launches traced: 75.9 us -> 71.8 us
  waiting for transfers between devices: 31 us -> 24.1 us
  starting transfers between devices: 28.2 us -> 31 us
    ppermute x8, waiting for transfers between devices: 19.3 us -> 9.64 us  [swap_owner(): return lax.ppermute(values, 'expert', [(i, i ^ 1) for i in range(owners)])]
    ppermute x6, waiting for transfers between devices: 9.29 us -> 12.1 us  [exchange(): lax.ppermute(values, 'expert', [(i, i ^ 2 * offset) for i in range(owners)])]
    ppermute x6, starting transfers between devices: 13.8 us -> 15.9 us  [exchange(): lax.ppermute(values, 'expert', [(i, i ^ 2 * offset) for i in range(owners)])]
    ppermute x17, starting transfers between devices: 3.29 us -> 4.11 us  [swap(): return lax.ppermute(values, 'section', [(0, 1), (1, 0)])]
  transfers between devices with their start and end apart: 31 -> 31, of which waited for: 10 -> 10; matrix products, arithmetic and copies ran while one was open for 1% -> 1% of each run, Pallas kernels for 15% -> 16%
where the time goes in v11:
time: 73.1 us; the launch traced here: 71.8 us
  starting transfers between devices  31 us (42%)
  waiting for transfers between devices  24.1 us (33%)
  Pallas kernels  15 us (21%)
  between operations  0.89 us (1%)
    ppermute x6, starting transfers between devices, exchange(): lax.ppermute(values, 'expert', [(i, i ^ 2 * offset) for i in range(owners)])  15.9 us
    pallas_call x9, Pallas kernels, call(): pl.pallas_call(kernel, out_shape=tuple((jax.ShapeDtypeStruct(*out) for ou...  15 us
    ppermute x6, waiting for transfers between devices, exchange(): lax.ppermute(values, 'expert', [(i, i ^ 2 * offset) for i in range(owners)])  12.1 us
    ppermute x8, starting transfers between devices, swap_owner(): return lax.ppermute(values, 'expert', [(i, i ^ 1) for i in range(owners)])  11 us
    ppermute x8, waiting for transfers between devices, swap_owner(): return lax.ppermute(values, 'expert', [(i, i ^ 1) for i in range(owners)])  9.64 us
    ppermute x17, starting transfers between devices, swap(): return lax.ppermute(values, 'section', [(0, 1), (1, 0)])  4.11 us
    ppermute x17, waiting for transfers between devices, swap(): return lax.ppermute(values, 'section', [(0, 1), (1, 0)])  2.36 us
  transfers between devices with their start and end apart: 31, of which 10 were waited for; matrix products, arithmetic and copies ran while one was open for 1% of the time, Pallas kernels for 16%

profile of v11, /device:TPU:0, one launch (start us, length us, event | category | flops | bytes accessed | tf_op | source)
XLA Modules:
  0.0 71.8 jit_solution(14631741393144001030)
XLA Ops:
  0.0 0.5 collective-permute-start
  0.5 0.1 collective-permute-start.1
  1.2 1.8 %attend_own.1 = (bf16[128,512]{1,0:T(8,128)(2,1)S(1)}, bf16[128,512]{1,0:T(8,128)(2,1)S(1)}, bf16[128,512]{1,0:T(8,128)(2,1)S(1)}) custom-call(s32[1]{0:T(128)} %bitcast.core_ref, s32[1]{0:T(128)S(6)} %copy.22.source_ref, bf16[1,128,1024]{2,1,0:T(8,128)(2,1)} %x_in.1, f32[1,1024]{1,0:T(1,128)} %bitcast.40, bf16[2,80,512]{2,1,0:T(8,128)(2,1)} %keys_in.1, ...), custom_call_target="tpu_custom_call" | custom-call | tf_op jit(solution)/shard_map/attend_own/pallas_call | solution.py:25
  2.9 0.0 collective-permute-done.keys_ref
  2.9 0.0 collective-permute-done.1.values_ref
  3.0 1.2 %attend_other.1 = (bf16[128,1024]{1,0:T(8,128)(2,1)S(1)}, bf16[128,512]{1,0:T(8,128)(2,1)S(1)}, bf16[128,512]{1,0:T(8,128)(2,1)S(1)}, f32[2,128]{1,0:T(2,128)S(1)}, s32[2,2,128]{2,1,0:T(2,128)S(1)}) custom-call(s32[1]{0:T(128)} %bitcast.core_ref, s32[1]{0:T(128)S(6)} %copy.22.source_ref, bf16[128,512]{1,0:T(8,128)(2,1)S(1)} %get-tuple-element.27.own_ref, ...), custom_call_target="tpu_custom_call" | custom-call | tf_op jit(solution)/shard_map/attend_other/pallas_call | solution.py:25
  4.2 0.5 collective-permute-start.3
  4.7 1.0 %collective-permute-done.3.other_ref = bf16[128,512]{1,0:T(8,128)(2,1)S(1)} collective-permute-done((bf16[128,512]{1,0:T(8,128)(2,1)S(1)}, bf16[128,512]{1,0:T(8,128)(2,1)S(1)}, u32[]{:S(2)}, u32[]{:S(2)}) %collective-permute-start.3) | collective-permute-done | bytes 131104 | tf_op jit(solution)/shard_map/ppermute | solution.py:338
  5.7 0.5 select.5
  6.2 3.0 %collective-permute-start.12 = (bf16[192,512]{1,0:T(8,128)(2,1)S(1)}, bf16[192,512]{1,0:T(8,128)(2,1)S(1)}, u32[]{:S(2)}, u32[]{:S(2)}) collective-permute-start(bf16[192,512]{1,0:T(8,128)(2,1)S(1)} %get-tuple-element.39), channel_id=1, source_target_pairs={{0,4},{2,6},{4,0},{6,2},{8,12},{10,14},{12,8},{14,10},{1,5},{3,7},... | collective-permute-start | bytes 589832 | tf_op jit(solution)/shard_map/ppermute | solution.py:348
  9.2 1.5 %collective-permute-start.4 = (bf16[192,512]{1,0:T(8,128)(2,1)S(1)}, bf16[192,512]{1,0:T(8,128)(2,1)S(1)}, u32[]{:S(2)}, u32[]{:S(2)}) collective-permute-start(bf16[192,512]{1,0:T(8,128)(2,1)S(1)} %get-tuple-element.35.p_ref), channel_id=1, source_target_pairs={{0,2},{2,0},{4,6},{6,4},{8,10},{10,8},{12,14},{14,12},{1,3},{3,1},... | collective-permute-start | bytes 589832 | tf_op jit(solution)/shard_map/ppermute | solution.py:343
  10.7 2.6 %collective-permute-start.21 = (bf16[192,512]{1,0:T(8,128)(2,1)S(1)}, bf16[192,512]{1,0:T(8,128)(2,1)S(1)}, u32[]{:S(2)}, u32[]{:S(2)}) collective-permute-start(bf16[192,512]{1,0:T(8,128)(2,1)S(1)} %get-tuple-element.44), channel_id=1, source_target_pairs={{0,8},{2,10},{4,12},{6,14},{8,0},{10,2},{12,4},{14,6},{1,9},{3,11}... | collective-permute-start | bytes 589832 | tf_op jit(solution)/shard_map/ppermute | solution.py:348
  13.3 3.7 %collective-permute-done.12.p_ref = bf16[192,512]{1,0:T(8,128)(2,1)S(1)} collective-permute-done((bf16[192,512]{1,0:T(8,128)(2,1)S(1)}, bf16[192,512]{1,0:T(8,128)(2,1)S(1)}, u32[]{:S(2)}, u32[]{:S(2)}) %collective-permute-start.12) | collective-permute-done | bytes 196640 | tf_op jit(solution)/shard_map/ppermute | solution.py:348
  17.0 3.0 %collective-permute-start.13 = (bf16[192,512]{1,0:T(8,128)(2,1)S(1)}, bf16[192,512]{1,0:T(8,128)(2,1)S(1)}, u32[]{:S(2)}, u32[]{:S(2)}) collective-permute-start(bf16[192,512]{1,0:T(8,128)(2,1)S(1)} %collective-permute-done.12.p_ref), channel_id=1, source_target_pairs={{0,2},{2,0},{4,6},{6,4},{8,10},{10,8},{12,14},{14,12},{1,3},{3,1},... | collective-permute-start | bytes 589832 | tf_op jit(solution)/shard_map/ppermute | solution.py:343
  20.0 0.5 collective-permute-start.6
  20.5 2.5 %collective-permute-start.8 = (bf16[192,512]{1,0:T(8,128)(2,1)S(1)}, bf16[192,512]{1,0:T(8,128)(2,1)S(1)}, u32[]{:S(2)}, u32[]{:S(2)}) collective-permute-start(bf16[192,512]{1,0:T(8,128)(2,1)S(1)} %get-tuple-element.38), channel_id=1, source_target_pairs={{0,12},{2,14},{4,8},{6,10},{8,4},{10,6},{12,0},{14,2},{1,13},{3,15... | collective-permute-start | bytes 589832 | tf_op jit(solution)/shard_map/ppermute | solution.py:348
  23.0 0.2 collective-permute-start.22
  23.1 1.2 %collective-permute-done.13.q_ref = bf16[192,512]{1,0:T(8,128)(2,1)S(1)} collective-permute-done((bf16[192,512]{1,0:T(8,128)(2,1)S(1)}, bf16[192,512]{1,0:T(8,128)(2,1)S(1)}, u32[]{:S(2)}, u32[]{:S(2)}) %collective-permute-start.13) | collective-permute-done | bytes 196640 | tf_op jit(solution)/shard_map/ppermute | solution.py:343
  24.3 0.0 collective-permute-start.15
  24.3 0.0 collective-permute-done.5.p2_ref
  24.3 0.0 collective-permute-done.6.q2_ref
  24.3 4.3 %first_expert.1 = (f32[2,192,512]{2,1,0:T(8,128)S(1)}, bf16[2,192,512]{2,1,0:T(8,128)(2,1)S(1)}) custom-call(s32[1]{0:T(128)} %bitcast.core_ref, bf16[192,512]{1,0:T(8,128)(2,1)S(1)} %get-tuple-element.35.p_ref, bf16[192,512]{1,0:T(8,128)(2,1)S(1)} %collective-permute-done.4.q_ref, bf16[192,512]{1,0:T(8,128)(2,1)S(1)} %collective-permute-done.5.p2_ref, ...), custom_call_target="tpu_custom_call" | custom-call | tf_op jit(solution)/shard_map/first_expert/pallas_call | solution.py:25
  28.7 0.6 collective-permute-start.7
  29.2 0.1 collective-permute-start.14
  29.3 2.1 %collective-permute-start.9 = (bf16[192,512]{1,0:T(8,128)(2,1)S(1)}, bf16[192,512]{1,0:T(8,128)(2,1)S(1)}, u32[]{:S(2)}, u32[]{:S(2)}) collective-permute-start(bf16[192,512]{1,0:T(8,128)(2,1)S(1)} %collective-permute-done.8.p_ref), channel_id=1, source_target_pairs={{0,2},{2,0},{4,6},{6,4},{8,10},{10,8},{12,14},{14,12},{1,3},{3,1},... | collective-permute-start | bytes 589832 | tf_op jit(solution)/shard_map/ppermute | solution.py:343
  31.4 0.0 collective-permute-done.22.q_ref
  31.4 0.2 collective-permute-start.24
  31.6 0.0 collective-permute-done.15.refs_0_
  31.6 0.3 collective-permute-start.23
  31.9 0.0 collective-permute-done.14.p2_ref
  31.9 0.2 collective-permute-start.2
  32.1 1.8 %expert.3 = (f32[2,192,512]{2,1,0:T(8,128)S(1)}, bf16[2,192,512]{2,1,0:T(8,128)(2,1)S(1)}) custom-call(s32[1]{0:T(128)} %bitcast.core_ref, bf16[192,512]{1,0:T(8,128)(2,1)S(1)} %collective-permute-done.12.p_ref, bf16[192,512]{1,0:T(8,128)(2,1)S(1)} %collective-permute-done.13.q_ref, bf16[192,512]{1,0:T(8,128)(2,1)S(1)} %collective-permute-done.14.p2_ref, ...), custom_call_target="tpu_custom_call" | custom-call | tf_op jit(solution)/shard_map/expert/pallas_call | solution.py:25
  34.0 3.0 %collective-permute-done.9.q_ref = bf16[192,512]{1,0:T(8,128)(2,1)S(1)} collective-permute-done((bf16[192,512]{1,0:T(8,128)(2,1)S(1)}, bf16[192,512]{1,0:T(8,128)(2,1)S(1)}, u32[]{:S(2)}, u32[]{:S(2)}) %collective-permute-start.9) | collective-permute-done | bytes 196640 | tf_op jit(solution)/shard_map/ppermute | solution.py:343
  36.9 0.5 collective-permute-start.11
  37.4 0.0 collective-permute-done.23.p2_ref
  37.4 0.1 collective-permute-start.16
  37.5 1.8 %expert.5 = (f32[2,192,512]{2,1,0:T(8,128)S(1)}, bf16[2,192,512]{2,1,0:T(8,128)(2,1)S(1)}) custom-call(s32[1]{0:T(128)} %bitcast.core_ref, bf16[192,512]{1,0:T(8,128)(2,1)S(1)} %collective-permute-done.21.p_ref, bf16[192,512]{1,0:T(8,128)(2,1)S(1)} %collective-permute-done.22.q_ref, bf16[192,512]{1,0:T(8,128)(2,1)S(1)} %collective-permute-done.23.p2_ref, ...), custom_call_target="tpu_custom_call" | custom-call | tf_op jit(solution)/shard_map/expert/pallas_call | solution.py:25
  39.4 0.5 collective-permute-start.25
  39.9 0.1 convert_add_fusion.3
  40.0 0.0 collective-permute-done.16
  40.0 0.1 convert_add_fusion.2
  40.2 1.8 %collective-permute-start.18 = (bf16[192,512]{1,0:T(8,128)(2,1)S(1)}, bf16[192,512]{1,0:T(8,128)(2,1)S(1)}, u32[]{:S(2)}, u32[]{:S(2)}) collective-permute-start(bf16[192,512]{1,0:T(8,128)(2,1)S(1)} %fusion.9.refs_1_), channel_id=1, source_target_pairs={{0,2},{2,0},{4,6},{6,4},{8,10},{10,8},{12,14},{14,12},{1,3},{3,1},... | collective-permute-start | bytes 589832 | tf_op jit(solution)/shard_map/ppermute | solution.py:343
  42.0 0.0 collective-permute-done.10.p2_ref
  42.0 1.8 %expert.4 = (f32[2,192,512]{2,1,0:T(8,128)S(1)}, bf16[2,192,512]{2,1,0:T(8,128)(2,1)S(1)}) custom-call(s32[1]{0:T(128)} %bitcast.core_ref, bf16[192,512]{1,0:T(8,128)(2,1)S(1)} %collective-permute-done.8.p_ref, bf16[192,512]{1,0:T(8,128)(2,1)S(1)} %collective-permute-done.9.q_ref, bf16[192,512]{1,0:T(8,128)(2,1)S(1)} %collective-permute-done.10.p2_ref, ...), custom_call_target="tpu_custom_call" | custom-call | tf_op jit(solution)/shard_map/expert/pallas_call | solution.py:25
  43.9 0.1 collective-permute-start.17
  44.0 0.1 convert_add_fusion
  44.1 0.3 collective-permute-start.26
  44.5 2.8 %collective-permute-done.18 = bf16[192,512]{1,0:T(8,128)(2,1)S(1)} collective-permute-done((bf16[192,512]{1,0:T(8,128)(2,1)S(1)}, bf16[192,512]{1,0:T(8,128)(2,1)S(1)}, u32[]{:S(2)}, u32[]{:S(2)}) %collective-permute-start.18) | collective-permute-done | bytes 196640 | tf_op jit(solution)/shard_map/ppermute | solution.py:343
  47.3 1.1 %collective-permute-start.20 = (bf16[192,512]{1,0:T(8,128)(2,1)S(1)}, bf16[192,512]{1,0:T(8,128)(2,1)S(1)}, u32[]{:S(2)}, u32[]{:S(2)}) collective-permute-start(bf16[192,512]{1,0:T(8,128)(2,1)S(1)} %fusion.5.refs_1_), channel_id=1, source_target_pairs={{0,4},{2,6},{4,0},{6,2},{8,12},{10,14},{12,8},{14,10},{1,5},{3,7},... | collective-permute-start | bytes 589832 | tf_op jit(solution)/shard_map/ppermute | solution.py:348
  48.5 0.0 collective-permute-done.17.refs_0_
  48.5 0.1 convert_add_fusion.1
  48.6 1.5 %collective-permute-start.28 = (bf16[192,512]{1,0:T(8,128)(2,1)S(1)}, bf16[192,512]{1,0:T(8,128)(2,1)S(1)}, u32[]{:S(2)}, u32[]{:S(2)}) collective-permute-start(bf16[192,512]{1,0:T(8,128)(2,1)S(1)} %fusion.10.refs_1_), channel_id=1, source_target_pairs={{0,2},{2,0},{4,6},{6,4},{8,10},{10,8},{12,14},{14,12},{1,3},{3,1},... | collective-permute-start | bytes 589832 | tf_op jit(solution)/shard_map/ppermute | solution.py:343
  50.1 1.7 %collective-permute-done.26 = bf16[192,512]{1,0:T(8,128)(2,1)S(1)} collective-permute-done((bf16[192,512]{1,0:T(8,128)(2,1)S(1)}, bf16[192,512]{1,0:T(8,128)(2,1)S(1)}, u32[]{:S(2)}, u32[]{:S(2)}) %collective-permute-start.26) | collective-permute-done | bytes 196640 | tf_op jit(solution)/shard_map/ppermute | solution.py:343
  51.9 2.6 %collective-permute-start.27 = (bf16[192,512]{1,0:T(8,128)(2,1)S(1)}, bf16[192,512]{1,0:T(8,128)(2,1)S(1)}, u32[]{:S(2)}, u32[]{:S(2)}) collective-permute-start(bf16[192,512]{1,0:T(8,128)(2,1)S(1)} %fusion.3), channel_id=1, source_target_pairs={{0,8},{2,10},{4,12},{6,14},{8,0},{10,2},{12,4},{14,6},{1,9},{3,11}... | collective-permute-start | bytes 589832 | tf_op jit(solution)/shard_map/ppermute | solution.py:348
  54.5 0.6 collective-permute-start.19
  55.1 0.7 collective-permute-done.28
  55.8 0.1 fusion.1
  55.8 4.1 %collective-permute-start.29 = (bf16[192,512]{1,0:T(8,128)(2,1)S(1)}, bf16[192,512]{1,0:T(8,128)(2,1)S(1)}, u32[]{:S(2)}, u32[]{:S(2)}) collective-permute-start(bf16[192,512]{1,0:T(8,128)(2,1)S(1)} %fusion.1), channel_id=1, source_target_pairs={{0,12},{2,14},{4,8},{6,10},{8,4},{10,6},{12,0},{14,2},{1,13},{3,15... | collective-permute-start | bytes 589832 | tf_op jit(solution)/shard_map/ppermute | solution.py:348
  59.9 0.2 collective-permute-done.19
  60.2 8.4 %collective-permute-done.27.rest_2_ = bf16[192,512]{1,0:T(8,128)(2,1)S(1)} collective-permute-done((bf16[192,512]{1,0:T(8,128)(2,1)S(1)}, bf16[192,512]{1,0:T(8,128)(2,1)S(1)}, u32[]{:S(2)}, u32[]{:S(2)}) %collective-permute-start.27) | collective-permute-done | bytes 196640 | tf_op jit(solution)/shard_map/ppermute | solution.py:348
  68.7 0.9 %combine.1 = (f32[128,512]{1,0:T(8,128)S(1)}, bf16[128,512]{1,0:T(8,128)(2,1)S(1)}) custom-call(s32[1]{0:T(128)} %bitcast.core_ref, s32[1]{0:T(128)} %bitcast.5.line_ref, s32[2,2,128]{2,1,0:T(2,128)S(1)} %get-tuple-element.31.routes_ref, f32[2,128]{1,0:T(2,128)S(1)} %get-tuple-element.32.own_gates_ref, f32[2,128]{1,0:T(2,128)S(1)} %collective-permute-done.2.other_gates_ref, ...), custom_call_target="tpu_custom_call" | custom-call | tf_op jit(solution)/shard_map/combine/pallas_call | solution.py:25
  69.6 0.1 collective-permute-start.30
  69.7 1.3 %collective-permute-done.30.other_ref = bf16[128,512]{1,0:T(8,128)(2,1)S(1)} collective-permute-done((bf16[128,512]{1,0:T(8,128)(2,1)S(1)}, bf16[128,512]{1,0:T(8,128)(2,1)S(1)}, u32[]{:S(2)}, u32[]{:S(2)}) %collective-permute-start.30) | collective-permute-done | bytes 131104 | tf_op jit(solution)/shard_map/ppermute | solution.py:338
  71.0 0.8 %finish.1 = bf16[128,1024]{1,0:T(8,128)(2,1)} custom-call(s32[1]{0:T(128)} %bitcast.core_ref, bf16[128,1024]{1,0:T(8,128)(2,1)S(1)} %get-tuple-element.30.state_ref, f32[128,512]{1,0:T(8,128)S(1)} %get-tuple-element.47.own_ref, bf16[128,512]{1,0:T(8,128)(2,1)S(1)} %collective-permute-done.30.other_ref), custom_call_target="tpu_custom_call" | custom-call | tf_op jit(solution)/shard_map/finish/pallas_call | solution.py:25
  (28 shorter events, 0.3 us)
Async XLA Ops:
  0.0 2.9 %collective-permute-start = (bf16[2,80,512]{2,1,0:T(8,128)(2,1)}, bf16[2,80,512]{2,1,0:T(8,128)(2,1)S(1)}, u32[]{:S(2)}, u32[]{:S(2)}) collective-permute-start(bf16[2,80,512]{2,1,0:T(8,128)(2,1)} %keys_in.1), channel_id=1, source_target_pairs={{0,1},{1,0},{2,3},{3,2},{4,5},{5,4},{6,7},{7,6},{8,9},{9,8},{10,11... | collective-permute-start | bytes 491528 | tf_op jit(solution)/shard_map/ppermute | solution.py:338
  0.5 2.5 %collective-permute-start.1 = (bf16[2,80,512]{2,1,0:T(8,128)(2,1)}, bf16[2,80,512]{2,1,0:T(8,128)(2,1)S(1)}, u32[]{:S(2)}, u32[]{:S(2)}) collective-permute-start(bf16[2,80,512]{2,1,0:T(8,128)(2,1)} %values_in.1), channel_id=1, source_target_pairs={{0,1},{1,0},{2,3},{3,2},{4,5},{5,4},{6,7},{7,6},{8,9},{9,8},{10,11... | collective-permute-start | bytes 491528 | tf_op jit(solution)/shard_map/ppermute | solution.py:338
  4.2 1.5 %collective-permute-start.3 = (bf16[128,512]{1,0:T(8,128)(2,1)S(1)}, bf16[128,512]{1,0:T(8,128)(2,1)S(1)}, u32[]{:S(2)}, u32[]{:S(2)}) collective-permute-start(bf16[128,512]{1,0:T(8,128)(2,1)S(1)} %get-tuple-element.34), channel_id=1, source_target_pairs={{0,1},{1,0},{2,3},{3,2},{4,5},{5,4},{6,7},{7,6},{8,9},{9,8},{10,11... | collective-permute-start | bytes 393224 | tf_op jit(solution)/shard_map/ppermute | solution.py:338
  6.2 10.8 %collective-permute-start.12 = (bf16[192,512]{1,0:T(8,128)(2,1)S(1)}, bf16[192,512]{1,0:T(8,128)(2,1)S(1)}, u32[]{:S(2)}, u32[]{:S(2)}) collective-permute-start(bf16[192,512]{1,0:T(8,128)(2,1)S(1)} %get-tuple-element.39), channel_id=1, source_target_pairs={{0,4},{2,6},{4,0},{6,2},{8,12},{10,14},{12,8},{14,10},{1,5},{3,7},... | collective-permute-start | bytes 589832 | tf_op jit(solution)/shard_map/ppermute | solution.py:348
  9.2 10.7 %collective-permute-start.4 = (bf16[192,512]{1,0:T(8,128)(2,1)S(1)}, bf16[192,512]{1,0:T(8,128)(2,1)S(1)}, u32[]{:S(2)}, u32[]{:S(2)}) collective-permute-start(bf16[192,512]{1,0:T(8,128)(2,1)S(1)} %get-tuple-element.35.p_ref), channel_id=1, source_target_pairs={{0,2},{2,0},{4,6},{6,4},{8,10},{10,8},{12,14},{14,12},{1,3},{3,1},... | collective-permute-start | bytes 589832 | tf_op jit(solution)/shard_map/ppermute | solution.py:343
  10.7 12.2 %collective-permute-start.21 = (bf16[192,512]{1,0:T(8,128)(2,1)S(1)}, bf16[192,512]{1,0:T(8,128)(2,1)S(1)}, u32[]{:S(2)}, u32[]{:S(2)}) collective-permute-start(bf16[192,512]{1,0:T(8,128)(2,1)S(1)} %get-tuple-element.44), channel_id=1, source_target_pairs={{0,8},{2,10},{4,12},{6,14},{8,0},{10,2},{12,4},{14,6},{1,9},{3,11}... | collective-permute-start | bytes 589832 | tf_op jit(solution)/shard_map/ppermute | solution.py:348
  17.0 7.3 %collective-permute-start.13 = (bf16[192,512]{1,0:T(8,128)(2,1)S(1)}, bf16[192,512]{1,0:T(8,128)(2,1)S(1)}, u32[]{:S(2)}, u32[]{:S(2)}) collective-permute-start(bf16[192,512]{1,0:T(8,128)(2,1)S(1)} %collective-permute-done.12.p_ref), channel_id=1, source_target_pairs={{0,2},{2,0},{4,6},{6,4},{8,10},{10,8},{12,14},{14,12},{1,3},{3,1},... | collective-permute-start | bytes 589832 | tf_op jit(solution)/shard_map/ppermute | solution.py:343
  19.9 4.4 %collective-permute-start.5 = (bf16[192,512]{1,0:T(8,128)(2,1)S(1)}, bf16[192,512]{1,0:T(8,128)(2,1)S(1)}, u32[]{:S(2)}, u32[]{:S(2)}) collective-permute-start(bf16[192,512]{1,0:T(8,128)(2,1)S(1)} %get-tuple-element.35.p_ref), channel_id=1, source_target_pairs={{0,1},{1,0},{2,3},{3,2},{4,5},{5,4},{6,7},{7,6},{8,9},{9,8},{10,11... | collective-permute-start | bytes 589832 | tf_op jit(solution)/shard_map/ppermute | solution.py:338
  20.0 4.4 %collective-permute-start.6 = (bf16[192,512]{1,0:T(8,128)(2,1)S(1)}, bf16[192,512]{1,0:T(8,128)(2,1)S(1)}, u32[]{:S(2)}, u32[]{:S(2)}) collective-permute-start(bf16[192,512]{1,0:T(8,128)(2,1)S(1)} %collective-permute-done.4.q_ref), channel_id=1, source_target_pairs={{0,1},{1,0},{2,3},{3,2},{4,5},{5,4},{6,7},{7,6},{8,9},{9,8},{10,11... | collective-permute-start | bytes 589832 | tf_op jit(solution)/shard_map/ppermute | solution.py:338
  20.5 11.6 %copy-start = (bf16[1024,1024]{1,0:T(8,128)(2,1)S(1)}, bf16[1024,1024]{1,0:T(8,128)(2,1)}, u32[]{:S(2)}) copy-start(bf16[1024,1024]{1,0:T(8,128)(2,1)} %in_ref.5) | copy-start | bytes 6291460
  20.5 11.6 %copy-start.1 = (bf16[1024,1024]{1,0:T(8,128)(2,1)S(1)}, bf16[1024,1024]{1,0:T(8,128)(2,1)}, u32[]{:S(2)}) copy-start(bf16[1024,1024]{1,0:T(8,128)(2,1)} %out_ref.5) | copy-start | bytes 6291460
  20.5 8.8 %collective-permute-start.8 = (bf16[192,512]{1,0:T(8,128)(2,1)S(1)}, bf16[192,512]{1,0:T(8,128)(2,1)S(1)}, u32[]{:S(2)}, u32[]{:S(2)}) collective-permute-start(bf16[192,512]{1,0:T(8,128)(2,1)S(1)} %get-tuple-element.38), channel_id=1, source_target_pairs={{0,12},{2,14},{4,8},{6,10},{8,4},{10,6},{12,0},{14,2},{1,13},{3,15... | collective-permute-start | bytes 589832 | tf_op jit(solution)/shard_map/ppermute | solution.py:348
  23.0 8.5 %collective-permute-start.22 = (bf16[192,512]{1,0:T(8,128)(2,1)S(1)}, bf16[192,512]{1,0:T(8,128)(2,1)S(1)}, u32[]{:S(2)}, u32[]{:S(2)}) collective-permute-start(bf16[192,512]{1,0:T(8,128)(2,1)S(1)} %collective-permute-done.21.p_ref), channel_id=1, source_target_pairs={{0,2},{2,0},{4,6},{6,4},{8,10},{10,8},{12,14},{14,12},{1,3},{3,1},... | collective-permute-start | bytes 589832 | tf_op jit(solution)/shard_map/ppermute | solution.py:343
  24.3 7.3 %collective-permute-start.15 = (bf16[192,512]{1,0:T(8,128)(2,1)S(1)}, bf16[192,512]{1,0:T(8,128)(2,1)S(1)}, u32[]{:S(2)}, u32[]{:S(2)}) collective-permute-start(bf16[192,512]{1,0:T(8,128)(2,1)S(1)} %collective-permute-done.13.q_ref), channel_id=1, source_target_pairs={{0,1},{1,0},{2,3},{3,2},{4,5},{5,4},{6,7},{7,6},{8,9},{9,8},{10,11... | collective-permute-start | bytes 589832 | tf_op jit(solution)/shard_map/ppermute | solution.py:338
  28.7 10.7 %collective-permute-start.7 = (bf16[2,192,512]{2,1,0:T(8,128)(2,1)S(1)}, bf16[2,192,512]{2,1,0:T(8,128)(2,1)S(1)}, u32[]{:S(2)}, u32[]{:S(2)}) collective-permute-start(bf16[2,192,512]{2,1,0:T(8,128)(2,1)S(1)} %get-tuple-element.37), channel_id=1, source_target_pairs={{0,1},{1,0},{2,3},{3,2},{4,5},{5,4},{6,7},{7,6},{8,9},{9,8},{10,11... | collective-permute-start | bytes 1179656 | tf_op jit(solution)/shard_map/ppermute | solution.py:338
  29.2 2.7 %collective-permute-start.14 = (bf16[192,512]{1,0:T(8,128)(2,1)S(1)}, bf16[192,512]{1,0:T(8,128)(2,1)S(1)}, u32[]{:S(2)}, u32[]{:S(2)}) collective-permute-start(bf16[192,512]{1,0:T(8,128)(2,1)S(1)} %collective-permute-done.12.p_ref), channel_id=1, source_target_pairs={{0,1},{1,0},{2,3},{3,2},{4,5},{5,4},{6,7},{7,6},{8,9},{9,8},{10,11... | collective-permute-start | bytes 589832 | tf_op jit(solution)/shard_map/ppermute | solution.py:338
  29.3 7.6 %collective-permute-start.9 = (bf16[192,512]{1,0:T(8,128)(2,1)S(1)}, bf16[192,512]{1,0:T(8,128)(2,1)S(1)}, u32[]{:S(2)}, u32[]{:S(2)}) collective-permute-start(bf16[192,512]{1,0:T(8,128)(2,1)S(1)} %collective-permute-done.8.p_ref), channel_id=1, source_target_pairs={{0,2},{2,0},{4,6},{6,4},{8,10},{10,8},{12,14},{14,12},{1,3},{3,1},... | collective-permute-start | bytes 589832 | tf_op jit(solution)/shard_map/ppermute | solution.py:343
  31.4 5.5 %collective-permute-start.24 = (bf16[192,512]{1,0:T(8,128)(2,1)S(1)}, bf16[192,512]{1,0:T(8,128)(2,1)S(1)}, u32[]{:S(2)}, u32[]{:S(2)}) collective-permute-start(bf16[192,512]{1,0:T(8,128)(2,1)S(1)} %collective-permute-done.22.q_ref), channel_id=1, source_target_pairs={{0,1},{1,0},{2,3},{3,2},{4,5},{5,4},{6,7},{7,6},{8,9},{9,8},{10,11... | collective-permute-start | bytes 589832 | tf_op jit(solution)/shard_map/ppermute | solution.py:338
  31.6 5.8 %collective-permute-start.23 = (bf16[192,512]{1,0:T(8,128)(2,1)S(1)}, bf16[192,512]{1,0:T(8,128)(2,1)S(1)}, u32[]{:S(2)}, u32[]{:S(2)}) collective-permute-start(bf16[192,512]{1,0:T(8,128)(2,1)S(1)} %collective-permute-done.21.p_ref), channel_id=1, source_target_pairs={{0,1},{1,0},{2,3},{3,2},{4,5},{5,4},{6,7},{7,6},{8,9},{9,8},{10,11... | collective-permute-start | bytes 589832 | tf_op jit(solution)/shard_map/ppermute | solution.py:338
  31.9 28.3 %collective-permute-start.2 = (f32[2,128]{1,0:T(2,128)S(1)}, f32[2,128]{1,0:T(2,128)S(1)}, u32[]{:S(2)}, u32[]{:S(2)}) collective-permute-start(f32[2,128]{1,0:T(2,128)S(1)} %get-tuple-element.32.own_gates_ref), channel_id=1, source_target_pairs={{0,1},{1,0},{2,3},{3,2},{4,5},{5,4},{6,7},{7,6},{8,9},{9,8},{10,11... | collective-permute-start | bytes 3080 | tf_op jit(solution)/shard_map/ppermute | solution.py:338
  36.9 5.1 %collective-permute-start.10 = (bf16[192,512]{1,0:T(8,128)(2,1)S(1)}, bf16[192,512]{1,0:T(8,128)(2,1)S(1)}, u32[]{:S(2)}, u32[]{:S(2)}) collective-permute-start(bf16[192,512]{1,0:T(8,128)(2,1)S(1)} %collective-permute-done.8.p_ref), channel_id=1, source_target_pairs={{0,1},{1,0},{2,3},{3,2},{4,5},{5,4},{6,7},{7,6},{8,9},{9,8},{10,11... | collective-permute-start | bytes 589832 | tf_op jit(solution)/shard_map/ppermute | solution.py:338
  36.9 5.1 %collective-permute-start.11 = (bf16[192,512]{1,0:T(8,128)(2,1)S(1)}, bf16[192,512]{1,0:T(8,128)(2,1)S(1)}, u32[]{:S(2)}, u32[]{:S(2)}) collective-permute-start(bf16[192,512]{1,0:T(8,128)(2,1)S(1)} %collective-permute-done.9.q_ref), channel_id=1, source_target_pairs={{0,1},{1,0},{2,3},{3,2},{4,5},{5,4},{6,7},{7,6},{8,9},{9,8},{10,11... | collective-permute-start | bytes 589832 | tf_op jit(solution)/shard_map/ppermute | solution.py:338
  37.4 2.6 %collective-permute-start.16 = (bf16[2,192,512]{2,1,0:T(8,128)(2,1)S(1)}, bf16[2,192,512]{2,1,0:T(8,128)(2,1)S(1)}, u32[]{:S(2)}, u32[]{:S(2)}) collective-permute-start(bf16[2,192,512]{2,1,0:T(8,128)(2,1)S(1)} %get-tuple-element.41), channel_id=1, source_target_pairs={{0,1},{1,0},{2,3},{3,2},{4,5},{5,4},{6,7},{7,6},{8,9},{9,8},{10,11... | collective-permute-start | bytes 1179656 | tf_op jit(solution)/shard_map/ppermute | solution.py:338
  39.4 4.6 %collective-permute-start.25 = (bf16[2,192,512]{2,1,0:T(8,128)(2,1)S(1)}, bf16[2,192,512]{2,1,0:T(8,128)(2,1)S(1)}, u32[]{:S(2)}, u32[]{:S(2)}) collective-permute-start(bf16[2,192,512]{2,1,0:T(8,128)(2,1)S(1)} %get-tuple-element.46), channel_id=1, source_target_pairs={{0,1},{1,0},{2,3},{3,2},{4,5},{5,4},{6,7},{7,6},{8,9},{9,8},{10,11... | collective-permute-start | bytes 1179656 | tf_op jit(solution)/shard_map/ppermute | solution.py:338
  40.2 7.1 %collective-permute-start.18 = (bf16[192,512]{1,0:T(8,128)(2,1)S(1)}, bf16[192,512]{1,0:T(8,128)(2,1)S(1)}, u32[]{:S(2)}, u32[]{:S(2)}) collective-permute-start(bf16[192,512]{1,0:T(8,128)(2,1)S(1)} %fusion.9.refs_1_), channel_id=1, source_target_pairs={{0,2},{2,0},{4,6},{6,4},{8,10},{10,8},{12,14},{14,12},{1,3},{3,1},... | collective-permute-start | bytes 589832 | tf_op jit(solution)/shard_map/ppermute | solution.py:343
  43.9 4.6 %collective-permute-start.17 = (bf16[2,192,512]{2,1,0:T(8,128)(2,1)S(1)}, bf16[2,192,512]{2,1,0:T(8,128)(2,1)S(1)}, u32[]{:S(2)}, u32[]{:S(2)}) collective-permute-start(bf16[2,192,512]{2,1,0:T(8,128)(2,1)S(1)} %get-tuple-element.43), channel_id=1, source_target_pairs={{0,1},{1,0},{2,3},{3,2},{4,5},{5,4},{6,7},{7,6},{8,9},{9,8},{10,11... | collective-permute-start | bytes 1179656 | tf_op jit(solution)/shard_map/ppermute | solution.py:338
  44.1 7.8 %collective-permute-start.26 = (bf16[192,512]{1,0:T(8,128)(2,1)S(1)}, bf16[192,512]{1,0:T(8,128)(2,1)S(1)}, u32[]{:S(2)}, u32[]{:S(2)}) collective-permute-start(bf16[192,512]{1,0:T(8,128)(2,1)S(1)} %fusion.11), channel_id=1, source_target_pairs={{0,2},{2,0},{4,6},{6,4},{8,10},{10,8},{12,14},{14,12},{1,3},{3,1},... | collective-permute-start | bytes 589832 | tf_op jit(solution)/shard_map/ppermute | solution.py:343
  47.3 21.3 %collective-permute-start.20 = (bf16[192,512]{1,0:T(8,128)(2,1)S(1)}, bf16[192,512]{1,0:T(8,128)(2,1)S(1)}, u32[]{:S(2)}, u32[]{:S(2)}) collective-permute-start(bf16[192,512]{1,0:T(8,128)(2,1)S(1)} %fusion.5.refs_1_), channel_id=1, source_target_pairs={{0,4},{2,6},{4,0},{6,2},{8,12},{10,14},{12,8},{14,10},{1,5},{3,7},... | collective-permute-start | bytes 589832 | tf_op jit(solution)/shard_map/ppermute | solution.py:348
  48.6 7.1 %collective-permute-start.28 = (bf16[192,512]{1,0:T(8,128)(2,1)S(1)}, bf16[192,512]{1,0:T(8,128)(2,1)S(1)}, u32[]{:S(2)}, u32[]{:S(2)}) collective-permute-start(bf16[192,512]{1,0:T(8,128)(2,1)S(1)} %fusion.10.refs_1_), channel_id=1, source_target_pairs={{0,2},{2,0},{4,6},{6,4},{8,10},{10,8},{12,14},{14,12},{1,3},{3,1},... | collective-permute-start | bytes 589832 | tf_op jit(solution)/shard_map/ppermute | solution.py:343
  51.9 16.8 %collective-permute-start.27 = (bf16[192,512]{1,0:T(8,128)(2,1)S(1)}, bf16[192,512]{1,0:T(8,128)(2,1)S(1)}, u32[]{:S(2)}, u32[]{:S(2)}) collective-permute-start(bf16[192,512]{1,0:T(8,128)(2,1)S(1)} %fusion.3), channel_id=1, source_target_pairs={{0,8},{2,10},{4,12},{6,14},{8,0},{10,2},{12,4},{14,6},{1,9},{3,11}... | collective-permute-start | bytes 589832 | tf_op jit(solution)/shard_map/ppermute | solution.py:348
  54.5 5.7 %collective-permute-start.19 = (bf16[192,512]{1,0:T(8,128)(2,1)S(1)}, bf16[192,512]{1,0:T(8,128)(2,1)S(1)}, u32[]{:S(2)}, u32[]{:S(2)}) collective-permute-start(bf16[192,512]{1,0:T(8,128)(2,1)S(1)} %after.8), channel_id=1, source_target_pairs={{0,2},{2,0},{4,6},{6,4},{8,10},{10,8},{12,14},{14,12},{1,3},{3,1},... | collective-permute-start | bytes 589832 | tf_op jit(solution)/shard_map/ppermute | solution.py:343
  55.8 12.8 %collective-permute-start.29 = (bf16[192,512]{1,0:T(8,128)(2,1)S(1)}, bf16[192,512]{1,0:T(8,128)(2,1)S(1)}, u32[]{:S(2)}, u32[]{:S(2)}) collective-permute-start(bf16[192,512]{1,0:T(8,128)(2,1)S(1)} %fusion.1), channel_id=1, source_target_pairs={{0,12},{2,14},{4,8},{6,10},{8,4},{10,6},{12,0},{14,2},{1,13},{3,15... | collective-permute-start | bytes 589832 | tf_op jit(solution)/shard_map/ppermute | solution.py:348
  69.6 1.4 %collective-permute-start.30 = (bf16[128,512]{1,0:T(8,128)(2,1)S(1)}, bf16[128,512]{1,0:T(8,128)(2,1)S(1)}, u32[]{:S(2)}, u32[]{:S(2)}) collective-permute-start(bf16[128,512]{1,0:T(8,128)(2,1)S(1)} %get-tuple-element.48), channel_id=1, source_target_pairs={{0,1},{1,0},{2,3},{3,2},{4,5},{5,4},{6,7},{7,6},{8,9},{9,8},{10,11... | collective-permute-start | bytes 393224 | tf_op jit(solution)/shard_map/ppermute | solution.py:338

commit v12 on v11

--- a/solution.py
+++ b/solution.py
@@ -244,50 +244,9 @@
     keep_ref[1] = keep[capacity:]
 
 
-def first_expert_kernel(
-    core_ref,
-    p_ref,
-    q_ref,
-    p2_ref,
-    q2_ref,
-    in_in,
-    out_in,
-    keep_ref,
-    send_ref,
-    rows_ref,
-    in_ref,
-    out_ref,
-    hidden_ref,
-    sems,
-):
-    core = core_ref[0]
-    capacity, half = p_ref.shape
-    tile = in_ref.shape[1] // 4
-    tiles = [slice(at, at + tile) for at in range(0, in_ref.shape[1], tile)]
-    copies = fetch(
-        sems,
-        *[(in_in.at[:, at], in_ref.at[:, at]) for at in tiles],
-        (out_in, out_ref),
-    )
-    rows_ref[:capacity, part_of(core, half)] = p_ref[...]
-    rows_ref[capacity:, part_of(core, half)] = q_ref[...]
-    rows_ref[:capacity, part_of(1 - core, half)] = p2_ref[...]
-    rows_ref[capacity:, part_of(1 - core, half)] = q2_ref[...]
-    for copy, at in zip(copies, tiles):
+def load_kernel(in_in, out_in, in_ref, out_ref, sems):
+    for copy in fetch(sems, (in_in, in_ref), (out_in, out_ref)):
         copy.wait()
-        hidden = jnp.dot(rows_ref[...], in_ref[:, at], preferred_element_type=jnp.float32)
-        hidden_ref[:, at] = jnp.maximum(hidden, 0.0).astype(jnp.bfloat16)
-    copies[-1].wait()
-    send = jnp.dot(
-        hidden_ref[...], out_ref[:, part_of(1 - core, half)], preferred_element_type=jnp.float32
-    ).astype(jnp.bfloat16)
-    send_ref[0] = send[:capacity]
-    send_ref[1] = send[capacity:]
-    keep = jnp.dot(
-        hidden_ref[...], out_ref[:, part_of(core, half)], preferred_element_type=jnp.float32
-    )
-    keep_ref[0] = keep[:capacity]
-    keep_ref[1] = keep[capacity:]
 
 
 def combine_kernel(core_ref, line_ref, routes_ref, own_gates_ref, other_gates_ref, *rest):
@@ -427,12 +386,23 @@
         [routes, keep, other],
         scratch=[pltpu.VMEM((2 * full_len, half), jnp.bfloat16)],
     )
+    near_in, near_out = call(
+        load_kernel,
+        "load",
+        [(fc_in.shape, jnp.bfloat16), (fc_out.shape, jnp.bfloat16)],
+        [],
+        [],
+        [fc_in, fc_out],
+        scratch=[pltpu.SemaphoreType.DMA((2,))],
+    )
     travelling = [exchange(selected[r], r) for r in range(1, count)]
     home = [None] * count
     kept, halves, wholes, ps, qs, q2s = {}, {}, {}, {}, {}, {}
     order = [0, 1, 2, 3]
     for offset in order:
         p = travelling[offset - 1] if offset else selected[0]
+        if offset == 1:
+            p = after(p, near_in)
         q = swap_owner(p)
         p2 = swap(p)
         q2 = swap(q)
@@ -445,35 +415,17 @@
         ps[offset], qs[offset], q2s[offset] = p, q, q2
         outs = [((2, capacity, half), jnp.float32), ((2, capacity, half), jnp.bfloat16)]
         rows = pltpu.VMEM((2 * capacity, width), jnp.bfloat16)
-        if offset == order[0]:
-            kept[offset], sent = call(
-                first_expert_kernel,
-                "first_expert",
-                outs,
-                [core],
-                [p, q, p2, q2],
-                [fc_in, fc_out],
-                scratch=[
-                    rows,
-                    pltpu.VMEM(fc_in.shape, jnp.bfloat16),
-                    pltpu.VMEM(fc_out.shape, jnp.bfloat16),
-                    pltpu.VMEM((2 * capacity, fc_in.shape[1]), jnp.bfloat16),
-                    pltpu.SemaphoreType.DMA((5,)),
-                ],
-                vmem_mib=20,
-            )
-        else:
-            kept[offset], sent = call(
-                expert_kernel,
-                "expert",
-                outs,
-                [core],
-                [p, q, p2, q2, fc_in, fc_out],
-                scratch=[rows],
-                vmem_mib=16,
-            )
+        kept[offset], sent = call(
+            expert_kernel,
+            "expert",
+            outs,
+            [core],
+            [p, q, p2, q2, near_in, near_out],
+            scratch=[rows],
+            vmem_mib=16,
+        )
         moving = swap(sent)
-        if offset == 3:
+        if offset == 2:
             moving = after(moving, wholes[1])
         both = kept[offset] + moving.astype(jnp.float32)
         halves[offset] = both[1].astype(jnp.bfloat16)
@@ -483,7 +435,7 @@
         across = swap_owner(halves[offset])
         wholes[offset] = (both[0] + across.astype(jnp.float32)).astype(jnp.bfloat16)
         home[offset] = exchange(wholes[offset], offset)
-    across = swap_owner(after(halves[0], halves[order[-1]]))
+    across = swap_owner(after(halves[0], halves[3]))
     home[0] = (own_both[0] + across.astype(jnp.float32)).astype(jnp.bfloat16)
     own_sum, other_sum = call(
         combine_kernel,

time: 73.1 us -> 75.6 us (1.034)
  waiting for transfers between devices: 24.1 us -> 30.3 us
  starting transfers between devices: 31 us -> 28.1 us
    ppermute x8, waiting for transfers between devices: 9.64 us -> 15 us  [swap_owner(): return lax.ppermute(values, 'expert', [(i, i ^ 1) for i in range(owners)])]
    ppermute x6, starting transfers between devices: 15.9 us -> 12.4 us  [exchange(): lax.ppermute(values, 'expert', [(i, i ^ 2 * offset) for i in range(owners)])]
    ppermute x8, starting transfers between devices: 11 us -> 11.9 us  [swap_owner(): return lax.ppermute(values, 'expert', [(i, i ^ 1) for i in range(owners)])]
    ppermute x6, waiting for transfers between devices: 12.1 us -> 12.9 us  [exchange(): lax.ppermute(values, 'expert', [(i, i ^ 2 * offset) for i in range(owners)])]
    pallas_call x9 -> x10, Pallas kernels: 15 us -> 14.8 us  [call(): pl.pallas_call(kernel, out_shape=tuple((jax.ShapeDtypeStruct(*out) for ou...]
  transfers between devices with their start and end apart: 31 -> 31, of which waited for: 10 -> 13; matrix products, arithmetic and copies ran while one was open for 1% -> 1% of each run, Pallas kernels for 16% -> 15%
where the time goes in v12:
time: 75.6 us; the launch traced here: 74.9 us
  waiting for transfers between devices  30.3 us (40%)
  starting transfers between devices  28.1 us (37%)
  Pallas kernels  14.8 us (20%)
  between operations  0.92 us (1%)
    ppermute x8, waiting for transfers between devices, swap_owner(): return lax.ppermute(values, 'expert', [(i, i ^ 1) for i in range(owners)])  15 us
    pallas_call x10, Pallas kernels, call(): pl.pallas_call(kernel, out_shape=tuple((jax.ShapeDtypeStruct(*out) for ou...  14.8 us
    ppermute x6, waiting for transfers between devices, exchange(): lax.ppermute(values, 'expert', [(i, i ^ 2 * offset) for i in range(owners)])  12.9 us
    ppermute x6, starting transfers between devices, exchange(): lax.ppermute(values, 'expert', [(i, i ^ 2 * offset) for i in range(owners)])  12.4 us
    ppermute x8, starting transfers between devices, swap_owner(): return lax.ppermute(values, 'expert', [(i, i ^ 1) for i in range(owners)])  11.9 us
    ppermute x17, starting transfers between devices, swap(): return lax.ppermute(values, 'section', [(0, 1), (1, 0)])  3.78 us
    ppermute x17, waiting for transfers between devices, swap(): return lax.ppermute(values, 'section', [(0, 1), (1, 0)])  2.36 us
  transfers between devices with their start and end apart: 31, of which 13 were waited for; matrix products, arithmetic and copies ran while one was open for 1% of the time, Pallas kernels for 15%

profile of v12, /device:TPU:0, one launch (start us, length us, event | category | flops | bytes accessed | tf_op | source)
XLA Modules:
  0.0 74.9 jit_solution(1757539718743049525)
XLA Ops:
  0.0 0.5 collective-permute-start
  0.5 0.1 collective-permute-start.1
  1.2 1.8 %attend_own.1 = (bf16[128,512]{1,0:T(8,128)(2,1)S(1)}, bf16[128,512]{1,0:T(8,128)(2,1)S(1)}, bf16[128,512]{1,0:T(8,128)(2,1)S(1)}) custom-call(s32[1]{0:T(128)} %bitcast.core_ref, s32[1]{0:T(128)S(6)} %copy.24.source_ref, bf16[1,128,1024]{2,1,0:T(8,128)(2,1)} %x_in.1, f32[1,1024]{1,0:T(1,128)} %bitcast.40, bf16[2,80,512]{2,1,0:T(8,128)(2,1)} %keys_in.1, ...), custom_call_target="tpu_custom_call" | custom-call | tf_op jit(solution)/shard_map/attend_own/pallas_call | solution.py:25
  2.9 0.0 collective-permute-done.1.values_ref
  3.0 1.2 %attend_other.1 = (bf16[128,1024]{1,0:T(8,128)(2,1)S(1)}, bf16[128,512]{1,0:T(8,128)(2,1)S(1)}, bf16[128,512]{1,0:T(8,128)(2,1)S(1)}, f32[2,128]{1,0:T(2,128)S(1)}, s32[2,2,128]{2,1,0:T(2,128)S(1)}) custom-call(s32[1]{0:T(128)} %bitcast.core_ref, s32[1]{0:T(128)S(6)} %copy.24.source_ref, bf16[128,512]{1,0:T(8,128)(2,1)S(1)} %get-tuple-element.29.own_ref, ...), custom_call_target="tpu_custom_call" | custom-call | tf_op jit(solution)/shard_map/attend_other/pallas_call | solution.py:25
  4.2 0.5 collective-permute-start.3
  4.7 1.0 %collective-permute-done.3.other_ref = bf16[128,512]{1,0:T(8,128)(2,1)S(1)} collective-permute-done((bf16[128,512]{1,0:T(8,128)(2,1)S(1)}, bf16[128,512]{1,0:T(8,128)(2,1)S(1)}, u32[]{:S(2)}, u32[]{:S(2)}) %collective-permute-start.3) | collective-permute-done | bytes 131104 | tf_op jit(solution)/shard_map/ppermute | solution.py:297
  5.7 0.5 select.5
  6.2 3.0 %collective-permute-start.12 = (bf16[192,512]{1,0:T(8,128)(2,1)S(1)}, bf16[192,512]{1,0:T(8,128)(2,1)S(1)}, u32[]{:S(2)}, u32[]{:S(2)}) collective-permute-start(bf16[192,512]{1,0:T(8,128)(2,1)S(1)} %get-tuple-element.43), channel_id=1, source_target_pairs={{0,4},{2,6},{4,0},{6,2},{8,12},{10,14},{12,8},{14,10},{1,5},{3,7},... | collective-permute-start | bytes 589832 | tf_op jit(solution)/shard_map/ppermute | solution.py:307
  9.2 1.5 %collective-permute-start.4 = (bf16[192,512]{1,0:T(8,128)(2,1)S(1)}, bf16[192,512]{1,0:T(8,128)(2,1)S(1)}, u32[]{:S(2)}, u32[]{:S(2)}) collective-permute-start(bf16[192,512]{1,0:T(8,128)(2,1)S(1)} %get-tuple-element.37.p_ref), channel_id=1, source_target_pairs={{0,2},{2,0},{4,6},{6,4},{8,10},{10,8},{12,14},{14,12},{1,3},{3,1},... | collective-permute-start | bytes 589832 | tf_op jit(solution)/shard_map/ppermute | solution.py:302
  10.7 2.6 %collective-permute-start.21 = (bf16[192,512]{1,0:T(8,128)(2,1)S(1)}, bf16[192,512]{1,0:T(8,128)(2,1)S(1)}, u32[]{:S(2)}, u32[]{:S(2)}) collective-permute-start(bf16[192,512]{1,0:T(8,128)(2,1)S(1)} %get-tuple-element.48), channel_id=1, source_target_pairs={{0,8},{2,10},{4,12},{6,14},{8,0},{10,2},{12,4},{14,6},{1,9},{3,11}... | collective-permute-start | bytes 589832 | tf_op jit(solution)/shard_map/ppermute | solution.py:307
  13.3 2.2 %load.1 = (bf16[1024,1024]{1,0:T(8,128)(2,1)S(1)}, bf16[1024,1024]{1,0:T(8,128)(2,1)S(1)}) custom-call(bf16[1024,1024]{1,0:T(8,128)(2,1)} %in_in.1, bf16[1024,1024]{1,0:T(8,128)(2,1)} %out_in.1), custom_call_target="tpu_custom_call" | custom-call | tf_op jit(solution)/shard_map/load/pallas_call | solution.py:25
  15.6 1.4 %collective-permute-done.12.refs_0_ = bf16[192,512]{1,0:T(8,128)(2,1)S(1)} collective-permute-done((bf16[192,512]{1,0:T(8,128)(2,1)S(1)}, bf16[192,512]{1,0:T(8,128)(2,1)S(1)}, u32[]{:S(2)}, u32[]{:S(2)}) %collective-permute-start.12) | collective-permute-done | bytes 196640 | tf_op jit(solution)/shard_map/ppermute | solution.py:307
  17.0 3.0 %collective-permute-start.13 = (bf16[192,512]{1,0:T(8,128)(2,1)S(1)}, bf16[192,512]{1,0:T(8,128)(2,1)S(1)}, u32[]{:S(2)}, u32[]{:S(2)}) collective-permute-start(bf16[192,512]{1,0:T(8,128)(2,1)S(1)} %after.6.p_ref), channel_id=1, source_target_pairs={{0,2},{2,0},{4,6},{6,4},{8,10},{10,8},{12,14},{14,12},{1,3},{3,1},... | collective-permute-start | bytes 589832 | tf_op jit(solution)/shard_map/ppermute | solution.py:302
  20.0 0.5 collective-permute-start.6
  20.5 1.8 %collective-permute-done.21.p_ref = bf16[192,512]{1,0:T(8,128)(2,1)S(1)} collective-permute-done((bf16[192,512]{1,0:T(8,128)(2,1)S(1)}, bf16[192,512]{1,0:T(8,128)(2,1)S(1)}, u32[]{:S(2)}, u32[]{:S(2)}) %collective-permute-start.21) | collective-permute-done | bytes 196640 | tf_op jit(solution)/shard_map/ppermute | solution.py:307
  22.3 0.5 collective-permute-start.22
  22.8 2.5 %collective-permute-start.8 = (bf16[192,512]{1,0:T(8,128)(2,1)S(1)}, bf16[192,512]{1,0:T(8,128)(2,1)S(1)}, u32[]{:S(2)}, u32[]{:S(2)}) collective-permute-start(bf16[192,512]{1,0:T(8,128)(2,1)S(1)} %get-tuple-element.42), channel_id=1, source_target_pairs={{0,12},{2,14},{4,8},{6,10},{8,4},{10,6},{12,0},{14,2},{1,13},{3,15... | collective-permute-start | bytes 589832 | tf_op jit(solution)/shard_map/ppermute | solution.py:307
  25.3 0.2 collective-permute-done.13.q_ref
  25.5 0.0 collective-permute-start.15
  25.5 0.0 collective-permute-done.5.p2_ref
  25.5 0.0 collective-permute-done.6.q2_ref
  25.5 1.8 %expert.4 = (f32[2,192,512]{2,1,0:T(8,128)S(1)}, bf16[2,192,512]{2,1,0:T(8,128)(2,1)S(1)}) custom-call(s32[1]{0:T(128)} %bitcast.core_ref, bf16[192,512]{1,0:T(8,128)(2,1)S(1)} %get-tuple-element.37.p_ref, bf16[192,512]{1,0:T(8,128)(2,1)S(1)} %collective-permute-done.4.q_ref, bf16[192,512]{1,0:T(8,128)(2,1)S(1)} %collective-permute-done.5.p2_ref, ...), custom_call_target="tpu_custom_call" | custom-call | tf_op jit(solution)/shard_map/expert/pallas_call | solution.py:25
  27.3 0.6 collective-permute-start.7
  27.9 0.1 collective-permute-start.14
  28.0 0.6 collective-permute-done.22.q_ref
  28.5 0.0 collective-permute-start.24
  28.5 1.8 %collective-permute-done.8.p_ref = bf16[192,512]{1,0:T(8,128)(2,1)S(1)} collective-permute-done((bf16[192,512]{1,0:T(8,128)(2,1)S(1)}, bf16[192,512]{1,0:T(8,128)(2,1)S(1)}, u32[]{:S(2)}, u32[]{:S(2)}) %collective-permute-start.8) | collective-permute-done | bytes 196640 | tf_op jit(solution)/shard_map/ppermute | solution.py:307
  30.4 1.5 %collective-permute-start.9 = (bf16[192,512]{1,0:T(8,128)(2,1)S(1)}, bf16[192,512]{1,0:T(8,128)(2,1)S(1)}, u32[]{:S(2)}, u32[]{:S(2)}) collective-permute-start(bf16[192,512]{1,0:T(8,128)(2,1)S(1)} %collective-permute-done.8.p_ref), channel_id=1, source_target_pairs={{0,2},{2,0},{4,6},{6,4},{8,10},{10,8},{12,14},{14,12},{1,3},{3,1},... | collective-permute-start | bytes 589832 | tf_op jit(solution)/shard_map/ppermute | solution.py:302
  31.9 0.0 collective-permute-done.14.p2_ref
  31.9 1.8 %expert.5 = (f32[2,192,512]{2,1,0:T(8,128)S(1)}, bf16[2,192,512]{2,1,0:T(8,128)(2,1)S(1)}) custom-call(s32[1]{0:T(128)} %bitcast.core_ref, bf16[192,512]{1,0:T(8,128)(2,1)S(1)} %after.6.p_ref, bf16[192,512]{1,0:T(8,128)(2,1)S(1)} %collective-permute-done.13.q_ref, bf16[192,512]{1,0:T(8,128)(2,1)S(1)} %collective-permute-done.14.p2_ref, ...), custom_call_target="tpu_custom_call" | custom-call | tf_op jit(solution)/shard_map/expert/pallas_call | solution.py:25
  33.8 0.6 collective-permute-start.16
  34.3 0.0 collective-permute-done.24.refs_0_
  34.3 0.1 collective-permute-start.2
  34.4 1.6 %collective-permute-done.9.q_ref = bf16[192,512]{1,0:T(8,128)(2,1)S(1)} collective-permute-done((bf16[192,512]{1,0:T(8,128)(2,1)S(1)}, bf16[192,512]{1,0:T(8,128)(2,1)S(1)}, u32[]{:S(2)}, u32[]{:S(2)}) %collective-permute-start.9) | collective-permute-done | bytes 196640 | tf_op jit(solution)/shard_map/ppermute | solution.py:302
  36.1 0.5 collective-permute-start.11
  36.6 1.8 %expert.7 = (f32[2,192,512]{2,1,0:T(8,128)S(1)}, bf16[2,192,512]{2,1,0:T(8,128)(2,1)S(1)}) custom-call(s32[1]{0:T(128)} %bitcast.core_ref, bf16[192,512]{1,0:T(8,128)(2,1)S(1)} %collective-permute-done.21.p_ref, bf16[192,512]{1,0:T(8,128)(2,1)S(1)} %collective-permute-done.22.q_ref, bf16[192,512]{1,0:T(8,128)(2,1)S(1)} %collective-permute-done.23.p2_ref, ...), custom_call_target="tpu_custom_call" | custom-call | tf_op jit(solution)/shard_map/expert/pallas_call | solution.py:25
  38.4 0.1 collective-permute-start.25
  38.5 0.1 convert_add_fusion.3
  38.6 0.1 convert_add_fusion.2
  38.8 1.6 %collective-permute-start.19 = (bf16[192,512]{1,0:T(8,128)(2,1)S(1)}, bf16[192,512]{1,0:T(8,128)(2,1)S(1)}, u32[]{:S(2)}, u32[]{:S(2)}) collective-permute-start(bf16[192,512]{1,0:T(8,128)(2,1)S(1)} %fusion.9.refs_1_), channel_id=1, source_target_pairs={{0,2},{2,0},{4,6},{6,4},{8,10},{10,8},{12,14},{14,12},{1,3},{3,1},... | collective-permute-start | bytes 589832 | tf_op jit(solution)/shard_map/ppermute | solution.py:302
  40.5 0.0 collective-permute-done.10.p2_ref
  40.5 1.8 %expert.6 = (f32[2,192,512]{2,1,0:T(8,128)S(1)}, bf16[2,192,512]{2,1,0:T(8,128)(2,1)S(1)}) custom-call(s32[1]{0:T(128)} %bitcast.core_ref, bf16[192,512]{1,0:T(8,128)(2,1)S(1)} %collective-permute-done.8.p_ref, bf16[192,512]{1,0:T(8,128)(2,1)S(1)} %collective-permute-done.9.q_ref, bf16[192,512]{1,0:T(8,128)(2,1)S(1)} %collective-permute-done.10.p2_ref, ...), custom_call_target="tpu_custom_call" | custom-call | tf_op jit(solution)/shard_map/expert/pallas_call | solution.py:25
  42.3 0.3 collective-permute-start.17
  42.6 3.5 %collective-permute-done.19 = bf16[192,512]{1,0:T(8,128)(2,1)S(1)} collective-permute-done((bf16[192,512]{1,0:T(8,128)(2,1)S(1)}, bf16[192,512]{1,0:T(8,128)(2,1)S(1)}, u32[]{:S(2)}, u32[]{:S(2)}) %collective-permute-start.19) | collective-permute-done | bytes 196640 | tf_op jit(solution)/shard_map/ppermute | solution.py:302
  46.2 2.8 %collective-permute-start.20 = (bf16[192,512]{1,0:T(8,128)(2,1)S(1)}, bf16[192,512]{1,0:T(8,128)(2,1)S(1)}, u32[]{:S(2)}, u32[]{:S(2)}) collective-permute-start(bf16[192,512]{1,0:T(8,128)(2,1)S(1)} %fusion.5.refs_1_), channel_id=1, source_target_pairs={{0,4},{2,6},{4,0},{6,2},{8,12},{10,14},{12,8},{14,10},{1,5},{3,7},... | collective-permute-start | bytes 589832 | tf_op jit(solution)/shard_map/ppermute | solution.py:307
  49.0 0.1 convert_add_fusion
  49.1 0.5 collective-permute-start.26
  49.7 0.1 convert_add_fusion.1
  49.8 1.6 %collective-permute-start.28 = (bf16[192,512]{1,0:T(8,128)(2,1)S(1)}, bf16[192,512]{1,0:T(8,128)(2,1)S(1)}, u32[]{:S(2)}, u32[]{:S(2)}) collective-permute-start(bf16[192,512]{1,0:T(8,128)(2,1)S(1)} %fusion.10.refs_1_), channel_id=1, source_target_pairs={{0,2},{2,0},{4,6},{6,4},{8,10},{10,8},{12,14},{14,12},{1,3},{3,1},... | collective-permute-start | bytes 589832 | tf_op jit(solution)/shard_map/ppermute | solution.py:302
  51.5 5.6 %collective-permute-done.26 = bf16[192,512]{1,0:T(8,128)(2,1)S(1)} collective-permute-done((bf16[192,512]{1,0:T(8,128)(2,1)S(1)}, bf16[192,512]{1,0:T(8,128)(2,1)S(1)}, u32[]{:S(2)}, u32[]{:S(2)}) %collective-permute-start.26) | collective-permute-done | bytes 196640 | tf_op jit(solution)/shard_map/ppermute | solution.py:302
  57.1 0.3 collective-permute-start.27
  57.4 1.6 %collective-permute-start.18 = (bf16[192,512]{1,0:T(8,128)(2,1)S(1)}, bf16[192,512]{1,0:T(8,128)(2,1)S(1)}, u32[]{:S(2)}, u32[]{:S(2)}) collective-permute-start(bf16[192,512]{1,0:T(8,128)(2,1)S(1)} %after.9), channel_id=1, source_target_pairs={{0,2},{2,0},{4,6},{6,4},{8,10},{10,8},{12,14},{14,12},{1,3},{3,1},... | collective-permute-start | bytes 589832 | tf_op jit(solution)/shard_map/ppermute | solution.py:302
  59.1 2.2 %collective-permute-done.28 = bf16[192,512]{1,0:T(8,128)(2,1)S(1)} collective-permute-done((bf16[192,512]{1,0:T(8,128)(2,1)S(1)}, bf16[192,512]{1,0:T(8,128)(2,1)S(1)}, u32[]{:S(2)}, u32[]{:S(2)}) %collective-permute-start.28) | collective-permute-done | bytes 196640 | tf_op jit(solution)/shard_map/ppermute | solution.py:302
  61.3 0.1 fusion.1
  61.3 1.2 %collective-permute-start.29 = (bf16[192,512]{1,0:T(8,128)(2,1)S(1)}, bf16[192,512]{1,0:T(8,128)(2,1)S(1)}, u32[]{:S(2)}, u32[]{:S(2)}) collective-permute-start(bf16[192,512]{1,0:T(8,128)(2,1)S(1)} %fusion.1), channel_id=1, source_target_pairs={{0,12},{2,14},{4,8},{6,10},{8,4},{10,6},{12,0},{14,2},{1,13},{3,15... | collective-permute-start | bytes 589832 | tf_op jit(solution)/shard_map/ppermute | solution.py:307
  62.6 1.3 %collective-permute-done.18 = bf16[192,512]{1,0:T(8,128)(2,1)S(1)} collective-permute-done((bf16[192,512]{1,0:T(8,128)(2,1)S(1)}, bf16[192,512]{1,0:T(8,128)(2,1)S(1)}, u32[]{:S(2)}, u32[]{:S(2)}) %collective-permute-start.18) | collective-permute-done | bytes 196640 | tf_op jit(solution)/shard_map/ppermute | solution.py:302
  63.9 0.0 collective-permute-done.2.other_gates_ref
  63.9 0.0 collective-permute-done.20.rest_1_
  63.9 7.8 %collective-permute-done.27.rest_2_ = bf16[192,512]{1,0:T(8,128)(2,1)S(1)} collective-permute-done((bf16[192,512]{1,0:T(8,128)(2,1)S(1)}, bf16[192,512]{1,0:T(8,128)(2,1)S(1)}, u32[]{:S(2)}, u32[]{:S(2)}) %collective-permute-start.27) | collective-permute-done | bytes 196640 | tf_op jit(solution)/shard_map/ppermute | solution.py:307
  71.8 0.9 %combine.1 = (f32[128,512]{1,0:T(8,128)S(1)}, bf16[128,512]{1,0:T(8,128)(2,1)S(1)}) custom-call(s32[1]{0:T(128)} %bitcast.core_ref, s32[1]{0:T(128)} %bitcast.5.line_ref, s32[2,2,128]{2,1,0:T(2,128)S(1)} %get-tuple-element.33.routes_ref, f32[2,128]{1,0:T(2,128)S(1)} %get-tuple-element.34.own_gates_ref, f32[2,128]{1,0:T(2,128)S(1)} %collective-permute-done.2.other_gates_ref, ...), custom_call_target="tpu_custom_call" | custom-call | tf_op jit(solution)/shard_map/combine/pallas_call | solution.py:25
  72.7 0.1 collective-permute-start.30
  72.8 1.3 %collective-permute-done.30.other_ref = bf16[128,512]{1,0:T(8,128)(2,1)S(1)} collective-permute-done((bf16[128,512]{1,0:T(8,128)(2,1)S(1)}, bf16[128,512]{1,0:T(8,128)(2,1)S(1)}, u32[]{:S(2)}, u32[]{:S(2)}) %collective-permute-start.30) | collective-permute-done | bytes 131104 | tf_op jit(solution)/shard_map/ppermute | solution.py:297
  74.1 0.8 %finish.1 = bf16[128,1024]{1,0:T(8,128)(2,1)} custom-call(s32[1]{0:T(128)} %bitcast.core_ref, bf16[128,1024]{1,0:T(8,128)(2,1)S(1)} %get-tuple-element.32.state_ref, f32[128,512]{1,0:T(8,128)S(1)} %get-tuple-element.51.own_ref, bf16[128,512]{1,0:T(8,128)(2,1)S(1)} %collective-permute-done.30.other_ref), custom_call_target="tpu_custom_call" | custom-call | tf_op jit(solution)/shard_map/finish/pallas_call | solution.py:25
  (26 shorter events, 0.3 us)
Async XLA Ops:
  0.0 2.9 %collective-permute-start = (bf16[2,80,512]{2,1,0:T(8,128)(2,1)}, bf16[2,80,512]{2,1,0:T(8,128)(2,1)S(1)}, u32[]{:S(2)}, u32[]{:S(2)}) collective-permute-start(bf16[2,80,512]{2,1,0:T(8,128)(2,1)} %keys_in.1), channel_id=1, source_target_pairs={{0,1},{1,0},{2,3},{3,2},{4,5},{5,4},{6,7},{7,6},{8,9},{9,8},{10,11... | collective-permute-start | bytes 491528 | tf_op jit(solution)/shard_map/ppermute | solution.py:297
  0.5 2.5 %collective-permute-start.1 = (bf16[2,80,512]{2,1,0:T(8,128)(2,1)}, bf16[2,80,512]{2,1,0:T(8,128)(2,1)S(1)}, u32[]{:S(2)}, u32[]{:S(2)}) collective-permute-start(bf16[2,80,512]{2,1,0:T(8,128)(2,1)} %values_in.1), channel_id=1, source_target_pairs={{0,1},{1,0},{2,3},{3,2},{4,5},{5,4},{6,7},{7,6},{8,9},{9,8},{10,11... | collective-permute-start | bytes 491528 | tf_op jit(solution)/shard_map/ppermute | solution.py:297
  4.2 1.5 %collective-permute-start.3 = (bf16[128,512]{1,0:T(8,128)(2,1)S(1)}, bf16[128,512]{1,0:T(8,128)(2,1)S(1)}, u32[]{:S(2)}, u32[]{:S(2)}) collective-permute-start(bf16[128,512]{1,0:T(8,128)(2,1)S(1)} %get-tuple-element.36), channel_id=1, source_target_pairs={{0,1},{1,0},{2,3},{3,2},{4,5},{5,4},{6,7},{7,6},{8,9},{9,8},{10,11... | collective-permute-start | bytes 393224 | tf_op jit(solution)/shard_map/ppermute | solution.py:297
  6.2 10.8 %collective-permute-start.12 = (bf16[192,512]{1,0:T(8,128)(2,1)S(1)}, bf16[192,512]{1,0:T(8,128)(2,1)S(1)}, u32[]{:S(2)}, u32[]{:S(2)}) collective-permute-start(bf16[192,512]{1,0:T(8,128)(2,1)S(1)} %get-tuple-element.43), channel_id=1, source_target_pairs={{0,4},{2,6},{4,0},{6,2},{8,12},{10,14},{12,8},{14,10},{1,5},{3,7},... | collective-permute-start | bytes 589832 | tf_op jit(solution)/shard_map/ppermute | solution.py:307
  9.2 10.7 %collective-permute-start.4 = (bf16[192,512]{1,0:T(8,128)(2,1)S(1)}, bf16[192,512]{1,0:T(8,128)(2,1)S(1)}, u32[]{:S(2)}, u32[]{:S(2)}) collective-permute-start(bf16[192,512]{1,0:T(8,128)(2,1)S(1)} %get-tuple-element.37.p_ref), channel_id=1, source_target_pairs={{0,2},{2,0},{4,6},{6,4},{8,10},{10,8},{12,14},{14,12},{1,3},{3,1},... | collective-permute-start | bytes 589832 | tf_op jit(solution)/shard_map/ppermute | solution.py:302
  10.7 11.6 %collective-permute-start.21 = (bf16[192,512]{1,0:T(8,128)(2,1)S(1)}, bf16[192,512]{1,0:T(8,128)(2,1)S(1)}, u32[]{:S(2)}, u32[]{:S(2)}) collective-permute-start(bf16[192,512]{1,0:T(8,128)(2,1)S(1)} %get-tuple-element.48), channel_id=1, source_target_pairs={{0,8},{2,10},{4,12},{6,14},{8,0},{10,2},{12,4},{14,6},{1,9},{3,11}... | collective-permute-start | bytes 589832 | tf_op jit(solution)/shard_map/ppermute | solution.py:307
  17.0 8.5 %collective-permute-start.13 = (bf16[192,512]{1,0:T(8,128)(2,1)S(1)}, bf16[192,512]{1,0:T(8,128)(2,1)S(1)}, u32[]{:S(2)}, u32[]{:S(2)}) collective-permute-start(bf16[192,512]{1,0:T(8,128)(2,1)S(1)} %after.6.p_ref), channel_id=1, source_target_pairs={{0,2},{2,0},{4,6},{6,4},{8,10},{10,8},{12,14},{14,12},{1,3},{3,1},... | collective-permute-start | bytes 589832 | tf_op jit(solution)/shard_map/ppermute | solution.py:302
  19.9 5.5 %collective-permute-start.5 = (bf16[192,512]{1,0:T(8,128)(2,1)S(1)}, bf16[192,512]{1,0:T(8,128)(2,1)S(1)}, u32[]{:S(2)}, u32[]{:S(2)}) collective-permute-start(bf16[192,512]{1,0:T(8,128)(2,1)S(1)} %get-tuple-element.37.p_ref), channel_id=1, source_target_pairs={{0,1},{1,0},{2,3},{3,2},{4,5},{5,4},{6,7},{7,6},{8,9},{9,8},{10,11... | collective-permute-start | bytes 589832 | tf_op jit(solution)/shard_map/ppermute | solution.py:297
  20.0 5.5 %collective-permute-start.6 = (bf16[192,512]{1,0:T(8,128)(2,1)S(1)}, bf16[192,512]{1,0:T(8,128)(2,1)S(1)}, u32[]{:S(2)}, u32[]{:S(2)}) collective-permute-start(bf16[192,512]{1,0:T(8,128)(2,1)S(1)} %collective-permute-done.4.q_ref), channel_id=1, source_target_pairs={{0,1},{1,0},{2,3},{3,2},{4,5},{5,4},{6,7},{7,6},{8,9},{9,8},{10,11... | collective-permute-start | bytes 589832 | tf_op jit(solution)/shard_map/ppermute | solution.py:297
  22.3 6.3 %collective-permute-start.22 = (bf16[192,512]{1,0:T(8,128)(2,1)S(1)}, bf16[192,512]{1,0:T(8,128)(2,1)S(1)}, u32[]{:S(2)}, u32[]{:S(2)}) collective-permute-start(bf16[192,512]{1,0:T(8,128)(2,1)S(1)} %collective-permute-done.21.p_ref), channel_id=1, source_target_pairs={{0,2},{2,0},{4,6},{6,4},{8,10},{10,8},{12,14},{14,12},{1,3},{3,1},... | collective-permute-start | bytes 589832 | tf_op jit(solution)/shard_map/ppermute | solution.py:302
  22.8 7.6 %collective-permute-start.8 = (bf16[192,512]{1,0:T(8,128)(2,1)S(1)}, bf16[192,512]{1,0:T(8,128)(2,1)S(1)}, u32[]{:S(2)}, u32[]{:S(2)}) collective-permute-start(bf16[192,512]{1,0:T(8,128)(2,1)S(1)} %get-tuple-element.42), channel_id=1, source_target_pairs={{0,12},{2,14},{4,8},{6,10},{8,4},{10,6},{12,0},{14,2},{1,13},{3,15... | collective-permute-start | bytes 589832 | tf_op jit(solution)/shard_map/ppermute | solution.py:307
  25.5 6.4 %collective-permute-start.15 = (bf16[192,512]{1,0:T(8,128)(2,1)S(1)}, bf16[192,512]{1,0:T(8,128)(2,1)S(1)}, u32[]{:S(2)}, u32[]{:S(2)}) collective-permute-start(bf16[192,512]{1,0:T(8,128)(2,1)S(1)} %collective-permute-done.13.q_ref), channel_id=1, source_target_pairs={{0,1},{1,0},{2,3},{3,2},{4,5},{5,4},{6,7},{7,6},{8,9},{9,8},{10,11... | collective-permute-start | bytes 589832 | tf_op jit(solution)/shard_map/ppermute | solution.py:297
  27.3 11.1 %collective-permute-start.7 = (bf16[2,192,512]{2,1,0:T(8,128)(2,1)S(1)}, bf16[2,192,512]{2,1,0:T(8,128)(2,1)S(1)}, u32[]{:S(2)}, u32[]{:S(2)}) collective-permute-start(bf16[2,192,512]{2,1,0:T(8,128)(2,1)S(1)} %get-tuple-element.41), channel_id=1, source_target_pairs={{0,1},{1,0},{2,3},{3,2},{4,5},{5,4},{6,7},{7,6},{8,9},{9,8},{10,11... | collective-permute-start | bytes 1179656 | tf_op jit(solution)/shard_map/ppermute | solution.py:297
  27.9 4.0 %collective-permute-start.14 = (bf16[192,512]{1,0:T(8,128)(2,1)S(1)}, bf16[192,512]{1,0:T(8,128)(2,1)S(1)}, u32[]{:S(2)}, u32[]{:S(2)}) collective-permute-start(bf16[192,512]{1,0:T(8,128)(2,1)S(1)} %after.6.p_ref), channel_id=1, source_target_pairs={{0,1},{1,0},{2,3},{3,2},{4,5},{5,4},{6,7},{7,6},{8,9},{9,8},{10,11... | collective-permute-start | bytes 589832 | tf_op jit(solution)/shard_map/ppermute | solution.py:297
  28.5 5.8 %collective-permute-start.24 = (bf16[192,512]{1,0:T(8,128)(2,1)S(1)}, bf16[192,512]{1,0:T(8,128)(2,1)S(1)}, u32[]{:S(2)}, u32[]{:S(2)}) collective-permute-start(bf16[192,512]{1,0:T(8,128)(2,1)S(1)} %collective-permute-done.22.q_ref), channel_id=1, source_target_pairs={{0,1},{1,0},{2,3},{3,2},{4,5},{5,4},{6,7},{7,6},{8,9},{9,8},{10,11... | collective-permute-start | bytes 589832 | tf_op jit(solution)/shard_map/ppermute | solution.py:297
  30.4 5.7 %collective-permute-start.9 = (bf16[192,512]{1,0:T(8,128)(2,1)S(1)}, bf16[192,512]{1,0:T(8,128)(2,1)S(1)}, u32[]{:S(2)}, u32[]{:S(2)}) collective-permute-start(bf16[192,512]{1,0:T(8,128)(2,1)S(1)} %collective-permute-done.8.p_ref), channel_id=1, source_target_pairs={{0,2},{2,0},{4,6},{6,4},{8,10},{10,8},{12,14},{14,12},{1,3},{3,1},... | collective-permute-start | bytes 589832 | tf_op jit(solution)/shard_map/ppermute | solution.py:302
  31.9 4.2 %collective-permute-start.23 = (bf16[192,512]{1,0:T(8,128)(2,1)S(1)}, bf16[192,512]{1,0:T(8,128)(2,1)S(1)}, u32[]{:S(2)}, u32[]{:S(2)}) collective-permute-start(bf16[192,512]{1,0:T(8,128)(2,1)S(1)} %collective-permute-done.21.p_ref), channel_id=1, source_target_pairs={{0,1},{1,0},{2,3},{3,2},{4,5},{5,4},{6,7},{7,6},{8,9},{9,8},{10,11... | collective-permute-start | bytes 589832 | tf_op jit(solution)/shard_map/ppermute | solution.py:297
  33.8 4.9 %collective-permute-start.16 = (bf16[2,192,512]{2,1,0:T(8,128)(2,1)S(1)}, bf16[2,192,512]{2,1,0:T(8,128)(2,1)S(1)}, u32[]{:S(2)}, u32[]{:S(2)}) collective-permute-start(bf16[2,192,512]{2,1,0:T(8,128)(2,1)S(1)} %get-tuple-element.45), channel_id=1, source_target_pairs={{0,1},{1,0},{2,3},{3,2},{4,5},{5,4},{6,7},{7,6},{8,9},{9,8},{10,11... | collective-permute-start | bytes 1179656 | tf_op jit(solution)/shard_map/ppermute | solution.py:297
  34.3 29.6 %collective-permute-start.2 = (f32[2,128]{1,0:T(2,128)S(1)}, f32[2,128]{1,0:T(2,128)S(1)}, u32[]{:S(2)}, u32[]{:S(2)}) collective-permute-start(f32[2,128]{1,0:T(2,128)S(1)} %get-tuple-element.34.own_gates_ref), channel_id=1, source_target_pairs={{0,1},{1,0},{2,3},{3,2},{4,5},{5,4},{6,7},{7,6},{8,9},{9,8},{10,11... | collective-permute-start | bytes 3080 | tf_op jit(solution)/shard_map/ppermute | solution.py:297
  36.1 4.4 %collective-permute-start.10 = (bf16[192,512]{1,0:T(8,128)(2,1)S(1)}, bf16[192,512]{1,0:T(8,128)(2,1)S(1)}, u32[]{:S(2)}, u32[]{:S(2)}) collective-permute-start(bf16[192,512]{1,0:T(8,128)(2,1)S(1)} %collective-permute-done.8.p_ref), channel_id=1, source_target_pairs={{0,1},{1,0},{2,3},{3,2},{4,5},{5,4},{6,7},{7,6},{8,9},{9,8},{10,11... | collective-permute-start | bytes 589832 | tf_op jit(solution)/shard_map/ppermute | solution.py:297
  36.1 4.4 %collective-permute-start.11 = (bf16[192,512]{1,0:T(8,128)(2,1)S(1)}, bf16[192,512]{1,0:T(8,128)(2,1)S(1)}, u32[]{:S(2)}, u32[]{:S(2)}) collective-permute-start(bf16[192,512]{1,0:T(8,128)(2,1)S(1)} %collective-permute-done.9.q_ref), channel_id=1, source_target_pairs={{0,1},{1,0},{2,3},{3,2},{4,5},{5,4},{6,7},{7,6},{8,9},{9,8},{10,11... | collective-permute-start | bytes 589832 | tf_op jit(solution)/shard_map/ppermute | solution.py:297
  38.4 10.6 %collective-permute-start.25 = (bf16[2,192,512]{2,1,0:T(8,128)(2,1)S(1)}, bf16[2,192,512]{2,1,0:T(8,128)(2,1)S(1)}, u32[]{:S(2)}, u32[]{:S(2)}) collective-permute-start(bf16[2,192,512]{2,1,0:T(8,128)(2,1)S(1)} %get-tuple-element.50), channel_id=1, source_target_pairs={{0,1},{1,0},{2,3},{3,2},{4,5},{5,4},{6,7},{7,6},{8,9},{9,8},{10,11... | collective-permute-start | bytes 1179656 | tf_op jit(solution)/shard_map/ppermute | solution.py:297
  38.8 7.4 %collective-permute-start.19 = (bf16[192,512]{1,0:T(8,128)(2,1)S(1)}, bf16[192,512]{1,0:T(8,128)(2,1)S(1)}, u32[]{:S(2)}, u32[]{:S(2)}) collective-permute-start(bf16[192,512]{1,0:T(8,128)(2,1)S(1)} %fusion.9.refs_1_), channel_id=1, source_target_pairs={{0,2},{2,0},{4,6},{6,4},{8,10},{10,8},{12,14},{14,12},{1,3},{3,1},... | collective-permute-start | bytes 589832 | tf_op jit(solution)/shard_map/ppermute | solution.py:302
  42.3 7.4 %collective-permute-start.17 = (bf16[2,192,512]{2,1,0:T(8,128)(2,1)S(1)}, bf16[2,192,512]{2,1,0:T(8,128)(2,1)S(1)}, u32[]{:S(2)}, u32[]{:S(2)}) collective-permute-start(bf16[2,192,512]{2,1,0:T(8,128)(2,1)S(1)} %get-tuple-element.47), channel_id=1, source_target_pairs={{0,1},{1,0},{2,3},{3,2},{4,5},{5,4},{6,7},{7,6},{8,9},{9,8},{10,11... | collective-permute-start | bytes 1179656 | tf_op jit(solution)/shard_map/ppermute | solution.py:297
  46.2 17.7 %collective-permute-start.20 = (bf16[192,512]{1,0:T(8,128)(2,1)S(1)}, bf16[192,512]{1,0:T(8,128)(2,1)S(1)}, u32[]{:S(2)}, u32[]{:S(2)}) collective-permute-start(bf16[192,512]{1,0:T(8,128)(2,1)S(1)} %fusion.5.refs_1_), channel_id=1, source_target_pairs={{0,4},{2,6},{4,0},{6,2},{8,12},{10,14},{12,8},{14,10},{1,5},{3,7},... | collective-permute-start | bytes 589832 | tf_op jit(solution)/shard_map/ppermute | solution.py:307
  49.1 7.9 %collective-permute-start.26 = (bf16[192,512]{1,0:T(8,128)(2,1)S(1)}, bf16[192,512]{1,0:T(8,128)(2,1)S(1)}, u32[]{:S(2)}, u32[]{:S(2)}) collective-permute-start(bf16[192,512]{1,0:T(8,128)(2,1)S(1)} %fusion.11), channel_id=1, source_target_pairs={{0,2},{2,0},{4,6},{6,4},{8,10},{10,8},{12,14},{14,12},{1,3},{3,1},... | collective-permute-start | bytes 589832 | tf_op jit(solution)/shard_map/ppermute | solution.py:302
  49.8 11.4 %collective-permute-start.28 = (bf16[192,512]{1,0:T(8,128)(2,1)S(1)}, bf16[192,512]{1,0:T(8,128)(2,1)S(1)}, u32[]{:S(2)}, u32[]{:S(2)}) collective-permute-start(bf16[192,512]{1,0:T(8,128)(2,1)S(1)} %fusion.10.refs_1_), channel_id=1, source_target_pairs={{0,2},{2,0},{4,6},{6,4},{8,10},{10,8},{12,14},{14,12},{1,3},{3,1},... | collective-permute-start | bytes 589832 | tf_op jit(solution)/shard_map/ppermute | solution.py:302
  57.1 14.7 %collective-permute-start.27 = (bf16[192,512]{1,0:T(8,128)(2,1)S(1)}, bf16[192,512]{1,0:T(8,128)(2,1)S(1)}, u32[]{:S(2)}, u32[]{:S(2)}) collective-permute-start(bf16[192,512]{1,0:T(8,128)(2,1)S(1)} %fusion.3), channel_id=1, source_target_pairs={{0,8},{2,10},{4,12},{6,14},{8,0},{10,2},{12,4},{14,6},{1,9},{3,11}... | collective-permute-start | bytes 589832 | tf_op jit(solution)/shard_map/ppermute | solution.py:307
  57.4 6.4 %collective-permute-start.18 = (bf16[192,512]{1,0:T(8,128)(2,1)S(1)}, bf16[192,512]{1,0:T(8,128)(2,1)S(1)}, u32[]{:S(2)}, u32[]{:S(2)}) collective-permute-start(bf16[192,512]{1,0:T(8,128)(2,1)S(1)} %after.9), channel_id=1, source_target_pairs={{0,2},{2,0},{4,6},{6,4},{8,10},{10,8},{12,14},{14,12},{1,3},{3,1},... | collective-permute-start | bytes 589832 | tf_op jit(solution)/shard_map/ppermute | solution.py:302
  61.3 10.4 %collective-permute-start.29 = (bf16[192,512]{1,0:T(8,128)(2,1)S(1)}, bf16[192,512]{1,0:T(8,128)(2,1)S(1)}, u32[]{:S(2)}, u32[]{:S(2)}) collective-permute-start(bf16[192,512]{1,0:T(8,128)(2,1)S(1)} %fusion.1), channel_id=1, source_target_pairs={{0,12},{2,14},{4,8},{6,10},{8,4},{10,6},{12,0},{14,2},{1,13},{3,15... | collective-permute-start | bytes 589832 | tf_op jit(solution)/shard_map/ppermute | solution.py:307
  72.7 1.4 %collective-permute-start.30 = (bf16[128,512]{1,0:T(8,128)(2,1)S(1)}, bf16[128,512]{1,0:T(8,128)(2,1)S(1)}, u32[]{:S(2)}, u32[]{:S(2)}) collective-permute-start(bf16[128,512]{1,0:T(8,128)(2,1)S(1)} %get-tuple-element.52), channel_id=1, source_target_pairs={{0,1},{1,0},{2,3},{3,2},{4,5},{5,4},{6,7},{7,6},{8,9},{9,8},{10,11... | collective-permute-start | bytes 393224 | tf_op jit(solution)/shard_map/ppermute | solution.py:297

commit v13 on v12

--- a/solution.py
+++ b/solution.py
@@ -397,46 +397,44 @@
     )
     travelling = [exchange(selected[r], r) for r in range(1, count)]
     home = [None] * count
-    kept, halves, wholes, ps, qs, q2s = {}, {}, {}, {}, {}, {}
-    order = [0, 1, 2, 3]
-    for offset in order:
+    ps, qs, kept, halves, wholes = {}, {}, {}, {}, {}
+    for offset in [0, 2, 1, 3]:
         p = travelling[offset - 1] if offset else selected[0]
+        if offset == 2:
+            p = after(p, near_in, qs[0])
+        q = swap_owner(p)
+        if offset == 3:
+            q = after(q, qs[1])
+        ps[offset], qs[offset] = p, q
+    for offset in [2, 3, 1, 0]:
+        p, q = ps[offset], qs[offset]
+        p2, q2 = swap(p), swap(q)
+        if offset == 3:
+            q2 = after(q2, kept[2])
         if offset == 1:
-            p = after(p, near_in)
-        q = swap_owner(p)
-        p2 = swap(p)
-        q2 = swap(q)
-        if offset == 1:
-            q2 = after(q2, kept[0])
-        if offset == 2:
-            q2 = after(q2, kept[0], kept[1])
-        if offset == 3:
-            q2 = after(q2, halves[1])
-        ps[offset], qs[offset], q2s[offset] = p, q, q2
-        outs = [((2, capacity, half), jnp.float32), ((2, capacity, half), jnp.bfloat16)]
-        rows = pltpu.VMEM((2 * capacity, width), jnp.bfloat16)
+            q2 = after(q2, wholes[2], kept[3])
+        if offset == 0:
+            q2 = after(q2, wholes[3], kept[1])
         kept[offset], sent = call(
             expert_kernel,
             "expert",
-            outs,
+            [((2, capacity, half), jnp.float32), ((2, capacity, half), jnp.bfloat16)],
             [core],
             [p, q, p2, q2, near_in, near_out],
-            scratch=[rows],
+            scratch=[pltpu.VMEM((2 * capacity, width), jnp.bfloat16)],
             vmem_mib=16,
         )
         moving = swap(sent)
-        if offset == 2:
-            moving = after(moving, wholes[1])
         both = kept[offset] + moving.astype(jnp.float32)
         halves[offset] = both[1].astype(jnp.bfloat16)
+        leaving = halves[offset]
         if offset == 0:
-            own_both = both
-            continue
-        across = swap_owner(halves[offset])
+            leaving = after(leaving, halves[1])
+        across = swap_owner(leaving)
+        if offset == 3:
+            across = after(across, home[2])
         wholes[offset] = (both[0] + across.astype(jnp.float32)).astype(jnp.bfloat16)
-        home[offset] = exchange(wholes[offset], offset)
-    across = swap_owner(after(halves[0], halves[3]))
-    home[0] = (own_both[0] + across.astype(jnp.float32)).astype(jnp.bfloat16)
+        home[offset] = exchange(wholes[offset], offset) if offset else wholes[offset]
     own_sum, other_sum = call(
         combine_kernel,
         "combine",

time: 75.6 us -> 85.4 us (1.13)
  waiting for transfers between devices: 30.3 us -> 44.3 us
  starting transfers between devices: 28.1 us -> 24.5 us
    ppermute x6, waiting for transfers between devices: 12.9 us -> 20.1 us  [exchange(): lax.ppermute(values, 'expert', [(i, i ^ 2 * offset) for i in range(owners)])]
    ppermute x8, starting transfers between devices: 11.9 us -> 6.86 us  [swap_owner(): return lax.ppermute(values, 'expert', [(i, i ^ 1) for i in range(owners)])]
    ppermute x8, waiting for transfers between devices: 15 us -> 19.5 us  [swap_owner(): return lax.ppermute(values, 'expert', [(i, i ^ 1) for i in range(owners)])]
    ppermute x17, waiting for transfers between devices: 2.36 us -> 4.73 us  [swap(): return lax.ppermute(values, 'section', [(0, 1), (1, 0)])]
    ppermute x6, starting transfers between devices: 12.4 us -> 14 us  [exchange(): lax.ppermute(values, 'expert', [(i, i ^ 2 * offset) for i in range(owners)])]
  transfers between devices with their start and end apart: 31 -> 31, of which waited for: 13 -> 16; matrix products, arithmetic and copies ran while one was open for 1% -> 1% of each run, Pallas kernels for 15% -> 13%
where the time goes in v13:
time: 85.4 us; the launch traced here: 85.2 us
  waiting for transfers between devices  44.3 us (52%)
  starting transfers between devices  24.5 us (29%)
  Pallas kernels  14.8 us (17%)
  between operations  0.92 us (1%)
    ppermute x6, waiting for transfers between devices, exchange(): lax.ppermute(values, 'expert', [(i, i ^ 2 * offset) for i in range(owners)])  20.1 us
    ppermute x8, waiting for transfers between devices, swap_owner(): return lax.ppermute(values, 'expert', [(i, i ^ 1) for i in range(owners)])  19.5 us
    pallas_call x10, Pallas kernels, call(): pl.pallas_call(kernel, out_shape=tuple((jax.ShapeDtypeStruct(*out) for ou...  14.8 us
    ppermute x6, starting transfers between devices, exchange(): lax.ppermute(values, 'expert', [(i, i ^ 2 * offset) for i in range(owners)])  14 us
    ppermute x8, starting transfers between devices, swap_owner(): return lax.ppermute(values, 'expert', [(i, i ^ 1) for i in range(owners)])  6.86 us
    ppermute x17, waiting for transfers between devices, swap(): return lax.ppermute(values, 'section', [(0, 1), (1, 0)])  4.73 us
    ppermute x17, starting transfers between devices, swap(): return lax.ppermute(values, 'section', [(0, 1), (1, 0)])  3.64 us
  transfers between devices with their start and end apart: 31, of which 16 were waited for; matrix products, arithmetic and copies ran while one was open for 1% of the time, Pallas kernels for 13%

profile of v13, /device:TPU:0, one launch (start us, length us, event | category | flops | bytes accessed | tf_op | source)
XLA Modules:
  0.0 85.2 jit_solution(12936433489494154141)
XLA Ops:
  0.0 0.5 collective-permute-start
  0.5 0.1 collective-permute-start.1
  1.2 1.8 %attend_own.1 = (bf16[128,512]{1,0:T(8,128)(2,1)S(1)}, bf16[128,512]{1,0:T(8,128)(2,1)S(1)}, bf16[128,512]{1,0:T(8,128)(2,1)S(1)}) custom-call(s32[1]{0:T(128)} %bitcast.core_ref, s32[1]{0:T(128)S(6)} %copy.26.source_ref, bf16[1,128,1024]{2,1,0:T(8,128)(2,1)} %x_in.1, f32[1,1024]{1,0:T(1,128)} %bitcast.40, bf16[2,80,512]{2,1,0:T(8,128)(2,1)} %keys_in.1, ...), custom_call_target="tpu_custom_call" | custom-call | tf_op jit(solution)/shard_map/attend_own/pallas_call | solution.py:25
  2.9 0.0 collective-permute-done.keys_ref
  2.9 0.0 collective-permute-done.1.values_ref
  3.0 1.2 %attend_other.1 = (bf16[128,1024]{1,0:T(8,128)(2,1)S(1)}, bf16[128,512]{1,0:T(8,128)(2,1)S(1)}, bf16[128,512]{1,0:T(8,128)(2,1)S(1)}, f32[2,128]{1,0:T(2,128)S(1)}, s32[2,2,128]{2,1,0:T(2,128)S(1)}) custom-call(s32[1]{0:T(128)} %bitcast.core_ref, s32[1]{0:T(128)S(6)} %copy.26.source_ref, bf16[128,512]{1,0:T(8,128)(2,1)S(1)} %get-tuple-element.29.own_ref, ...), custom_call_target="tpu_custom_call" | custom-call | tf_op jit(solution)/shard_map/attend_other/pallas_call | solution.py:25
  4.2 0.5 collective-permute-start.3
  4.7 1.0 %collective-permute-done.3.other_ref = bf16[128,512]{1,0:T(8,128)(2,1)S(1)} collective-permute-done((bf16[128,512]{1,0:T(8,128)(2,1)S(1)}, bf16[128,512]{1,0:T(8,128)(2,1)S(1)}, u32[]{:S(2)}, u32[]{:S(2)}) %collective-permute-start.3) | collective-permute-done | bytes 131104 | tf_op jit(solution)/shard_map/ppermute | solution.py:297
  5.7 0.5 select.5
  6.2 4.0 %collective-permute-start.13 = (bf16[192,512]{1,0:T(8,128)(2,1)S(1)}, bf16[192,512]{1,0:T(8,128)(2,1)S(1)}, u32[]{:S(2)}, u32[]{:S(2)}) collective-permute-start(bf16[192,512]{1,0:T(8,128)(2,1)S(1)} %get-tuple-element.40), channel_id=1, source_target_pairs={{0,8},{2,10},{4,12},{6,14},{8,0},{10,2},{12,4},{14,6},{1,9},{3,11}... | collective-permute-start | bytes 589832 | tf_op jit(solution)/shard_map/ppermute | solution.py:307
  10.2 1.5 %collective-permute-start.4 = (bf16[192,512]{1,0:T(8,128)(2,1)S(1)}, bf16[192,512]{1,0:T(8,128)(2,1)S(1)}, u32[]{:S(2)}, u32[]{:S(2)}) collective-permute-start(bf16[192,512]{1,0:T(8,128)(2,1)S(1)} %get-tuple-element.37.p_ref), channel_id=1, source_target_pairs={{0,2},{2,0},{4,6},{6,4},{8,10},{10,8},{12,14},{14,12},{1,3},{3,1},... | collective-permute-start | bytes 589832 | tf_op jit(solution)/shard_map/ppermute | solution.py:302
  11.7 2.2 %load.1 = (bf16[1024,1024]{1,0:T(8,128)(2,1)S(1)}, bf16[1024,1024]{1,0:T(8,128)(2,1)S(1)}) custom-call(bf16[1024,1024]{1,0:T(8,128)(2,1)} %in_in.1, bf16[1024,1024]{1,0:T(8,128)(2,1)} %out_in.1), custom_call_target="tpu_custom_call" | custom-call | tf_op jit(solution)/shard_map/load/pallas_call | solution.py:25
  14.0 5.7 %collective-permute-done.13.refs_0_ = bf16[192,512]{1,0:T(8,128)(2,1)S(1)} collective-permute-done((bf16[192,512]{1,0:T(8,128)(2,1)S(1)}, bf16[192,512]{1,0:T(8,128)(2,1)S(1)}, u32[]{:S(2)}, u32[]{:S(2)}) %collective-permute-start.13) | collective-permute-done | bytes 196640 | tf_op jit(solution)/shard_map/ppermute | solution.py:307
  19.7 0.0 collective-permute-done.4.refs_2_.q_ref
  19.7 1.5 %collective-permute-start.14 = (bf16[192,512]{1,0:T(8,128)(2,1)S(1)}, bf16[192,512]{1,0:T(8,128)(2,1)S(1)}, u32[]{:S(2)}, u32[]{:S(2)}) collective-permute-start(bf16[192,512]{1,0:T(8,128)(2,1)S(1)} %after.8.p_ref), channel_id=1, source_target_pairs={{0,2},{2,0},{4,6},{6,4},{8,10},{10,8},{12,14},{14,12},{1,3},{3,1},... | collective-permute-start | bytes 589832 | tf_op jit(solution)/shard_map/ppermute | solution.py:302
  21.2 0.7 collective-permute-start.9
  21.9 2.8 %collective-permute-start.7 = (bf16[192,512]{1,0:T(8,128)(2,1)S(1)}, bf16[192,512]{1,0:T(8,128)(2,1)S(1)}, u32[]{:S(2)}, u32[]{:S(2)}) collective-permute-start(bf16[192,512]{1,0:T(8,128)(2,1)S(1)} %get-tuple-element.38), channel_id=1, source_target_pairs={{0,12},{2,14},{4,8},{6,10},{8,4},{10,6},{12,0},{14,2},{1,13},{3,15... | collective-permute-start | bytes 589832 | tf_op jit(solution)/shard_map/ppermute | solution.py:307
  24.7 0.0 collective-permute-start.15
  24.7 1.4 %collective-permute-done.14.q_ref = bf16[192,512]{1,0:T(8,128)(2,1)S(1)} collective-permute-done((bf16[192,512]{1,0:T(8,128)(2,1)S(1)}, bf16[192,512]{1,0:T(8,128)(2,1)S(1)}, u32[]{:S(2)}, u32[]{:S(2)}) %collective-permute-start.14) | collective-permute-done | bytes 196640 | tf_op jit(solution)/shard_map/ppermute | solution.py:302
  26.1 0.0 collective-permute-start.16
  26.1 1.1 %collective-permute-done.9.p_ref = bf16[192,512]{1,0:T(8,128)(2,1)S(1)} collective-permute-done((bf16[192,512]{1,0:T(8,128)(2,1)S(1)}, bf16[192,512]{1,0:T(8,128)(2,1)S(1)}, u32[]{:S(2)}, u32[]{:S(2)}) %collective-permute-start.9) | collective-permute-done | bytes 196640 | tf_op jit(solution)/shard_map/ppermute | solution.py:307
  27.2 0.6 collective-permute-start.10
  27.9 6.0 %collective-permute-done.7.p_ref = bf16[192,512]{1,0:T(8,128)(2,1)S(1)} collective-permute-done((bf16[192,512]{1,0:T(8,128)(2,1)S(1)}, bf16[192,512]{1,0:T(8,128)(2,1)S(1)}, u32[]{:S(2)}, u32[]{:S(2)}) %collective-permute-start.7) | collective-permute-done | bytes 196640 | tf_op jit(solution)/shard_map/ppermute | solution.py:307
  33.8 0.5 collective-permute-start.8
  34.4 1.8 %expert.4 = (f32[2,192,512]{2,1,0:T(8,128)S(1)}, bf16[2,192,512]{2,1,0:T(8,128)(2,1)S(1)}) custom-call(s32[1]{0:T(128)} %bitcast.core_ref, bf16[192,512]{1,0:T(8,128)(2,1)S(1)} %after.8.p_ref, bf16[192,512]{1,0:T(8,128)(2,1)S(1)} %collective-permute-done.14.q_ref, bf16[192,512]{1,0:T(8,128)(2,1)S(1)} %collective-permute-done.15.p2_ref, ...), custom_call_target="tpu_custom_call" | custom-call | tf_op jit(solution)/shard_map/expert/pallas_call | solution.py:25
  36.2 0.1 collective-permute-start.19
  36.3 3.5 %collective-permute-done.8.refs_0_ = bf16[192,512]{1,0:T(8,128)(2,1)S(1)} collective-permute-done((bf16[192,512]{1,0:T(8,128)(2,1)S(1)}, bf16[192,512]{1,0:T(8,128)(2,1)S(1)}, u32[]{:S(2)}, u32[]{:S(2)}) %collective-permute-start.8) | collective-permute-done | bytes 196640 | tf_op jit(solution)/shard_map/ppermute | solution.py:302
  39.8 0.5 collective-permute-start.11
  40.3 0.0 collective-permute-start.22
  40.3 0.5 collective-permute-start.23
  40.8 0.4 collective-permute-done.12.refs_0_
  41.2 0.3 collective-permute-done.11.p2_ref
  41.5 1.8 %expert.5 = (f32[2,192,512]{2,1,0:T(8,128)S(1)}, bf16[2,192,512]{2,1,0:T(8,128)(2,1)S(1)}) custom-call(s32[1]{0:T(128)} %bitcast.core_ref, bf16[192,512]{1,0:T(8,128)(2,1)S(1)} %collective-permute-done.7.p_ref, bf16[192,512]{1,0:T(8,128)(2,1)S(1)} %after.7.q_ref, bf16[192,512]{1,0:T(8,128)(2,1)S(1)} %collective-permute-done.11.p2_ref, ...), custom_call_target="tpu_custom_call" | custom-call | tf_op jit(solution)/shard_map/expert/pallas_call | solution.py:25
  43.4 0.3 collective-permute-start.17
  43.7 0.1 convert_add_fusion.2
  43.8 0.6 collective-permute-start.20
  44.4 0.7 collective-permute-done.17
  45.2 0.1 convert_add_fusion.3
  45.3 0.8 collective-permute-start.18
  46.1 5.5 %collective-permute-done.20 = bf16[192,512]{1,0:T(8,128)(2,1)S(1)} collective-permute-done((bf16[192,512]{1,0:T(8,128)(2,1)S(1)}, bf16[192,512]{1,0:T(8,128)(2,1)S(1)}, u32[]{:S(2)}, u32[]{:S(2)}) %collective-permute-start.20) | collective-permute-done | bytes 196640 | tf_op jit(solution)/shard_map/ppermute | solution.py:302
  51.6 3.7 %collective-permute-start.21 = (bf16[192,512]{1,0:T(8,128)(2,1)S(1)}, bf16[192,512]{1,0:T(8,128)(2,1)S(1)}, u32[]{:S(2)}, u32[]{:S(2)}) collective-permute-start(bf16[192,512]{1,0:T(8,128)(2,1)S(1)} %fusion.5.refs_1_), channel_id=1, source_target_pairs={{0,8},{2,10},{4,12},{6,14},{8,0},{10,2},{12,4},{14,6},{1,9},{3,11}... | collective-permute-start | bytes 589832 | tf_op jit(solution)/shard_map/ppermute | solution.py:307
  55.4 1.8 %expert.6 = (f32[2,192,512]{2,1,0:T(8,128)S(1)}, bf16[2,192,512]{2,1,0:T(8,128)(2,1)S(1)}) custom-call(s32[1]{0:T(128)} %bitcast.core_ref, bf16[192,512]{1,0:T(8,128)(2,1)S(1)} %collective-permute-done.9.p_ref, bf16[192,512]{1,0:T(8,128)(2,1)S(1)} %collective-permute-done.10.refs_1_.q_ref, bf16[192,512]{1,0:T(8,128)(2,1)S(1)} %collective-permute-done.22.p2_ref, ...), custom_call_target="tpu_custom_call" | custom-call | tf_op jit(solution)/shard_map/expert/pallas_call | solution.py:25
  57.2 0.1 collective-permute-start.25
  57.3 0.5 collective-permute-start.2
  57.8 0.1 collective-permute-start.5
  57.9 0.4 collective-permute-start.6
  58.3 5.0 %collective-permute-done.21.refs_1_.rest_2_ = bf16[192,512]{1,0:T(8,128)(2,1)S(1)} collective-permute-done((bf16[192,512]{1,0:T(8,128)(2,1)S(1)}, bf16[192,512]{1,0:T(8,128)(2,1)S(1)}, u32[]{:S(2)}, u32[]{:S(2)}) %collective-permute-start.21) | collective-permute-done | bytes 196640 | tf_op jit(solution)/shard_map/ppermute | solution.py:307
  63.3 2.7 %collective-permute-start.29 = (bf16[192,512]{1,0:T(8,128)(2,1)S(1)}, bf16[192,512]{1,0:T(8,128)(2,1)S(1)}, u32[]{:S(2)}, u32[]{:S(2)}) collective-permute-start(bf16[192,512]{1,0:T(8,128)(2,1)S(1)} %fusion.7.refs_1_), channel_id=1, source_target_pairs={{0,12},{2,14},{4,8},{6,10},{8,4},{10,6},{12,0},{14,2},{1,13},{3,15... | collective-permute-start | bytes 589832 | tf_op jit(solution)/shard_map/ppermute | solution.py:307
  66.0 1.8 %expert.7 = (f32[2,192,512]{2,1,0:T(8,128)S(1)}, bf16[2,192,512]{2,1,0:T(8,128)(2,1)S(1)}) custom-call(s32[1]{0:T(128)} %bitcast.core_ref, bf16[192,512]{1,0:T(8,128)(2,1)S(1)} %get-tuple-element.37.p_ref, bf16[192,512]{1,0:T(8,128)(2,1)S(1)} %collective-permute-done.4.refs_2_.q_ref, bf16[192,512]{1,0:T(8,128)(2,1)S(1)} %collective-permute-done.5.p2_ref, ...), custom_call_target="tpu_custom_call" | custom-call | tf_op jit(solution)/shard_map/expert/pallas_call | solution.py:25
  67.9 0.1 collective-permute-start.24
  68.0 0.1 convert_add_fusion
  68.1 0.6 collective-permute-start.27
  68.7 0.9 %collective-permute-done.24 = bf16[2,192,512]{2,1,0:T(8,128)(2,1)S(1)} collective-permute-done((bf16[2,192,512]{2,1,0:T(8,128)(2,1)S(1)}, bf16[2,192,512]{2,1,0:T(8,128)(2,1)S(1)}, u32[]{:S(2)}, u32[]{:S(2)}) %collective-permute-start.24) | collective-permute-done | bytes 393248 | tf_op jit(solution)/shard_map/ppermute | solution.py:297
  69.7 0.1 convert_add_fusion.1
  69.8 0.6 collective-permute-start.26
  70.5 5.4 %collective-permute-done.27 = bf16[192,512]{1,0:T(8,128)(2,1)S(1)} collective-permute-done((bf16[192,512]{1,0:T(8,128)(2,1)S(1)}, bf16[192,512]{1,0:T(8,128)(2,1)S(1)}, u32[]{:S(2)}, u32[]{:S(2)}) %collective-permute-start.27) | collective-permute-done | bytes 196640 | tf_op jit(solution)/shard_map/ppermute | solution.py:302
  75.9 0.1 collective-permute-start.28
  76.0 3.7 %collective-permute-done.26 = bf16[192,512]{1,0:T(8,128)(2,1)S(1)} collective-permute-done((bf16[192,512]{1,0:T(8,128)(2,1)S(1)}, bf16[192,512]{1,0:T(8,128)(2,1)S(1)}, u32[]{:S(2)}, u32[]{:S(2)}) %collective-permute-start.26) | collective-permute-done | bytes 196640 | tf_op jit(solution)/shard_map/ppermute | solution.py:302
  79.7 0.1 fusion.3.rest_0_
  79.8 2.3 %collective-permute-done.28.rest_1_ = bf16[192,512]{1,0:T(8,128)(2,1)S(1)} collective-permute-done((bf16[192,512]{1,0:T(8,128)(2,1)S(1)}, bf16[192,512]{1,0:T(8,128)(2,1)S(1)}, u32[]{:S(2)}, u32[]{:S(2)}) %collective-permute-start.28) | collective-permute-done | bytes 196640 | tf_op jit(solution)/shard_map/ppermute | solution.py:307
  82.1 0.9 %combine.1 = (f32[128,512]{1,0:T(8,128)S(1)}, bf16[128,512]{1,0:T(8,128)(2,1)S(1)}) custom-call(s32[1]{0:T(128)} %bitcast.core_ref, s32[1]{0:T(128)} %bitcast.5.line_ref, s32[2,2,128]{2,1,0:T(2,128)S(1)} %get-tuple-element.33.routes_ref, f32[2,128]{1,0:T(2,128)S(1)} %get-tuple-element.34.own_gates_ref, f32[2,128]{1,0:T(2,128)S(1)} %collective-permute-done.2.other_gates_ref, ...), custom_call_target="tpu_custom_call" | custom-call | tf_op jit(solution)/shard_map/combine/pallas_call | solution.py:25
  83.0 0.1 collective-permute-start.30
  83.1 1.3 %collective-permute-done.30.other_ref = bf16[128,512]{1,0:T(8,128)(2,1)S(1)} collective-permute-done((bf16[128,512]{1,0:T(8,128)(2,1)S(1)}, bf16[128,512]{1,0:T(8,128)(2,1)S(1)}, u32[]{:S(2)}, u32[]{:S(2)}) %collective-permute-start.30) | collective-permute-done | bytes 131104 | tf_op jit(solution)/shard_map/ppermute | solution.py:297
  84.5 0.8 finish.1
  (27 shorter events, 0.3 us)
Async XLA Ops:
  0.0 2.9 %collective-permute-start = (bf16[2,80,512]{2,1,0:T(8,128)(2,1)}, bf16[2,80,512]{2,1,0:T(8,128)(2,1)S(1)}, u32[]{:S(2)}, u32[]{:S(2)}) collective-permute-start(bf16[2,80,512]{2,1,0:T(8,128)(2,1)} %keys_in.1), channel_id=1, source_target_pairs={{0,1},{1,0},{2,3},{3,2},{4,5},{5,4},{6,7},{7,6},{8,9},{9,8},{10,11... | collective-permute-start | bytes 491528 | tf_op jit(solution)/shard_map/ppermute | solution.py:297
  0.5 2.5 %collective-permute-start.1 = (bf16[2,80,512]{2,1,0:T(8,128)(2,1)}, bf16[2,80,512]{2,1,0:T(8,128)(2,1)S(1)}, u32[]{:S(2)}, u32[]{:S(2)}) collective-permute-start(bf16[2,80,512]{2,1,0:T(8,128)(2,1)} %values_in.1), channel_id=1, source_target_pairs={{0,1},{1,0},{2,3},{3,2},{4,5},{5,4},{6,7},{7,6},{8,9},{9,8},{10,11... | collective-permute-start | bytes 491528 | tf_op jit(solution)/shard_map/ppermute | solution.py:297
  4.2 1.5 %collective-permute-start.3 = (bf16[128,512]{1,0:T(8,128)(2,1)S(1)}, bf16[128,512]{1,0:T(8,128)(2,1)S(1)}, u32[]{:S(2)}, u32[]{:S(2)}) collective-permute-start(bf16[128,512]{1,0:T(8,128)(2,1)S(1)} %get-tuple-element.36), channel_id=1, source_target_pairs={{0,1},{1,0},{2,3},{3,2},{4,5},{5,4},{6,7},{7,6},{8,9},{9,8},{10,11... | collective-permute-start | bytes 393224 | tf_op jit(solution)/shard_map/ppermute | solution.py:297
  6.2 13.4 %collective-permute-start.13 = (bf16[192,512]{1,0:T(8,128)(2,1)S(1)}, bf16[192,512]{1,0:T(8,128)(2,1)S(1)}, u32[]{:S(2)}, u32[]{:S(2)}) collective-permute-start(bf16[192,512]{1,0:T(8,128)(2,1)S(1)} %get-tuple-element.40), channel_id=1, source_target_pairs={{0,8},{2,10},{4,12},{6,14},{8,0},{10,2},{12,4},{14,6},{1,9},{3,11}... | collective-permute-start | bytes 589832 | tf_op jit(solution)/shard_map/ppermute | solution.py:307
  10.2 9.4 %collective-permute-start.4 = (bf16[192,512]{1,0:T(8,128)(2,1)S(1)}, bf16[192,512]{1,0:T(8,128)(2,1)S(1)}, u32[]{:S(2)}, u32[]{:S(2)}) collective-permute-start(bf16[192,512]{1,0:T(8,128)(2,1)S(1)} %get-tuple-element.37.p_ref), channel_id=1, source_target_pairs={{0,2},{2,0},{4,6},{6,4},{8,10},{10,8},{12,14},{14,12},{1,3},{3,1},... | collective-permute-start | bytes 589832 | tf_op jit(solution)/shard_map/ppermute | solution.py:302
  19.7 6.4 %collective-permute-start.14 = (bf16[192,512]{1,0:T(8,128)(2,1)S(1)}, bf16[192,512]{1,0:T(8,128)(2,1)S(1)}, u32[]{:S(2)}, u32[]{:S(2)}) collective-permute-start(bf16[192,512]{1,0:T(8,128)(2,1)S(1)} %after.8.p_ref), channel_id=1, source_target_pairs={{0,2},{2,0},{4,6},{6,4},{8,10},{10,8},{12,14},{14,12},{1,3},{3,1},... | collective-permute-start | bytes 589832 | tf_op jit(solution)/shard_map/ppermute | solution.py:302
  21.2 6.0 %collective-permute-start.9 = (bf16[192,512]{1,0:T(8,128)(2,1)S(1)}, bf16[192,512]{1,0:T(8,128)(2,1)S(1)}, u32[]{:S(2)}, u32[]{:S(2)}) collective-permute-start(bf16[192,512]{1,0:T(8,128)(2,1)S(1)} %get-tuple-element.39), channel_id=1, source_target_pairs={{0,4},{2,6},{4,0},{6,2},{8,12},{10,14},{12,8},{14,10},{1,5},{3,7},... | collective-permute-start | bytes 589832 | tf_op jit(solution)/shard_map/ppermute | solution.py:307
  21.9 11.9 %collective-permute-start.7 = (bf16[192,512]{1,0:T(8,128)(2,1)S(1)}, bf16[192,512]{1,0:T(8,128)(2,1)S(1)}, u32[]{:S(2)}, u32[]{:S(2)}) collective-permute-start(bf16[192,512]{1,0:T(8,128)(2,1)S(1)} %get-tuple-element.38), channel_id=1, source_target_pairs={{0,12},{2,14},{4,8},{6,10},{8,4},{10,6},{12,0},{14,2},{1,13},{3,15... | collective-permute-start | bytes 589832 | tf_op jit(solution)/shard_map/ppermute | solution.py:307
  24.7 9.7 %collective-permute-start.15 = (bf16[192,512]{1,0:T(8,128)(2,1)S(1)}, bf16[192,512]{1,0:T(8,128)(2,1)S(1)}, u32[]{:S(2)}, u32[]{:S(2)}) collective-permute-start(bf16[192,512]{1,0:T(8,128)(2,1)S(1)} %after.8.p_ref), channel_id=1, source_target_pairs={{0,1},{1,0},{2,3},{3,2},{4,5},{5,4},{6,7},{7,6},{8,9},{9,8},{10,11... | collective-permute-start | bytes 589832 | tf_op jit(solution)/shard_map/ppermute | solution.py:297
  26.1 8.3 %collective-permute-start.16 = (bf16[192,512]{1,0:T(8,128)(2,1)S(1)}, bf16[192,512]{1,0:T(8,128)(2,1)S(1)}, u32[]{:S(2)}, u32[]{:S(2)}) collective-permute-start(bf16[192,512]{1,0:T(8,128)(2,1)S(1)} %collective-permute-done.14.q_ref), channel_id=1, source_target_pairs={{0,1},{1,0},{2,3},{3,2},{4,5},{5,4},{6,7},{7,6},{8,9},{9,8},{10,11... | collective-permute-start | bytes 589832 | tf_op jit(solution)/shard_map/ppermute | solution.py:297
  27.2 9.1 %collective-permute-start.10 = (bf16[192,512]{1,0:T(8,128)(2,1)S(1)}, bf16[192,512]{1,0:T(8,128)(2,1)S(1)}, u32[]{:S(2)}, u32[]{:S(2)}) collective-permute-start(bf16[192,512]{1,0:T(8,128)(2,1)S(1)} %collective-permute-done.9.p_ref), channel_id=1, source_target_pairs={{0,2},{2,0},{4,6},{6,4},{8,10},{10,8},{12,14},{14,12},{1,3},{3,1},... | collective-permute-start | bytes 589832 | tf_op jit(solution)/shard_map/ppermute | solution.py:302
  33.8 5.9 %collective-permute-start.8 = (bf16[192,512]{1,0:T(8,128)(2,1)S(1)}, bf16[192,512]{1,0:T(8,128)(2,1)S(1)}, u32[]{:S(2)}, u32[]{:S(2)}) collective-permute-start(bf16[192,512]{1,0:T(8,128)(2,1)S(1)} %collective-permute-done.7.p_ref), channel_id=1, source_target_pairs={{0,2},{2,0},{4,6},{6,4},{8,10},{10,8},{12,14},{14,12},{1,3},{3,1},... | collective-permute-start | bytes 589832 | tf_op jit(solution)/shard_map/ppermute | solution.py:302
  36.2 7.4 %collective-permute-start.19 = (bf16[2,192,512]{2,1,0:T(8,128)(2,1)S(1)}, bf16[2,192,512]{2,1,0:T(8,128)(2,1)S(1)}, u32[]{:S(2)}, u32[]{:S(2)}) collective-permute-start(bf16[2,192,512]{2,1,0:T(8,128)(2,1)S(1)} %get-tuple-element.46), channel_id=1, source_target_pairs={{0,1},{1,0},{2,3},{3,2},{4,5},{5,4},{6,7},{7,6},{8,9},{9,8},{10,11... | collective-permute-start | bytes 1179656 | tf_op jit(solution)/shard_map/ppermute | solution.py:297
  39.8 1.4 %collective-permute-start.12 = (bf16[192,512]{1,0:T(8,128)(2,1)S(1)}, bf16[192,512]{1,0:T(8,128)(2,1)S(1)}, u32[]{:S(2)}, u32[]{:S(2)}) collective-permute-start(bf16[192,512]{1,0:T(8,128)(2,1)S(1)} %after.7.q_ref), channel_id=1, source_target_pairs={{0,1},{1,0},{2,3},{3,2},{4,5},{5,4},{6,7},{7,6},{8,9},{9,8},{10,11... | collective-permute-start | bytes 589832 | tf_op jit(solution)/shard_map/ppermute | solution.py:297
  39.8 1.7 %collective-permute-start.11 = (bf16[192,512]{1,0:T(8,128)(2,1)S(1)}, bf16[192,512]{1,0:T(8,128)(2,1)S(1)}, u32[]{:S(2)}, u32[]{:S(2)}) collective-permute-start(bf16[192,512]{1,0:T(8,128)(2,1)S(1)} %collective-permute-done.7.p_ref), channel_id=1, source_target_pairs={{0,1},{1,0},{2,3},{3,2},{4,5},{5,4},{6,7},{7,6},{8,9},{9,8},{10,11... | collective-permute-start | bytes 589832 | tf_op jit(solution)/shard_map/ppermute | solution.py:297
  40.3 15.1 %collective-permute-start.22 = (bf16[192,512]{1,0:T(8,128)(2,1)S(1)}, bf16[192,512]{1,0:T(8,128)(2,1)S(1)}, u32[]{:S(2)}, u32[]{:S(2)}) collective-permute-start(bf16[192,512]{1,0:T(8,128)(2,1)S(1)} %collective-permute-done.9.p_ref), channel_id=1, source_target_pairs={{0,1},{1,0},{2,3},{3,2},{4,5},{5,4},{6,7},{7,6},{8,9},{9,8},{10,11... | collective-permute-start | bytes 589832 | tf_op jit(solution)/shard_map/ppermute | solution.py:297
  40.3 15.1 %collective-permute-start.23 = (bf16[192,512]{1,0:T(8,128)(2,1)S(1)}, bf16[192,512]{1,0:T(8,128)(2,1)S(1)}, u32[]{:S(2)}, u32[]{:S(2)}) collective-permute-start(bf16[192,512]{1,0:T(8,128)(2,1)S(1)} %collective-permute-done.10.refs_1_.q_ref), channel_id=1, source_target_pairs={{0,1},{1,0},{2,3},{3,2},{4,5},{5,4},{6,7},{7,6},{8,9},{9,8},{10,11... | collective-permute-start | bytes 589832 | tf_op jit(solution)/shard_map/ppermute | solution.py:297
  43.4 1.8 %collective-permute-start.17 = (bf16[2,192,512]{2,1,0:T(8,128)(2,1)S(1)}, bf16[2,192,512]{2,1,0:T(8,128)(2,1)S(1)}, u32[]{:S(2)}, u32[]{:S(2)}) collective-permute-start(bf16[2,192,512]{2,1,0:T(8,128)(2,1)S(1)} %get-tuple-element.45), channel_id=1, source_target_pairs={{0,1},{1,0},{2,3},{3,2},{4,5},{5,4},{6,7},{7,6},{8,9},{9,8},{10,11... | collective-permute-start | bytes 1179656 | tf_op jit(solution)/shard_map/ppermute | solution.py:297
  43.8 7.8 %collective-permute-start.20 = (bf16[192,512]{1,0:T(8,128)(2,1)S(1)}, bf16[192,512]{1,0:T(8,128)(2,1)S(1)}, u32[]{:S(2)}, u32[]{:S(2)}) collective-permute-start(bf16[192,512]{1,0:T(8,128)(2,1)S(1)} %fusion.9), channel_id=1, source_target_pairs={{0,2},{2,0},{4,6},{6,4},{8,10},{10,8},{12,14},{14,12},{1,3},{3,1},... | collective-permute-start | bytes 589832 | tf_op jit(solution)/shard_map/ppermute | solution.py:302
  45.3 12.6 %collective-permute-start.18 = (bf16[192,512]{1,0:T(8,128)(2,1)S(1)}, bf16[192,512]{1,0:T(8,128)(2,1)S(1)}, u32[]{:S(2)}, u32[]{:S(2)}) collective-permute-start(bf16[192,512]{1,0:T(8,128)(2,1)S(1)} %fusion.8), channel_id=1, source_target_pairs={{0,2},{2,0},{4,6},{6,4},{8,10},{10,8},{12,14},{14,12},{1,3},{3,1},... | collective-permute-start | bytes 589832 | tf_op jit(solution)/shard_map/ppermute | solution.py:302
  51.6 11.6 %collective-permute-start.21 = (bf16[192,512]{1,0:T(8,128)(2,1)S(1)}, bf16[192,512]{1,0:T(8,128)(2,1)S(1)}, u32[]{:S(2)}, u32[]{:S(2)}) collective-permute-start(bf16[192,512]{1,0:T(8,128)(2,1)S(1)} %fusion.5.refs_1_), channel_id=1, source_target_pairs={{0,8},{2,10},{4,12},{6,14},{8,0},{10,2},{12,4},{14,6},{1,9},{3,11}... | collective-permute-start | bytes 589832 | tf_op jit(solution)/shard_map/ppermute | solution.py:307
  57.2 10.7 %collective-permute-start.25 = (bf16[2,192,512]{2,1,0:T(8,128)(2,1)S(1)}, bf16[2,192,512]{2,1,0:T(8,128)(2,1)S(1)}, u32[]{:S(2)}, u32[]{:S(2)}) collective-permute-start(bf16[2,192,512]{2,1,0:T(8,128)(2,1)S(1)} %get-tuple-element.50), channel_id=1, source_target_pairs={{0,1},{1,0},{2,3},{3,2},{4,5},{5,4},{6,7},{7,6},{8,9},{9,8},{10,11... | collective-permute-start | bytes 1179656 | tf_op jit(solution)/shard_map/ppermute | solution.py:297
  57.3 22.5 %collective-permute-start.2 = (f32[2,128]{1,0:T(2,128)S(1)}, f32[2,128]{1,0:T(2,128)S(1)}, u32[]{:S(2)}, u32[]{:S(2)}) collective-permute-start(f32[2,128]{1,0:T(2,128)S(1)} %get-tuple-element.34.own_gates_ref), channel_id=1, source_target_pairs={{0,1},{1,0},{2,3},{3,2},{4,5},{5,4},{6,7},{7,6},{8,9},{9,8},{10,11... | collective-permute-start | bytes 3080 | tf_op jit(solution)/shard_map/ppermute | solution.py:297
  57.8 8.2 %collective-permute-start.5 = (bf16[192,512]{1,0:T(8,128)(2,1)S(1)}, bf16[192,512]{1,0:T(8,128)(2,1)S(1)}, u32[]{:S(2)}, u32[]{:S(2)}) collective-permute-start(bf16[192,512]{1,0:T(8,128)(2,1)S(1)} %get-tuple-element.37.p_ref), channel_id=1, source_target_pairs={{0,1},{1,0},{2,3},{3,2},{4,5},{5,4},{6,7},{7,6},{8,9},{9,8},{10,11... | collective-permute-start | bytes 589832 | tf_op jit(solution)/shard_map/ppermute | solution.py:297
  57.9 8.1 %collective-permute-start.6 = (bf16[192,512]{1,0:T(8,128)(2,1)S(1)}, bf16[192,512]{1,0:T(8,128)(2,1)S(1)}, u32[]{:S(2)}, u32[]{:S(2)}) collective-permute-start(bf16[192,512]{1,0:T(8,128)(2,1)S(1)} %collective-permute-done.4.refs_2_.q_ref), channel_id=1, source_target_pairs={{0,1},{1,0},{2,3},{3,2},{4,5},{5,4},{6,7},{7,6},{8,9},{9,8},{10,11... | collective-permute-start | bytes 589832 | tf_op jit(solution)/shard_map/ppermute | solution.py:297
  63.3 16.4 %collective-permute-start.29 = (bf16[192,512]{1,0:T(8,128)(2,1)S(1)}, bf16[192,512]{1,0:T(8,128)(2,1)S(1)}, u32[]{:S(2)}, u32[]{:S(2)}) collective-permute-start(bf16[192,512]{1,0:T(8,128)(2,1)S(1)} %fusion.7.refs_1_), channel_id=1, source_target_pairs={{0,12},{2,14},{4,8},{6,10},{8,4},{10,6},{12,0},{14,2},{1,13},{3,15... | collective-permute-start | bytes 589832 | tf_op jit(solution)/shard_map/ppermute | solution.py:307
  67.9 1.8 %collective-permute-start.24 = (bf16[2,192,512]{2,1,0:T(8,128)(2,1)S(1)}, bf16[2,192,512]{2,1,0:T(8,128)(2,1)S(1)}, u32[]{:S(2)}, u32[]{:S(2)}) collective-permute-start(bf16[2,192,512]{2,1,0:T(8,128)(2,1)S(1)} %get-tuple-element.49), channel_id=1, source_target_pairs={{0,1},{1,0},{2,3},{3,2},{4,5},{5,4},{6,7},{7,6},{8,9},{9,8},{10,11... | collective-permute-start | bytes 1179656 | tf_op jit(solution)/shard_map/ppermute | solution.py:297
  68.1 7.8 %collective-permute-start.27 = (bf16[192,512]{1,0:T(8,128)(2,1)S(1)}, bf16[192,512]{1,0:T(8,128)(2,1)S(1)}, u32[]{:S(2)}, u32[]{:S(2)}) collective-permute-start(bf16[192,512]{1,0:T(8,128)(2,1)S(1)} %fusion.11.refs_1_), channel_id=1, source_target_pairs={{0,2},{2,0},{4,6},{6,4},{8,10},{10,8},{12,14},{14,12},{1,3},{3,1},... | collective-permute-start | bytes 589832 | tf_op jit(solution)/shard_map/ppermute | solution.py:302
  69.8 9.9 %collective-permute-start.26 = (bf16[192,512]{1,0:T(8,128)(2,1)S(1)}, bf16[192,512]{1,0:T(8,128)(2,1)S(1)}, u32[]{:S(2)}, u32[]{:S(2)}) collective-permute-start(bf16[192,512]{1,0:T(8,128)(2,1)S(1)} %after.13), channel_id=1, source_target_pairs={{0,2},{2,0},{4,6},{6,4},{8,10},{10,8},{12,14},{14,12},{1,3},{3,1},... | collective-permute-start | bytes 589832 | tf_op jit(solution)/shard_map/ppermute | solution.py:302
  75.9 6.2 %collective-permute-start.28 = (bf16[192,512]{1,0:T(8,128)(2,1)S(1)}, bf16[192,512]{1,0:T(8,128)(2,1)S(1)}, u32[]{:S(2)}, u32[]{:S(2)}) collective-permute-start(bf16[192,512]{1,0:T(8,128)(2,1)S(1)} %fusion.1), channel_id=1, source_target_pairs={{0,4},{2,6},{4,0},{6,2},{8,12},{10,14},{12,8},{14,10},{1,5},{3,7},... | collective-permute-start | bytes 589832 | tf_op jit(solution)/shard_map/ppermute | solution.py:307
  83.0 1.4 %collective-permute-start.30 = (bf16[128,512]{1,0:T(8,128)(2,1)S(1)}, bf16[128,512]{1,0:T(8,128)(2,1)S(1)}, u32[]{:S(2)}, u32[]{:S(2)}) collective-permute-start(bf16[128,512]{1,0:T(8,128)(2,1)S(1)} %get-tuple-element.52), channel_id=1, source_target_pairs={{0,1},{1,0},{2,3},{3,2},{4,5},{5,4},{6,7},{7,6},{8,9},{9,8},{10,11... | collective-permute-start | bytes 393224 | tf_op jit(solution)/shard_map/ppermute | solution.py:297

commit v14 on v13

--- a/solution.py
+++ b/solution.py
@@ -397,24 +397,22 @@
     )
     travelling = [exchange(selected[r], r) for r in range(1, count)]
     home = [None] * count
-    ps, qs, kept, halves, wholes = {}, {}, {}, {}, {}
-    for offset in [0, 2, 1, 3]:
+    ps, qs, kept, halves, wholes, boths = {}, {}, {}, {}, {}, {}
+    for offset in [0, 1, 2, 3]:
         p = travelling[offset - 1] if offset else selected[0]
         if offset == 2:
-            p = after(p, near_in, qs[0])
+            p = after(p, near_in)
         q = swap_owner(p)
-        if offset == 3:
-            q = after(q, qs[1])
         ps[offset], qs[offset] = p, q
-    for offset in [2, 3, 1, 0]:
+    for offset in [0, 1, 2, 3]:
         p, q = ps[offset], qs[offset]
         p2, q2 = swap(p), swap(q)
+        if offset == 1:
+            q2 = after(q2, kept[0])
+        if offset == 2:
+            q2 = after(q2, kept[0], kept[1])
         if offset == 3:
-            q2 = after(q2, kept[2])
-        if offset == 1:
-            q2 = after(q2, wholes[2], kept[3])
-        if offset == 0:
-            q2 = after(q2, wholes[3], kept[1])
+            q2 = after(q2, halves[2])
         kept[offset], sent = call(
             expert_kernel,
             "expert",
@@ -427,12 +425,14 @@
         moving = swap(sent)
         both = kept[offset] + moving.astype(jnp.float32)
         halves[offset] = both[1].astype(jnp.bfloat16)
-        leaving = halves[offset]
+        boths[offset] = both
+    for offset in [2, 3, 1, 0]:
+        both, leaving = boths[offset], halves[offset]
+        if offset == 1:
+            leaving = after(leaving, halves[3])
         if offset == 0:
-            leaving = after(leaving, halves[1])
+            leaving = after(leaving, wholes[3])
         across = swap_owner(leaving)
-        if offset == 3:
-            across = after(across, home[2])
         wholes[offset] = (both[0] + across.astype(jnp.float32)).astype(jnp.bfloat16)
         home[offset] = exchange(wholes[offset], offset) if offset else wholes[offset]
     own_sum, other_sum = call(

time: 85.4 us -> 72.1 us (0.84)
  waiting for transfers between devices: 44.3 us -> 26.4 us
  starting transfers between devices: 24.5 us -> 29 us
    ppermute x8, waiting for transfers between devices: 19.5 us -> 7.28 us  [swap_owner(): return lax.ppermute(values, 'expert', [(i, i ^ 1) for i in range(owners)])]
    ppermute x6, waiting for transfers between devices: 20.1 us -> 14.2 us  [exchange(): lax.ppermute(values, 'expert', [(i, i ^ 2 * offset) for i in range(owners)])]
    ppermute x6, starting transfers between devices: 14 us -> 16.2 us  [exchange(): lax.ppermute(values, 'expert', [(i, i ^ 2 * offset) for i in range(owners)])]
    ppermute x8, starting transfers between devices: 6.86 us -> 8.82 us  [swap_owner(): return lax.ppermute(values, 'expert', [(i, i ^ 1) for i in range(owners)])]
  transfers between devices with their start and end apart: 31 -> 31, of which waited for: 16 -> 13; matrix products, arithmetic and copies ran while one was open for 1% -> 1% of each run, Pallas kernels for 13% -> 16%
where the time goes in v14:
time: 72.1 us; the launch traced here: 71.9 us
  starting transfers between devices  29 us (40%)
  waiting for transfers between devices  26.4 us (37%)
  Pallas kernels  14.8 us (21%)
  between operations  0.9 us (1%)
    ppermute x6, starting transfers between devices, exchange(): lax.ppermute(values, 'expert', [(i, i ^ 2 * offset) for i in range(owners)])  16.2 us
    pallas_call x10, Pallas kernels, call(): pl.pallas_call(kernel, out_shape=tuple((jax.ShapeDtypeStruct(*out) for ou...  14.8 us
    ppermute x6, waiting for transfers between devices, exchange(): lax.ppermute(values, 'expert', [(i, i ^ 2 * offset) for i in range(owners)])  14.2 us
    ppermute x8, starting transfers between devices, swap_owner(): return lax.ppermute(values, 'expert', [(i, i ^ 1) for i in range(owners)])  8.82 us
    ppermute x8, waiting for transfers between devices, swap_owner(): return lax.ppermute(values, 'expert', [(i, i ^ 1) for i in range(owners)])  7.28 us
    ppermute x17, waiting for transfers between devices, swap(): return lax.ppermute(values, 'section', [(0, 1), (1, 0)])  4.95 us
    ppermute x17, starting transfers between devices, swap(): return lax.ppermute(values, 'section', [(0, 1), (1, 0)])  4.05 us
  transfers between devices with their start and end apart: 31, of which 13 were waited for; matrix products, arithmetic and copies ran while one was open for 1% of the time, Pallas kernels for 16%

profile of v14, /device:TPU:0, one launch (start us, length us, event | category | flops | bytes accessed | tf_op | source)
XLA Modules:
  0.0 71.9 jit_solution(11654320259099436910)
XLA Ops:
  0.0 0.5 collective-permute-start
  0.5 0.1 collective-permute-start.1
  1.2 1.8 %attend_own.1 = (bf16[128,512]{1,0:T(8,128)(2,1)S(1)}, bf16[128,512]{1,0:T(8,128)(2,1)S(1)}, bf16[128,512]{1,0:T(8,128)(2,1)S(1)}) custom-call(s32[1]{0:T(128)} %bitcast.core_ref, s32[1]{0:T(128)S(6)} %copy.24.source_ref, bf16[1,128,1024]{2,1,0:T(8,128)(2,1)} %x_in.1, f32[1,1024]{1,0:T(1,128)} %bitcast.40, bf16[2,80,512]{2,1,0:T(8,128)(2,1)} %keys_in.1, ...), custom_call_target="tpu_custom_call" | custom-call | tf_op jit(solution)/shard_map/attend_own/pallas_call | solution.py:25
  2.9 0.0 collective-permute-done.1.values_ref
  3.0 1.2 %attend_other.1 = (bf16[128,1024]{1,0:T(8,128)(2,1)S(1)}, bf16[128,512]{1,0:T(8,128)(2,1)S(1)}, bf16[128,512]{1,0:T(8,128)(2,1)S(1)}, f32[2,128]{1,0:T(2,128)S(1)}, s32[2,2,128]{2,1,0:T(2,128)S(1)}) custom-call(s32[1]{0:T(128)} %bitcast.core_ref, s32[1]{0:T(128)S(6)} %copy.24.source_ref, bf16[128,512]{1,0:T(8,128)(2,1)S(1)} %get-tuple-element.29.own_ref, ...), custom_call_target="tpu_custom_call" | custom-call | tf_op jit(solution)/shard_map/attend_other/pallas_call | solution.py:25
  4.2 0.5 collective-permute-start.3
  4.7 1.0 %collective-permute-done.3.other_ref = bf16[128,512]{1,0:T(8,128)(2,1)S(1)} collective-permute-done((bf16[128,512]{1,0:T(8,128)(2,1)S(1)}, bf16[128,512]{1,0:T(8,128)(2,1)S(1)}, u32[]{:S(2)}, u32[]{:S(2)}) %collective-permute-start.3) | collective-permute-done | bytes 131104 | tf_op jit(solution)/shard_map/ppermute | solution.py:297
  5.7 0.5 select.5
  6.2 3.0 %collective-permute-start.16 = (bf16[192,512]{1,0:T(8,128)(2,1)S(1)}, bf16[192,512]{1,0:T(8,128)(2,1)S(1)}, u32[]{:S(2)}, u32[]{:S(2)}) collective-permute-start(bf16[192,512]{1,0:T(8,128)(2,1)S(1)} %get-tuple-element.44), channel_id=1, source_target_pairs={{0,4},{2,6},{4,0},{6,2},{8,12},{10,14},{12,8},{14,10},{1,5},{3,7},... | collective-permute-start | bytes 589832 | tf_op jit(solution)/shard_map/ppermute | solution.py:307
  9.2 1.5 %collective-permute-start.4 = (bf16[192,512]{1,0:T(8,128)(2,1)S(1)}, bf16[192,512]{1,0:T(8,128)(2,1)S(1)}, u32[]{:S(2)}, u32[]{:S(2)}) collective-permute-start(bf16[192,512]{1,0:T(8,128)(2,1)S(1)} %get-tuple-element.37.p_ref), channel_id=1, source_target_pairs={{0,2},{2,0},{4,6},{6,4},{8,10},{10,8},{12,14},{14,12},{1,3},{3,1},... | collective-permute-start | bytes 589832 | tf_op jit(solution)/shard_map/ppermute | solution.py:302
  10.7 2.6 %collective-permute-start.12 = (bf16[192,512]{1,0:T(8,128)(2,1)S(1)}, bf16[192,512]{1,0:T(8,128)(2,1)S(1)}, u32[]{:S(2)}, u32[]{:S(2)}) collective-permute-start(bf16[192,512]{1,0:T(8,128)(2,1)S(1)} %get-tuple-element.43), channel_id=1, source_target_pairs={{0,8},{2,10},{4,12},{6,14},{8,0},{10,2},{12,4},{14,6},{1,9},{3,11}... | collective-permute-start | bytes 589832 | tf_op jit(solution)/shard_map/ppermute | solution.py:307
  13.3 3.7 %collective-permute-done.16.p_ref = bf16[192,512]{1,0:T(8,128)(2,1)S(1)} collective-permute-done((bf16[192,512]{1,0:T(8,128)(2,1)S(1)}, bf16[192,512]{1,0:T(8,128)(2,1)S(1)}, u32[]{:S(2)}, u32[]{:S(2)}) %collective-permute-start.16) | collective-permute-done | bytes 196640 | tf_op jit(solution)/shard_map/ppermute | solution.py:307
  17.0 3.0 %collective-permute-start.17 = (bf16[192,512]{1,0:T(8,128)(2,1)S(1)}, bf16[192,512]{1,0:T(8,128)(2,1)S(1)}, u32[]{:S(2)}, u32[]{:S(2)}) collective-permute-start(bf16[192,512]{1,0:T(8,128)(2,1)S(1)} %collective-permute-done.16.p_ref), channel_id=1, source_target_pairs={{0,2},{2,0},{4,6},{6,4},{8,10},{10,8},{12,14},{14,12},{1,3},{3,1},... | collective-permute-start | bytes 589832 | tf_op jit(solution)/shard_map/ppermute | solution.py:302
  19.9 0.0 collective-permute-start.5
  20.0 0.0 collective-permute-done.4.q_ref
  20.0 0.5 collective-permute-start.6
  20.5 2.2 %load.1 = (bf16[1024,1024]{1,0:T(8,128)(2,1)S(1)}, bf16[1024,1024]{1,0:T(8,128)(2,1)S(1)}) custom-call(bf16[1024,1024]{1,0:T(8,128)(2,1)} %in_in.1, bf16[1024,1024]{1,0:T(8,128)(2,1)} %out_in.1), custom_call_target="tpu_custom_call" | custom-call | tf_op jit(solution)/shard_map/load/pallas_call | solution.py:25
  22.7 2.6 %collective-permute-start.8 = (bf16[192,512]{1,0:T(8,128)(2,1)S(1)}, bf16[192,512]{1,0:T(8,128)(2,1)S(1)}, u32[]{:S(2)}, u32[]{:S(2)}) collective-permute-start(bf16[192,512]{1,0:T(8,128)(2,1)S(1)} %get-tuple-element.42), channel_id=1, source_target_pairs={{0,12},{2,14},{4,8},{6,10},{8,4},{10,6},{12,0},{14,2},{1,13},{3,15... | collective-permute-start | bytes 589832 | tf_op jit(solution)/shard_map/ppermute | solution.py:307
  25.3 0.0 collective-permute-done.12.refs_0_
  25.3 0.0 collective-permute-start.13
  25.3 0.1 collective-permute-start.19
  25.4 0.0 collective-permute-done.6.q2_ref
  25.4 1.8 %expert.4 = (f32[2,192,512]{2,1,0:T(8,128)S(1)}, bf16[2,192,512]{2,1,0:T(8,128)(2,1)S(1)}) custom-call(s32[1]{0:T(128)} %bitcast.core_ref, bf16[192,512]{1,0:T(8,128)(2,1)S(1)} %get-tuple-element.37.p_ref, bf16[192,512]{1,0:T(8,128)(2,1)S(1)} %collective-permute-done.4.q_ref, bf16[192,512]{1,0:T(8,128)(2,1)S(1)} %collective-permute-done.5.p2_ref, ...), custom_call_target="tpu_custom_call" | custom-call | tf_op jit(solution)/shard_map/expert/pallas_call | solution.py:25
  27.2 0.5 collective-permute-start.7
  27.8 0.1 collective-permute-start.18
  27.9 3.6 %collective-permute-done.8.p_ref = bf16[192,512]{1,0:T(8,128)(2,1)S(1)} collective-permute-done((bf16[192,512]{1,0:T(8,128)(2,1)S(1)}, bf16[192,512]{1,0:T(8,128)(2,1)S(1)}, u32[]{:S(2)}, u32[]{:S(2)}) %collective-permute-start.8) | collective-permute-done | bytes 196640 | tf_op jit(solution)/shard_map/ppermute | solution.py:307
  31.5 0.1 collective-permute-start.9
  31.6 0.2 collective-permute-done.13.q_ref
  31.8 0.0 collective-permute-start.15
  31.8 0.5 collective-permute-start.14
  32.3 0.0 collective-permute-done.18.p2_ref
  32.3 0.1 collective-permute-start.2
  32.4 1.8 %expert.5 = (f32[2,192,512]{2,1,0:T(8,128)S(1)}, bf16[2,192,512]{2,1,0:T(8,128)(2,1)S(1)}) custom-call(s32[1]{0:T(128)} %bitcast.core_ref, bf16[192,512]{1,0:T(8,128)(2,1)S(1)} %collective-permute-done.16.p_ref, bf16[192,512]{1,0:T(8,128)(2,1)S(1)} %collective-permute-done.17.q_ref, bf16[192,512]{1,0:T(8,128)(2,1)S(1)} %collective-permute-done.18.p2_ref, ...), custom_call_target="tpu_custom_call" | custom-call | tf_op jit(solution)/shard_map/expert/pallas_call | solution.py:25
  34.2 3.2 %collective-permute-done.9.q_ref = bf16[192,512]{1,0:T(8,128)(2,1)S(1)} collective-permute-done((bf16[192,512]{1,0:T(8,128)(2,1)S(1)}, bf16[192,512]{1,0:T(8,128)(2,1)S(1)}, u32[]{:S(2)}, u32[]{:S(2)}) %collective-permute-start.9) | collective-permute-done | bytes 196640 | tf_op jit(solution)/shard_map/ppermute | solution.py:302
  37.4 0.0 collective-permute-start.10
  37.4 0.0 collective-permute-done.15.refs_0_
  37.4 0.5 collective-permute-start.11
  37.9 1.8 %expert.6 = (f32[2,192,512]{2,1,0:T(8,128)S(1)}, bf16[2,192,512]{2,1,0:T(8,128)(2,1)S(1)}) custom-call(s32[1]{0:T(128)} %bitcast.core_ref, bf16[192,512]{1,0:T(8,128)(2,1)S(1)} %after.6.p_ref, bf16[192,512]{1,0:T(8,128)(2,1)S(1)} %collective-permute-done.13.q_ref, bf16[192,512]{1,0:T(8,128)(2,1)S(1)} %collective-permute-done.14.p2_ref, ...), custom_call_target="tpu_custom_call" | custom-call | tf_op jit(solution)/shard_map/expert/pallas_call | solution.py:25
  39.8 0.1 collective-permute-start.20
  39.8 0.5 collective-permute-start.24
  40.3 0.1 convert_add_fusion.3
  40.5 1.1 %collective-permute-done.20 = bf16[2,192,512]{2,1,0:T(8,128)(2,1)S(1)} collective-permute-done((bf16[2,192,512]{2,1,0:T(8,128)(2,1)S(1)}, bf16[2,192,512]{2,1,0:T(8,128)(2,1)S(1)}, u32[]{:S(2)}, u32[]{:S(2)}) %collective-permute-start.20) | collective-permute-done | bytes 393248 | tf_op jit(solution)/shard_map/ppermute | solution.py:297
  41.5 0.1 convert_add_fusion.2
  41.7 0.3 collective-permute-start.27
  42.1 1.8 %expert.7 = (f32[2,192,512]{2,1,0:T(8,128)S(1)}, bf16[2,192,512]{2,1,0:T(8,128)(2,1)S(1)}) custom-call(s32[1]{0:T(128)} %bitcast.core_ref, bf16[192,512]{1,0:T(8,128)(2,1)S(1)} %collective-permute-done.8.p_ref, bf16[192,512]{1,0:T(8,128)(2,1)S(1)} %collective-permute-done.9.q_ref, bf16[192,512]{1,0:T(8,128)(2,1)S(1)} %collective-permute-done.10.p2_ref, ...), custom_call_target="tpu_custom_call" | custom-call | tf_op jit(solution)/shard_map/expert/pallas_call | solution.py:25
  43.9 0.1 collective-permute-start.21
  44.0 0.1 convert_add_fusion
  44.2 1.5 %collective-permute-done.21 = bf16[2,192,512]{2,1,0:T(8,128)(2,1)S(1)} collective-permute-done((bf16[2,192,512]{2,1,0:T(8,128)(2,1)S(1)}, bf16[2,192,512]{2,1,0:T(8,128)(2,1)S(1)}, u32[]{:S(2)}, u32[]{:S(2)}) %collective-permute-start.21) | collective-permute-done | bytes 393248 | tf_op jit(solution)/shard_map/ppermute | solution.py:297
  45.7 0.1 convert_add_fusion.1
  45.8 1.8 %collective-permute-start.22 = (bf16[192,512]{1,0:T(8,128)(2,1)S(1)}, bf16[192,512]{1,0:T(8,128)(2,1)S(1)}, u32[]{:S(2)}, u32[]{:S(2)}) collective-permute-start(bf16[192,512]{1,0:T(8,128)(2,1)S(1)} %fusion.10.refs_1_), channel_id=1, source_target_pairs={{0,2},{2,0},{4,6},{6,4},{8,10},{10,8},{12,14},{14,12},{1,3},{3,1},... | collective-permute-start | bytes 589832 | tf_op jit(solution)/shard_map/ppermute | solution.py:302
  47.7 1.1 %collective-permute-done.27 = bf16[192,512]{1,0:T(8,128)(2,1)S(1)} collective-permute-done((bf16[192,512]{1,0:T(8,128)(2,1)S(1)}, bf16[192,512]{1,0:T(8,128)(2,1)S(1)}, u32[]{:S(2)}, u32[]{:S(2)}) %collective-permute-start.27) | collective-permute-done | bytes 196640 | tf_op jit(solution)/shard_map/ppermute | solution.py:302
  48.8 3.0 %collective-permute-start.28 = (bf16[192,512]{1,0:T(8,128)(2,1)S(1)}, bf16[192,512]{1,0:T(8,128)(2,1)S(1)}, u32[]{:S(2)}, u32[]{:S(2)}) collective-permute-start(bf16[192,512]{1,0:T(8,128)(2,1)S(1)} %fusion.1), channel_id=1, source_target_pairs={{0,8},{2,10},{4,12},{6,14},{8,0},{10,2},{12,4},{14,6},{1,9},{3,11}... | collective-permute-start | bytes 589832 | tf_op jit(solution)/shard_map/ppermute | solution.py:307
  51.8 0.3 collective-permute-start.25
  52.0 0.9 %collective-permute-done.22 = bf16[192,512]{1,0:T(8,128)(2,1)S(1)} collective-permute-done((bf16[192,512]{1,0:T(8,128)(2,1)S(1)}, bf16[192,512]{1,0:T(8,128)(2,1)S(1)}, u32[]{:S(2)}, u32[]{:S(2)}) %collective-permute-start.22) | collective-permute-done | bytes 196640 | tf_op jit(solution)/shard_map/ppermute | solution.py:302
  53.0 3.2 %collective-permute-start.29 = (bf16[192,512]{1,0:T(8,128)(2,1)S(1)}, bf16[192,512]{1,0:T(8,128)(2,1)S(1)}, u32[]{:S(2)}, u32[]{:S(2)}) collective-permute-start(bf16[192,512]{1,0:T(8,128)(2,1)S(1)} %fusion.5.refs_1_), channel_id=1, source_target_pairs={{0,12},{2,14},{4,8},{6,10},{8,4},{10,6},{12,0},{14,2},{1,13},{3,15... | collective-permute-start | bytes 589832 | tf_op jit(solution)/shard_map/ppermute | solution.py:307
  56.2 1.8 %collective-permute-start.23 = (bf16[192,512]{1,0:T(8,128)(2,1)S(1)}, bf16[192,512]{1,0:T(8,128)(2,1)S(1)}, u32[]{:S(2)}, u32[]{:S(2)}) collective-permute-start(bf16[192,512]{1,0:T(8,128)(2,1)S(1)} %after.10), channel_id=1, source_target_pairs={{0,2},{2,0},{4,6},{6,4},{8,10},{10,8},{12,14},{14,12},{1,3},{3,1},... | collective-permute-start | bytes 589832 | tf_op jit(solution)/shard_map/ppermute | solution.py:302
  58.1 1.8 %collective-permute-start.26 = (bf16[192,512]{1,0:T(8,128)(2,1)S(1)}, bf16[192,512]{1,0:T(8,128)(2,1)S(1)}, u32[]{:S(2)}, u32[]{:S(2)}) collective-permute-start(bf16[192,512]{1,0:T(8,128)(2,1)S(1)} %fusion.3), channel_id=1, source_target_pairs={{0,4},{2,6},{4,0},{6,2},{8,12},{10,14},{12,8},{14,10},{1,5},{3,7},... | collective-permute-start | bytes 589832 | tf_op jit(solution)/shard_map/ppermute | solution.py:307
  59.9 1.9 %collective-permute-done.23 = bf16[192,512]{1,0:T(8,128)(2,1)S(1)} collective-permute-done((bf16[192,512]{1,0:T(8,128)(2,1)S(1)}, bf16[192,512]{1,0:T(8,128)(2,1)S(1)}, u32[]{:S(2)}, u32[]{:S(2)}) %collective-permute-start.23) | collective-permute-done | bytes 196640 | tf_op jit(solution)/shard_map/ppermute | solution.py:302
  61.9 3.9 %collective-permute-done.28.rest_2_ = bf16[192,512]{1,0:T(8,128)(2,1)S(1)} collective-permute-done((bf16[192,512]{1,0:T(8,128)(2,1)S(1)}, bf16[192,512]{1,0:T(8,128)(2,1)S(1)}, u32[]{:S(2)}, u32[]{:S(2)}) %collective-permute-start.28) | collective-permute-done | bytes 196640 | tf_op jit(solution)/shard_map/ppermute | solution.py:307
  65.8 3.0 %collective-permute-done.26.rest_1_ = bf16[192,512]{1,0:T(8,128)(2,1)S(1)} collective-permute-done((bf16[192,512]{1,0:T(8,128)(2,1)S(1)}, bf16[192,512]{1,0:T(8,128)(2,1)S(1)}, u32[]{:S(2)}, u32[]{:S(2)}) %collective-permute-start.26) | collective-permute-done | bytes 196640 | tf_op jit(solution)/shard_map/ppermute | solution.py:307
  68.8 0.9 %combine.1 = (f32[128,512]{1,0:T(8,128)S(1)}, bf16[128,512]{1,0:T(8,128)(2,1)S(1)}) custom-call(s32[1]{0:T(128)} %bitcast.core_ref, s32[1]{0:T(128)} %bitcast.5.line_ref, s32[2,2,128]{2,1,0:T(2,128)S(1)} %get-tuple-element.33.routes_ref, f32[2,128]{1,0:T(2,128)S(1)} %get-tuple-element.34.own_gates_ref, f32[2,128]{1,0:T(2,128)S(1)} %collective-permute-done.2.other_gates_ref, ...), custom_call_target="tpu_custom_call" | custom-call | tf_op jit(solution)/shard_map/combine/pallas_call | solution.py:25
  69.7 0.1 collective-permute-start.30
  69.8 1.3 %collective-permute-done.30.other_ref = bf16[128,512]{1,0:T(8,128)(2,1)S(1)} collective-permute-done((bf16[128,512]{1,0:T(8,128)(2,1)S(1)}, bf16[128,512]{1,0:T(8,128)(2,1)S(1)}, u32[]{:S(2)}, u32[]{:S(2)}) %collective-permute-start.30) | collective-permute-done | bytes 131104 | tf_op jit(solution)/shard_map/ppermute | solution.py:297
  71.1 0.8 %finish.1 = bf16[128,1024]{1,0:T(8,128)(2,1)} custom-call(s32[1]{0:T(128)} %bitcast.core_ref, bf16[128,1024]{1,0:T(8,128)(2,1)S(1)} %get-tuple-element.32.state_ref, f32[128,512]{1,0:T(8,128)S(1)} %get-tuple-element.51.own_ref, bf16[128,512]{1,0:T(8,128)(2,1)S(1)} %collective-permute-done.30.other_ref), custom_call_target="tpu_custom_call" | custom-call | tf_op jit(solution)/shard_map/finish/pallas_call | solution.py:25
  (26 shorter events, 0.3 us)
Async XLA Ops:
  0.0 2.9 %collective-permute-start = (bf16[2,80,512]{2,1,0:T(8,128)(2,1)}, bf16[2,80,512]{2,1,0:T(8,128)(2,1)S(1)}, u32[]{:S(2)}, u32[]{:S(2)}) collective-permute-start(bf16[2,80,512]{2,1,0:T(8,128)(2,1)} %keys_in.1), channel_id=1, source_target_pairs={{0,1},{1,0},{2,3},{3,2},{4,5},{5,4},{6,7},{7,6},{8,9},{9,8},{10,11... | collective-permute-start | bytes 491528 | tf_op jit(solution)/shard_map/ppermute | solution.py:297
  0.5 2.5 %collective-permute-start.1 = (bf16[2,80,512]{2,1,0:T(8,128)(2,1)}, bf16[2,80,512]{2,1,0:T(8,128)(2,1)S(1)}, u32[]{:S(2)}, u32[]{:S(2)}) collective-permute-start(bf16[2,80,512]{2,1,0:T(8,128)(2,1)} %values_in.1), channel_id=1, source_target_pairs={{0,1},{1,0},{2,3},{3,2},{4,5},{5,4},{6,7},{7,6},{8,9},{9,8},{10,11... | collective-permute-start | bytes 491528 | tf_op jit(solution)/shard_map/ppermute | solution.py:297
  4.2 1.5 %collective-permute-start.3 = (bf16[128,512]{1,0:T(8,128)(2,1)S(1)}, bf16[128,512]{1,0:T(8,128)(2,1)S(1)}, u32[]{:S(2)}, u32[]{:S(2)}) collective-permute-start(bf16[128,512]{1,0:T(8,128)(2,1)S(1)} %get-tuple-element.36), channel_id=1, source_target_pairs={{0,1},{1,0},{2,3},{3,2},{4,5},{5,4},{6,7},{7,6},{8,9},{9,8},{10,11... | collective-permute-start | bytes 393224 | tf_op jit(solution)/shard_map/ppermute | solution.py:297
  6.2 10.8 %collective-permute-start.16 = (bf16[192,512]{1,0:T(8,128)(2,1)S(1)}, bf16[192,512]{1,0:T(8,128)(2,1)S(1)}, u32[]{:S(2)}, u32[]{:S(2)}) collective-permute-start(bf16[192,512]{1,0:T(8,128)(2,1)S(1)} %get-tuple-element.44), channel_id=1, source_target_pairs={{0,4},{2,6},{4,0},{6,2},{8,12},{10,14},{12,8},{14,10},{1,5},{3,7},... | collective-permute-start | bytes 589832 | tf_op jit(solution)/shard_map/ppermute | solution.py:307
  9.2 10.7 %collective-permute-start.4 = (bf16[192,512]{1,0:T(8,128)(2,1)S(1)}, bf16[192,512]{1,0:T(8,128)(2,1)S(1)}, u32[]{:S(2)}, u32[]{:S(2)}) collective-permute-start(bf16[192,512]{1,0:T(8,128)(2,1)S(1)} %get-tuple-element.37.p_ref), channel_id=1, source_target_pairs={{0,2},{2,0},{4,6},{6,4},{8,10},{10,8},{12,14},{14,12},{1,3},{3,1},... | collective-permute-start | bytes 589832 | tf_op jit(solution)/shard_map/ppermute | solution.py:302
  10.7 14.5 %collective-permute-start.12 = (bf16[192,512]{1,0:T(8,128)(2,1)S(1)}, bf16[192,512]{1,0:T(8,128)(2,1)S(1)}, u32[]{:S(2)}, u32[]{:S(2)}) collective-permute-start(bf16[192,512]{1,0:T(8,128)(2,1)S(1)} %get-tuple-element.43), channel_id=1, source_target_pairs={{0,8},{2,10},{4,12},{6,14},{8,0},{10,2},{12,4},{14,6},{1,9},{3,11}... | collective-permute-start | bytes 589832 | tf_op jit(solution)/shard_map/ppermute | solution.py:307
  17.0 8.3 %collective-permute-start.17 = (bf16[192,512]{1,0:T(8,128)(2,1)S(1)}, bf16[192,512]{1,0:T(8,128)(2,1)S(1)}, u32[]{:S(2)}, u32[]{:S(2)}) collective-permute-start(bf16[192,512]{1,0:T(8,128)(2,1)S(1)} %collective-permute-done.16.p_ref), channel_id=1, source_target_pairs={{0,2},{2,0},{4,6},{6,4},{8,10},{10,8},{12,14},{14,12},{1,3},{3,1},... | collective-permute-start | bytes 589832 | tf_op jit(solution)/shard_map/ppermute | solution.py:302
  19.9 5.4 %collective-permute-start.5 = (bf16[192,512]{1,0:T(8,128)(2,1)S(1)}, bf16[192,512]{1,0:T(8,128)(2,1)S(1)}, u32[]{:S(2)}, u32[]{:S(2)}) collective-permute-start(bf16[192,512]{1,0:T(8,128)(2,1)S(1)} %get-tuple-element.37.p_ref), channel_id=1, source_target_pairs={{0,1},{1,0},{2,3},{3,2},{4,5},{5,4},{6,7},{7,6},{8,9},{9,8},{10,11... | collective-permute-start | bytes 589832 | tf_op jit(solution)/shard_map/ppermute | solution.py:297
  20.0 5.4 %collective-permute-start.6 = (bf16[192,512]{1,0:T(8,128)(2,1)S(1)}, bf16[192,512]{1,0:T(8,128)(2,1)S(1)}, u32[]{:S(2)}, u32[]{:S(2)}) collective-permute-start(bf16[192,512]{1,0:T(8,128)(2,1)S(1)} %collective-permute-done.4.q_ref), channel_id=1, source_target_pairs={{0,1},{1,0},{2,3},{3,2},{4,5},{5,4},{6,7},{7,6},{8,9},{9,8},{10,11... | collective-permute-start | bytes 589832 | tf_op jit(solution)/shard_map/ppermute | solution.py:297
  22.7 8.8 %collective-permute-start.8 = (bf16[192,512]{1,0:T(8,128)(2,1)S(1)}, bf16[192,512]{1,0:T(8,128)(2,1)S(1)}, u32[]{:S(2)}, u32[]{:S(2)}) collective-permute-start(bf16[192,512]{1,0:T(8,128)(2,1)S(1)} %get-tuple-element.42), channel_id=1, source_target_pairs={{0,12},{2,14},{4,8},{6,10},{8,4},{10,6},{12,0},{14,2},{1,13},{3,15... | collective-permute-start | bytes 589832 | tf_op jit(solution)/shard_map/ppermute | solution.py:307
  25.3 6.5 %collective-permute-start.13 = (bf16[192,512]{1,0:T(8,128)(2,1)S(1)}, bf16[192,512]{1,0:T(8,128)(2,1)S(1)}, u32[]{:S(2)}, u32[]{:S(2)}) collective-permute-start(bf16[192,512]{1,0:T(8,128)(2,1)S(1)} %after.6.p_ref), channel_id=1, source_target_pairs={{0,2},{2,0},{4,6},{6,4},{8,10},{10,8},{12,14},{14,12},{1,3},{3,1},... | collective-permute-start | bytes 589832 | tf_op jit(solution)/shard_map/ppermute | solution.py:302
  25.3 6.5 %collective-permute-start.19 = (bf16[192,512]{1,0:T(8,128)(2,1)S(1)}, bf16[192,512]{1,0:T(8,128)(2,1)S(1)}, u32[]{:S(2)}, u32[]{:S(2)}) collective-permute-start(bf16[192,512]{1,0:T(8,128)(2,1)S(1)} %collective-permute-done.17.q_ref), channel_id=1, source_target_pairs={{0,1},{1,0},{2,3},{3,2},{4,5},{5,4},{6,7},{7,6},{8,9},{9,8},{10,11... | collective-permute-start | bytes 589832 | tf_op jit(solution)/shard_map/ppermute | solution.py:297
  27.2 12.6 %collective-permute-start.7 = (bf16[2,192,512]{2,1,0:T(8,128)(2,1)S(1)}, bf16[2,192,512]{2,1,0:T(8,128)(2,1)S(1)}, u32[]{:S(2)}, u32[]{:S(2)}) collective-permute-start(bf16[2,192,512]{2,1,0:T(8,128)(2,1)S(1)} %get-tuple-element.41), channel_id=1, source_target_pairs={{0,1},{1,0},{2,3},{3,2},{4,5},{5,4},{6,7},{7,6},{8,9},{9,8},{10,11... | collective-permute-start | bytes 1179656 | tf_op jit(solution)/shard_map/ppermute | solution.py:297
  27.8 4.5 %collective-permute-start.18 = (bf16[192,512]{1,0:T(8,128)(2,1)S(1)}, bf16[192,512]{1,0:T(8,128)(2,1)S(1)}, u32[]{:S(2)}, u32[]{:S(2)}) collective-permute-start(bf16[192,512]{1,0:T(8,128)(2,1)S(1)} %collective-permute-done.16.p_ref), channel_id=1, source_target_pairs={{0,1},{1,0},{2,3},{3,2},{4,5},{5,4},{6,7},{7,6},{8,9},{9,8},{10,11... | collective-permute-start | bytes 589832 | tf_op jit(solution)/shard_map/ppermute | solution.py:297
  31.5 5.9 %collective-permute-start.9 = (bf16[192,512]{1,0:T(8,128)(2,1)S(1)}, bf16[192,512]{1,0:T(8,128)(2,1)S(1)}, u32[]{:S(2)}, u32[]{:S(2)}) collective-permute-start(bf16[192,512]{1,0:T(8,128)(2,1)S(1)} %collective-permute-done.8.p_ref), channel_id=1, source_target_pairs={{0,2},{2,0},{4,6},{6,4},{8,10},{10,8},{12,14},{14,12},{1,3},{3,1},... | collective-permute-start | bytes 589832 | tf_op jit(solution)/shard_map/ppermute | solution.py:302
  31.8 5.6 %collective-permute-start.15 = (bf16[192,512]{1,0:T(8,128)(2,1)S(1)}, bf16[192,512]{1,0:T(8,128)(2,1)S(1)}, u32[]{:S(2)}, u32[]{:S(2)}) collective-permute-start(bf16[192,512]{1,0:T(8,128)(2,1)S(1)} %collective-permute-done.13.q_ref), channel_id=1, source_target_pairs={{0,1},{1,0},{2,3},{3,2},{4,5},{5,4},{6,7},{7,6},{8,9},{9,8},{10,11... | collective-permute-start | bytes 589832 | tf_op jit(solution)/shard_map/ppermute | solution.py:297
  31.8 6.1 %collective-permute-start.14 = (bf16[192,512]{1,0:T(8,128)(2,1)S(1)}, bf16[192,512]{1,0:T(8,128)(2,1)S(1)}, u32[]{:S(2)}, u32[]{:S(2)}) collective-permute-start(bf16[192,512]{1,0:T(8,128)(2,1)S(1)} %after.6.p_ref), channel_id=1, source_target_pairs={{0,1},{1,0},{2,3},{3,2},{4,5},{5,4},{6,7},{7,6},{8,9},{9,8},{10,11... | collective-permute-start | bytes 589832 | tf_op jit(solution)/shard_map/ppermute | solution.py:297
  32.3 29.6 %collective-permute-start.2 = (f32[2,128]{1,0:T(2,128)S(1)}, f32[2,128]{1,0:T(2,128)S(1)}, u32[]{:S(2)}, u32[]{:S(2)}) collective-permute-start(f32[2,128]{1,0:T(2,128)S(1)} %get-tuple-element.34.own_gates_ref), channel_id=1, source_target_pairs={{0,1},{1,0},{2,3},{3,2},{4,5},{5,4},{6,7},{7,6},{8,9},{9,8},{10,11... | collective-permute-start | bytes 3080 | tf_op jit(solution)/shard_map/ppermute | solution.py:297
  37.4 4.7 %collective-permute-start.10 = (bf16[192,512]{1,0:T(8,128)(2,1)S(1)}, bf16[192,512]{1,0:T(8,128)(2,1)S(1)}, u32[]{:S(2)}, u32[]{:S(2)}) collective-permute-start(bf16[192,512]{1,0:T(8,128)(2,1)S(1)} %collective-permute-done.8.p_ref), channel_id=1, source_target_pairs={{0,1},{1,0},{2,3},{3,2},{4,5},{5,4},{6,7},{7,6},{8,9},{9,8},{10,11... | collective-permute-start | bytes 589832 | tf_op jit(solution)/shard_map/ppermute | solution.py:297
  37.4 4.7 %collective-permute-start.11 = (bf16[192,512]{1,0:T(8,128)(2,1)S(1)}, bf16[192,512]{1,0:T(8,128)(2,1)S(1)}, u32[]{:S(2)}, u32[]{:S(2)}) collective-permute-start(bf16[192,512]{1,0:T(8,128)(2,1)S(1)} %collective-permute-done.9.q_ref), channel_id=1, source_target_pairs={{0,1},{1,0},{2,3},{3,2},{4,5},{5,4},{6,7},{7,6},{8,9},{9,8},{10,11... | collective-permute-start | bytes 589832 | tf_op jit(solution)/shard_map/ppermute | solution.py:297
  39.8 1.8 %collective-permute-start.20 = (bf16[2,192,512]{2,1,0:T(8,128)(2,1)S(1)}, bf16[2,192,512]{2,1,0:T(8,128)(2,1)S(1)}, u32[]{:S(2)}, u32[]{:S(2)}) collective-permute-start(bf16[2,192,512]{2,1,0:T(8,128)(2,1)S(1)} %get-tuple-element.47), channel_id=1, source_target_pairs={{0,1},{1,0},{2,3},{3,2},{4,5},{5,4},{6,7},{7,6},{8,9},{9,8},{10,11... | collective-permute-start | bytes 1179656 | tf_op jit(solution)/shard_map/ppermute | solution.py:297
  39.8 4.1 %collective-permute-start.24 = (bf16[2,192,512]{2,1,0:T(8,128)(2,1)S(1)}, bf16[2,192,512]{2,1,0:T(8,128)(2,1)S(1)}, u32[]{:S(2)}, u32[]{:S(2)}) collective-permute-start(bf16[2,192,512]{2,1,0:T(8,128)(2,1)S(1)} %get-tuple-element.50), channel_id=1, source_target_pairs={{0,1},{1,0},{2,3},{3,2},{4,5},{5,4},{6,7},{7,6},{8,9},{9,8},{10,11... | collective-permute-start | bytes 1179656 | tf_op jit(solution)/shard_map/ppermute | solution.py:297
  41.7 7.0 %collective-permute-start.27 = (bf16[192,512]{1,0:T(8,128)(2,1)S(1)}, bf16[192,512]{1,0:T(8,128)(2,1)S(1)}, u32[]{:S(2)}, u32[]{:S(2)}) collective-permute-start(bf16[192,512]{1,0:T(8,128)(2,1)S(1)} %fusion.9.refs_1_), channel_id=1, source_target_pairs={{0,2},{2,0},{4,6},{6,4},{8,10},{10,8},{12,14},{14,12},{1,3},{3,1},... | collective-permute-start | bytes 589832 | tf_op jit(solution)/shard_map/ppermute | solution.py:302
  43.9 1.8 %collective-permute-start.21 = (bf16[2,192,512]{2,1,0:T(8,128)(2,1)S(1)}, bf16[2,192,512]{2,1,0:T(8,128)(2,1)S(1)}, u32[]{:S(2)}, u32[]{:S(2)}) collective-permute-start(bf16[2,192,512]{2,1,0:T(8,128)(2,1)S(1)} %get-tuple-element.49), channel_id=1, source_target_pairs={{0,1},{1,0},{2,3},{3,2},{4,5},{5,4},{6,7},{7,6},{8,9},{9,8},{10,11... | collective-permute-start | bytes 1179656 | tf_op jit(solution)/shard_map/ppermute | solution.py:297
  45.8 7.1 %collective-permute-start.22 = (bf16[192,512]{1,0:T(8,128)(2,1)S(1)}, bf16[192,512]{1,0:T(8,128)(2,1)S(1)}, u32[]{:S(2)}, u32[]{:S(2)}) collective-permute-start(bf16[192,512]{1,0:T(8,128)(2,1)S(1)} %fusion.10.refs_1_), channel_id=1, source_target_pairs={{0,2},{2,0},{4,6},{6,4},{8,10},{10,8},{12,14},{14,12},{1,3},{3,1},... | collective-permute-start | bytes 589832 | tf_op jit(solution)/shard_map/ppermute | solution.py:302
  48.8 17.0 %collective-permute-start.28 = (bf16[192,512]{1,0:T(8,128)(2,1)S(1)}, bf16[192,512]{1,0:T(8,128)(2,1)S(1)}, u32[]{:S(2)}, u32[]{:S(2)}) collective-permute-start(bf16[192,512]{1,0:T(8,128)(2,1)S(1)} %fusion.1), channel_id=1, source_target_pairs={{0,8},{2,10},{4,12},{6,14},{8,0},{10,2},{12,4},{14,6},{1,9},{3,11}... | collective-permute-start | bytes 589832 | tf_op jit(solution)/shard_map/ppermute | solution.py:307
  51.8 6.2 %collective-permute-start.25 = (bf16[192,512]{1,0:T(8,128)(2,1)S(1)}, bf16[192,512]{1,0:T(8,128)(2,1)S(1)}, u32[]{:S(2)}, u32[]{:S(2)}) collective-permute-start(bf16[192,512]{1,0:T(8,128)(2,1)S(1)} %after.11), channel_id=1, source_target_pairs={{0,2},{2,0},{4,6},{6,4},{8,10},{10,8},{12,14},{14,12},{1,3},{3,1},... | collective-permute-start | bytes 589832 | tf_op jit(solution)/shard_map/ppermute | solution.py:302
  53.0 15.8 %collective-permute-start.29 = (bf16[192,512]{1,0:T(8,128)(2,1)S(1)}, bf16[192,512]{1,0:T(8,128)(2,1)S(1)}, u32[]{:S(2)}, u32[]{:S(2)}) collective-permute-start(bf16[192,512]{1,0:T(8,128)(2,1)S(1)} %fusion.5.refs_1_), channel_id=1, source_target_pairs={{0,12},{2,14},{4,8},{6,10},{8,4},{10,6},{12,0},{14,2},{1,13},{3,15... | collective-permute-start | bytes 589832 | tf_op jit(solution)/shard_map/ppermute | solution.py:307
  56.2 5.7 %collective-permute-start.23 = (bf16[192,512]{1,0:T(8,128)(2,1)S(1)}, bf16[192,512]{1,0:T(8,128)(2,1)S(1)}, u32[]{:S(2)}, u32[]{:S(2)}) collective-permute-start(bf16[192,512]{1,0:T(8,128)(2,1)S(1)} %after.10), channel_id=1, source_target_pairs={{0,2},{2,0},{4,6},{6,4},{8,10},{10,8},{12,14},{14,12},{1,3},{3,1},... | collective-permute-start | bytes 589832 | tf_op jit(solution)/shard_map/ppermute | solution.py:302
  58.1 10.7 %collective-permute-start.26 = (bf16[192,512]{1,0:T(8,128)(2,1)S(1)}, bf16[192,512]{1,0:T(8,128)(2,1)S(1)}, u32[]{:S(2)}, u32[]{:S(2)}) collective-permute-start(bf16[192,512]{1,0:T(8,128)(2,1)S(1)} %fusion.3), channel_id=1, source_target_pairs={{0,4},{2,6},{4,0},{6,2},{8,12},{10,14},{12,8},{14,10},{1,5},{3,7},... | collective-permute-start | bytes 589832 | tf_op jit(solution)/shard_map/ppermute | solution.py:307
  69.7 1.4 %collective-permute-start.30 = (bf16[128,512]{1,0:T(8,128)(2,1)S(1)}, bf16[128,512]{1,0:T(8,128)(2,1)S(1)}, u32[]{:S(2)}, u32[]{:S(2)}) collective-permute-start(bf16[128,512]{1,0:T(8,128)(2,1)S(1)} %get-tuple-element.52), channel_id=1, source_target_pairs={{0,1},{1,0},{2,3},{3,2},{4,5},{5,4},{6,7},{7,6},{8,9},{9,8},{10,11... | collective-permute-start | bytes 393224 | tf_op jit(solution)/shard_map/ppermute | solution.py:297

commit v15 on v14

--- a/solution.py
+++ b/solution.py
@@ -400,15 +400,13 @@
     ps, qs, kept, halves, wholes, boths = {}, {}, {}, {}, {}, {}
     for offset in [0, 1, 2, 3]:
         p = travelling[offset - 1] if offset else selected[0]
-        if offset == 2:
+        if offset == 1:
             p = after(p, near_in)
         q = swap_owner(p)
         ps[offset], qs[offset] = p, q
     for offset in [0, 1, 2, 3]:
         p, q = ps[offset], qs[offset]
         p2, q2 = swap(p), swap(q)
-        if offset == 1:
-            q2 = after(q2, kept[0])
         if offset == 2:
             q2 = after(q2, kept[0], kept[1])
         if offset == 3:

time: 72.1 us -> 70.2 us (0.974)
  waiting for transfers between devices: 26.4 us -> 23.2 us
  starting transfers between devices: 29 us -> 30.5 us
    ppermute x6, waiting for transfers between devices: 14.2 us -> 11.1 us  [exchange(): lax.ppermute(values, 'expert', [(i, i ^ 2 * offset) for i in range(owners)])]
    ppermute x8, starting transfers between devices: 8.82 us -> 10.9 us  [swap_owner(): return lax.ppermute(values, 'expert', [(i, i ^ 1) for i in range(owners)])]
  transfers between devices with their start and end apart: 31 -> 31, of which waited for: 13 -> 15; matrix products, arithmetic and copies ran while one was open for 1% -> 1% of each run, Pallas kernels for 16% -> 16%
where the time goes in v15:
time: 70.2 us; the launch traced here: 70.1 us
  starting transfers between devices  30.5 us (43%)
  waiting for transfers between devices  23.2 us (33%)
  Pallas kernels  14.8 us (21%)
  between operations  0.88 us (1%)
    ppermute x6, starting transfers between devices, exchange(): lax.ppermute(values, 'expert', [(i, i ^ 2 * offset) for i in range(owners)])  16 us
    pallas_call x10, Pallas kernels, call(): pl.pallas_call(kernel, out_shape=tuple((jax.ShapeDtypeStruct(*out) for ou...  14.8 us
    ppermute x6, waiting for transfers between devices, exchange(): lax.ppermute(values, 'expert', [(i, i ^ 2 * offset) for i in range(owners)])  11.1 us
    ppermute x8, starting transfers between devices, swap_owner(): return lax.ppermute(values, 'expert', [(i, i ^ 1) for i in range(owners)])  10.9 us
    ppermute x8, waiting for transfers between devices, swap_owner(): return lax.ppermute(values, 'expert', [(i, i ^ 1) for i in range(owners)])  7.16 us
    ppermute x17, waiting for transfers between devices, swap(): return lax.ppermute(values, 'section', [(0, 1), (1, 0)])  4.95 us
    ppermute x17, starting transfers between devices, swap(): return lax.ppermute(values, 'section', [(0, 1), (1, 0)])  3.5 us
  transfers between devices with their start and end apart: 31, of which 15 were waited for; matrix products, arithmetic and copies ran while one was open for 1% of the time, Pallas kernels for 16%

profile of v15, /device:TPU:0, one launch (start us, length us, event | category | flops | bytes accessed | tf_op | source)
XLA Modules:
  0.0 70.1 jit_solution(4641005780805067808)
XLA Ops:
  0.0 0.5 collective-permute-start
  0.5 0.1 collective-permute-start.1
  1.2 1.8 %attend_own.1 = (bf16[128,512]{1,0:T(8,128)(2,1)S(1)}, bf16[128,512]{1,0:T(8,128)(2,1)S(1)}, bf16[128,512]{1,0:T(8,128)(2,1)S(1)}) custom-call(s32[1]{0:T(128)} %bitcast.core_ref, s32[1]{0:T(128)S(6)} %copy.22.source_ref, bf16[1,128,1024]{2,1,0:T(8,128)(2,1)} %x_in.1, f32[1,1024]{1,0:T(1,128)} %bitcast.40, bf16[2,80,512]{2,1,0:T(8,128)(2,1)} %keys_in.1, ...), custom_call_target="tpu_custom_call" | custom-call | tf_op jit(solution)/shard_map/attend_own/pallas_call | solution.py:25
  3.0 1.2 %attend_other.1 = (bf16[128,1024]{1,0:T(8,128)(2,1)S(1)}, bf16[128,512]{1,0:T(8,128)(2,1)S(1)}, bf16[128,512]{1,0:T(8,128)(2,1)S(1)}, f32[2,128]{1,0:T(2,128)S(1)}, s32[2,2,128]{2,1,0:T(2,128)S(1)}) custom-call(s32[1]{0:T(128)} %bitcast.core_ref, s32[1]{0:T(128)S(6)} %copy.22.source_ref, bf16[128,512]{1,0:T(8,128)(2,1)S(1)} %get-tuple-element.29.own_ref, ...), custom_call_target="tpu_custom_call" | custom-call | tf_op jit(solution)/shard_map/attend_other/pallas_call | solution.py:25
  4.2 0.5 collective-permute-start.3
  4.7 1.0 %collective-permute-done.3.other_ref = bf16[128,512]{1,0:T(8,128)(2,1)S(1)} collective-permute-done((bf16[128,512]{1,0:T(8,128)(2,1)S(1)}, bf16[128,512]{1,0:T(8,128)(2,1)S(1)}, u32[]{:S(2)}, u32[]{:S(2)}) %collective-permute-start.3) | collective-permute-done | bytes 131104 | tf_op jit(solution)/shard_map/ppermute | solution.py:297
  5.7 0.5 select.5
  6.2 2.9 %collective-permute-start.4 = (bf16[192,512]{1,0:T(8,128)(2,1)S(1)}, bf16[192,512]{1,0:T(8,128)(2,1)S(1)}, u32[]{:S(2)}, u32[]{:S(2)}) collective-permute-start(bf16[192,512]{1,0:T(8,128)(2,1)S(1)} %get-tuple-element.37.p_ref), channel_id=1, source_target_pairs={{0,2},{2,0},{4,6},{6,4},{8,10},{10,8},{12,14},{14,12},{1,3},{3,1},... | collective-permute-start | bytes 589832 | tf_op jit(solution)/shard_map/ppermute | solution.py:302
  9.2 1.6 %collective-permute-start.16 = (bf16[192,512]{1,0:T(8,128)(2,1)S(1)}, bf16[192,512]{1,0:T(8,128)(2,1)S(1)}, u32[]{:S(2)}, u32[]{:S(2)}) collective-permute-start(bf16[192,512]{1,0:T(8,128)(2,1)S(1)} %get-tuple-element.44), channel_id=1, source_target_pairs={{0,4},{2,6},{4,0},{6,2},{8,12},{10,14},{12,8},{14,10},{1,5},{3,7},... | collective-permute-start | bytes 589832 | tf_op jit(solution)/shard_map/ppermute | solution.py:307
  10.7 2.6 %collective-permute-start.12 = (bf16[192,512]{1,0:T(8,128)(2,1)S(1)}, bf16[192,512]{1,0:T(8,128)(2,1)S(1)}, u32[]{:S(2)}, u32[]{:S(2)}) collective-permute-start(bf16[192,512]{1,0:T(8,128)(2,1)S(1)} %get-tuple-element.43), channel_id=1, source_target_pairs={{0,8},{2,10},{4,12},{6,14},{8,0},{10,2},{12,4},{14,6},{1,9},{3,11}... | collective-permute-start | bytes 589832 | tf_op jit(solution)/shard_map/ppermute | solution.py:307
  13.3 1.1 %collective-permute-done.4.q_ref = bf16[192,512]{1,0:T(8,128)(2,1)S(1)} collective-permute-done((bf16[192,512]{1,0:T(8,128)(2,1)S(1)}, bf16[192,512]{1,0:T(8,128)(2,1)S(1)}, u32[]{:S(2)}, u32[]{:S(2)}) %collective-permute-start.4) | collective-permute-done | bytes 196640 | tf_op jit(solution)/shard_map/ppermute | solution.py:302
  14.4 2.2 %load.1 = (bf16[1024,1024]{1,0:T(8,128)(2,1)S(1)}, bf16[1024,1024]{1,0:T(8,128)(2,1)S(1)}) custom-call(bf16[1024,1024]{1,0:T(8,128)(2,1)} %in_in.1, bf16[1024,1024]{1,0:T(8,128)(2,1)} %out_in.1), custom_call_target="tpu_custom_call" | custom-call | tf_op jit(solution)/shard_map/load/pallas_call | solution.py:25
  16.6 3.3 %collective-permute-done.16.refs_0_ = bf16[192,512]{1,0:T(8,128)(2,1)S(1)} collective-permute-done((bf16[192,512]{1,0:T(8,128)(2,1)S(1)}, bf16[192,512]{1,0:T(8,128)(2,1)S(1)}, u32[]{:S(2)}, u32[]{:S(2)}) %collective-permute-start.16) | collective-permute-done | bytes 196640 | tf_op jit(solution)/shard_map/ppermute | solution.py:307
  19.9 0.4 collective-permute-start.17
  20.3 2.6 %collective-permute-start.8 = (bf16[192,512]{1,0:T(8,128)(2,1)S(1)}, bf16[192,512]{1,0:T(8,128)(2,1)S(1)}, u32[]{:S(2)}, u32[]{:S(2)}) collective-permute-start(bf16[192,512]{1,0:T(8,128)(2,1)S(1)} %get-tuple-element.42), channel_id=1, source_target_pairs={{0,12},{2,14},{4,8},{6,10},{8,4},{10,6},{12,0},{14,2},{1,13},{3,15... | collective-permute-start | bytes 589832 | tf_op jit(solution)/shard_map/ppermute | solution.py:307
  22.9 1.5 %collective-permute-start.13 = (bf16[192,512]{1,0:T(8,128)(2,1)S(1)}, bf16[192,512]{1,0:T(8,128)(2,1)S(1)}, u32[]{:S(2)}, u32[]{:S(2)}) collective-permute-start(bf16[192,512]{1,0:T(8,128)(2,1)S(1)} %collective-permute-done.12.p_ref), channel_id=1, source_target_pairs={{0,2},{2,0},{4,6},{6,4},{8,10},{10,8},{12,14},{14,12},{1,3},{3,1},... | collective-permute-start | bytes 589832 | tf_op jit(solution)/shard_map/ppermute | solution.py:302
  24.4 0.0 collective-permute-done.5.p2_ref
  24.5 0.0 collective-permute-start.18
  24.5 0.0 collective-permute-done.6.q2_ref
  24.5 1.8 %expert.4 = (f32[2,192,512]{2,1,0:T(8,128)S(1)}, bf16[2,192,512]{2,1,0:T(8,128)(2,1)S(1)}) custom-call(s32[1]{0:T(128)} %bitcast.core_ref, bf16[192,512]{1,0:T(8,128)(2,1)S(1)} %get-tuple-element.37.p_ref, bf16[192,512]{1,0:T(8,128)(2,1)S(1)} %collective-permute-done.4.q_ref, bf16[192,512]{1,0:T(8,128)(2,1)S(1)} %collective-permute-done.5.p2_ref, ...), custom_call_target="tpu_custom_call" | custom-call | tf_op jit(solution)/shard_map/expert/pallas_call | solution.py:25
  26.3 0.6 collective-permute-start.7
  26.9 0.0 collective-permute-done.17.q_ref
  26.9 0.1 collective-permute-start.19
  27.0 0.9 %collective-permute-done.8.p_ref = bf16[192,512]{1,0:T(8,128)(2,1)S(1)} collective-permute-done((bf16[192,512]{1,0:T(8,128)(2,1)S(1)}, bf16[192,512]{1,0:T(8,128)(2,1)S(1)}, u32[]{:S(2)}, u32[]{:S(2)}) %collective-permute-start.8) | collective-permute-done | bytes 196640 | tf_op jit(solution)/shard_map/ppermute | solution.py:307
  27.8 1.6 %collective-permute-start.9 = (bf16[192,512]{1,0:T(8,128)(2,1)S(1)}, bf16[192,512]{1,0:T(8,128)(2,1)S(1)}, u32[]{:S(2)}, u32[]{:S(2)}) collective-permute-start(bf16[192,512]{1,0:T(8,128)(2,1)S(1)} %collective-permute-done.8.p_ref), channel_id=1, source_target_pairs={{0,2},{2,0},{4,6},{6,4},{8,10},{10,8},{12,14},{14,12},{1,3},{3,1},... | collective-permute-start | bytes 589832 | tf_op jit(solution)/shard_map/ppermute | solution.py:302
  29.5 0.3 collective-permute-done.13.q_ref
  29.8 0.0 collective-permute-start.15
  29.8 0.0 collective-permute-done.18.p2_ref
  29.8 0.5 collective-permute-start.14
  30.3 0.0 collective-permute-done.19.q2_ref
  30.3 0.1 collective-permute-start.2
  30.4 1.8 %expert.5 = (f32[2,192,512]{2,1,0:T(8,128)S(1)}, bf16[2,192,512]{2,1,0:T(8,128)(2,1)S(1)}) custom-call(s32[1]{0:T(128)} %bitcast.core_ref, bf16[192,512]{1,0:T(8,128)(2,1)S(1)} %after.5.p_ref, bf16[192,512]{1,0:T(8,128)(2,1)S(1)} %collective-permute-done.17.q_ref, bf16[192,512]{1,0:T(8,128)(2,1)S(1)} %collective-permute-done.18.p2_ref, ...), custom_call_target="tpu_custom_call" | custom-call | tf_op jit(solution)/shard_map/expert/pallas_call | solution.py:25
  32.2 2.0 %collective-permute-done.9.q_ref = bf16[192,512]{1,0:T(8,128)(2,1)S(1)} collective-permute-done((bf16[192,512]{1,0:T(8,128)(2,1)S(1)}, bf16[192,512]{1,0:T(8,128)(2,1)S(1)}, u32[]{:S(2)}, u32[]{:S(2)}) %collective-permute-start.9) | collective-permute-done | bytes 196640 | tf_op jit(solution)/shard_map/ppermute | solution.py:302
  34.2 0.0 collective-permute-start.10
  34.2 0.0 collective-permute-done.15.refs_0_
  34.2 0.5 collective-permute-start.11
  34.7 1.8 %expert.6 = (f32[2,192,512]{2,1,0:T(8,128)S(1)}, bf16[2,192,512]{2,1,0:T(8,128)(2,1)S(1)}) custom-call(s32[1]{0:T(128)} %bitcast.core_ref, bf16[192,512]{1,0:T(8,128)(2,1)S(1)} %collective-permute-done.12.p_ref, bf16[192,512]{1,0:T(8,128)(2,1)S(1)} %collective-permute-done.13.q_ref, bf16[192,512]{1,0:T(8,128)(2,1)S(1)} %collective-permute-done.14.p2_ref, ...), custom_call_target="tpu_custom_call" | custom-call | tf_op jit(solution)/shard_map/expert/pallas_call | solution.py:25
  36.6 0.1 collective-permute-start.20
  36.7 0.5 collective-permute-start.24
  37.2 0.1 convert_add_fusion.3
  37.3 1.1 %collective-permute-done.20 = bf16[2,192,512]{2,1,0:T(8,128)(2,1)S(1)} collective-permute-done((bf16[2,192,512]{2,1,0:T(8,128)(2,1)S(1)}, bf16[2,192,512]{2,1,0:T(8,128)(2,1)S(1)}, u32[]{:S(2)}, u32[]{:S(2)}) %collective-permute-start.20) | collective-permute-done | bytes 393248 | tf_op jit(solution)/shard_map/ppermute | solution.py:297
  38.4 0.1 convert_add_fusion.2
  38.5 1.0 %collective-permute-start.27 = (bf16[192,512]{1,0:T(8,128)(2,1)S(1)}, bf16[192,512]{1,0:T(8,128)(2,1)S(1)}, u32[]{:S(2)}, u32[]{:S(2)}) collective-permute-start(bf16[192,512]{1,0:T(8,128)(2,1)S(1)} %fusion.9.refs_1_), channel_id=1, source_target_pairs={{0,2},{2,0},{4,6},{6,4},{8,10},{10,8},{12,14},{14,12},{1,3},{3,1},... | collective-permute-start | bytes 589832 | tf_op jit(solution)/shard_map/ppermute | solution.py:302
  39.5 1.8 %expert.7 = (f32[2,192,512]{2,1,0:T(8,128)S(1)}, bf16[2,192,512]{2,1,0:T(8,128)(2,1)S(1)}) custom-call(s32[1]{0:T(128)} %bitcast.core_ref, bf16[192,512]{1,0:T(8,128)(2,1)S(1)} %collective-permute-done.8.p_ref, bf16[192,512]{1,0:T(8,128)(2,1)S(1)} %collective-permute-done.9.q_ref, bf16[192,512]{1,0:T(8,128)(2,1)S(1)} %collective-permute-done.10.p2_ref, ...), custom_call_target="tpu_custom_call" | custom-call | tf_op jit(solution)/shard_map/expert/pallas_call | solution.py:25
  41.4 0.1 collective-permute-start.21
  41.4 0.1 convert_add_fusion
  41.6 1.5 %collective-permute-done.21 = bf16[2,192,512]{2,1,0:T(8,128)(2,1)S(1)} collective-permute-done((bf16[2,192,512]{2,1,0:T(8,128)(2,1)S(1)}, bf16[2,192,512]{2,1,0:T(8,128)(2,1)S(1)}, u32[]{:S(2)}, u32[]{:S(2)}) %collective-permute-start.21) | collective-permute-done | bytes 393248 | tf_op jit(solution)/shard_map/ppermute | solution.py:297
  43.1 0.1 convert_add_fusion.1
  43.3 1.2 %collective-permute-start.22 = (bf16[192,512]{1,0:T(8,128)(2,1)S(1)}, bf16[192,512]{1,0:T(8,128)(2,1)S(1)}, u32[]{:S(2)}, u32[]{:S(2)}) collective-permute-start(bf16[192,512]{1,0:T(8,128)(2,1)S(1)} %fusion.10.refs_1_), channel_id=1, source_target_pairs={{0,2},{2,0},{4,6},{6,4},{8,10},{10,8},{12,14},{14,12},{1,3},{3,1},... | collective-permute-start | bytes 589832 | tf_op jit(solution)/shard_map/ppermute | solution.py:302
  44.5 1.1 %collective-permute-done.27 = bf16[192,512]{1,0:T(8,128)(2,1)S(1)} collective-permute-done((bf16[192,512]{1,0:T(8,128)(2,1)S(1)}, bf16[192,512]{1,0:T(8,128)(2,1)S(1)}, u32[]{:S(2)}, u32[]{:S(2)}) %collective-permute-start.27) | collective-permute-done | bytes 196640 | tf_op jit(solution)/shard_map/ppermute | solution.py:302
  45.6 4.4 %collective-permute-start.28 = (bf16[192,512]{1,0:T(8,128)(2,1)S(1)}, bf16[192,512]{1,0:T(8,128)(2,1)S(1)}, u32[]{:S(2)}, u32[]{:S(2)}) collective-permute-start(bf16[192,512]{1,0:T(8,128)(2,1)S(1)} %fusion.1), channel_id=1, source_target_pairs={{0,8},{2,10},{4,12},{6,14},{8,0},{10,2},{12,4},{14,6},{1,9},{3,11}... | collective-permute-start | bytes 589832 | tf_op jit(solution)/shard_map/ppermute | solution.py:307
  49.9 0.3 collective-permute-start.25
  50.2 0.1 collective-permute-done.22
  50.4 3.3 %collective-permute-start.29 = (bf16[192,512]{1,0:T(8,128)(2,1)S(1)}, bf16[192,512]{1,0:T(8,128)(2,1)S(1)}, u32[]{:S(2)}, u32[]{:S(2)}) collective-permute-start(bf16[192,512]{1,0:T(8,128)(2,1)S(1)} %fusion.5.refs_1_), channel_id=1, source_target_pairs={{0,12},{2,14},{4,8},{6,10},{8,4},{10,6},{12,0},{14,2},{1,13},{3,15... | collective-permute-start | bytes 589832 | tf_op jit(solution)/shard_map/ppermute | solution.py:307
  53.6 2.1 %collective-permute-start.23 = (bf16[192,512]{1,0:T(8,128)(2,1)S(1)}, bf16[192,512]{1,0:T(8,128)(2,1)S(1)}, u32[]{:S(2)}, u32[]{:S(2)}) collective-permute-start(bf16[192,512]{1,0:T(8,128)(2,1)S(1)} %after.8), channel_id=1, source_target_pairs={{0,2},{2,0},{4,6},{6,4},{8,10},{10,8},{12,14},{14,12},{1,3},{3,1},... | collective-permute-start | bytes 589832 | tf_op jit(solution)/shard_map/ppermute | solution.py:302
  55.7 0.8 %collective-permute-done.25 = bf16[192,512]{1,0:T(8,128)(2,1)S(1)} collective-permute-done((bf16[192,512]{1,0:T(8,128)(2,1)S(1)}, bf16[192,512]{1,0:T(8,128)(2,1)S(1)}, u32[]{:S(2)}, u32[]{:S(2)}) %collective-permute-start.25) | collective-permute-done | bytes 196640 | tf_op jit(solution)/shard_map/ppermute | solution.py:302
  56.5 1.6 %collective-permute-start.26 = (bf16[192,512]{1,0:T(8,128)(2,1)S(1)}, bf16[192,512]{1,0:T(8,128)(2,1)S(1)}, u32[]{:S(2)}, u32[]{:S(2)}) collective-permute-start(bf16[192,512]{1,0:T(8,128)(2,1)S(1)} %fusion.3), channel_id=1, source_target_pairs={{0,4},{2,6},{4,0},{6,2},{8,12},{10,14},{12,8},{14,10},{1,5},{3,7},... | collective-permute-start | bytes 589832 | tf_op jit(solution)/shard_map/ppermute | solution.py:307
  58.1 1.9 %collective-permute-done.23 = bf16[192,512]{1,0:T(8,128)(2,1)S(1)} collective-permute-done((bf16[192,512]{1,0:T(8,128)(2,1)S(1)}, bf16[192,512]{1,0:T(8,128)(2,1)S(1)}, u32[]{:S(2)}, u32[]{:S(2)}) %collective-permute-start.23) | collective-permute-done | bytes 196640 | tf_op jit(solution)/shard_map/ppermute | solution.py:302
  60.0 4.0 %collective-permute-done.28.rest_2_ = bf16[192,512]{1,0:T(8,128)(2,1)S(1)} collective-permute-done((bf16[192,512]{1,0:T(8,128)(2,1)S(1)}, bf16[192,512]{1,0:T(8,128)(2,1)S(1)}, u32[]{:S(2)}, u32[]{:S(2)}) %collective-permute-start.28) | collective-permute-done | bytes 196640 | tf_op jit(solution)/shard_map/ppermute | solution.py:307
  64.0 2.9 %collective-permute-done.26.rest_1_ = bf16[192,512]{1,0:T(8,128)(2,1)S(1)} collective-permute-done((bf16[192,512]{1,0:T(8,128)(2,1)S(1)}, bf16[192,512]{1,0:T(8,128)(2,1)S(1)}, u32[]{:S(2)}, u32[]{:S(2)}) %collective-permute-start.26) | collective-permute-done | bytes 196640 | tf_op jit(solution)/shard_map/ppermute | solution.py:307
  66.9 0.9 %combine.1 = (f32[128,512]{1,0:T(8,128)S(1)}, bf16[128,512]{1,0:T(8,128)(2,1)S(1)}) custom-call(s32[1]{0:T(128)} %bitcast.core_ref, s32[1]{0:T(128)} %bitcast.5.line_ref, s32[2,2,128]{2,1,0:T(2,128)S(1)} %get-tuple-element.33.routes_ref, f32[2,128]{1,0:T(2,128)S(1)} %get-tuple-element.34.own_gates_ref, f32[2,128]{1,0:T(2,128)S(1)} %collective-permute-done.2.other_gates_ref, ...), custom_call_target="tpu_custom_call" | custom-call | tf_op jit(solution)/shard_map/combine/pallas_call | solution.py:25
  67.9 0.1 collective-permute-start.30
  68.0 1.3 %collective-permute-done.30.other_ref = bf16[128,512]{1,0:T(8,128)(2,1)S(1)} collective-permute-done((bf16[128,512]{1,0:T(8,128)(2,1)S(1)}, bf16[128,512]{1,0:T(8,128)(2,1)S(1)}, u32[]{:S(2)}, u32[]{:S(2)}) %collective-permute-start.30) | collective-permute-done | bytes 131104 | tf_op jit(solution)/shard_map/ppermute | solution.py:297
  69.3 0.8 %finish.1 = bf16[128,1024]{1,0:T(8,128)(2,1)} custom-call(s32[1]{0:T(128)} %bitcast.core_ref, bf16[128,1024]{1,0:T(8,128)(2,1)S(1)} %get-tuple-element.32.state_ref, f32[128,512]{1,0:T(8,128)S(1)} %get-tuple-element.51.own_ref, bf16[128,512]{1,0:T(8,128)(2,1)S(1)} %collective-permute-done.30.other_ref), custom_call_target="tpu_custom_call" | custom-call | tf_op jit(solution)/shard_map/finish/pallas_call | solution.py:25
  (25 shorter events, 0.3 us)
Async XLA Ops:
  0.0 2.9 %collective-permute-start = (bf16[2,80,512]{2,1,0:T(8,128)(2,1)}, bf16[2,80,512]{2,1,0:T(8,128)(2,1)S(1)}, u32[]{:S(2)}, u32[]{:S(2)}) collective-permute-start(bf16[2,80,512]{2,1,0:T(8,128)(2,1)} %keys_in.1), channel_id=1, source_target_pairs={{0,1},{1,0},{2,3},{3,2},{4,5},{5,4},{6,7},{7,6},{8,9},{9,8},{10,11... | collective-permute-start | bytes 491528 | tf_op jit(solution)/shard_map/ppermute | solution.py:297
  0.5 2.5 %collective-permute-start.1 = (bf16[2,80,512]{2,1,0:T(8,128)(2,1)}, bf16[2,80,512]{2,1,0:T(8,128)(2,1)S(1)}, u32[]{:S(2)}, u32[]{:S(2)}) collective-permute-start(bf16[2,80,512]{2,1,0:T(8,128)(2,1)} %values_in.1), channel_id=1, source_target_pairs={{0,1},{1,0},{2,3},{3,2},{4,5},{5,4},{6,7},{7,6},{8,9},{9,8},{10,11... | collective-permute-start | bytes 491528 | tf_op jit(solution)/shard_map/ppermute | solution.py:297
  4.2 1.5 %collective-permute-start.3 = (bf16[128,512]{1,0:T(8,128)(2,1)S(1)}, bf16[128,512]{1,0:T(8,128)(2,1)S(1)}, u32[]{:S(2)}, u32[]{:S(2)}) collective-permute-start(bf16[128,512]{1,0:T(8,128)(2,1)S(1)} %get-tuple-element.36), channel_id=1, source_target_pairs={{0,1},{1,0},{2,3},{3,2},{4,5},{5,4},{6,7},{7,6},{8,9},{9,8},{10,11... | collective-permute-start | bytes 393224 | tf_op jit(solution)/shard_map/ppermute | solution.py:297
  6.2 8.1 %collective-permute-start.4 = (bf16[192,512]{1,0:T(8,128)(2,1)S(1)}, bf16[192,512]{1,0:T(8,128)(2,1)S(1)}, u32[]{:S(2)}, u32[]{:S(2)}) collective-permute-start(bf16[192,512]{1,0:T(8,128)(2,1)S(1)} %get-tuple-element.37.p_ref), channel_id=1, source_target_pairs={{0,2},{2,0},{4,6},{6,4},{8,10},{10,8},{12,14},{14,12},{1,3},{3,1},... | collective-permute-start | bytes 589832 | tf_op jit(solution)/shard_map/ppermute | solution.py:302
  9.2 10.8 %collective-permute-start.16 = (bf16[192,512]{1,0:T(8,128)(2,1)S(1)}, bf16[192,512]{1,0:T(8,128)(2,1)S(1)}, u32[]{:S(2)}, u32[]{:S(2)}) collective-permute-start(bf16[192,512]{1,0:T(8,128)(2,1)S(1)} %get-tuple-element.44), channel_id=1, source_target_pairs={{0,4},{2,6},{4,0},{6,2},{8,12},{10,14},{12,8},{14,10},{1,5},{3,7},... | collective-permute-start | bytes 589832 | tf_op jit(solution)/shard_map/ppermute | solution.py:307
  10.7 12.2 %collective-permute-start.12 = (bf16[192,512]{1,0:T(8,128)(2,1)S(1)}, bf16[192,512]{1,0:T(8,128)(2,1)S(1)}, u32[]{:S(2)}, u32[]{:S(2)}) collective-permute-start(bf16[192,512]{1,0:T(8,128)(2,1)S(1)} %get-tuple-element.43), channel_id=1, source_target_pairs={{0,8},{2,10},{4,12},{6,14},{8,0},{10,2},{12,4},{14,6},{1,9},{3,11}... | collective-permute-start | bytes 589832 | tf_op jit(solution)/shard_map/ppermute | solution.py:307
  13.3 11.1 %collective-permute-start.5 = (bf16[192,512]{1,0:T(8,128)(2,1)S(1)}, bf16[192,512]{1,0:T(8,128)(2,1)S(1)}, u32[]{:S(2)}, u32[]{:S(2)}) collective-permute-start(bf16[192,512]{1,0:T(8,128)(2,1)S(1)} %get-tuple-element.37.p_ref), channel_id=1, source_target_pairs={{0,1},{1,0},{2,3},{3,2},{4,5},{5,4},{6,7},{7,6},{8,9},{9,8},{10,11... | collective-permute-start | bytes 589832 | tf_op jit(solution)/shard_map/ppermute | solution.py:297
  14.4 10.1 %collective-permute-start.6 = (bf16[192,512]{1,0:T(8,128)(2,1)S(1)}, bf16[192,512]{1,0:T(8,128)(2,1)S(1)}, u32[]{:S(2)}, u32[]{:S(2)}) collective-permute-start(bf16[192,512]{1,0:T(8,128)(2,1)S(1)} %collective-permute-done.4.q_ref), channel_id=1, source_target_pairs={{0,1},{1,0},{2,3},{3,2},{4,5},{5,4},{6,7},{7,6},{8,9},{9,8},{10,11... | collective-permute-start | bytes 589832 | tf_op jit(solution)/shard_map/ppermute | solution.py:297
  19.9 7.0 %collective-permute-start.17 = (bf16[192,512]{1,0:T(8,128)(2,1)S(1)}, bf16[192,512]{1,0:T(8,128)(2,1)S(1)}, u32[]{:S(2)}, u32[]{:S(2)}) collective-permute-start(bf16[192,512]{1,0:T(8,128)(2,1)S(1)} %after.5.p_ref), channel_id=1, source_target_pairs={{0,2},{2,0},{4,6},{6,4},{8,10},{10,8},{12,14},{14,12},{1,3},{3,1},... | collective-permute-start | bytes 589832 | tf_op jit(solution)/shard_map/ppermute | solution.py:302
  20.3 7.5 %collective-permute-start.8 = (bf16[192,512]{1,0:T(8,128)(2,1)S(1)}, bf16[192,512]{1,0:T(8,128)(2,1)S(1)}, u32[]{:S(2)}, u32[]{:S(2)}) collective-permute-start(bf16[192,512]{1,0:T(8,128)(2,1)S(1)} %get-tuple-element.42), channel_id=1, source_target_pairs={{0,12},{2,14},{4,8},{6,10},{8,4},{10,6},{12,0},{14,2},{1,13},{3,15... | collective-permute-start | bytes 589832 | tf_op jit(solution)/shard_map/ppermute | solution.py:307
  22.9 6.9 %collective-permute-start.13 = (bf16[192,512]{1,0:T(8,128)(2,1)S(1)}, bf16[192,512]{1,0:T(8,128)(2,1)S(1)}, u32[]{:S(2)}, u32[]{:S(2)}) collective-permute-start(bf16[192,512]{1,0:T(8,128)(2,1)S(1)} %collective-permute-done.12.p_ref), channel_id=1, source_target_pairs={{0,2},{2,0},{4,6},{6,4},{8,10},{10,8},{12,14},{14,12},{1,3},{3,1},... | collective-permute-start | bytes 589832 | tf_op jit(solution)/shard_map/ppermute | solution.py:302
  24.5 5.3 %collective-permute-start.18 = (bf16[192,512]{1,0:T(8,128)(2,1)S(1)}, bf16[192,512]{1,0:T(8,128)(2,1)S(1)}, u32[]{:S(2)}, u32[]{:S(2)}) collective-permute-start(bf16[192,512]{1,0:T(8,128)(2,1)S(1)} %after.5.p_ref), channel_id=1, source_target_pairs={{0,1},{1,0},{2,3},{3,2},{4,5},{5,4},{6,7},{7,6},{8,9},{9,8},{10,11... | collective-permute-start | bytes 589832 | tf_op jit(solution)/shard_map/ppermute | solution.py:297
  26.3 10.3 %collective-permute-start.7 = (bf16[2,192,512]{2,1,0:T(8,128)(2,1)S(1)}, bf16[2,192,512]{2,1,0:T(8,128)(2,1)S(1)}, u32[]{:S(2)}, u32[]{:S(2)}) collective-permute-start(bf16[2,192,512]{2,1,0:T(8,128)(2,1)S(1)} %get-tuple-element.41), channel_id=1, source_target_pairs={{0,1},{1,0},{2,3},{3,2},{4,5},{5,4},{6,7},{7,6},{8,9},{9,8},{10,11... | collective-permute-start | bytes 1179656 | tf_op jit(solution)/shard_map/ppermute | solution.py:297
  26.9 3.4 %collective-permute-start.19 = (bf16[192,512]{1,0:T(8,128)(2,1)S(1)}, bf16[192,512]{1,0:T(8,128)(2,1)S(1)}, u32[]{:S(2)}, u32[]{:S(2)}) collective-permute-start(bf16[192,512]{1,0:T(8,128)(2,1)S(1)} %collective-permute-done.17.q_ref), channel_id=1, source_target_pairs={{0,1},{1,0},{2,3},{3,2},{4,5},{5,4},{6,7},{7,6},{8,9},{9,8},{10,11... | collective-permute-start | bytes 589832 | tf_op jit(solution)/shard_map/ppermute | solution.py:297
  27.8 6.4 %collective-permute-start.9 = (bf16[192,512]{1,0:T(8,128)(2,1)S(1)}, bf16[192,512]{1,0:T(8,128)(2,1)S(1)}, u32[]{:S(2)}, u32[]{:S(2)}) collective-permute-start(bf16[192,512]{1,0:T(8,128)(2,1)S(1)} %collective-permute-done.8.p_ref), channel_id=1, source_target_pairs={{0,2},{2,0},{4,6},{6,4},{8,10},{10,8},{12,14},{14,12},{1,3},{3,1},... | collective-permute-start | bytes 589832 | tf_op jit(solution)/shard_map/ppermute | solution.py:302
  29.8 4.4 %collective-permute-start.15 = (bf16[192,512]{1,0:T(8,128)(2,1)S(1)}, bf16[192,512]{1,0:T(8,128)(2,1)S(1)}, u32[]{:S(2)}, u32[]{:S(2)}) collective-permute-start(bf16[192,512]{1,0:T(8,128)(2,1)S(1)} %collective-permute-done.13.q_ref), channel_id=1, source_target_pairs={{0,1},{1,0},{2,3},{3,2},{4,5},{5,4},{6,7},{7,6},{8,9},{9,8},{10,11... | collective-permute-start | bytes 589832 | tf_op jit(solution)/shard_map/ppermute | solution.py:297
  29.8 4.9 %collective-permute-start.14 = (bf16[192,512]{1,0:T(8,128)(2,1)S(1)}, bf16[192,512]{1,0:T(8,128)(2,1)S(1)}, u32[]{:S(2)}, u32[]{:S(2)}) collective-permute-start(bf16[192,512]{1,0:T(8,128)(2,1)S(1)} %collective-permute-done.12.p_ref), channel_id=1, source_target_pairs={{0,1},{1,0},{2,3},{3,2},{4,5},{5,4},{6,7},{7,6},{8,9},{9,8},{10,11... | collective-permute-start | bytes 589832 | tf_op jit(solution)/shard_map/ppermute | solution.py:297
  30.3 29.7 %collective-permute-start.2 = (f32[2,128]{1,0:T(2,128)S(1)}, f32[2,128]{1,0:T(2,128)S(1)}, u32[]{:S(2)}, u32[]{:S(2)}) collective-permute-start(f32[2,128]{1,0:T(2,128)S(1)} %get-tuple-element.34.own_gates_ref), channel_id=1, source_target_pairs={{0,1},{1,0},{2,3},{3,2},{4,5},{5,4},{6,7},{7,6},{8,9},{9,8},{10,11... | collective-permute-start | bytes 3080 | tf_op jit(solution)/shard_map/ppermute | solution.py:297
  34.2 5.3 %collective-permute-start.10 = (bf16[192,512]{1,0:T(8,128)(2,1)S(1)}, bf16[192,512]{1,0:T(8,128)(2,1)S(1)}, u32[]{:S(2)}, u32[]{:S(2)}) collective-permute-start(bf16[192,512]{1,0:T(8,128)(2,1)S(1)} %collective-permute-done.8.p_ref), channel_id=1, source_target_pairs={{0,1},{1,0},{2,3},{3,2},{4,5},{5,4},{6,7},{7,6},{8,9},{9,8},{10,11... | collective-permute-start | bytes 589832 | tf_op jit(solution)/shard_map/ppermute | solution.py:297
  34.2 5.3 %collective-permute-start.11 = (bf16[192,512]{1,0:T(8,128)(2,1)S(1)}, bf16[192,512]{1,0:T(8,128)(2,1)S(1)}, u32[]{:S(2)}, u32[]{:S(2)}) collective-permute-start(bf16[192,512]{1,0:T(8,128)(2,1)S(1)} %collective-permute-done.9.q_ref), channel_id=1, source_target_pairs={{0,1},{1,0},{2,3},{3,2},{4,5},{5,4},{6,7},{7,6},{8,9},{9,8},{10,11... | collective-permute-start | bytes 589832 | tf_op jit(solution)/shard_map/ppermute | solution.py:297
  36.6 1.8 %collective-permute-start.20 = (bf16[2,192,512]{2,1,0:T(8,128)(2,1)S(1)}, bf16[2,192,512]{2,1,0:T(8,128)(2,1)S(1)}, u32[]{:S(2)}, u32[]{:S(2)}) collective-permute-start(bf16[2,192,512]{2,1,0:T(8,128)(2,1)S(1)} %get-tuple-element.47), channel_id=1, source_target_pairs={{0,1},{1,0},{2,3},{3,2},{4,5},{5,4},{6,7},{7,6},{8,9},{9,8},{10,11... | collective-permute-start | bytes 1179656 | tf_op jit(solution)/shard_map/ppermute | solution.py:297
  36.7 4.8 %collective-permute-start.24 = (bf16[2,192,512]{2,1,0:T(8,128)(2,1)S(1)}, bf16[2,192,512]{2,1,0:T(8,128)(2,1)S(1)}, u32[]{:S(2)}, u32[]{:S(2)}) collective-permute-start(bf16[2,192,512]{2,1,0:T(8,128)(2,1)S(1)} %get-tuple-element.50), channel_id=1, source_target_pairs={{0,1},{1,0},{2,3},{3,2},{4,5},{5,4},{6,7},{7,6},{8,9},{9,8},{10,11... | collective-permute-start | bytes 1179656 | tf_op jit(solution)/shard_map/ppermute | solution.py:297
  38.5 7.0 %collective-permute-start.27 = (bf16[192,512]{1,0:T(8,128)(2,1)S(1)}, bf16[192,512]{1,0:T(8,128)(2,1)S(1)}, u32[]{:S(2)}, u32[]{:S(2)}) collective-permute-start(bf16[192,512]{1,0:T(8,128)(2,1)S(1)} %fusion.9.refs_1_), channel_id=1, source_target_pairs={{0,2},{2,0},{4,6},{6,4},{8,10},{10,8},{12,14},{14,12},{1,3},{3,1},... | collective-permute-start | bytes 589832 | tf_op jit(solution)/shard_map/ppermute | solution.py:302
  41.4 1.8 %collective-permute-start.21 = (bf16[2,192,512]{2,1,0:T(8,128)(2,1)S(1)}, bf16[2,192,512]{2,1,0:T(8,128)(2,1)S(1)}, u32[]{:S(2)}, u32[]{:S(2)}) collective-permute-start(bf16[2,192,512]{2,1,0:T(8,128)(2,1)S(1)} %get-tuple-element.49), channel_id=1, source_target_pairs={{0,1},{1,0},{2,3},{3,2},{4,5},{5,4},{6,7},{7,6},{8,9},{9,8},{10,11... | collective-permute-start | bytes 1179656 | tf_op jit(solution)/shard_map/ppermute | solution.py:297
  43.3 7.0 %collective-permute-start.22 = (bf16[192,512]{1,0:T(8,128)(2,1)S(1)}, bf16[192,512]{1,0:T(8,128)(2,1)S(1)}, u32[]{:S(2)}, u32[]{:S(2)}) collective-permute-start(bf16[192,512]{1,0:T(8,128)(2,1)S(1)} %fusion.10.refs_1_), channel_id=1, source_target_pairs={{0,2},{2,0},{4,6},{6,4},{8,10},{10,8},{12,14},{14,12},{1,3},{3,1},... | collective-permute-start | bytes 589832 | tf_op jit(solution)/shard_map/ppermute | solution.py:302
  45.6 18.4 %collective-permute-start.28 = (bf16[192,512]{1,0:T(8,128)(2,1)S(1)}, bf16[192,512]{1,0:T(8,128)(2,1)S(1)}, u32[]{:S(2)}, u32[]{:S(2)}) collective-permute-start(bf16[192,512]{1,0:T(8,128)(2,1)S(1)} %fusion.1), channel_id=1, source_target_pairs={{0,8},{2,10},{4,12},{6,14},{8,0},{10,2},{12,4},{14,6},{1,9},{3,11}... | collective-permute-start | bytes 589832 | tf_op jit(solution)/shard_map/ppermute | solution.py:307
  49.9 6.5 %collective-permute-start.25 = (bf16[192,512]{1,0:T(8,128)(2,1)S(1)}, bf16[192,512]{1,0:T(8,128)(2,1)S(1)}, u32[]{:S(2)}, u32[]{:S(2)}) collective-permute-start(bf16[192,512]{1,0:T(8,128)(2,1)S(1)} %after.9), channel_id=1, source_target_pairs={{0,2},{2,0},{4,6},{6,4},{8,10},{10,8},{12,14},{14,12},{1,3},{3,1},... | collective-permute-start | bytes 589832 | tf_op jit(solution)/shard_map/ppermute | solution.py:302
  50.4 16.6 %collective-permute-start.29 = (bf16[192,512]{1,0:T(8,128)(2,1)S(1)}, bf16[192,512]{1,0:T(8,128)(2,1)S(1)}, u32[]{:S(2)}, u32[]{:S(2)}) collective-permute-start(bf16[192,512]{1,0:T(8,128)(2,1)S(1)} %fusion.5.refs_1_), channel_id=1, source_target_pairs={{0,12},{2,14},{4,8},{6,10},{8,4},{10,6},{12,0},{14,2},{1,13},{3,15... | collective-permute-start | bytes 589832 | tf_op jit(solution)/shard_map/ppermute | solution.py:307
  53.6 6.3 %collective-permute-start.23 = (bf16[192,512]{1,0:T(8,128)(2,1)S(1)}, bf16[192,512]{1,0:T(8,128)(2,1)S(1)}, u32[]{:S(2)}, u32[]{:S(2)}) collective-permute-start(bf16[192,512]{1,0:T(8,128)(2,1)S(1)} %after.8), channel_id=1, source_target_pairs={{0,2},{2,0},{4,6},{6,4},{8,10},{10,8},{12,14},{14,12},{1,3},{3,1},... | collective-permute-start | bytes 589832 | tf_op jit(solution)/shard_map/ppermute | solution.py:302
  56.5 10.4 %collective-permute-start.26 = (bf16[192,512]{1,0:T(8,128)(2,1)S(1)}, bf16[192,512]{1,0:T(8,128)(2,1)S(1)}, u32[]{:S(2)}, u32[]{:S(2)}) collective-permute-start(bf16[192,512]{1,0:T(8,128)(2,1)S(1)} %fusion.3), channel_id=1, source_target_pairs={{0,4},{2,6},{4,0},{6,2},{8,12},{10,14},{12,8},{14,10},{1,5},{3,7},... | collective-permute-start | bytes 589832 | tf_op jit(solution)/shard_map/ppermute | solution.py:307
  67.9 1.4 %collective-permute-start.30 = (bf16[128,512]{1,0:T(8,128)(2,1)S(1)}, bf16[128,512]{1,0:T(8,128)(2,1)S(1)}, u32[]{:S(2)}, u32[]{:S(2)}) collective-permute-start(bf16[128,512]{1,0:T(8,128)(2,1)S(1)} %get-tuple-element.52), channel_id=1, source_target_pairs={{0,1},{1,0},{2,3},{3,2},{4,5},{5,4},{6,7},{7,6},{8,9},{9,8},{10,11... | collective-permute-start | bytes 393224 | tf_op jit(solution)/shard_map/ppermute | solution.py:297

commit v16 on v15

--- a/solution.py
+++ b/solution.py
@@ -406,6 +406,8 @@
         ps[offset], qs[offset] = p, q
     for offset in [0, 1, 2, 3]:
         p, q = ps[offset], qs[offset]
+        if offset == 3:
+            q = after(q, kept[2])
         p2, q2 = swap(p), swap(q)
         if offset == 2:
             q2 = after(q2, kept[0], kept[1])

time: 70.2 us -> 68.7 us (0.979)
  starting transfers between devices: 30.5 us -> 28.5 us
    ppermute x6, starting transfers between devices: 16 us -> 14.6 us  [exchange(): lax.ppermute(values, 'expert', [(i, i ^ 2 * offset) for i in range(owners)])]
    ppermute x17, waiting for transfers between devices: 4.95 us -> 3.9 us  [swap(): return lax.ppermute(values, 'section', [(0, 1), (1, 0)])]
    ppermute x8, waiting for transfers between devices: 7.16 us -> 8.14 us  [swap_owner(): return lax.ppermute(values, 'expert', [(i, i ^ 1) for i in range(owners)])]
  transfers between devices with their start and end apart: 31 -> 31, of which waited for: 15 -> 14; matrix products, arithmetic and copies ran while one was open for 1% -> 1% of each run, Pallas kernels for 16% -> 17%
where the time goes in v16:
time: 68.7 us; the launch traced here: 68.5 us
  starting transfers between devices  28.5 us (41%)
  waiting for transfers between devices  23.5 us (34%)
  Pallas kernels  14.8 us (22%)
  between operations  0.9 us (1%)
    pallas_call x10, Pallas kernels, call(): pl.pallas_call(kernel, out_shape=tuple((jax.ShapeDtypeStruct(*out) for ou...  14.8 us
    ppermute x6, starting transfers between devices, exchange(): lax.ppermute(values, 'expert', [(i, i ^ 2 * offset) for i in range(owners)])  14.6 us
    ppermute x6, waiting for transfers between devices, exchange(): lax.ppermute(values, 'expert', [(i, i ^ 2 * offset) for i in range(owners)])  11.5 us
    ppermute x8, starting transfers between devices, swap_owner(): return lax.ppermute(values, 'expert', [(i, i ^ 1) for i in range(owners)])  10.7 us
    ppermute x8, waiting for transfers between devices, swap_owner(): return lax.ppermute(values, 'expert', [(i, i ^ 1) for i in range(owners)])  8.14 us
    ppermute x17, waiting for transfers between devices, swap(): return lax.ppermute(values, 'section', [(0, 1), (1, 0)])  3.9 us
    ppermute x17, starting transfers between devices, swap(): return lax.ppermute(values, 'section', [(0, 1), (1, 0)])  3.22 us
  transfers between devices with their start and end apart: 31, of which 14 were waited for; matrix products, arithmetic and copies ran while one was open for 1% of the time, Pallas kernels for 17%

profile of v16, /device:TPU:0, one launch (start us, length us, event | category | flops | bytes accessed | tf_op | source)
XLA Modules:
  0.0 68.5 jit_solution(11688503846204692841)
XLA Ops:
  0.0 0.5 collective-permute-start
  0.5 0.1 collective-permute-start.1
  1.2 1.8 %attend_own.1 = (bf16[128,512]{1,0:T(8,128)(2,1)S(1)}, bf16[128,512]{1,0:T(8,128)(2,1)S(1)}, bf16[128,512]{1,0:T(8,128)(2,1)S(1)}) custom-call(s32[1]{0:T(128)} %bitcast.core_ref, s32[1]{0:T(128)S(6)} %copy.24.source_ref, bf16[1,128,1024]{2,1,0:T(8,128)(2,1)} %x_in.1, f32[1,1024]{1,0:T(1,128)} %bitcast.40, bf16[2,80,512]{2,1,0:T(8,128)(2,1)} %keys_in.1, ...), custom_call_target="tpu_custom_call" | custom-call | tf_op jit(solution)/shard_map/attend_own/pallas_call | solution.py:25
  2.9 0.0 collective-permute-done.1.values_ref
  3.0 1.2 %attend_other.1 = (bf16[128,1024]{1,0:T(8,128)(2,1)S(1)}, bf16[128,512]{1,0:T(8,128)(2,1)S(1)}, bf16[128,512]{1,0:T(8,128)(2,1)S(1)}, f32[2,128]{1,0:T(2,128)S(1)}, s32[2,2,128]{2,1,0:T(2,128)S(1)}) custom-call(s32[1]{0:T(128)} %bitcast.core_ref, s32[1]{0:T(128)S(6)} %copy.24.source_ref, bf16[128,512]{1,0:T(8,128)(2,1)S(1)} %get-tuple-element.29.own_ref, ...), custom_call_target="tpu_custom_call" | custom-call | tf_op jit(solution)/shard_map/attend_other/pallas_call | solution.py:25
  4.2 0.5 collective-permute-start.3
  4.7 1.0 %collective-permute-done.3.other_ref = bf16[128,512]{1,0:T(8,128)(2,1)S(1)} collective-permute-done((bf16[128,512]{1,0:T(8,128)(2,1)S(1)}, bf16[128,512]{1,0:T(8,128)(2,1)S(1)}, u32[]{:S(2)}, u32[]{:S(2)}) %collective-permute-start.3) | collective-permute-done | bytes 131104 | tf_op jit(solution)/shard_map/ppermute | solution.py:297
  5.7 0.5 select.5
  6.2 2.9 %collective-permute-start.4 = (bf16[192,512]{1,0:T(8,128)(2,1)S(1)}, bf16[192,512]{1,0:T(8,128)(2,1)S(1)}, u32[]{:S(2)}, u32[]{:S(2)}) collective-permute-start(bf16[192,512]{1,0:T(8,128)(2,1)S(1)} %get-tuple-element.37.p_ref), channel_id=1, source_target_pairs={{0,2},{2,0},{4,6},{6,4},{8,10},{10,8},{12,14},{14,12},{1,3},{3,1},... | collective-permute-start | bytes 589832 | tf_op jit(solution)/shard_map/ppermute | solution.py:302
  9.2 1.6 %collective-permute-start.14 = (bf16[192,512]{1,0:T(8,128)(2,1)S(1)}, bf16[192,512]{1,0:T(8,128)(2,1)S(1)}, u32[]{:S(2)}, u32[]{:S(2)}) collective-permute-start(bf16[192,512]{1,0:T(8,128)(2,1)S(1)} %get-tuple-element.44), channel_id=1, source_target_pairs={{0,4},{2,6},{4,0},{6,2},{8,12},{10,14},{12,8},{14,10},{1,5},{3,7},... | collective-permute-start | bytes 589832 | tf_op jit(solution)/shard_map/ppermute | solution.py:307
  10.7 2.6 %collective-permute-start.10 = (bf16[192,512]{1,0:T(8,128)(2,1)S(1)}, bf16[192,512]{1,0:T(8,128)(2,1)S(1)}, u32[]{:S(2)}, u32[]{:S(2)}) collective-permute-start(bf16[192,512]{1,0:T(8,128)(2,1)S(1)} %get-tuple-element.43), channel_id=1, source_target_pairs={{0,8},{2,10},{4,12},{6,14},{8,0},{10,2},{12,4},{14,6},{1,9},{3,11}... | collective-permute-start | bytes 589832 | tf_op jit(solution)/shard_map/ppermute | solution.py:307
  13.3 1.1 %collective-permute-done.4.q_ref = bf16[192,512]{1,0:T(8,128)(2,1)S(1)} collective-permute-done((bf16[192,512]{1,0:T(8,128)(2,1)S(1)}, bf16[192,512]{1,0:T(8,128)(2,1)S(1)}, u32[]{:S(2)}, u32[]{:S(2)}) %collective-permute-start.4) | collective-permute-done | bytes 196640 | tf_op jit(solution)/shard_map/ppermute | solution.py:302
  14.4 2.2 %load.1 = (bf16[1024,1024]{1,0:T(8,128)(2,1)S(1)}, bf16[1024,1024]{1,0:T(8,128)(2,1)S(1)}) custom-call(bf16[1024,1024]{1,0:T(8,128)(2,1)} %in_in.1, bf16[1024,1024]{1,0:T(8,128)(2,1)} %out_in.1), custom_call_target="tpu_custom_call" | custom-call | tf_op jit(solution)/shard_map/load/pallas_call | solution.py:25
  16.6 3.3 %collective-permute-done.14.refs_0_ = bf16[192,512]{1,0:T(8,128)(2,1)S(1)} collective-permute-done((bf16[192,512]{1,0:T(8,128)(2,1)S(1)}, bf16[192,512]{1,0:T(8,128)(2,1)S(1)}, u32[]{:S(2)}, u32[]{:S(2)}) %collective-permute-start.14) | collective-permute-done | bytes 196640 | tf_op jit(solution)/shard_map/ppermute | solution.py:307
  19.9 0.4 collective-permute-start.15
  20.3 2.0 %collective-permute-done.10.p_ref = bf16[192,512]{1,0:T(8,128)(2,1)S(1)} collective-permute-done((bf16[192,512]{1,0:T(8,128)(2,1)S(1)}, bf16[192,512]{1,0:T(8,128)(2,1)S(1)}, u32[]{:S(2)}, u32[]{:S(2)}) %collective-permute-start.10) | collective-permute-done | bytes 196640 | tf_op jit(solution)/shard_map/ppermute | solution.py:307
  22.3 0.5 collective-permute-start.11
  22.8 2.5 %collective-permute-start.8 = (bf16[192,512]{1,0:T(8,128)(2,1)S(1)}, bf16[192,512]{1,0:T(8,128)(2,1)S(1)}, u32[]{:S(2)}, u32[]{:S(2)}) collective-permute-start(bf16[192,512]{1,0:T(8,128)(2,1)S(1)} %get-tuple-element.42), channel_id=1, source_target_pairs={{0,12},{2,14},{4,8},{6,10},{8,4},{10,6},{12,0},{14,2},{1,13},{3,15... | collective-permute-start | bytes 589832 | tf_op jit(solution)/shard_map/ppermute | solution.py:307
  25.3 0.0 collective-permute-done.5.p2_ref
  25.3 1.8 %expert.4 = (f32[2,192,512]{2,1,0:T(8,128)S(1)}, bf16[2,192,512]{2,1,0:T(8,128)(2,1)S(1)}) custom-call(s32[1]{0:T(128)} %bitcast.core_ref, bf16[192,512]{1,0:T(8,128)(2,1)S(1)} %get-tuple-element.37.p_ref, bf16[192,512]{1,0:T(8,128)(2,1)S(1)} %collective-permute-done.4.q_ref, bf16[192,512]{1,0:T(8,128)(2,1)S(1)} %collective-permute-done.5.p2_ref, ...), custom_call_target="tpu_custom_call" | custom-call | tf_op jit(solution)/shard_map/expert/pallas_call | solution.py:25
  27.2 0.6 collective-permute-start.7
  27.7 0.1 collective-permute-start.17
  27.8 1.8 %collective-permute-done.11.q_ref = bf16[192,512]{1,0:T(8,128)(2,1)S(1)} collective-permute-done((bf16[192,512]{1,0:T(8,128)(2,1)S(1)}, bf16[192,512]{1,0:T(8,128)(2,1)S(1)}, u32[]{:S(2)}, u32[]{:S(2)}) %collective-permute-start.11) | collective-permute-done | bytes 196640 | tf_op jit(solution)/shard_map/ppermute | solution.py:302
  29.6 0.0 collective-permute-start.13
  29.6 0.8 %collective-permute-done.8.p_ref = bf16[192,512]{1,0:T(8,128)(2,1)S(1)} collective-permute-done((bf16[192,512]{1,0:T(8,128)(2,1)S(1)}, bf16[192,512]{1,0:T(8,128)(2,1)S(1)}, u32[]{:S(2)}, u32[]{:S(2)}) %collective-permute-start.8) | collective-permute-done | bytes 196640 | tf_op jit(solution)/shard_map/ppermute | solution.py:307
  30.4 0.0 collective-permute-start.12
  30.4 0.0 collective-permute-done.16.p2_ref
  30.4 1.5 %collective-permute-start.9 = (bf16[192,512]{1,0:T(8,128)(2,1)S(1)}, bf16[192,512]{1,0:T(8,128)(2,1)S(1)}, u32[]{:S(2)}, u32[]{:S(2)}) collective-permute-start(bf16[192,512]{1,0:T(8,128)(2,1)S(1)} %collective-permute-done.8.p_ref), channel_id=1, source_target_pairs={{0,2},{2,0},{4,6},{6,4},{8,10},{10,8},{12,14},{14,12},{1,3},{3,1},... | collective-permute-start | bytes 589832 | tf_op jit(solution)/shard_map/ppermute | solution.py:302
  31.9 0.0 collective-permute-done.17.q2_ref
  31.9 0.2 collective-permute-start.2
  32.1 1.8 %expert.5 = (f32[2,192,512]{2,1,0:T(8,128)S(1)}, bf16[2,192,512]{2,1,0:T(8,128)(2,1)S(1)}) custom-call(s32[1]{0:T(128)} %bitcast.core_ref, bf16[192,512]{1,0:T(8,128)(2,1)S(1)} %after.6.p_ref, bf16[192,512]{1,0:T(8,128)(2,1)S(1)} %collective-permute-done.15.q_ref, bf16[192,512]{1,0:T(8,128)(2,1)S(1)} %collective-permute-done.16.p2_ref, ...), custom_call_target="tpu_custom_call" | custom-call | tf_op jit(solution)/shard_map/expert/pallas_call | solution.py:25
  34.0 0.0 collective-permute-done.13.refs_0_
  34.0 0.4 collective-permute-start.18
  34.3 0.0 collective-permute-done.12.p2_ref
  34.4 1.8 %expert.6 = (f32[2,192,512]{2,1,0:T(8,128)S(1)}, bf16[2,192,512]{2,1,0:T(8,128)(2,1)S(1)}) custom-call(s32[1]{0:T(128)} %bitcast.core_ref, bf16[192,512]{1,0:T(8,128)(2,1)S(1)} %collective-permute-done.10.p_ref, bf16[192,512]{1,0:T(8,128)(2,1)S(1)} %collective-permute-done.11.q_ref, bf16[192,512]{1,0:T(8,128)(2,1)S(1)} %collective-permute-done.12.p2_ref, ...), custom_call_target="tpu_custom_call" | custom-call | tf_op jit(solution)/shard_map/expert/pallas_call | solution.py:25
  36.2 0.3 collective-permute-start.20
  36.5 1.2 %collective-permute-done.9.refs_0_ = bf16[192,512]{1,0:T(8,128)(2,1)S(1)} collective-permute-done((bf16[192,512]{1,0:T(8,128)(2,1)S(1)}, bf16[192,512]{1,0:T(8,128)(2,1)S(1)}, u32[]{:S(2)}, u32[]{:S(2)}) %collective-permute-start.9) | collective-permute-done | bytes 196640 | tf_op jit(solution)/shard_map/ppermute | solution.py:302
  37.7 0.0 collective-permute-start.24
  37.7 0.5 collective-permute-start.19
  38.2 0.1 convert_add_fusion.3
  38.4 0.0 collective-permute-done.20
  38.4 0.1 convert_add_fusion.2
  38.5 1.6 %collective-permute-start.27 = (bf16[192,512]{1,0:T(8,128)(2,1)S(1)}, bf16[192,512]{1,0:T(8,128)(2,1)S(1)}, u32[]{:S(2)}, u32[]{:S(2)}) collective-permute-start(bf16[192,512]{1,0:T(8,128)(2,1)S(1)} %fusion.9.refs_1_), channel_id=1, source_target_pairs={{0,2},{2,0},{4,6},{6,4},{8,10},{10,8},{12,14},{14,12},{1,3},{3,1},... | collective-permute-start | bytes 589832 | tf_op jit(solution)/shard_map/ppermute | solution.py:302
  40.1 0.0 collective-permute-done.19.refs_0_
  40.1 1.8 %expert.7 = (f32[2,192,512]{2,1,0:T(8,128)S(1)}, bf16[2,192,512]{2,1,0:T(8,128)(2,1)S(1)}) custom-call(s32[1]{0:T(128)} %bitcast.core_ref, bf16[192,512]{1,0:T(8,128)(2,1)S(1)} %collective-permute-done.8.p_ref, bf16[192,512]{1,0:T(8,128)(2,1)S(1)} %after.8.q_ref, bf16[192,512]{1,0:T(8,128)(2,1)S(1)} %collective-permute-done.18.p2_ref, ...), custom_call_target="tpu_custom_call" | custom-call | tf_op jit(solution)/shard_map/expert/pallas_call | solution.py:25
  42.0 0.1 collective-permute-start.21
  42.1 0.1 convert_add_fusion
  42.2 1.5 %collective-permute-done.21 = bf16[2,192,512]{2,1,0:T(8,128)(2,1)S(1)} collective-permute-done((bf16[2,192,512]{2,1,0:T(8,128)(2,1)S(1)}, bf16[2,192,512]{2,1,0:T(8,128)(2,1)S(1)}, u32[]{:S(2)}, u32[]{:S(2)}) %collective-permute-start.21) | collective-permute-done | bytes 393248 | tf_op jit(solution)/shard_map/ppermute | solution.py:297
  43.8 0.1 convert_add_fusion.1
  43.9 1.2 %collective-permute-start.22 = (bf16[192,512]{1,0:T(8,128)(2,1)S(1)}, bf16[192,512]{1,0:T(8,128)(2,1)S(1)}, u32[]{:S(2)}, u32[]{:S(2)}) collective-permute-start(bf16[192,512]{1,0:T(8,128)(2,1)S(1)} %fusion.10.refs_1_), channel_id=1, source_target_pairs={{0,2},{2,0},{4,6},{6,4},{8,10},{10,8},{12,14},{14,12},{1,3},{3,1},... | collective-permute-start | bytes 589832 | tf_op jit(solution)/shard_map/ppermute | solution.py:302
  45.1 0.4 collective-permute-done.27
  45.5 2.5 %collective-permute-start.28 = (bf16[192,512]{1,0:T(8,128)(2,1)S(1)}, bf16[192,512]{1,0:T(8,128)(2,1)S(1)}, u32[]{:S(2)}, u32[]{:S(2)}) collective-permute-start(bf16[192,512]{1,0:T(8,128)(2,1)S(1)} %fusion.1), channel_id=1, source_target_pairs={{0,8},{2,10},{4,12},{6,14},{8,0},{10,2},{12,4},{14,6},{1,9},{3,11}... | collective-permute-start | bytes 589832 | tf_op jit(solution)/shard_map/ppermute | solution.py:307
  48.0 1.5 %collective-permute-start.25 = (bf16[192,512]{1,0:T(8,128)(2,1)S(1)}, bf16[192,512]{1,0:T(8,128)(2,1)S(1)}, u32[]{:S(2)}, u32[]{:S(2)}) collective-permute-start(bf16[192,512]{1,0:T(8,128)(2,1)S(1)} %after.11), channel_id=1, source_target_pairs={{0,2},{2,0},{4,6},{6,4},{8,10},{10,8},{12,14},{14,12},{1,3},{3,1},... | collective-permute-start | bytes 589832 | tf_op jit(solution)/shard_map/ppermute | solution.py:302
  49.5 2.2 %collective-permute-done.22 = bf16[192,512]{1,0:T(8,128)(2,1)S(1)} collective-permute-done((bf16[192,512]{1,0:T(8,128)(2,1)S(1)}, bf16[192,512]{1,0:T(8,128)(2,1)S(1)}, u32[]{:S(2)}, u32[]{:S(2)}) %collective-permute-start.22) | collective-permute-done | bytes 196640 | tf_op jit(solution)/shard_map/ppermute | solution.py:302
  51.8 2.5 %collective-permute-start.29 = (bf16[192,512]{1,0:T(8,128)(2,1)S(1)}, bf16[192,512]{1,0:T(8,128)(2,1)S(1)}, u32[]{:S(2)}, u32[]{:S(2)}) collective-permute-start(bf16[192,512]{1,0:T(8,128)(2,1)S(1)} %fusion.5.refs_1_), channel_id=1, source_target_pairs={{0,12},{2,14},{4,8},{6,10},{8,4},{10,6},{12,0},{14,2},{1,13},{3,15... | collective-permute-start | bytes 589832 | tf_op jit(solution)/shard_map/ppermute | solution.py:307
  54.3 1.1 %collective-permute-start.23 = (bf16[192,512]{1,0:T(8,128)(2,1)S(1)}, bf16[192,512]{1,0:T(8,128)(2,1)S(1)}, u32[]{:S(2)}, u32[]{:S(2)}) collective-permute-start(bf16[192,512]{1,0:T(8,128)(2,1)S(1)} %after.10), channel_id=1, source_target_pairs={{0,2},{2,0},{4,6},{6,4},{8,10},{10,8},{12,14},{14,12},{1,3},{3,1},... | collective-permute-start | bytes 589832 | tf_op jit(solution)/shard_map/ppermute | solution.py:302
  55.4 3.0 %collective-permute-start.26 = (bf16[192,512]{1,0:T(8,128)(2,1)S(1)}, bf16[192,512]{1,0:T(8,128)(2,1)S(1)}, u32[]{:S(2)}, u32[]{:S(2)}) collective-permute-start(bf16[192,512]{1,0:T(8,128)(2,1)S(1)} %fusion.3), channel_id=1, source_target_pairs={{0,4},{2,6},{4,0},{6,2},{8,12},{10,14},{12,8},{14,10},{1,5},{3,7},... | collective-permute-start | bytes 589832 | tf_op jit(solution)/shard_map/ppermute | solution.py:307
  58.4 1.6 %collective-permute-done.23 = bf16[192,512]{1,0:T(8,128)(2,1)S(1)} collective-permute-done((bf16[192,512]{1,0:T(8,128)(2,1)S(1)}, bf16[192,512]{1,0:T(8,128)(2,1)S(1)}, u32[]{:S(2)}, u32[]{:S(2)}) %collective-permute-start.23) | collective-permute-done | bytes 196640 | tf_op jit(solution)/shard_map/ppermute | solution.py:302
  60.0 2.8 %collective-permute-done.28.rest_2_ = bf16[192,512]{1,0:T(8,128)(2,1)S(1)} collective-permute-done((bf16[192,512]{1,0:T(8,128)(2,1)S(1)}, bf16[192,512]{1,0:T(8,128)(2,1)S(1)}, u32[]{:S(2)}, u32[]{:S(2)}) %collective-permute-start.28) | collective-permute-done | bytes 196640 | tf_op jit(solution)/shard_map/ppermute | solution.py:307
  62.8 2.6 %collective-permute-done.26.rest_1_ = bf16[192,512]{1,0:T(8,128)(2,1)S(1)} collective-permute-done((bf16[192,512]{1,0:T(8,128)(2,1)S(1)}, bf16[192,512]{1,0:T(8,128)(2,1)S(1)}, u32[]{:S(2)}, u32[]{:S(2)}) %collective-permute-start.26) | collective-permute-done | bytes 196640 | tf_op jit(solution)/shard_map/ppermute | solution.py:307
  65.4 0.9 %combine.1 = (f32[128,512]{1,0:T(8,128)S(1)}, bf16[128,512]{1,0:T(8,128)(2,1)S(1)}) custom-call(s32[1]{0:T(128)} %bitcast.core_ref, s32[1]{0:T(128)} %bitcast.5.line_ref, s32[2,2,128]{2,1,0:T(2,128)S(1)} %get-tuple-element.33.routes_ref, f32[2,128]{1,0:T(2,128)S(1)} %get-tuple-element.34.own_gates_ref, f32[2,128]{1,0:T(2,128)S(1)} %collective-permute-done.2.other_gates_ref, ...), custom_call_target="tpu_custom_call" | custom-call | tf_op jit(solution)/shard_map/combine/pallas_call | solution.py:25
  66.3 0.1 collective-permute-start.30
  66.4 1.3 %collective-permute-done.30.other_ref = bf16[128,512]{1,0:T(8,128)(2,1)S(1)} collective-permute-done((bf16[128,512]{1,0:T(8,128)(2,1)S(1)}, bf16[128,512]{1,0:T(8,128)(2,1)S(1)}, u32[]{:S(2)}, u32[]{:S(2)}) %collective-permute-start.30) | collective-permute-done | bytes 131104 | tf_op jit(solution)/shard_map/ppermute | solution.py:297
  67.8 0.8 %finish.1 = bf16[128,1024]{1,0:T(8,128)(2,1)} custom-call(s32[1]{0:T(128)} %bitcast.core_ref, bf16[128,1024]{1,0:T(8,128)(2,1)S(1)} %get-tuple-element.32.state_ref, f32[128,512]{1,0:T(8,128)S(1)} %get-tuple-element.51.own_ref, bf16[128,512]{1,0:T(8,128)(2,1)S(1)} %collective-permute-done.30.other_ref), custom_call_target="tpu_custom_call" | custom-call | tf_op jit(solution)/shard_map/finish/pallas_call | solution.py:25
  (26 shorter events, 0.3 us)
Async XLA Ops:
  0.0 2.9 %collective-permute-start = (bf16[2,80,512]{2,1,0:T(8,128)(2,1)}, bf16[2,80,512]{2,1,0:T(8,128)(2,1)S(1)}, u32[]{:S(2)}, u32[]{:S(2)}) collective-permute-start(bf16[2,80,512]{2,1,0:T(8,128)(2,1)} %keys_in.1), channel_id=1, source_target_pairs={{0,1},{1,0},{2,3},{3,2},{4,5},{5,4},{6,7},{7,6},{8,9},{9,8},{10,11... | collective-permute-start | bytes 491528 | tf_op jit(solution)/shard_map/ppermute | solution.py:297
  0.5 2.5 %collective-permute-start.1 = (bf16[2,80,512]{2,1,0:T(8,128)(2,1)}, bf16[2,80,512]{2,1,0:T(8,128)(2,1)S(1)}, u32[]{:S(2)}, u32[]{:S(2)}) collective-permute-start(bf16[2,80,512]{2,1,0:T(8,128)(2,1)} %values_in.1), channel_id=1, source_target_pairs={{0,1},{1,0},{2,3},{3,2},{4,5},{5,4},{6,7},{7,6},{8,9},{9,8},{10,11... | collective-permute-start | bytes 491528 | tf_op jit(solution)/shard_map/ppermute | solution.py:297
  4.2 1.5 %collective-permute-start.3 = (bf16[128,512]{1,0:T(8,128)(2,1)S(1)}, bf16[128,512]{1,0:T(8,128)(2,1)S(1)}, u32[]{:S(2)}, u32[]{:S(2)}) collective-permute-start(bf16[128,512]{1,0:T(8,128)(2,1)S(1)} %get-tuple-element.36), channel_id=1, source_target_pairs={{0,1},{1,0},{2,3},{3,2},{4,5},{5,4},{6,7},{7,6},{8,9},{9,8},{10,11... | collective-permute-start | bytes 393224 | tf_op jit(solution)/shard_map/ppermute | solution.py:297
  6.2 8.1 %collective-permute-start.4 = (bf16[192,512]{1,0:T(8,128)(2,1)S(1)}, bf16[192,512]{1,0:T(8,128)(2,1)S(1)}, u32[]{:S(2)}, u32[]{:S(2)}) collective-permute-start(bf16[192,512]{1,0:T(8,128)(2,1)S(1)} %get-tuple-element.37.p_ref), channel_id=1, source_target_pairs={{0,2},{2,0},{4,6},{6,4},{8,10},{10,8},{12,14},{14,12},{1,3},{3,1},... | collective-permute-start | bytes 589832 | tf_op jit(solution)/shard_map/ppermute | solution.py:302
  9.2 10.8 %collective-permute-start.14 = (bf16[192,512]{1,0:T(8,128)(2,1)S(1)}, bf16[192,512]{1,0:T(8,128)(2,1)S(1)}, u32[]{:S(2)}, u32[]{:S(2)}) collective-permute-start(bf16[192,512]{1,0:T(8,128)(2,1)S(1)} %get-tuple-element.44), channel_id=1, source_target_pairs={{0,4},{2,6},{4,0},{6,2},{8,12},{10,14},{12,8},{14,10},{1,5},{3,7},... | collective-permute-start | bytes 589832 | tf_op jit(solution)/shard_map/ppermute | solution.py:307
  10.7 11.6 %collective-permute-start.10 = (bf16[192,512]{1,0:T(8,128)(2,1)S(1)}, bf16[192,512]{1,0:T(8,128)(2,1)S(1)}, u32[]{:S(2)}, u32[]{:S(2)}) collective-permute-start(bf16[192,512]{1,0:T(8,128)(2,1)S(1)} %get-tuple-element.43), channel_id=1, source_target_pairs={{0,8},{2,10},{4,12},{6,14},{8,0},{10,2},{12,4},{14,6},{1,9},{3,11}... | collective-permute-start | bytes 589832 | tf_op jit(solution)/shard_map/ppermute | solution.py:307
  13.3 12.0 %collective-permute-start.5 = (bf16[192,512]{1,0:T(8,128)(2,1)S(1)}, bf16[192,512]{1,0:T(8,128)(2,1)S(1)}, u32[]{:S(2)}, u32[]{:S(2)}) collective-permute-start(bf16[192,512]{1,0:T(8,128)(2,1)S(1)} %get-tuple-element.37.p_ref), channel_id=1, source_target_pairs={{0,1},{1,0},{2,3},{3,2},{4,5},{5,4},{6,7},{7,6},{8,9},{9,8},{10,11... | collective-permute-start | bytes 589832 | tf_op jit(solution)/shard_map/ppermute | solution.py:297
  14.4 10.9 %collective-permute-start.6 = (bf16[192,512]{1,0:T(8,128)(2,1)S(1)}, bf16[192,512]{1,0:T(8,128)(2,1)S(1)}, u32[]{:S(2)}, u32[]{:S(2)}) collective-permute-start(bf16[192,512]{1,0:T(8,128)(2,1)S(1)} %collective-permute-done.4.q_ref), channel_id=1, source_target_pairs={{0,1},{1,0},{2,3},{3,2},{4,5},{5,4},{6,7},{7,6},{8,9},{9,8},{10,11... | collective-permute-start | bytes 589832 | tf_op jit(solution)/shard_map/ppermute | solution.py:297
  19.9 7.8 %collective-permute-start.15 = (bf16[192,512]{1,0:T(8,128)(2,1)S(1)}, bf16[192,512]{1,0:T(8,128)(2,1)S(1)}, u32[]{:S(2)}, u32[]{:S(2)}) collective-permute-start(bf16[192,512]{1,0:T(8,128)(2,1)S(1)} %after.6.p_ref), channel_id=1, source_target_pairs={{0,2},{2,0},{4,6},{6,4},{8,10},{10,8},{12,14},{14,12},{1,3},{3,1},... | collective-permute-start | bytes 589832 | tf_op jit(solution)/shard_map/ppermute | solution.py:302
  22.3 7.3 %collective-permute-start.11 = (bf16[192,512]{1,0:T(8,128)(2,1)S(1)}, bf16[192,512]{1,0:T(8,128)(2,1)S(1)}, u32[]{:S(2)}, u32[]{:S(2)}) collective-permute-start(bf16[192,512]{1,0:T(8,128)(2,1)S(1)} %collective-permute-done.10.p_ref), channel_id=1, source_target_pairs={{0,2},{2,0},{4,6},{6,4},{8,10},{10,8},{12,14},{14,12},{1,3},{3,1},... | collective-permute-start | bytes 589832 | tf_op jit(solution)/shard_map/ppermute | solution.py:302
  22.8 7.6 %collective-permute-start.8 = (bf16[192,512]{1,0:T(8,128)(2,1)S(1)}, bf16[192,512]{1,0:T(8,128)(2,1)S(1)}, u32[]{:S(2)}, u32[]{:S(2)}) collective-permute-start(bf16[192,512]{1,0:T(8,128)(2,1)S(1)} %get-tuple-element.42), channel_id=1, source_target_pairs={{0,12},{2,14},{4,8},{6,10},{8,4},{10,6},{12,0},{14,2},{1,13},{3,15... | collective-permute-start | bytes 589832 | tf_op jit(solution)/shard_map/ppermute | solution.py:307
  25.3 5.1 %collective-permute-start.16 = (bf16[192,512]{1,0:T(8,128)(2,1)S(1)}, bf16[192,512]{1,0:T(8,128)(2,1)S(1)}, u32[]{:S(2)}, u32[]{:S(2)}) collective-permute-start(bf16[192,512]{1,0:T(8,128)(2,1)S(1)} %after.6.p_ref), channel_id=1, source_target_pairs={{0,1},{1,0},{2,3},{3,2},{4,5},{5,4},{6,7},{7,6},{8,9},{9,8},{10,11... | collective-permute-start | bytes 589832 | tf_op jit(solution)/shard_map/ppermute | solution.py:297
  27.2 10.6 %collective-permute-start.7 = (bf16[2,192,512]{2,1,0:T(8,128)(2,1)S(1)}, bf16[2,192,512]{2,1,0:T(8,128)(2,1)S(1)}, u32[]{:S(2)}, u32[]{:S(2)}) collective-permute-start(bf16[2,192,512]{2,1,0:T(8,128)(2,1)S(1)} %get-tuple-element.41), channel_id=1, source_target_pairs={{0,1},{1,0},{2,3},{3,2},{4,5},{5,4},{6,7},{7,6},{8,9},{9,8},{10,11... | collective-permute-start | bytes 1179656 | tf_op jit(solution)/shard_map/ppermute | solution.py:297
  27.7 4.2 %collective-permute-start.17 = (bf16[192,512]{1,0:T(8,128)(2,1)S(1)}, bf16[192,512]{1,0:T(8,128)(2,1)S(1)}, u32[]{:S(2)}, u32[]{:S(2)}) collective-permute-start(bf16[192,512]{1,0:T(8,128)(2,1)S(1)} %collective-permute-done.15.q_ref), channel_id=1, source_target_pairs={{0,1},{1,0},{2,3},{3,2},{4,5},{5,4},{6,7},{7,6},{8,9},{9,8},{10,11... | collective-permute-start | bytes 589832 | tf_op jit(solution)/shard_map/ppermute | solution.py:297
  29.6 4.4 %collective-permute-start.13 = (bf16[192,512]{1,0:T(8,128)(2,1)S(1)}, bf16[192,512]{1,0:T(8,128)(2,1)S(1)}, u32[]{:S(2)}, u32[]{:S(2)}) collective-permute-start(bf16[192,512]{1,0:T(8,128)(2,1)S(1)} %collective-permute-done.11.q_ref), channel_id=1, source_target_pairs={{0,1},{1,0},{2,3},{3,2},{4,5},{5,4},{6,7},{7,6},{8,9},{9,8},{10,11... | collective-permute-start | bytes 589832 | tf_op jit(solution)/shard_map/ppermute | solution.py:297
  30.4 4.0 %collective-permute-start.12 = (bf16[192,512]{1,0:T(8,128)(2,1)S(1)}, bf16[192,512]{1,0:T(8,128)(2,1)S(1)}, u32[]{:S(2)}, u32[]{:S(2)}) collective-permute-start(bf16[192,512]{1,0:T(8,128)(2,1)S(1)} %collective-permute-done.10.p_ref), channel_id=1, source_target_pairs={{0,1},{1,0},{2,3},{3,2},{4,5},{5,4},{6,7},{7,6},{8,9},{9,8},{10,11... | collective-permute-start | bytes 589832 | tf_op jit(solution)/shard_map/ppermute | solution.py:297
  30.4 7.3 %collective-permute-start.9 = (bf16[192,512]{1,0:T(8,128)(2,1)S(1)}, bf16[192,512]{1,0:T(8,128)(2,1)S(1)}, u32[]{:S(2)}, u32[]{:S(2)}) collective-permute-start(bf16[192,512]{1,0:T(8,128)(2,1)S(1)} %collective-permute-done.8.p_ref), channel_id=1, source_target_pairs={{0,2},{2,0},{4,6},{6,4},{8,10},{10,8},{12,14},{14,12},{1,3},{3,1},... | collective-permute-start | bytes 589832 | tf_op jit(solution)/shard_map/ppermute | solution.py:302
  31.9 28.1 %collective-permute-start.2 = (f32[2,128]{1,0:T(2,128)S(1)}, f32[2,128]{1,0:T(2,128)S(1)}, u32[]{:S(2)}, u32[]{:S(2)}) collective-permute-start(f32[2,128]{1,0:T(2,128)S(1)} %get-tuple-element.34.own_gates_ref), channel_id=1, source_target_pairs={{0,1},{1,0},{2,3},{3,2},{4,5},{5,4},{6,7},{7,6},{8,9},{9,8},{10,11... | collective-permute-start | bytes 3080 | tf_op jit(solution)/shard_map/ppermute | solution.py:297
  34.0 6.1 %collective-permute-start.18 = (bf16[192,512]{1,0:T(8,128)(2,1)S(1)}, bf16[192,512]{1,0:T(8,128)(2,1)S(1)}, u32[]{:S(2)}, u32[]{:S(2)}) collective-permute-start(bf16[192,512]{1,0:T(8,128)(2,1)S(1)} %collective-permute-done.8.p_ref), channel_id=1, source_target_pairs={{0,1},{1,0},{2,3},{3,2},{4,5},{5,4},{6,7},{7,6},{8,9},{9,8},{10,11... | collective-permute-start | bytes 589832 | tf_op jit(solution)/shard_map/ppermute | solution.py:297
  36.2 2.2 %collective-permute-start.20 = (bf16[2,192,512]{2,1,0:T(8,128)(2,1)S(1)}, bf16[2,192,512]{2,1,0:T(8,128)(2,1)S(1)}, u32[]{:S(2)}, u32[]{:S(2)}) collective-permute-start(bf16[2,192,512]{2,1,0:T(8,128)(2,1)S(1)} %get-tuple-element.47), channel_id=1, source_target_pairs={{0,1},{1,0},{2,3},{3,2},{4,5},{5,4},{6,7},{7,6},{8,9},{9,8},{10,11... | collective-permute-start | bytes 1179656 | tf_op jit(solution)/shard_map/ppermute | solution.py:297
  37.7 4.4 %collective-permute-start.24 = (bf16[2,192,512]{2,1,0:T(8,128)(2,1)S(1)}, bf16[2,192,512]{2,1,0:T(8,128)(2,1)S(1)}, u32[]{:S(2)}, u32[]{:S(2)}) collective-permute-start(bf16[2,192,512]{2,1,0:T(8,128)(2,1)S(1)} %get-tuple-element.50), channel_id=1, source_target_pairs={{0,1},{1,0},{2,3},{3,2},{4,5},{5,4},{6,7},{7,6},{8,9},{9,8},{10,11... | collective-permute-start | bytes 1179656 | tf_op jit(solution)/shard_map/ppermute | solution.py:297
  37.7 2.4 %collective-permute-start.19 = (bf16[192,512]{1,0:T(8,128)(2,1)S(1)}, bf16[192,512]{1,0:T(8,128)(2,1)S(1)}, u32[]{:S(2)}, u32[]{:S(2)}) collective-permute-start(bf16[192,512]{1,0:T(8,128)(2,1)S(1)} %after.8.q_ref), channel_id=1, source_target_pairs={{0,1},{1,0},{2,3},{3,2},{4,5},{5,4},{6,7},{7,6},{8,9},{9,8},{10,11... | collective-permute-start | bytes 589832 | tf_op jit(solution)/shard_map/ppermute | solution.py:297
  38.5 6.9 %collective-permute-start.27 = (bf16[192,512]{1,0:T(8,128)(2,1)S(1)}, bf16[192,512]{1,0:T(8,128)(2,1)S(1)}, u32[]{:S(2)}, u32[]{:S(2)}) collective-permute-start(bf16[192,512]{1,0:T(8,128)(2,1)S(1)} %fusion.9.refs_1_), channel_id=1, source_target_pairs={{0,2},{2,0},{4,6},{6,4},{8,10},{10,8},{12,14},{14,12},{1,3},{3,1},... | collective-permute-start | bytes 589832 | tf_op jit(solution)/shard_map/ppermute | solution.py:302
  42.0 1.8 %collective-permute-start.21 = (bf16[2,192,512]{2,1,0:T(8,128)(2,1)S(1)}, bf16[2,192,512]{2,1,0:T(8,128)(2,1)S(1)}, u32[]{:S(2)}, u32[]{:S(2)}) collective-permute-start(bf16[2,192,512]{2,1,0:T(8,128)(2,1)S(1)} %get-tuple-element.49), channel_id=1, source_target_pairs={{0,1},{1,0},{2,3},{3,2},{4,5},{5,4},{6,7},{7,6},{8,9},{9,8},{10,11... | collective-permute-start | bytes 1179656 | tf_op jit(solution)/shard_map/ppermute | solution.py:297
  43.9 7.8 %collective-permute-start.22 = (bf16[192,512]{1,0:T(8,128)(2,1)S(1)}, bf16[192,512]{1,0:T(8,128)(2,1)S(1)}, u32[]{:S(2)}, u32[]{:S(2)}) collective-permute-start(bf16[192,512]{1,0:T(8,128)(2,1)S(1)} %fusion.10.refs_1_), channel_id=1, source_target_pairs={{0,2},{2,0},{4,6},{6,4},{8,10},{10,8},{12,14},{14,12},{1,3},{3,1},... | collective-permute-start | bytes 589832 | tf_op jit(solution)/shard_map/ppermute | solution.py:302
  45.5 17.3 %collective-permute-start.28 = (bf16[192,512]{1,0:T(8,128)(2,1)S(1)}, bf16[192,512]{1,0:T(8,128)(2,1)S(1)}, u32[]{:S(2)}, u32[]{:S(2)}) collective-permute-start(bf16[192,512]{1,0:T(8,128)(2,1)S(1)} %fusion.1), channel_id=1, source_target_pairs={{0,8},{2,10},{4,12},{6,14},{8,0},{10,2},{12,4},{14,6},{1,9},{3,11}... | collective-permute-start | bytes 589832 | tf_op jit(solution)/shard_map/ppermute | solution.py:307
  48.0 7.4 %collective-permute-start.25 = (bf16[192,512]{1,0:T(8,128)(2,1)S(1)}, bf16[192,512]{1,0:T(8,128)(2,1)S(1)}, u32[]{:S(2)}, u32[]{:S(2)}) collective-permute-start(bf16[192,512]{1,0:T(8,128)(2,1)S(1)} %after.11), channel_id=1, source_target_pairs={{0,2},{2,0},{4,6},{6,4},{8,10},{10,8},{12,14},{14,12},{1,3},{3,1},... | collective-permute-start | bytes 589832 | tf_op jit(solution)/shard_map/ppermute | solution.py:302
  51.8 13.6 %collective-permute-start.29 = (bf16[192,512]{1,0:T(8,128)(2,1)S(1)}, bf16[192,512]{1,0:T(8,128)(2,1)S(1)}, u32[]{:S(2)}, u32[]{:S(2)}) collective-permute-start(bf16[192,512]{1,0:T(8,128)(2,1)S(1)} %fusion.5.refs_1_), channel_id=1, source_target_pairs={{0,12},{2,14},{4,8},{6,10},{8,4},{10,6},{12,0},{14,2},{1,13},{3,15... | collective-permute-start | bytes 589832 | tf_op jit(solution)/shard_map/ppermute | solution.py:307
  54.3 5.7 %collective-permute-start.23 = (bf16[192,512]{1,0:T(8,128)(2,1)S(1)}, bf16[192,512]{1,0:T(8,128)(2,1)S(1)}, u32[]{:S(2)}, u32[]{:S(2)}) collective-permute-start(bf16[192,512]{1,0:T(8,128)(2,1)S(1)} %after.10), channel_id=1, source_target_pairs={{0,2},{2,0},{4,6},{6,4},{8,10},{10,8},{12,14},{14,12},{1,3},{3,1},... | collective-permute-start | bytes 589832 | tf_op jit(solution)/shard_map/ppermute | solution.py:302
  55.4 10.0 %collective-permute-start.26 = (bf16[192,512]{1,0:T(8,128)(2,1)S(1)}, bf16[192,512]{1,0:T(8,128)(2,1)S(1)}, u32[]{:S(2)}, u32[]{:S(2)}) collective-permute-start(bf16[192,512]{1,0:T(8,128)(2,1)S(1)} %fusion.3), channel_id=1, source_target_pairs={{0,4},{2,6},{4,0},{6,2},{8,12},{10,14},{12,8},{14,10},{1,5},{3,7},... | collective-permute-start | bytes 589832 | tf_op jit(solution)/shard_map/ppermute | solution.py:307
  66.3 1.4 %collective-permute-start.30 = (bf16[128,512]{1,0:T(8,128)(2,1)S(1)}, bf16[128,512]{1,0:T(8,128)(2,1)S(1)}, u32[]{:S(2)}, u32[]{:S(2)}) collective-permute-start(bf16[128,512]{1,0:T(8,128)(2,1)S(1)} %get-tuple-element.52), channel_id=1, source_target_pairs={{0,1},{1,0},{2,3},{3,2},{4,5},{5,4},{6,7},{7,6},{8,9},{9,8},{10,11... | collective-permute-start | bytes 393224 | tf_op jit(solution)/shard_map/ppermute | solution.py:297

commit v17 on v15

--- a/solution.py
+++ b/solution.py
@@ -203,7 +203,7 @@
 
 
 def select_kernel(core_ref, line_ref, routes_ref, own_ref, other_ref, *rest):
-    pieces, block_ref = rest[:-1], rest[-1]
+    pieces, (slots_ref, block_ref) = rest[:-2], rest[-2:]
     experts_count = len(pieces)
     full_len = own_ref.shape[0]
     capacity = pieces[0].shape[0]
@@ -211,6 +211,7 @@
     block_ref[part_of(core, full_len)] = own_ref[...]
     block_ref[part_of(1 - core, full_len)] = other_ref[...]
     named, earlier = slots_of(routes_ref, experts_count)
+    slots_ref[...] = earlier
     slot = jnp.where(named, earlier, -1.0)
     ids = lax.broadcasted_iota(jnp.int32, slot.shape, 0)
     numbers = lax.broadcasted_iota(jnp.int32, (capacity, slot.shape[1]), 0).astype(jnp.float32)
@@ -249,48 +250,56 @@
         copy.wait()
 
 
-def combine_kernel(core_ref, line_ref, routes_ref, own_gates_ref, other_gates_ref, *rest):
-    pieces, (own_ref, other_ref, rows_ref, gates_ref, sum_ref) = rest[:-5], rest[-5:]
-    experts_count = len(pieces)
-    capacity, half = pieces[0].shape
-    sents, _, full_len = routes_ref.shape
-    core = core_ref[0]
+def gated_sum(sent, line, routes, gates, slots_ref, rows):
+    full_len = routes.shape[1]
+    experts_count = slots_ref.shape[0]
+    parts = [slots_ref[:, at : at + full_len] for at in range(0, slots_ref.shape[1], full_len)]
+    slots = jnp.where(sent == 0, parts[0], parts[1])
+    ids = lax.broadcasted_iota(jnp.int32, (experts_count, full_len), 0)
+    numbers = lax.broadcasted_iota(jnp.int32, (full_len, rows.shape[0]), 1).astype(jnp.float32)
+    capacity = rows.shape[0] // (lax.axis_size("expert") // 2)
+    total = None
+    for k in range(2):
+        route = routes[k : k + 1]
+        slot = jnp.sum(jnp.where(ids == route, slots, 0.0), axis=0, keepdims=True)
+        place = (route ^ line).astype(jnp.float32) * capacity + slot
+        place, gate = (
+            jnp.broadcast_to(row, (full_len, full_len)).T[:, :1]
+            for row in (place, gates[k : k + 1])
+        )
+        picks = jnp.where(numbers == place, 1.0, 0.0).astype(jnp.bfloat16)
+        term = gate * jnp.dot(picks, rows, preferred_element_type=jnp.float32)
+        total = term if total is None else total + term
+    return total
+
+
+def combine_other_kernel(core_ref, line_ref, routes_ref, gates_ref, slots_ref, *rest):
+    pieces, (other_ref, rows_ref) = rest[:-2], rest[-2:]
+    capacity = pieces[0].shape[0]
     for offset, piece_ref in enumerate(pieces):
         rows_ref[offset * capacity : (offset + 1) * capacity] = piece_ref[...]
-    gates_ref[core] = own_gates_ref[...]
-    gates_ref[1 - core] = other_gates_ref[...]
-    _, earlier = slots_of(routes_ref, experts_count)
-    ids = lax.broadcasted_iota(jnp.int32, (earlier.shape[0], full_len), 0)
-    numbers = lax.broadcasted_iota(
-        jnp.int32, (full_len, experts_count * capacity), 1
-    ).astype(jnp.float32)
-    for sent in range(sents):
-        slots = earlier[:, sent * full_len : (sent + 1) * full_len]
-        total = None
-        for k in range(2):
-            route = routes_ref[sent, k : k + 1]
-            slot = jnp.sum(jnp.where(ids == route, slots, 0.0), axis=0, keepdims=True)
-            place = (route ^ line_ref[0]).astype(jnp.float32) * capacity + slot
-            place, gate = (
-                jnp.broadcast_to(row, (full_len, full_len)).T[:, :1]
-                for row in (place, gates_ref[sent, k : k + 1])
-            )
-            picks = jnp.where(numbers == place, 1.0, 0.0).astype(jnp.bfloat16)
-            term = gate * jnp.dot(picks, rows_ref[...], preferred_element_type=jnp.float32)
-            total = term if total is None else total + term
-        sum_ref[sent] = total
-    own_ref[...] = sum_ref[core]
-    other_ref[...] = sum_ref[1 - core].astype(jnp.bfloat16)
+    sent = 1 - core_ref[0]
+    other_ref[...] = gated_sum(
+        sent, line_ref[0], routes_ref[sent], gates_ref[...], slots_ref, rows_ref[...]
+    ).astype(jnp.bfloat16)
+
+
+def combine_own_kernel(
+    core_ref, line_ref, routes_ref, gates_ref, slots_ref, rows_ref, state_ref, own_ref
+):
+    core = core_ref[0]
+    summed = gated_sum(
+        core, line_ref[0], routes_ref[core], gates_ref[...], slots_ref, rows_ref[...]
+    )
+    own_ref[...] = add_rounded(state_ref[:, part_of(core, own_ref.shape[1])], summed)
 
 
 def finish_kernel(core_ref, state_ref, own_ref, other_ref, mixed_ref):
     core = core_ref[0]
     half = own_ref.shape[-1]
-    for part, summed in ((core, own_ref), (1 - core, other_ref)):
-        span = part_of(part, half)
-        mixed_ref[:, span] = (
-            state_ref[:, span].astype(jnp.float32) + summed[...].astype(jnp.float32)
-        ).astype(jnp.bfloat16)
+    mixed_ref[:, part_of(core, half)] = own_ref[...]
+    span = part_of(1 - core, half)
+    mixed_ref[:, span] = add_rounded(state_ref[:, span], other_ref[...].astype(jnp.float32))
 
 
 def swap(values):
@@ -378,10 +387,10 @@
     other = swap(send)
     other_gates = swap(gates)
     piece = ((capacity, half), jnp.bfloat16)
-    selected = call(
+    *selected, slots = call(
         select_kernel,
         "select",
-        [piece] * count,
+        [piece] * count + [((max(8, count), 2 * full_len), jnp.float32)],
         [core, line],
         [routes, keep, other],
         scratch=[pltpu.VMEM((2 * full_len, half), jnp.bfloat16)],
@@ -395,23 +404,8 @@
         [fc_in, fc_out],
         scratch=[pltpu.SemaphoreType.DMA((2,))],
     )
-    travelling = [exchange(selected[r], r) for r in range(1, count)]
-    home = [None] * count
-    ps, qs, kept, halves, wholes, boths = {}, {}, {}, {}, {}, {}
-    for offset in [0, 1, 2, 3]:
-        p = travelling[offset - 1] if offset else selected[0]
-        if offset == 1:
-            p = after(p, near_in)
-        q = swap_owner(p)
-        ps[offset], qs[offset] = p, q
-    for offset in [0, 1, 2, 3]:
-        p, q = ps[offset], qs[offset]
-        p2, q2 = swap(p), swap(q)
-        if offset == 2:
-            q2 = after(q2, kept[0], kept[1])
-        if offset == 3:
-            q2 = after(q2, halves[2])
-        kept[offset], sent = call(
+    def run(p, q, p2, q2):
+        keep, sent = call(
             expert_kernel,
             "expert",
             [((2, capacity, half), jnp.float32), ((2, capacity, half), jnp.bfloat16)],
@@ -420,37 +414,89 @@
             scratch=[pltpu.VMEM((2 * capacity, width), jnp.bfloat16)],
             vmem_mib=16,
         )
-        moving = swap(sent)
-        both = kept[offset] + moving.astype(jnp.float32)
-        halves[offset] = both[1].astype(jnp.bfloat16)
-        boths[offset] = both
-    for offset in [2, 3, 1, 0]:
-        both, leaving = boths[offset], halves[offset]
-        if offset == 1:
-            leaving = after(leaving, halves[3])
-        if offset == 0:
-            leaving = after(leaving, wholes[3])
-        across = swap_owner(leaving)
-        wholes[offset] = (both[0] + across.astype(jnp.float32)).astype(jnp.bfloat16)
-        home[offset] = exchange(wholes[offset], offset) if offset else wholes[offset]
-    own_sum, other_sum = call(
-        combine_kernel,
-        "combine",
-        [((full_len, half), jnp.float32), ((full_len, half), jnp.bfloat16)],
+        return keep, swap(sent)
+
+    def sums(keep, moving):
+        both = keep + moving.astype(jnp.float32)
+        return both, both[1].astype(jnp.bfloat16)
+
+    def whole(both, across):
+        return (both[0] + across.astype(jnp.float32)).astype(jnp.bfloat16)
+
+    travelling = [exchange(selected[r], r) for r in range(1, count)]
+    home = [None] * count
+    ps, qs, kept, halves, wholes, boths = {}, {}, {}, {}, {}, {}
+    p = selected[0]
+    q = swap_owner(p)
+    ps[0], qs[0] = p, q
+    p = travelling[0]
+    p = after(p, near_in)
+    q = swap_owner(p)
+    ps[1], qs[1] = p, q
+    p = travelling[1]
+    q = swap_owner(p)
+    ps[2], qs[2] = p, q
+    p = travelling[2]
+    q = swap_owner(p)
+    ps[3], qs[3] = p, q
+    p, q = ps[0], qs[0]
+    p2, q2 = swap(p), swap(q)
+    kept[0], moving = run(p, q, p2, q2)
+    boths[0], halves[0] = sums(kept[0], moving)
+    p, q = ps[2], qs[2]
+    p2, q2 = swap(p), swap(q)
+    kept[2], moving = run(p, q, p2, q2)
+    boths[2], halves[2] = sums(kept[2], moving)
+    p, q = ps[1], qs[1]
+    p2, q2 = swap(p), swap(q)
+    q2 = after(q2, kept[0], kept[2])
+    kept[1], moving = run(p, q, p2, q2)
+    boths[1], halves[1] = sums(kept[1], moving)
+    p, q = ps[3], qs[3]
+    q = after(q, kept[2])
+    p2, q2 = swap(p), swap(q)
+    q2 = after(q2, halves[2], kept[1])
+    kept[3], moving = run(p, q, p2, q2)
+    boths[3], halves[3] = sums(kept[3], moving)
+    leaving = halves[2]
+    across = swap_owner(leaving)
+    wholes[2] = whole(boths[2], across)
+    home[2] = exchange(wholes[2], 2)
+    leaving = halves[3]
+    across = swap_owner(leaving)
+    wholes[3] = whole(boths[3], across)
+    home[3] = exchange(wholes[3], 3)
+    leaving = halves[1]
+    leaving = after(leaving, halves[3])
+    across = swap_owner(leaving)
+    wholes[1] = whole(boths[1], across)
+    home[1] = exchange(wholes[1], 1)
+    leaving = halves[0]
+    leaving = after(leaving, wholes[3])
+    across = swap_owner(leaving)
+    wholes[0] = whole(boths[0], across)
+    home[0] = wholes[0]
+    leaving, rows = call(
+        combine_other_kernel,
+        "combine_other",
+        [((full_len, half), jnp.bfloat16), ((count * capacity, half), jnp.bfloat16)],
         [core, line],
-        [routes, gates, other_gates, *home],
-        scratch=[
-            pltpu.VMEM((count * capacity, half), jnp.bfloat16),
-            pltpu.VMEM((2, 2, full_len), jnp.float32),
-            pltpu.VMEM((2, full_len, half), jnp.float32),
-        ],
+        [routes, other_gates, slots, *home],
+    )
+    arriving = swap(leaving)
+    (own,) = call(
+        combine_own_kernel,
+        "combine_own",
+        [((full_len, half), jnp.bfloat16)],
+        [core, line],
+        [routes, gates, slots, rows, state],
     )
     (mixed,) = call(
         finish_kernel,
         "finish",
         [((full_len, width), jnp.bfloat16)],
         [core],
-        [state, own_sum, swap(other_sum)],
+        [state, own, arriving],
     )
     return mixed
 

time: 70.2 us -> 68.9 us (0.981)
  starting transfers between devices: 30.5 us -> 29.6 us
    ppermute x8, waiting for transfers between devices: 7.16 us -> 10.8 us  [swap_owner(): return lax.ppermute(values, 'expert', [(i, i ^ 1) for i in range(owners)])]
    ppermute x6, waiting for transfers between devices: 11.1 us -> 8.22 us  [exchange(): lax.ppermute(values, 'expert', [(i, i ^ 2 * offset) for i in range(owners)])]
    ppermute x8, starting transfers between devices: 10.9 us -> 9.14 us  [swap_owner(): return lax.ppermute(values, 'expert', [(i, i ^ 1) for i in range(owners)])]
    ppermute x17, waiting for transfers between devices: 4.95 us -> 3.6 us  [swap(): return lax.ppermute(values, 'section', [(0, 1), (1, 0)])]
    ppermute x6, starting transfers between devices: 16 us -> 16.8 us  [exchange(): lax.ppermute(values, 'expert', [(i, i ^ 2 * offset) for i in range(owners)])]
    pallas_call x10 -> x11, Pallas kernels: 14.8 us -> 14.9 us  [call(): pl.pallas_call(kernel, out_shape=tuple((jax.ShapeDtypeStruct(*out) for ou...]
  transfers between devices with their start and end apart: 31 -> 31, of which waited for: 15 -> 14; matrix products, arithmetic and copies ran while one was open for 1% -> 1% of each run, Pallas kernels for 16% -> 17%
where the time goes in v17:
time: 68.9 us; the launch traced here: 68.7 us
  starting transfers between devices  29.6 us (43%)
  waiting for transfers between devices  22.7 us (33%)
  Pallas kernels  14.9 us (22%)
  between operations  0.89 us (1%)
    ppermute x6, starting transfers between devices, exchange(): lax.ppermute(values, 'expert', [(i, i ^ 2 * offset) for i in range(owners)])  16.8 us
    pallas_call x11, Pallas kernels, call(): pl.pallas_call(kernel, out_shape=tuple((jax.ShapeDtypeStruct(*out) for ou...  14.9 us
    ppermute x8, waiting for transfers between devices, swap_owner(): return lax.ppermute(values, 'expert', [(i, i ^ 1) for i in range(owners)])  10.8 us
    ppermute x8, starting transfers between devices, swap_owner(): return lax.ppermute(values, 'expert', [(i, i ^ 1) for i in range(owners)])  9.14 us
    ppermute x6, waiting for transfers between devices, exchange(): lax.ppermute(values, 'expert', [(i, i ^ 2 * offset) for i in range(owners)])  8.22 us
    ppermute x17, starting transfers between devices, swap(): return lax.ppermute(values, 'section', [(0, 1), (1, 0)])  3.6 us
    ppermute x17, waiting for transfers between devices, swap(): return lax.ppermute(values, 'section', [(0, 1), (1, 0)])  3.6 us
  transfers between devices with their start and end apart: 31, of which 14 were waited for; matrix products, arithmetic and copies ran while one was open for 1% of the time, Pallas kernels for 17%

profile of v17, /device:TPU:0, one launch (start us, length us, event | category | flops | bytes accessed | tf_op | source)
XLA Modules:
  0.0 68.7 jit_solution(6883893479593719053)
XLA Ops:
  0.0 0.5 collective-permute-start
  0.5 0.1 collective-permute-start.1
  1.2 1.8 %attend_own.1 = (bf16[128,512]{1,0:T(8,128)(2,1)S(1)}, bf16[128,512]{1,0:T(8,128)(2,1)S(1)}, bf16[128,512]{1,0:T(8,128)(2,1)S(1)}) custom-call(s32[1]{0:T(128)} %bitcast.core_ref, s32[1]{0:T(128)S(6)} %copy.24.source_ref, bf16[1,128,1024]{2,1,0:T(8,128)(2,1)} %x_in.1, f32[1,1024]{1,0:T(1,128)} %bitcast.40, bf16[2,80,512]{2,1,0:T(8,128)(2,1)} %keys_in.1, ...), custom_call_target="tpu_custom_call" | custom-call | tf_op jit(solution)/shard_map/attend_own/pallas_call | solution.py:25
  3.0 1.2 %attend_other.1 = (bf16[128,1024]{1,0:T(8,128)(2,1)S(1)}, bf16[128,512]{1,0:T(8,128)(2,1)S(1)}, bf16[128,512]{1,0:T(8,128)(2,1)S(1)}, f32[2,128]{1,0:T(2,128)S(1)}, s32[2,2,128]{2,1,0:T(2,128)S(1)}) custom-call(s32[1]{0:T(128)} %bitcast.core_ref, s32[1]{0:T(128)S(6)} %copy.24.source_ref, bf16[128,512]{1,0:T(8,128)(2,1)S(1)} %get-tuple-element.30.own_ref, ...), custom_call_target="tpu_custom_call" | custom-call | tf_op jit(solution)/shard_map/attend_other/pallas_call | solution.py:25
  4.2 0.5 collective-permute-start.2
  4.7 1.0 %collective-permute-done.2.other_ref = bf16[128,512]{1,0:T(8,128)(2,1)S(1)} collective-permute-done((bf16[128,512]{1,0:T(8,128)(2,1)S(1)}, bf16[128,512]{1,0:T(8,128)(2,1)S(1)}, u32[]{:S(2)}, u32[]{:S(2)}) %collective-permute-start.2) | collective-permute-done | bytes 131104 | tf_op jit(solution)/shard_map/ppermute | solution.py:306
  5.7 0.5 select.5
  6.2 2.9 %collective-permute-start.4 = (bf16[192,512]{1,0:T(8,128)(2,1)S(1)}, bf16[192,512]{1,0:T(8,128)(2,1)S(1)}, u32[]{:S(2)}, u32[]{:S(2)}) collective-permute-start(bf16[192,512]{1,0:T(8,128)(2,1)S(1)} %get-tuple-element.39.p_ref), channel_id=1, source_target_pairs={{0,2},{2,0},{4,6},{6,4},{8,10},{10,8},{12,14},{14,12},{1,3},{3,1},... | collective-permute-start | bytes 589832 | tf_op jit(solution)/shard_map/ppermute | solution.py:311
  9.2 2.6 %collective-permute-start.10 = (bf16[192,512]{1,0:T(8,128)(2,1)S(1)}, bf16[192,512]{1,0:T(8,128)(2,1)S(1)}, u32[]{:S(2)}, u32[]{:S(2)}) collective-permute-start(bf16[192,512]{1,0:T(8,128)(2,1)S(1)} %get-tuple-element.45), channel_id=1, source_target_pairs={{0,8},{2,10},{4,12},{6,14},{8,0},{10,2},{12,4},{14,6},{1,9},{3,11}... | collective-permute-start | bytes 589832 | tf_op jit(solution)/shard_map/ppermute | solution.py:316
  11.7 1.6 %collective-permute-start.17 = (bf16[192,512]{1,0:T(8,128)(2,1)S(1)}, bf16[192,512]{1,0:T(8,128)(2,1)S(1)}, u32[]{:S(2)}, u32[]{:S(2)}) collective-permute-start(bf16[192,512]{1,0:T(8,128)(2,1)S(1)} %get-tuple-element.48), channel_id=1, source_target_pairs={{0,4},{2,6},{4,0},{6,2},{8,12},{10,14},{12,8},{14,10},{1,5},{3,7},... | collective-permute-start | bytes 589832 | tf_op jit(solution)/shard_map/ppermute | solution.py:316
  13.3 1.1 %collective-permute-done.4.q_ref = bf16[192,512]{1,0:T(8,128)(2,1)S(1)} collective-permute-done((bf16[192,512]{1,0:T(8,128)(2,1)S(1)}, bf16[192,512]{1,0:T(8,128)(2,1)S(1)}, u32[]{:S(2)}, u32[]{:S(2)}) %collective-permute-start.4) | collective-permute-done | bytes 196640 | tf_op jit(solution)/shard_map/ppermute | solution.py:311
  14.4 0.0 collective-permute-start.6
  14.4 2.2 %load.1 = (bf16[1024,1024]{1,0:T(8,128)(2,1)S(1)}, bf16[1024,1024]{1,0:T(8,128)(2,1)S(1)}) custom-call(bf16[1024,1024]{1,0:T(8,128)(2,1)} %in_in.1, bf16[1024,1024]{1,0:T(8,128)(2,1)} %out_in.1), custom_call_target="tpu_custom_call" | custom-call | tf_op jit(solution)/shard_map/load/pallas_call | solution.py:25
  16.6 4.4 %collective-permute-done.10.p_ref = bf16[192,512]{1,0:T(8,128)(2,1)S(1)} collective-permute-done((bf16[192,512]{1,0:T(8,128)(2,1)S(1)}, bf16[192,512]{1,0:T(8,128)(2,1)S(1)}, u32[]{:S(2)}, u32[]{:S(2)}) %collective-permute-start.10) | collective-permute-done | bytes 196640 | tf_op jit(solution)/shard_map/ppermute | solution.py:316
  21.1 0.5 collective-permute-start.11
  21.5 1.6 %collective-permute-start.18 = (bf16[192,512]{1,0:T(8,128)(2,1)S(1)}, bf16[192,512]{1,0:T(8,128)(2,1)S(1)}, u32[]{:S(2)}, u32[]{:S(2)}) collective-permute-start(bf16[192,512]{1,0:T(8,128)(2,1)S(1)} %after.7.p_ref), channel_id=1, source_target_pairs={{0,2},{2,0},{4,6},{6,4},{8,10},{10,8},{12,14},{14,12},{1,3},{3,1},... | collective-permute-start | bytes 589832 | tf_op jit(solution)/shard_map/ppermute | solution.py:311
  23.1 3.4 %collective-permute-start.8 = (bf16[192,512]{1,0:T(8,128)(2,1)S(1)}, bf16[192,512]{1,0:T(8,128)(2,1)S(1)}, u32[]{:S(2)}, u32[]{:S(2)}) collective-permute-start(bf16[192,512]{1,0:T(8,128)(2,1)S(1)} %get-tuple-element.44), channel_id=1, source_target_pairs={{0,12},{2,14},{4,8},{6,10},{8,4},{10,6},{12,0},{14,2},{1,13},{3,15... | collective-permute-start | bytes 589832 | tf_op jit(solution)/shard_map/ppermute | solution.py:316
  26.5 1.8 %expert.4 = (f32[2,192,512]{2,1,0:T(8,128)S(1)}, bf16[2,192,512]{2,1,0:T(8,128)(2,1)S(1)}) custom-call(s32[1]{0:T(128)} %bitcast.core_ref, bf16[192,512]{1,0:T(8,128)(2,1)S(1)} %get-tuple-element.39.p_ref, bf16[192,512]{1,0:T(8,128)(2,1)S(1)} %collective-permute-done.4.q_ref, bf16[192,512]{1,0:T(8,128)(2,1)S(1)} %collective-permute-done.5.p2_ref, ...), custom_call_target="tpu_custom_call" | custom-call | tf_op jit(solution)/shard_map/expert/pallas_call | solution.py:25
  28.3 0.6 collective-permute-start.7
  28.9 0.0 collective-permute-done.11.q_ref
  28.9 0.1 collective-permute-start.13
  29.0 2.0 %collective-permute-done.18.q_ref = bf16[192,512]{1,0:T(8,128)(2,1)S(1)} collective-permute-done((bf16[192,512]{1,0:T(8,128)(2,1)S(1)}, bf16[192,512]{1,0:T(8,128)(2,1)S(1)}, u32[]{:S(2)}, u32[]{:S(2)}) %collective-permute-start.18) | collective-permute-done | bytes 196640 | tf_op jit(solution)/shard_map/ppermute | solution.py:311
  31.0 0.1 collective-permute-done.8.p_ref
  31.1 0.5 collective-permute-start.19
  31.5 0.8 %collective-permute-start.9 = (bf16[192,512]{1,0:T(8,128)(2,1)S(1)}, bf16[192,512]{1,0:T(8,128)(2,1)S(1)}, u32[]{:S(2)}, u32[]{:S(2)}) collective-permute-start(bf16[192,512]{1,0:T(8,128)(2,1)S(1)} %collective-permute-done.8.p_ref), channel_id=1, source_target_pairs={{0,2},{2,0},{4,6},{6,4},{8,10},{10,8},{12,14},{14,12},{1,3},{3,1},... | collective-permute-start | bytes 589832 | tf_op jit(solution)/shard_map/ppermute | solution.py:311
  32.3 0.0 collective-permute-done.13.q2_ref
  32.3 0.0 collective-permute-start.3
  32.3 1.8 %expert.5 = (f32[2,192,512]{2,1,0:T(8,128)S(1)}, bf16[2,192,512]{2,1,0:T(8,128)(2,1)S(1)}) custom-call(s32[1]{0:T(128)} %bitcast.core_ref, bf16[192,512]{1,0:T(8,128)(2,1)S(1)} %collective-permute-done.10.p_ref, bf16[192,512]{1,0:T(8,128)(2,1)S(1)} %collective-permute-done.11.q_ref, bf16[192,512]{1,0:T(8,128)(2,1)S(1)} %collective-permute-done.12.p2_ref, ...), custom_call_target="tpu_custom_call" | custom-call | tf_op jit(solution)/shard_map/expert/pallas_call | solution.py:25
  34.2 0.0 collective-permute-done.20.refs_0_
  34.2 0.6 collective-permute-start.14
  34.8 0.0 collective-permute-done.19.p2_ref
  34.8 0.1 collective-permute-start.16
  34.9 1.8 %expert.6 = (f32[2,192,512]{2,1,0:T(8,128)S(1)}, bf16[2,192,512]{2,1,0:T(8,128)(2,1)S(1)}) custom-call(s32[1]{0:T(128)} %bitcast.core_ref, bf16[192,512]{1,0:T(8,128)(2,1)S(1)} %after.7.p_ref, bf16[192,512]{1,0:T(8,128)(2,1)S(1)} %collective-permute-done.18.q_ref, bf16[192,512]{1,0:T(8,128)(2,1)S(1)} %collective-permute-done.19.p2_ref, ...), custom_call_target="tpu_custom_call" | custom-call | tf_op jit(solution)/shard_map/expert/pallas_call | solution.py:25
  36.7 1.7 %collective-permute-done.9.refs_0_ = bf16[192,512]{1,0:T(8,128)(2,1)S(1)} collective-permute-done((bf16[192,512]{1,0:T(8,128)(2,1)S(1)}, bf16[192,512]{1,0:T(8,128)(2,1)S(1)}, u32[]{:S(2)}, u32[]{:S(2)}) %collective-permute-start.9) | collective-permute-done | bytes 196640 | tf_op jit(solution)/shard_map/ppermute | solution.py:311
  38.4 0.0 collective-permute-done.7
  38.4 0.5 collective-permute-start.15
  38.9 0.1 convert_add_fusion.3
  39.1 0.1 convert_add_fusion.2
  39.3 0.8 %collective-permute-start.27 = (bf16[192,512]{1,0:T(8,128)(2,1)S(1)}, bf16[192,512]{1,0:T(8,128)(2,1)S(1)}, u32[]{:S(2)}, u32[]{:S(2)}) collective-permute-start(bf16[192,512]{1,0:T(8,128)(2,1)S(1)} %fusion.9.refs_1_), channel_id=1, source_target_pairs={{0,2},{2,0},{4,6},{6,4},{8,10},{10,8},{12,14},{14,12},{1,3},{3,1},... | collective-permute-start | bytes 589832 | tf_op jit(solution)/shard_map/ppermute | solution.py:311
  40.1 0.3 collective-permute-done.15.refs_0_
  40.4 0.0 collective-permute-done.14.p2_ref
  40.4 1.8 %expert.7 = (f32[2,192,512]{2,1,0:T(8,128)S(1)}, bf16[2,192,512]{2,1,0:T(8,128)(2,1)S(1)}) custom-call(s32[1]{0:T(128)} %bitcast.core_ref, bf16[192,512]{1,0:T(8,128)(2,1)S(1)} %collective-permute-done.8.p_ref, bf16[192,512]{1,0:T(8,128)(2,1)S(1)} %after.6.q_ref, bf16[192,512]{1,0:T(8,128)(2,1)S(1)} %collective-permute-done.14.p2_ref, ...), custom_call_target="tpu_custom_call" | custom-call | tf_op jit(solution)/shard_map/expert/pallas_call | solution.py:25
  42.3 0.2 collective-permute-start.21
  42.5 0.1 convert_add_fusion
  42.6 1.4 %collective-permute-done.21 = bf16[2,192,512]{2,1,0:T(8,128)(2,1)S(1)} collective-permute-done((bf16[2,192,512]{2,1,0:T(8,128)(2,1)S(1)}, bf16[2,192,512]{2,1,0:T(8,128)(2,1)S(1)}, u32[]{:S(2)}, u32[]{:S(2)}) %collective-permute-start.21) | collective-permute-done | bytes 393248 | tf_op jit(solution)/shard_map/ppermute | solution.py:306
  44.1 0.1 convert_add_fusion.1
  44.2 1.0 %collective-permute-start.22 = (bf16[192,512]{1,0:T(8,128)(2,1)S(1)}, bf16[192,512]{1,0:T(8,128)(2,1)S(1)}, u32[]{:S(2)}, u32[]{:S(2)}) collective-permute-start(bf16[192,512]{1,0:T(8,128)(2,1)S(1)} %fusion.10.refs_1_), channel_id=1, source_target_pairs={{0,2},{2,0},{4,6},{6,4},{8,10},{10,8},{12,14},{14,12},{1,3},{3,1},... | collective-permute-start | bytes 589832 | tf_op jit(solution)/shard_map/ppermute | solution.py:311
  45.2 1.0 %collective-permute-done.27 = bf16[192,512]{1,0:T(8,128)(2,1)S(1)} collective-permute-done((bf16[192,512]{1,0:T(8,128)(2,1)S(1)}, bf16[192,512]{1,0:T(8,128)(2,1)S(1)}, u32[]{:S(2)}, u32[]{:S(2)}) %collective-permute-start.27) | collective-permute-done | bytes 196640 | tf_op jit(solution)/shard_map/ppermute | solution.py:311
  46.2 2.8 %collective-permute-start.28 = (bf16[192,512]{1,0:T(8,128)(2,1)S(1)}, bf16[192,512]{1,0:T(8,128)(2,1)S(1)}, u32[]{:S(2)}, u32[]{:S(2)}) collective-permute-start(bf16[192,512]{1,0:T(8,128)(2,1)S(1)} %fusion.1), channel_id=1, source_target_pairs={{0,8},{2,10},{4,12},{6,14},{8,0},{10,2},{12,4},{14,6},{1,9},{3,11}... | collective-permute-start | bytes 589832 | tf_op jit(solution)/shard_map/ppermute | solution.py:316
  49.0 0.6 collective-permute-start.25
  49.7 2.2 %collective-permute-done.22 = bf16[192,512]{1,0:T(8,128)(2,1)S(1)} collective-permute-done((bf16[192,512]{1,0:T(8,128)(2,1)S(1)}, bf16[192,512]{1,0:T(8,128)(2,1)S(1)}, u32[]{:S(2)}, u32[]{:S(2)}) %collective-permute-start.22) | collective-permute-done | bytes 196640 | tf_op jit(solution)/shard_map/ppermute | solution.py:311
  51.8 0.1 fusion.5.refs_1_
  51.9 4.7 %collective-permute-start.29 = (bf16[192,512]{1,0:T(8,128)(2,1)S(1)}, bf16[192,512]{1,0:T(8,128)(2,1)S(1)}, u32[]{:S(2)}, u32[]{:S(2)}) collective-permute-start(bf16[192,512]{1,0:T(8,128)(2,1)S(1)} %fusion.5.refs_1_), channel_id=1, source_target_pairs={{0,12},{2,14},{4,8},{6,10},{8,4},{10,6},{12,0},{14,2},{1,13},{3,15... | collective-permute-start | bytes 589832 | tf_op jit(solution)/shard_map/ppermute | solution.py:316
  56.6 0.9 %collective-permute-start.23 = (bf16[192,512]{1,0:T(8,128)(2,1)S(1)}, bf16[192,512]{1,0:T(8,128)(2,1)S(1)}, u32[]{:S(2)}, u32[]{:S(2)}) collective-permute-start(bf16[192,512]{1,0:T(8,128)(2,1)S(1)} %after.10), channel_id=1, source_target_pairs={{0,2},{2,0},{4,6},{6,4},{8,10},{10,8},{12,14},{14,12},{1,3},{3,1},... | collective-permute-start | bytes 589832 | tf_op jit(solution)/shard_map/ppermute | solution.py:311
  57.6 1.8 %collective-permute-start.26 = (bf16[192,512]{1,0:T(8,128)(2,1)S(1)}, bf16[192,512]{1,0:T(8,128)(2,1)S(1)}, u32[]{:S(2)}, u32[]{:S(2)}) collective-permute-start(bf16[192,512]{1,0:T(8,128)(2,1)S(1)} %fusion.3), channel_id=1, source_target_pairs={{0,4},{2,6},{4,0},{6,2},{8,12},{10,14},{12,8},{14,10},{1,5},{3,7},... | collective-permute-start | bytes 589832 | tf_op jit(solution)/shard_map/ppermute | solution.py:316
  59.4 2.9 %collective-permute-done.23 = bf16[192,512]{1,0:T(8,128)(2,1)S(1)} collective-permute-done((bf16[192,512]{1,0:T(8,128)(2,1)S(1)}, bf16[192,512]{1,0:T(8,128)(2,1)S(1)}, u32[]{:S(2)}, u32[]{:S(2)}) %collective-permute-start.23) | collective-permute-done | bytes 196640 | tf_op jit(solution)/shard_map/ppermute | solution.py:311
  62.3 0.1 fusion.7.rest_0_
  62.3 1.1 %collective-permute-done.28.rest_2_ = bf16[192,512]{1,0:T(8,128)(2,1)S(1)} collective-permute-done((bf16[192,512]{1,0:T(8,128)(2,1)S(1)}, bf16[192,512]{1,0:T(8,128)(2,1)S(1)}, u32[]{:S(2)}, u32[]{:S(2)}) %collective-permute-start.28) | collective-permute-done | bytes 196640 | tf_op jit(solution)/shard_map/ppermute | solution.py:316
  63.5 2.6 %collective-permute-done.26.rest_1_ = bf16[192,512]{1,0:T(8,128)(2,1)S(1)} collective-permute-done((bf16[192,512]{1,0:T(8,128)(2,1)S(1)}, bf16[192,512]{1,0:T(8,128)(2,1)S(1)}, u32[]{:S(2)}, u32[]{:S(2)}) %collective-permute-start.26) | collective-permute-done | bytes 196640 | tf_op jit(solution)/shard_map/ppermute | solution.py:316
  66.1 0.5 combine_other.1
  66.6 0.1 collective-permute-start.30
  66.7 0.5 combine_own.1.own_ref
  67.2 0.8 %collective-permute-done.30.other_ref = bf16[128,512]{1,0:T(8,128)(2,1)S(1)} collective-permute-done((bf16[128,512]{1,0:T(8,128)(2,1)S(1)}, bf16[128,512]{1,0:T(8,128)(2,1)S(1)}, u32[]{:S(2)}, u32[]{:S(2)}) %collective-permute-start.30) | collective-permute-done | bytes 131104 | tf_op jit(solution)/shard_map/ppermute | solution.py:306
  68.0 0.7 %finish.1 = bf16[128,1024]{1,0:T(8,128)(2,1)} custom-call(s32[1]{0:T(128)} %bitcast.core_ref, bf16[128,1024]{1,0:T(8,128)(2,1)S(1)} %get-tuple-element.33.state_ref, bf16[128,512]{1,0:T(8,128)(2,1)S(1)} %combine_own.1.own_ref, bf16[128,512]{1,0:T(8,128)(2,1)S(1)} %collective-permute-done.30.other_ref), custom_call_target="tpu_custom_call" | custom-call | tf_op jit(solution)/shard_map/finish/pallas_call | solution.py:25
  (27 shorter events, 0.2 us)
Async XLA Ops:
  0.0 2.9 %collective-permute-start = (bf16[2,80,512]{2,1,0:T(8,128)(2,1)}, bf16[2,80,512]{2,1,0:T(8,128)(2,1)S(1)}, u32[]{:S(2)}, u32[]{:S(2)}) collective-permute-start(bf16[2,80,512]{2,1,0:T(8,128)(2,1)} %keys_in.1), channel_id=1, source_target_pairs={{0,1},{1,0},{2,3},{3,2},{4,5},{5,4},{6,7},{7,6},{8,9},{9,8},{10,11... | collective-permute-start | bytes 491528 | tf_op jit(solution)/shard_map/ppermute | solution.py:306
  0.5 2.5 %collective-permute-start.1 = (bf16[2,80,512]{2,1,0:T(8,128)(2,1)}, bf16[2,80,512]{2,1,0:T(8,128)(2,1)S(1)}, u32[]{:S(2)}, u32[]{:S(2)}) collective-permute-start(bf16[2,80,512]{2,1,0:T(8,128)(2,1)} %values_in.1), channel_id=1, source_target_pairs={{0,1},{1,0},{2,3},{3,2},{4,5},{5,4},{6,7},{7,6},{8,9},{9,8},{10,11... | collective-permute-start | bytes 491528 | tf_op jit(solution)/shard_map/ppermute | solution.py:306
  4.2 1.5 %collective-permute-start.2 = (bf16[128,512]{1,0:T(8,128)(2,1)S(1)}, bf16[128,512]{1,0:T(8,128)(2,1)S(1)}, u32[]{:S(2)}, u32[]{:S(2)}) collective-permute-start(bf16[128,512]{1,0:T(8,128)(2,1)S(1)} %get-tuple-element.37), channel_id=1, source_target_pairs={{0,1},{1,0},{2,3},{3,2},{4,5},{5,4},{6,7},{7,6},{8,9},{9,8},{10,11... | collective-permute-start | bytes 393224 | tf_op jit(solution)/shard_map/ppermute | solution.py:306
  6.2 8.1 %collective-permute-start.4 = (bf16[192,512]{1,0:T(8,128)(2,1)S(1)}, bf16[192,512]{1,0:T(8,128)(2,1)S(1)}, u32[]{:S(2)}, u32[]{:S(2)}) collective-permute-start(bf16[192,512]{1,0:T(8,128)(2,1)S(1)} %get-tuple-element.39.p_ref), channel_id=1, source_target_pairs={{0,2},{2,0},{4,6},{6,4},{8,10},{10,8},{12,14},{14,12},{1,3},{3,1},... | collective-permute-start | bytes 589832 | tf_op jit(solution)/shard_map/ppermute | solution.py:311
  9.2 11.9 %collective-permute-start.10 = (bf16[192,512]{1,0:T(8,128)(2,1)S(1)}, bf16[192,512]{1,0:T(8,128)(2,1)S(1)}, u32[]{:S(2)}, u32[]{:S(2)}) collective-permute-start(bf16[192,512]{1,0:T(8,128)(2,1)S(1)} %get-tuple-element.45), channel_id=1, source_target_pairs={{0,8},{2,10},{4,12},{6,14},{8,0},{10,2},{12,4},{14,6},{1,9},{3,11}... | collective-permute-start | bytes 589832 | tf_op jit(solution)/shard_map/ppermute | solution.py:316
  11.7 9.8 %collective-permute-start.17 = (bf16[192,512]{1,0:T(8,128)(2,1)S(1)}, bf16[192,512]{1,0:T(8,128)(2,1)S(1)}, u32[]{:S(2)}, u32[]{:S(2)}) collective-permute-start(bf16[192,512]{1,0:T(8,128)(2,1)S(1)} %get-tuple-element.48), channel_id=1, source_target_pairs={{0,4},{2,6},{4,0},{6,2},{8,12},{10,14},{12,8},{14,10},{1,5},{3,7},... | collective-permute-start | bytes 589832 | tf_op jit(solution)/shard_map/ppermute | solution.py:316
  13.3 13.1 %collective-permute-start.5 = (bf16[192,512]{1,0:T(8,128)(2,1)S(1)}, bf16[192,512]{1,0:T(8,128)(2,1)S(1)}, u32[]{:S(2)}, u32[]{:S(2)}) collective-permute-start(bf16[192,512]{1,0:T(8,128)(2,1)S(1)} %get-tuple-element.39.p_ref), channel_id=1, source_target_pairs={{0,1},{1,0},{2,3},{3,2},{4,5},{5,4},{6,7},{7,6},{8,9},{9,8},{10,11... | collective-permute-start | bytes 589832 | tf_op jit(solution)/shard_map/ppermute | solution.py:306
  14.4 12.1 %collective-permute-start.6 = (bf16[192,512]{1,0:T(8,128)(2,1)S(1)}, bf16[192,512]{1,0:T(8,128)(2,1)S(1)}, u32[]{:S(2)}, u32[]{:S(2)}) collective-permute-start(bf16[192,512]{1,0:T(8,128)(2,1)S(1)} %collective-permute-done.4.q_ref), channel_id=1, source_target_pairs={{0,1},{1,0},{2,3},{3,2},{4,5},{5,4},{6,7},{7,6},{8,9},{9,8},{10,11... | collective-permute-start | bytes 589832 | tf_op jit(solution)/shard_map/ppermute | solution.py:306
  21.1 7.8 %collective-permute-start.11 = (bf16[192,512]{1,0:T(8,128)(2,1)S(1)}, bf16[192,512]{1,0:T(8,128)(2,1)S(1)}, u32[]{:S(2)}, u32[]{:S(2)}) collective-permute-start(bf16[192,512]{1,0:T(8,128)(2,1)S(1)} %collective-permute-done.10.p_ref), channel_id=1, source_target_pairs={{0,2},{2,0},{4,6},{6,4},{8,10},{10,8},{12,14},{14,12},{1,3},{3,1},... | collective-permute-start | bytes 589832 | tf_op jit(solution)/shard_map/ppermute | solution.py:311
  21.5 9.5 %collective-permute-start.18 = (bf16[192,512]{1,0:T(8,128)(2,1)S(1)}, bf16[192,512]{1,0:T(8,128)(2,1)S(1)}, u32[]{:S(2)}, u32[]{:S(2)}) collective-permute-start(bf16[192,512]{1,0:T(8,128)(2,1)S(1)} %after.7.p_ref), channel_id=1, source_target_pairs={{0,2},{2,0},{4,6},{6,4},{8,10},{10,8},{12,14},{14,12},{1,3},{3,1},... | collective-permute-start | bytes 589832 | tf_op jit(solution)/shard_map/ppermute | solution.py:311
  23.1 8.0 %collective-permute-start.8 = (bf16[192,512]{1,0:T(8,128)(2,1)S(1)}, bf16[192,512]{1,0:T(8,128)(2,1)S(1)}, u32[]{:S(2)}, u32[]{:S(2)}) collective-permute-start(bf16[192,512]{1,0:T(8,128)(2,1)S(1)} %get-tuple-element.44), channel_id=1, source_target_pairs={{0,12},{2,14},{4,8},{6,10},{8,4},{10,6},{12,0},{14,2},{1,13},{3,15... | collective-permute-start | bytes 589832 | tf_op jit(solution)/shard_map/ppermute | solution.py:316
  26.5 5.1 %collective-permute-start.12 = (bf16[192,512]{1,0:T(8,128)(2,1)S(1)}, bf16[192,512]{1,0:T(8,128)(2,1)S(1)}, u32[]{:S(2)}, u32[]{:S(2)}) collective-permute-start(bf16[192,512]{1,0:T(8,128)(2,1)S(1)} %collective-permute-done.10.p_ref), channel_id=1, source_target_pairs={{0,1},{1,0},{2,3},{3,2},{4,5},{5,4},{6,7},{7,6},{8,9},{9,8},{10,11... | collective-permute-start | bytes 589832 | tf_op jit(solution)/shard_map/ppermute | solution.py:306
  28.3 10.1 %collective-permute-start.7 = (bf16[2,192,512]{2,1,0:T(8,128)(2,1)S(1)}, bf16[2,192,512]{2,1,0:T(8,128)(2,1)S(1)}, u32[]{:S(2)}, u32[]{:S(2)}) collective-permute-start(bf16[2,192,512]{2,1,0:T(8,128)(2,1)S(1)} %get-tuple-element.43), channel_id=1, source_target_pairs={{0,1},{1,0},{2,3},{3,2},{4,5},{5,4},{6,7},{7,6},{8,9},{9,8},{10,11... | collective-permute-start | bytes 1179656 | tf_op jit(solution)/shard_map/ppermute | solution.py:306
  28.9 3.4 %collective-permute-start.13 = (bf16[192,512]{1,0:T(8,128)(2,1)S(1)}, bf16[192,512]{1,0:T(8,128)(2,1)S(1)}, u32[]{:S(2)}, u32[]{:S(2)}) collective-permute-start(bf16[192,512]{1,0:T(8,128)(2,1)S(1)} %collective-permute-done.11.q_ref), channel_id=1, source_target_pairs={{0,1},{1,0},{2,3},{3,2},{4,5},{5,4},{6,7},{7,6},{8,9},{9,8},{10,11... | collective-permute-start | bytes 589832 | tf_op jit(solution)/shard_map/ppermute | solution.py:306
  31.0 3.2 %collective-permute-start.20 = (bf16[192,512]{1,0:T(8,128)(2,1)S(1)}, bf16[192,512]{1,0:T(8,128)(2,1)S(1)}, u32[]{:S(2)}, u32[]{:S(2)}) collective-permute-start(bf16[192,512]{1,0:T(8,128)(2,1)S(1)} %collective-permute-done.18.q_ref), channel_id=1, source_target_pairs={{0,1},{1,0},{2,3},{3,2},{4,5},{5,4},{6,7},{7,6},{8,9},{9,8},{10,11... | collective-permute-start | bytes 589832 | tf_op jit(solution)/shard_map/ppermute | solution.py:306
  31.1 3.7 %collective-permute-start.19 = (bf16[192,512]{1,0:T(8,128)(2,1)S(1)}, bf16[192,512]{1,0:T(8,128)(2,1)S(1)}, u32[]{:S(2)}, u32[]{:S(2)}) collective-permute-start(bf16[192,512]{1,0:T(8,128)(2,1)S(1)} %after.7.p_ref), channel_id=1, source_target_pairs={{0,1},{1,0},{2,3},{3,2},{4,5},{5,4},{6,7},{7,6},{8,9},{9,8},{10,11... | collective-permute-start | bytes 589832 | tf_op jit(solution)/shard_map/ppermute | solution.py:306
  31.5 6.9 %collective-permute-start.9 = (bf16[192,512]{1,0:T(8,128)(2,1)S(1)}, bf16[192,512]{1,0:T(8,128)(2,1)S(1)}, u32[]{:S(2)}, u32[]{:S(2)}) collective-permute-start(bf16[192,512]{1,0:T(8,128)(2,1)S(1)} %collective-permute-done.8.p_ref), channel_id=1, source_target_pairs={{0,2},{2,0},{4,6},{6,4},{8,10},{10,8},{12,14},{14,12},{1,3},{3,1},... | collective-permute-start | bytes 589832 | tf_op jit(solution)/shard_map/ppermute | solution.py:311
  32.3 30.0 %collective-permute-start.3 = (f32[2,128]{1,0:T(2,128)S(1)}, f32[2,128]{1,0:T(2,128)S(1)}, u32[]{:S(2)}, u32[]{:S(2)}) collective-permute-start(f32[2,128]{1,0:T(2,128)S(1)} %get-tuple-element.35.gates_ref), channel_id=1, source_target_pairs={{0,1},{1,0},{2,3},{3,2},{4,5},{5,4},{6,7},{7,6},{8,9},{9,8},{10,11... | collective-permute-start | bytes 3080 | tf_op jit(solution)/shard_map/ppermute | solution.py:306
  34.2 6.2 %collective-permute-start.14 = (bf16[192,512]{1,0:T(8,128)(2,1)S(1)}, bf16[192,512]{1,0:T(8,128)(2,1)S(1)}, u32[]{:S(2)}, u32[]{:S(2)}) collective-permute-start(bf16[192,512]{1,0:T(8,128)(2,1)S(1)} %collective-permute-done.8.p_ref), channel_id=1, source_target_pairs={{0,1},{1,0},{2,3},{3,2},{4,5},{5,4},{6,7},{7,6},{8,9},{9,8},{10,11... | collective-permute-start | bytes 589832 | tf_op jit(solution)/shard_map/ppermute | solution.py:306
  34.8 4.3 %collective-permute-start.16 = (bf16[2,192,512]{2,1,0:T(8,128)(2,1)S(1)}, bf16[2,192,512]{2,1,0:T(8,128)(2,1)S(1)}, u32[]{:S(2)}, u32[]{:S(2)}) collective-permute-start(bf16[2,192,512]{2,1,0:T(8,128)(2,1)S(1)} %get-tuple-element.47), channel_id=1, source_target_pairs={{0,1},{1,0},{2,3},{3,2},{4,5},{5,4},{6,7},{7,6},{8,9},{9,8},{10,11... | collective-permute-start | bytes 1179656 | tf_op jit(solution)/shard_map/ppermute | solution.py:306
  38.4 4.1 %collective-permute-start.24 = (bf16[2,192,512]{2,1,0:T(8,128)(2,1)S(1)}, bf16[2,192,512]{2,1,0:T(8,128)(2,1)S(1)}, u32[]{:S(2)}, u32[]{:S(2)}) collective-permute-start(bf16[2,192,512]{2,1,0:T(8,128)(2,1)S(1)} %get-tuple-element.52), channel_id=1, source_target_pairs={{0,1},{1,0},{2,3},{3,2},{4,5},{5,4},{6,7},{7,6},{8,9},{9,8},{10,11... | collective-permute-start | bytes 1179656 | tf_op jit(solution)/shard_map/ppermute | solution.py:306
  38.4 2.0 %collective-permute-start.15 = (bf16[192,512]{1,0:T(8,128)(2,1)S(1)}, bf16[192,512]{1,0:T(8,128)(2,1)S(1)}, u32[]{:S(2)}, u32[]{:S(2)}) collective-permute-start(bf16[192,512]{1,0:T(8,128)(2,1)S(1)} %after.6.q_ref), channel_id=1, source_target_pairs={{0,1},{1,0},{2,3},{3,2},{4,5},{5,4},{6,7},{7,6},{8,9},{9,8},{10,11... | collective-permute-start | bytes 589832 | tf_op jit(solution)/shard_map/ppermute | solution.py:306
  39.3 6.9 %collective-permute-start.27 = (bf16[192,512]{1,0:T(8,128)(2,1)S(1)}, bf16[192,512]{1,0:T(8,128)(2,1)S(1)}, u32[]{:S(2)}, u32[]{:S(2)}) collective-permute-start(bf16[192,512]{1,0:T(8,128)(2,1)S(1)} %fusion.9.refs_1_), channel_id=1, source_target_pairs={{0,2},{2,0},{4,6},{6,4},{8,10},{10,8},{12,14},{14,12},{1,3},{3,1},... | collective-permute-start | bytes 589832 | tf_op jit(solution)/shard_map/ppermute | solution.py:311
  42.3 1.8 %collective-permute-start.21 = (bf16[2,192,512]{2,1,0:T(8,128)(2,1)S(1)}, bf16[2,192,512]{2,1,0:T(8,128)(2,1)S(1)}, u32[]{:S(2)}, u32[]{:S(2)}) collective-permute-start(bf16[2,192,512]{2,1,0:T(8,128)(2,1)S(1)} %get-tuple-element.51), channel_id=1, source_target_pairs={{0,1},{1,0},{2,3},{3,2},{4,5},{5,4},{6,7},{7,6},{8,9},{9,8},{10,11... | collective-permute-start | bytes 1179656 | tf_op jit(solution)/shard_map/ppermute | solution.py:306
  44.2 7.6 %collective-permute-start.22 = (bf16[192,512]{1,0:T(8,128)(2,1)S(1)}, bf16[192,512]{1,0:T(8,128)(2,1)S(1)}, u32[]{:S(2)}, u32[]{:S(2)}) collective-permute-start(bf16[192,512]{1,0:T(8,128)(2,1)S(1)} %fusion.10.refs_1_), channel_id=1, source_target_pairs={{0,2},{2,0},{4,6},{6,4},{8,10},{10,8},{12,14},{14,12},{1,3},{3,1},... | collective-permute-start | bytes 589832 | tf_op jit(solution)/shard_map/ppermute | solution.py:311
  46.2 17.2 %collective-permute-start.28 = (bf16[192,512]{1,0:T(8,128)(2,1)S(1)}, bf16[192,512]{1,0:T(8,128)(2,1)S(1)}, u32[]{:S(2)}, u32[]{:S(2)}) collective-permute-start(bf16[192,512]{1,0:T(8,128)(2,1)S(1)} %fusion.1), channel_id=1, source_target_pairs={{0,8},{2,10},{4,12},{6,14},{8,0},{10,2},{12,4},{14,6},{1,9},{3,11}... | collective-permute-start | bytes 589832 | tf_op jit(solution)/shard_map/ppermute | solution.py:316
  49.0 8.5 %collective-permute-start.25 = (bf16[192,512]{1,0:T(8,128)(2,1)S(1)}, bf16[192,512]{1,0:T(8,128)(2,1)S(1)}, u32[]{:S(2)}, u32[]{:S(2)}) collective-permute-start(bf16[192,512]{1,0:T(8,128)(2,1)S(1)} %after.11), channel_id=1, source_target_pairs={{0,2},{2,0},{4,6},{6,4},{8,10},{10,8},{12,14},{14,12},{1,3},{3,1},... | collective-permute-start | bytes 589832 | tf_op jit(solution)/shard_map/ppermute | solution.py:311
  51.9 14.2 %collective-permute-start.29 = (bf16[192,512]{1,0:T(8,128)(2,1)S(1)}, bf16[192,512]{1,0:T(8,128)(2,1)S(1)}, u32[]{:S(2)}, u32[]{:S(2)}) collective-permute-start(bf16[192,512]{1,0:T(8,128)(2,1)S(1)} %fusion.5.refs_1_), channel_id=1, source_target_pairs={{0,12},{2,14},{4,8},{6,10},{8,4},{10,6},{12,0},{14,2},{1,13},{3,15... | collective-permute-start | bytes 589832 | tf_op jit(solution)/shard_map/ppermute | solution.py:316
  56.6 5.7 %collective-permute-start.23 = (bf16[192,512]{1,0:T(8,128)(2,1)S(1)}, bf16[192,512]{1,0:T(8,128)(2,1)S(1)}, u32[]{:S(2)}, u32[]{:S(2)}) collective-permute-start(bf16[192,512]{1,0:T(8,128)(2,1)S(1)} %after.10), channel_id=1, source_target_pairs={{0,2},{2,0},{4,6},{6,4},{8,10},{10,8},{12,14},{14,12},{1,3},{3,1},... | collective-permute-start | bytes 589832 | tf_op jit(solution)/shard_map/ppermute | solution.py:311
  57.6 8.5 %collective-permute-start.26 = (bf16[192,512]{1,0:T(8,128)(2,1)S(1)}, bf16[192,512]{1,0:T(8,128)(2,1)S(1)}, u32[]{:S(2)}, u32[]{:S(2)}) collective-permute-start(bf16[192,512]{1,0:T(8,128)(2,1)S(1)} %fusion.3), channel_id=1, source_target_pairs={{0,4},{2,6},{4,0},{6,2},{8,12},{10,14},{12,8},{14,10},{1,5},{3,7},... | collective-permute-start | bytes 589832 | tf_op jit(solution)/shard_map/ppermute | solution.py:316
  66.6 1.4 %collective-permute-start.30 = (bf16[128,512]{1,0:T(8,128)(2,1)S(1)}, bf16[128,512]{1,0:T(8,128)(2,1)S(1)}, u32[]{:S(2)}, u32[]{:S(2)}) collective-permute-start(bf16[128,512]{1,0:T(8,128)(2,1)S(1)} %get-tuple-element.54), channel_id=1, source_target_pairs={{0,1},{1,0},{2,3},{3,2},{4,5},{5,4},{6,7},{7,6},{8,9},{9,8},{10,11... | collective-permute-start | bytes 393224 | tf_op jit(solution)/shard_map/ppermute | solution.py:306

commit v18 on v17

--- a/solution.py
+++ b/solution.py
@@ -224,15 +224,18 @@
         ).astype(jnp.bfloat16)
 
 
-def expert_kernel(
-    core_ref, p_ref, q_ref, p2_ref, q2_ref, in_ref, out_ref, keep_ref, send_ref, rows_ref
-):
+def pair_kernel(p_ref, q_ref, pair_ref):
+    capacity = p_ref.shape[0]
+    pair_ref[:capacity] = p_ref[...]
+    pair_ref[capacity:] = q_ref[...]
+
+
+def expert_kernel(core_ref, pair_ref, pair2_ref, in_ref, out_ref, keep_ref, send_ref, rows_ref):
     core = core_ref[0]
-    capacity, half = p_ref.shape
-    rows_ref[:capacity, part_of(core, half)] = p_ref[...]
-    rows_ref[capacity:, part_of(core, half)] = q_ref[...]
-    rows_ref[:capacity, part_of(1 - core, half)] = p2_ref[...]
-    rows_ref[capacity:, part_of(1 - core, half)] = q2_ref[...]
+    half = pair_ref.shape[1]
+    capacity = pair_ref.shape[0] // 2
+    rows_ref[:, part_of(core, half)] = pair_ref[...]
+    rows_ref[:, part_of(1 - core, half)] = pair2_ref[...]
     hidden = jnp.dot(rows_ref[...], in_ref[...], preferred_element_type=jnp.float32)
     hidden = jnp.maximum(hidden, 0.0).astype(jnp.bfloat16)
     send = jnp.dot(
@@ -404,13 +407,15 @@
         [fc_in, fc_out],
         scratch=[pltpu.SemaphoreType.DMA((2,))],
     )
-    def run(p, q, p2, q2):
+    both_blocks = [((2 * capacity, half), jnp.bfloat16)]
+
+    def run(own, other):
         keep, sent = call(
             expert_kernel,
             "expert",
             [((2, capacity, half), jnp.float32), ((2, capacity, half), jnp.bfloat16)],
             [core],
-            [p, q, p2, q2, near_in, near_out],
+            [own, other, near_in, near_out],
             scratch=[pltpu.VMEM((2 * capacity, width), jnp.bfloat16)],
             vmem_mib=16,
         )
@@ -430,33 +435,39 @@
     q = swap_owner(p)
     ps[0], qs[0] = p, q
     p = travelling[0]
-    p = after(p, near_in)
     q = swap_owner(p)
     ps[1], qs[1] = p, q
     p = travelling[1]
+    p = after(p, near_in)
     q = swap_owner(p)
     ps[2], qs[2] = p, q
     p = travelling[2]
     q = swap_owner(p)
     ps[3], qs[3] = p, q
     p, q = ps[0], qs[0]
-    p2, q2 = swap(p), swap(q)
-    kept[0], moving = run(p, q, p2, q2)
+    (own,) = call(pair_kernel, "pair", both_blocks, [], [p, q])
+    q2 = swap(own)
+    kept[0], moving = run(own, q2)
     boths[0], halves[0] = sums(kept[0], moving)
     p, q = ps[2], qs[2]
-    p2, q2 = swap(p), swap(q)
-    kept[2], moving = run(p, q, p2, q2)
+    q = after(q, kept[0])
+    (own,) = call(pair_kernel, "pair", both_blocks, [], [p, q])
+    q2 = swap(own)
+    kept[2], moving = run(own, q2)
     boths[2], halves[2] = sums(kept[2], moving)
     p, q = ps[1], qs[1]
-    p2, q2 = swap(p), swap(q)
-    q2 = after(q2, kept[0], kept[2])
-    kept[1], moving = run(p, q, p2, q2)
+    q = after(q, travelling[2])
+    (own,) = call(pair_kernel, "pair", both_blocks, [], [p, q])
+    q2 = swap(own)
+    q2 = after(q2, kept[2])
+    kept[1], moving = run(own, q2)
     boths[1], halves[1] = sums(kept[1], moving)
     p, q = ps[3], qs[3]
     q = after(q, kept[2])
-    p2, q2 = swap(p), swap(q)
-    q2 = after(q2, halves[2], kept[1])
-    kept[3], moving = run(p, q, p2, q2)
+    (own,) = call(pair_kernel, "pair", both_blocks, [], [p, q])
+    q2 = swap(own)
+    q2 = after(q2, kept[1], halves[2])
+    kept[3], moving = run(own, q2)
     boths[3], halves[3] = sums(kept[3], moving)
     leaving = halves[2]
     across = swap_owner(leaving)

time: 68.9 us -> 69.9 us (1.015)
  waiting for transfers between devices: 22.7 us -> 23.8 us
    ppermute x8, waiting for transfers between devices: 10.8 us -> 11.9 us  [swap_owner(): return lax.ppermute(values, 'expert', [(i, i ^ 1) for i in range(owners)])]
    ppermute x17 -> x13, starting transfers between devices: 3.6 us -> 2.78 us  [swap(): return lax.ppermute(values, 'section', [(0, 1), (1, 0)])]
    ppermute x17 -> x13, waiting for transfers between devices: 3.6 us -> 3.37 us  [swap(): return lax.ppermute(values, 'section', [(0, 1), (1, 0)])]
    pallas_call x11 -> x15, Pallas kernels: 14.9 us -> 15 us  [call(): pl.pallas_call(kernel, out_shape=tuple((jax.ShapeDtypeStruct(*out) for ou...]
  transfers between devices with their start and end apart: 31 -> 27, of which waited for: 14 -> 14; matrix products, arithmetic and copies ran while one was open for 1% -> 1% of each run, Pallas kernels for 17% -> 17%
where the time goes in v18:
time: 69.9 us; the launch traced here: 69.7 us
  starting transfers between devices  29.2 us (42%)
  waiting for transfers between devices  23.8 us (34%)
  Pallas kernels  15 us (21%)
  between operations  0.94 us (1%)
    ppermute x6, starting transfers between devices, exchange(): lax.ppermute(values, 'expert', [(i, i ^ 2 * offset) for i in range(owners)])  16.6 us
    pallas_call x15, Pallas kernels, call(): pl.pallas_call(kernel, out_shape=tuple((jax.ShapeDtypeStruct(*out) for ou...  15 us
    ppermute x8, waiting for transfers between devices, swap_owner(): return lax.ppermute(values, 'expert', [(i, i ^ 1) for i in range(owners)])  11.9 us
    ppermute x8, starting transfers between devices, swap_owner(): return lax.ppermute(values, 'expert', [(i, i ^ 1) for i in range(owners)])  9.82 us
    ppermute x6, waiting for transfers between devices, exchange(): lax.ppermute(values, 'expert', [(i, i ^ 2 * offset) for i in range(owners)])  8.6 us
    ppermute x13, waiting for transfers between devices, swap(): return lax.ppermute(values, 'section', [(0, 1), (1, 0)])  3.37 us
    ppermute x13, starting transfers between devices, swap(): return lax.ppermute(values, 'section', [(0, 1), (1, 0)])  2.78 us
  transfers between devices with their start and end apart: 27, of which 14 were waited for; matrix products, arithmetic and copies ran while one was open for 1% of the time, Pallas kernels for 17%

profile of v18, /device:TPU:0, one launch (start us, length us, event | category | flops | bytes accessed | tf_op | source)
XLA Modules:
  0.0 69.7 jit_solution(13509734982738837986)
XLA Ops:
  0.0 0.5 collective-permute-start
  0.5 0.1 collective-permute-start.1
  1.2 1.8 %attend_own.1 = (bf16[128,512]{1,0:T(8,128)(2,1)S(1)}, bf16[128,512]{1,0:T(8,128)(2,1)S(1)}, bf16[128,512]{1,0:T(8,128)(2,1)S(1)}) custom-call(s32[1]{0:T(128)} %bitcast.core_ref, s32[1]{0:T(128)S(6)} %copy.28.source_ref, bf16[1,128,1024]{2,1,0:T(8,128)(2,1)} %x_in.1, f32[1,1024]{1,0:T(1,128)} %bitcast.40, bf16[2,80,512]{2,1,0:T(8,128)(2,1)} %keys_in.1, ...), custom_call_target="tpu_custom_call" | custom-call | tf_op jit(solution)/shard_map/attend_own/pallas_call | solution.py:25
  2.9 0.0 collective-permute-done.keys_ref
  2.9 0.0 collective-permute-done.1.values_ref
  3.0 1.2 %attend_other.1 = (bf16[128,1024]{1,0:T(8,128)(2,1)S(1)}, bf16[128,512]{1,0:T(8,128)(2,1)S(1)}, bf16[128,512]{1,0:T(8,128)(2,1)S(1)}, f32[2,128]{1,0:T(2,128)S(1)}, s32[2,2,128]{2,1,0:T(2,128)S(1)}) custom-call(s32[1]{0:T(128)} %bitcast.core_ref, s32[1]{0:T(128)S(6)} %copy.28.source_ref, bf16[128,512]{1,0:T(8,128)(2,1)S(1)} %get-tuple-element.30.own_ref, ...), custom_call_target="tpu_custom_call" | custom-call | tf_op jit(solution)/shard_map/attend_other/pallas_call | solution.py:25
  4.2 0.5 collective-permute-start.2
  4.7 1.0 %collective-permute-done.2.other_ref = bf16[128,512]{1,0:T(8,128)(2,1)S(1)} collective-permute-done((bf16[128,512]{1,0:T(8,128)(2,1)S(1)}, bf16[128,512]{1,0:T(8,128)(2,1)S(1)}, u32[]{:S(2)}, u32[]{:S(2)}) %collective-permute-start.2) | collective-permute-done | bytes 131104 | tf_op jit(solution)/shard_map/ppermute | solution.py:309
  5.7 0.5 select.5
  6.2 2.9 %collective-permute-start.4 = (bf16[192,512]{1,0:T(8,128)(2,1)S(1)}, bf16[192,512]{1,0:T(8,128)(2,1)S(1)}, u32[]{:S(2)}, u32[]{:S(2)}) collective-permute-start(bf16[192,512]{1,0:T(8,128)(2,1)S(1)} %get-tuple-element.39.p_ref), channel_id=1, source_target_pairs={{0,2},{2,0},{4,6},{6,4},{8,10},{10,8},{12,14},{14,12},{1,3},{3,1},... | collective-permute-start | bytes 589832 | tf_op jit(solution)/shard_map/ppermute | solution.py:314
  9.2 2.6 %collective-permute-start.9 = (bf16[192,512]{1,0:T(8,128)(2,1)S(1)}, bf16[192,512]{1,0:T(8,128)(2,1)S(1)}, u32[]{:S(2)}, u32[]{:S(2)}) collective-permute-start(bf16[192,512]{1,0:T(8,128)(2,1)S(1)} %get-tuple-element.45), channel_id=1, source_target_pairs={{0,8},{2,10},{4,12},{6,14},{8,0},{10,2},{12,4},{14,6},{1,9},{3,11}... | collective-permute-start | bytes 589832 | tf_op jit(solution)/shard_map/ppermute | solution.py:319
  11.7 2.6 %collective-permute-done.4.q_ref = bf16[192,512]{1,0:T(8,128)(2,1)S(1)} collective-permute-done((bf16[192,512]{1,0:T(8,128)(2,1)S(1)}, bf16[192,512]{1,0:T(8,128)(2,1)S(1)}, u32[]{:S(2)}, u32[]{:S(2)}) %collective-permute-start.4) | collective-permute-done | bytes 196640 | tf_op jit(solution)/shard_map/ppermute | solution.py:314
  14.4 0.1 collective-permute-start.5
  14.5 1.9 %collective-permute-start.13 = (bf16[192,512]{1,0:T(8,128)(2,1)S(1)}, bf16[192,512]{1,0:T(8,128)(2,1)S(1)}, u32[]{:S(2)}, u32[]{:S(2)}) collective-permute-start(bf16[192,512]{1,0:T(8,128)(2,1)S(1)} %get-tuple-element.47), channel_id=1, source_target_pairs={{0,4},{2,6},{4,0},{6,2},{8,12},{10,14},{12,8},{14,10},{1,5},{3,7},... | collective-permute-start | bytes 589832 | tf_op jit(solution)/shard_map/ppermute | solution.py:319
  16.4 2.2 %load.1 = (bf16[1024,1024]{1,0:T(8,128)(2,1)S(1)}, bf16[1024,1024]{1,0:T(8,128)(2,1)S(1)}) custom-call(bf16[1024,1024]{1,0:T(8,128)(2,1)} %in_in.1, bf16[1024,1024]{1,0:T(8,128)(2,1)} %out_in.1), custom_call_target="tpu_custom_call" | custom-call | tf_op jit(solution)/shard_map/load/pallas_call | solution.py:25
  18.6 2.4 %collective-permute-done.9.refs_0_ = bf16[192,512]{1,0:T(8,128)(2,1)S(1)} collective-permute-done((bf16[192,512]{1,0:T(8,128)(2,1)S(1)}, bf16[192,512]{1,0:T(8,128)(2,1)S(1)}, u32[]{:S(2)}, u32[]{:S(2)}) %collective-permute-start.9) | collective-permute-done | bytes 196640 | tf_op jit(solution)/shard_map/ppermute | solution.py:319
  21.1 0.5 collective-permute-start.10
  21.5 3.5 %collective-permute-start.7 = (bf16[192,512]{1,0:T(8,128)(2,1)S(1)}, bf16[192,512]{1,0:T(8,128)(2,1)S(1)}, u32[]{:S(2)}, u32[]{:S(2)}) collective-permute-start(bf16[192,512]{1,0:T(8,128)(2,1)S(1)} %get-tuple-element.44), channel_id=1, source_target_pairs={{0,12},{2,14},{4,8},{6,10},{8,4},{10,6},{12,0},{14,2},{1,13},{3,15... | collective-permute-start | bytes 589832 | tf_op jit(solution)/shard_map/ppermute | solution.py:319
  25.1 0.0 collective-permute-done.13.p_ref
  25.1 1.5 %collective-permute-start.14 = (bf16[192,512]{1,0:T(8,128)(2,1)S(1)}, bf16[192,512]{1,0:T(8,128)(2,1)S(1)}, u32[]{:S(2)}, u32[]{:S(2)}) collective-permute-start(bf16[192,512]{1,0:T(8,128)(2,1)S(1)} %collective-permute-done.13.p_ref), channel_id=1, source_target_pairs={{0,2},{2,0},{4,6},{6,4},{8,10},{10,8},{12,14},{14,12},{1,3},{3,1},... | collective-permute-start | bytes 589832 | tf_op jit(solution)/shard_map/ppermute | solution.py:314
  26.6 0.0 collective-permute-done.5.pair2_ref
  26.6 1.8 %expert.4 = (f32[2,192,512]{2,1,0:T(8,128)S(1)}, bf16[2,192,512]{2,1,0:T(8,128)(2,1)S(1)}) custom-call(s32[1]{0:T(128)} %bitcast.core_ref, bf16[384,512]{1,0:T(8,128)(2,1)S(1)} %pair.4.pair_ref, bf16[384,512]{1,0:T(8,128)(2,1)S(1)} %collective-permute-done.5.pair2_ref, bf16[1024,1024]{1,0:T(8,128)(2,1)S(1)} %get-tuple-element.40.in_ref.refs_1_, ...), custom_call_target="tpu_custom_call" | custom-call | tf_op jit(solution)/shard_map/expert/pallas_call | solution.py:25
  28.4 0.0 collective-permute-done.10.refs_0_
  28.5 0.1 collective-permute-start.11
  28.5 1.4 %collective-permute-done.7.p_ref.refs_1_ = bf16[192,512]{1,0:T(8,128)(2,1)S(1)} collective-permute-done((bf16[192,512]{1,0:T(8,128)(2,1)S(1)}, bf16[192,512]{1,0:T(8,128)(2,1)S(1)}, u32[]{:S(2)}, u32[]{:S(2)}) %collective-permute-start.7) | collective-permute-done | bytes 196640 | tf_op jit(solution)/shard_map/ppermute | solution.py:319
  29.9 1.7 %collective-permute-done.14.refs_0_ = bf16[192,512]{1,0:T(8,128)(2,1)S(1)} collective-permute-done((bf16[192,512]{1,0:T(8,128)(2,1)S(1)}, bf16[192,512]{1,0:T(8,128)(2,1)S(1)}, u32[]{:S(2)}, u32[]{:S(2)}) %collective-permute-start.14) | collective-permute-done | bytes 196640 | tf_op jit(solution)/shard_map/ppermute | solution.py:314
  31.6 0.1 collective-permute-start.15
  31.7 0.5 collective-permute-start.6
  32.2 1.2 %collective-permute-start.8 = (bf16[192,512]{1,0:T(8,128)(2,1)S(1)}, bf16[192,512]{1,0:T(8,128)(2,1)S(1)}, u32[]{:S(2)}, u32[]{:S(2)}) collective-permute-start(bf16[192,512]{1,0:T(8,128)(2,1)S(1)} %collective-permute-done.7.p_ref.refs_1_), channel_id=1, source_target_pairs={{0,2},{2,0},{4,6},{6,4},{8,10},{10,8},{12,14},{14,12},{1,3},{3,1},... | collective-permute-start | bytes 589832 | tf_op jit(solution)/shard_map/ppermute | solution.py:314
  33.4 1.8 %expert.5 = (f32[2,192,512]{2,1,0:T(8,128)S(1)}, bf16[2,192,512]{2,1,0:T(8,128)(2,1)S(1)}) custom-call(s32[1]{0:T(128)} %bitcast.core_ref, bf16[384,512]{1,0:T(8,128)(2,1)S(1)} %pair.5.pair_ref, bf16[384,512]{1,0:T(8,128)(2,1)S(1)} %collective-permute-done.11.pair2_ref, bf16[1024,1024]{1,0:T(8,128)(2,1)S(1)} %get-tuple-element.40.in_ref.refs_1_, ...), custom_call_target="tpu_custom_call" | custom-call | tf_op jit(solution)/shard_map/expert/pallas_call | solution.py:25
  35.2 0.6 collective-permute-start.16
  35.8 1.8 %expert.6 = (f32[2,192,512]{2,1,0:T(8,128)S(1)}, bf16[2,192,512]{2,1,0:T(8,128)(2,1)S(1)}) custom-call(s32[1]{0:T(128)} %bitcast.core_ref, bf16[384,512]{1,0:T(8,128)(2,1)S(1)} %pair.7.pair_ref, bf16[384,512]{1,0:T(8,128)(2,1)S(1)} %after.12.pair2_ref, bf16[1024,1024]{1,0:T(8,128)(2,1)S(1)} %get-tuple-element.40.in_ref.refs_1_, ...), custom_call_target="tpu_custom_call" | custom-call | tf_op jit(solution)/shard_map/expert/pallas_call | solution.py:25
  37.7 0.1 collective-permute-start.20
  37.8 1.3 %collective-permute-done.8.refs_0_ = bf16[192,512]{1,0:T(8,128)(2,1)S(1)} collective-permute-done((bf16[192,512]{1,0:T(8,128)(2,1)S(1)}, bf16[192,512]{1,0:T(8,128)(2,1)S(1)}, u32[]{:S(2)}, u32[]{:S(2)}) %collective-permute-start.8) | collective-permute-done | bytes 196640 | tf_op jit(solution)/shard_map/ppermute | solution.py:314
  39.1 0.1 collective-permute-start.12
  39.2 0.0 collective-permute-done.6
  39.2 0.1 convert_add_fusion.3
  39.3 0.0 collective-permute-done.16
  39.4 0.1 convert_add_fusion.2
  39.5 1.3 %collective-permute-start.23 = (bf16[192,512]{1,0:T(8,128)(2,1)S(1)}, bf16[192,512]{1,0:T(8,128)(2,1)S(1)}, u32[]{:S(2)}, u32[]{:S(2)}) collective-permute-start(bf16[192,512]{1,0:T(8,128)(2,1)S(1)} %fusion.9.refs_2_), channel_id=1, source_target_pairs={{0,2},{2,0},{4,6},{6,4},{8,10},{10,8},{12,14},{14,12},{1,3},{3,1},... | collective-permute-start | bytes 589832 | tf_op jit(solution)/shard_map/ppermute | solution.py:314
  40.8 0.1 collective-permute-done.12.refs_0_
  40.9 1.8 %expert.7 = (f32[2,192,512]{2,1,0:T(8,128)S(1)}, bf16[2,192,512]{2,1,0:T(8,128)(2,1)S(1)}) custom-call(s32[1]{0:T(128)} %bitcast.core_ref, bf16[384,512]{1,0:T(8,128)(2,1)S(1)} %pair.6.pair_ref, bf16[384,512]{1,0:T(8,128)(2,1)S(1)} %after.13.pair2_ref, bf16[1024,1024]{1,0:T(8,128)(2,1)S(1)} %get-tuple-element.40.in_ref.refs_1_, ...), custom_call_target="tpu_custom_call" | custom-call | tf_op jit(solution)/shard_map/expert/pallas_call | solution.py:25
  42.7 0.2 collective-permute-start.17
  42.9 0.0 collective-permute-done.20
  42.9 0.1 convert_add_fusion
  43.1 1.4 %collective-permute-done.17 = bf16[2,192,512]{2,1,0:T(8,128)(2,1)S(1)} collective-permute-done((bf16[2,192,512]{2,1,0:T(8,128)(2,1)S(1)}, bf16[2,192,512]{2,1,0:T(8,128)(2,1)S(1)}, u32[]{:S(2)}, u32[]{:S(2)}) %collective-permute-start.17) | collective-permute-done | bytes 393248 | tf_op jit(solution)/shard_map/ppermute | solution.py:309
  44.5 0.1 convert_add_fusion.1
  44.7 1.3 %collective-permute-start.18 = (bf16[192,512]{1,0:T(8,128)(2,1)S(1)}, bf16[192,512]{1,0:T(8,128)(2,1)S(1)}, u32[]{:S(2)}, u32[]{:S(2)}) collective-permute-start(bf16[192,512]{1,0:T(8,128)(2,1)S(1)} %fusion.10.refs_1_), channel_id=1, source_target_pairs={{0,2},{2,0},{4,6},{6,4},{8,10},{10,8},{12,14},{14,12},{1,3},{3,1},... | collective-permute-start | bytes 589832 | tf_op jit(solution)/shard_map/ppermute | solution.py:314
  45.9 0.9 %collective-permute-done.23 = bf16[192,512]{1,0:T(8,128)(2,1)S(1)} collective-permute-done((bf16[192,512]{1,0:T(8,128)(2,1)S(1)}, bf16[192,512]{1,0:T(8,128)(2,1)S(1)}, u32[]{:S(2)}, u32[]{:S(2)}) %collective-permute-start.23) | collective-permute-done | bytes 196640 | tf_op jit(solution)/shard_map/ppermute | solution.py:314
  46.9 0.1 fusion.1
  46.9 2.2 %collective-permute-start.24 = (bf16[192,512]{1,0:T(8,128)(2,1)S(1)}, bf16[192,512]{1,0:T(8,128)(2,1)S(1)}, u32[]{:S(2)}, u32[]{:S(2)}) collective-permute-start(bf16[192,512]{1,0:T(8,128)(2,1)S(1)} %fusion.1), channel_id=1, source_target_pairs={{0,8},{2,10},{4,12},{6,14},{8,0},{10,2},{12,4},{14,6},{1,9},{3,11}... | collective-permute-start | bytes 589832 | tf_op jit(solution)/shard_map/ppermute | solution.py:319
  49.1 0.5 collective-permute-start.21
  49.6 2.5 %collective-permute-done.18 = bf16[192,512]{1,0:T(8,128)(2,1)S(1)} collective-permute-done((bf16[192,512]{1,0:T(8,128)(2,1)S(1)}, bf16[192,512]{1,0:T(8,128)(2,1)S(1)}, u32[]{:S(2)}, u32[]{:S(2)}) %collective-permute-start.18) | collective-permute-done | bytes 196640 | tf_op jit(solution)/shard_map/ppermute | solution.py:314
  52.2 4.3 %collective-permute-start.25 = (bf16[192,512]{1,0:T(8,128)(2,1)S(1)}, bf16[192,512]{1,0:T(8,128)(2,1)S(1)}, u32[]{:S(2)}, u32[]{:S(2)}) collective-permute-start(bf16[192,512]{1,0:T(8,128)(2,1)S(1)} %fusion.5.refs_1_), channel_id=1, source_target_pairs={{0,12},{2,14},{4,8},{6,10},{8,4},{10,6},{12,0},{14,2},{1,13},{3,15... | collective-permute-start | bytes 589832 | tf_op jit(solution)/shard_map/ppermute | solution.py:319
  56.5 0.7 %collective-permute-start.19 = (bf16[192,512]{1,0:T(8,128)(2,1)S(1)}, bf16[192,512]{1,0:T(8,128)(2,1)S(1)}, u32[]{:S(2)}, u32[]{:S(2)}) collective-permute-start(bf16[192,512]{1,0:T(8,128)(2,1)S(1)} %after.14), channel_id=1, source_target_pairs={{0,2},{2,0},{4,6},{6,4},{8,10},{10,8},{12,14},{14,12},{1,3},{3,1},... | collective-permute-start | bytes 589832 | tf_op jit(solution)/shard_map/ppermute | solution.py:314
  57.3 2.1 %collective-permute-start.22 = (bf16[192,512]{1,0:T(8,128)(2,1)S(1)}, bf16[192,512]{1,0:T(8,128)(2,1)S(1)}, u32[]{:S(2)}, u32[]{:S(2)}) collective-permute-start(bf16[192,512]{1,0:T(8,128)(2,1)S(1)} %fusion.3), channel_id=1, source_target_pairs={{0,4},{2,6},{4,0},{6,2},{8,12},{10,14},{12,8},{14,10},{1,5},{3,7},... | collective-permute-start | bytes 589832 | tf_op jit(solution)/shard_map/ppermute | solution.py:319
  59.4 2.8 %collective-permute-done.19 = bf16[192,512]{1,0:T(8,128)(2,1)S(1)} collective-permute-done((bf16[192,512]{1,0:T(8,128)(2,1)S(1)}, bf16[192,512]{1,0:T(8,128)(2,1)S(1)}, u32[]{:S(2)}, u32[]{:S(2)}) %collective-permute-start.19) | collective-permute-done | bytes 196640 | tf_op jit(solution)/shard_map/ppermute | solution.py:314
  62.3 1.9 %collective-permute-done.24.rest_2_ = bf16[192,512]{1,0:T(8,128)(2,1)S(1)} collective-permute-done((bf16[192,512]{1,0:T(8,128)(2,1)S(1)}, bf16[192,512]{1,0:T(8,128)(2,1)S(1)}, u32[]{:S(2)}, u32[]{:S(2)}) %collective-permute-start.24) | collective-permute-done | bytes 196640 | tf_op jit(solution)/shard_map/ppermute | solution.py:319
  64.2 2.9 %collective-permute-done.22.rest_1_ = bf16[192,512]{1,0:T(8,128)(2,1)S(1)} collective-permute-done((bf16[192,512]{1,0:T(8,128)(2,1)S(1)}, bf16[192,512]{1,0:T(8,128)(2,1)S(1)}, u32[]{:S(2)}, u32[]{:S(2)}) %collective-permute-start.22) | collective-permute-done | bytes 196640 | tf_op jit(solution)/shard_map/ppermute | solution.py:319
  67.0 0.5 combine_other.1
  67.5 0.1 collective-permute-start.26
  67.6 0.5 combine_own.1.own_ref
  68.1 0.8 %collective-permute-done.26.other_ref = bf16[128,512]{1,0:T(8,128)(2,1)S(1)} collective-permute-done((bf16[128,512]{1,0:T(8,128)(2,1)S(1)}, bf16[128,512]{1,0:T(8,128)(2,1)S(1)}, u32[]{:S(2)}, u32[]{:S(2)}) %collective-permute-start.26) | collective-permute-done | bytes 131104 | tf_op jit(solution)/shard_map/ppermute | solution.py:309
  69.0 0.7 %finish.1 = bf16[128,1024]{1,0:T(8,128)(2,1)} custom-call(s32[1]{0:T(128)} %bitcast.core_ref, bf16[128,1024]{1,0:T(8,128)(2,1)S(1)} %get-tuple-element.33.state_ref, bf16[128,512]{1,0:T(8,128)(2,1)S(1)} %combine_own.1.own_ref, bf16[128,512]{1,0:T(8,128)(2,1)S(1)} %collective-permute-done.26.other_ref), custom_call_target="tpu_custom_call" | custom-call | tf_op jit(solution)/shard_map/finish/pallas_call | solution.py:25
  (25 shorter events, 0.4 us)
Async XLA Ops:
  0.0 2.9 %collective-permute-start = (bf16[2,80,512]{2,1,0:T(8,128)(2,1)}, bf16[2,80,512]{2,1,0:T(8,128)(2,1)S(1)}, u32[]{:S(2)}, u32[]{:S(2)}) collective-permute-start(bf16[2,80,512]{2,1,0:T(8,128)(2,1)} %keys_in.1), channel_id=1, source_target_pairs={{0,1},{1,0},{2,3},{3,2},{4,5},{5,4},{6,7},{7,6},{8,9},{9,8},{10,11... | collective-permute-start | bytes 491528 | tf_op jit(solution)/shard_map/ppermute | solution.py:309
  0.5 2.5 %collective-permute-start.1 = (bf16[2,80,512]{2,1,0:T(8,128)(2,1)}, bf16[2,80,512]{2,1,0:T(8,128)(2,1)S(1)}, u32[]{:S(2)}, u32[]{:S(2)}) collective-permute-start(bf16[2,80,512]{2,1,0:T(8,128)(2,1)} %values_in.1), channel_id=1, source_target_pairs={{0,1},{1,0},{2,3},{3,2},{4,5},{5,4},{6,7},{7,6},{8,9},{9,8},{10,11... | collective-permute-start | bytes 491528 | tf_op jit(solution)/shard_map/ppermute | solution.py:309
  4.2 1.5 %collective-permute-start.2 = (bf16[128,512]{1,0:T(8,128)(2,1)S(1)}, bf16[128,512]{1,0:T(8,128)(2,1)S(1)}, u32[]{:S(2)}, u32[]{:S(2)}) collective-permute-start(bf16[128,512]{1,0:T(8,128)(2,1)S(1)} %get-tuple-element.37), channel_id=1, source_target_pairs={{0,1},{1,0},{2,3},{3,2},{4,5},{5,4},{6,7},{7,6},{8,9},{9,8},{10,11... | collective-permute-start | bytes 393224 | tf_op jit(solution)/shard_map/ppermute | solution.py:309
  6.2 8.1 %collective-permute-start.4 = (bf16[192,512]{1,0:T(8,128)(2,1)S(1)}, bf16[192,512]{1,0:T(8,128)(2,1)S(1)}, u32[]{:S(2)}, u32[]{:S(2)}) collective-permute-start(bf16[192,512]{1,0:T(8,128)(2,1)S(1)} %get-tuple-element.39.p_ref), channel_id=1, source_target_pairs={{0,2},{2,0},{4,6},{6,4},{8,10},{10,8},{12,14},{14,12},{1,3},{3,1},... | collective-permute-start | bytes 589832 | tf_op jit(solution)/shard_map/ppermute | solution.py:314
  9.2 11.9 %collective-permute-start.9 = (bf16[192,512]{1,0:T(8,128)(2,1)S(1)}, bf16[192,512]{1,0:T(8,128)(2,1)S(1)}, u32[]{:S(2)}, u32[]{:S(2)}) collective-permute-start(bf16[192,512]{1,0:T(8,128)(2,1)S(1)} %get-tuple-element.45), channel_id=1, source_target_pairs={{0,8},{2,10},{4,12},{6,14},{8,0},{10,2},{12,4},{14,6},{1,9},{3,11}... | collective-permute-start | bytes 589832 | tf_op jit(solution)/shard_map/ppermute | solution.py:319
  14.4 12.2 %collective-permute-start.5 = (bf16[384,512]{1,0:T(8,128)(2,1)S(1)}, bf16[384,512]{1,0:T(8,128)(2,1)S(1)}, u32[]{:S(2)}, u32[]{:S(2)}) collective-permute-start(bf16[384,512]{1,0:T(8,128)(2,1)S(1)} %pair.4.pair_ref), channel_id=1, source_target_pairs={{0,1},{1,0},{2,3},{3,2},{4,5},{5,4},{6,7},{7,6},{8,9},{9,8},{10,11... | collective-permute-start | bytes 1179656 | tf_op jit(solution)/shard_map/ppermute | solution.py:309
  14.5 10.6 %collective-permute-start.13 = (bf16[192,512]{1,0:T(8,128)(2,1)S(1)}, bf16[192,512]{1,0:T(8,128)(2,1)S(1)}, u32[]{:S(2)}, u32[]{:S(2)}) collective-permute-start(bf16[192,512]{1,0:T(8,128)(2,1)S(1)} %get-tuple-element.47), channel_id=1, source_target_pairs={{0,4},{2,6},{4,0},{6,2},{8,12},{10,14},{12,8},{14,10},{1,5},{3,7},... | collective-permute-start | bytes 589832 | tf_op jit(solution)/shard_map/ppermute | solution.py:319
  21.1 7.4 %collective-permute-start.10 = (bf16[192,512]{1,0:T(8,128)(2,1)S(1)}, bf16[192,512]{1,0:T(8,128)(2,1)S(1)}, u32[]{:S(2)}, u32[]{:S(2)}) collective-permute-start(bf16[192,512]{1,0:T(8,128)(2,1)S(1)} %after.8.p_ref), channel_id=1, source_target_pairs={{0,2},{2,0},{4,6},{6,4},{8,10},{10,8},{12,14},{14,12},{1,3},{3,1},... | collective-permute-start | bytes 589832 | tf_op jit(solution)/shard_map/ppermute | solution.py:314
  21.5 8.4 %collective-permute-start.7 = (bf16[192,512]{1,0:T(8,128)(2,1)S(1)}, bf16[192,512]{1,0:T(8,128)(2,1)S(1)}, u32[]{:S(2)}, u32[]{:S(2)}) collective-permute-start(bf16[192,512]{1,0:T(8,128)(2,1)S(1)} %get-tuple-element.44), channel_id=1, source_target_pairs={{0,12},{2,14},{4,8},{6,10},{8,4},{10,6},{12,0},{14,2},{1,13},{3,15... | collective-permute-start | bytes 589832 | tf_op jit(solution)/shard_map/ppermute | solution.py:319
  25.1 6.5 %collective-permute-start.14 = (bf16[192,512]{1,0:T(8,128)(2,1)S(1)}, bf16[192,512]{1,0:T(8,128)(2,1)S(1)}, u32[]{:S(2)}, u32[]{:S(2)}) collective-permute-start(bf16[192,512]{1,0:T(8,128)(2,1)S(1)} %collective-permute-done.13.p_ref), channel_id=1, source_target_pairs={{0,2},{2,0},{4,6},{6,4},{8,10},{10,8},{12,14},{14,12},{1,3},{3,1},... | collective-permute-start | bytes 589832 | tf_op jit(solution)/shard_map/ppermute | solution.py:314
  28.5 4.9 %collective-permute-start.11 = (bf16[384,512]{1,0:T(8,128)(2,1)S(1)}, bf16[384,512]{1,0:T(8,128)(2,1)S(1)}, u32[]{:S(2)}, u32[]{:S(2)}) collective-permute-start(bf16[384,512]{1,0:T(8,128)(2,1)S(1)} %pair.5.pair_ref), channel_id=1, source_target_pairs={{0,1},{1,0},{2,3},{3,2},{4,5},{5,4},{6,7},{7,6},{8,9},{9,8},{10,11... | collective-permute-start | bytes 1179656 | tf_op jit(solution)/shard_map/ppermute | solution.py:309
  31.6 4.2 %collective-permute-start.15 = (bf16[384,512]{1,0:T(8,128)(2,1)S(1)}, bf16[384,512]{1,0:T(8,128)(2,1)S(1)}, u32[]{:S(2)}, u32[]{:S(2)}) collective-permute-start(bf16[384,512]{1,0:T(8,128)(2,1)S(1)} %pair.7.pair_ref), channel_id=1, source_target_pairs={{0,1},{1,0},{2,3},{3,2},{4,5},{5,4},{6,7},{7,6},{8,9},{9,8},{10,11... | collective-permute-start | bytes 1179656 | tf_op jit(solution)/shard_map/ppermute | solution.py:309
  31.7 7.5 %collective-permute-start.6 = (bf16[2,192,512]{2,1,0:T(8,128)(2,1)S(1)}, bf16[2,192,512]{2,1,0:T(8,128)(2,1)S(1)}, u32[]{:S(2)}, u32[]{:S(2)}) collective-permute-start(bf16[2,192,512]{2,1,0:T(8,128)(2,1)S(1)} %get-tuple-element.43), channel_id=1, source_target_pairs={{0,1},{1,0},{2,3},{3,2},{4,5},{5,4},{6,7},{7,6},{8,9},{9,8},{10,11... | collective-permute-start | bytes 1179656 | tf_op jit(solution)/shard_map/ppermute | solution.py:309
  32.2 6.9 %collective-permute-start.8 = (bf16[192,512]{1,0:T(8,128)(2,1)S(1)}, bf16[192,512]{1,0:T(8,128)(2,1)S(1)}, u32[]{:S(2)}, u32[]{:S(2)}) collective-permute-start(bf16[192,512]{1,0:T(8,128)(2,1)S(1)} %collective-permute-done.7.p_ref.refs_1_), channel_id=1, source_target_pairs={{0,2},{2,0},{4,6},{6,4},{8,10},{10,8},{12,14},{14,12},{1,3},{3,1},... | collective-permute-start | bytes 589832 | tf_op jit(solution)/shard_map/ppermute | solution.py:314
  33.4 28.9 %collective-permute-start.3 = (f32[2,128]{1,0:T(2,128)S(1)}, f32[2,128]{1,0:T(2,128)S(1)}, u32[]{:S(2)}, u32[]{:S(2)}) collective-permute-start(f32[2,128]{1,0:T(2,128)S(1)} %get-tuple-element.35.gates_ref), channel_id=1, source_target_pairs={{0,1},{1,0},{2,3},{3,2},{4,5},{5,4},{6,7},{7,6},{8,9},{9,8},{10,11... | collective-permute-start | bytes 3080 | tf_op jit(solution)/shard_map/ppermute | solution.py:309
  35.2 4.1 %collective-permute-start.16 = (bf16[2,192,512]{2,1,0:T(8,128)(2,1)S(1)}, bf16[2,192,512]{2,1,0:T(8,128)(2,1)S(1)}, u32[]{:S(2)}, u32[]{:S(2)}) collective-permute-start(bf16[2,192,512]{2,1,0:T(8,128)(2,1)S(1)} %get-tuple-element.49), channel_id=1, source_target_pairs={{0,1},{1,0},{2,3},{3,2},{4,5},{5,4},{6,7},{7,6},{8,9},{9,8},{10,11... | collective-permute-start | bytes 1179656 | tf_op jit(solution)/shard_map/ppermute | solution.py:309
  37.7 5.3 %collective-permute-start.20 = (bf16[2,192,512]{2,1,0:T(8,128)(2,1)S(1)}, bf16[2,192,512]{2,1,0:T(8,128)(2,1)S(1)}, u32[]{:S(2)}, u32[]{:S(2)}) collective-permute-start(bf16[2,192,512]{2,1,0:T(8,128)(2,1)S(1)} %get-tuple-element.52), channel_id=1, source_target_pairs={{0,1},{1,0},{2,3},{3,2},{4,5},{5,4},{6,7},{7,6},{8,9},{9,8},{10,11... | collective-permute-start | bytes 1179656 | tf_op jit(solution)/shard_map/ppermute | solution.py:309
  39.1 1.8 %collective-permute-start.12 = (bf16[384,512]{1,0:T(8,128)(2,1)S(1)}, bf16[384,512]{1,0:T(8,128)(2,1)S(1)}, u32[]{:S(2)}, u32[]{:S(2)}) collective-permute-start(bf16[384,512]{1,0:T(8,128)(2,1)S(1)} %pair.6.pair_ref), channel_id=1, source_target_pairs={{0,1},{1,0},{2,3},{3,2},{4,5},{5,4},{6,7},{7,6},{8,9},{9,8},{10,11... | collective-permute-start | bytes 1179656 | tf_op jit(solution)/shard_map/ppermute | solution.py:309
  39.5 7.4 %collective-permute-start.23 = (bf16[192,512]{1,0:T(8,128)(2,1)S(1)}, bf16[192,512]{1,0:T(8,128)(2,1)S(1)}, u32[]{:S(2)}, u32[]{:S(2)}) collective-permute-start(bf16[192,512]{1,0:T(8,128)(2,1)S(1)} %fusion.9.refs_2_), channel_id=1, source_target_pairs={{0,2},{2,0},{4,6},{6,4},{8,10},{10,8},{12,14},{14,12},{1,3},{3,1},... | collective-permute-start | bytes 589832 | tf_op jit(solution)/shard_map/ppermute | solution.py:314
  42.7 1.8 %collective-permute-start.17 = (bf16[2,192,512]{2,1,0:T(8,128)(2,1)S(1)}, bf16[2,192,512]{2,1,0:T(8,128)(2,1)S(1)}, u32[]{:S(2)}, u32[]{:S(2)}) collective-permute-start(bf16[2,192,512]{2,1,0:T(8,128)(2,1)S(1)} %get-tuple-element.51), channel_id=1, source_target_pairs={{0,1},{1,0},{2,3},{3,2},{4,5},{5,4},{6,7},{7,6},{8,9},{9,8},{10,11... | collective-permute-start | bytes 1179656 | tf_op jit(solution)/shard_map/ppermute | solution.py:309
  44.7 7.5 %collective-permute-start.18 = (bf16[192,512]{1,0:T(8,128)(2,1)S(1)}, bf16[192,512]{1,0:T(8,128)(2,1)S(1)}, u32[]{:S(2)}, u32[]{:S(2)}) collective-permute-start(bf16[192,512]{1,0:T(8,128)(2,1)S(1)} %fusion.10.refs_1_), channel_id=1, source_target_pairs={{0,2},{2,0},{4,6},{6,4},{8,10},{10,8},{12,14},{14,12},{1,3},{3,1},... | collective-permute-start | bytes 589832 | tf_op jit(solution)/shard_map/ppermute | solution.py:314
  46.9 17.2 %collective-permute-start.24 = (bf16[192,512]{1,0:T(8,128)(2,1)S(1)}, bf16[192,512]{1,0:T(8,128)(2,1)S(1)}, u32[]{:S(2)}, u32[]{:S(2)}) collective-permute-start(bf16[192,512]{1,0:T(8,128)(2,1)S(1)} %fusion.1), channel_id=1, source_target_pairs={{0,8},{2,10},{4,12},{6,14},{8,0},{10,2},{12,4},{14,6},{1,9},{3,11}... | collective-permute-start | bytes 589832 | tf_op jit(solution)/shard_map/ppermute | solution.py:319
  49.1 8.1 %collective-permute-start.21 = (bf16[192,512]{1,0:T(8,128)(2,1)S(1)}, bf16[192,512]{1,0:T(8,128)(2,1)S(1)}, u32[]{:S(2)}, u32[]{:S(2)}) collective-permute-start(bf16[192,512]{1,0:T(8,128)(2,1)S(1)} %after.15), channel_id=1, source_target_pairs={{0,2},{2,0},{4,6},{6,4},{8,10},{10,8},{12,14},{14,12},{1,3},{3,1},... | collective-permute-start | bytes 589832 | tf_op jit(solution)/shard_map/ppermute | solution.py:314
  52.2 14.8 %collective-permute-start.25 = (bf16[192,512]{1,0:T(8,128)(2,1)S(1)}, bf16[192,512]{1,0:T(8,128)(2,1)S(1)}, u32[]{:S(2)}, u32[]{:S(2)}) collective-permute-start(bf16[192,512]{1,0:T(8,128)(2,1)S(1)} %fusion.5.refs_1_), channel_id=1, source_target_pairs={{0,12},{2,14},{4,8},{6,10},{8,4},{10,6},{12,0},{14,2},{1,13},{3,15... | collective-permute-start | bytes 589832 | tf_op jit(solution)/shard_map/ppermute | solution.py:319
  56.5 5.7 %collective-permute-start.19 = (bf16[192,512]{1,0:T(8,128)(2,1)S(1)}, bf16[192,512]{1,0:T(8,128)(2,1)S(1)}, u32[]{:S(2)}, u32[]{:S(2)}) collective-permute-start(bf16[192,512]{1,0:T(8,128)(2,1)S(1)} %after.14), channel_id=1, source_target_pairs={{0,2},{2,0},{4,6},{6,4},{8,10},{10,8},{12,14},{14,12},{1,3},{3,1},... | collective-permute-start | bytes 589832 | tf_op jit(solution)/shard_map/ppermute | solution.py:314
  57.3 9.7 %collective-permute-start.22 = (bf16[192,512]{1,0:T(8,128)(2,1)S(1)}, bf16[192,512]{1,0:T(8,128)(2,1)S(1)}, u32[]{:S(2)}, u32[]{:S(2)}) collective-permute-start(bf16[192,512]{1,0:T(8,128)(2,1)S(1)} %fusion.3), channel_id=1, source_target_pairs={{0,4},{2,6},{4,0},{6,2},{8,12},{10,14},{12,8},{14,10},{1,5},{3,7},... | collective-permute-start | bytes 589832 | tf_op jit(solution)/shard_map/ppermute | solution.py:319
  67.5 1.4 %collective-permute-start.26 = (bf16[128,512]{1,0:T(8,128)(2,1)S(1)}, bf16[128,512]{1,0:T(8,128)(2,1)S(1)}, u32[]{:S(2)}, u32[]{:S(2)}) collective-permute-start(bf16[128,512]{1,0:T(8,128)(2,1)S(1)} %get-tuple-element.54), channel_id=1, source_target_pairs={{0,1},{1,0},{2,3},{3,2},{4,5},{5,4},{6,7},{7,6},{8,9},{9,8},{10,11... | collective-permute-start | bytes 393224 | tf_op jit(solution)/shard_map/ppermute | solution.py:309

commit v19 on v18

--- a/solution.py
+++ b/solution.py
@@ -435,10 +435,10 @@
     q = swap_owner(p)
     ps[0], qs[0] = p, q
     p = travelling[0]
+    p = after(p, near_in)
     q = swap_owner(p)
     ps[1], qs[1] = p, q
     p = travelling[1]
-    p = after(p, near_in)
     q = swap_owner(p)
     ps[2], qs[2] = p, q
     p = travelling[2]
@@ -450,16 +450,16 @@
     kept[0], moving = run(own, q2)
     boths[0], halves[0] = sums(kept[0], moving)
     p, q = ps[2], qs[2]
-    q = after(q, kept[0])
+    q = after(q, travelling[2], qs[1])
     (own,) = call(pair_kernel, "pair", both_blocks, [], [p, q])
     q2 = swap(own)
+    q2 = after(q2, kept[0])
     kept[2], moving = run(own, q2)
     boths[2], halves[2] = sums(kept[2], moving)
     p, q = ps[1], qs[1]
-    q = after(q, travelling[2])
+    q = after(q, kept[2])
     (own,) = call(pair_kernel, "pair", both_blocks, [], [p, q])
     q2 = swap(own)
-    q2 = after(q2, kept[2])
     kept[1], moving = run(own, q2)
     boths[1], halves[1] = sums(kept[1], moving)
     p, q = ps[3], qs[3]

time: 69.9 us -> 72.9 us (1.043)
  waiting for transfers between devices: 23.8 us -> 27.5 us
    ppermute x8, waiting for transfers between devices: 11.9 us -> 18.1 us  [swap_owner(): return lax.ppermute(values, 'expert', [(i, i ^ 1) for i in range(owners)])]
    ppermute x13, waiting for transfers between devices: 3.37 us -> 1.84 us  [swap(): return lax.ppermute(values, 'section', [(0, 1), (1, 0)])]
    ppermute x6, waiting for transfers between devices: 8.6 us -> 7.57 us  [exchange(): lax.ppermute(values, 'expert', [(i, i ^ 2 * offset) for i in range(owners)])]
  transfers between devices with their start and end apart: 27 -> 27, of which waited for: 14 -> 11; matrix products, arithmetic and copies ran while one was open for 1% -> 1% of each run, Pallas kernels for 17% -> 16%
where the time goes in v19:
time: 72.9 us; the launch traced here: 72.7 us
  starting transfers between devices  28.5 us (39%)
  waiting for transfers between devices  27.5 us (38%)
  Pallas kernels  15 us (21%)
  between operations  0.96 us (1%)
    ppermute x8, waiting for transfers between devices, swap_owner(): return lax.ppermute(values, 'expert', [(i, i ^ 1) for i in range(owners)])  18.1 us
    ppermute x6, starting transfers between devices, exchange(): lax.ppermute(values, 'expert', [(i, i ^ 2 * offset) for i in range(owners)])  16.2 us
    pallas_call x15, Pallas kernels, call(): pl.pallas_call(kernel, out_shape=tuple((jax.ShapeDtypeStruct(*out) for ou...  15 us
    ppermute x8, starting transfers between devices, swap_owner(): return lax.ppermute(values, 'expert', [(i, i ^ 1) for i in range(owners)])  9.13 us
    ppermute x6, waiting for transfers between devices, exchange(): lax.ppermute(values, 'expert', [(i, i ^ 2 * offset) for i in range(owners)])  7.57 us
    ppermute x13, starting transfers between devices, swap(): return lax.ppermute(values, 'section', [(0, 1), (1, 0)])  3.22 us
    ppermute x13, waiting for transfers between devices, swap(): return lax.ppermute(values, 'section', [(0, 1), (1, 0)])  1.84 us
  transfers between devices with their start and end apart: 27, of which 11 were waited for; matrix products, arithmetic and copies ran while one was open for 1% of the time, Pallas kernels for 16%

profile of v19, /device:TPU:0, one launch (start us, length us, event | category | flops | bytes accessed | tf_op | source)
XLA Modules:
  0.0 72.7 jit_solution(14253480641808372010)
XLA Ops:
  0.0 0.5 collective-permute-start
  0.5 0.1 collective-permute-start.1
  1.2 1.8 %attend_own.1 = (bf16[128,512]{1,0:T(8,128)(2,1)S(1)}, bf16[128,512]{1,0:T(8,128)(2,1)S(1)}, bf16[128,512]{1,0:T(8,128)(2,1)S(1)}) custom-call(s32[1]{0:T(128)} %bitcast.core_ref, s32[1]{0:T(128)S(6)} %copy.28.source_ref, bf16[1,128,1024]{2,1,0:T(8,128)(2,1)} %x_in.1, f32[1,1024]{1,0:T(1,128)} %bitcast.40, bf16[2,80,512]{2,1,0:T(8,128)(2,1)} %keys_in.1, ...), custom_call_target="tpu_custom_call" | custom-call | tf_op jit(solution)/shard_map/attend_own/pallas_call | solution.py:25
  2.9 0.0 collective-permute-done.keys_ref
  2.9 0.0 collective-permute-done.1.values_ref
  3.0 1.2 %attend_other.1 = (bf16[128,1024]{1,0:T(8,128)(2,1)S(1)}, bf16[128,512]{1,0:T(8,128)(2,1)S(1)}, bf16[128,512]{1,0:T(8,128)(2,1)S(1)}, f32[2,128]{1,0:T(2,128)S(1)}, s32[2,2,128]{2,1,0:T(2,128)S(1)}) custom-call(s32[1]{0:T(128)} %bitcast.core_ref, s32[1]{0:T(128)S(6)} %copy.28.source_ref, bf16[128,512]{1,0:T(8,128)(2,1)S(1)} %get-tuple-element.30.own_ref, ...), custom_call_target="tpu_custom_call" | custom-call | tf_op jit(solution)/shard_map/attend_other/pallas_call | solution.py:25
  4.2 0.5 collective-permute-start.2
  4.7 1.0 %collective-permute-done.2.other_ref = bf16[128,512]{1,0:T(8,128)(2,1)S(1)} collective-permute-done((bf16[128,512]{1,0:T(8,128)(2,1)S(1)}, bf16[128,512]{1,0:T(8,128)(2,1)S(1)}, u32[]{:S(2)}, u32[]{:S(2)}) %collective-permute-start.2) | collective-permute-done | bytes 131104 | tf_op jit(solution)/shard_map/ppermute | solution.py:309
  5.7 0.5 select.5
  6.2 2.9 %collective-permute-start.4 = (bf16[192,512]{1,0:T(8,128)(2,1)S(1)}, bf16[192,512]{1,0:T(8,128)(2,1)S(1)}, u32[]{:S(2)}, u32[]{:S(2)}) collective-permute-start(bf16[192,512]{1,0:T(8,128)(2,1)S(1)} %get-tuple-element.39.p_ref), channel_id=1, source_target_pairs={{0,2},{2,0},{4,6},{6,4},{8,10},{10,8},{12,14},{14,12},{1,3},{3,1},... | collective-permute-start | bytes 589832 | tf_op jit(solution)/shard_map/ppermute | solution.py:314
  9.2 1.6 %collective-permute-start.11 = (bf16[192,512]{1,0:T(8,128)(2,1)S(1)}, bf16[192,512]{1,0:T(8,128)(2,1)S(1)}, u32[]{:S(2)}, u32[]{:S(2)}) collective-permute-start(bf16[192,512]{1,0:T(8,128)(2,1)S(1)} %get-tuple-element.46), channel_id=1, source_target_pairs={{0,4},{2,6},{4,0},{6,2},{8,12},{10,14},{12,8},{14,10},{1,5},{3,7},... | collective-permute-start | bytes 589832 | tf_op jit(solution)/shard_map/ppermute | solution.py:319
  10.7 2.6 %collective-permute-start.9 = (bf16[192,512]{1,0:T(8,128)(2,1)S(1)}, bf16[192,512]{1,0:T(8,128)(2,1)S(1)}, u32[]{:S(2)}, u32[]{:S(2)}) collective-permute-start(bf16[192,512]{1,0:T(8,128)(2,1)S(1)} %get-tuple-element.45), channel_id=1, source_target_pairs={{0,8},{2,10},{4,12},{6,14},{8,0},{10,2},{12,4},{14,6},{1,9},{3,11}... | collective-permute-start | bytes 589832 | tf_op jit(solution)/shard_map/ppermute | solution.py:319
  13.3 1.1 %collective-permute-done.4.q_ref = bf16[192,512]{1,0:T(8,128)(2,1)S(1)} collective-permute-done((bf16[192,512]{1,0:T(8,128)(2,1)S(1)}, bf16[192,512]{1,0:T(8,128)(2,1)S(1)}, u32[]{:S(2)}, u32[]{:S(2)}) %collective-permute-start.4) | collective-permute-done | bytes 196640 | tf_op jit(solution)/shard_map/ppermute | solution.py:314
  14.4 0.1 collective-permute-start.5
  14.5 2.2 %load.1 = (bf16[1024,1024]{1,0:T(8,128)(2,1)S(1)}, bf16[1024,1024]{1,0:T(8,128)(2,1)S(1)}) custom-call(bf16[1024,1024]{1,0:T(8,128)(2,1)} %in_in.1, bf16[1024,1024]{1,0:T(8,128)(2,1)} %out_in.1), custom_call_target="tpu_custom_call" | custom-call | tf_op jit(solution)/shard_map/load/pallas_call | solution.py:25
  16.7 3.9 %collective-permute-start.7 = (bf16[192,512]{1,0:T(8,128)(2,1)S(1)}, bf16[192,512]{1,0:T(8,128)(2,1)S(1)}, u32[]{:S(2)}, u32[]{:S(2)}) collective-permute-start(bf16[192,512]{1,0:T(8,128)(2,1)S(1)} %get-tuple-element.44), channel_id=1, source_target_pairs={{0,12},{2,14},{4,8},{6,10},{8,4},{10,6},{12,0},{14,2},{1,13},{3,15... | collective-permute-start | bytes 589832 | tf_op jit(solution)/shard_map/ppermute | solution.py:319
  20.6 0.0 collective-permute-done.11.refs_0_
  20.6 1.5 %collective-permute-start.12 = (bf16[192,512]{1,0:T(8,128)(2,1)S(1)}, bf16[192,512]{1,0:T(8,128)(2,1)S(1)}, u32[]{:S(2)}, u32[]{:S(2)}) collective-permute-start(bf16[192,512]{1,0:T(8,128)(2,1)S(1)} %after.8.p_ref), channel_id=1, source_target_pairs={{0,2},{2,0},{4,6},{6,4},{8,10},{10,8},{12,14},{14,12},{1,3},{3,1},... | collective-permute-start | bytes 589832 | tf_op jit(solution)/shard_map/ppermute | solution.py:314
  22.1 4.4 %collective-permute-done.9.p_ref = bf16[192,512]{1,0:T(8,128)(2,1)S(1)} collective-permute-done((bf16[192,512]{1,0:T(8,128)(2,1)S(1)}, bf16[192,512]{1,0:T(8,128)(2,1)S(1)}, u32[]{:S(2)}, u32[]{:S(2)}) %collective-permute-start.9) | collective-permute-done | bytes 196640 | tf_op jit(solution)/shard_map/ppermute | solution.py:319
  26.6 0.0 collective-permute-start.10
  26.6 0.0 collective-permute-done.7.refs_1_.p_ref
  26.6 1.8 %collective-permute-done.12.refs_2_.refs_0_ = bf16[192,512]{1,0:T(8,128)(2,1)S(1)} collective-permute-done((bf16[192,512]{1,0:T(8,128)(2,1)S(1)}, bf16[192,512]{1,0:T(8,128)(2,1)S(1)}, u32[]{:S(2)}, u32[]{:S(2)}) %collective-permute-start.12) | collective-permute-done | bytes 196640 | tf_op jit(solution)/shard_map/ppermute | solution.py:314
  28.4 3.9 %collective-permute-done.10.refs_0_ = bf16[192,512]{1,0:T(8,128)(2,1)S(1)} collective-permute-done((bf16[192,512]{1,0:T(8,128)(2,1)S(1)}, bf16[192,512]{1,0:T(8,128)(2,1)S(1)}, u32[]{:S(2)}, u32[]{:S(2)}) %collective-permute-start.10) | collective-permute-done | bytes 196640 | tf_op jit(solution)/shard_map/ppermute | solution.py:314
  32.3 0.1 collective-permute-start.13
  32.4 0.0 collective-permute-done.5.pair2_ref
  32.4 1.8 %expert.4 = (f32[2,192,512]{2,1,0:T(8,128)S(1)}, bf16[2,192,512]{2,1,0:T(8,128)(2,1)S(1)}) custom-call(s32[1]{0:T(128)} %bitcast.core_ref, bf16[384,512]{1,0:T(8,128)(2,1)S(1)} %pair.4.pair_ref, bf16[384,512]{1,0:T(8,128)(2,1)S(1)} %collective-permute-done.5.pair2_ref, bf16[1024,1024]{1,0:T(8,128)(2,1)S(1)} %get-tuple-element.40.in_ref.refs_1_, ...), custom_call_target="tpu_custom_call" | custom-call | tf_op jit(solution)/shard_map/expert/pallas_call | solution.py:25
  34.2 0.6 collective-permute-start.6
  34.8 1.1 %collective-permute-start.8 = (bf16[192,512]{1,0:T(8,128)(2,1)S(1)}, bf16[192,512]{1,0:T(8,128)(2,1)S(1)}, u32[]{:S(2)}, u32[]{:S(2)}) collective-permute-start(bf16[192,512]{1,0:T(8,128)(2,1)S(1)} %collective-permute-done.7.refs_1_.p_ref), channel_id=1, source_target_pairs={{0,2},{2,0},{4,6},{6,4},{8,10},{10,8},{12,14},{14,12},{1,3},{3,1},... | collective-permute-start | bytes 589832 | tf_op jit(solution)/shard_map/ppermute | solution.py:314
  35.9 0.0 collective-permute-done.13.refs_0_
  35.9 1.8 %expert.5 = (f32[2,192,512]{2,1,0:T(8,128)S(1)}, bf16[2,192,512]{2,1,0:T(8,128)(2,1)S(1)}) custom-call(s32[1]{0:T(128)} %bitcast.core_ref, bf16[384,512]{1,0:T(8,128)(2,1)S(1)} %pair.5.pair_ref, bf16[384,512]{1,0:T(8,128)(2,1)S(1)} %after.10.pair2_ref, bf16[1024,1024]{1,0:T(8,128)(2,1)S(1)} %get-tuple-element.40.in_ref.refs_1_, ...), custom_call_target="tpu_custom_call" | custom-call | tf_op jit(solution)/shard_map/expert/pallas_call | solution.py:25
  37.7 0.1 collective-permute-start.16
  37.8 0.5 collective-permute-start.3
  38.4 0.1 collective-permute-start.15
  38.5 3.2 %collective-permute-done.8.refs_0_ = bf16[192,512]{1,0:T(8,128)(2,1)S(1)} collective-permute-done((bf16[192,512]{1,0:T(8,128)(2,1)S(1)}, bf16[192,512]{1,0:T(8,128)(2,1)S(1)}, u32[]{:S(2)}, u32[]{:S(2)}) %collective-permute-start.8) | collective-permute-done | bytes 196640 | tf_op jit(solution)/shard_map/ppermute | solution.py:314
  41.7 0.1 collective-permute-start.14
  41.8 0.0 collective-permute-done.6
  41.8 0.1 convert_add_fusion.3
  41.9 0.0 collective-permute-done.16
  41.9 0.1 convert_add_fusion.2
  42.1 1.2 %collective-permute-start.23 = (bf16[192,512]{1,0:T(8,128)(2,1)S(1)}, bf16[192,512]{1,0:T(8,128)(2,1)S(1)}, u32[]{:S(2)}, u32[]{:S(2)}) collective-permute-start(bf16[192,512]{1,0:T(8,128)(2,1)S(1)} %fusion.9.refs_2_), channel_id=1, source_target_pairs={{0,2},{2,0},{4,6},{6,4},{8,10},{10,8},{12,14},{14,12},{1,3},{3,1},... | collective-permute-start | bytes 589832 | tf_op jit(solution)/shard_map/ppermute | solution.py:314
  43.2 0.0 collective-permute-done.15.pair2_ref
  43.3 1.8 %expert.6 = (f32[2,192,512]{2,1,0:T(8,128)S(1)}, bf16[2,192,512]{2,1,0:T(8,128)(2,1)S(1)}) custom-call(s32[1]{0:T(128)} %bitcast.core_ref, bf16[384,512]{1,0:T(8,128)(2,1)S(1)} %pair.7.pair_ref, bf16[384,512]{1,0:T(8,128)(2,1)S(1)} %collective-permute-done.15.pair2_ref, bf16[1024,1024]{1,0:T(8,128)(2,1)S(1)} %get-tuple-element.40.in_ref.refs_1_, ...), custom_call_target="tpu_custom_call" | custom-call | tf_op jit(solution)/shard_map/expert/pallas_call | solution.py:25
  45.1 1.8 %expert.7 = (f32[2,192,512]{2,1,0:T(8,128)S(1)}, bf16[2,192,512]{2,1,0:T(8,128)(2,1)S(1)}) custom-call(s32[1]{0:T(128)} %bitcast.core_ref, bf16[384,512]{1,0:T(8,128)(2,1)S(1)} %pair.6.pair_ref, bf16[384,512]{1,0:T(8,128)(2,1)S(1)} %after.13.pair2_ref, bf16[1024,1024]{1,0:T(8,128)(2,1)S(1)} %get-tuple-element.40.in_ref.refs_1_, ...), custom_call_target="tpu_custom_call" | custom-call | tf_op jit(solution)/shard_map/expert/pallas_call | solution.py:25
  47.0 0.3 collective-permute-start.17
  47.3 0.4 collective-permute-start.20
  47.6 1.8 %collective-permute-done.23 = bf16[192,512]{1,0:T(8,128)(2,1)S(1)} collective-permute-done((bf16[192,512]{1,0:T(8,128)(2,1)S(1)}, bf16[192,512]{1,0:T(8,128)(2,1)S(1)}, u32[]{:S(2)}, u32[]{:S(2)}) %collective-permute-start.23) | collective-permute-done | bytes 196640 | tf_op jit(solution)/shard_map/ppermute | solution.py:314
  49.5 0.1 collective-permute-start.24
  49.6 0.0 collective-permute-done.17
  49.6 0.1 convert_add_fusion.1
  49.7 1.2 %collective-permute-start.18 = (bf16[192,512]{1,0:T(8,128)(2,1)S(1)}, bf16[192,512]{1,0:T(8,128)(2,1)S(1)}, u32[]{:S(2)}, u32[]{:S(2)}) collective-permute-start(bf16[192,512]{1,0:T(8,128)(2,1)S(1)} %fusion.10.refs_1_), channel_id=1, source_target_pairs={{0,2},{2,0},{4,6},{6,4},{8,10},{10,8},{12,14},{14,12},{1,3},{3,1},... | collective-permute-start | bytes 589832 | tf_op jit(solution)/shard_map/ppermute | solution.py:314
  50.9 0.1 convert_add_fusion
  51.1 1.0 %collective-permute-start.21 = (bf16[192,512]{1,0:T(8,128)(2,1)S(1)}, bf16[192,512]{1,0:T(8,128)(2,1)S(1)}, u32[]{:S(2)}, u32[]{:S(2)}) collective-permute-start(bf16[192,512]{1,0:T(8,128)(2,1)S(1)} %after.15), channel_id=1, source_target_pairs={{0,2},{2,0},{4,6},{6,4},{8,10},{10,8},{12,14},{14,12},{1,3},{3,1},... | collective-permute-start | bytes 589832 | tf_op jit(solution)/shard_map/ppermute | solution.py:314
  52.1 5.6 %collective-permute-done.18 = bf16[192,512]{1,0:T(8,128)(2,1)S(1)} collective-permute-done((bf16[192,512]{1,0:T(8,128)(2,1)S(1)}, bf16[192,512]{1,0:T(8,128)(2,1)S(1)}, u32[]{:S(2)}, u32[]{:S(2)}) %collective-permute-start.18) | collective-permute-done | bytes 196640 | tf_op jit(solution)/shard_map/ppermute | solution.py:314
  57.7 3.5 %collective-permute-start.25 = (bf16[192,512]{1,0:T(8,128)(2,1)S(1)}, bf16[192,512]{1,0:T(8,128)(2,1)S(1)}, u32[]{:S(2)}, u32[]{:S(2)}) collective-permute-start(bf16[192,512]{1,0:T(8,128)(2,1)S(1)} %fusion.5.refs_1_), channel_id=1, source_target_pairs={{0,12},{2,14},{4,8},{6,10},{8,4},{10,6},{12,0},{14,2},{1,13},{3,15... | collective-permute-start | bytes 589832 | tf_op jit(solution)/shard_map/ppermute | solution.py:319
  61.2 0.2 collective-permute-start.19
  61.5 4.5 %collective-permute-start.22 = (bf16[192,512]{1,0:T(8,128)(2,1)S(1)}, bf16[192,512]{1,0:T(8,128)(2,1)S(1)}, u32[]{:S(2)}, u32[]{:S(2)}) collective-permute-start(bf16[192,512]{1,0:T(8,128)(2,1)S(1)} %fusion.3), channel_id=1, source_target_pairs={{0,4},{2,6},{4,0},{6,2},{8,12},{10,14},{12,8},{14,10},{1,5},{3,7},... | collective-permute-start | bytes 589832 | tf_op jit(solution)/shard_map/ppermute | solution.py:319
  66.0 0.9 %collective-permute-done.19 = bf16[192,512]{1,0:T(8,128)(2,1)S(1)} collective-permute-done((bf16[192,512]{1,0:T(8,128)(2,1)S(1)}, bf16[192,512]{1,0:T(8,128)(2,1)S(1)}, u32[]{:S(2)}, u32[]{:S(2)}) %collective-permute-start.19) | collective-permute-done | bytes 196640 | tf_op jit(solution)/shard_map/ppermute | solution.py:314
  66.9 0.0 collective-permute-done.24.rest_2_
  66.9 3.1 %collective-permute-done.22.rest_1_ = bf16[192,512]{1,0:T(8,128)(2,1)S(1)} collective-permute-done((bf16[192,512]{1,0:T(8,128)(2,1)S(1)}, bf16[192,512]{1,0:T(8,128)(2,1)S(1)}, u32[]{:S(2)}, u32[]{:S(2)}) %collective-permute-start.22) | collective-permute-done | bytes 196640 | tf_op jit(solution)/shard_map/ppermute | solution.py:319
  70.0 0.5 combine_other.1
  70.5 0.1 collective-permute-start.26
  70.6 0.5 combine_own.1.own_ref
  71.1 0.8 %collective-permute-done.26.other_ref = bf16[128,512]{1,0:T(8,128)(2,1)S(1)} collective-permute-done((bf16[128,512]{1,0:T(8,128)(2,1)S(1)}, bf16[128,512]{1,0:T(8,128)(2,1)S(1)}, u32[]{:S(2)}, u32[]{:S(2)}) %collective-permute-start.26) | collective-permute-done | bytes 131104 | tf_op jit(solution)/shard_map/ppermute | solution.py:309
  71.9 0.7 %finish.1 = bf16[128,1024]{1,0:T(8,128)(2,1)} custom-call(s32[1]{0:T(128)} %bitcast.core_ref, bf16[128,1024]{1,0:T(8,128)(2,1)S(1)} %get-tuple-element.33.state_ref, bf16[128,512]{1,0:T(8,128)(2,1)S(1)} %combine_own.1.own_ref, bf16[128,512]{1,0:T(8,128)(2,1)S(1)} %collective-permute-done.26.other_ref), custom_call_target="tpu_custom_call" | custom-call | tf_op jit(solution)/shard_map/finish/pallas_call | solution.py:25
  (25 shorter events, 0.4 us)
Async XLA Ops:
  0.0 2.9 %collective-permute-start = (bf16[2,80,512]{2,1,0:T(8,128)(2,1)}, bf16[2,80,512]{2,1,0:T(8,128)(2,1)S(1)}, u32[]{:S(2)}, u32[]{:S(2)}) collective-permute-start(bf16[2,80,512]{2,1,0:T(8,128)(2,1)} %keys_in.1), channel_id=1, source_target_pairs={{0,1},{1,0},{2,3},{3,2},{4,5},{5,4},{6,7},{7,6},{8,9},{9,8},{10,11... | collective-permute-start | bytes 491528 | tf_op jit(solution)/shard_map/ppermute | solution.py:309
  0.5 2.5 %collective-permute-start.1 = (bf16[2,80,512]{2,1,0:T(8,128)(2,1)}, bf16[2,80,512]{2,1,0:T(8,128)(2,1)S(1)}, u32[]{:S(2)}, u32[]{:S(2)}) collective-permute-start(bf16[2,80,512]{2,1,0:T(8,128)(2,1)} %values_in.1), channel_id=1, source_target_pairs={{0,1},{1,0},{2,3},{3,2},{4,5},{5,4},{6,7},{7,6},{8,9},{9,8},{10,11... | collective-permute-start | bytes 491528 | tf_op jit(solution)/shard_map/ppermute | solution.py:309
  4.2 1.5 %collective-permute-start.2 = (bf16[128,512]{1,0:T(8,128)(2,1)S(1)}, bf16[128,512]{1,0:T(8,128)(2,1)S(1)}, u32[]{:S(2)}, u32[]{:S(2)}) collective-permute-start(bf16[128,512]{1,0:T(8,128)(2,1)S(1)} %get-tuple-element.37), channel_id=1, source_target_pairs={{0,1},{1,0},{2,3},{3,2},{4,5},{5,4},{6,7},{7,6},{8,9},{9,8},{10,11... | collective-permute-start | bytes 393224 | tf_op jit(solution)/shard_map/ppermute | solution.py:309
  6.2 8.1 %collective-permute-start.4 = (bf16[192,512]{1,0:T(8,128)(2,1)S(1)}, bf16[192,512]{1,0:T(8,128)(2,1)S(1)}, u32[]{:S(2)}, u32[]{:S(2)}) collective-permute-start(bf16[192,512]{1,0:T(8,128)(2,1)S(1)} %get-tuple-element.39.p_ref), channel_id=1, source_target_pairs={{0,2},{2,0},{4,6},{6,4},{8,10},{10,8},{12,14},{14,12},{1,3},{3,1},... | collective-permute-start | bytes 589832 | tf_op jit(solution)/shard_map/ppermute | solution.py:314
  9.2 11.5 %collective-permute-start.11 = (bf16[192,512]{1,0:T(8,128)(2,1)S(1)}, bf16[192,512]{1,0:T(8,128)(2,1)S(1)}, u32[]{:S(2)}, u32[]{:S(2)}) collective-permute-start(bf16[192,512]{1,0:T(8,128)(2,1)S(1)} %get-tuple-element.46), channel_id=1, source_target_pairs={{0,4},{2,6},{4,0},{6,2},{8,12},{10,14},{12,8},{14,10},{1,5},{3,7},... | collective-permute-start | bytes 589832 | tf_op jit(solution)/shard_map/ppermute | solution.py:319
  10.7 15.8 %collective-permute-start.9 = (bf16[192,512]{1,0:T(8,128)(2,1)S(1)}, bf16[192,512]{1,0:T(8,128)(2,1)S(1)}, u32[]{:S(2)}, u32[]{:S(2)}) collective-permute-start(bf16[192,512]{1,0:T(8,128)(2,1)S(1)} %get-tuple-element.45), channel_id=1, source_target_pairs={{0,8},{2,10},{4,12},{6,14},{8,0},{10,2},{12,4},{14,6},{1,9},{3,11}... | collective-permute-start | bytes 589832 | tf_op jit(solution)/shard_map/ppermute | solution.py:319
  14.4 17.9 %collective-permute-start.5 = (bf16[384,512]{1,0:T(8,128)(2,1)S(1)}, bf16[384,512]{1,0:T(8,128)(2,1)S(1)}, u32[]{:S(2)}, u32[]{:S(2)}) collective-permute-start(bf16[384,512]{1,0:T(8,128)(2,1)S(1)} %pair.4.pair_ref), channel_id=1, source_target_pairs={{0,1},{1,0},{2,3},{3,2},{4,5},{5,4},{6,7},{7,6},{8,9},{9,8},{10,11... | collective-permute-start | bytes 1179656 | tf_op jit(solution)/shard_map/ppermute | solution.py:309
  16.7 9.8 %collective-permute-start.7 = (bf16[192,512]{1,0:T(8,128)(2,1)S(1)}, bf16[192,512]{1,0:T(8,128)(2,1)S(1)}, u32[]{:S(2)}, u32[]{:S(2)}) collective-permute-start(bf16[192,512]{1,0:T(8,128)(2,1)S(1)} %get-tuple-element.44), channel_id=1, source_target_pairs={{0,12},{2,14},{4,8},{6,10},{8,4},{10,6},{12,0},{14,2},{1,13},{3,15... | collective-permute-start | bytes 589832 | tf_op jit(solution)/shard_map/ppermute | solution.py:319
  20.6 7.7 %collective-permute-start.12 = (bf16[192,512]{1,0:T(8,128)(2,1)S(1)}, bf16[192,512]{1,0:T(8,128)(2,1)S(1)}, u32[]{:S(2)}, u32[]{:S(2)}) collective-permute-start(bf16[192,512]{1,0:T(8,128)(2,1)S(1)} %after.8.p_ref), channel_id=1, source_target_pairs={{0,2},{2,0},{4,6},{6,4},{8,10},{10,8},{12,14},{14,12},{1,3},{3,1},... | collective-permute-start | bytes 589832 | tf_op jit(solution)/shard_map/ppermute | solution.py:314
  26.6 5.7 %collective-permute-start.10 = (bf16[192,512]{1,0:T(8,128)(2,1)S(1)}, bf16[192,512]{1,0:T(8,128)(2,1)S(1)}, u32[]{:S(2)}, u32[]{:S(2)}) collective-permute-start(bf16[192,512]{1,0:T(8,128)(2,1)S(1)} %collective-permute-done.9.p_ref), channel_id=1, source_target_pairs={{0,2},{2,0},{4,6},{6,4},{8,10},{10,8},{12,14},{14,12},{1,3},{3,1},... | collective-permute-start | bytes 589832 | tf_op jit(solution)/shard_map/ppermute | solution.py:314
  32.3 3.6 %collective-permute-start.13 = (bf16[384,512]{1,0:T(8,128)(2,1)S(1)}, bf16[384,512]{1,0:T(8,128)(2,1)S(1)}, u32[]{:S(2)}, u32[]{:S(2)}) collective-permute-start(bf16[384,512]{1,0:T(8,128)(2,1)S(1)} %pair.5.pair_ref), channel_id=1, source_target_pairs={{0,1},{1,0},{2,3},{3,2},{4,5},{5,4},{6,7},{7,6},{8,9},{9,8},{10,11... | collective-permute-start | bytes 1179656 | tf_op jit(solution)/shard_map/ppermute | solution.py:309
  34.2 7.6 %collective-permute-start.6 = (bf16[2,192,512]{2,1,0:T(8,128)(2,1)S(1)}, bf16[2,192,512]{2,1,0:T(8,128)(2,1)S(1)}, u32[]{:S(2)}, u32[]{:S(2)}) collective-permute-start(bf16[2,192,512]{2,1,0:T(8,128)(2,1)S(1)} %get-tuple-element.43), channel_id=1, source_target_pairs={{0,1},{1,0},{2,3},{3,2},{4,5},{5,4},{6,7},{7,6},{8,9},{9,8},{10,11... | collective-permute-start | bytes 1179656 | tf_op jit(solution)/shard_map/ppermute | solution.py:309
  34.8 6.9 %collective-permute-start.8 = (bf16[192,512]{1,0:T(8,128)(2,1)S(1)}, bf16[192,512]{1,0:T(8,128)(2,1)S(1)}, u32[]{:S(2)}, u32[]{:S(2)}) collective-permute-start(bf16[192,512]{1,0:T(8,128)(2,1)S(1)} %collective-permute-done.7.refs_1_.p_ref), channel_id=1, source_target_pairs={{0,2},{2,0},{4,6},{6,4},{8,10},{10,8},{12,14},{14,12},{1,3},{3,1},... | collective-permute-start | bytes 589832 | tf_op jit(solution)/shard_map/ppermute | solution.py:314
  37.7 4.2 %collective-permute-start.16 = (bf16[2,192,512]{2,1,0:T(8,128)(2,1)S(1)}, bf16[2,192,512]{2,1,0:T(8,128)(2,1)S(1)}, u32[]{:S(2)}, u32[]{:S(2)}) collective-permute-start(bf16[2,192,512]{2,1,0:T(8,128)(2,1)S(1)} %get-tuple-element.49), channel_id=1, source_target_pairs={{0,1},{1,0},{2,3},{3,2},{4,5},{5,4},{6,7},{7,6},{8,9},{9,8},{10,11... | collective-permute-start | bytes 1179656 | tf_op jit(solution)/shard_map/ppermute | solution.py:309
  37.8 29.1 %collective-permute-start.3 = (f32[2,128]{1,0:T(2,128)S(1)}, f32[2,128]{1,0:T(2,128)S(1)}, u32[]{:S(2)}, u32[]{:S(2)}) collective-permute-start(f32[2,128]{1,0:T(2,128)S(1)} %get-tuple-element.35.gates_ref), channel_id=1, source_target_pairs={{0,1},{1,0},{2,3},{3,2},{4,5},{5,4},{6,7},{7,6},{8,9},{9,8},{10,11... | collective-permute-start | bytes 3080 | tf_op jit(solution)/shard_map/ppermute | solution.py:309
  38.4 4.9 %collective-permute-start.15 = (bf16[384,512]{1,0:T(8,128)(2,1)S(1)}, bf16[384,512]{1,0:T(8,128)(2,1)S(1)}, u32[]{:S(2)}, u32[]{:S(2)}) collective-permute-start(bf16[384,512]{1,0:T(8,128)(2,1)S(1)} %pair.7.pair_ref), channel_id=1, source_target_pairs={{0,1},{1,0},{2,3},{3,2},{4,5},{5,4},{6,7},{7,6},{8,9},{9,8},{10,11... | collective-permute-start | bytes 1179656 | tf_op jit(solution)/shard_map/ppermute | solution.py:309
  41.7 3.4 %collective-permute-start.14 = (bf16[384,512]{1,0:T(8,128)(2,1)S(1)}, bf16[384,512]{1,0:T(8,128)(2,1)S(1)}, u32[]{:S(2)}, u32[]{:S(2)}) collective-permute-start(bf16[384,512]{1,0:T(8,128)(2,1)S(1)} %pair.6.pair_ref), channel_id=1, source_target_pairs={{0,1},{1,0},{2,3},{3,2},{4,5},{5,4},{6,7},{7,6},{8,9},{9,8},{10,11... | collective-permute-start | bytes 1179656 | tf_op jit(solution)/shard_map/ppermute | solution.py:309
  42.1 7.4 %collective-permute-start.23 = (bf16[192,512]{1,0:T(8,128)(2,1)S(1)}, bf16[192,512]{1,0:T(8,128)(2,1)S(1)}, u32[]{:S(2)}, u32[]{:S(2)}) collective-permute-start(bf16[192,512]{1,0:T(8,128)(2,1)S(1)} %fusion.9.refs_2_), channel_id=1, source_target_pairs={{0,2},{2,0},{4,6},{6,4},{8,10},{10,8},{12,14},{14,12},{1,3},{3,1},... | collective-permute-start | bytes 589832 | tf_op jit(solution)/shard_map/ppermute | solution.py:314
  47.0 2.6 %collective-permute-start.17 = (bf16[2,192,512]{2,1,0:T(8,128)(2,1)S(1)}, bf16[2,192,512]{2,1,0:T(8,128)(2,1)S(1)}, u32[]{:S(2)}, u32[]{:S(2)}) collective-permute-start(bf16[2,192,512]{2,1,0:T(8,128)(2,1)S(1)} %get-tuple-element.51), channel_id=1, source_target_pairs={{0,1},{1,0},{2,3},{3,2},{4,5},{5,4},{6,7},{7,6},{8,9},{9,8},{10,11... | collective-permute-start | bytes 1179656 | tf_op jit(solution)/shard_map/ppermute | solution.py:309
  47.3 3.6 %collective-permute-start.20 = (bf16[2,192,512]{2,1,0:T(8,128)(2,1)S(1)}, bf16[2,192,512]{2,1,0:T(8,128)(2,1)S(1)}, u32[]{:S(2)}, u32[]{:S(2)}) collective-permute-start(bf16[2,192,512]{2,1,0:T(8,128)(2,1)S(1)} %get-tuple-element.52), channel_id=1, source_target_pairs={{0,1},{1,0},{2,3},{3,2},{4,5},{5,4},{6,7},{7,6},{8,9},{9,8},{10,11... | collective-permute-start | bytes 1179656 | tf_op jit(solution)/shard_map/ppermute | solution.py:309
  49.5 17.4 %collective-permute-start.24 = (bf16[192,512]{1,0:T(8,128)(2,1)S(1)}, bf16[192,512]{1,0:T(8,128)(2,1)S(1)}, u32[]{:S(2)}, u32[]{:S(2)}) collective-permute-start(bf16[192,512]{1,0:T(8,128)(2,1)S(1)} %fusion.1), channel_id=1, source_target_pairs={{0,8},{2,10},{4,12},{6,14},{8,0},{10,2},{12,4},{14,6},{1,9},{3,11}... | collective-permute-start | bytes 589832 | tf_op jit(solution)/shard_map/ppermute | solution.py:319
  49.7 7.9 %collective-permute-start.18 = (bf16[192,512]{1,0:T(8,128)(2,1)S(1)}, bf16[192,512]{1,0:T(8,128)(2,1)S(1)}, u32[]{:S(2)}, u32[]{:S(2)}) collective-permute-start(bf16[192,512]{1,0:T(8,128)(2,1)S(1)} %fusion.10.refs_1_), channel_id=1, source_target_pairs={{0,2},{2,0},{4,6},{6,4},{8,10},{10,8},{12,14},{14,12},{1,3},{3,1},... | collective-permute-start | bytes 589832 | tf_op jit(solution)/shard_map/ppermute | solution.py:314
  51.1 10.3 %collective-permute-start.21 = (bf16[192,512]{1,0:T(8,128)(2,1)S(1)}, bf16[192,512]{1,0:T(8,128)(2,1)S(1)}, u32[]{:S(2)}, u32[]{:S(2)}) collective-permute-start(bf16[192,512]{1,0:T(8,128)(2,1)S(1)} %after.15), channel_id=1, source_target_pairs={{0,2},{2,0},{4,6},{6,4},{8,10},{10,8},{12,14},{14,12},{1,3},{3,1},... | collective-permute-start | bytes 589832 | tf_op jit(solution)/shard_map/ppermute | solution.py:314
  57.7 12.4 %collective-permute-start.25 = (bf16[192,512]{1,0:T(8,128)(2,1)S(1)}, bf16[192,512]{1,0:T(8,128)(2,1)S(1)}, u32[]{:S(2)}, u32[]{:S(2)}) collective-permute-start(bf16[192,512]{1,0:T(8,128)(2,1)S(1)} %fusion.5.refs_1_), channel_id=1, source_target_pairs={{0,12},{2,14},{4,8},{6,10},{8,4},{10,6},{12,0},{14,2},{1,13},{3,15... | collective-permute-start | bytes 589832 | tf_op jit(solution)/shard_map/ppermute | solution.py:319
  61.2 5.7 %collective-permute-start.19 = (bf16[192,512]{1,0:T(8,128)(2,1)S(1)}, bf16[192,512]{1,0:T(8,128)(2,1)S(1)}, u32[]{:S(2)}, u32[]{:S(2)}) collective-permute-start(bf16[192,512]{1,0:T(8,128)(2,1)S(1)} %after.14), channel_id=1, source_target_pairs={{0,2},{2,0},{4,6},{6,4},{8,10},{10,8},{12,14},{14,12},{1,3},{3,1},... | collective-permute-start | bytes 589832 | tf_op jit(solution)/shard_map/ppermute | solution.py:314
  61.5 8.6 %collective-permute-start.22 = (bf16[192,512]{1,0:T(8,128)(2,1)S(1)}, bf16[192,512]{1,0:T(8,128)(2,1)S(1)}, u32[]{:S(2)}, u32[]{:S(2)}) collective-permute-start(bf16[192,512]{1,0:T(8,128)(2,1)S(1)} %fusion.3), channel_id=1, source_target_pairs={{0,4},{2,6},{4,0},{6,2},{8,12},{10,14},{12,8},{14,10},{1,5},{3,7},... | collective-permute-start | bytes 589832 | tf_op jit(solution)/shard_map/ppermute | solution.py:319
  70.5 1.4 %collective-permute-start.26 = (bf16[128,512]{1,0:T(8,128)(2,1)S(1)}, bf16[128,512]{1,0:T(8,128)(2,1)S(1)}, u32[]{:S(2)}, u32[]{:S(2)}) collective-permute-start(bf16[128,512]{1,0:T(8,128)(2,1)S(1)} %get-tuple-element.54), channel_id=1, source_target_pairs={{0,1},{1,0},{2,3},{3,2},{4,5},{5,4},{6,7},{7,6},{8,9},{9,8},{10,11... | collective-permute-start | bytes 393224 | tf_op jit(solution)/shard_map/ppermute | solution.py:309

commit v20 on v17

--- a/solution.py
+++ b/solution.py
@@ -443,19 +443,19 @@
     p2, q2 = swap(p), swap(q)
     kept[0], moving = run(p, q, p2, q2)
     boths[0], halves[0] = sums(kept[0], moving)
+    p, q = ps[1], qs[1]
+    p2, q2 = swap(p), swap(q)
+    kept[1], moving = run(p, q, p2, q2)
+    boths[1], halves[1] = sums(kept[1], moving)
     p, q = ps[2], qs[2]
     p2, q2 = swap(p), swap(q)
+    q2 = after(q2, kept[0], kept[1])
     kept[2], moving = run(p, q, p2, q2)
     boths[2], halves[2] = sums(kept[2], moving)
-    p, q = ps[1], qs[1]
-    p2, q2 = swap(p), swap(q)
-    q2 = after(q2, kept[0], kept[2])
-    kept[1], moving = run(p, q, p2, q2)
-    boths[1], halves[1] = sums(kept[1], moving)
     p, q = ps[3], qs[3]
     q = after(q, kept[2])
     p2, q2 = swap(p), swap(q)
-    q2 = after(q2, halves[2], kept[1])
+    q2 = after(q2, halves[2])
     kept[3], moving = run(p, q, p2, q2)
     boths[3], halves[3] = sums(kept[3], moving)
     leaving = halves[2]

time: 68.9 us -> 68.3 us (level)
  starting transfers between devices: 29.6 us -> 28.6 us
    ppermute x6, waiting for transfers between devices: 8.22 us -> 11.5 us  [exchange(): lax.ppermute(values, 'expert', [(i, i ^ 2 * offset) for i in range(owners)])]
    ppermute x8, waiting for transfers between devices: 10.8 us -> 8.15 us  [swap_owner(): return lax.ppermute(values, 'expert', [(i, i ^ 1) for i in range(owners)])]
    ppermute x6, starting transfers between devices: 16.8 us -> 14.7 us  [exchange(): lax.ppermute(values, 'expert', [(i, i ^ 2 * offset) for i in range(owners)])]
    ppermute x8, starting transfers between devices: 9.14 us -> 10.7 us  [swap_owner(): return lax.ppermute(values, 'expert', [(i, i ^ 1) for i in range(owners)])]
where the time goes in v20:
time: 68.3 us; the launch traced here: 68.1 us
  starting transfers between devices  28.6 us (42%)
  waiting for transfers between devices  23 us (34%)
  Pallas kernels  14.9 us (22%)
  between operations  0.9 us (1%)
    pallas_call x11, Pallas kernels, call(): pl.pallas_call(kernel, out_shape=tuple((jax.ShapeDtypeStruct(*out) for ou...  14.9 us
    ppermute x6, starting transfers between devices, exchange(): lax.ppermute(values, 'expert', [(i, i ^ 2 * offset) for i in range(owners)])  14.7 us
    ppermute x6, waiting for transfers between devices, exchange(): lax.ppermute(values, 'expert', [(i, i ^ 2 * offset) for i in range(owners)])  11.5 us
    ppermute x8, starting transfers between devices, swap_owner(): return lax.ppermute(values, 'expert', [(i, i ^ 1) for i in range(owners)])  10.7 us
    ppermute x8, waiting for transfers between devices, swap_owner(): return lax.ppermute(values, 'expert', [(i, i ^ 1) for i in range(owners)])  8.15 us
    ppermute x17, waiting for transfers between devices, swap(): return lax.ppermute(values, 'section', [(0, 1), (1, 0)])  3.39 us
    ppermute x17, starting transfers between devices, swap(): return lax.ppermute(values, 'section', [(0, 1), (1, 0)])  3.22 us
  transfers between devices with their start and end apart: 31, of which 14 were waited for; matrix products, arithmetic and copies ran while one was open for 1% of the time, Pallas kernels for 17%

profile of v20, /device:TPU:0, one launch (start us, length us, event | category | flops | bytes accessed | tf_op | source)
XLA Modules:
  0.0 68.1 jit_solution(15960687690425114401)
XLA Ops:
  0.0 0.5 collective-permute-start
  0.5 0.1 collective-permute-start.1
  1.2 1.8 %attend_own.1 = (bf16[128,512]{1,0:T(8,128)(2,1)S(1)}, bf16[128,512]{1,0:T(8,128)(2,1)S(1)}, bf16[128,512]{1,0:T(8,128)(2,1)S(1)}) custom-call(s32[1]{0:T(128)} %bitcast.core_ref, s32[1]{0:T(128)S(6)} %copy.24.source_ref, bf16[1,128,1024]{2,1,0:T(8,128)(2,1)} %x_in.1, f32[1,1024]{1,0:T(1,128)} %bitcast.40, bf16[2,80,512]{2,1,0:T(8,128)(2,1)} %keys_in.1, ...), custom_call_target="tpu_custom_call" | custom-call | tf_op jit(solution)/shard_map/attend_own/pallas_call | solution.py:25
  2.9 0.0 collective-permute-done.1.values_ref
  3.0 1.2 %attend_other.1 = (bf16[128,1024]{1,0:T(8,128)(2,1)S(1)}, bf16[128,512]{1,0:T(8,128)(2,1)S(1)}, bf16[128,512]{1,0:T(8,128)(2,1)S(1)}, f32[2,128]{1,0:T(2,128)S(1)}, s32[2,2,128]{2,1,0:T(2,128)S(1)}) custom-call(s32[1]{0:T(128)} %bitcast.core_ref, s32[1]{0:T(128)S(6)} %copy.24.source_ref, bf16[128,512]{1,0:T(8,128)(2,1)S(1)} %get-tuple-element.30.own_ref, ...), custom_call_target="tpu_custom_call" | custom-call | tf_op jit(solution)/shard_map/attend_other/pallas_call | solution.py:25
  4.2 0.5 collective-permute-start.2
  4.7 1.0 %collective-permute-done.2.other_ref = bf16[128,512]{1,0:T(8,128)(2,1)S(1)} collective-permute-done((bf16[128,512]{1,0:T(8,128)(2,1)S(1)}, bf16[128,512]{1,0:T(8,128)(2,1)S(1)}, u32[]{:S(2)}, u32[]{:S(2)}) %collective-permute-start.2) | collective-permute-done | bytes 131104 | tf_op jit(solution)/shard_map/ppermute | solution.py:306
  5.7 0.5 select.5
  6.2 2.9 %collective-permute-start.4 = (bf16[192,512]{1,0:T(8,128)(2,1)S(1)}, bf16[192,512]{1,0:T(8,128)(2,1)S(1)}, u32[]{:S(2)}, u32[]{:S(2)}) collective-permute-start(bf16[192,512]{1,0:T(8,128)(2,1)S(1)} %get-tuple-element.39.p_ref), channel_id=1, source_target_pairs={{0,2},{2,0},{4,6},{6,4},{8,10},{10,8},{12,14},{14,12},{1,3},{3,1},... | collective-permute-start | bytes 589832 | tf_op jit(solution)/shard_map/ppermute | solution.py:311
  9.2 1.6 %collective-permute-start.14 = (bf16[192,512]{1,0:T(8,128)(2,1)S(1)}, bf16[192,512]{1,0:T(8,128)(2,1)S(1)}, u32[]{:S(2)}, u32[]{:S(2)}) collective-permute-start(bf16[192,512]{1,0:T(8,128)(2,1)S(1)} %get-tuple-element.46), channel_id=1, source_target_pairs={{0,4},{2,6},{4,0},{6,2},{8,12},{10,14},{12,8},{14,10},{1,5},{3,7},... | collective-permute-start | bytes 589832 | tf_op jit(solution)/shard_map/ppermute | solution.py:316
  10.7 2.6 %collective-permute-start.10 = (bf16[192,512]{1,0:T(8,128)(2,1)S(1)}, bf16[192,512]{1,0:T(8,128)(2,1)S(1)}, u32[]{:S(2)}, u32[]{:S(2)}) collective-permute-start(bf16[192,512]{1,0:T(8,128)(2,1)S(1)} %get-tuple-element.45), channel_id=1, source_target_pairs={{0,8},{2,10},{4,12},{6,14},{8,0},{10,2},{12,4},{14,6},{1,9},{3,11}... | collective-permute-start | bytes 589832 | tf_op jit(solution)/shard_map/ppermute | solution.py:316
  13.3 0.0 collective-permute-start.5
  13.3 1.1 %collective-permute-done.4.q_ref = bf16[192,512]{1,0:T(8,128)(2,1)S(1)} collective-permute-done((bf16[192,512]{1,0:T(8,128)(2,1)S(1)}, bf16[192,512]{1,0:T(8,128)(2,1)S(1)}, u32[]{:S(2)}, u32[]{:S(2)}) %collective-permute-start.4) | collective-permute-done | bytes 196640 | tf_op jit(solution)/shard_map/ppermute | solution.py:311
  14.4 0.0 collective-permute-start.6
  14.4 2.2 %load.1 = (bf16[1024,1024]{1,0:T(8,128)(2,1)S(1)}, bf16[1024,1024]{1,0:T(8,128)(2,1)S(1)}) custom-call(bf16[1024,1024]{1,0:T(8,128)(2,1)} %in_in.1, bf16[1024,1024]{1,0:T(8,128)(2,1)} %out_in.1), custom_call_target="tpu_custom_call" | custom-call | tf_op jit(solution)/shard_map/load/pallas_call | solution.py:25
  16.6 3.3 %collective-permute-done.14.refs_0_ = bf16[192,512]{1,0:T(8,128)(2,1)S(1)} collective-permute-done((bf16[192,512]{1,0:T(8,128)(2,1)S(1)}, bf16[192,512]{1,0:T(8,128)(2,1)S(1)}, u32[]{:S(2)}, u32[]{:S(2)}) %collective-permute-start.14) | collective-permute-done | bytes 196640 | tf_op jit(solution)/shard_map/ppermute | solution.py:316
  19.9 0.4 collective-permute-start.15
  20.3 2.0 %collective-permute-done.10.p_ref = bf16[192,512]{1,0:T(8,128)(2,1)S(1)} collective-permute-done((bf16[192,512]{1,0:T(8,128)(2,1)S(1)}, bf16[192,512]{1,0:T(8,128)(2,1)S(1)}, u32[]{:S(2)}, u32[]{:S(2)}) %collective-permute-start.10) | collective-permute-done | bytes 196640 | tf_op jit(solution)/shard_map/ppermute | solution.py:316
  22.3 0.5 collective-permute-start.11
  22.8 2.5 %collective-permute-start.8 = (bf16[192,512]{1,0:T(8,128)(2,1)S(1)}, bf16[192,512]{1,0:T(8,128)(2,1)S(1)}, u32[]{:S(2)}, u32[]{:S(2)}) collective-permute-start(bf16[192,512]{1,0:T(8,128)(2,1)S(1)} %get-tuple-element.44), channel_id=1, source_target_pairs={{0,12},{2,14},{4,8},{6,10},{8,4},{10,6},{12,0},{14,2},{1,13},{3,15... | collective-permute-start | bytes 589832 | tf_op jit(solution)/shard_map/ppermute | solution.py:316
  25.3 0.0 collective-permute-done.5.p2_ref
  25.3 1.8 %expert.4 = (f32[2,192,512]{2,1,0:T(8,128)S(1)}, bf16[2,192,512]{2,1,0:T(8,128)(2,1)S(1)}) custom-call(s32[1]{0:T(128)} %bitcast.core_ref, bf16[192,512]{1,0:T(8,128)(2,1)S(1)} %get-tuple-element.39.p_ref, bf16[192,512]{1,0:T(8,128)(2,1)S(1)} %collective-permute-done.4.q_ref, bf16[192,512]{1,0:T(8,128)(2,1)S(1)} %collective-permute-done.5.p2_ref, ...), custom_call_target="tpu_custom_call" | custom-call | tf_op jit(solution)/shard_map/expert/pallas_call | solution.py:25
  27.2 0.6 collective-permute-start.7
  27.7 0.1 collective-permute-start.17
  27.8 1.8 %collective-permute-done.11.q_ref = bf16[192,512]{1,0:T(8,128)(2,1)S(1)} collective-permute-done((bf16[192,512]{1,0:T(8,128)(2,1)S(1)}, bf16[192,512]{1,0:T(8,128)(2,1)S(1)}, u32[]{:S(2)}, u32[]{:S(2)}) %collective-permute-start.11) | collective-permute-done | bytes 196640 | tf_op jit(solution)/shard_map/ppermute | solution.py:311
  29.6 0.8 %collective-permute-done.8.p_ref = bf16[192,512]{1,0:T(8,128)(2,1)S(1)} collective-permute-done((bf16[192,512]{1,0:T(8,128)(2,1)S(1)}, bf16[192,512]{1,0:T(8,128)(2,1)S(1)}, u32[]{:S(2)}, u32[]{:S(2)}) %collective-permute-start.8) | collective-permute-done | bytes 196640 | tf_op jit(solution)/shard_map/ppermute | solution.py:316
  30.4 1.5 %collective-permute-start.9 = (bf16[192,512]{1,0:T(8,128)(2,1)S(1)}, bf16[192,512]{1,0:T(8,128)(2,1)S(1)}, u32[]{:S(2)}, u32[]{:S(2)}) collective-permute-start(bf16[192,512]{1,0:T(8,128)(2,1)S(1)} %collective-permute-done.8.p_ref), channel_id=1, source_target_pairs={{0,2},{2,0},{4,6},{6,4},{8,10},{10,8},{12,14},{14,12},{1,3},{3,1},... | collective-permute-start | bytes 589832 | tf_op jit(solution)/shard_map/ppermute | solution.py:311
  31.9 0.2 collective-permute-start.3
  32.1 1.8 %expert.5 = (f32[2,192,512]{2,1,0:T(8,128)S(1)}, bf16[2,192,512]{2,1,0:T(8,128)(2,1)S(1)}) custom-call(s32[1]{0:T(128)} %bitcast.core_ref, bf16[192,512]{1,0:T(8,128)(2,1)S(1)} %after.6.p_ref, bf16[192,512]{1,0:T(8,128)(2,1)S(1)} %collective-permute-done.15.q_ref, bf16[192,512]{1,0:T(8,128)(2,1)S(1)} %collective-permute-done.16.p2_ref, ...), custom_call_target="tpu_custom_call" | custom-call | tf_op jit(solution)/shard_map/expert/pallas_call | solution.py:25
  34.0 0.3 collective-permute-start.18
  34.3 1.8 %expert.6 = (f32[2,192,512]{2,1,0:T(8,128)S(1)}, bf16[2,192,512]{2,1,0:T(8,128)(2,1)S(1)}) custom-call(s32[1]{0:T(128)} %bitcast.core_ref, bf16[192,512]{1,0:T(8,128)(2,1)S(1)} %collective-permute-done.10.p_ref, bf16[192,512]{1,0:T(8,128)(2,1)S(1)} %collective-permute-done.11.q_ref, bf16[192,512]{1,0:T(8,128)(2,1)S(1)} %collective-permute-done.12.p2_ref, ...), custom_call_target="tpu_custom_call" | custom-call | tf_op jit(solution)/shard_map/expert/pallas_call | solution.py:25
  36.2 0.3 collective-permute-start.20
  36.5 1.2 %collective-permute-done.9.refs_0_ = bf16[192,512]{1,0:T(8,128)(2,1)S(1)} collective-permute-done((bf16[192,512]{1,0:T(8,128)(2,1)S(1)}, bf16[192,512]{1,0:T(8,128)(2,1)S(1)}, u32[]{:S(2)}, u32[]{:S(2)}) %collective-permute-start.9) | collective-permute-done | bytes 196640 | tf_op jit(solution)/shard_map/ppermute | solution.py:311
  37.7 0.0 collective-permute-done.7
  37.7 0.5 collective-permute-start.19
  38.2 0.1 convert_add_fusion.3
  38.4 0.1 convert_add_fusion.2
  38.5 1.6 %collective-permute-start.27 = (bf16[192,512]{1,0:T(8,128)(2,1)S(1)}, bf16[192,512]{1,0:T(8,128)(2,1)S(1)}, u32[]{:S(2)}, u32[]{:S(2)}) collective-permute-start(bf16[192,512]{1,0:T(8,128)(2,1)S(1)} %fusion.9.refs_1_), channel_id=1, source_target_pairs={{0,2},{2,0},{4,6},{6,4},{8,10},{10,8},{12,14},{14,12},{1,3},{3,1},... | collective-permute-start | bytes 589832 | tf_op jit(solution)/shard_map/ppermute | solution.py:311
  40.1 0.0 collective-permute-done.19.refs_0_
  40.1 1.8 %expert.7 = (f32[2,192,512]{2,1,0:T(8,128)S(1)}, bf16[2,192,512]{2,1,0:T(8,128)(2,1)S(1)}) custom-call(s32[1]{0:T(128)} %bitcast.core_ref, bf16[192,512]{1,0:T(8,128)(2,1)S(1)} %collective-permute-done.8.p_ref, bf16[192,512]{1,0:T(8,128)(2,1)S(1)} %after.8.q_ref, bf16[192,512]{1,0:T(8,128)(2,1)S(1)} %collective-permute-done.18.p2_ref, ...), custom_call_target="tpu_custom_call" | custom-call | tf_op jit(solution)/shard_map/expert/pallas_call | solution.py:25
  42.0 0.1 collective-permute-start.21
  42.1 0.1 convert_add_fusion
  42.2 1.5 %collective-permute-done.21 = bf16[2,192,512]{2,1,0:T(8,128)(2,1)S(1)} collective-permute-done((bf16[2,192,512]{2,1,0:T(8,128)(2,1)S(1)}, bf16[2,192,512]{2,1,0:T(8,128)(2,1)S(1)}, u32[]{:S(2)}, u32[]{:S(2)}) %collective-permute-start.21) | collective-permute-done | bytes 393248 | tf_op jit(solution)/shard_map/ppermute | solution.py:306
  43.8 0.1 convert_add_fusion.1
  43.9 1.2 %collective-permute-start.22 = (bf16[192,512]{1,0:T(8,128)(2,1)S(1)}, bf16[192,512]{1,0:T(8,128)(2,1)S(1)}, u32[]{:S(2)}, u32[]{:S(2)}) collective-permute-start(bf16[192,512]{1,0:T(8,128)(2,1)S(1)} %fusion.10.refs_1_), channel_id=1, source_target_pairs={{0,2},{2,0},{4,6},{6,4},{8,10},{10,8},{12,14},{14,12},{1,3},{3,1},... | collective-permute-start | bytes 589832 | tf_op jit(solution)/shard_map/ppermute | solution.py:311
  45.1 0.4 collective-permute-done.27
  45.5 0.1 fusion.1
  45.5 2.5 %collective-permute-start.28 = (bf16[192,512]{1,0:T(8,128)(2,1)S(1)}, bf16[192,512]{1,0:T(8,128)(2,1)S(1)}, u32[]{:S(2)}, u32[]{:S(2)}) collective-permute-start(bf16[192,512]{1,0:T(8,128)(2,1)S(1)} %fusion.1), channel_id=1, source_target_pairs={{0,8},{2,10},{4,12},{6,14},{8,0},{10,2},{12,4},{14,6},{1,9},{3,11}... | collective-permute-start | bytes 589832 | tf_op jit(solution)/shard_map/ppermute | solution.py:316
  48.0 1.5 %collective-permute-start.25 = (bf16[192,512]{1,0:T(8,128)(2,1)S(1)}, bf16[192,512]{1,0:T(8,128)(2,1)S(1)}, u32[]{:S(2)}, u32[]{:S(2)}) collective-permute-start(bf16[192,512]{1,0:T(8,128)(2,1)S(1)} %after.11), channel_id=1, source_target_pairs={{0,2},{2,0},{4,6},{6,4},{8,10},{10,8},{12,14},{14,12},{1,3},{3,1},... | collective-permute-start | bytes 589832 | tf_op jit(solution)/shard_map/ppermute | solution.py:311
  49.6 2.2 %collective-permute-done.22 = bf16[192,512]{1,0:T(8,128)(2,1)S(1)} collective-permute-done((bf16[192,512]{1,0:T(8,128)(2,1)S(1)}, bf16[192,512]{1,0:T(8,128)(2,1)S(1)}, u32[]{:S(2)}, u32[]{:S(2)}) %collective-permute-start.22) | collective-permute-done | bytes 196640 | tf_op jit(solution)/shard_map/ppermute | solution.py:311
  51.8 2.5 %collective-permute-start.29 = (bf16[192,512]{1,0:T(8,128)(2,1)S(1)}, bf16[192,512]{1,0:T(8,128)(2,1)S(1)}, u32[]{:S(2)}, u32[]{:S(2)}) collective-permute-start(bf16[192,512]{1,0:T(8,128)(2,1)S(1)} %fusion.5.refs_1_), channel_id=1, source_target_pairs={{0,12},{2,14},{4,8},{6,10},{8,4},{10,6},{12,0},{14,2},{1,13},{3,15... | collective-permute-start | bytes 589832 | tf_op jit(solution)/shard_map/ppermute | solution.py:316
  54.3 1.1 %collective-permute-start.23 = (bf16[192,512]{1,0:T(8,128)(2,1)S(1)}, bf16[192,512]{1,0:T(8,128)(2,1)S(1)}, u32[]{:S(2)}, u32[]{:S(2)}) collective-permute-start(bf16[192,512]{1,0:T(8,128)(2,1)S(1)} %after.10), channel_id=1, source_target_pairs={{0,2},{2,0},{4,6},{6,4},{8,10},{10,8},{12,14},{14,12},{1,3},{3,1},... | collective-permute-start | bytes 589832 | tf_op jit(solution)/shard_map/ppermute | solution.py:311
  55.4 0.0 collective-permute-done.25
  55.4 3.0 %collective-permute-start.26 = (bf16[192,512]{1,0:T(8,128)(2,1)S(1)}, bf16[192,512]{1,0:T(8,128)(2,1)S(1)}, u32[]{:S(2)}, u32[]{:S(2)}) collective-permute-start(bf16[192,512]{1,0:T(8,128)(2,1)S(1)} %fusion.3), channel_id=1, source_target_pairs={{0,4},{2,6},{4,0},{6,2},{8,12},{10,14},{12,8},{14,10},{1,5},{3,7},... | collective-permute-start | bytes 589832 | tf_op jit(solution)/shard_map/ppermute | solution.py:316
  58.4 1.5 %collective-permute-done.23 = bf16[192,512]{1,0:T(8,128)(2,1)S(1)} collective-permute-done((bf16[192,512]{1,0:T(8,128)(2,1)S(1)}, bf16[192,512]{1,0:T(8,128)(2,1)S(1)}, u32[]{:S(2)}, u32[]{:S(2)}) %collective-permute-start.23) | collective-permute-done | bytes 196640 | tf_op jit(solution)/shard_map/ppermute | solution.py:311
  60.0 0.1 fusion.7.rest_0_
  60.0 0.0 collective-permute-done.3.gates_ref
  60.0 2.8 %collective-permute-done.28.rest_2_ = bf16[192,512]{1,0:T(8,128)(2,1)S(1)} collective-permute-done((bf16[192,512]{1,0:T(8,128)(2,1)S(1)}, bf16[192,512]{1,0:T(8,128)(2,1)S(1)}, u32[]{:S(2)}, u32[]{:S(2)}) %collective-permute-start.28) | collective-permute-done | bytes 196640 | tf_op jit(solution)/shard_map/ppermute | solution.py:316
  62.8 2.6 %collective-permute-done.26.rest_1_ = bf16[192,512]{1,0:T(8,128)(2,1)S(1)} collective-permute-done((bf16[192,512]{1,0:T(8,128)(2,1)S(1)}, bf16[192,512]{1,0:T(8,128)(2,1)S(1)}, u32[]{:S(2)}, u32[]{:S(2)}) %collective-permute-start.26) | collective-permute-done | bytes 196640 | tf_op jit(solution)/shard_map/ppermute | solution.py:316
  65.4 0.5 combine_other.1
  65.9 0.1 collective-permute-start.30
  66.0 0.5 combine_own.1.own_ref
  66.5 0.8 %collective-permute-done.30.other_ref = bf16[128,512]{1,0:T(8,128)(2,1)S(1)} collective-permute-done((bf16[128,512]{1,0:T(8,128)(2,1)S(1)}, bf16[128,512]{1,0:T(8,128)(2,1)S(1)}, u32[]{:S(2)}, u32[]{:S(2)}) %collective-permute-start.30) | collective-permute-done | bytes 131104 | tf_op jit(solution)/shard_map/ppermute | solution.py:306
  67.3 0.7 %finish.1 = bf16[128,1024]{1,0:T(8,128)(2,1)} custom-call(s32[1]{0:T(128)} %bitcast.core_ref, bf16[128,1024]{1,0:T(8,128)(2,1)S(1)} %get-tuple-element.33.state_ref, bf16[128,512]{1,0:T(8,128)(2,1)S(1)} %combine_own.1.own_ref, bf16[128,512]{1,0:T(8,128)(2,1)S(1)} %collective-permute-done.30.other_ref), custom_call_target="tpu_custom_call" | custom-call | tf_op jit(solution)/shard_map/finish/pallas_call | solution.py:25
  (27 shorter events, 0.2 us)
Async XLA Ops:
  0.0 2.9 %collective-permute-start = (bf16[2,80,512]{2,1,0:T(8,128)(2,1)}, bf16[2,80,512]{2,1,0:T(8,128)(2,1)S(1)}, u32[]{:S(2)}, u32[]{:S(2)}) collective-permute-start(bf16[2,80,512]{2,1,0:T(8,128)(2,1)} %keys_in.1), channel_id=1, source_target_pairs={{0,1},{1,0},{2,3},{3,2},{4,5},{5,4},{6,7},{7,6},{8,9},{9,8},{10,11... | collective-permute-start | bytes 491528 | tf_op jit(solution)/shard_map/ppermute | solution.py:306
  0.5 2.5 %collective-permute-start.1 = (bf16[2,80,512]{2,1,0:T(8,128)(2,1)}, bf16[2,80,512]{2,1,0:T(8,128)(2,1)S(1)}, u32[]{:S(2)}, u32[]{:S(2)}) collective-permute-start(bf16[2,80,512]{2,1,0:T(8,128)(2,1)} %values_in.1), channel_id=1, source_target_pairs={{0,1},{1,0},{2,3},{3,2},{4,5},{5,4},{6,7},{7,6},{8,9},{9,8},{10,11... | collective-permute-start | bytes 491528 | tf_op jit(solution)/shard_map/ppermute | solution.py:306
  4.2 1.5 %collective-permute-start.2 = (bf16[128,512]{1,0:T(8,128)(2,1)S(1)}, bf16[128,512]{1,0:T(8,128)(2,1)S(1)}, u32[]{:S(2)}, u32[]{:S(2)}) collective-permute-start(bf16[128,512]{1,0:T(8,128)(2,1)S(1)} %get-tuple-element.37), channel_id=1, source_target_pairs={{0,1},{1,0},{2,3},{3,2},{4,5},{5,4},{6,7},{7,6},{8,9},{9,8},{10,11... | collective-permute-start | bytes 393224 | tf_op jit(solution)/shard_map/ppermute | solution.py:306
  6.2 8.1 %collective-permute-start.4 = (bf16[192,512]{1,0:T(8,128)(2,1)S(1)}, bf16[192,512]{1,0:T(8,128)(2,1)S(1)}, u32[]{:S(2)}, u32[]{:S(2)}) collective-permute-start(bf16[192,512]{1,0:T(8,128)(2,1)S(1)} %get-tuple-element.39.p_ref), channel_id=1, source_target_pairs={{0,2},{2,0},{4,6},{6,4},{8,10},{10,8},{12,14},{14,12},{1,3},{3,1},... | collective-permute-start | bytes 589832 | tf_op jit(solution)/shard_map/ppermute | solution.py:311
  9.2 10.8 %collective-permute-start.14 = (bf16[192,512]{1,0:T(8,128)(2,1)S(1)}, bf16[192,512]{1,0:T(8,128)(2,1)S(1)}, u32[]{:S(2)}, u32[]{:S(2)}) collective-permute-start(bf16[192,512]{1,0:T(8,128)(2,1)S(1)} %get-tuple-element.46), channel_id=1, source_target_pairs={{0,4},{2,6},{4,0},{6,2},{8,12},{10,14},{12,8},{14,10},{1,5},{3,7},... | collective-permute-start | bytes 589832 | tf_op jit(solution)/shard_map/ppermute | solution.py:316
  10.7 11.6 %collective-permute-start.10 = (bf16[192,512]{1,0:T(8,128)(2,1)S(1)}, bf16[192,512]{1,0:T(8,128)(2,1)S(1)}, u32[]{:S(2)}, u32[]{:S(2)}) collective-permute-start(bf16[192,512]{1,0:T(8,128)(2,1)S(1)} %get-tuple-element.45), channel_id=1, source_target_pairs={{0,8},{2,10},{4,12},{6,14},{8,0},{10,2},{12,4},{14,6},{1,9},{3,11}... | collective-permute-start | bytes 589832 | tf_op jit(solution)/shard_map/ppermute | solution.py:316
  13.3 12.0 %collective-permute-start.5 = (bf16[192,512]{1,0:T(8,128)(2,1)S(1)}, bf16[192,512]{1,0:T(8,128)(2,1)S(1)}, u32[]{:S(2)}, u32[]{:S(2)}) collective-permute-start(bf16[192,512]{1,0:T(8,128)(2,1)S(1)} %get-tuple-element.39.p_ref), channel_id=1, source_target_pairs={{0,1},{1,0},{2,3},{3,2},{4,5},{5,4},{6,7},{7,6},{8,9},{9,8},{10,11... | collective-permute-start | bytes 589832 | tf_op jit(solution)/shard_map/ppermute | solution.py:306
  14.4 10.9 %collective-permute-start.6 = (bf16[192,512]{1,0:T(8,128)(2,1)S(1)}, bf16[192,512]{1,0:T(8,128)(2,1)S(1)}, u32[]{:S(2)}, u32[]{:S(2)}) collective-permute-start(bf16[192,512]{1,0:T(8,128)(2,1)S(1)} %collective-permute-done.4.q_ref), channel_id=1, source_target_pairs={{0,1},{1,0},{2,3},{3,2},{4,5},{5,4},{6,7},{7,6},{8,9},{9,8},{10,11... | collective-permute-start | bytes 589832 | tf_op jit(solution)/shard_map/ppermute | solution.py:306
  19.9 7.8 %collective-permute-start.15 = (bf16[192,512]{1,0:T(8,128)(2,1)S(1)}, bf16[192,512]{1,0:T(8,128)(2,1)S(1)}, u32[]{:S(2)}, u32[]{:S(2)}) collective-permute-start(bf16[192,512]{1,0:T(8,128)(2,1)S(1)} %after.6.p_ref), channel_id=1, source_target_pairs={{0,2},{2,0},{4,6},{6,4},{8,10},{10,8},{12,14},{14,12},{1,3},{3,1},... | collective-permute-start | bytes 589832 | tf_op jit(solution)/shard_map/ppermute | solution.py:311
  22.3 7.3 %collective-permute-start.11 = (bf16[192,512]{1,0:T(8,128)(2,1)S(1)}, bf16[192,512]{1,0:T(8,128)(2,1)S(1)}, u32[]{:S(2)}, u32[]{:S(2)}) collective-permute-start(bf16[192,512]{1,0:T(8,128)(2,1)S(1)} %collective-permute-done.10.p_ref), channel_id=1, source_target_pairs={{0,2},{2,0},{4,6},{6,4},{8,10},{10,8},{12,14},{14,12},{1,3},{3,1},... | collective-permute-start | bytes 589832 | tf_op jit(solution)/shard_map/ppermute | solution.py:311
  22.8 7.6 %collective-permute-start.8 = (bf16[192,512]{1,0:T(8,128)(2,1)S(1)}, bf16[192,512]{1,0:T(8,128)(2,1)S(1)}, u32[]{:S(2)}, u32[]{:S(2)}) collective-permute-start(bf16[192,512]{1,0:T(8,128)(2,1)S(1)} %get-tuple-element.44), channel_id=1, source_target_pairs={{0,12},{2,14},{4,8},{6,10},{8,4},{10,6},{12,0},{14,2},{1,13},{3,15... | collective-permute-start | bytes 589832 | tf_op jit(solution)/shard_map/ppermute | solution.py:316
  25.3 5.1 %collective-permute-start.16 = (bf16[192,512]{1,0:T(8,128)(2,1)S(1)}, bf16[192,512]{1,0:T(8,128)(2,1)S(1)}, u32[]{:S(2)}, u32[]{:S(2)}) collective-permute-start(bf16[192,512]{1,0:T(8,128)(2,1)S(1)} %after.6.p_ref), channel_id=1, source_target_pairs={{0,1},{1,0},{2,3},{3,2},{4,5},{5,4},{6,7},{7,6},{8,9},{9,8},{10,11... | collective-permute-start | bytes 589832 | tf_op jit(solution)/shard_map/ppermute | solution.py:306
  27.2 10.6 %collective-permute-start.7 = (bf16[2,192,512]{2,1,0:T(8,128)(2,1)S(1)}, bf16[2,192,512]{2,1,0:T(8,128)(2,1)S(1)}, u32[]{:S(2)}, u32[]{:S(2)}) collective-permute-start(bf16[2,192,512]{2,1,0:T(8,128)(2,1)S(1)} %get-tuple-element.43), channel_id=1, source_target_pairs={{0,1},{1,0},{2,3},{3,2},{4,5},{5,4},{6,7},{7,6},{8,9},{9,8},{10,11... | collective-permute-start | bytes 1179656 | tf_op jit(solution)/shard_map/ppermute | solution.py:306
  27.7 4.2 %collective-permute-start.17 = (bf16[192,512]{1,0:T(8,128)(2,1)S(1)}, bf16[192,512]{1,0:T(8,128)(2,1)S(1)}, u32[]{:S(2)}, u32[]{:S(2)}) collective-permute-start(bf16[192,512]{1,0:T(8,128)(2,1)S(1)} %collective-permute-done.15.q_ref), channel_id=1, source_target_pairs={{0,1},{1,0},{2,3},{3,2},{4,5},{5,4},{6,7},{7,6},{8,9},{9,8},{10,11... | collective-permute-start | bytes 589832 | tf_op jit(solution)/shard_map/ppermute | solution.py:306
  29.6 4.4 %collective-permute-start.13 = (bf16[192,512]{1,0:T(8,128)(2,1)S(1)}, bf16[192,512]{1,0:T(8,128)(2,1)S(1)}, u32[]{:S(2)}, u32[]{:S(2)}) collective-permute-start(bf16[192,512]{1,0:T(8,128)(2,1)S(1)} %collective-permute-done.11.q_ref), channel_id=1, source_target_pairs={{0,1},{1,0},{2,3},{3,2},{4,5},{5,4},{6,7},{7,6},{8,9},{9,8},{10,11... | collective-permute-start | bytes 589832 | tf_op jit(solution)/shard_map/ppermute | solution.py:306
  30.4 4.0 %collective-permute-start.12 = (bf16[192,512]{1,0:T(8,128)(2,1)S(1)}, bf16[192,512]{1,0:T(8,128)(2,1)S(1)}, u32[]{:S(2)}, u32[]{:S(2)}) collective-permute-start(bf16[192,512]{1,0:T(8,128)(2,1)S(1)} %collective-permute-done.10.p_ref), channel_id=1, source_target_pairs={{0,1},{1,0},{2,3},{3,2},{4,5},{5,4},{6,7},{7,6},{8,9},{9,8},{10,11... | collective-permute-start | bytes 589832 | tf_op jit(solution)/shard_map/ppermute | solution.py:306
  30.4 7.3 %collective-permute-start.9 = (bf16[192,512]{1,0:T(8,128)(2,1)S(1)}, bf16[192,512]{1,0:T(8,128)(2,1)S(1)}, u32[]{:S(2)}, u32[]{:S(2)}) collective-permute-start(bf16[192,512]{1,0:T(8,128)(2,1)S(1)} %collective-permute-done.8.p_ref), channel_id=1, source_target_pairs={{0,2},{2,0},{4,6},{6,4},{8,10},{10,8},{12,14},{14,12},{1,3},{3,1},... | collective-permute-start | bytes 589832 | tf_op jit(solution)/shard_map/ppermute | solution.py:311
  31.9 28.1 %collective-permute-start.3 = (f32[2,128]{1,0:T(2,128)S(1)}, f32[2,128]{1,0:T(2,128)S(1)}, u32[]{:S(2)}, u32[]{:S(2)}) collective-permute-start(f32[2,128]{1,0:T(2,128)S(1)} %get-tuple-element.35.gates_ref), channel_id=1, source_target_pairs={{0,1},{1,0},{2,3},{3,2},{4,5},{5,4},{6,7},{7,6},{8,9},{9,8},{10,11... | collective-permute-start | bytes 3080 | tf_op jit(solution)/shard_map/ppermute | solution.py:306
  34.0 6.1 %collective-permute-start.18 = (bf16[192,512]{1,0:T(8,128)(2,1)S(1)}, bf16[192,512]{1,0:T(8,128)(2,1)S(1)}, u32[]{:S(2)}, u32[]{:S(2)}) collective-permute-start(bf16[192,512]{1,0:T(8,128)(2,1)S(1)} %collective-permute-done.8.p_ref), channel_id=1, source_target_pairs={{0,1},{1,0},{2,3},{3,2},{4,5},{5,4},{6,7},{7,6},{8,9},{9,8},{10,11... | collective-permute-start | bytes 589832 | tf_op jit(solution)/shard_map/ppermute | solution.py:306
  36.2 2.2 %collective-permute-start.20 = (bf16[2,192,512]{2,1,0:T(8,128)(2,1)S(1)}, bf16[2,192,512]{2,1,0:T(8,128)(2,1)S(1)}, u32[]{:S(2)}, u32[]{:S(2)}) collective-permute-start(bf16[2,192,512]{2,1,0:T(8,128)(2,1)S(1)} %get-tuple-element.49), channel_id=1, source_target_pairs={{0,1},{1,0},{2,3},{3,2},{4,5},{5,4},{6,7},{7,6},{8,9},{9,8},{10,11... | collective-permute-start | bytes 1179656 | tf_op jit(solution)/shard_map/ppermute | solution.py:306
  37.7 4.3 %collective-permute-start.24 = (bf16[2,192,512]{2,1,0:T(8,128)(2,1)S(1)}, bf16[2,192,512]{2,1,0:T(8,128)(2,1)S(1)}, u32[]{:S(2)}, u32[]{:S(2)}) collective-permute-start(bf16[2,192,512]{2,1,0:T(8,128)(2,1)S(1)} %get-tuple-element.52), channel_id=1, source_target_pairs={{0,1},{1,0},{2,3},{3,2},{4,5},{5,4},{6,7},{7,6},{8,9},{9,8},{10,11... | collective-permute-start | bytes 1179656 | tf_op jit(solution)/shard_map/ppermute | solution.py:306
  37.7 2.4 %collective-permute-start.19 = (bf16[192,512]{1,0:T(8,128)(2,1)S(1)}, bf16[192,512]{1,0:T(8,128)(2,1)S(1)}, u32[]{:S(2)}, u32[]{:S(2)}) collective-permute-start(bf16[192,512]{1,0:T(8,128)(2,1)S(1)} %after.8.q_ref), channel_id=1, source_target_pairs={{0,1},{1,0},{2,3},{3,2},{4,5},{5,4},{6,7},{7,6},{8,9},{9,8},{10,11... | collective-permute-start | bytes 589832 | tf_op jit(solution)/shard_map/ppermute | solution.py:306
  38.5 6.9 %collective-permute-start.27 = (bf16[192,512]{1,0:T(8,128)(2,1)S(1)}, bf16[192,512]{1,0:T(8,128)(2,1)S(1)}, u32[]{:S(2)}, u32[]{:S(2)}) collective-permute-start(bf16[192,512]{1,0:T(8,128)(2,1)S(1)} %fusion.9.refs_1_), channel_id=1, source_target_pairs={{0,2},{2,0},{4,6},{6,4},{8,10},{10,8},{12,14},{14,12},{1,3},{3,1},... | collective-permute-start | bytes 589832 | tf_op jit(solution)/shard_map/ppermute | solution.py:311
  42.0 1.8 %collective-permute-start.21 = (bf16[2,192,512]{2,1,0:T(8,128)(2,1)S(1)}, bf16[2,192,512]{2,1,0:T(8,128)(2,1)S(1)}, u32[]{:S(2)}, u32[]{:S(2)}) collective-permute-start(bf16[2,192,512]{2,1,0:T(8,128)(2,1)S(1)} %get-tuple-element.51), channel_id=1, source_target_pairs={{0,1},{1,0},{2,3},{3,2},{4,5},{5,4},{6,7},{7,6},{8,9},{9,8},{10,11... | collective-permute-start | bytes 1179656 | tf_op jit(solution)/shard_map/ppermute | solution.py:306
  43.9 7.8 %collective-permute-start.22 = (bf16[192,512]{1,0:T(8,128)(2,1)S(1)}, bf16[192,512]{1,0:T(8,128)(2,1)S(1)}, u32[]{:S(2)}, u32[]{:S(2)}) collective-permute-start(bf16[192,512]{1,0:T(8,128)(2,1)S(1)} %fusion.10.refs_1_), channel_id=1, source_target_pairs={{0,2},{2,0},{4,6},{6,4},{8,10},{10,8},{12,14},{14,12},{1,3},{3,1},... | collective-permute-start | bytes 589832 | tf_op jit(solution)/shard_map/ppermute | solution.py:311
  45.5 17.3 %collective-permute-start.28 = (bf16[192,512]{1,0:T(8,128)(2,1)S(1)}, bf16[192,512]{1,0:T(8,128)(2,1)S(1)}, u32[]{:S(2)}, u32[]{:S(2)}) collective-permute-start(bf16[192,512]{1,0:T(8,128)(2,1)S(1)} %fusion.1), channel_id=1, source_target_pairs={{0,8},{2,10},{4,12},{6,14},{8,0},{10,2},{12,4},{14,6},{1,9},{3,11}... | collective-permute-start | bytes 589832 | tf_op jit(solution)/shard_map/ppermute | solution.py:316
  48.0 7.3 %collective-permute-start.25 = (bf16[192,512]{1,0:T(8,128)(2,1)S(1)}, bf16[192,512]{1,0:T(8,128)(2,1)S(1)}, u32[]{:S(2)}, u32[]{:S(2)}) collective-permute-start(bf16[192,512]{1,0:T(8,128)(2,1)S(1)} %after.11), channel_id=1, source_target_pairs={{0,2},{2,0},{4,6},{6,4},{8,10},{10,8},{12,14},{14,12},{1,3},{3,1},... | collective-permute-start | bytes 589832 | tf_op jit(solution)/shard_map/ppermute | solution.py:311
  51.8 13.6 %collective-permute-start.29 = (bf16[192,512]{1,0:T(8,128)(2,1)S(1)}, bf16[192,512]{1,0:T(8,128)(2,1)S(1)}, u32[]{:S(2)}, u32[]{:S(2)}) collective-permute-start(bf16[192,512]{1,0:T(8,128)(2,1)S(1)} %fusion.5.refs_1_), channel_id=1, source_target_pairs={{0,12},{2,14},{4,8},{6,10},{8,4},{10,6},{12,0},{14,2},{1,13},{3,15... | collective-permute-start | bytes 589832 | tf_op jit(solution)/shard_map/ppermute | solution.py:316
  54.3 5.7 %collective-permute-start.23 = (bf16[192,512]{1,0:T(8,128)(2,1)S(1)}, bf16[192,512]{1,0:T(8,128)(2,1)S(1)}, u32[]{:S(2)}, u32[]{:S(2)}) collective-permute-start(bf16[192,512]{1,0:T(8,128)(2,1)S(1)} %after.10), channel_id=1, source_target_pairs={{0,2},{2,0},{4,6},{6,4},{8,10},{10,8},{12,14},{14,12},{1,3},{3,1},... | collective-permute-start | bytes 589832 | tf_op jit(solution)/shard_map/ppermute | solution.py:311
  55.4 10.0 %collective-permute-start.26 = (bf16[192,512]{1,0:T(8,128)(2,1)S(1)}, bf16[192,512]{1,0:T(8,128)(2,1)S(1)}, u32[]{:S(2)}, u32[]{:S(2)}) collective-permute-start(bf16[192,512]{1,0:T(8,128)(2,1)S(1)} %fusion.3), channel_id=1, source_target_pairs={{0,4},{2,6},{4,0},{6,2},{8,12},{10,14},{12,8},{14,10},{1,5},{3,7},... | collective-permute-start | bytes 589832 | tf_op jit(solution)/shard_map/ppermute | solution.py:316
  65.9 1.4 %collective-permute-start.30 = (bf16[128,512]{1,0:T(8,128)(2,1)S(1)}, bf16[128,512]{1,0:T(8,128)(2,1)S(1)}, u32[]{:S(2)}, u32[]{:S(2)}) collective-permute-start(bf16[128,512]{1,0:T(8,128)(2,1)S(1)} %get-tuple-element.54), channel_id=1, source_target_pairs={{0,1},{1,0},{2,3},{3,2},{4,5},{5,4},{6,7},{7,6},{8,9},{9,8},{10,11... | collective-permute-start | bytes 393224 | tf_op jit(solution)/shard_map/ppermute | solution.py:306

commit v21 on v20

--- a/solution.py
+++ b/solution.py
@@ -443,13 +443,10 @@
     p2, q2 = swap(p), swap(q)
     kept[0], moving = run(p, q, p2, q2)
     boths[0], halves[0] = sums(kept[0], moving)
-    p, q = ps[1], qs[1]
+    p, q = ps[2], qs[2]
+    q = after(q, qs[1])
     p2, q2 = swap(p), swap(q)
-    kept[1], moving = run(p, q, p2, q2)
-    boths[1], halves[1] = sums(kept[1], moving)
-    p, q = ps[2], qs[2]
-    p2, q2 = swap(p), swap(q)
-    q2 = after(q2, kept[0], kept[1])
+    q2 = after(q2, kept[0])
     kept[2], moving = run(p, q, p2, q2)
     boths[2], halves[2] = sums(kept[2], moving)
     p, q = ps[3], qs[3]
@@ -458,6 +455,11 @@
     q2 = after(q2, halves[2])
     kept[3], moving = run(p, q, p2, q2)
     boths[3], halves[3] = sums(kept[3], moving)
+    p, q = ps[1], qs[1]
+    p2, q2 = swap(p), swap(q)
+    q2 = after(q2, kept[3])
+    kept[1], moving = run(p, q, p2, q2)
+    boths[1], halves[1] = sums(kept[1], moving)
     leaving = halves[2]
     across = swap_owner(leaving)
     wholes[2] = whole(boths[2], across)

time: 68.3 us -> 69.4 us (1.016)
  waiting for transfers between devices: 23 us -> 26.4 us
  starting transfers between devices: 28.6 us -> 26.3 us
    ppermute x8, waiting for transfers between devices: 8.15 us -> 15.9 us  [swap_owner(): return lax.ppermute(values, 'expert', [(i, i ^ 1) for i in range(owners)])]
    ppermute x6, waiting for transfers between devices: 11.5 us -> 7.43 us  [exchange(): lax.ppermute(values, 'expert', [(i, i ^ 2 * offset) for i in range(owners)])]
    ppermute x6, starting transfers between devices: 14.7 us -> 12.8 us  [exchange(): lax.ppermute(values, 'expert', [(i, i ^ 2 * offset) for i in range(owners)])]
    ppermute x8, starting transfers between devices: 10.7 us -> 9.87 us  [swap_owner(): return lax.ppermute(values, 'expert', [(i, i ^ 1) for i in range(owners)])]
where the time goes in v21:
time: 69.4 us; the launch traced here: 69.3 us
  waiting for transfers between devices  26.4 us (38%)
  starting transfers between devices  26.3 us (38%)
  Pallas kernels  14.9 us (21%)
  between operations  0.94 us (1%)
    ppermute x8, waiting for transfers between devices, swap_owner(): return lax.ppermute(values, 'expert', [(i, i ^ 1) for i in range(owners)])  15.9 us
    pallas_call x11, Pallas kernels, call(): pl.pallas_call(kernel, out_shape=tuple((jax.ShapeDtypeStruct(*out) for ou...  14.9 us
    ppermute x6, starting transfers between devices, exchange(): lax.ppermute(values, 'expert', [(i, i ^ 2 * offset) for i in range(owners)])  12.8 us
    ppermute x8, starting transfers between devices, swap_owner(): return lax.ppermute(values, 'expert', [(i, i ^ 1) for i in range(owners)])  9.87 us
    ppermute x6, waiting for transfers between devices, exchange(): lax.ppermute(values, 'expert', [(i, i ^ 2 * offset) for i in range(owners)])  7.43 us
    ppermute x17, starting transfers between devices, swap(): return lax.ppermute(values, 'section', [(0, 1), (1, 0)])  3.6 us
    ppermute x17, waiting for transfers between devices, swap(): return lax.ppermute(values, 'section', [(0, 1), (1, 0)])  3.06 us
  transfers between devices with their start and end apart: 31, of which 14 were waited for; matrix products, arithmetic and copies ran while one was open for 1% of the time, Pallas kernels for 17%

profile of v21, /device:TPU:0, one launch (start us, length us, event | category | flops | bytes accessed | tf_op | source)
XLA Modules:
  0.0 69.3 jit_solution(13597983501991835362)
XLA Ops:
  0.0 0.5 collective-permute-start
  0.5 0.1 collective-permute-start.1
  1.2 1.8 %attend_own.1 = (bf16[128,512]{1,0:T(8,128)(2,1)S(1)}, bf16[128,512]{1,0:T(8,128)(2,1)S(1)}, bf16[128,512]{1,0:T(8,128)(2,1)S(1)}) custom-call(s32[1]{0:T(128)} %bitcast.core_ref, s32[1]{0:T(128)S(6)} %copy.28.source_ref, bf16[1,128,1024]{2,1,0:T(8,128)(2,1)} %x_in.1, f32[1,1024]{1,0:T(1,128)} %bitcast.40, bf16[2,80,512]{2,1,0:T(8,128)(2,1)} %keys_in.1, ...), custom_call_target="tpu_custom_call" | custom-call | tf_op jit(solution)/shard_map/attend_own/pallas_call | solution.py:25
  2.9 0.0 collective-permute-done.keys_ref
  3.0 1.2 %attend_other.1 = (bf16[128,1024]{1,0:T(8,128)(2,1)S(1)}, bf16[128,512]{1,0:T(8,128)(2,1)S(1)}, bf16[128,512]{1,0:T(8,128)(2,1)S(1)}, f32[2,128]{1,0:T(2,128)S(1)}, s32[2,2,128]{2,1,0:T(2,128)S(1)}) custom-call(s32[1]{0:T(128)} %bitcast.core_ref, s32[1]{0:T(128)S(6)} %copy.28.source_ref, bf16[128,512]{1,0:T(8,128)(2,1)S(1)} %get-tuple-element.30.own_ref, ...), custom_call_target="tpu_custom_call" | custom-call | tf_op jit(solution)/shard_map/attend_other/pallas_call | solution.py:25
  4.2 0.5 collective-permute-start.2
  4.7 1.0 %collective-permute-done.2.other_ref = bf16[128,512]{1,0:T(8,128)(2,1)S(1)} collective-permute-done((bf16[128,512]{1,0:T(8,128)(2,1)S(1)}, bf16[128,512]{1,0:T(8,128)(2,1)S(1)}, u32[]{:S(2)}, u32[]{:S(2)}) %collective-permute-start.2) | collective-permute-done | bytes 131104 | tf_op jit(solution)/shard_map/ppermute | solution.py:306
  5.7 0.5 select.5
  6.2 2.9 %collective-permute-start.4 = (bf16[192,512]{1,0:T(8,128)(2,1)S(1)}, bf16[192,512]{1,0:T(8,128)(2,1)S(1)}, u32[]{:S(2)}, u32[]{:S(2)}) collective-permute-start(bf16[192,512]{1,0:T(8,128)(2,1)S(1)} %get-tuple-element.39.p_ref), channel_id=1, source_target_pairs={{0,2},{2,0},{4,6},{6,4},{8,10},{10,8},{12,14},{14,12},{1,3},{3,1},... | collective-permute-start | bytes 589832 | tf_op jit(solution)/shard_map/ppermute | solution.py:311
  9.2 1.6 %collective-permute-start.12 = (bf16[192,512]{1,0:T(8,128)(2,1)S(1)}, bf16[192,512]{1,0:T(8,128)(2,1)S(1)}, u32[]{:S(2)}, u32[]{:S(2)}) collective-permute-start(bf16[192,512]{1,0:T(8,128)(2,1)S(1)} %get-tuple-element.46), channel_id=1, source_target_pairs={{0,4},{2,6},{4,0},{6,2},{8,12},{10,14},{12,8},{14,10},{1,5},{3,7},... | collective-permute-start | bytes 589832 | tf_op jit(solution)/shard_map/ppermute | solution.py:316
  10.7 2.6 %collective-permute-start.10 = (bf16[192,512]{1,0:T(8,128)(2,1)S(1)}, bf16[192,512]{1,0:T(8,128)(2,1)S(1)}, u32[]{:S(2)}, u32[]{:S(2)}) collective-permute-start(bf16[192,512]{1,0:T(8,128)(2,1)S(1)} %get-tuple-element.45), channel_id=1, source_target_pairs={{0,8},{2,10},{4,12},{6,14},{8,0},{10,2},{12,4},{14,6},{1,9},{3,11}... | collective-permute-start | bytes 589832 | tf_op jit(solution)/shard_map/ppermute | solution.py:316
  13.3 1.1 %collective-permute-done.4.q_ref = bf16[192,512]{1,0:T(8,128)(2,1)S(1)} collective-permute-done((bf16[192,512]{1,0:T(8,128)(2,1)S(1)}, bf16[192,512]{1,0:T(8,128)(2,1)S(1)}, u32[]{:S(2)}, u32[]{:S(2)}) %collective-permute-start.4) | collective-permute-done | bytes 196640 | tf_op jit(solution)/shard_map/ppermute | solution.py:311
  14.4 2.2 %load.1 = (bf16[1024,1024]{1,0:T(8,128)(2,1)S(1)}, bf16[1024,1024]{1,0:T(8,128)(2,1)S(1)}) custom-call(bf16[1024,1024]{1,0:T(8,128)(2,1)} %in_in.1, bf16[1024,1024]{1,0:T(8,128)(2,1)} %out_in.1), custom_call_target="tpu_custom_call" | custom-call | tf_op jit(solution)/shard_map/load/pallas_call | solution.py:25
  16.6 3.3 %collective-permute-done.12.refs_0_ = bf16[192,512]{1,0:T(8,128)(2,1)S(1)} collective-permute-done((bf16[192,512]{1,0:T(8,128)(2,1)S(1)}, bf16[192,512]{1,0:T(8,128)(2,1)S(1)}, u32[]{:S(2)}, u32[]{:S(2)}) %collective-permute-start.12) | collective-permute-done | bytes 196640 | tf_op jit(solution)/shard_map/ppermute | solution.py:316
  19.9 0.4 collective-permute-start.13
  20.3 2.0 %collective-permute-done.10.p_ref = bf16[192,512]{1,0:T(8,128)(2,1)S(1)} collective-permute-done((bf16[192,512]{1,0:T(8,128)(2,1)S(1)}, bf16[192,512]{1,0:T(8,128)(2,1)S(1)}, u32[]{:S(2)}, u32[]{:S(2)}) %collective-permute-start.10) | collective-permute-done | bytes 196640 | tf_op jit(solution)/shard_map/ppermute | solution.py:316
  22.3 0.5 collective-permute-start.11
  22.8 2.5 %collective-permute-start.8 = (bf16[192,512]{1,0:T(8,128)(2,1)S(1)}, bf16[192,512]{1,0:T(8,128)(2,1)S(1)}, u32[]{:S(2)}, u32[]{:S(2)}) collective-permute-start(bf16[192,512]{1,0:T(8,128)(2,1)S(1)} %get-tuple-element.44), channel_id=1, source_target_pairs={{0,12},{2,14},{4,8},{6,10},{8,4},{10,6},{12,0},{14,2},{1,13},{3,15... | collective-permute-start | bytes 589832 | tf_op jit(solution)/shard_map/ppermute | solution.py:316
  25.3 0.0 collective-permute-done.5.p2_ref
  25.3 0.0 collective-permute-done.6.q2_ref
  25.3 1.8 %expert.4 = (f32[2,192,512]{2,1,0:T(8,128)S(1)}, bf16[2,192,512]{2,1,0:T(8,128)(2,1)S(1)}) custom-call(s32[1]{0:T(128)} %bitcast.core_ref, bf16[192,512]{1,0:T(8,128)(2,1)S(1)} %get-tuple-element.39.p_ref, bf16[192,512]{1,0:T(8,128)(2,1)S(1)} %collective-permute-done.4.q_ref, bf16[192,512]{1,0:T(8,128)(2,1)S(1)} %collective-permute-done.5.p2_ref, ...), custom_call_target="tpu_custom_call" | custom-call | tf_op jit(solution)/shard_map/expert/pallas_call | solution.py:25
  27.1 0.1 collective-permute-start.7
  27.2 0.3 collective-permute-done.13.refs_1_.q_ref
  27.5 2.1 %collective-permute-done.11.refs_0_ = bf16[192,512]{1,0:T(8,128)(2,1)S(1)} collective-permute-done((bf16[192,512]{1,0:T(8,128)(2,1)S(1)}, bf16[192,512]{1,0:T(8,128)(2,1)S(1)}, u32[]{:S(2)}, u32[]{:S(2)}) %collective-permute-start.11) | collective-permute-done | bytes 196640 | tf_op jit(solution)/shard_map/ppermute | solution.py:311
  29.6 0.5 collective-permute-start.14
  30.1 0.3 collective-permute-done.8.p_ref
  30.4 1.5 %collective-permute-start.9 = (bf16[192,512]{1,0:T(8,128)(2,1)S(1)}, bf16[192,512]{1,0:T(8,128)(2,1)S(1)}, u32[]{:S(2)}, u32[]{:S(2)}) collective-permute-start(bf16[192,512]{1,0:T(8,128)(2,1)S(1)} %collective-permute-done.8.p_ref), channel_id=1, source_target_pairs={{0,2},{2,0},{4,6},{6,4},{8,10},{10,8},{12,14},{14,12},{1,3},{3,1},... | collective-permute-start | bytes 589832 | tf_op jit(solution)/shard_map/ppermute | solution.py:311
  31.9 0.0 collective-permute-done.14.p2_ref
  31.9 1.8 %expert.5 = (f32[2,192,512]{2,1,0:T(8,128)S(1)}, bf16[2,192,512]{2,1,0:T(8,128)(2,1)S(1)}) custom-call(s32[1]{0:T(128)} %bitcast.core_ref, bf16[192,512]{1,0:T(8,128)(2,1)S(1)} %collective-permute-done.10.p_ref, bf16[192,512]{1,0:T(8,128)(2,1)S(1)} %after.9.q_ref, bf16[192,512]{1,0:T(8,128)(2,1)S(1)} %collective-permute-done.14.p2_ref, ...), custom_call_target="tpu_custom_call" | custom-call | tf_op jit(solution)/shard_map/expert/pallas_call | solution.py:25
  33.8 0.1 collective-permute-start.18
  33.8 0.5 collective-permute-start.3
  34.3 0.1 collective-permute-start.22
  34.4 2.5 %collective-permute-done.9.refs_0_ = bf16[192,512]{1,0:T(8,128)(2,1)S(1)} collective-permute-done((bf16[192,512]{1,0:T(8,128)(2,1)S(1)}, bf16[192,512]{1,0:T(8,128)(2,1)S(1)}, u32[]{:S(2)}, u32[]{:S(2)}) %collective-permute-start.9) | collective-permute-done | bytes 196640 | tf_op jit(solution)/shard_map/ppermute | solution.py:311
  36.9 0.0 collective-permute-done.7
  36.9 0.5 collective-permute-start.23
  37.4 0.1 convert_add_fusion.3
  37.5 0.0 collective-permute-done.18
  37.6 0.1 collective-permute-start.17
  37.7 0.1 convert_add_fusion.2
  37.8 1.2 %collective-permute-done.17.refs_0_ = bf16[192,512]{1,0:T(8,128)(2,1)S(1)} collective-permute-done((bf16[192,512]{1,0:T(8,128)(2,1)S(1)}, bf16[192,512]{1,0:T(8,128)(2,1)S(1)}, u32[]{:S(2)}, u32[]{:S(2)}) %collective-permute-start.17) | collective-permute-done | bytes 196640 | tf_op jit(solution)/shard_map/ppermute | solution.py:306
  39.1 0.9 %collective-permute-start.27 = (bf16[192,512]{1,0:T(8,128)(2,1)S(1)}, bf16[192,512]{1,0:T(8,128)(2,1)S(1)}, u32[]{:S(2)}, u32[]{:S(2)}) collective-permute-start(bf16[192,512]{1,0:T(8,128)(2,1)S(1)} %fusion.9.refs_1_), channel_id=1, source_target_pairs={{0,2},{2,0},{4,6},{6,4},{8,10},{10,8},{12,14},{14,12},{1,3},{3,1},... | collective-permute-start | bytes 589832 | tf_op jit(solution)/shard_map/ppermute | solution.py:311
  39.9 0.0 collective-permute-done.16.p2_ref
  39.9 1.8 %expert.6 = (f32[2,192,512]{2,1,0:T(8,128)S(1)}, bf16[2,192,512]{2,1,0:T(8,128)(2,1)S(1)}) custom-call(s32[1]{0:T(128)} %bitcast.core_ref, bf16[192,512]{1,0:T(8,128)(2,1)S(1)} %collective-permute-done.8.p_ref, bf16[192,512]{1,0:T(8,128)(2,1)S(1)} %after.11.q_ref, bf16[192,512]{1,0:T(8,128)(2,1)S(1)} %collective-permute-done.16.p2_ref, ...), custom_call_target="tpu_custom_call" | custom-call | tf_op jit(solution)/shard_map/expert/pallas_call | solution.py:25
  41.8 0.1 collective-permute-start.19
  41.9 1.8 %expert.7 = (f32[2,192,512]{2,1,0:T(8,128)S(1)}, bf16[2,192,512]{2,1,0:T(8,128)(2,1)S(1)}) custom-call(s32[1]{0:T(128)} %bitcast.core_ref, bf16[192,512]{1,0:T(8,128)(2,1)S(1)} %after.8.p_ref, bf16[192,512]{1,0:T(8,128)(2,1)S(1)} %collective-permute-done.13.refs_1_.q_ref, bf16[192,512]{1,0:T(8,128)(2,1)S(1)} %collective-permute-done.22.p2_ref, ...), custom_call_target="tpu_custom_call" | custom-call | tf_op jit(solution)/shard_map/expert/pallas_call | solution.py:25
  43.8 0.6 collective-permute-start.24
  44.3 1.7 %collective-permute-done.27 = bf16[192,512]{1,0:T(8,128)(2,1)S(1)} collective-permute-done((bf16[192,512]{1,0:T(8,128)(2,1)S(1)}, bf16[192,512]{1,0:T(8,128)(2,1)S(1)}, u32[]{:S(2)}, u32[]{:S(2)}) %collective-permute-start.27) | collective-permute-done | bytes 196640 | tf_op jit(solution)/shard_map/ppermute | solution.py:311
  46.0 0.1 fusion.1
  46.1 1.7 %collective-permute-start.28 = (bf16[192,512]{1,0:T(8,128)(2,1)S(1)}, bf16[192,512]{1,0:T(8,128)(2,1)S(1)}, u32[]{:S(2)}, u32[]{:S(2)}) collective-permute-start(bf16[192,512]{1,0:T(8,128)(2,1)S(1)} %fusion.1), channel_id=1, source_target_pairs={{0,8},{2,10},{4,12},{6,14},{8,0},{10,2},{12,4},{14,6},{1,9},{3,11}... | collective-permute-start | bytes 589832 | tf_op jit(solution)/shard_map/ppermute | solution.py:316
  47.7 0.1 convert_add_fusion.1
  47.9 1.6 %collective-permute-start.20 = (bf16[192,512]{1,0:T(8,128)(2,1)S(1)}, bf16[192,512]{1,0:T(8,128)(2,1)S(1)}, u32[]{:S(2)}, u32[]{:S(2)}) collective-permute-start(bf16[192,512]{1,0:T(8,128)(2,1)S(1)} %fusion.10.refs_1_), channel_id=1, source_target_pairs={{0,2},{2,0},{4,6},{6,4},{8,10},{10,8},{12,14},{14,12},{1,3},{3,1},... | collective-permute-start | bytes 589832 | tf_op jit(solution)/shard_map/ppermute | solution.py:311
  49.5 0.1 convert_add_fusion
  49.6 0.6 collective-permute-start.25
  50.2 5.6 %collective-permute-done.20 = bf16[192,512]{1,0:T(8,128)(2,1)S(1)} collective-permute-done((bf16[192,512]{1,0:T(8,128)(2,1)S(1)}, bf16[192,512]{1,0:T(8,128)(2,1)S(1)}, u32[]{:S(2)}, u32[]{:S(2)}) %collective-permute-start.20) | collective-permute-done | bytes 196640 | tf_op jit(solution)/shard_map/ppermute | solution.py:311
  55.8 3.2 %collective-permute-start.29 = (bf16[192,512]{1,0:T(8,128)(2,1)S(1)}, bf16[192,512]{1,0:T(8,128)(2,1)S(1)}, u32[]{:S(2)}, u32[]{:S(2)}) collective-permute-start(bf16[192,512]{1,0:T(8,128)(2,1)S(1)} %fusion.5.refs_1_), channel_id=1, source_target_pairs={{0,12},{2,14},{4,8},{6,10},{8,4},{10,6},{12,0},{14,2},{1,13},{3,15... | collective-permute-start | bytes 589832 | tf_op jit(solution)/shard_map/ppermute | solution.py:316
  59.0 1.5 %collective-permute-start.21 = (bf16[192,512]{1,0:T(8,128)(2,1)S(1)}, bf16[192,512]{1,0:T(8,128)(2,1)S(1)}, u32[]{:S(2)}, u32[]{:S(2)}) collective-permute-start(bf16[192,512]{1,0:T(8,128)(2,1)S(1)} %after.13), channel_id=1, source_target_pairs={{0,2},{2,0},{4,6},{6,4},{8,10},{10,8},{12,14},{14,12},{1,3},{3,1},... | collective-permute-start | bytes 589832 | tf_op jit(solution)/shard_map/ppermute | solution.py:311
  60.6 1.4 %collective-permute-start.26 = (bf16[192,512]{1,0:T(8,128)(2,1)S(1)}, bf16[192,512]{1,0:T(8,128)(2,1)S(1)}, u32[]{:S(2)}, u32[]{:S(2)}) collective-permute-start(bf16[192,512]{1,0:T(8,128)(2,1)S(1)} %fusion.3), channel_id=1, source_target_pairs={{0,4},{2,6},{4,0},{6,2},{8,12},{10,14},{12,8},{14,10},{1,5},{3,7},... | collective-permute-start | bytes 589832 | tf_op jit(solution)/shard_map/ppermute | solution.py:316
  61.9 2.7 %collective-permute-done.21 = bf16[192,512]{1,0:T(8,128)(2,1)S(1)} collective-permute-done((bf16[192,512]{1,0:T(8,128)(2,1)S(1)}, bf16[192,512]{1,0:T(8,128)(2,1)S(1)}, u32[]{:S(2)}, u32[]{:S(2)}) %collective-permute-start.21) | collective-permute-done | bytes 196640 | tf_op jit(solution)/shard_map/ppermute | solution.py:311
  64.7 1.9 %collective-permute-done.26.rest_1_ = bf16[192,512]{1,0:T(8,128)(2,1)S(1)} collective-permute-done((bf16[192,512]{1,0:T(8,128)(2,1)S(1)}, bf16[192,512]{1,0:T(8,128)(2,1)S(1)}, u32[]{:S(2)}, u32[]{:S(2)}) %collective-permute-start.26) | collective-permute-done | bytes 196640 | tf_op jit(solution)/shard_map/ppermute | solution.py:316
  66.6 0.5 combine_other.1
  67.1 0.1 collective-permute-start.30
  67.2 0.5 combine_own.1.own_ref
  67.7 0.8 %collective-permute-done.30.other_ref = bf16[128,512]{1,0:T(8,128)(2,1)S(1)} collective-permute-done((bf16[128,512]{1,0:T(8,128)(2,1)S(1)}, bf16[128,512]{1,0:T(8,128)(2,1)S(1)}, u32[]{:S(2)}, u32[]{:S(2)}) %collective-permute-start.30) | collective-permute-done | bytes 131104 | tf_op jit(solution)/shard_map/ppermute | solution.py:306
  68.5 0.7 %finish.1 = bf16[128,1024]{1,0:T(8,128)(2,1)} custom-call(s32[1]{0:T(128)} %bitcast.core_ref, bf16[128,1024]{1,0:T(8,128)(2,1)S(1)} %get-tuple-element.33.state_ref, bf16[128,512]{1,0:T(8,128)(2,1)S(1)} %combine_own.1.own_ref, bf16[128,512]{1,0:T(8,128)(2,1)S(1)} %collective-permute-done.30.other_ref), custom_call_target="tpu_custom_call" | custom-call | tf_op jit(solution)/shard_map/finish/pallas_call | solution.py:25
  (29 shorter events, 0.3 us)
Async XLA Ops:
  0.0 2.9 %collective-permute-start = (bf16[2,80,512]{2,1,0:T(8,128)(2,1)}, bf16[2,80,512]{2,1,0:T(8,128)(2,1)S(1)}, u32[]{:S(2)}, u32[]{:S(2)}) collective-permute-start(bf16[2,80,512]{2,1,0:T(8,128)(2,1)} %keys_in.1), channel_id=1, source_target_pairs={{0,1},{1,0},{2,3},{3,2},{4,5},{5,4},{6,7},{7,6},{8,9},{9,8},{10,11... | collective-permute-start | bytes 491528 | tf_op jit(solution)/shard_map/ppermute | solution.py:306
  0.5 2.5 %collective-permute-start.1 = (bf16[2,80,512]{2,1,0:T(8,128)(2,1)}, bf16[2,80,512]{2,1,0:T(8,128)(2,1)S(1)}, u32[]{:S(2)}, u32[]{:S(2)}) collective-permute-start(bf16[2,80,512]{2,1,0:T(8,128)(2,1)} %values_in.1), channel_id=1, source_target_pairs={{0,1},{1,0},{2,3},{3,2},{4,5},{5,4},{6,7},{7,6},{8,9},{9,8},{10,11... | collective-permute-start | bytes 491528 | tf_op jit(solution)/shard_map/ppermute | solution.py:306
  4.2 1.5 %collective-permute-start.2 = (bf16[128,512]{1,0:T(8,128)(2,1)S(1)}, bf16[128,512]{1,0:T(8,128)(2,1)S(1)}, u32[]{:S(2)}, u32[]{:S(2)}) collective-permute-start(bf16[128,512]{1,0:T(8,128)(2,1)S(1)} %get-tuple-element.37), channel_id=1, source_target_pairs={{0,1},{1,0},{2,3},{3,2},{4,5},{5,4},{6,7},{7,6},{8,9},{9,8},{10,11... | collective-permute-start | bytes 393224 | tf_op jit(solution)/shard_map/ppermute | solution.py:306
  6.2 8.1 %collective-permute-start.4 = (bf16[192,512]{1,0:T(8,128)(2,1)S(1)}, bf16[192,512]{1,0:T(8,128)(2,1)S(1)}, u32[]{:S(2)}, u32[]{:S(2)}) collective-permute-start(bf16[192,512]{1,0:T(8,128)(2,1)S(1)} %get-tuple-element.39.p_ref), channel_id=1, source_target_pairs={{0,2},{2,0},{4,6},{6,4},{8,10},{10,8},{12,14},{14,12},{1,3},{3,1},... | collective-permute-start | bytes 589832 | tf_op jit(solution)/shard_map/ppermute | solution.py:311
  9.2 10.8 %collective-permute-start.12 = (bf16[192,512]{1,0:T(8,128)(2,1)S(1)}, bf16[192,512]{1,0:T(8,128)(2,1)S(1)}, u32[]{:S(2)}, u32[]{:S(2)}) collective-permute-start(bf16[192,512]{1,0:T(8,128)(2,1)S(1)} %get-tuple-element.46), channel_id=1, source_target_pairs={{0,4},{2,6},{4,0},{6,2},{8,12},{10,14},{12,8},{14,10},{1,5},{3,7},... | collective-permute-start | bytes 589832 | tf_op jit(solution)/shard_map/ppermute | solution.py:316
  10.7 11.6 %collective-permute-start.10 = (bf16[192,512]{1,0:T(8,128)(2,1)S(1)}, bf16[192,512]{1,0:T(8,128)(2,1)S(1)}, u32[]{:S(2)}, u32[]{:S(2)}) collective-permute-start(bf16[192,512]{1,0:T(8,128)(2,1)S(1)} %get-tuple-element.45), channel_id=1, source_target_pairs={{0,8},{2,10},{4,12},{6,14},{8,0},{10,2},{12,4},{14,6},{1,9},{3,11}... | collective-permute-start | bytes 589832 | tf_op jit(solution)/shard_map/ppermute | solution.py:316
  13.3 12.0 %collective-permute-start.5 = (bf16[192,512]{1,0:T(8,128)(2,1)S(1)}, bf16[192,512]{1,0:T(8,128)(2,1)S(1)}, u32[]{:S(2)}, u32[]{:S(2)}) collective-permute-start(bf16[192,512]{1,0:T(8,128)(2,1)S(1)} %get-tuple-element.39.p_ref), channel_id=1, source_target_pairs={{0,1},{1,0},{2,3},{3,2},{4,5},{5,4},{6,7},{7,6},{8,9},{9,8},{10,11... | collective-permute-start | bytes 589832 | tf_op jit(solution)/shard_map/ppermute | solution.py:306
  14.4 10.9 %collective-permute-start.6 = (bf16[192,512]{1,0:T(8,128)(2,1)S(1)}, bf16[192,512]{1,0:T(8,128)(2,1)S(1)}, u32[]{:S(2)}, u32[]{:S(2)}) collective-permute-start(bf16[192,512]{1,0:T(8,128)(2,1)S(1)} %collective-permute-done.4.q_ref), channel_id=1, source_target_pairs={{0,1},{1,0},{2,3},{3,2},{4,5},{5,4},{6,7},{7,6},{8,9},{9,8},{10,11... | collective-permute-start | bytes 589832 | tf_op jit(solution)/shard_map/ppermute | solution.py:306
  19.9 7.6 %collective-permute-start.13 = (bf16[192,512]{1,0:T(8,128)(2,1)S(1)}, bf16[192,512]{1,0:T(8,128)(2,1)S(1)}, u32[]{:S(2)}, u32[]{:S(2)}) collective-permute-start(bf16[192,512]{1,0:T(8,128)(2,1)S(1)} %after.8.p_ref), channel_id=1, source_target_pairs={{0,2},{2,0},{4,6},{6,4},{8,10},{10,8},{12,14},{14,12},{1,3},{3,1},... | collective-permute-start | bytes 589832 | tf_op jit(solution)/shard_map/ppermute | solution.py:311
  22.3 7.3 %collective-permute-start.11 = (bf16[192,512]{1,0:T(8,128)(2,1)S(1)}, bf16[192,512]{1,0:T(8,128)(2,1)S(1)}, u32[]{:S(2)}, u32[]{:S(2)}) collective-permute-start(bf16[192,512]{1,0:T(8,128)(2,1)S(1)} %collective-permute-done.10.p_ref), channel_id=1, source_target_pairs={{0,2},{2,0},{4,6},{6,4},{8,10},{10,8},{12,14},{14,12},{1,3},{3,1},... | collective-permute-start | bytes 589832 | tf_op jit(solution)/shard_map/ppermute | solution.py:311
  22.8 7.6 %collective-permute-start.8 = (bf16[192,512]{1,0:T(8,128)(2,1)S(1)}, bf16[192,512]{1,0:T(8,128)(2,1)S(1)}, u32[]{:S(2)}, u32[]{:S(2)}) collective-permute-start(bf16[192,512]{1,0:T(8,128)(2,1)S(1)} %get-tuple-element.44), channel_id=1, source_target_pairs={{0,12},{2,14},{4,8},{6,10},{8,4},{10,6},{12,0},{14,2},{1,13},{3,15... | collective-permute-start | bytes 589832 | tf_op jit(solution)/shard_map/ppermute | solution.py:316
  27.1 9.8 %collective-permute-start.7 = (bf16[2,192,512]{2,1,0:T(8,128)(2,1)S(1)}, bf16[2,192,512]{2,1,0:T(8,128)(2,1)S(1)}, u32[]{:S(2)}, u32[]{:S(2)}) collective-permute-start(bf16[2,192,512]{2,1,0:T(8,128)(2,1)S(1)} %get-tuple-element.43), channel_id=1, source_target_pairs={{0,1},{1,0},{2,3},{3,2},{4,5},{5,4},{6,7},{7,6},{8,9},{9,8},{10,11... | collective-permute-start | bytes 1179656 | tf_op jit(solution)/shard_map/ppermute | solution.py:306
  29.6 2.3 %collective-permute-start.15 = (bf16[192,512]{1,0:T(8,128)(2,1)S(1)}, bf16[192,512]{1,0:T(8,128)(2,1)S(1)}, u32[]{:S(2)}, u32[]{:S(2)}) collective-permute-start(bf16[192,512]{1,0:T(8,128)(2,1)S(1)} %after.9.q_ref), channel_id=1, source_target_pairs={{0,1},{1,0},{2,3},{3,2},{4,5},{5,4},{6,7},{7,6},{8,9},{9,8},{10,11... | collective-permute-start | bytes 589832 | tf_op jit(solution)/shard_map/ppermute | solution.py:306
  29.6 2.3 %collective-permute-start.14 = (bf16[192,512]{1,0:T(8,128)(2,1)S(1)}, bf16[192,512]{1,0:T(8,128)(2,1)S(1)}, u32[]{:S(2)}, u32[]{:S(2)}) collective-permute-start(bf16[192,512]{1,0:T(8,128)(2,1)S(1)} %collective-permute-done.10.p_ref), channel_id=1, source_target_pairs={{0,1},{1,0},{2,3},{3,2},{4,5},{5,4},{6,7},{7,6},{8,9},{9,8},{10,11... | collective-permute-start | bytes 589832 | tf_op jit(solution)/shard_map/ppermute | solution.py:306
  30.4 6.5 %collective-permute-start.9 = (bf16[192,512]{1,0:T(8,128)(2,1)S(1)}, bf16[192,512]{1,0:T(8,128)(2,1)S(1)}, u32[]{:S(2)}, u32[]{:S(2)}) collective-permute-start(bf16[192,512]{1,0:T(8,128)(2,1)S(1)} %collective-permute-done.8.p_ref), channel_id=1, source_target_pairs={{0,2},{2,0},{4,6},{6,4},{8,10},{10,8},{12,14},{14,12},{1,3},{3,1},... | collective-permute-start | bytes 589832 | tf_op jit(solution)/shard_map/ppermute | solution.py:311
  33.8 3.8 %collective-permute-start.18 = (bf16[2,192,512]{2,1,0:T(8,128)(2,1)S(1)}, bf16[2,192,512]{2,1,0:T(8,128)(2,1)S(1)}, u32[]{:S(2)}, u32[]{:S(2)}) collective-permute-start(bf16[2,192,512]{2,1,0:T(8,128)(2,1)S(1)} %get-tuple-element.48), channel_id=1, source_target_pairs={{0,1},{1,0},{2,3},{3,2},{4,5},{5,4},{6,7},{7,6},{8,9},{9,8},{10,11... | collective-permute-start | bytes 1179656 | tf_op jit(solution)/shard_map/ppermute | solution.py:306
  33.8 30.9 %collective-permute-start.3 = (f32[2,128]{1,0:T(2,128)S(1)}, f32[2,128]{1,0:T(2,128)S(1)}, u32[]{:S(2)}, u32[]{:S(2)}) collective-permute-start(f32[2,128]{1,0:T(2,128)S(1)} %get-tuple-element.35.gates_ref), channel_id=1, source_target_pairs={{0,1},{1,0},{2,3},{3,2},{4,5},{5,4},{6,7},{7,6},{8,9},{9,8},{10,11... | collective-permute-start | bytes 3080 | tf_op jit(solution)/shard_map/ppermute | solution.py:306
  34.3 7.6 %collective-permute-start.22 = (bf16[192,512]{1,0:T(8,128)(2,1)S(1)}, bf16[192,512]{1,0:T(8,128)(2,1)S(1)}, u32[]{:S(2)}, u32[]{:S(2)}) collective-permute-start(bf16[192,512]{1,0:T(8,128)(2,1)S(1)} %after.8.p_ref), channel_id=1, source_target_pairs={{0,1},{1,0},{2,3},{3,2},{4,5},{5,4},{6,7},{7,6},{8,9},{9,8},{10,11... | collective-permute-start | bytes 589832 | tf_op jit(solution)/shard_map/ppermute | solution.py:306
  36.9 3.0 %collective-permute-start.16 = (bf16[192,512]{1,0:T(8,128)(2,1)S(1)}, bf16[192,512]{1,0:T(8,128)(2,1)S(1)}, u32[]{:S(2)}, u32[]{:S(2)}) collective-permute-start(bf16[192,512]{1,0:T(8,128)(2,1)S(1)} %collective-permute-done.8.p_ref), channel_id=1, source_target_pairs={{0,1},{1,0},{2,3},{3,2},{4,5},{5,4},{6,7},{7,6},{8,9},{9,8},{10,11... | collective-permute-start | bytes 589832 | tf_op jit(solution)/shard_map/ppermute | solution.py:306
  36.9 5.0 %collective-permute-start.23 = (bf16[192,512]{1,0:T(8,128)(2,1)S(1)}, bf16[192,512]{1,0:T(8,128)(2,1)S(1)}, u32[]{:S(2)}, u32[]{:S(2)}) collective-permute-start(bf16[192,512]{1,0:T(8,128)(2,1)S(1)} %collective-permute-done.13.refs_1_.q_ref), channel_id=1, source_target_pairs={{0,1},{1,0},{2,3},{3,2},{4,5},{5,4},{6,7},{7,6},{8,9},{9,8},{10,11... | collective-permute-start | bytes 589832 | tf_op jit(solution)/shard_map/ppermute | solution.py:306
  37.6 1.5 %collective-permute-start.17 = (bf16[192,512]{1,0:T(8,128)(2,1)S(1)}, bf16[192,512]{1,0:T(8,128)(2,1)S(1)}, u32[]{:S(2)}, u32[]{:S(2)}) collective-permute-start(bf16[192,512]{1,0:T(8,128)(2,1)S(1)} %after.11.q_ref), channel_id=1, source_target_pairs={{0,1},{1,0},{2,3},{3,2},{4,5},{5,4},{6,7},{7,6},{8,9},{9,8},{10,11... | collective-permute-start | bytes 589832 | tf_op jit(solution)/shard_map/ppermute | solution.py:306
  39.1 6.9 %collective-permute-start.27 = (bf16[192,512]{1,0:T(8,128)(2,1)S(1)}, bf16[192,512]{1,0:T(8,128)(2,1)S(1)}, u32[]{:S(2)}, u32[]{:S(2)}) collective-permute-start(bf16[192,512]{1,0:T(8,128)(2,1)S(1)} %fusion.9.refs_1_), channel_id=1, source_target_pairs={{0,2},{2,0},{4,6},{6,4},{8,10},{10,8},{12,14},{14,12},{1,3},{3,1},... | collective-permute-start | bytes 589832 | tf_op jit(solution)/shard_map/ppermute | solution.py:311
  41.8 6.0 %collective-permute-start.19 = (bf16[2,192,512]{2,1,0:T(8,128)(2,1)S(1)}, bf16[2,192,512]{2,1,0:T(8,128)(2,1)S(1)}, u32[]{:S(2)}, u32[]{:S(2)}) collective-permute-start(bf16[2,192,512]{2,1,0:T(8,128)(2,1)S(1)} %get-tuple-element.50), channel_id=1, source_target_pairs={{0,1},{1,0},{2,3},{3,2},{4,5},{5,4},{6,7},{7,6},{8,9},{9,8},{10,11... | collective-permute-start | bytes 1179656 | tf_op jit(solution)/shard_map/ppermute | solution.py:306
  43.8 5.7 %collective-permute-start.24 = (bf16[2,192,512]{2,1,0:T(8,128)(2,1)S(1)}, bf16[2,192,512]{2,1,0:T(8,128)(2,1)S(1)}, u32[]{:S(2)}, u32[]{:S(2)}) collective-permute-start(bf16[2,192,512]{2,1,0:T(8,128)(2,1)S(1)} %get-tuple-element.52), channel_id=1, source_target_pairs={{0,1},{1,0},{2,3},{3,2},{4,5},{5,4},{6,7},{7,6},{8,9},{9,8},{10,11... | collective-permute-start | bytes 1179656 | tf_op jit(solution)/shard_map/ppermute | solution.py:306
  46.1 18.7 %collective-permute-start.28 = (bf16[192,512]{1,0:T(8,128)(2,1)S(1)}, bf16[192,512]{1,0:T(8,128)(2,1)S(1)}, u32[]{:S(2)}, u32[]{:S(2)}) collective-permute-start(bf16[192,512]{1,0:T(8,128)(2,1)S(1)} %fusion.1), channel_id=1, source_target_pairs={{0,8},{2,10},{4,12},{6,14},{8,0},{10,2},{12,4},{14,6},{1,9},{3,11}... | collective-permute-start | bytes 589832 | tf_op jit(solution)/shard_map/ppermute | solution.py:316
  47.9 7.9 %collective-permute-start.20 = (bf16[192,512]{1,0:T(8,128)(2,1)S(1)}, bf16[192,512]{1,0:T(8,128)(2,1)S(1)}, u32[]{:S(2)}, u32[]{:S(2)}) collective-permute-start(bf16[192,512]{1,0:T(8,128)(2,1)S(1)} %fusion.10.refs_1_), channel_id=1, source_target_pairs={{0,2},{2,0},{4,6},{6,4},{8,10},{10,8},{12,14},{14,12},{1,3},{3,1},... | collective-permute-start | bytes 589832 | tf_op jit(solution)/shard_map/ppermute | solution.py:311
  49.6 10.9 %collective-permute-start.25 = (bf16[192,512]{1,0:T(8,128)(2,1)S(1)}, bf16[192,512]{1,0:T(8,128)(2,1)S(1)}, u32[]{:S(2)}, u32[]{:S(2)}) collective-permute-start(bf16[192,512]{1,0:T(8,128)(2,1)S(1)} %after.15), channel_id=1, source_target_pairs={{0,2},{2,0},{4,6},{6,4},{8,10},{10,8},{12,14},{14,12},{1,3},{3,1},... | collective-permute-start | bytes 589832 | tf_op jit(solution)/shard_map/ppermute | solution.py:311
  55.8 10.8 %collective-permute-start.29 = (bf16[192,512]{1,0:T(8,128)(2,1)S(1)}, bf16[192,512]{1,0:T(8,128)(2,1)S(1)}, u32[]{:S(2)}, u32[]{:S(2)}) collective-permute-start(bf16[192,512]{1,0:T(8,128)(2,1)S(1)} %fusion.5.refs_1_), channel_id=1, source_target_pairs={{0,12},{2,14},{4,8},{6,10},{8,4},{10,6},{12,0},{14,2},{1,13},{3,15... | collective-permute-start | bytes 589832 | tf_op jit(solution)/shard_map/ppermute | solution.py:316
  59.0 5.7 %collective-permute-start.21 = (bf16[192,512]{1,0:T(8,128)(2,1)S(1)}, bf16[192,512]{1,0:T(8,128)(2,1)S(1)}, u32[]{:S(2)}, u32[]{:S(2)}) collective-permute-start(bf16[192,512]{1,0:T(8,128)(2,1)S(1)} %after.13), channel_id=1, source_target_pairs={{0,2},{2,0},{4,6},{6,4},{8,10},{10,8},{12,14},{14,12},{1,3},{3,1},... | collective-permute-start | bytes 589832 | tf_op jit(solution)/shard_map/ppermute | solution.py:311
  60.6 6.0 %collective-permute-start.26 = (bf16[192,512]{1,0:T(8,128)(2,1)S(1)}, bf16[192,512]{1,0:T(8,128)(2,1)S(1)}, u32[]{:S(2)}, u32[]{:S(2)}) collective-permute-start(bf16[192,512]{1,0:T(8,128)(2,1)S(1)} %fusion.3), channel_id=1, source_target_pairs={{0,4},{2,6},{4,0},{6,2},{8,12},{10,14},{12,8},{14,10},{1,5},{3,7},... | collective-permute-start | bytes 589832 | tf_op jit(solution)/shard_map/ppermute | solution.py:316
  67.1 1.4 %collective-permute-start.30 = (bf16[128,512]{1,0:T(8,128)(2,1)S(1)}, bf16[128,512]{1,0:T(8,128)(2,1)S(1)}, u32[]{:S(2)}, u32[]{:S(2)}) collective-permute-start(bf16[128,512]{1,0:T(8,128)(2,1)S(1)} %get-tuple-element.54), channel_id=1, source_target_pairs={{0,1},{1,0},{2,3},{3,2},{4,5},{5,4},{6,7},{7,6},{8,9},{9,8},{10,11... | collective-permute-start | bytes 393224 | tf_op jit(solution)/shard_map/ppermute | solution.py:306

commit v22 on v17

--- a/solution.py
+++ b/solution.py
@@ -430,10 +430,10 @@
     q = swap_owner(p)
     ps[0], qs[0] = p, q
     p = travelling[0]
-    p = after(p, near_in)
     q = swap_owner(p)
     ps[1], qs[1] = p, q
     p = travelling[1]
+    p = after(p, near_in)
     q = swap_owner(p)
     ps[2], qs[2] = p, q
     p = travelling[2]
@@ -445,17 +445,17 @@
     boths[0], halves[0] = sums(kept[0], moving)
     p, q = ps[2], qs[2]
     p2, q2 = swap(p), swap(q)
+    q2 = after(q2, kept[0])
     kept[2], moving = run(p, q, p2, q2)
     boths[2], halves[2] = sums(kept[2], moving)
     p, q = ps[1], qs[1]
     p2, q2 = swap(p), swap(q)
-    q2 = after(q2, kept[0], kept[2])
     kept[1], moving = run(p, q, p2, q2)
     boths[1], halves[1] = sums(kept[1], moving)
     p, q = ps[3], qs[3]
     q = after(q, kept[2])
     p2, q2 = swap(p), swap(q)
-    q2 = after(q2, halves[2], kept[1])
+    q2 = after(q2, kept[1], halves[2])
     kept[3], moving = run(p, q, p2, q2)
     boths[3], halves[3] = sums(kept[3], moving)
     leaving = halves[2]

time: 68.9 us -> 69.5 us (level)
  waiting for transfers between devices: 22.7 us -> 26.2 us
  starting transfers between devices: 29.6 us -> 26.6 us
    ppermute x6, waiting for transfers between devices: 8.22 us -> 11.2 us  [exchange(): lax.ppermute(values, 'expert', [(i, i ^ 2 * offset) for i in range(owners)])]
    ppermute x8, starting transfers between devices: 9.14 us -> 7.37 us  [swap_owner(): return lax.ppermute(values, 'expert', [(i, i ^ 1) for i in range(owners)])]
    ppermute x6, starting transfers between devices: 16.8 us -> 15.4 us  [exchange(): lax.ppermute(values, 'expert', [(i, i ^ 2 * offset) for i in range(owners)])]
where the time goes in v22:
time: 69.5 us; the launch traced here: 69.3 us
  starting transfers between devices  26.6 us (38%)
  waiting for transfers between devices  26.2 us (38%)
  Pallas kernels  14.9 us (21%)
  between operations  0.88 us (1%)
    ppermute x6, starting transfers between devices, exchange(): lax.ppermute(values, 'expert', [(i, i ^ 2 * offset) for i in range(owners)])  15.4 us
    pallas_call x11, Pallas kernels, call(): pl.pallas_call(kernel, out_shape=tuple((jax.ShapeDtypeStruct(*out) for ou...  14.9 us
    ppermute x6, waiting for transfers between devices, exchange(): lax.ppermute(values, 'expert', [(i, i ^ 2 * offset) for i in range(owners)])  11.2 us
    ppermute x8, waiting for transfers between devices, swap_owner(): return lax.ppermute(values, 'expert', [(i, i ^ 1) for i in range(owners)])  11.2 us
    ppermute x8, starting transfers between devices, swap_owner(): return lax.ppermute(values, 'expert', [(i, i ^ 1) for i in range(owners)])  7.37 us
    ppermute x17, waiting for transfers between devices, swap(): return lax.ppermute(values, 'section', [(0, 1), (1, 0)])  3.82 us
    ppermute x17, starting transfers between devices, swap(): return lax.ppermute(values, 'section', [(0, 1), (1, 0)])  3.8 us
  transfers between devices with their start and end apart: 31, of which 14 were waited for; matrix products, arithmetic and copies ran while one was open for 1% of the time, Pallas kernels for 17%

profile of v22, /device:TPU:0, one launch (start us, length us, event | category | flops | bytes accessed | tf_op | source)
XLA Modules:
  0.0 69.3 jit_solution(17759450072584527991)
XLA Ops:
  0.0 0.5 collective-permute-start
  0.5 0.1 collective-permute-start.1
  1.2 1.8 %attend_own.1 = (bf16[128,512]{1,0:T(8,128)(2,1)S(1)}, bf16[128,512]{1,0:T(8,128)(2,1)S(1)}, bf16[128,512]{1,0:T(8,128)(2,1)S(1)}) custom-call(s32[1]{0:T(128)} %bitcast.core_ref, s32[1]{0:T(128)S(6)} %copy.24.source_ref, bf16[1,128,1024]{2,1,0:T(8,128)(2,1)} %x_in.1, f32[1,1024]{1,0:T(1,128)} %bitcast.40, bf16[2,80,512]{2,1,0:T(8,128)(2,1)} %keys_in.1, ...), custom_call_target="tpu_custom_call" | custom-call | tf_op jit(solution)/shard_map/attend_own/pallas_call | solution.py:25
  2.9 0.0 collective-permute-done.1.values_ref
  3.0 1.2 %attend_other.1 = (bf16[128,1024]{1,0:T(8,128)(2,1)S(1)}, bf16[128,512]{1,0:T(8,128)(2,1)S(1)}, bf16[128,512]{1,0:T(8,128)(2,1)S(1)}, f32[2,128]{1,0:T(2,128)S(1)}, s32[2,2,128]{2,1,0:T(2,128)S(1)}) custom-call(s32[1]{0:T(128)} %bitcast.core_ref, s32[1]{0:T(128)S(6)} %copy.24.source_ref, bf16[128,512]{1,0:T(8,128)(2,1)S(1)} %get-tuple-element.30.own_ref, ...), custom_call_target="tpu_custom_call" | custom-call | tf_op jit(solution)/shard_map/attend_other/pallas_call | solution.py:25
  4.2 0.5 collective-permute-start.2
  4.7 1.0 %collective-permute-done.2.other_ref = bf16[128,512]{1,0:T(8,128)(2,1)S(1)} collective-permute-done((bf16[128,512]{1,0:T(8,128)(2,1)S(1)}, bf16[128,512]{1,0:T(8,128)(2,1)S(1)}, u32[]{:S(2)}, u32[]{:S(2)}) %collective-permute-start.2) | collective-permute-done | bytes 131104 | tf_op jit(solution)/shard_map/ppermute | solution.py:306
  5.7 0.5 select.5
  6.2 4.0 %collective-permute-start.10 = (bf16[192,512]{1,0:T(8,128)(2,1)S(1)}, bf16[192,512]{1,0:T(8,128)(2,1)S(1)}, u32[]{:S(2)}, u32[]{:S(2)}) collective-permute-start(bf16[192,512]{1,0:T(8,128)(2,1)S(1)} %get-tuple-element.45), channel_id=1, source_target_pairs={{0,8},{2,10},{4,12},{6,14},{8,0},{10,2},{12,4},{14,6},{1,9},{3,11}... | collective-permute-start | bytes 589832 | tf_op jit(solution)/shard_map/ppermute | solution.py:316
  10.2 1.5 %collective-permute-start.4 = (bf16[192,512]{1,0:T(8,128)(2,1)S(1)}, bf16[192,512]{1,0:T(8,128)(2,1)S(1)}, u32[]{:S(2)}, u32[]{:S(2)}) collective-permute-start(bf16[192,512]{1,0:T(8,128)(2,1)S(1)} %get-tuple-element.39.p_ref), channel_id=1, source_target_pairs={{0,2},{2,0},{4,6},{6,4},{8,10},{10,8},{12,14},{14,12},{1,3},{3,1},... | collective-permute-start | bytes 589832 | tf_op jit(solution)/shard_map/ppermute | solution.py:311
  11.7 2.2 %load.1 = (bf16[1024,1024]{1,0:T(8,128)(2,1)S(1)}, bf16[1024,1024]{1,0:T(8,128)(2,1)S(1)}) custom-call(bf16[1024,1024]{1,0:T(8,128)(2,1)} %in_in.1, bf16[1024,1024]{1,0:T(8,128)(2,1)} %out_in.1), custom_call_target="tpu_custom_call" | custom-call | tf_op jit(solution)/shard_map/load/pallas_call | solution.py:25
  14.0 1.6 %collective-permute-start.16 = (bf16[192,512]{1,0:T(8,128)(2,1)S(1)}, bf16[192,512]{1,0:T(8,128)(2,1)S(1)}, u32[]{:S(2)}, u32[]{:S(2)}) collective-permute-start(bf16[192,512]{1,0:T(8,128)(2,1)S(1)} %get-tuple-element.47), channel_id=1, source_target_pairs={{0,4},{2,6},{4,0},{6,2},{8,12},{10,14},{12,8},{14,10},{1,5},{3,7},... | collective-permute-start | bytes 589832 | tf_op jit(solution)/shard_map/ppermute | solution.py:316
  15.6 4.2 %collective-permute-done.10.refs_0_ = bf16[192,512]{1,0:T(8,128)(2,1)S(1)} collective-permute-done((bf16[192,512]{1,0:T(8,128)(2,1)S(1)}, bf16[192,512]{1,0:T(8,128)(2,1)S(1)}, u32[]{:S(2)}, u32[]{:S(2)}) %collective-permute-start.10) | collective-permute-done | bytes 196640 | tf_op jit(solution)/shard_map/ppermute | solution.py:316
  19.8 1.6 %collective-permute-start.11 = (bf16[192,512]{1,0:T(8,128)(2,1)S(1)}, bf16[192,512]{1,0:T(8,128)(2,1)S(1)}, u32[]{:S(2)}, u32[]{:S(2)}) collective-permute-start(bf16[192,512]{1,0:T(8,128)(2,1)S(1)} %after.6.p_ref), channel_id=1, source_target_pairs={{0,2},{2,0},{4,6},{6,4},{8,10},{10,8},{12,14},{14,12},{1,3},{3,1},... | collective-permute-start | bytes 589832 | tf_op jit(solution)/shard_map/ppermute | solution.py:311
  21.3 0.0 collective-permute-start.5
  21.3 0.0 collective-permute-done.4.q_ref
  21.3 0.5 collective-permute-start.6
  21.9 3.5 %collective-permute-start.8 = (bf16[192,512]{1,0:T(8,128)(2,1)S(1)}, bf16[192,512]{1,0:T(8,128)(2,1)S(1)}, u32[]{:S(2)}, u32[]{:S(2)}) collective-permute-start(bf16[192,512]{1,0:T(8,128)(2,1)S(1)} %get-tuple-element.44), channel_id=1, source_target_pairs={{0,12},{2,14},{4,8},{6,10},{8,4},{10,6},{12,0},{14,2},{1,13},{3,15... | collective-permute-start | bytes 589832 | tf_op jit(solution)/shard_map/ppermute | solution.py:316
  25.3 0.0 collective-permute-done.16.p_ref
  25.3 0.5 collective-permute-start.17
  25.9 0.3 collective-permute-done.11.q_ref
  26.2 0.0 collective-permute-start.13
  26.2 0.0 collective-permute-done.5.p2_ref
  26.2 0.0 collective-permute-done.6.q2_ref
  26.2 1.8 %expert.4 = (f32[2,192,512]{2,1,0:T(8,128)S(1)}, bf16[2,192,512]{2,1,0:T(8,128)(2,1)S(1)}) custom-call(s32[1]{0:T(128)} %bitcast.core_ref, bf16[192,512]{1,0:T(8,128)(2,1)S(1)} %get-tuple-element.39.p_ref, bf16[192,512]{1,0:T(8,128)(2,1)S(1)} %collective-permute-done.4.q_ref, bf16[192,512]{1,0:T(8,128)(2,1)S(1)} %collective-permute-done.5.p2_ref, ...), custom_call_target="tpu_custom_call" | custom-call | tf_op jit(solution)/shard_map/expert/pallas_call | solution.py:25
  28.0 0.6 collective-permute-start.7
  28.6 0.1 collective-permute-start.12
  28.7 1.9 %collective-permute-done.8.p_ref = bf16[192,512]{1,0:T(8,128)(2,1)S(1)} collective-permute-done((bf16[192,512]{1,0:T(8,128)(2,1)S(1)}, bf16[192,512]{1,0:T(8,128)(2,1)S(1)}, u32[]{:S(2)}, u32[]{:S(2)}) %collective-permute-start.8) | collective-permute-done | bytes 196640 | tf_op jit(solution)/shard_map/ppermute | solution.py:316
  30.6 1.3 %collective-permute-done.17.q_ref = bf16[192,512]{1,0:T(8,128)(2,1)S(1)} collective-permute-done((bf16[192,512]{1,0:T(8,128)(2,1)S(1)}, bf16[192,512]{1,0:T(8,128)(2,1)S(1)}, u32[]{:S(2)}, u32[]{:S(2)}) %collective-permute-start.17) | collective-permute-done | bytes 196640 | tf_op jit(solution)/shard_map/ppermute | solution.py:311
  31.9 0.5 collective-permute-start.9
  32.4 0.2 collective-permute-start.3
  32.6 1.8 %expert.5 = (f32[2,192,512]{2,1,0:T(8,128)S(1)}, bf16[2,192,512]{2,1,0:T(8,128)(2,1)S(1)}) custom-call(s32[1]{0:T(128)} %bitcast.core_ref, bf16[192,512]{1,0:T(8,128)(2,1)S(1)} %after.6.p_ref, bf16[192,512]{1,0:T(8,128)(2,1)S(1)} %collective-permute-done.11.q_ref, bf16[192,512]{1,0:T(8,128)(2,1)S(1)} %collective-permute-done.12.p2_ref, ...), custom_call_target="tpu_custom_call" | custom-call | tf_op jit(solution)/shard_map/expert/pallas_call | solution.py:25
  34.5 0.3 collective-permute-start.14
  34.9 0.2 collective-permute-start.20
  35.1 1.8 %expert.6 = (f32[2,192,512]{2,1,0:T(8,128)S(1)}, bf16[2,192,512]{2,1,0:T(8,128)(2,1)S(1)}) custom-call(s32[1]{0:T(128)} %bitcast.core_ref, bf16[192,512]{1,0:T(8,128)(2,1)S(1)} %collective-permute-done.16.p_ref, bf16[192,512]{1,0:T(8,128)(2,1)S(1)} %collective-permute-done.17.q_ref, bf16[192,512]{1,0:T(8,128)(2,1)S(1)} %collective-permute-done.18.p2_ref, ...), custom_call_target="tpu_custom_call" | custom-call | tf_op jit(solution)/shard_map/expert/pallas_call | solution.py:25
  36.9 2.3 %collective-permute-done.9.refs_0_ = bf16[192,512]{1,0:T(8,128)(2,1)S(1)} collective-permute-done((bf16[192,512]{1,0:T(8,128)(2,1)S(1)}, bf16[192,512]{1,0:T(8,128)(2,1)S(1)}, u32[]{:S(2)}, u32[]{:S(2)}) %collective-permute-start.9) | collective-permute-done | bytes 196640 | tf_op jit(solution)/shard_map/ppermute | solution.py:311
  39.2 0.5 collective-permute-start.15
  39.7 0.1 convert_add_fusion.3
  39.9 0.1 convert_add_fusion.2
  40.0 0.6 collective-permute-start.27
  40.6 0.6 collective-permute-done.15.refs_0_
  41.2 1.8 %expert.7 = (f32[2,192,512]{2,1,0:T(8,128)S(1)}, bf16[2,192,512]{2,1,0:T(8,128)(2,1)S(1)}) custom-call(s32[1]{0:T(128)} %bitcast.core_ref, bf16[192,512]{1,0:T(8,128)(2,1)S(1)} %collective-permute-done.8.p_ref, bf16[192,512]{1,0:T(8,128)(2,1)S(1)} %after.8.q_ref, bf16[192,512]{1,0:T(8,128)(2,1)S(1)} %collective-permute-done.14.p2_ref, ...), custom_call_target="tpu_custom_call" | custom-call | tf_op jit(solution)/shard_map/expert/pallas_call | solution.py:25
  43.0 0.2 collective-permute-start.21
  43.2 0.1 convert_add_fusion
  43.4 1.4 %collective-permute-done.21 = bf16[2,192,512]{2,1,0:T(8,128)(2,1)S(1)} collective-permute-done((bf16[2,192,512]{2,1,0:T(8,128)(2,1)S(1)}, bf16[2,192,512]{2,1,0:T(8,128)(2,1)S(1)}, u32[]{:S(2)}, u32[]{:S(2)}) %collective-permute-start.21) | collective-permute-done | bytes 393248 | tf_op jit(solution)/shard_map/ppermute | solution.py:306
  44.8 0.1 convert_add_fusion.1
  45.0 1.0 %collective-permute-start.22 = (bf16[192,512]{1,0:T(8,128)(2,1)S(1)}, bf16[192,512]{1,0:T(8,128)(2,1)S(1)}, u32[]{:S(2)}, u32[]{:S(2)}) collective-permute-start(bf16[192,512]{1,0:T(8,128)(2,1)S(1)} %fusion.10.refs_1_), channel_id=1, source_target_pairs={{0,2},{2,0},{4,6},{6,4},{8,10},{10,8},{12,14},{14,12},{1,3},{3,1},... | collective-permute-start | bytes 589832 | tf_op jit(solution)/shard_map/ppermute | solution.py:311
  46.0 1.0 %collective-permute-done.27 = bf16[192,512]{1,0:T(8,128)(2,1)S(1)} collective-permute-done((bf16[192,512]{1,0:T(8,128)(2,1)S(1)}, bf16[192,512]{1,0:T(8,128)(2,1)S(1)}, u32[]{:S(2)}, u32[]{:S(2)}) %collective-permute-start.27) | collective-permute-done | bytes 196640 | tf_op jit(solution)/shard_map/ppermute | solution.py:311
  47.0 1.5 %collective-permute-start.28 = (bf16[192,512]{1,0:T(8,128)(2,1)S(1)}, bf16[192,512]{1,0:T(8,128)(2,1)S(1)}, u32[]{:S(2)}, u32[]{:S(2)}) collective-permute-start(bf16[192,512]{1,0:T(8,128)(2,1)S(1)} %fusion.1), channel_id=1, source_target_pairs={{0,8},{2,10},{4,12},{6,14},{8,0},{10,2},{12,4},{14,6},{1,9},{3,11}... | collective-permute-start | bytes 589832 | tf_op jit(solution)/shard_map/ppermute | solution.py:316
  48.5 0.5 collective-permute-start.25
  49.0 3.8 %collective-permute-done.22 = bf16[192,512]{1,0:T(8,128)(2,1)S(1)} collective-permute-done((bf16[192,512]{1,0:T(8,128)(2,1)S(1)}, bf16[192,512]{1,0:T(8,128)(2,1)S(1)}, u32[]{:S(2)}, u32[]{:S(2)}) %collective-permute-start.22) | collective-permute-done | bytes 196640 | tf_op jit(solution)/shard_map/ppermute | solution.py:311
  52.8 2.9 %collective-permute-start.29 = (bf16[192,512]{1,0:T(8,128)(2,1)S(1)}, bf16[192,512]{1,0:T(8,128)(2,1)S(1)}, u32[]{:S(2)}, u32[]{:S(2)}) collective-permute-start(bf16[192,512]{1,0:T(8,128)(2,1)S(1)} %fusion.5.refs_1_), channel_id=1, source_target_pairs={{0,12},{2,14},{4,8},{6,10},{8,4},{10,6},{12,0},{14,2},{1,13},{3,15... | collective-permute-start | bytes 589832 | tf_op jit(solution)/shard_map/ppermute | solution.py:316
  55.7 1.1 %collective-permute-start.23 = (bf16[192,512]{1,0:T(8,128)(2,1)S(1)}, bf16[192,512]{1,0:T(8,128)(2,1)S(1)}, u32[]{:S(2)}, u32[]{:S(2)}) collective-permute-start(bf16[192,512]{1,0:T(8,128)(2,1)S(1)} %after.10), channel_id=1, source_target_pairs={{0,2},{2,0},{4,6},{6,4},{8,10},{10,8},{12,14},{14,12},{1,3},{3,1},... | collective-permute-start | bytes 589832 | tf_op jit(solution)/shard_map/ppermute | solution.py:311
  56.9 0.1 fusion.3
  56.9 1.9 %collective-permute-start.26 = (bf16[192,512]{1,0:T(8,128)(2,1)S(1)}, bf16[192,512]{1,0:T(8,128)(2,1)S(1)}, u32[]{:S(2)}, u32[]{:S(2)}) collective-permute-start(bf16[192,512]{1,0:T(8,128)(2,1)S(1)} %fusion.3), channel_id=1, source_target_pairs={{0,4},{2,6},{4,0},{6,2},{8,12},{10,14},{12,8},{14,10},{1,5},{3,7},... | collective-permute-start | bytes 589832 | tf_op jit(solution)/shard_map/ppermute | solution.py:316
  58.8 2.6 %collective-permute-done.23 = bf16[192,512]{1,0:T(8,128)(2,1)S(1)} collective-permute-done((bf16[192,512]{1,0:T(8,128)(2,1)S(1)}, bf16[192,512]{1,0:T(8,128)(2,1)S(1)}, u32[]{:S(2)}, u32[]{:S(2)}) %collective-permute-start.23) | collective-permute-done | bytes 196640 | tf_op jit(solution)/shard_map/ppermute | solution.py:311
  61.4 0.1 fusion.7.rest_0_
  61.5 2.3 %collective-permute-done.28.rest_2_ = bf16[192,512]{1,0:T(8,128)(2,1)S(1)} collective-permute-done((bf16[192,512]{1,0:T(8,128)(2,1)S(1)}, bf16[192,512]{1,0:T(8,128)(2,1)S(1)}, u32[]{:S(2)}, u32[]{:S(2)}) %collective-permute-start.28) | collective-permute-done | bytes 196640 | tf_op jit(solution)/shard_map/ppermute | solution.py:316
  63.8 2.9 %collective-permute-done.26.rest_1_ = bf16[192,512]{1,0:T(8,128)(2,1)S(1)} collective-permute-done((bf16[192,512]{1,0:T(8,128)(2,1)S(1)}, bf16[192,512]{1,0:T(8,128)(2,1)S(1)}, u32[]{:S(2)}, u32[]{:S(2)}) %collective-permute-start.26) | collective-permute-done | bytes 196640 | tf_op jit(solution)/shard_map/ppermute | solution.py:316
  66.6 0.5 combine_other.1
  67.1 0.1 collective-permute-start.30
  67.2 0.5 combine_own.1.own_ref
  67.7 0.8 %collective-permute-done.30.other_ref = bf16[128,512]{1,0:T(8,128)(2,1)S(1)} collective-permute-done((bf16[128,512]{1,0:T(8,128)(2,1)S(1)}, bf16[128,512]{1,0:T(8,128)(2,1)S(1)}, u32[]{:S(2)}, u32[]{:S(2)}) %collective-permute-start.30) | collective-permute-done | bytes 131104 | tf_op jit(solution)/shard_map/ppermute | solution.py:306
  68.5 0.7 %finish.1 = bf16[128,1024]{1,0:T(8,128)(2,1)} custom-call(s32[1]{0:T(128)} %bitcast.core_ref, bf16[128,1024]{1,0:T(8,128)(2,1)S(1)} %get-tuple-element.33.state_ref, bf16[128,512]{1,0:T(8,128)(2,1)S(1)} %combine_own.1.own_ref, bf16[128,512]{1,0:T(8,128)(2,1)S(1)} %collective-permute-done.30.other_ref), custom_call_target="tpu_custom_call" | custom-call | tf_op jit(solution)/shard_map/finish/pallas_call | solution.py:25
  (27 shorter events, 0.2 us)
Async XLA Ops:
  0.0 2.9 %collective-permute-start = (bf16[2,80,512]{2,1,0:T(8,128)(2,1)}, bf16[2,80,512]{2,1,0:T(8,128)(2,1)S(1)}, u32[]{:S(2)}, u32[]{:S(2)}) collective-permute-start(bf16[2,80,512]{2,1,0:T(8,128)(2,1)} %keys_in.1), channel_id=1, source_target_pairs={{0,1},{1,0},{2,3},{3,2},{4,5},{5,4},{6,7},{7,6},{8,9},{9,8},{10,11... | collective-permute-start | bytes 491528 | tf_op jit(solution)/shard_map/ppermute | solution.py:306
  0.5 2.5 %collective-permute-start.1 = (bf16[2,80,512]{2,1,0:T(8,128)(2,1)}, bf16[2,80,512]{2,1,0:T(8,128)(2,1)S(1)}, u32[]{:S(2)}, u32[]{:S(2)}) collective-permute-start(bf16[2,80,512]{2,1,0:T(8,128)(2,1)} %values_in.1), channel_id=1, source_target_pairs={{0,1},{1,0},{2,3},{3,2},{4,5},{5,4},{6,7},{7,6},{8,9},{9,8},{10,11... | collective-permute-start | bytes 491528 | tf_op jit(solution)/shard_map/ppermute | solution.py:306
  4.2 1.5 %collective-permute-start.2 = (bf16[128,512]{1,0:T(8,128)(2,1)S(1)}, bf16[128,512]{1,0:T(8,128)(2,1)S(1)}, u32[]{:S(2)}, u32[]{:S(2)}) collective-permute-start(bf16[128,512]{1,0:T(8,128)(2,1)S(1)} %get-tuple-element.37), channel_id=1, source_target_pairs={{0,1},{1,0},{2,3},{3,2},{4,5},{5,4},{6,7},{7,6},{8,9},{9,8},{10,11... | collective-permute-start | bytes 393224 | tf_op jit(solution)/shard_map/ppermute | solution.py:306
  6.2 13.5 %collective-permute-start.10 = (bf16[192,512]{1,0:T(8,128)(2,1)S(1)}, bf16[192,512]{1,0:T(8,128)(2,1)S(1)}, u32[]{:S(2)}, u32[]{:S(2)}) collective-permute-start(bf16[192,512]{1,0:T(8,128)(2,1)S(1)} %get-tuple-element.45), channel_id=1, source_target_pairs={{0,8},{2,10},{4,12},{6,14},{8,0},{10,2},{12,4},{14,6},{1,9},{3,11}... | collective-permute-start | bytes 589832 | tf_op jit(solution)/shard_map/ppermute | solution.py:316
  10.2 11.1 %collective-permute-start.4 = (bf16[192,512]{1,0:T(8,128)(2,1)S(1)}, bf16[192,512]{1,0:T(8,128)(2,1)S(1)}, u32[]{:S(2)}, u32[]{:S(2)}) collective-permute-start(bf16[192,512]{1,0:T(8,128)(2,1)S(1)} %get-tuple-element.39.p_ref), channel_id=1, source_target_pairs={{0,2},{2,0},{4,6},{6,4},{8,10},{10,8},{12,14},{14,12},{1,3},{3,1},... | collective-permute-start | bytes 589832 | tf_op jit(solution)/shard_map/ppermute | solution.py:311
  14.0 11.3 %collective-permute-start.16 = (bf16[192,512]{1,0:T(8,128)(2,1)S(1)}, bf16[192,512]{1,0:T(8,128)(2,1)S(1)}, u32[]{:S(2)}, u32[]{:S(2)}) collective-permute-start(bf16[192,512]{1,0:T(8,128)(2,1)S(1)} %get-tuple-element.47), channel_id=1, source_target_pairs={{0,4},{2,6},{4,0},{6,2},{8,12},{10,14},{12,8},{14,10},{1,5},{3,7},... | collective-permute-start | bytes 589832 | tf_op jit(solution)/shard_map/ppermute | solution.py:316
  19.8 6.4 %collective-permute-start.11 = (bf16[192,512]{1,0:T(8,128)(2,1)S(1)}, bf16[192,512]{1,0:T(8,128)(2,1)S(1)}, u32[]{:S(2)}, u32[]{:S(2)}) collective-permute-start(bf16[192,512]{1,0:T(8,128)(2,1)S(1)} %after.6.p_ref), channel_id=1, source_target_pairs={{0,2},{2,0},{4,6},{6,4},{8,10},{10,8},{12,14},{14,12},{1,3},{3,1},... | collective-permute-start | bytes 589832 | tf_op jit(solution)/shard_map/ppermute | solution.py:311
  21.3 4.8 %collective-permute-start.5 = (bf16[192,512]{1,0:T(8,128)(2,1)S(1)}, bf16[192,512]{1,0:T(8,128)(2,1)S(1)}, u32[]{:S(2)}, u32[]{:S(2)}) collective-permute-start(bf16[192,512]{1,0:T(8,128)(2,1)S(1)} %get-tuple-element.39.p_ref), channel_id=1, source_target_pairs={{0,1},{1,0},{2,3},{3,2},{4,5},{5,4},{6,7},{7,6},{8,9},{9,8},{10,11... | collective-permute-start | bytes 589832 | tf_op jit(solution)/shard_map/ppermute | solution.py:306
  21.3 4.8 %collective-permute-start.6 = (bf16[192,512]{1,0:T(8,128)(2,1)S(1)}, bf16[192,512]{1,0:T(8,128)(2,1)S(1)}, u32[]{:S(2)}, u32[]{:S(2)}) collective-permute-start(bf16[192,512]{1,0:T(8,128)(2,1)S(1)} %collective-permute-done.4.q_ref), channel_id=1, source_target_pairs={{0,1},{1,0},{2,3},{3,2},{4,5},{5,4},{6,7},{7,6},{8,9},{9,8},{10,11... | collective-permute-start | bytes 589832 | tf_op jit(solution)/shard_map/ppermute | solution.py:306
  21.9 8.7 %collective-permute-start.8 = (bf16[192,512]{1,0:T(8,128)(2,1)S(1)}, bf16[192,512]{1,0:T(8,128)(2,1)S(1)}, u32[]{:S(2)}, u32[]{:S(2)}) collective-permute-start(bf16[192,512]{1,0:T(8,128)(2,1)S(1)} %get-tuple-element.44), channel_id=1, source_target_pairs={{0,12},{2,14},{4,8},{6,10},{8,4},{10,6},{12,0},{14,2},{1,13},{3,15... | collective-permute-start | bytes 589832 | tf_op jit(solution)/shard_map/ppermute | solution.py:316
  25.3 6.5 %collective-permute-start.17 = (bf16[192,512]{1,0:T(8,128)(2,1)S(1)}, bf16[192,512]{1,0:T(8,128)(2,1)S(1)}, u32[]{:S(2)}, u32[]{:S(2)}) collective-permute-start(bf16[192,512]{1,0:T(8,128)(2,1)S(1)} %collective-permute-done.16.p_ref), channel_id=1, source_target_pairs={{0,2},{2,0},{4,6},{6,4},{8,10},{10,8},{12,14},{14,12},{1,3},{3,1},... | collective-permute-start | bytes 589832 | tf_op jit(solution)/shard_map/ppermute | solution.py:311
  26.2 5.7 %collective-permute-start.13 = (bf16[192,512]{1,0:T(8,128)(2,1)S(1)}, bf16[192,512]{1,0:T(8,128)(2,1)S(1)}, u32[]{:S(2)}, u32[]{:S(2)}) collective-permute-start(bf16[192,512]{1,0:T(8,128)(2,1)S(1)} %collective-permute-done.11.q_ref), channel_id=1, source_target_pairs={{0,1},{1,0},{2,3},{3,2},{4,5},{5,4},{6,7},{7,6},{8,9},{9,8},{10,11... | collective-permute-start | bytes 589832 | tf_op jit(solution)/shard_map/ppermute | solution.py:306
  28.0 11.2 %collective-permute-start.7 = (bf16[2,192,512]{2,1,0:T(8,128)(2,1)S(1)}, bf16[2,192,512]{2,1,0:T(8,128)(2,1)S(1)}, u32[]{:S(2)}, u32[]{:S(2)}) collective-permute-start(bf16[2,192,512]{2,1,0:T(8,128)(2,1)S(1)} %get-tuple-element.43), channel_id=1, source_target_pairs={{0,1},{1,0},{2,3},{3,2},{4,5},{5,4},{6,7},{7,6},{8,9},{9,8},{10,11... | collective-permute-start | bytes 1179656 | tf_op jit(solution)/shard_map/ppermute | solution.py:306
  28.6 3.8 %collective-permute-start.12 = (bf16[192,512]{1,0:T(8,128)(2,1)S(1)}, bf16[192,512]{1,0:T(8,128)(2,1)S(1)}, u32[]{:S(2)}, u32[]{:S(2)}) collective-permute-start(bf16[192,512]{1,0:T(8,128)(2,1)S(1)} %after.6.p_ref), channel_id=1, source_target_pairs={{0,1},{1,0},{2,3},{3,2},{4,5},{5,4},{6,7},{7,6},{8,9},{9,8},{10,11... | collective-permute-start | bytes 589832 | tf_op jit(solution)/shard_map/ppermute | solution.py:306
  30.6 3.9 %collective-permute-start.18 = (bf16[192,512]{1,0:T(8,128)(2,1)S(1)}, bf16[192,512]{1,0:T(8,128)(2,1)S(1)}, u32[]{:S(2)}, u32[]{:S(2)}) collective-permute-start(bf16[192,512]{1,0:T(8,128)(2,1)S(1)} %collective-permute-done.16.p_ref), channel_id=1, source_target_pairs={{0,1},{1,0},{2,3},{3,2},{4,5},{5,4},{6,7},{7,6},{8,9},{9,8},{10,11... | collective-permute-start | bytes 589832 | tf_op jit(solution)/shard_map/ppermute | solution.py:306
  31.9 3.0 %collective-permute-start.19 = (bf16[192,512]{1,0:T(8,128)(2,1)S(1)}, bf16[192,512]{1,0:T(8,128)(2,1)S(1)}, u32[]{:S(2)}, u32[]{:S(2)}) collective-permute-start(bf16[192,512]{1,0:T(8,128)(2,1)S(1)} %collective-permute-done.17.q_ref), channel_id=1, source_target_pairs={{0,1},{1,0},{2,3},{3,2},{4,5},{5,4},{6,7},{7,6},{8,9},{9,8},{10,11... | collective-permute-start | bytes 589832 | tf_op jit(solution)/shard_map/ppermute | solution.py:306
  31.9 7.3 %collective-permute-start.9 = (bf16[192,512]{1,0:T(8,128)(2,1)S(1)}, bf16[192,512]{1,0:T(8,128)(2,1)S(1)}, u32[]{:S(2)}, u32[]{:S(2)}) collective-permute-start(bf16[192,512]{1,0:T(8,128)(2,1)S(1)} %collective-permute-done.8.p_ref), channel_id=1, source_target_pairs={{0,2},{2,0},{4,6},{6,4},{8,10},{10,8},{12,14},{14,12},{1,3},{3,1},... | collective-permute-start | bytes 589832 | tf_op jit(solution)/shard_map/ppermute | solution.py:311
  32.4 29.1 %collective-permute-start.3 = (f32[2,128]{1,0:T(2,128)S(1)}, f32[2,128]{1,0:T(2,128)S(1)}, u32[]{:S(2)}, u32[]{:S(2)}) collective-permute-start(f32[2,128]{1,0:T(2,128)S(1)} %get-tuple-element.35.gates_ref), channel_id=1, source_target_pairs={{0,1},{1,0},{2,3},{3,2},{4,5},{5,4},{6,7},{7,6},{8,9},{9,8},{10,11... | collective-permute-start | bytes 3080 | tf_op jit(solution)/shard_map/ppermute | solution.py:306
  34.5 6.7 %collective-permute-start.14 = (bf16[192,512]{1,0:T(8,128)(2,1)S(1)}, bf16[192,512]{1,0:T(8,128)(2,1)S(1)}, u32[]{:S(2)}, u32[]{:S(2)}) collective-permute-start(bf16[192,512]{1,0:T(8,128)(2,1)S(1)} %collective-permute-done.8.p_ref), channel_id=1, source_target_pairs={{0,1},{1,0},{2,3},{3,2},{4,5},{5,4},{6,7},{7,6},{8,9},{9,8},{10,11... | collective-permute-start | bytes 589832 | tf_op jit(solution)/shard_map/ppermute | solution.py:306
  34.9 5.0 %collective-permute-start.20 = (bf16[2,192,512]{2,1,0:T(8,128)(2,1)S(1)}, bf16[2,192,512]{2,1,0:T(8,128)(2,1)S(1)}, u32[]{:S(2)}, u32[]{:S(2)}) collective-permute-start(bf16[2,192,512]{2,1,0:T(8,128)(2,1)S(1)} %get-tuple-element.49), channel_id=1, source_target_pairs={{0,1},{1,0},{2,3},{3,2},{4,5},{5,4},{6,7},{7,6},{8,9},{9,8},{10,11... | collective-permute-start | bytes 1179656 | tf_op jit(solution)/shard_map/ppermute | solution.py:306
  39.2 4.1 %collective-permute-start.24 = (bf16[2,192,512]{2,1,0:T(8,128)(2,1)S(1)}, bf16[2,192,512]{2,1,0:T(8,128)(2,1)S(1)}, u32[]{:S(2)}, u32[]{:S(2)}) collective-permute-start(bf16[2,192,512]{2,1,0:T(8,128)(2,1)S(1)} %get-tuple-element.52), channel_id=1, source_target_pairs={{0,1},{1,0},{2,3},{3,2},{4,5},{5,4},{6,7},{7,6},{8,9},{9,8},{10,11... | collective-permute-start | bytes 1179656 | tf_op jit(solution)/shard_map/ppermute | solution.py:306
  39.2 2.0 %collective-permute-start.15 = (bf16[192,512]{1,0:T(8,128)(2,1)S(1)}, bf16[192,512]{1,0:T(8,128)(2,1)S(1)}, u32[]{:S(2)}, u32[]{:S(2)}) collective-permute-start(bf16[192,512]{1,0:T(8,128)(2,1)S(1)} %after.8.q_ref), channel_id=1, source_target_pairs={{0,1},{1,0},{2,3},{3,2},{4,5},{5,4},{6,7},{7,6},{8,9},{9,8},{10,11... | collective-permute-start | bytes 589832 | tf_op jit(solution)/shard_map/ppermute | solution.py:306
  40.0 6.9 %collective-permute-start.27 = (bf16[192,512]{1,0:T(8,128)(2,1)S(1)}, bf16[192,512]{1,0:T(8,128)(2,1)S(1)}, u32[]{:S(2)}, u32[]{:S(2)}) collective-permute-start(bf16[192,512]{1,0:T(8,128)(2,1)S(1)} %fusion.9.refs_2_), channel_id=1, source_target_pairs={{0,2},{2,0},{4,6},{6,4},{8,10},{10,8},{12,14},{14,12},{1,3},{3,1},... | collective-permute-start | bytes 589832 | tf_op jit(solution)/shard_map/ppermute | solution.py:311
  43.0 1.8 %collective-permute-start.21 = (bf16[2,192,512]{2,1,0:T(8,128)(2,1)S(1)}, bf16[2,192,512]{2,1,0:T(8,128)(2,1)S(1)}, u32[]{:S(2)}, u32[]{:S(2)}) collective-permute-start(bf16[2,192,512]{2,1,0:T(8,128)(2,1)S(1)} %get-tuple-element.51), channel_id=1, source_target_pairs={{0,1},{1,0},{2,3},{3,2},{4,5},{5,4},{6,7},{7,6},{8,9},{9,8},{10,11... | collective-permute-start | bytes 1179656 | tf_op jit(solution)/shard_map/ppermute | solution.py:306
  45.0 7.8 %collective-permute-start.22 = (bf16[192,512]{1,0:T(8,128)(2,1)S(1)}, bf16[192,512]{1,0:T(8,128)(2,1)S(1)}, u32[]{:S(2)}, u32[]{:S(2)}) collective-permute-start(bf16[192,512]{1,0:T(8,128)(2,1)S(1)} %fusion.10.refs_1_), channel_id=1, source_target_pairs={{0,2},{2,0},{4,6},{6,4},{8,10},{10,8},{12,14},{14,12},{1,3},{3,1},... | collective-permute-start | bytes 589832 | tf_op jit(solution)/shard_map/ppermute | solution.py:311
  47.0 16.8 %collective-permute-start.28 = (bf16[192,512]{1,0:T(8,128)(2,1)S(1)}, bf16[192,512]{1,0:T(8,128)(2,1)S(1)}, u32[]{:S(2)}, u32[]{:S(2)}) collective-permute-start(bf16[192,512]{1,0:T(8,128)(2,1)S(1)} %fusion.1), channel_id=1, source_target_pairs={{0,8},{2,10},{4,12},{6,14},{8,0},{10,2},{12,4},{14,6},{1,9},{3,11}... | collective-permute-start | bytes 589832 | tf_op jit(solution)/shard_map/ppermute | solution.py:316
  48.5 8.4 %collective-permute-start.25 = (bf16[192,512]{1,0:T(8,128)(2,1)S(1)}, bf16[192,512]{1,0:T(8,128)(2,1)S(1)}, u32[]{:S(2)}, u32[]{:S(2)}) collective-permute-start(bf16[192,512]{1,0:T(8,128)(2,1)S(1)} %after.11), channel_id=1, source_target_pairs={{0,2},{2,0},{4,6},{6,4},{8,10},{10,8},{12,14},{14,12},{1,3},{3,1},... | collective-permute-start | bytes 589832 | tf_op jit(solution)/shard_map/ppermute | solution.py:311
  52.8 13.8 %collective-permute-start.29 = (bf16[192,512]{1,0:T(8,128)(2,1)S(1)}, bf16[192,512]{1,0:T(8,128)(2,1)S(1)}, u32[]{:S(2)}, u32[]{:S(2)}) collective-permute-start(bf16[192,512]{1,0:T(8,128)(2,1)S(1)} %fusion.5.refs_1_), channel_id=1, source_target_pairs={{0,12},{2,14},{4,8},{6,10},{8,4},{10,6},{12,0},{14,2},{1,13},{3,15... | collective-permute-start | bytes 589832 | tf_op jit(solution)/shard_map/ppermute | solution.py:316
  55.7 5.7 %collective-permute-start.23 = (bf16[192,512]{1,0:T(8,128)(2,1)S(1)}, bf16[192,512]{1,0:T(8,128)(2,1)S(1)}, u32[]{:S(2)}, u32[]{:S(2)}) collective-permute-start(bf16[192,512]{1,0:T(8,128)(2,1)S(1)} %after.10), channel_id=1, source_target_pairs={{0,2},{2,0},{4,6},{6,4},{8,10},{10,8},{12,14},{14,12},{1,3},{3,1},... | collective-permute-start | bytes 589832 | tf_op jit(solution)/shard_map/ppermute | solution.py:311
  56.9 9.7 %collective-permute-start.26 = (bf16[192,512]{1,0:T(8,128)(2,1)S(1)}, bf16[192,512]{1,0:T(8,128)(2,1)S(1)}, u32[]{:S(2)}, u32[]{:S(2)}) collective-permute-start(bf16[192,512]{1,0:T(8,128)(2,1)S(1)} %fusion.3), channel_id=1, source_target_pairs={{0,4},{2,6},{4,0},{6,2},{8,12},{10,14},{12,8},{14,10},{1,5},{3,7},... | collective-permute-start | bytes 589832 | tf_op jit(solution)/shard_map/ppermute | solution.py:316
  67.1 1.4 %collective-permute-start.30 = (bf16[128,512]{1,0:T(8,128)(2,1)S(1)}, bf16[128,512]{1,0:T(8,128)(2,1)S(1)}, u32[]{:S(2)}, u32[]{:S(2)}) collective-permute-start(bf16[128,512]{1,0:T(8,128)(2,1)S(1)} %get-tuple-element.54), channel_id=1, source_target_pairs={{0,1},{1,0},{2,3},{3,2},{4,5},{5,4},{6,7},{7,6},{8,9},{9,8},{10,11... | collective-permute-start | bytes 393224 | tf_op jit(solution)/shard_map/ppermute | solution.py:306

commit v23 on v20

--- a/solution.py
+++ b/solution.py
@@ -250,14 +250,14 @@
         copy.wait()
 
 
-def gated_sum(sent, line, routes, gates, slots_ref, rows):
+def gated_sum(sent, line, routes, gates, slots_ref, pieces):
     full_len = routes.shape[1]
     experts_count = slots_ref.shape[0]
     parts = [slots_ref[:, at : at + full_len] for at in range(0, slots_ref.shape[1], full_len)]
     slots = jnp.where(sent == 0, parts[0], parts[1])
     ids = lax.broadcasted_iota(jnp.int32, (experts_count, full_len), 0)
-    numbers = lax.broadcasted_iota(jnp.int32, (full_len, rows.shape[0]), 1).astype(jnp.float32)
-    capacity = rows.shape[0] // (lax.axis_size("expert") // 2)
+    capacity = pieces[0].shape[0]
+    numbers = lax.broadcasted_iota(jnp.int32, (full_len, capacity), 1).astype(jnp.float32)
     total = None
     for k in range(2):
         route = routes[k : k + 1]
@@ -267,30 +267,27 @@
             jnp.broadcast_to(row, (full_len, full_len)).T[:, :1]
             for row in (place, gates[k : k + 1])
         )
-        picks = jnp.where(numbers == place, 1.0, 0.0).astype(jnp.bfloat16)
-        term = gate * jnp.dot(picks, rows, preferred_element_type=jnp.float32)
-        total = term if total is None else total + term
+        found = None
+        for offset, piece in enumerate(pieces):
+            picks = jnp.where(numbers == place - offset * capacity, 1.0, 0.0).astype(jnp.bfloat16)
+            part = jnp.dot(picks, piece[...], preferred_element_type=jnp.float32)
+            found = part if found is None else found + part
+        total = gate * found if total is None else total + gate * found
     return total
 
 
 def combine_other_kernel(core_ref, line_ref, routes_ref, gates_ref, slots_ref, *rest):
-    pieces, (other_ref, rows_ref) = rest[:-2], rest[-2:]
-    capacity = pieces[0].shape[0]
-    for offset, piece_ref in enumerate(pieces):
-        rows_ref[offset * capacity : (offset + 1) * capacity] = piece_ref[...]
+    pieces, other_ref = rest[:-1], rest[-1]
     sent = 1 - core_ref[0]
     other_ref[...] = gated_sum(
-        sent, line_ref[0], routes_ref[sent], gates_ref[...], slots_ref, rows_ref[...]
+        sent, line_ref[0], routes_ref[sent], gates_ref[...], slots_ref, pieces
     ).astype(jnp.bfloat16)
 
 
-def combine_own_kernel(
-    core_ref, line_ref, routes_ref, gates_ref, slots_ref, rows_ref, state_ref, own_ref
-):
+def combine_own_kernel(core_ref, line_ref, routes_ref, gates_ref, slots_ref, state_ref, *rest):
+    pieces, own_ref = rest[:-1], rest[-1]
     core = core_ref[0]
-    summed = gated_sum(
-        core, line_ref[0], routes_ref[core], gates_ref[...], slots_ref, rows_ref[...]
-    )
+    summed = gated_sum(core, line_ref[0], routes_ref[core], gates_ref[...], slots_ref, pieces)
     own_ref[...] = add_rounded(state_ref[:, part_of(core, own_ref.shape[1])], summed)
 
 
@@ -476,10 +473,10 @@
     across = swap_owner(leaving)
     wholes[0] = whole(boths[0], across)
     home[0] = wholes[0]
-    leaving, rows = call(
+    (leaving,) = call(
         combine_other_kernel,
         "combine_other",
-        [((full_len, half), jnp.bfloat16), ((count * capacity, half), jnp.bfloat16)],
+        [((full_len, half), jnp.bfloat16)],
         [core, line],
         [routes, other_gates, slots, *home],
     )
@@ -489,7 +486,7 @@
         "combine_own",
         [((full_len, half), jnp.bfloat16)],
         [core, line],
-        [routes, gates, slots, rows, state],
+        [routes, gates, slots, state, *home],
     )
     (mixed,) = call(
         finish_kernel,

time: 68.3 us -> 68.3 us (level)
  transfers between devices with their start and end apart: 31 -> 31, of which waited for: 14 -> 14; matrix products, arithmetic and copies ran while one was open for 1% -> 1% of each run, Pallas kernels for 17% -> 18%
where the time goes in v23:
time: 68.3 us; the launch traced here: 68.2 us
  starting transfers between devices  28.6 us (42%)
  waiting for transfers between devices  22.9 us (34%)
  Pallas kernels  15.1 us (22%)
  between operations  0.9 us (1%)
    pallas_call x11, Pallas kernels, call(): pl.pallas_call(kernel, out_shape=tuple((jax.ShapeDtypeStruct(*out) for ou...  15 us
    ppermute x6, starting transfers between devices, exchange(): lax.ppermute(values, 'expert', [(i, i ^ 2 * offset) for i in range(owners)])  14.7 us
    ppermute x6, waiting for transfers between devices, exchange(): lax.ppermute(values, 'expert', [(i, i ^ 2 * offset) for i in range(owners)])  11.5 us
    ppermute x8, starting transfers between devices, swap_owner(): return lax.ppermute(values, 'expert', [(i, i ^ 1) for i in range(owners)])  10.7 us
    ppermute x8, waiting for transfers between devices, swap_owner(): return lax.ppermute(values, 'expert', [(i, i ^ 1) for i in range(owners)])  8.15 us
    ppermute x17, waiting for transfers between devices, swap(): return lax.ppermute(values, 'section', [(0, 1), (1, 0)])  3.3 us
    ppermute x17, starting transfers between devices, swap(): return lax.ppermute(values, 'section', [(0, 1), (1, 0)])  3.22 us
  transfers between devices with their start and end apart: 31, of which 14 were waited for; matrix products, arithmetic and copies ran while one was open for 1% of the time, Pallas kernels for 18%

profile of v23, /device:TPU:0, one launch (start us, length us, event | category | flops | bytes accessed | tf_op | source)
XLA Modules:
  0.0 68.2 jit_solution(4005243086095075073)
XLA Ops:
  0.0 0.5 collective-permute-start
  0.5 0.1 collective-permute-start.1
  1.2 1.8 %attend_own.1 = (bf16[128,512]{1,0:T(8,128)(2,1)S(1)}, bf16[128,512]{1,0:T(8,128)(2,1)S(1)}, bf16[128,512]{1,0:T(8,128)(2,1)S(1)}) custom-call(s32[1]{0:T(128)} %bitcast.core_ref, s32[1]{0:T(128)S(6)} %copy.24.source_ref, bf16[1,128,1024]{2,1,0:T(8,128)(2,1)} %x_in.1, f32[1,1024]{1,0:T(1,128)} %bitcast.40, bf16[2,80,512]{2,1,0:T(8,128)(2,1)} %keys_in.1, ...), custom_call_target="tpu_custom_call" | custom-call | tf_op jit(solution)/shard_map/attend_own/pallas_call | solution.py:25
  2.9 0.0 collective-permute-done.1.values_ref
  3.0 1.2 %attend_other.1 = (bf16[128,1024]{1,0:T(8,128)(2,1)S(1)}, bf16[128,512]{1,0:T(8,128)(2,1)S(1)}, bf16[128,512]{1,0:T(8,128)(2,1)S(1)}, f32[2,128]{1,0:T(2,128)S(1)}, s32[2,2,128]{2,1,0:T(2,128)S(1)}) custom-call(s32[1]{0:T(128)} %bitcast.core_ref, s32[1]{0:T(128)S(6)} %copy.24.source_ref, bf16[128,512]{1,0:T(8,128)(2,1)S(1)} %get-tuple-element.28.own_ref, ...), custom_call_target="tpu_custom_call" | custom-call | tf_op jit(solution)/shard_map/attend_other/pallas_call | solution.py:25
  4.2 0.5 collective-permute-start.2
  4.7 1.0 %collective-permute-done.2.other_ref = bf16[128,512]{1,0:T(8,128)(2,1)S(1)} collective-permute-done((bf16[128,512]{1,0:T(8,128)(2,1)S(1)}, bf16[128,512]{1,0:T(8,128)(2,1)S(1)}, u32[]{:S(2)}, u32[]{:S(2)}) %collective-permute-start.2) | collective-permute-done | bytes 131104 | tf_op jit(solution)/shard_map/ppermute | solution.py:303
  5.7 0.5 select.5
  6.2 2.9 %collective-permute-start.3 = (bf16[192,512]{1,0:T(8,128)(2,1)S(1)}, bf16[192,512]{1,0:T(8,128)(2,1)S(1)}, u32[]{:S(2)}, u32[]{:S(2)}) collective-permute-start(bf16[192,512]{1,0:T(8,128)(2,1)S(1)} %get-tuple-element.37.p_ref), channel_id=1, source_target_pairs={{0,2},{2,0},{4,6},{6,4},{8,10},{10,8},{12,14},{14,12},{1,3},{3,1},... | collective-permute-start | bytes 589832 | tf_op jit(solution)/shard_map/ppermute | solution.py:308
  9.2 1.6 %collective-permute-start.13 = (bf16[192,512]{1,0:T(8,128)(2,1)S(1)}, bf16[192,512]{1,0:T(8,128)(2,1)S(1)}, u32[]{:S(2)}, u32[]{:S(2)}) collective-permute-start(bf16[192,512]{1,0:T(8,128)(2,1)S(1)} %get-tuple-element.44), channel_id=1, source_target_pairs={{0,4},{2,6},{4,0},{6,2},{8,12},{10,14},{12,8},{14,10},{1,5},{3,7},... | collective-permute-start | bytes 589832 | tf_op jit(solution)/shard_map/ppermute | solution.py:313
  10.7 2.6 %collective-permute-start.9 = (bf16[192,512]{1,0:T(8,128)(2,1)S(1)}, bf16[192,512]{1,0:T(8,128)(2,1)S(1)}, u32[]{:S(2)}, u32[]{:S(2)}) collective-permute-start(bf16[192,512]{1,0:T(8,128)(2,1)S(1)} %get-tuple-element.43), channel_id=1, source_target_pairs={{0,8},{2,10},{4,12},{6,14},{8,0},{10,2},{12,4},{14,6},{1,9},{3,11}... | collective-permute-start | bytes 589832 | tf_op jit(solution)/shard_map/ppermute | solution.py:313
  13.3 0.0 collective-permute-start.4
  13.3 1.1 %collective-permute-done.3.q_ref = bf16[192,512]{1,0:T(8,128)(2,1)S(1)} collective-permute-done((bf16[192,512]{1,0:T(8,128)(2,1)S(1)}, bf16[192,512]{1,0:T(8,128)(2,1)S(1)}, u32[]{:S(2)}, u32[]{:S(2)}) %collective-permute-start.3) | collective-permute-done | bytes 196640 | tf_op jit(solution)/shard_map/ppermute | solution.py:308
  14.4 0.0 collective-permute-start.5
  14.4 2.2 %load.1 = (bf16[1024,1024]{1,0:T(8,128)(2,1)S(1)}, bf16[1024,1024]{1,0:T(8,128)(2,1)S(1)}) custom-call(bf16[1024,1024]{1,0:T(8,128)(2,1)} %in_in.1, bf16[1024,1024]{1,0:T(8,128)(2,1)} %out_in.1), custom_call_target="tpu_custom_call" | custom-call | tf_op jit(solution)/shard_map/load/pallas_call | solution.py:25
  16.6 3.3 %collective-permute-done.13.refs_0_ = bf16[192,512]{1,0:T(8,128)(2,1)S(1)} collective-permute-done((bf16[192,512]{1,0:T(8,128)(2,1)S(1)}, bf16[192,512]{1,0:T(8,128)(2,1)S(1)}, u32[]{:S(2)}, u32[]{:S(2)}) %collective-permute-start.13) | collective-permute-done | bytes 196640 | tf_op jit(solution)/shard_map/ppermute | solution.py:313
  19.9 0.4 collective-permute-start.14
  20.3 2.0 %collective-permute-done.9.p_ref = bf16[192,512]{1,0:T(8,128)(2,1)S(1)} collective-permute-done((bf16[192,512]{1,0:T(8,128)(2,1)S(1)}, bf16[192,512]{1,0:T(8,128)(2,1)S(1)}, u32[]{:S(2)}, u32[]{:S(2)}) %collective-permute-start.9) | collective-permute-done | bytes 196640 | tf_op jit(solution)/shard_map/ppermute | solution.py:313
  22.3 0.5 collective-permute-start.10
  22.8 2.5 %collective-permute-start.7 = (bf16[192,512]{1,0:T(8,128)(2,1)S(1)}, bf16[192,512]{1,0:T(8,128)(2,1)S(1)}, u32[]{:S(2)}, u32[]{:S(2)}) collective-permute-start(bf16[192,512]{1,0:T(8,128)(2,1)S(1)} %get-tuple-element.42), channel_id=1, source_target_pairs={{0,12},{2,14},{4,8},{6,10},{8,4},{10,6},{12,0},{14,2},{1,13},{3,15... | collective-permute-start | bytes 589832 | tf_op jit(solution)/shard_map/ppermute | solution.py:313
  25.3 1.8 %expert.4 = (f32[2,192,512]{2,1,0:T(8,128)S(1)}, bf16[2,192,512]{2,1,0:T(8,128)(2,1)S(1)}) custom-call(s32[1]{0:T(128)} %bitcast.core_ref, bf16[192,512]{1,0:T(8,128)(2,1)S(1)} %get-tuple-element.37.p_ref, bf16[192,512]{1,0:T(8,128)(2,1)S(1)} %collective-permute-done.3.q_ref, bf16[192,512]{1,0:T(8,128)(2,1)S(1)} %collective-permute-done.4.p2_ref, ...), custom_call_target="tpu_custom_call" | custom-call | tf_op jit(solution)/shard_map/expert/pallas_call | solution.py:25
  27.2 0.6 collective-permute-start.6
  27.7 0.1 collective-permute-start.16
  27.8 1.8 %collective-permute-done.10.q_ref = bf16[192,512]{1,0:T(8,128)(2,1)S(1)} collective-permute-done((bf16[192,512]{1,0:T(8,128)(2,1)S(1)}, bf16[192,512]{1,0:T(8,128)(2,1)S(1)}, u32[]{:S(2)}, u32[]{:S(2)}) %collective-permute-start.10) | collective-permute-done | bytes 196640 | tf_op jit(solution)/shard_map/ppermute | solution.py:308
  29.6 0.0 collective-permute-start.12
  29.6 0.8 %collective-permute-done.7.p_ref = bf16[192,512]{1,0:T(8,128)(2,1)S(1)} collective-permute-done((bf16[192,512]{1,0:T(8,128)(2,1)S(1)}, bf16[192,512]{1,0:T(8,128)(2,1)S(1)}, u32[]{:S(2)}, u32[]{:S(2)}) %collective-permute-start.7) | collective-permute-done | bytes 196640 | tf_op jit(solution)/shard_map/ppermute | solution.py:313
  30.4 1.5 %collective-permute-start.8 = (bf16[192,512]{1,0:T(8,128)(2,1)S(1)}, bf16[192,512]{1,0:T(8,128)(2,1)S(1)}, u32[]{:S(2)}, u32[]{:S(2)}) collective-permute-start(bf16[192,512]{1,0:T(8,128)(2,1)S(1)} %collective-permute-done.7.p_ref), channel_id=1, source_target_pairs={{0,2},{2,0},{4,6},{6,4},{8,10},{10,8},{12,14},{14,12},{1,3},{3,1},... | collective-permute-start | bytes 589832 | tf_op jit(solution)/shard_map/ppermute | solution.py:308
  31.9 0.2 collective-permute-start.29
  32.1 1.8 %expert.5 = (f32[2,192,512]{2,1,0:T(8,128)S(1)}, bf16[2,192,512]{2,1,0:T(8,128)(2,1)S(1)}) custom-call(s32[1]{0:T(128)} %bitcast.core_ref, bf16[192,512]{1,0:T(8,128)(2,1)S(1)} %after.6.p_ref, bf16[192,512]{1,0:T(8,128)(2,1)S(1)} %collective-permute-done.14.q_ref, bf16[192,512]{1,0:T(8,128)(2,1)S(1)} %collective-permute-done.15.p2_ref, ...), custom_call_target="tpu_custom_call" | custom-call | tf_op jit(solution)/shard_map/expert/pallas_call | solution.py:25
  34.0 0.3 collective-permute-start.17
  34.3 0.0 collective-permute-done.11.p2_ref
  34.3 1.8 %expert.6 = (f32[2,192,512]{2,1,0:T(8,128)S(1)}, bf16[2,192,512]{2,1,0:T(8,128)(2,1)S(1)}) custom-call(s32[1]{0:T(128)} %bitcast.core_ref, bf16[192,512]{1,0:T(8,128)(2,1)S(1)} %collective-permute-done.9.p_ref, bf16[192,512]{1,0:T(8,128)(2,1)S(1)} %collective-permute-done.10.q_ref, bf16[192,512]{1,0:T(8,128)(2,1)S(1)} %collective-permute-done.11.p2_ref, ...), custom_call_target="tpu_custom_call" | custom-call | tf_op jit(solution)/shard_map/expert/pallas_call | solution.py:25
  36.2 0.3 collective-permute-start.19
  36.5 1.2 %collective-permute-done.8.refs_0_ = bf16[192,512]{1,0:T(8,128)(2,1)S(1)} collective-permute-done((bf16[192,512]{1,0:T(8,128)(2,1)S(1)}, bf16[192,512]{1,0:T(8,128)(2,1)S(1)}, u32[]{:S(2)}, u32[]{:S(2)}) %collective-permute-start.8) | collective-permute-done | bytes 196640 | tf_op jit(solution)/shard_map/ppermute | solution.py:308
  37.7 0.0 collective-permute-done.6
  37.7 0.5 collective-permute-start.18
  38.2 0.1 convert_add_fusion.3
  38.4 0.0 collective-permute-done.19
  38.4 0.1 convert_add_fusion.2
  38.5 1.6 %collective-permute-start.26 = (bf16[192,512]{1,0:T(8,128)(2,1)S(1)}, bf16[192,512]{1,0:T(8,128)(2,1)S(1)}, u32[]{:S(2)}, u32[]{:S(2)}) collective-permute-start(bf16[192,512]{1,0:T(8,128)(2,1)S(1)} %fusion.9.refs_1_), channel_id=1, source_target_pairs={{0,2},{2,0},{4,6},{6,4},{8,10},{10,8},{12,14},{14,12},{1,3},{3,1},... | collective-permute-start | bytes 589832 | tf_op jit(solution)/shard_map/ppermute | solution.py:308
  40.1 0.0 collective-permute-done.18.refs_0_
  40.1 0.0 collective-permute-done.17.p2_ref
  40.1 1.8 %expert.7 = (f32[2,192,512]{2,1,0:T(8,128)S(1)}, bf16[2,192,512]{2,1,0:T(8,128)(2,1)S(1)}) custom-call(s32[1]{0:T(128)} %bitcast.core_ref, bf16[192,512]{1,0:T(8,128)(2,1)S(1)} %collective-permute-done.7.p_ref, bf16[192,512]{1,0:T(8,128)(2,1)S(1)} %after.8.q_ref, bf16[192,512]{1,0:T(8,128)(2,1)S(1)} %collective-permute-done.17.p2_ref, ...), custom_call_target="tpu_custom_call" | custom-call | tf_op jit(solution)/shard_map/expert/pallas_call | solution.py:25
  42.0 0.1 collective-permute-start.20
  42.1 0.1 convert_add_fusion
  42.2 1.5 %collective-permute-done.20 = bf16[2,192,512]{2,1,0:T(8,128)(2,1)S(1)} collective-permute-done((bf16[2,192,512]{2,1,0:T(8,128)(2,1)S(1)}, bf16[2,192,512]{2,1,0:T(8,128)(2,1)S(1)}, u32[]{:S(2)}, u32[]{:S(2)}) %collective-permute-start.20) | collective-permute-done | bytes 393248 | tf_op jit(solution)/shard_map/ppermute | solution.py:303
  43.8 0.1 convert_add_fusion.1
  43.9 1.2 %collective-permute-start.21 = (bf16[192,512]{1,0:T(8,128)(2,1)S(1)}, bf16[192,512]{1,0:T(8,128)(2,1)S(1)}, u32[]{:S(2)}, u32[]{:S(2)}) collective-permute-start(bf16[192,512]{1,0:T(8,128)(2,1)S(1)} %fusion.10.refs_1_), channel_id=1, source_target_pairs={{0,2},{2,0},{4,6},{6,4},{8,10},{10,8},{12,14},{14,12},{1,3},{3,1},... | collective-permute-start | bytes 589832 | tf_op jit(solution)/shard_map/ppermute | solution.py:308
  45.1 0.4 collective-permute-done.26
  45.5 0.1 fusion.1
  45.5 2.5 %collective-permute-start.27 = (bf16[192,512]{1,0:T(8,128)(2,1)S(1)}, bf16[192,512]{1,0:T(8,128)(2,1)S(1)}, u32[]{:S(2)}, u32[]{:S(2)}) collective-permute-start(bf16[192,512]{1,0:T(8,128)(2,1)S(1)} %fusion.1), channel_id=1, source_target_pairs={{0,8},{2,10},{4,12},{6,14},{8,0},{10,2},{12,4},{14,6},{1,9},{3,11}... | collective-permute-start | bytes 589832 | tf_op jit(solution)/shard_map/ppermute | solution.py:313
  48.0 1.5 %collective-permute-start.24 = (bf16[192,512]{1,0:T(8,128)(2,1)S(1)}, bf16[192,512]{1,0:T(8,128)(2,1)S(1)}, u32[]{:S(2)}, u32[]{:S(2)}) collective-permute-start(bf16[192,512]{1,0:T(8,128)(2,1)S(1)} %after.11), channel_id=1, source_target_pairs={{0,2},{2,0},{4,6},{6,4},{8,10},{10,8},{12,14},{14,12},{1,3},{3,1},... | collective-permute-start | bytes 589832 | tf_op jit(solution)/shard_map/ppermute | solution.py:308
  49.6 2.2 %collective-permute-done.21 = bf16[192,512]{1,0:T(8,128)(2,1)S(1)} collective-permute-done((bf16[192,512]{1,0:T(8,128)(2,1)S(1)}, bf16[192,512]{1,0:T(8,128)(2,1)S(1)}, u32[]{:S(2)}, u32[]{:S(2)}) %collective-permute-start.21) | collective-permute-done | bytes 196640 | tf_op jit(solution)/shard_map/ppermute | solution.py:308
  51.8 2.5 %collective-permute-start.28 = (bf16[192,512]{1,0:T(8,128)(2,1)S(1)}, bf16[192,512]{1,0:T(8,128)(2,1)S(1)}, u32[]{:S(2)}, u32[]{:S(2)}) collective-permute-start(bf16[192,512]{1,0:T(8,128)(2,1)S(1)} %fusion.5.refs_1_), channel_id=1, source_target_pairs={{0,12},{2,14},{4,8},{6,10},{8,4},{10,6},{12,0},{14,2},{1,13},{3,15... | collective-permute-start | bytes 589832 | tf_op jit(solution)/shard_map/ppermute | solution.py:313
  54.3 1.1 %collective-permute-start.22 = (bf16[192,512]{1,0:T(8,128)(2,1)S(1)}, bf16[192,512]{1,0:T(8,128)(2,1)S(1)}, u32[]{:S(2)}, u32[]{:S(2)}) collective-permute-start(bf16[192,512]{1,0:T(8,128)(2,1)S(1)} %after.10), channel_id=1, source_target_pairs={{0,2},{2,0},{4,6},{6,4},{8,10},{10,8},{12,14},{14,12},{1,3},{3,1},... | collective-permute-start | bytes 589832 | tf_op jit(solution)/shard_map/ppermute | solution.py:308
  55.4 3.0 %collective-permute-start.25 = (bf16[192,512]{1,0:T(8,128)(2,1)S(1)}, bf16[192,512]{1,0:T(8,128)(2,1)S(1)}, u32[]{:S(2)}, u32[]{:S(2)}) collective-permute-start(bf16[192,512]{1,0:T(8,128)(2,1)S(1)} %fusion.3), channel_id=1, source_target_pairs={{0,4},{2,6},{4,0},{6,2},{8,12},{10,14},{12,8},{14,10},{1,5},{3,7},... | collective-permute-start | bytes 589832 | tf_op jit(solution)/shard_map/ppermute | solution.py:313
  58.4 1.5 %collective-permute-done.22 = bf16[192,512]{1,0:T(8,128)(2,1)S(1)} collective-permute-done((bf16[192,512]{1,0:T(8,128)(2,1)S(1)}, bf16[192,512]{1,0:T(8,128)(2,1)S(1)}, u32[]{:S(2)}, u32[]{:S(2)}) %collective-permute-start.22) | collective-permute-done | bytes 196640 | tf_op jit(solution)/shard_map/ppermute | solution.py:308
  60.0 2.8 %collective-permute-done.27.rest_2_ = bf16[192,512]{1,0:T(8,128)(2,1)S(1)} collective-permute-done((bf16[192,512]{1,0:T(8,128)(2,1)S(1)}, bf16[192,512]{1,0:T(8,128)(2,1)S(1)}, u32[]{:S(2)}, u32[]{:S(2)}) %collective-permute-start.27) | collective-permute-done | bytes 196640 | tf_op jit(solution)/shard_map/ppermute | solution.py:313
  62.8 2.6 %collective-permute-done.25.rest_1_ = bf16[192,512]{1,0:T(8,128)(2,1)S(1)} collective-permute-done((bf16[192,512]{1,0:T(8,128)(2,1)S(1)}, bf16[192,512]{1,0:T(8,128)(2,1)S(1)}, u32[]{:S(2)}, u32[]{:S(2)}) %collective-permute-start.25) | collective-permute-done | bytes 196640 | tf_op jit(solution)/shard_map/ppermute | solution.py:313
  65.4 0.6 combine_other.1
  66.0 0.1 collective-permute-start.30
  66.1 0.6 combine_own.1.own_ref
  66.7 0.7 %collective-permute-done.30.other_ref = bf16[128,512]{1,0:T(8,128)(2,1)S(1)} collective-permute-done((bf16[128,512]{1,0:T(8,128)(2,1)S(1)}, bf16[128,512]{1,0:T(8,128)(2,1)S(1)}, u32[]{:S(2)}, u32[]{:S(2)}) %collective-permute-start.30) | collective-permute-done | bytes 131104 | tf_op jit(solution)/shard_map/ppermute | solution.py:303
  67.4 0.7 %finish.1 = bf16[128,1024]{1,0:T(8,128)(2,1)} custom-call(s32[1]{0:T(128)} %bitcast.core_ref, bf16[128,1024]{1,0:T(8,128)(2,1)S(1)} %get-tuple-element.31.state_ref, bf16[128,512]{1,0:T(8,128)(2,1)S(1)} %combine_own.1.own_ref, bf16[128,512]{1,0:T(8,128)(2,1)S(1)} %collective-permute-done.30.other_ref), custom_call_target="tpu_custom_call" | custom-call | tf_op jit(solution)/shard_map/finish/pallas_call | solution.py:25
  (27 shorter events, 0.3 us)
Async XLA Ops:
  0.0 2.9 %collective-permute-start = (bf16[2,80,512]{2,1,0:T(8,128)(2,1)}, bf16[2,80,512]{2,1,0:T(8,128)(2,1)S(1)}, u32[]{:S(2)}, u32[]{:S(2)}) collective-permute-start(bf16[2,80,512]{2,1,0:T(8,128)(2,1)} %keys_in.1), channel_id=1, source_target_pairs={{0,1},{1,0},{2,3},{3,2},{4,5},{5,4},{6,7},{7,6},{8,9},{9,8},{10,11... | collective-permute-start | bytes 491528 | tf_op jit(solution)/shard_map/ppermute | solution.py:303
  0.5 2.5 %collective-permute-start.1 = (bf16[2,80,512]{2,1,0:T(8,128)(2,1)}, bf16[2,80,512]{2,1,0:T(8,128)(2,1)S(1)}, u32[]{:S(2)}, u32[]{:S(2)}) collective-permute-start(bf16[2,80,512]{2,1,0:T(8,128)(2,1)} %values_in.1), channel_id=1, source_target_pairs={{0,1},{1,0},{2,3},{3,2},{4,5},{5,4},{6,7},{7,6},{8,9},{9,8},{10,11... | collective-permute-start | bytes 491528 | tf_op jit(solution)/shard_map/ppermute | solution.py:303
  4.2 1.5 %collective-permute-start.2 = (bf16[128,512]{1,0:T(8,128)(2,1)S(1)}, bf16[128,512]{1,0:T(8,128)(2,1)S(1)}, u32[]{:S(2)}, u32[]{:S(2)}) collective-permute-start(bf16[128,512]{1,0:T(8,128)(2,1)S(1)} %get-tuple-element.35), channel_id=1, source_target_pairs={{0,1},{1,0},{2,3},{3,2},{4,5},{5,4},{6,7},{7,6},{8,9},{9,8},{10,11... | collective-permute-start | bytes 393224 | tf_op jit(solution)/shard_map/ppermute | solution.py:303
  6.2 8.1 %collective-permute-start.3 = (bf16[192,512]{1,0:T(8,128)(2,1)S(1)}, bf16[192,512]{1,0:T(8,128)(2,1)S(1)}, u32[]{:S(2)}, u32[]{:S(2)}) collective-permute-start(bf16[192,512]{1,0:T(8,128)(2,1)S(1)} %get-tuple-element.37.p_ref), channel_id=1, source_target_pairs={{0,2},{2,0},{4,6},{6,4},{8,10},{10,8},{12,14},{14,12},{1,3},{3,1},... | collective-permute-start | bytes 589832 | tf_op jit(solution)/shard_map/ppermute | solution.py:308
  9.2 10.8 %collective-permute-start.13 = (bf16[192,512]{1,0:T(8,128)(2,1)S(1)}, bf16[192,512]{1,0:T(8,128)(2,1)S(1)}, u32[]{:S(2)}, u32[]{:S(2)}) collective-permute-start(bf16[192,512]{1,0:T(8,128)(2,1)S(1)} %get-tuple-element.44), channel_id=1, source_target_pairs={{0,4},{2,6},{4,0},{6,2},{8,12},{10,14},{12,8},{14,10},{1,5},{3,7},... | collective-permute-start | bytes 589832 | tf_op jit(solution)/shard_map/ppermute | solution.py:313
  10.7 11.6 %collective-permute-start.9 = (bf16[192,512]{1,0:T(8,128)(2,1)S(1)}, bf16[192,512]{1,0:T(8,128)(2,1)S(1)}, u32[]{:S(2)}, u32[]{:S(2)}) collective-permute-start(bf16[192,512]{1,0:T(8,128)(2,1)S(1)} %get-tuple-element.43), channel_id=1, source_target_pairs={{0,8},{2,10},{4,12},{6,14},{8,0},{10,2},{12,4},{14,6},{1,9},{3,11}... | collective-permute-start | bytes 589832 | tf_op jit(solution)/shard_map/ppermute | solution.py:313
  13.3 12.0 %collective-permute-start.4 = (bf16[192,512]{1,0:T(8,128)(2,1)S(1)}, bf16[192,512]{1,0:T(8,128)(2,1)S(1)}, u32[]{:S(2)}, u32[]{:S(2)}) collective-permute-start(bf16[192,512]{1,0:T(8,128)(2,1)S(1)} %get-tuple-element.37.p_ref), channel_id=1, source_target_pairs={{0,1},{1,0},{2,3},{3,2},{4,5},{5,4},{6,7},{7,6},{8,9},{9,8},{10,11... | collective-permute-start | bytes 589832 | tf_op jit(solution)/shard_map/ppermute | solution.py:303
  14.4 10.9 %collective-permute-start.5 = (bf16[192,512]{1,0:T(8,128)(2,1)S(1)}, bf16[192,512]{1,0:T(8,128)(2,1)S(1)}, u32[]{:S(2)}, u32[]{:S(2)}) collective-permute-start(bf16[192,512]{1,0:T(8,128)(2,1)S(1)} %collective-permute-done.3.q_ref), channel_id=1, source_target_pairs={{0,1},{1,0},{2,3},{3,2},{4,5},{5,4},{6,7},{7,6},{8,9},{9,8},{10,11... | collective-permute-start | bytes 589832 | tf_op jit(solution)/shard_map/ppermute | solution.py:303
  19.9 7.8 %collective-permute-start.14 = (bf16[192,512]{1,0:T(8,128)(2,1)S(1)}, bf16[192,512]{1,0:T(8,128)(2,1)S(1)}, u32[]{:S(2)}, u32[]{:S(2)}) collective-permute-start(bf16[192,512]{1,0:T(8,128)(2,1)S(1)} %after.6.p_ref), channel_id=1, source_target_pairs={{0,2},{2,0},{4,6},{6,4},{8,10},{10,8},{12,14},{14,12},{1,3},{3,1},... | collective-permute-start | bytes 589832 | tf_op jit(solution)/shard_map/ppermute | solution.py:308
  22.3 7.3 %collective-permute-start.10 = (bf16[192,512]{1,0:T(8,128)(2,1)S(1)}, bf16[192,512]{1,0:T(8,128)(2,1)S(1)}, u32[]{:S(2)}, u32[]{:S(2)}) collective-permute-start(bf16[192,512]{1,0:T(8,128)(2,1)S(1)} %collective-permute-done.9.p_ref), channel_id=1, source_target_pairs={{0,2},{2,0},{4,6},{6,4},{8,10},{10,8},{12,14},{14,12},{1,3},{3,1},... | collective-permute-start | bytes 589832 | tf_op jit(solution)/shard_map/ppermute | solution.py:308
  22.8 7.6 %collective-permute-start.7 = (bf16[192,512]{1,0:T(8,128)(2,1)S(1)}, bf16[192,512]{1,0:T(8,128)(2,1)S(1)}, u32[]{:S(2)}, u32[]{:S(2)}) collective-permute-start(bf16[192,512]{1,0:T(8,128)(2,1)S(1)} %get-tuple-element.42), channel_id=1, source_target_pairs={{0,12},{2,14},{4,8},{6,10},{8,4},{10,6},{12,0},{14,2},{1,13},{3,15... | collective-permute-start | bytes 589832 | tf_op jit(solution)/shard_map/ppermute | solution.py:313
  25.3 5.1 %collective-permute-start.15 = (bf16[192,512]{1,0:T(8,128)(2,1)S(1)}, bf16[192,512]{1,0:T(8,128)(2,1)S(1)}, u32[]{:S(2)}, u32[]{:S(2)}) collective-permute-start(bf16[192,512]{1,0:T(8,128)(2,1)S(1)} %after.6.p_ref), channel_id=1, source_target_pairs={{0,1},{1,0},{2,3},{3,2},{4,5},{5,4},{6,7},{7,6},{8,9},{9,8},{10,11... | collective-permute-start | bytes 589832 | tf_op jit(solution)/shard_map/ppermute | solution.py:303
  27.2 10.6 %collective-permute-start.6 = (bf16[2,192,512]{2,1,0:T(8,128)(2,1)S(1)}, bf16[2,192,512]{2,1,0:T(8,128)(2,1)S(1)}, u32[]{:S(2)}, u32[]{:S(2)}) collective-permute-start(bf16[2,192,512]{2,1,0:T(8,128)(2,1)S(1)} %get-tuple-element.41), channel_id=1, source_target_pairs={{0,1},{1,0},{2,3},{3,2},{4,5},{5,4},{6,7},{7,6},{8,9},{9,8},{10,11... | collective-permute-start | bytes 1179656 | tf_op jit(solution)/shard_map/ppermute | solution.py:303
  27.7 4.2 %collective-permute-start.16 = (bf16[192,512]{1,0:T(8,128)(2,1)S(1)}, bf16[192,512]{1,0:T(8,128)(2,1)S(1)}, u32[]{:S(2)}, u32[]{:S(2)}) collective-permute-start(bf16[192,512]{1,0:T(8,128)(2,1)S(1)} %collective-permute-done.14.q_ref), channel_id=1, source_target_pairs={{0,1},{1,0},{2,3},{3,2},{4,5},{5,4},{6,7},{7,6},{8,9},{9,8},{10,11... | collective-permute-start | bytes 589832 | tf_op jit(solution)/shard_map/ppermute | solution.py:303
  29.6 4.4 %collective-permute-start.12 = (bf16[192,512]{1,0:T(8,128)(2,1)S(1)}, bf16[192,512]{1,0:T(8,128)(2,1)S(1)}, u32[]{:S(2)}, u32[]{:S(2)}) collective-permute-start(bf16[192,512]{1,0:T(8,128)(2,1)S(1)} %collective-permute-done.10.q_ref), channel_id=1, source_target_pairs={{0,1},{1,0},{2,3},{3,2},{4,5},{5,4},{6,7},{7,6},{8,9},{9,8},{10,11... | collective-permute-start | bytes 589832 | tf_op jit(solution)/shard_map/ppermute | solution.py:303
  30.4 4.0 %collective-permute-start.11 = (bf16[192,512]{1,0:T(8,128)(2,1)S(1)}, bf16[192,512]{1,0:T(8,128)(2,1)S(1)}, u32[]{:S(2)}, u32[]{:S(2)}) collective-permute-start(bf16[192,512]{1,0:T(8,128)(2,1)S(1)} %collective-permute-done.9.p_ref), channel_id=1, source_target_pairs={{0,1},{1,0},{2,3},{3,2},{4,5},{5,4},{6,7},{7,6},{8,9},{9,8},{10,11... | collective-permute-start | bytes 589832 | tf_op jit(solution)/shard_map/ppermute | solution.py:303
  30.4 7.3 %collective-permute-start.8 = (bf16[192,512]{1,0:T(8,128)(2,1)S(1)}, bf16[192,512]{1,0:T(8,128)(2,1)S(1)}, u32[]{:S(2)}, u32[]{:S(2)}) collective-permute-start(bf16[192,512]{1,0:T(8,128)(2,1)S(1)} %collective-permute-done.7.p_ref), channel_id=1, source_target_pairs={{0,2},{2,0},{4,6},{6,4},{8,10},{10,8},{12,14},{14,12},{1,3},{3,1},... | collective-permute-start | bytes 589832 | tf_op jit(solution)/shard_map/ppermute | solution.py:308
  31.9 28.1 %collective-permute-start.29 = (f32[2,128]{1,0:T(2,128)S(1)}, f32[2,128]{1,0:T(2,128)S(1)}, u32[]{:S(2)}, u32[]{:S(2)}) collective-permute-start(f32[2,128]{1,0:T(2,128)S(1)} %get-tuple-element.33.gates_ref), channel_id=1, source_target_pairs={{0,1},{1,0},{2,3},{3,2},{4,5},{5,4},{6,7},{7,6},{8,9},{9,8},{10,11... | collective-permute-start | bytes 3080 | tf_op jit(solution)/shard_map/ppermute | solution.py:303
  34.0 6.1 %collective-permute-start.17 = (bf16[192,512]{1,0:T(8,128)(2,1)S(1)}, bf16[192,512]{1,0:T(8,128)(2,1)S(1)}, u32[]{:S(2)}, u32[]{:S(2)}) collective-permute-start(bf16[192,512]{1,0:T(8,128)(2,1)S(1)} %collective-permute-done.7.p_ref), channel_id=1, source_target_pairs={{0,1},{1,0},{2,3},{3,2},{4,5},{5,4},{6,7},{7,6},{8,9},{9,8},{10,11... | collective-permute-start | bytes 589832 | tf_op jit(solution)/shard_map/ppermute | solution.py:303
  36.2 2.2 %collective-permute-start.19 = (bf16[2,192,512]{2,1,0:T(8,128)(2,1)S(1)}, bf16[2,192,512]{2,1,0:T(8,128)(2,1)S(1)}, u32[]{:S(2)}, u32[]{:S(2)}) collective-permute-start(bf16[2,192,512]{2,1,0:T(8,128)(2,1)S(1)} %get-tuple-element.47), channel_id=1, source_target_pairs={{0,1},{1,0},{2,3},{3,2},{4,5},{5,4},{6,7},{7,6},{8,9},{9,8},{10,11... | collective-permute-start | bytes 1179656 | tf_op jit(solution)/shard_map/ppermute | solution.py:303
  37.7 4.3 %collective-permute-start.23 = (bf16[2,192,512]{2,1,0:T(8,128)(2,1)S(1)}, bf16[2,192,512]{2,1,0:T(8,128)(2,1)S(1)}, u32[]{:S(2)}, u32[]{:S(2)}) collective-permute-start(bf16[2,192,512]{2,1,0:T(8,128)(2,1)S(1)} %get-tuple-element.50), channel_id=1, source_target_pairs={{0,1},{1,0},{2,3},{3,2},{4,5},{5,4},{6,7},{7,6},{8,9},{9,8},{10,11... | collective-permute-start | bytes 1179656 | tf_op jit(solution)/shard_map/ppermute | solution.py:303
  37.7 2.4 %collective-permute-start.18 = (bf16[192,512]{1,0:T(8,128)(2,1)S(1)}, bf16[192,512]{1,0:T(8,128)(2,1)S(1)}, u32[]{:S(2)}, u32[]{:S(2)}) collective-permute-start(bf16[192,512]{1,0:T(8,128)(2,1)S(1)} %after.8.q_ref), channel_id=1, source_target_pairs={{0,1},{1,0},{2,3},{3,2},{4,5},{5,4},{6,7},{7,6},{8,9},{9,8},{10,11... | collective-permute-start | bytes 589832 | tf_op jit(solution)/shard_map/ppermute | solution.py:303
  38.5 6.9 %collective-permute-start.26 = (bf16[192,512]{1,0:T(8,128)(2,1)S(1)}, bf16[192,512]{1,0:T(8,128)(2,1)S(1)}, u32[]{:S(2)}, u32[]{:S(2)}) collective-permute-start(bf16[192,512]{1,0:T(8,128)(2,1)S(1)} %fusion.9.refs_1_), channel_id=1, source_target_pairs={{0,2},{2,0},{4,6},{6,4},{8,10},{10,8},{12,14},{14,12},{1,3},{3,1},... | collective-permute-start | bytes 589832 | tf_op jit(solution)/shard_map/ppermute | solution.py:308
  42.0 1.8 %collective-permute-start.20 = (bf16[2,192,512]{2,1,0:T(8,128)(2,1)S(1)}, bf16[2,192,512]{2,1,0:T(8,128)(2,1)S(1)}, u32[]{:S(2)}, u32[]{:S(2)}) collective-permute-start(bf16[2,192,512]{2,1,0:T(8,128)(2,1)S(1)} %get-tuple-element.49), channel_id=1, source_target_pairs={{0,1},{1,0},{2,3},{3,2},{4,5},{5,4},{6,7},{7,6},{8,9},{9,8},{10,11... | collective-permute-start | bytes 1179656 | tf_op jit(solution)/shard_map/ppermute | solution.py:303
  43.9 7.8 %collective-permute-start.21 = (bf16[192,512]{1,0:T(8,128)(2,1)S(1)}, bf16[192,512]{1,0:T(8,128)(2,1)S(1)}, u32[]{:S(2)}, u32[]{:S(2)}) collective-permute-start(bf16[192,512]{1,0:T(8,128)(2,1)S(1)} %fusion.10.refs_1_), channel_id=1, source_target_pairs={{0,2},{2,0},{4,6},{6,4},{8,10},{10,8},{12,14},{14,12},{1,3},{3,1},... | collective-permute-start | bytes 589832 | tf_op jit(solution)/shard_map/ppermute | solution.py:308
  45.5 17.3 %collective-permute-start.27 = (bf16[192,512]{1,0:T(8,128)(2,1)S(1)}, bf16[192,512]{1,0:T(8,128)(2,1)S(1)}, u32[]{:S(2)}, u32[]{:S(2)}) collective-permute-start(bf16[192,512]{1,0:T(8,128)(2,1)S(1)} %fusion.1), channel_id=1, source_target_pairs={{0,8},{2,10},{4,12},{6,14},{8,0},{10,2},{12,4},{14,6},{1,9},{3,11}... | collective-permute-start | bytes 589832 | tf_op jit(solution)/shard_map/ppermute | solution.py:313
  48.0 7.3 %collective-permute-start.24 = (bf16[192,512]{1,0:T(8,128)(2,1)S(1)}, bf16[192,512]{1,0:T(8,128)(2,1)S(1)}, u32[]{:S(2)}, u32[]{:S(2)}) collective-permute-start(bf16[192,512]{1,0:T(8,128)(2,1)S(1)} %after.11), channel_id=1, source_target_pairs={{0,2},{2,0},{4,6},{6,4},{8,10},{10,8},{12,14},{14,12},{1,3},{3,1},... | collective-permute-start | bytes 589832 | tf_op jit(solution)/shard_map/ppermute | solution.py:308
  51.8 13.6 %collective-permute-start.28 = (bf16[192,512]{1,0:T(8,128)(2,1)S(1)}, bf16[192,512]{1,0:T(8,128)(2,1)S(1)}, u32[]{:S(2)}, u32[]{:S(2)}) collective-permute-start(bf16[192,512]{1,0:T(8,128)(2,1)S(1)} %fusion.5.refs_1_), channel_id=1, source_target_pairs={{0,12},{2,14},{4,8},{6,10},{8,4},{10,6},{12,0},{14,2},{1,13},{3,15... | collective-permute-start | bytes 589832 | tf_op jit(solution)/shard_map/ppermute | solution.py:313
  54.3 5.7 %collective-permute-start.22 = (bf16[192,512]{1,0:T(8,128)(2,1)S(1)}, bf16[192,512]{1,0:T(8,128)(2,1)S(1)}, u32[]{:S(2)}, u32[]{:S(2)}) collective-permute-start(bf16[192,512]{1,0:T(8,128)(2,1)S(1)} %after.10), channel_id=1, source_target_pairs={{0,2},{2,0},{4,6},{6,4},{8,10},{10,8},{12,14},{14,12},{1,3},{3,1},... | collective-permute-start | bytes 589832 | tf_op jit(solution)/shard_map/ppermute | solution.py:308
  55.4 10.0 %collective-permute-start.25 = (bf16[192,512]{1,0:T(8,128)(2,1)S(1)}, bf16[192,512]{1,0:T(8,128)(2,1)S(1)}, u32[]{:S(2)}, u32[]{:S(2)}) collective-permute-start(bf16[192,512]{1,0:T(8,128)(2,1)S(1)} %fusion.3), channel_id=1, source_target_pairs={{0,4},{2,6},{4,0},{6,2},{8,12},{10,14},{12,8},{14,10},{1,5},{3,7},... | collective-permute-start | bytes 589832 | tf_op jit(solution)/shard_map/ppermute | solution.py:313
  66.0 1.4 %collective-permute-start.30 = (bf16[128,512]{1,0:T(8,128)(2,1)S(1)}, bf16[128,512]{1,0:T(8,128)(2,1)S(1)}, u32[]{:S(2)}, u32[]{:S(2)}) collective-permute-start(bf16[128,512]{1,0:T(8,128)(2,1)S(1)} %combine_other.1), channel_id=1, source_target_pairs={{0,1},{1,0},{2,3},{3,2},{4,5},{5,4},{6,7},{7,6},{8,9},{9,8},{10,11... | collective-permute-start | bytes 393224 | tf_op jit(solution)/shard_map/ppermute | solution.py:303

commit v24 on v23

--- a/solution.py
+++ b/solution.py
@@ -64,7 +64,7 @@
     valid = lax.broadcasted_iota(jnp.int32, (1, keys.shape[0]), 1) < length
     scores = jnp.where(valid, scores, -jnp.inf)
     expon = jnp.exp(scores - jnp.max(scores, axis=-1, keepdims=True))
-    weights = (expon / jnp.sum(expon, axis=-1, keepdims=True)).astype(jnp.bfloat16)
+    weights = (expon * (1.0 / jnp.sum(expon, axis=-1, keepdims=True))).astype(jnp.bfloat16)
     return jnp.concatenate(
         [
             jnp.dot(

time: 68.3 us -> 68.3 us (level)
  no operation moved by 1% of the time
where the time goes in v24:
time: 68.3 us; the launch traced here: 68.2 us
  starting transfers between devices  28.6 us (42%)
  waiting for transfers between devices  22.9 us (34%)
  Pallas kernels  15.1 us (22%)
  between operations  0.9 us (1%)
    pallas_call x11, Pallas kernels, call(): pl.pallas_call(kernel, out_shape=tuple((jax.ShapeDtypeStruct(*out) for ou...  15 us
    ppermute x6, starting transfers between devices, exchange(): lax.ppermute(values, 'expert', [(i, i ^ 2 * offset) for i in range(owners)])  14.7 us
    ppermute x6, waiting for transfers between devices, exchange(): lax.ppermute(values, 'expert', [(i, i ^ 2 * offset) for i in range(owners)])  11.5 us
    ppermute x8, starting transfers between devices, swap_owner(): return lax.ppermute(values, 'expert', [(i, i ^ 1) for i in range(owners)])  10.7 us
    ppermute x8, waiting for transfers between devices, swap_owner(): return lax.ppermute(values, 'expert', [(i, i ^ 1) for i in range(owners)])  8.15 us
    ppermute x17, waiting for transfers between devices, swap(): return lax.ppermute(values, 'section', [(0, 1), (1, 0)])  3.3 us
    ppermute x17, starting transfers between devices, swap(): return lax.ppermute(values, 'section', [(0, 1), (1, 0)])  3.22 us
  transfers between devices with their start and end apart: 31, of which 14 were waited for; matrix products, arithmetic and copies ran while one was open for 1% of the time, Pallas kernels for 18%

profile of v24, /device:TPU:0, one launch (start us, length us, event | category | flops | bytes accessed | tf_op | source)
XLA Modules:
  0.0 68.2 jit_solution(4005243086095075073)
XLA Ops:
  0.0 0.5 collective-permute-start
  0.5 0.1 collective-permute-start.1
  1.2 1.8 %attend_own.1 = (bf16[128,512]{1,0:T(8,128)(2,1)S(1)}, bf16[128,512]{1,0:T(8,128)(2,1)S(1)}, bf16[128,512]{1,0:T(8,128)(2,1)S(1)}) custom-call(s32[1]{0:T(128)} %bitcast.core_ref, s32[1]{0:T(128)S(6)} %copy.24.source_ref, bf16[1,128,1024]{2,1,0:T(8,128)(2,1)} %x_in.1, f32[1,1024]{1,0:T(1,128)} %bitcast.40, bf16[2,80,512]{2,1,0:T(8,128)(2,1)} %keys_in.1, ...), custom_call_target="tpu_custom_call" | custom-call | tf_op jit(solution)/shard_map/attend_own/pallas_call | solution.py:25
  2.9 0.0 collective-permute-done.1.values_ref
  3.0 1.2 %attend_other.1 = (bf16[128,1024]{1,0:T(8,128)(2,1)S(1)}, bf16[128,512]{1,0:T(8,128)(2,1)S(1)}, bf16[128,512]{1,0:T(8,128)(2,1)S(1)}, f32[2,128]{1,0:T(2,128)S(1)}, s32[2,2,128]{2,1,0:T(2,128)S(1)}) custom-call(s32[1]{0:T(128)} %bitcast.core_ref, s32[1]{0:T(128)S(6)} %copy.24.source_ref, bf16[128,512]{1,0:T(8,128)(2,1)S(1)} %get-tuple-element.28.own_ref, ...), custom_call_target="tpu_custom_call" | custom-call | tf_op jit(solution)/shard_map/attend_other/pallas_call | solution.py:25
  4.2 0.5 collective-permute-start.2
  4.7 1.0 %collective-permute-done.2.other_ref = bf16[128,512]{1,0:T(8,128)(2,1)S(1)} collective-permute-done((bf16[128,512]{1,0:T(8,128)(2,1)S(1)}, bf16[128,512]{1,0:T(8,128)(2,1)S(1)}, u32[]{:S(2)}, u32[]{:S(2)}) %collective-permute-start.2) | collective-permute-done | bytes 131104 | tf_op jit(solution)/shard_map/ppermute | solution.py:303
  5.7 0.5 select.5
  6.2 2.9 %collective-permute-start.3 = (bf16[192,512]{1,0:T(8,128)(2,1)S(1)}, bf16[192,512]{1,0:T(8,128)(2,1)S(1)}, u32[]{:S(2)}, u32[]{:S(2)}) collective-permute-start(bf16[192,512]{1,0:T(8,128)(2,1)S(1)} %get-tuple-element.37.p_ref), channel_id=1, source_target_pairs={{0,2},{2,0},{4,6},{6,4},{8,10},{10,8},{12,14},{14,12},{1,3},{3,1},... | collective-permute-start | bytes 589832 | tf_op jit(solution)/shard_map/ppermute | solution.py:308
  9.2 1.6 %collective-permute-start.13 = (bf16[192,512]{1,0:T(8,128)(2,1)S(1)}, bf16[192,512]{1,0:T(8,128)(2,1)S(1)}, u32[]{:S(2)}, u32[]{:S(2)}) collective-permute-start(bf16[192,512]{1,0:T(8,128)(2,1)S(1)} %get-tuple-element.44), channel_id=1, source_target_pairs={{0,4},{2,6},{4,0},{6,2},{8,12},{10,14},{12,8},{14,10},{1,5},{3,7},... | collective-permute-start | bytes 589832 | tf_op jit(solution)/shard_map/ppermute | solution.py:313
  10.7 2.6 %collective-permute-start.9 = (bf16[192,512]{1,0:T(8,128)(2,1)S(1)}, bf16[192,512]{1,0:T(8,128)(2,1)S(1)}, u32[]{:S(2)}, u32[]{:S(2)}) collective-permute-start(bf16[192,512]{1,0:T(8,128)(2,1)S(1)} %get-tuple-element.43), channel_id=1, source_target_pairs={{0,8},{2,10},{4,12},{6,14},{8,0},{10,2},{12,4},{14,6},{1,9},{3,11}... | collective-permute-start | bytes 589832 | tf_op jit(solution)/shard_map/ppermute | solution.py:313
  13.3 0.0 collective-permute-start.4
  13.3 1.1 %collective-permute-done.3.q_ref = bf16[192,512]{1,0:T(8,128)(2,1)S(1)} collective-permute-done((bf16[192,512]{1,0:T(8,128)(2,1)S(1)}, bf16[192,512]{1,0:T(8,128)(2,1)S(1)}, u32[]{:S(2)}, u32[]{:S(2)}) %collective-permute-start.3) | collective-permute-done | bytes 196640 | tf_op jit(solution)/shard_map/ppermute | solution.py:308
  14.4 0.0 collective-permute-start.5
  14.4 2.2 %load.1 = (bf16[1024,1024]{1,0:T(8,128)(2,1)S(1)}, bf16[1024,1024]{1,0:T(8,128)(2,1)S(1)}) custom-call(bf16[1024,1024]{1,0:T(8,128)(2,1)} %in_in.1, bf16[1024,1024]{1,0:T(8,128)(2,1)} %out_in.1), custom_call_target="tpu_custom_call" | custom-call | tf_op jit(solution)/shard_map/load/pallas_call | solution.py:25
  16.6 3.3 %collective-permute-done.13.refs_0_ = bf16[192,512]{1,0:T(8,128)(2,1)S(1)} collective-permute-done((bf16[192,512]{1,0:T(8,128)(2,1)S(1)}, bf16[192,512]{1,0:T(8,128)(2,1)S(1)}, u32[]{:S(2)}, u32[]{:S(2)}) %collective-permute-start.13) | collective-permute-done | bytes 196640 | tf_op jit(solution)/shard_map/ppermute | solution.py:313
  19.9 0.4 collective-permute-start.14
  20.3 2.0 %collective-permute-done.9.p_ref = bf16[192,512]{1,0:T(8,128)(2,1)S(1)} collective-permute-done((bf16[192,512]{1,0:T(8,128)(2,1)S(1)}, bf16[192,512]{1,0:T(8,128)(2,1)S(1)}, u32[]{:S(2)}, u32[]{:S(2)}) %collective-permute-start.9) | collective-permute-done | bytes 196640 | tf_op jit(solution)/shard_map/ppermute | solution.py:313
  22.3 0.5 collective-permute-start.10
  22.8 2.5 %collective-permute-start.7 = (bf16[192,512]{1,0:T(8,128)(2,1)S(1)}, bf16[192,512]{1,0:T(8,128)(2,1)S(1)}, u32[]{:S(2)}, u32[]{:S(2)}) collective-permute-start(bf16[192,512]{1,0:T(8,128)(2,1)S(1)} %get-tuple-element.42), channel_id=1, source_target_pairs={{0,12},{2,14},{4,8},{6,10},{8,4},{10,6},{12,0},{14,2},{1,13},{3,15... | collective-permute-start | bytes 589832 | tf_op jit(solution)/shard_map/ppermute | solution.py:313
  25.3 1.8 %expert.4 = (f32[2,192,512]{2,1,0:T(8,128)S(1)}, bf16[2,192,512]{2,1,0:T(8,128)(2,1)S(1)}) custom-call(s32[1]{0:T(128)} %bitcast.core_ref, bf16[192,512]{1,0:T(8,128)(2,1)S(1)} %get-tuple-element.37.p_ref, bf16[192,512]{1,0:T(8,128)(2,1)S(1)} %collective-permute-done.3.q_ref, bf16[192,512]{1,0:T(8,128)(2,1)S(1)} %collective-permute-done.4.p2_ref, ...), custom_call_target="tpu_custom_call" | custom-call | tf_op jit(solution)/shard_map/expert/pallas_call | solution.py:25
  27.2 0.6 collective-permute-start.6
  27.7 0.1 collective-permute-start.16
  27.8 1.8 %collective-permute-done.10.q_ref = bf16[192,512]{1,0:T(8,128)(2,1)S(1)} collective-permute-done((bf16[192,512]{1,0:T(8,128)(2,1)S(1)}, bf16[192,512]{1,0:T(8,128)(2,1)S(1)}, u32[]{:S(2)}, u32[]{:S(2)}) %collective-permute-start.10) | collective-permute-done | bytes 196640 | tf_op jit(solution)/shard_map/ppermute | solution.py:308
  29.6 0.0 collective-permute-start.12
  29.6 0.8 %collective-permute-done.7.p_ref = bf16[192,512]{1,0:T(8,128)(2,1)S(1)} collective-permute-done((bf16[192,512]{1,0:T(8,128)(2,1)S(1)}, bf16[192,512]{1,0:T(8,128)(2,1)S(1)}, u32[]{:S(2)}, u32[]{:S(2)}) %collective-permute-start.7) | collective-permute-done | bytes 196640 | tf_op jit(solution)/shard_map/ppermute | solution.py:313
  30.4 1.5 %collective-permute-start.8 = (bf16[192,512]{1,0:T(8,128)(2,1)S(1)}, bf16[192,512]{1,0:T(8,128)(2,1)S(1)}, u32[]{:S(2)}, u32[]{:S(2)}) collective-permute-start(bf16[192,512]{1,0:T(8,128)(2,1)S(1)} %collective-permute-done.7.p_ref), channel_id=1, source_target_pairs={{0,2},{2,0},{4,6},{6,4},{8,10},{10,8},{12,14},{14,12},{1,3},{3,1},... | collective-permute-start | bytes 589832 | tf_op jit(solution)/shard_map/ppermute | solution.py:308
  31.9 0.2 collective-permute-start.29
  32.1 1.8 %expert.5 = (f32[2,192,512]{2,1,0:T(8,128)S(1)}, bf16[2,192,512]{2,1,0:T(8,128)(2,1)S(1)}) custom-call(s32[1]{0:T(128)} %bitcast.core_ref, bf16[192,512]{1,0:T(8,128)(2,1)S(1)} %after.6.p_ref, bf16[192,512]{1,0:T(8,128)(2,1)S(1)} %collective-permute-done.14.q_ref, bf16[192,512]{1,0:T(8,128)(2,1)S(1)} %collective-permute-done.15.p2_ref, ...), custom_call_target="tpu_custom_call" | custom-call | tf_op jit(solution)/shard_map/expert/pallas_call | solution.py:25
  34.0 0.3 collective-permute-start.17
  34.3 0.0 collective-permute-done.11.p2_ref
  34.3 1.8 %expert.6 = (f32[2,192,512]{2,1,0:T(8,128)S(1)}, bf16[2,192,512]{2,1,0:T(8,128)(2,1)S(1)}) custom-call(s32[1]{0:T(128)} %bitcast.core_ref, bf16[192,512]{1,0:T(8,128)(2,1)S(1)} %collective-permute-done.9.p_ref, bf16[192,512]{1,0:T(8,128)(2,1)S(1)} %collective-permute-done.10.q_ref, bf16[192,512]{1,0:T(8,128)(2,1)S(1)} %collective-permute-done.11.p2_ref, ...), custom_call_target="tpu_custom_call" | custom-call | tf_op jit(solution)/shard_map/expert/pallas_call | solution.py:25
  36.2 0.3 collective-permute-start.19
  36.5 1.2 %collective-permute-done.8.refs_0_ = bf16[192,512]{1,0:T(8,128)(2,1)S(1)} collective-permute-done((bf16[192,512]{1,0:T(8,128)(2,1)S(1)}, bf16[192,512]{1,0:T(8,128)(2,1)S(1)}, u32[]{:S(2)}, u32[]{:S(2)}) %collective-permute-start.8) | collective-permute-done | bytes 196640 | tf_op jit(solution)/shard_map/ppermute | solution.py:308
  37.7 0.0 collective-permute-done.6
  37.7 0.5 collective-permute-start.18
  38.2 0.1 convert_add_fusion.3
  38.4 0.0 collective-permute-done.19
  38.4 0.1 convert_add_fusion.2
  38.5 1.6 %collective-permute-start.26 = (bf16[192,512]{1,0:T(8,128)(2,1)S(1)}, bf16[192,512]{1,0:T(8,128)(2,1)S(1)}, u32[]{:S(2)}, u32[]{:S(2)}) collective-permute-start(bf16[192,512]{1,0:T(8,128)(2,1)S(1)} %fusion.9.refs_1_), channel_id=1, source_target_pairs={{0,2},{2,0},{4,6},{6,4},{8,10},{10,8},{12,14},{14,12},{1,3},{3,1},... | collective-permute-start | bytes 589832 | tf_op jit(solution)/shard_map/ppermute | solution.py:308
  40.1 0.0 collective-permute-done.18.refs_0_
  40.1 0.0 collective-permute-done.17.p2_ref
  40.1 1.8 %expert.7 = (f32[2,192,512]{2,1,0:T(8,128)S(1)}, bf16[2,192,512]{2,1,0:T(8,128)(2,1)S(1)}) custom-call(s32[1]{0:T(128)} %bitcast.core_ref, bf16[192,512]{1,0:T(8,128)(2,1)S(1)} %collective-permute-done.7.p_ref, bf16[192,512]{1,0:T(8,128)(2,1)S(1)} %after.8.q_ref, bf16[192,512]{1,0:T(8,128)(2,1)S(1)} %collective-permute-done.17.p2_ref, ...), custom_call_target="tpu_custom_call" | custom-call | tf_op jit(solution)/shard_map/expert/pallas_call | solution.py:25
  42.0 0.1 collective-permute-start.20
  42.1 0.1 convert_add_fusion
  42.2 1.5 %collective-permute-done.20 = bf16[2,192,512]{2,1,0:T(8,128)(2,1)S(1)} collective-permute-done((bf16[2,192,512]{2,1,0:T(8,128)(2,1)S(1)}, bf16[2,192,512]{2,1,0:T(8,128)(2,1)S(1)}, u32[]{:S(2)}, u32[]{:S(2)}) %collective-permute-start.20) | collective-permute-done | bytes 393248 | tf_op jit(solution)/shard_map/ppermute | solution.py:303
  43.8 0.1 convert_add_fusion.1
  43.9 1.2 %collective-permute-start.21 = (bf16[192,512]{1,0:T(8,128)(2,1)S(1)}, bf16[192,512]{1,0:T(8,128)(2,1)S(1)}, u32[]{:S(2)}, u32[]{:S(2)}) collective-permute-start(bf16[192,512]{1,0:T(8,128)(2,1)S(1)} %fusion.10.refs_1_), channel_id=1, source_target_pairs={{0,2},{2,0},{4,6},{6,4},{8,10},{10,8},{12,14},{14,12},{1,3},{3,1},... | collective-permute-start | bytes 589832 | tf_op jit(solution)/shard_map/ppermute | solution.py:308
  45.1 0.4 collective-permute-done.26
  45.5 0.1 fusion.1
  45.5 2.5 %collective-permute-start.27 = (bf16[192,512]{1,0:T(8,128)(2,1)S(1)}, bf16[192,512]{1,0:T(8,128)(2,1)S(1)}, u32[]{:S(2)}, u32[]{:S(2)}) collective-permute-start(bf16[192,512]{1,0:T(8,128)(2,1)S(1)} %fusion.1), channel_id=1, source_target_pairs={{0,8},{2,10},{4,12},{6,14},{8,0},{10,2},{12,4},{14,6},{1,9},{3,11}... | collective-permute-start | bytes 589832 | tf_op jit(solution)/shard_map/ppermute | solution.py:313
  48.0 1.5 %collective-permute-start.24 = (bf16[192,512]{1,0:T(8,128)(2,1)S(1)}, bf16[192,512]{1,0:T(8,128)(2,1)S(1)}, u32[]{:S(2)}, u32[]{:S(2)}) collective-permute-start(bf16[192,512]{1,0:T(8,128)(2,1)S(1)} %after.11), channel_id=1, source_target_pairs={{0,2},{2,0},{4,6},{6,4},{8,10},{10,8},{12,14},{14,12},{1,3},{3,1},... | collective-permute-start | bytes 589832 | tf_op jit(solution)/shard_map/ppermute | solution.py:308
  49.6 2.2 %collective-permute-done.21 = bf16[192,512]{1,0:T(8,128)(2,1)S(1)} collective-permute-done((bf16[192,512]{1,0:T(8,128)(2,1)S(1)}, bf16[192,512]{1,0:T(8,128)(2,1)S(1)}, u32[]{:S(2)}, u32[]{:S(2)}) %collective-permute-start.21) | collective-permute-done | bytes 196640 | tf_op jit(solution)/shard_map/ppermute | solution.py:308
  51.8 2.5 %collective-permute-start.28 = (bf16[192,512]{1,0:T(8,128)(2,1)S(1)}, bf16[192,512]{1,0:T(8,128)(2,1)S(1)}, u32[]{:S(2)}, u32[]{:S(2)}) collective-permute-start(bf16[192,512]{1,0:T(8,128)(2,1)S(1)} %fusion.5.refs_1_), channel_id=1, source_target_pairs={{0,12},{2,14},{4,8},{6,10},{8,4},{10,6},{12,0},{14,2},{1,13},{3,15... | collective-permute-start | bytes 589832 | tf_op jit(solution)/shard_map/ppermute | solution.py:313
  54.3 1.1 %collective-permute-start.22 = (bf16[192,512]{1,0:T(8,128)(2,1)S(1)}, bf16[192,512]{1,0:T(8,128)(2,1)S(1)}, u32[]{:S(2)}, u32[]{:S(2)}) collective-permute-start(bf16[192,512]{1,0:T(8,128)(2,1)S(1)} %after.10), channel_id=1, source_target_pairs={{0,2},{2,0},{4,6},{6,4},{8,10},{10,8},{12,14},{14,12},{1,3},{3,1},... | collective-permute-start | bytes 589832 | tf_op jit(solution)/shard_map/ppermute | solution.py:308
  55.4 3.0 %collective-permute-start.25 = (bf16[192,512]{1,0:T(8,128)(2,1)S(1)}, bf16[192,512]{1,0:T(8,128)(2,1)S(1)}, u32[]{:S(2)}, u32[]{:S(2)}) collective-permute-start(bf16[192,512]{1,0:T(8,128)(2,1)S(1)} %fusion.3), channel_id=1, source_target_pairs={{0,4},{2,6},{4,0},{6,2},{8,12},{10,14},{12,8},{14,10},{1,5},{3,7},... | collective-permute-start | bytes 589832 | tf_op jit(solution)/shard_map/ppermute | solution.py:313
  58.4 1.5 %collective-permute-done.22 = bf16[192,512]{1,0:T(8,128)(2,1)S(1)} collective-permute-done((bf16[192,512]{1,0:T(8,128)(2,1)S(1)}, bf16[192,512]{1,0:T(8,128)(2,1)S(1)}, u32[]{:S(2)}, u32[]{:S(2)}) %collective-permute-start.22) | collective-permute-done | bytes 196640 | tf_op jit(solution)/shard_map/ppermute | solution.py:308
  60.0 2.8 %collective-permute-done.27.rest_2_ = bf16[192,512]{1,0:T(8,128)(2,1)S(1)} collective-permute-done((bf16[192,512]{1,0:T(8,128)(2,1)S(1)}, bf16[192,512]{1,0:T(8,128)(2,1)S(1)}, u32[]{:S(2)}, u32[]{:S(2)}) %collective-permute-start.27) | collective-permute-done | bytes 196640 | tf_op jit(solution)/shard_map/ppermute | solution.py:313
  62.8 2.6 %collective-permute-done.25.rest_1_ = bf16[192,512]{1,0:T(8,128)(2,1)S(1)} collective-permute-done((bf16[192,512]{1,0:T(8,128)(2,1)S(1)}, bf16[192,512]{1,0:T(8,128)(2,1)S(1)}, u32[]{:S(2)}, u32[]{:S(2)}) %collective-permute-start.25) | collective-permute-done | bytes 196640 | tf_op jit(solution)/shard_map/ppermute | solution.py:313
  65.4 0.6 combine_other.1
  66.0 0.1 collective-permute-start.30
  66.1 0.6 combine_own.1.own_ref
  66.7 0.7 %collective-permute-done.30.other_ref = bf16[128,512]{1,0:T(8,128)(2,1)S(1)} collective-permute-done((bf16[128,512]{1,0:T(8,128)(2,1)S(1)}, bf16[128,512]{1,0:T(8,128)(2,1)S(1)}, u32[]{:S(2)}, u32[]{:S(2)}) %collective-permute-start.30) | collective-permute-done | bytes 131104 | tf_op jit(solution)/shard_map/ppermute | solution.py:303
  67.4 0.7 %finish.1 = bf16[128,1024]{1,0:T(8,128)(2,1)} custom-call(s32[1]{0:T(128)} %bitcast.core_ref, bf16[128,1024]{1,0:T(8,128)(2,1)S(1)} %get-tuple-element.31.state_ref, bf16[128,512]{1,0:T(8,128)(2,1)S(1)} %combine_own.1.own_ref, bf16[128,512]{1,0:T(8,128)(2,1)S(1)} %collective-permute-done.30.other_ref), custom_call_target="tpu_custom_call" | custom-call | tf_op jit(solution)/shard_map/finish/pallas_call | solution.py:25
  (27 shorter events, 0.3 us)
Async XLA Ops:
  0.0 2.9 %collective-permute-start = (bf16[2,80,512]{2,1,0:T(8,128)(2,1)}, bf16[2,80,512]{2,1,0:T(8,128)(2,1)S(1)}, u32[]{:S(2)}, u32[]{:S(2)}) collective-permute-start(bf16[2,80,512]{2,1,0:T(8,128)(2,1)} %keys_in.1), channel_id=1, source_target_pairs={{0,1},{1,0},{2,3},{3,2},{4,5},{5,4},{6,7},{7,6},{8,9},{9,8},{10,11... | collective-permute-start | bytes 491528 | tf_op jit(solution)/shard_map/ppermute | solution.py:303
  0.5 2.5 %collective-permute-start.1 = (bf16[2,80,512]{2,1,0:T(8,128)(2,1)}, bf16[2,80,512]{2,1,0:T(8,128)(2,1)S(1)}, u32[]{:S(2)}, u32[]{:S(2)}) collective-permute-start(bf16[2,80,512]{2,1,0:T(8,128)(2,1)} %values_in.1), channel_id=1, source_target_pairs={{0,1},{1,0},{2,3},{3,2},{4,5},{5,4},{6,7},{7,6},{8,9},{9,8},{10,11... | collective-permute-start | bytes 491528 | tf_op jit(solution)/shard_map/ppermute | solution.py:303
  4.2 1.5 %collective-permute-start.2 = (bf16[128,512]{1,0:T(8,128)(2,1)S(1)}, bf16[128,512]{1,0:T(8,128)(2,1)S(1)}, u32[]{:S(2)}, u32[]{:S(2)}) collective-permute-start(bf16[128,512]{1,0:T(8,128)(2,1)S(1)} %get-tuple-element.35), channel_id=1, source_target_pairs={{0,1},{1,0},{2,3},{3,2},{4,5},{5,4},{6,7},{7,6},{8,9},{9,8},{10,11... | collective-permute-start | bytes 393224 | tf_op jit(solution)/shard_map/ppermute | solution.py:303
  6.2 8.1 %collective-permute-start.3 = (bf16[192,512]{1,0:T(8,128)(2,1)S(1)}, bf16[192,512]{1,0:T(8,128)(2,1)S(1)}, u32[]{:S(2)}, u32[]{:S(2)}) collective-permute-start(bf16[192,512]{1,0:T(8,128)(2,1)S(1)} %get-tuple-element.37.p_ref), channel_id=1, source_target_pairs={{0,2},{2,0},{4,6},{6,4},{8,10},{10,8},{12,14},{14,12},{1,3},{3,1},... | collective-permute-start | bytes 589832 | tf_op jit(solution)/shard_map/ppermute | solution.py:308
  9.2 10.8 %collective-permute-start.13 = (bf16[192,512]{1,0:T(8,128)(2,1)S(1)}, bf16[192,512]{1,0:T(8,128)(2,1)S(1)}, u32[]{:S(2)}, u32[]{:S(2)}) collective-permute-start(bf16[192,512]{1,0:T(8,128)(2,1)S(1)} %get-tuple-element.44), channel_id=1, source_target_pairs={{0,4},{2,6},{4,0},{6,2},{8,12},{10,14},{12,8},{14,10},{1,5},{3,7},... | collective-permute-start | bytes 589832 | tf_op jit(solution)/shard_map/ppermute | solution.py:313
  10.7 11.6 %collective-permute-start.9 = (bf16[192,512]{1,0:T(8,128)(2,1)S(1)}, bf16[192,512]{1,0:T(8,128)(2,1)S(1)}, u32[]{:S(2)}, u32[]{:S(2)}) collective-permute-start(bf16[192,512]{1,0:T(8,128)(2,1)S(1)} %get-tuple-element.43), channel_id=1, source_target_pairs={{0,8},{2,10},{4,12},{6,14},{8,0},{10,2},{12,4},{14,6},{1,9},{3,11}... | collective-permute-start | bytes 589832 | tf_op jit(solution)/shard_map/ppermute | solution.py:313
  13.3 12.0 %collective-permute-start.4 = (bf16[192,512]{1,0:T(8,128)(2,1)S(1)}, bf16[192,512]{1,0:T(8,128)(2,1)S(1)}, u32[]{:S(2)}, u32[]{:S(2)}) collective-permute-start(bf16[192,512]{1,0:T(8,128)(2,1)S(1)} %get-tuple-element.37.p_ref), channel_id=1, source_target_pairs={{0,1},{1,0},{2,3},{3,2},{4,5},{5,4},{6,7},{7,6},{8,9},{9,8},{10,11... | collective-permute-start | bytes 589832 | tf_op jit(solution)/shard_map/ppermute | solution.py:303
  14.4 10.9 %collective-permute-start.5 = (bf16[192,512]{1,0:T(8,128)(2,1)S(1)}, bf16[192,512]{1,0:T(8,128)(2,1)S(1)}, u32[]{:S(2)}, u32[]{:S(2)}) collective-permute-start(bf16[192,512]{1,0:T(8,128)(2,1)S(1)} %collective-permute-done.3.q_ref), channel_id=1, source_target_pairs={{0,1},{1,0},{2,3},{3,2},{4,5},{5,4},{6,7},{7,6},{8,9},{9,8},{10,11... | collective-permute-start | bytes 589832 | tf_op jit(solution)/shard_map/ppermute | solution.py:303
  19.9 7.8 %collective-permute-start.14 = (bf16[192,512]{1,0:T(8,128)(2,1)S(1)}, bf16[192,512]{1,0:T(8,128)(2,1)S(1)}, u32[]{:S(2)}, u32[]{:S(2)}) collective-permute-start(bf16[192,512]{1,0:T(8,128)(2,1)S(1)} %after.6.p_ref), channel_id=1, source_target_pairs={{0,2},{2,0},{4,6},{6,4},{8,10},{10,8},{12,14},{14,12},{1,3},{3,1},... | collective-permute-start | bytes 589832 | tf_op jit(solution)/shard_map/ppermute | solution.py:308
  22.3 7.3 %collective-permute-start.10 = (bf16[192,512]{1,0:T(8,128)(2,1)S(1)}, bf16[192,512]{1,0:T(8,128)(2,1)S(1)}, u32[]{:S(2)}, u32[]{:S(2)}) collective-permute-start(bf16[192,512]{1,0:T(8,128)(2,1)S(1)} %collective-permute-done.9.p_ref), channel_id=1, source_target_pairs={{0,2},{2,0},{4,6},{6,4},{8,10},{10,8},{12,14},{14,12},{1,3},{3,1},... | collective-permute-start | bytes 589832 | tf_op jit(solution)/shard_map/ppermute | solution.py:308
  22.8 7.6 %collective-permute-start.7 = (bf16[192,512]{1,0:T(8,128)(2,1)S(1)}, bf16[192,512]{1,0:T(8,128)(2,1)S(1)}, u32[]{:S(2)}, u32[]{:S(2)}) collective-permute-start(bf16[192,512]{1,0:T(8,128)(2,1)S(1)} %get-tuple-element.42), channel_id=1, source_target_pairs={{0,12},{2,14},{4,8},{6,10},{8,4},{10,6},{12,0},{14,2},{1,13},{3,15... | collective-permute-start | bytes 589832 | tf_op jit(solution)/shard_map/ppermute | solution.py:313
  25.3 5.1 %collective-permute-start.15 = (bf16[192,512]{1,0:T(8,128)(2,1)S(1)}, bf16[192,512]{1,0:T(8,128)(2,1)S(1)}, u32[]{:S(2)}, u32[]{:S(2)}) collective-permute-start(bf16[192,512]{1,0:T(8,128)(2,1)S(1)} %after.6.p_ref), channel_id=1, source_target_pairs={{0,1},{1,0},{2,3},{3,2},{4,5},{5,4},{6,7},{7,6},{8,9},{9,8},{10,11... | collective-permute-start | bytes 589832 | tf_op jit(solution)/shard_map/ppermute | solution.py:303
  27.2 10.6 %collective-permute-start.6 = (bf16[2,192,512]{2,1,0:T(8,128)(2,1)S(1)}, bf16[2,192,512]{2,1,0:T(8,128)(2,1)S(1)}, u32[]{:S(2)}, u32[]{:S(2)}) collective-permute-start(bf16[2,192,512]{2,1,0:T(8,128)(2,1)S(1)} %get-tuple-element.41), channel_id=1, source_target_pairs={{0,1},{1,0},{2,3},{3,2},{4,5},{5,4},{6,7},{7,6},{8,9},{9,8},{10,11... | collective-permute-start | bytes 1179656 | tf_op jit(solution)/shard_map/ppermute | solution.py:303
  27.7 4.2 %collective-permute-start.16 = (bf16[192,512]{1,0:T(8,128)(2,1)S(1)}, bf16[192,512]{1,0:T(8,128)(2,1)S(1)}, u32[]{:S(2)}, u32[]{:S(2)}) collective-permute-start(bf16[192,512]{1,0:T(8,128)(2,1)S(1)} %collective-permute-done.14.q_ref), channel_id=1, source_target_pairs={{0,1},{1,0},{2,3},{3,2},{4,5},{5,4},{6,7},{7,6},{8,9},{9,8},{10,11... | collective-permute-start | bytes 589832 | tf_op jit(solution)/shard_map/ppermute | solution.py:303
  29.6 4.4 %collective-permute-start.12 = (bf16[192,512]{1,0:T(8,128)(2,1)S(1)}, bf16[192,512]{1,0:T(8,128)(2,1)S(1)}, u32[]{:S(2)}, u32[]{:S(2)}) collective-permute-start(bf16[192,512]{1,0:T(8,128)(2,1)S(1)} %collective-permute-done.10.q_ref), channel_id=1, source_target_pairs={{0,1},{1,0},{2,3},{3,2},{4,5},{5,4},{6,7},{7,6},{8,9},{9,8},{10,11... | collective-permute-start | bytes 589832 | tf_op jit(solution)/shard_map/ppermute | solution.py:303
  30.4 4.0 %collective-permute-start.11 = (bf16[192,512]{1,0:T(8,128)(2,1)S(1)}, bf16[192,512]{1,0:T(8,128)(2,1)S(1)}, u32[]{:S(2)}, u32[]{:S(2)}) collective-permute-start(bf16[192,512]{1,0:T(8,128)(2,1)S(1)} %collective-permute-done.9.p_ref), channel_id=1, source_target_pairs={{0,1},{1,0},{2,3},{3,2},{4,5},{5,4},{6,7},{7,6},{8,9},{9,8},{10,11... | collective-permute-start | bytes 589832 | tf_op jit(solution)/shard_map/ppermute | solution.py:303
  30.4 7.3 %collective-permute-start.8 = (bf16[192,512]{1,0:T(8,128)(2,1)S(1)}, bf16[192,512]{1,0:T(8,128)(2,1)S(1)}, u32[]{:S(2)}, u32[]{:S(2)}) collective-permute-start(bf16[192,512]{1,0:T(8,128)(2,1)S(1)} %collective-permute-done.7.p_ref), channel_id=1, source_target_pairs={{0,2},{2,0},{4,6},{6,4},{8,10},{10,8},{12,14},{14,12},{1,3},{3,1},... | collective-permute-start | bytes 589832 | tf_op jit(solution)/shard_map/ppermute | solution.py:308
  31.9 28.1 %collective-permute-start.29 = (f32[2,128]{1,0:T(2,128)S(1)}, f32[2,128]{1,0:T(2,128)S(1)}, u32[]{:S(2)}, u32[]{:S(2)}) collective-permute-start(f32[2,128]{1,0:T(2,128)S(1)} %get-tuple-element.33.gates_ref), channel_id=1, source_target_pairs={{0,1},{1,0},{2,3},{3,2},{4,5},{5,4},{6,7},{7,6},{8,9},{9,8},{10,11... | collective-permute-start | bytes 3080 | tf_op jit(solution)/shard_map/ppermute | solution.py:303
  34.0 6.1 %collective-permute-start.17 = (bf16[192,512]{1,0:T(8,128)(2,1)S(1)}, bf16[192,512]{1,0:T(8,128)(2,1)S(1)}, u32[]{:S(2)}, u32[]{:S(2)}) collective-permute-start(bf16[192,512]{1,0:T(8,128)(2,1)S(1)} %collective-permute-done.7.p_ref), channel_id=1, source_target_pairs={{0,1},{1,0},{2,3},{3,2},{4,5},{5,4},{6,7},{7,6},{8,9},{9,8},{10,11... | collective-permute-start | bytes 589832 | tf_op jit(solution)/shard_map/ppermute | solution.py:303
  36.2 2.2 %collective-permute-start.19 = (bf16[2,192,512]{2,1,0:T(8,128)(2,1)S(1)}, bf16[2,192,512]{2,1,0:T(8,128)(2,1)S(1)}, u32[]{:S(2)}, u32[]{:S(2)}) collective-permute-start(bf16[2,192,512]{2,1,0:T(8,128)(2,1)S(1)} %get-tuple-element.47), channel_id=1, source_target_pairs={{0,1},{1,0},{2,3},{3,2},{4,5},{5,4},{6,7},{7,6},{8,9},{9,8},{10,11... | collective-permute-start | bytes 1179656 | tf_op jit(solution)/shard_map/ppermute | solution.py:303
  37.7 4.3 %collective-permute-start.23 = (bf16[2,192,512]{2,1,0:T(8,128)(2,1)S(1)}, bf16[2,192,512]{2,1,0:T(8,128)(2,1)S(1)}, u32[]{:S(2)}, u32[]{:S(2)}) collective-permute-start(bf16[2,192,512]{2,1,0:T(8,128)(2,1)S(1)} %get-tuple-element.50), channel_id=1, source_target_pairs={{0,1},{1,0},{2,3},{3,2},{4,5},{5,4},{6,7},{7,6},{8,9},{9,8},{10,11... | collective-permute-start | bytes 1179656 | tf_op jit(solution)/shard_map/ppermute | solution.py:303
  37.7 2.4 %collective-permute-start.18 = (bf16[192,512]{1,0:T(8,128)(2,1)S(1)}, bf16[192,512]{1,0:T(8,128)(2,1)S(1)}, u32[]{:S(2)}, u32[]{:S(2)}) collective-permute-start(bf16[192,512]{1,0:T(8,128)(2,1)S(1)} %after.8.q_ref), channel_id=1, source_target_pairs={{0,1},{1,0},{2,3},{3,2},{4,5},{5,4},{6,7},{7,6},{8,9},{9,8},{10,11... | collective-permute-start | bytes 589832 | tf_op jit(solution)/shard_map/ppermute | solution.py:303
  38.5 6.9 %collective-permute-start.26 = (bf16[192,512]{1,0:T(8,128)(2,1)S(1)}, bf16[192,512]{1,0:T(8,128)(2,1)S(1)}, u32[]{:S(2)}, u32[]{:S(2)}) collective-permute-start(bf16[192,512]{1,0:T(8,128)(2,1)S(1)} %fusion.9.refs_1_), channel_id=1, source_target_pairs={{0,2},{2,0},{4,6},{6,4},{8,10},{10,8},{12,14},{14,12},{1,3},{3,1},... | collective-permute-start | bytes 589832 | tf_op jit(solution)/shard_map/ppermute | solution.py:308
  42.0 1.8 %collective-permute-start.20 = (bf16[2,192,512]{2,1,0:T(8,128)(2,1)S(1)}, bf16[2,192,512]{2,1,0:T(8,128)(2,1)S(1)}, u32[]{:S(2)}, u32[]{:S(2)}) collective-permute-start(bf16[2,192,512]{2,1,0:T(8,128)(2,1)S(1)} %get-tuple-element.49), channel_id=1, source_target_pairs={{0,1},{1,0},{2,3},{3,2},{4,5},{5,4},{6,7},{7,6},{8,9},{9,8},{10,11... | collective-permute-start | bytes 1179656 | tf_op jit(solution)/shard_map/ppermute | solution.py:303
  43.9 7.8 %collective-permute-start.21 = (bf16[192,512]{1,0:T(8,128)(2,1)S(1)}, bf16[192,512]{1,0:T(8,128)(2,1)S(1)}, u32[]{:S(2)}, u32[]{:S(2)}) collective-permute-start(bf16[192,512]{1,0:T(8,128)(2,1)S(1)} %fusion.10.refs_1_), channel_id=1, source_target_pairs={{0,2},{2,0},{4,6},{6,4},{8,10},{10,8},{12,14},{14,12},{1,3},{3,1},... | collective-permute-start | bytes 589832 | tf_op jit(solution)/shard_map/ppermute | solution.py:308
  45.5 17.3 %collective-permute-start.27 = (bf16[192,512]{1,0:T(8,128)(2,1)S(1)}, bf16[192,512]{1,0:T(8,128)(2,1)S(1)}, u32[]{:S(2)}, u32[]{:S(2)}) collective-permute-start(bf16[192,512]{1,0:T(8,128)(2,1)S(1)} %fusion.1), channel_id=1, source_target_pairs={{0,8},{2,10},{4,12},{6,14},{8,0},{10,2},{12,4},{14,6},{1,9},{3,11}... | collective-permute-start | bytes 589832 | tf_op jit(solution)/shard_map/ppermute | solution.py:313
  48.0 7.3 %collective-permute-start.24 = (bf16[192,512]{1,0:T(8,128)(2,1)S(1)}, bf16[192,512]{1,0:T(8,128)(2,1)S(1)}, u32[]{:S(2)}, u32[]{:S(2)}) collective-permute-start(bf16[192,512]{1,0:T(8,128)(2,1)S(1)} %after.11), channel_id=1, source_target_pairs={{0,2},{2,0},{4,6},{6,4},{8,10},{10,8},{12,14},{14,12},{1,3},{3,1},... | collective-permute-start | bytes 589832 | tf_op jit(solution)/shard_map/ppermute | solution.py:308
  51.8 13.6 %collective-permute-start.28 = (bf16[192,512]{1,0:T(8,128)(2,1)S(1)}, bf16[192,512]{1,0:T(8,128)(2,1)S(1)}, u32[]{:S(2)}, u32[]{:S(2)}) collective-permute-start(bf16[192,512]{1,0:T(8,128)(2,1)S(1)} %fusion.5.refs_1_), channel_id=1, source_target_pairs={{0,12},{2,14},{4,8},{6,10},{8,4},{10,6},{12,0},{14,2},{1,13},{3,15... | collective-permute-start | bytes 589832 | tf_op jit(solution)/shard_map/ppermute | solution.py:313
  54.3 5.7 %collective-permute-start.22 = (bf16[192,512]{1,0:T(8,128)(2,1)S(1)}, bf16[192,512]{1,0:T(8,128)(2,1)S(1)}, u32[]{:S(2)}, u32[]{:S(2)}) collective-permute-start(bf16[192,512]{1,0:T(8,128)(2,1)S(1)} %after.10), channel_id=1, source_target_pairs={{0,2},{2,0},{4,6},{6,4},{8,10},{10,8},{12,14},{14,12},{1,3},{3,1},... | collective-permute-start | bytes 589832 | tf_op jit(solution)/shard_map/ppermute | solution.py:308
  55.4 10.0 %collective-permute-start.25 = (bf16[192,512]{1,0:T(8,128)(2,1)S(1)}, bf16[192,512]{1,0:T(8,128)(2,1)S(1)}, u32[]{:S(2)}, u32[]{:S(2)}) collective-permute-start(bf16[192,512]{1,0:T(8,128)(2,1)S(1)} %fusion.3), channel_id=1, source_target_pairs={{0,4},{2,6},{4,0},{6,2},{8,12},{10,14},{12,8},{14,10},{1,5},{3,7},... | collective-permute-start | bytes 589832 | tf_op jit(solution)/shard_map/ppermute | solution.py:313
  66.0 1.4 %collective-permute-start.30 = (bf16[128,512]{1,0:T(8,128)(2,1)S(1)}, bf16[128,512]{1,0:T(8,128)(2,1)S(1)}, u32[]{:S(2)}, u32[]{:S(2)}) collective-permute-start(bf16[128,512]{1,0:T(8,128)(2,1)S(1)} %combine_other.1), channel_id=1, source_target_pairs={{0,1},{1,0},{2,3},{3,2},{4,5},{5,4},{6,7},{7,6},{8,9},{9,8},{10,11... | collective-permute-start | bytes 393224 | tf_op jit(solution)/shard_map/ppermute | solution.py:303
